TPU v7x, 32 devices: a whole 2x2x4 slice. The times are simulated.
32 devices in a mesh: gx: 8 (over z, y), gy: 4 (over x, core).
Axes of the slice: x: 2, y: 2, z: 4, core: 2. Of those that a mesh axis runs over, the one named last changes fastest.
Arguments:
- signal: bfloat16 [16384, 384], P(('gx', 'gy')), may hold values from -6 to 6
- w_up: bfloat16 [768, 1536], replicated, may hold values from -0.21875 to 0.21875
- w_down: bfloat16 [768, 1536], replicated, may hold values from -0.15625 to 0.15625
- cotangent: bfloat16 [16384, 384], P(('gx', 'gy')), may hold values from -0.046875 to 0.046875
Outputs:
- mixed_out: bfloat16 [16384, 384], P(('gx', 'gy'))
- grad_up: float32 [768, 1536], P('gx', 'gy')
- grad_down: float32 [768, 1536], P('gx', 'gy')
All inputs are finite; a program needn't handle non-finite values.
Results may differ from a plain program's by a relative error of at most 0.023.
Values may be sent and summed in bfloat16 or wider, within the bound.
No kernel may reach another device: no remote copies, remote signals or barrier semaphores. Data moves between devices by JAX's collectives and lax.ppermute only.
A program may use at most 128 MiB of HBM per device.

v0:
```python
import math

import jax
import jax.numpy as jnp
from jax import lax
from jax.sharding import PartitionSpec as P


def swapped(value, axis, distance):
    mask = 2**distance
    pairs = [(source, source ^ mask) for source in range(lax.axis_size(axis))]
    return lax.ppermute(value, axis, pairs)


def normalize(pair):
    values = pair.astype(jnp.float32)
    centre = jnp.mean(values, axis=-1, keepdims=True)
    shifted = values - centre
    spread = jnp.mean(shifted * shifted, axis=-1, keepdims=True)
    factor = lax.rsqrt(spread + 1e-05)
    return (shifted * factor, factor)


def gelu_value(pre):
    return 0.5 * pre * (1.0 + lax.erf(pre * (1.0 / math.sqrt(2.0))))


def gelu_slope(pre):
    return 0.5 * (1.0 + lax.erf(pre * (1.0 / math.sqrt(2.0)))) + pre * jnp.exp(-0.5 * pre * pre) * (
        1.0 / math.sqrt(2.0 * math.pi)
    )


def contract_last(left, right):
    return lax.dot_general(
        left, right, (((1,), (1,)), ((), ())), preferred_element_type=jnp.float32
    )


def contract_first(left, right):
    return lax.dot_general(
        left, right, (((0,), (0,)), ((), ())), preferred_element_type=jnp.float32
    )


def switch_forward(pair, w_up, w_down):
    normed, factor = normalize(pair)
    normed_bf = normed.astype(jnp.bfloat16)
    pre = jnp.dot(normed_bf, w_up, preferred_element_type=jnp.float32)
    hidden = gelu_value(pre).astype(jnp.bfloat16)
    mixed = pair.astype(jnp.float32) + contract_last(hidden, w_down)
    return (mixed.astype(jnp.bfloat16), pre)


def switch_backward(pair, pre, pair_grad, w_up, w_down, need_input):
    normed, factor = normalize(pair)
    normed_bf = normed.astype(jnp.bfloat16)
    hidden = gelu_value(pre).astype(jnp.bfloat16)
    d_hidden = jnp.dot(pair_grad, w_down, preferred_element_type=jnp.float32)
    grad_down = contract_first(pair_grad, hidden)
    d_pre = (d_hidden * gelu_slope(pre)).astype(jnp.bfloat16)
    grad_up = contract_first(normed_bf, d_pre)
    d_input = None
    if need_input:
        d_norm = contract_last(d_pre, w_up)
        d_pair = factor * (
            d_norm
            - jnp.mean(d_norm, axis=-1, keepdims=True)
            - normed * jnp.mean(d_norm * normed, axis=-1, keepdims=True)
        )
        d_input = (pair_grad.astype(jnp.float32) + d_pair).astype(jnp.bfloat16)
    return (grad_up, grad_down, d_input)


def there_gx(block, bit):
    return swapped(block, "gx", bit)


def back_gx(block, bit):
    return swapped(block, "gx", bit)


def there_gy(block, bit):
    return swapped(block, "gy", bit)


def back_gy(block, bit):
    return swapped(block, "gy", bit)


def join_pair(lower, mine, theirs):
    return jnp.where(lower, jnp.concatenate([mine, theirs], 1), jnp.concatenate([theirs, mine], 1))


def split_halves(lower, block):
    half = block.shape[0] // 2
    first, second = (block[:half], block[half:])
    return (jnp.where(lower, first, second), jnp.where(lower, second, first))


def return_halves(lower, bit, pairs, bring):
    width = pairs.shape[1] // 2
    low_part, high_part = (pairs[:, :width], pairs[:, width:])
    returned = bring(jnp.where(lower, high_part, low_part), bit)
    mine = jnp.where(lower, low_part, high_part)
    return jnp.where(
        lower, jnp.concatenate([mine, returned], 0), jnp.concatenate([returned, mine], 0)
    )


def halves_forward(state, lower, bit, send, bring, w_up, w_down):
    keep, give = split_halves(lower, state)
    pair = join_pair(lower, keep, send(give, bit))
    mixed, pre = switch_forward(pair, w_up, w_down)
    return (return_halves(lower, bit, mixed, bring), (pair, pre))


def halves_backward(grad, lower, bit, send, bring, saved, need_input, w_up, w_down):
    keep, give = split_halves(lower, grad)
    pair_grad = join_pair(lower, keep, send(give, bit))
    part_up, part_down, d_input = switch_backward(
        saved[0], saved[1], pair_grad, w_up, w_down, need_input
    )
    new_grad = None
    if need_input:
        new_grad = return_halves(lower, bit, d_input, bring)
    return (new_grad, part_up, part_down)


def local(signal, w_up, w_down, cotangent):
    span_x = lax.axis_size("gx")
    span_y = lax.axis_size("gy")
    bits_x = [span_x.bit_length() - 2, 0]
    bits_y = [span_y.bit_length() - 2, 0]
    total_up = jnp.zeros(w_up.shape, jnp.float32)
    total_down = jnp.zeros(w_down.shape, jnp.float32)
    index_x = lax.axis_index("gx")
    index_y = lax.axis_index("gy")
    plan = []
    for bit in bits_x:
        plan.append((index_x // (1 << bit) % 2 == 0, bit, there_gx, back_gx))
    for bit in bits_y:
        plan.append((index_y // (1 << bit) % 2 == 0, bit, there_gy, back_gy))
    state = signal
    saved = []
    for lower, bit, send, bring in plan:
        state, kept = halves_forward(state, lower, bit, send, bring, w_up, w_down)
        saved.append(kept)
    grad = cotangent
    for section in [3, 2, 1, 0]:
        lower, bit, send, bring = plan[section]
        grad, part_up, part_down = halves_backward(
            grad, lower, bit, send, bring, saved[section], section > 0, w_up, w_down
        )
        total_up = total_up + part_up
        total_down = total_down + part_down
    partial_up, partial_down = (
        lax.psum_scatter(
            total_up.astype(jnp.bfloat16), "gx", scatter_dimension=0, tiled=True
        ).astype(jnp.float32),
        lax.psum_scatter(
            total_down.astype(jnp.bfloat16), "gx", scatter_dimension=0, tiled=True
        ).astype(jnp.float32),
    )
    grad_up, grad_down = (
        lax.psum_scatter(
            partial_up.astype(jnp.bfloat16), "gy", scatter_dimension=1, tiled=True
        ).astype(jnp.float32),
        lax.psum_scatter(
            partial_down.astype(jnp.bfloat16), "gy", scatter_dimension=1, tiled=True
        ).astype(jnp.float32),
    )
    return (state, grad_up, grad_down)


def solution(mesh):
    return jax.shard_map(
        local,
        mesh=mesh,
        in_specs=(P(("gx", "gy"), None), P(), P(), P(("gx", "gy"), None)),
        out_specs=(P(("gx", "gy"), None), P("gx", "gy"), P("gx", "gy")),
        check_vma=False,
    )
```

profile of v0, /device:TPU:0, one launch (start us, length us, event | category | flops | bytes accessed | tf_op | source)
XLA Modules:
  0.0 317.4 jit_solution(18181582104506923445)
XLA Ops:
  8.5 4.1 %collective-permute-start = (bf16[256,384]{1,0:T(8,128)(2,1)S(1)}, bf16[256,384]{1,0:T(8,128)(2,1)S(1)}, u32[]{:S(2)}, u32[]{:S(2)}) collective-permute-start(bf16[256,384]{1,0:T(8,128)(2,1)S(1)} %get-tuple-element.37), channel_id=1, source_target_pairs={{0,16},{4,20},{8,24},{12,28},{16,0},{20,4},{24,8},{28,12},{1,17},{... | collective-permute-start | bytes 589832 | tf_op jit(solution)/shard_map/ppermute | solution.py:12
  12.6 9.1 %collective-permute-done = bf16[256,384]{1,0:T(8,128)(2,1)S(1)} collective-permute-done((bf16[256,384]{1,0:T(8,128)(2,1)S(1)}, bf16[256,384]{1,0:T(8,128)(2,1)S(1)}, u32[]{:S(2)}, u32[]{:S(2)}) %collective-permute-start) | collective-permute-done | bytes 196640 | tf_op jit(solution)/shard_map/ppermute | solution.py:12
  25.2 11.2 %collective-permute-done.1 = bf16[256,384]{1,0:T(8,128)(2,1)S(1)} collective-permute-done((bf16[256,384]{1,0:T(8,128)(2,1)S(1)}, bf16[256,384]{1,0:T(8,128)(2,1)S(1)}, u32[]{:S(2)}, u32[]{:S(2)}) %collective-permute-start.1) | collective-permute-done | bytes 196640 | tf_op jit(solution)/shard_map/ppermute | solution.py:12
  36.6 1.3 collective-permute-start.2
  37.9 4.4 %collective-permute-done.2 = bf16[256,384]{1,0:T(8,128)(2,1)S(1)} collective-permute-done((bf16[256,384]{1,0:T(8,128)(2,1)S(1)}, bf16[256,384]{1,0:T(8,128)(2,1)S(1)}, u32[]{:S(2)}, u32[]{:S(2)}) %collective-permute-start.2) | collective-permute-done | bytes 196640 | tf_op jit(solution)/shard_map/ppermute | solution.py:12
  42.8 2.1 multiply_convert_fusion.2
  45.9 1.3 collective-permute-start.3
  47.2 4.4 %collective-permute-done.3 = bf16[256,384]{1,0:T(8,128)(2,1)S(1)} collective-permute-done((bf16[256,384]{1,0:T(8,128)(2,1)S(1)}, bf16[256,384]{1,0:T(8,128)(2,1)S(1)}, u32[]{:S(2)}, u32[]{:S(2)}) %collective-permute-start.3) | collective-permute-done | bytes 196640 | tf_op jit(solution)/shard_map/ppermute | solution.py:12
  51.8 1.3 collective-permute-start.4
  53.1 4.4 %collective-permute-done.4 = bf16[256,384]{1,0:T(8,128)(2,1)S(1)} collective-permute-done((bf16[256,384]{1,0:T(8,128)(2,1)S(1)}, bf16[256,384]{1,0:T(8,128)(2,1)S(1)}, u32[]{:S(2)}, u32[]{:S(2)}) %collective-permute-start.4) | collective-permute-done | bytes 196640 | tf_op jit(solution)/shard_map/ppermute | solution.py:12
  58.0 2.1 multiply_convert_fusion.1
  62.3 4.5 %collective-permute-done.5 = bf16[256,384]{1,0:T(8,128)(2,1)} collective-permute-done((bf16[256,384]{1,0:T(8,128)(2,1)S(1)}, bf16[256,384]{1,0:T(8,128)(2,1)}, u32[]{:S(2)}, u32[]{:S(2)}) %collective-permute-start.5) | collective-permute-done | bytes 196640 | tf_op jit(solution)/shard_map/ppermute | solution.py:12
  70.1 1.8 multiply_convert_fusion
  77.2 5.7 %collective-permute-done.10 = bf16[256,384]{1,0:T(8,128)(2,1)S(1)} collective-permute-done((bf16[256,384]{1,0:T(8,128)(2,1)S(1)}, bf16[256,384]{1,0:T(8,128)(2,1)S(1)}, u32[]{:S(2)}, u32[]{:S(2)}) %collective-permute-start.10) | collective-permute-done | bytes 196640 | tf_op jit(solution)/shard_map/ppermute | solution.py:12
  86.6 4.9 %collective-permute-done.11 = bf16[256,384]{1,0:T(8,128)(2,1)S(1)} collective-permute-done((bf16[256,384]{1,0:T(8,128)(2,1)S(1)}, bf16[256,384]{1,0:T(8,128)(2,1)S(1)}, u32[]{:S(2)}, u32[]{:S(2)}) %collective-permute-start.11) | collective-permute-done | bytes 196640 | tf_op jit(solution)/shard_map/ppermute | solution.py:12
  91.7 1.5 collective-permute-start.12
  93.2 3.1 fusion.71
  99.9 1.3 collective-permute-start.13
  101.3 3.2 %fusion.75 = f32[768,1536]{1,0:T(8,128)} fusion(bf16[256,1536]{1,0:T(8,128)(2,1)S(1)} %fusion.1, f32[256]{0:T(256)S(1)} %add_rsqrt_fusion.1, f32[256]{0:T(256)S(1)} %broadcast_multiply_fusion.7, bf16[256,384]{1,0:T(8,128)(2,1)S(1)} %copy-done.5, bf16[256,384]{1,0:T(8,128)(2,1)S(1)} %get-tuple-element.30, pred[]{:T(512)S(6)} %eq.18), kind=kOutput, calls=%fused_computation.159 | convolution fusion | flops 606535680 | bytes 5900289 | tf_op jit(solution)/shard_map/dot_general | solution.py:41
  106.0 3.1 fusion.79
  109.1 5.3 %collective-permute-done.14 = bf16[256,384]{1,0:T(8,128)(2,1)S(1)} collective-permute-done((bf16[256,384]{1,0:T(8,128)(2,1)S(1)}, bf16[256,384]{1,0:T(8,128)(2,1)S(1)}, u32[]{:S(2)}, u32[]{:S(2)}) %collective-permute-start.14) | collective-permute-done | bytes 196640 | tf_op jit(solution)/shard_map/ppermute | solution.py:12
  114.4 9.1 %add_convert_fusion.1 = bf16[768,1536]{1,0:T(8,128)(2,1)} fusion(f32[768,1536]{1,0:T(8,128)} %fusion.79, f32[768,1536]{1,0:T(8,128)} %fusion.71, f32[768,1536]{1,0:T(8,128)} %fusion.75, bf16[768,1536]{1,0:T(8,128)(2,1)} %param.6, f32[256,1536]{1,0:T(8,128)S(1)} %copy-done.3, bf16[256,384]{1,0:T(8,128)(2,1)S(1)} %collective-permute-done.14, ...), kind=kOutput, calls=%fused_computation.1 | convolution fusion | flops 1220935680 | bytes 21235712 | tf_op jit(solution)/shard_map/dot_general | solution.py:41
  124.5 2.0 fusion.85
  128.7 2.5 add_convert_fusion
  131.2 60.7 %reduce-scatter.9.cloned.1.call-done = bf16[96,1536]{1,0:T(8,128)(2,1)} async-done(((bf16[768,1536]{1,0:T(8,128)(2,1)}), bf16[96,1536]{1,0:T(8,128)(2,1)}) %reduce-scatter.9.cloned.1.call-update) | async-done | bytes 294928 | tf_op jit(solution)/shard_map/reduce_scatter | solution.py:158
  191.9 1.9 copy.7
  193.9 69.7 %reduce-scatter.11.cloned.1.call-done = bf16[96,1536]{1,0:T(8,128)(2,1)} async-done(((bf16[768,1536]{1,0:T(8,128)(2,1)}), bf16[96,1536]{1,0:T(8,128)(2,1)}) %reduce-scatter.11.cloned.1.call-update) | async-done | bytes 294928 | tf_op jit(solution)/shard_map/reduce_scatter | solution.py:161
  263.5 1.9 copy.9
  265.5 2.9 fusion.23
  268.5 1.4 collective-permute-done.7
  270.8 15.2 %reduce-scatter.13.cloned.1.call-done = bf16[384,96]{1,0:T(8,128)(2,1)} async-done(((bf16[1536,96]{1,0:T(8,128)(2,1)}), bf16[384,96]{1,0:T(8,128)(2,1)}) %reduce-scatter.13.cloned.1.call-update) | async-done | bytes 73744
  287.6 21.5 %reduce-scatter.15.cloned.1.call-done = bf16[384,96]{1,0:T(8,128)(2,1)} async-done(((bf16[1536,96]{1,0:T(8,128)(2,1)}), bf16[384,96]{1,0:T(8,128)(2,1)}) %reduce-scatter.15.cloned.1.call-update) | async-done | bytes 73744
  (154 shorter events, 34.1 us)
Async XLA Ops:
  7.2 15.0 %copy-start = (bf16[768,1536]{1,0:T(8,128)(2,1)S(1)}, bf16[768,1536]{1,0:T(8,128)(2,1)}, u32[]{:S(2)}) copy-start(bf16[768,1536]{1,0:T(8,128)(2,1)} %param.5) | copy-start | bytes 7077892
  7.2 184.7 %reduce-scatter.9.cloned.1.call-start = ((), (), s32[]{:S(2)}) async-start(), calls=%async_computation.4 | async-start | bytes 2654208 | tf_op jit(solution)/shard_map/reduce_scatter | solution.py:158
  8.5 13.2 %collective-permute-start = (bf16[256,384]{1,0:T(8,128)(2,1)S(1)}, bf16[256,384]{1,0:T(8,128)(2,1)S(1)}, u32[]{:S(2)}, u32[]{:S(2)}) collective-permute-start(bf16[256,384]{1,0:T(8,128)(2,1)S(1)} %get-tuple-element.37), channel_id=1, source_target_pairs={{0,16},{4,20},{8,24},{12,28},{16,0},{20,4},{24,8},{28,12},{1,17},{... | collective-permute-start | bytes 589832 | tf_op jit(solution)/shard_map/ppermute | solution.py:12
  25.1 11.3 %collective-permute-start.1 = (bf16[256,384]{1,0:T(8,128)(2,1)S(1)}, bf16[256,384]{1,0:T(8,128)(2,1)S(1)}, u32[]{:S(2)}, u32[]{:S(2)}) collective-permute-start(bf16[256,384]{1,0:T(8,128)(2,1)S(1)} %get-tuple-element.36), channel_id=1, source_target_pairs={{0,16},{4,20},{8,24},{12,28},{16,0},{20,4},{24,8},{28,12},{1,17},{... | collective-permute-start | bytes 589832 | tf_op jit(solution)/shard_map/ppermute | solution.py:12
  36.6 5.7 %collective-permute-start.2 = (bf16[256,384]{1,0:T(8,128)(2,1)S(1)}, bf16[256,384]{1,0:T(8,128)(2,1)S(1)}, u32[]{:S(2)}, u32[]{:S(2)}) collective-permute-start(bf16[256,384]{1,0:T(8,128)(2,1)S(1)} %get-tuple-element.33), channel_id=1, source_target_pairs={{0,4},{4,0},{8,12},{12,8},{16,20},{20,16},{24,28},{28,24},{1,5},{5... | collective-permute-start | bytes 589832 | tf_op jit(solution)/shard_map/ppermute | solution.py:12
  45.9 5.7 %collective-permute-start.3 = (bf16[256,384]{1,0:T(8,128)(2,1)S(1)}, bf16[256,384]{1,0:T(8,128)(2,1)S(1)}, u32[]{:S(2)}, u32[]{:S(2)}) collective-permute-start(bf16[256,384]{1,0:T(8,128)(2,1)S(1)} %get-tuple-element.32), channel_id=1, source_target_pairs={{0,4},{4,0},{8,12},{12,8},{16,20},{20,16},{24,28},{28,24},{1,5},{5... | collective-permute-start | bytes 589832 | tf_op jit(solution)/shard_map/ppermute | solution.py:12
  51.8 5.7 %collective-permute-start.4 = (bf16[256,384]{1,0:T(8,128)(2,1)S(1)}, bf16[256,384]{1,0:T(8,128)(2,1)S(1)}, u32[]{:S(2)}, u32[]{:S(2)}) collective-permute-start(bf16[256,384]{1,0:T(8,128)(2,1)S(1)} %get-tuple-element.29), channel_id=1, source_target_pairs={{0,2},{1,3},{2,0},{3,1},{4,6},{5,7},{6,4},{7,5},{8,10},{9,11},{10,... | collective-permute-start | bytes 589832 | tf_op jit(solution)/shard_map/ppermute | solution.py:12
  57.5 2.6 copy-start.4
  61.0 5.8 %collective-permute-start.5 = (bf16[256,384]{1,0:T(8,128)(2,1)S(1)}, bf16[256,384]{1,0:T(8,128)(2,1)}, u32[]{:S(2)}, u32[]{:S(2)}) collective-permute-start(bf16[256,384]{1,0:T(8,128)(2,1)S(1)} %get-tuple-element.28), channel_id=1, source_target_pairs={{0,2},{1,3},{2,0},{3,1},{4,6},{5,7},{6,4},{7,5},{8,10},{9,11},{10,... | collective-permute-start | bytes 589832 | tf_op jit(solution)/shard_map/ppermute | solution.py:12
  62.3 5.8 %copy-start.28 = (bf16[512,384]{1,0:T(8,128)(2,1)S(1)}, bf16[512,384]{1,0:T(8,128)(2,1)}, u32[]{:S(2)}) copy-start(bf16[512,384]{1,0:T(8,128)(2,1)} %param.7) | copy-start | bytes 1179652
  68.0 1.5 collective-permute-start.6
  68.2 5.6 %copy-start.12 = (bf16[256,384]{1,0:T(8,128)(2,1)}, bf16[256,384]{1,0:T(8,128)(2,1)S(1)}, u32[]{:S(2)}) copy-start(bf16[256,384]{1,0:T(8,128)(2,1)S(1)} %get-tuple-element.21) | copy-start | bytes 589828
  68.2 3.7 %collective-permute-start.8 = (bf16[256,384]{1,0:T(8,128)(2,1)S(1)}, bf16[256,384]{1,0:T(8,128)(2,1)S(1)}, u32[]{:S(2)}, u32[]{:S(2)}) collective-permute-start(bf16[256,384]{1,0:T(8,128)(2,1)S(1)} %get-tuple-element.22), channel_id=1, source_target_pairs={{0,1},{1,0},{2,3},{3,2},{4,5},{5,4},{6,7},{7,6},{8,9},{9,8},{10,11... | collective-permute-start | bytes 589832 | tf_op jit(solution)/shard_map/ppermute | solution.py:12
  74.1 8.8 %copy-start.34 = (f32[256,1536]{1,0:T(8,128)S(1)}, f32[256,1536]{1,0:T(8,128)}, u32[]{:S(2)}) copy-start(f32[256,1536]{1,0:T(8,128)} %get-tuple-element.42) | copy-start | bytes 4718596
  74.2 1.5 collective-permute-start.9
  75.9 9.0 %copy-start.14 = (bf16[256,384]{1,0:T(8,128)(2,1)}, bf16[256,384]{1,0:T(8,128)(2,1)S(1)}, u32[]{:S(2)}) copy-start(bf16[256,384]{1,0:T(8,128)(2,1)S(1)} %get-tuple-element.17) | copy-start | bytes 589828
  75.9 7.0 %collective-permute-start.10 = (bf16[256,384]{1,0:T(8,128)(2,1)S(1)}, bf16[256,384]{1,0:T(8,128)(2,1)S(1)}, u32[]{:S(2)}, u32[]{:S(2)}) collective-permute-start(bf16[256,384]{1,0:T(8,128)(2,1)S(1)} %get-tuple-element.18), channel_id=1, source_target_pairs={{0,2},{1,3},{2,0},{3,1},{4,6},{5,7},{6,4},{7,5},{8,10},{9,11},{10,... | collective-permute-start | bytes 589832 | tf_op jit(solution)/shard_map/ppermute | solution.py:12
  85.3 6.2 %collective-permute-start.11 = (bf16[256,384]{1,0:T(8,128)(2,1)S(1)}, bf16[256,384]{1,0:T(8,128)(2,1)S(1)}, u32[]{:S(2)}, u32[]{:S(2)}) collective-permute-start(bf16[256,384]{1,0:T(8,128)(2,1)S(1)} %get-tuple-element.16), channel_id=1, source_target_pairs={{0,2},{1,3},{2,0},{3,1},{4,6},{5,7},{6,4},{7,5},{8,10},{9,11},{10,... | collective-permute-start | bytes 589832 | tf_op jit(solution)/shard_map/ppermute | solution.py:12
  91.7 7.8 %copy-start.16 = (bf16[256,384]{1,0:T(8,128)(2,1)}, bf16[256,384]{1,0:T(8,128)(2,1)S(1)}, u32[]{:S(2)}) copy-start(bf16[256,384]{1,0:T(8,128)(2,1)S(1)} %get-tuple-element.13) | copy-start | bytes 589828
  91.7 5.9 %copy-start.33 = (f32[256,1536]{1,0:T(8,128)S(1)}, f32[256,1536]{1,0:T(8,128)}, u32[]{:S(2)}) copy-start(f32[256,1536]{1,0:T(8,128)} %get-tuple-element.40) | copy-start | bytes 4718596
  91.7 5.9 %collective-permute-start.12 = (bf16[256,384]{1,0:T(8,128)(2,1)S(1)}, bf16[256,384]{1,0:T(8,128)(2,1)S(1)}, u32[]{:S(2)}, u32[]{:S(2)}) collective-permute-start(bf16[256,384]{1,0:T(8,128)(2,1)S(1)} %get-tuple-element.14), channel_id=1, source_target_pairs={{0,4},{4,0},{8,12},{12,8},{16,20},{20,16},{24,28},{28,24},{1,5},{5... | collective-permute-start | bytes 589832 | tf_op jit(solution)/shard_map/ppermute | solution.py:12
  99.9 5.7 %collective-permute-start.13 = (bf16[256,384]{1,0:T(8,128)(2,1)S(1)}, bf16[256,384]{1,0:T(8,128)(2,1)S(1)}, u32[]{:S(2)}, u32[]{:S(2)}) collective-permute-start(bf16[256,384]{1,0:T(8,128)(2,1)S(1)} %get-tuple-element.12), channel_id=1, source_target_pairs={{0,4},{4,0},{8,12},{12,8},{16,20},{20,16},{24,28},{28,24},{1,5},{5... | collective-permute-start | bytes 589832 | tf_op jit(solution)/shard_map/ppermute | solution.py:12
  105.9 8.5 %copy-start.3 = (f32[256,1536]{1,0:T(8,128)S(1)}, f32[256,1536]{1,0:T(8,128)}, u32[]{:S(2)}) copy-start(f32[256,1536]{1,0:T(8,128)} %copy-done.2) | copy-start | bytes 4718596
  105.9 8.5 %copy-start.11 = (bf16[256,384]{1,0:T(8,128)(2,1)S(1)}, bf16[256,384]{1,0:T(8,128)(2,1)}, u32[]{:S(2)}) copy-start(bf16[256,384]{1,0:T(8,128)(2,1)} %copy-done.10) | copy-start | bytes 589828
  105.9 8.5 %copy-start.30 = (f32[256]{0:T(256)S(1)}, f32[256]{0:T(256)}, u32[]{:S(2)}) copy-start(f32[256]{0:T(256)} %copy-done.29) | copy-start | bytes 3076
  105.9 8.5 %copy-start.32 = (f32[256]{0:T(256)S(1)}, f32[256]{0:T(256)}, u32[]{:S(2)}) copy-start(f32[256]{0:T(256)} %copy-done.31) | copy-start | bytes 3076
  105.9 8.5 %collective-permute-start.14 = (bf16[256,384]{1,0:T(8,128)(2,1)S(1)}, bf16[256,384]{1,0:T(8,128)(2,1)S(1)}, u32[]{:S(2)}, u32[]{:S(2)}) collective-permute-start(bf16[256,384]{1,0:T(8,128)(2,1)S(1)} %get-tuple-element.10), channel_id=1, source_target_pairs={{0,16},{4,20},{8,24},{12,28},{16,0},{20,4},{24,8},{28,12},{1,17},{... | collective-permute-start | bytes 589832 | tf_op jit(solution)/shard_map/ppermute | solution.py:12
  123.5 140.0 %reduce-scatter.11.cloned.1.call-start = ((), (), s32[]{:S(2)}) async-start(), calls=%async_computation.5 | async-start | bytes 2654208 | tf_op jit(solution)/shard_map/reduce_scatter | solution.py:161
  131.1 154.8 %reduce-scatter.13.cloned.1.call-start = ((), (), s32[]{:S(2)}) async-start(), calls=%async_computation.6 | async-start | bytes 491520
  193.8 115.3 %reduce-scatter.15.cloned.1.call-start = ((), (), s32[]{:S(2)}) async-start(), calls=%async_computation.7 | async-start | bytes 491520
  265.5 45.4 %copy-start.1 = (bf16[768,1536]{1,0:T(8,128)(2,1)S(1)}, bf16[768,1536]{1,0:T(8,128)(2,1)}, u32[]{:S(2)}) copy-start(bf16[768,1536]{1,0:T(8,128)(2,1)} %param.5) | copy-start | bytes 7077892
  268.4 1.5 collective-permute-start.7
  (22 other events, 32.5 us)
Sparse Core Ops, SparseCore 0:
  123.6 68.2 reduce-scatter.8
  195.4 68.1 reduce-scatter.10
  266.0 19.8 reduce-scatter.12
  288.3 20.7 reduce-scatter.14
where the time goes:
time: 318 us; the launch traced here: 317 us
  waiting for transfers between devices  227 us (71%)
  matrix products  42.3 us (13%)
  starting transfers between devices  16.1 us (5%)
  between operations  14.4 us (5%)
  other arithmetic  8.89 us (3%)
  local copies, waits for them, and re-layouts  8.63 us (3%)
    reduce_scatter x1, waiting for transfers between devices, local(): lax.psum_scatter(total_down.astype(jnp.bfloat16), 'gx', scatter_dimension...  69.7 us
    reduce_scatter x1, waiting for transfers between devices, local(): lax.psum_scatter(total_up.astype(jnp.bfloat16), 'gx', scatter_dimension=0...  60.7 us
    ppermute x15, waiting for transfers between devices, swapped(): return lax.ppermute(value, axis, pairs)  60 us
    unnamed x6, waiting for transfers between devices  36.8 us
    dot_general x8, matrix products, contract_first(): lax.dot_general(left, right, (((0,), (0,)), ((), ())), preferred_element_...  24.6 us
    ppermute x15, starting transfers between devices, swapped(): return lax.ppermute(value, axis, pairs)  15.9 us
    unnamed x74, local copies, waits for them, and re-layouts  8.63 us
    dot_general x7, matrix products, contract_last(): lax.dot_general(left, right, (((1,), (1,)), ((), ())), preferred_element_...  8.15 us
  transfers between devices with their start and end apart: 19, of which 18 were waited for; matrix products, arithmetic and copies ran while one was open for 9% of the time, Pallas kernels for 0%

commit v1 on v0

v1 whole, which is shorter than its diff:
```python
import math

import jax
import jax.numpy as jnp
from jax import lax
from jax.sharding import PartitionSpec as P


def normalize(pair):
    values = pair.astype(jnp.float32)
    centre = jnp.mean(values, axis=-1, keepdims=True)
    shifted = values - centre
    spread = jnp.mean(shifted * shifted, axis=-1, keepdims=True)
    factor = lax.rsqrt(spread + 1e-05)
    return (shifted * factor, factor)


def gelu_value(pre):
    return 0.5 * pre * (1.0 + lax.erf(pre * (1.0 / math.sqrt(2.0))))


def gelu_slope(pre):
    return 0.5 * (1.0 + lax.erf(pre * (1.0 / math.sqrt(2.0)))) + pre * jnp.exp(-0.5 * pre * pre) * (
        1.0 / math.sqrt(2.0 * math.pi)
    )


def contract_last(left, right):
    return lax.dot_general(
        left, right, (((1,), (1,)), ((), ())), preferred_element_type=jnp.float32
    )


def contract_first(left, right):
    return lax.dot_general(
        left, right, (((0,), (0,)), ((), ())), preferred_element_type=jnp.float32
    )


def section_groups(span_x, span_y):
    bits_x = [span_x.bit_length() - 2, 0]
    bits_y = [span_y.bit_length() - 2, 0]
    mask_x = sum(1 << bit for bit in bits_x)
    mask_y = sum(1 << bit for bit in bits_y)
    groups = []
    for base_x in range(span_x):
        for base_y in range(span_y):
            if base_x & mask_x or base_y & mask_y:
                continue
            group = []
            for member in range(16):
                at_x, at_y = base_x, base_y
                at_x |= (member >> 3 & 1) << bits_x[0] | (member >> 2 & 1) << bits_x[1]
                at_y |= (member >> 1 & 1) << bits_y[0] | (member & 1) << bits_y[1]
                group.append(at_x * span_y + at_y)
            groups.append(group)
    return groups


def exchange(block, groups):
    return lax.all_to_all(
        block, ("gx", "gy"), split_axis=0, concat_axis=0, axis_index_groups=groups, tiled=True
    )


def to_pairs(state, mask):
    members, rows, width = state.shape
    blocks = state.reshape(members // (2 * mask), 2, mask * rows, width)
    return jnp.concatenate([blocks[:, 0], blocks[:, 1]], axis=-1).reshape(-1, 2 * width)


def from_pairs(pairs, mask, members):
    width = pairs.shape[1] // 2
    blocks = pairs.reshape(members // (2 * mask), -1, 2 * width)
    return jnp.stack([blocks[..., :width], blocks[..., width:]], axis=1).reshape(members, -1, width)


def halve(total, axis, bit, dim):
    mine = lax.axis_index(axis) // (1 << bit) % 2
    give = lax.dynamic_index_in_dim(total, 1 - mine, dim, keepdims=False).astype(jnp.bfloat16)
    keep = lax.dynamic_index_in_dim(total, mine, dim, keepdims=False)
    pairs = [(source, source ^ (1 << bit)) for source in range(lax.axis_size(axis))]
    taken = lax.ppermute(give, axis, pairs)
    return (keep.astype(jnp.float32) + taken.astype(jnp.float32)).astype(jnp.bfloat16)


def scatter_sum(total, order):
    span_x = lax.axis_size("gx")
    span_y = lax.axis_size("gy")
    count_x = span_x.bit_length() - 1
    count_y = span_y.bit_length() - 1
    rows = total.shape[0] // span_x
    columns = total.shape[1] // span_y
    left = [("gy", bit) for bit in range(count_y)][::-1] + [("gx", bit) for bit in range(count_x)][::-1]
    blocks = total.reshape(span_x, rows, span_y, columns).transpose(2, 0, 1, 3)
    blocks = blocks.reshape((2,) * len(left) + (rows, columns)).astype(jnp.bfloat16)
    for step in order:
        dim = left.index(step)
        blocks = halve(blocks, step[0], step[1], dim)
        left.pop(dim)
    return blocks.astype(jnp.float32)


def local(signal, w_up, w_down, cotangent):
    span_x = lax.axis_size("gx")
    span_y = lax.axis_size("gy")
    groups = section_groups(span_x, span_y)
    rows, width = signal.shape
    state = exchange(signal.reshape(16, rows // 16, width), groups)
    grad = exchange(cotangent.reshape(16, rows // 16, width), groups)
    masks = [8, 4, 2, 1]
    saved = []
    for mask in masks:
        pair = to_pairs(state, mask)
        normed, factor = normalize(pair)
        normed_bf = normed.astype(jnp.bfloat16)
        pre = jnp.dot(normed_bf, w_up, preferred_element_type=jnp.float32)
        hidden = gelu_value(pre).astype(jnp.bfloat16)
        mixed = (pair.astype(jnp.float32) + contract_last(hidden, w_down)).astype(jnp.bfloat16)
        state = from_pairs(mixed, mask, 16)
        saved.append((normed, normed_bf, factor, pre, hidden))
    mixed_out = exchange(state, groups).reshape(rows, width)
    grads, slopes = [], []
    for section in [3, 2, 1, 0]:
        normed, normed_bf, factor, pre, hidden = saved[section]
        pair_grad = to_pairs(grad, masks[section])
        d_hidden = jnp.dot(pair_grad, w_down, preferred_element_type=jnp.float32)
        d_pre = (d_hidden * gelu_slope(pre)).astype(jnp.bfloat16)
        grads.append(pair_grad)
        slopes.append(d_pre)
        if section > 0:
            d_norm = contract_last(d_pre, w_up)
            d_pair = factor * (
                d_norm
                - jnp.mean(d_norm, axis=-1, keepdims=True)
                - normed * jnp.mean(d_norm * normed, axis=-1, keepdims=True)
            )
            d_input = (pair_grad.astype(jnp.float32) + d_pair).astype(jnp.bfloat16)
            grad = from_pairs(d_input, masks[section], 16)
    order = [3, 2, 1, 0]
    total_down = contract_first(
        jnp.concatenate(grads, 0), jnp.concatenate([saved[k][4] for k in order], 0)
    )
    total_up = contract_first(
        jnp.concatenate([saved[k][1] for k in order], 0), jnp.concatenate(slopes, 0)
    )
    rest_y = [("gy", bit) for bit in range(1, span_y.bit_length() - 1)]
    rest_x = [("gx", bit) for bit in range(1, span_x.bit_length() - 1)]
    core, across = ("gy", 0), ("gx", 0)
    grad_up = scatter_sum(total_up, [core] + rest_y + [across] + rest_x)
    grad_down = scatter_sum(total_down, [core, across] + rest_y + rest_x)
    return (mixed_out, grad_up, grad_down)


def solution(mesh):
    return jax.shard_map(
        local,
        mesh=mesh,
        in_specs=(P(("gx", "gy"), None), P(), P(), P(("gx", "gy"), None)),
        out_specs=(P(("gx", "gy"), None), P("gx", "gy"), P("gx", "gy")),
        check_vma=False,
    )
```

time: 318 us -> 146 us (0.46)
  waiting for transfers between devices: 227 us -> 42 us
  local copies, waits for them, and re-layouts: 8.63 us -> 32.2 us
  between operations: 14.4 us -> 1.54 us
  matrix products: 42.3 us -> 29.9 us
  starting transfers between devices: 16.1 us -> 27.2 us
  other arithmetic: 8.89 us -> 12.5 us
    reduce_scatter x2 -> x0, waiting for transfers between devices: 130 us -> none  [the longest x1 69.7 us: local(): lax.psum_scatter(total_down.astype(jnp.bfloat16), 'gx', scatter_dimension...]
    unnamed x6 -> x0, waiting for transfers between devices: 36.8 us -> none
    ppermute x15 -> x10, waiting for transfers between devices: 60 us -> 23.3 us  [halve(): taken = lax.ppermute(give, axis, pairs)]
    all_to_all x0 -> x3, waiting for transfers between devices: none -> 18.7 us  [exchange(): lax.all_to_all(block, ('gx', 'gy'), split_axis=0, concat_axis=0, axis_ind...]
    all_to_all x0 -> x3, starting transfers between devices: none -> 17.6 us  [exchange(): lax.all_to_all(block, ('gx', 'gy'), split_axis=0, concat_axis=0, axis_ind...]
    dot_general x8 -> x2, matrix products: 24.6 us -> 8.13 us  [contract_first(): lax.dot_general(left, right, (((0,), (0,)), ((), ())), preferred_element_...]
    convert_element_type x0 -> x4, local copies, waits for them, and re-layouts: none -> 14.5 us  [scatter_sum(): blocks.reshape((2,) * len(left) + (rows, columns)).astype(jnp.bfloat16)]
    convert_element_type x5 -> x17, other arithmetic: 2.4 us -> 9.64 us  [the longest x8 6.53 us: halve(): (keep.astype(jnp.float32) + taken.astype(jnp.float32)).astype(jnp.bfloat16)]
  transfers between devices with their start and end apart: 19 -> 13, of which waited for: 18 -> 9; matrix products, arithmetic and copies ran while one was open for 9% -> 27% of each run, Pallas kernels for 0% -> 0%
where the time goes in v1:
time: 146 us; the launch traced here: 145 us
  waiting for transfers between devices  42 us (29%)
  local copies, waits for them, and re-layouts  32.2 us (22%)
  matrix products  29.9 us (20%)
  starting transfers between devices  27.2 us (19%)
  other arithmetic  12.5 us (9%)
  between operations  1.54 us (1%)
    ppermute x10, waiting for transfers between devices, halve(): taken = lax.ppermute(give, axis, pairs)  23.3 us
    all_to_all x3, waiting for transfers between devices, exchange(): lax.all_to_all(block, ('gx', 'gy'), split_axis=0, concat_axis=0, axis_ind...  18.7 us
    all_to_all x3, starting transfers between devices, exchange(): lax.all_to_all(block, ('gx', 'gy'), split_axis=0, concat_axis=0, axis_ind...  17.6 us
    convert_element_type x4, local copies, waits for them, and re-layouts, scatter_sum(): blocks.reshape((2,) * len(left) + (rows, columns)).astype(jnp.bfloat16)  14.5 us
    unnamed x81, local copies, waits for them, and re-layouts  11.7 us
    ppermute x10, starting transfers between devices, halve(): taken = lax.ppermute(give, axis, pairs)  9.6 us
    dot_general x4, matrix products, local(): pre = jnp.dot(normed_bf, w_up, preferred_element_type=jnp.float32)  8.19 us
    dot_general x2, matrix products, contract_first(): lax.dot_general(left, right, (((0,), (0,)), ((), ())), preferred_element_...  8.13 us
  transfers between devices with their start and end apart: 13, of which 9 were waited for; matrix products, arithmetic and copies ran while one was open for 27% of the time, Pallas kernels for 0%

profile of v1, /device:TPU:0, one launch (start us, length us, event | category | flops | bytes accessed | tf_op | source)
XLA Modules:
  0.0 145.3 jit_solution(5746555399722253218)
XLA Ops:
  0.6 7.4 %all-to-all-start = ((bf16[16,32,384]{2,1,0:T(8,128)(2,1)}), bf16[16,32,384]{2,1,0:T(8,128)(2,1)S(1)}, u32[]{:S(2)}, u32[]{:S(2)}) async-start(bf16[16,32,384]{2,1,0:T(8,128)(2,1)} %bitcast.243), calls=%async_computation | async-start | bytes 786432 | tf_op jit(solution)/shard_map/all_to_all | solution.py:61
  8.1 14.2 %all-to-all-done = bf16[16,32,384]{2,1,0:T(8,128)(2,1)S(1)} async-done(((bf16[16,32,384]{2,1,0:T(8,128)(2,1)}), bf16[16,32,384]{2,1,0:T(8,128)(2,1)S(1)}, u32[]{:S(2)}, u32[]{:S(2)}) %all-to-all-start) | async-done | bytes 393248 | tf_op jit(solution)/shard_map/all_to_all | solution.py:61
  22.4 4.2 %all-to-all-start.2 = ((bf16[16,32,384]{2,1,0:T(8,128)(2,1)}), bf16[16,32,384]{2,1,0:T(8,128)(2,1)}, u32[]{:S(2)}, u32[]{:S(2)}) async-start(bf16[16,32,384]{2,1,0:T(8,128)(2,1)} %bitcast.244), calls=%async_computation.2 | async-start | bytes 786432 | tf_op jit(solution)/shard_map/all_to_all | solution.py:61
  27.3 2.0 %multiply_convert_fusion.3 = (bf16[256,1536]{1,0:T(8,128)(2,1)S(1)}, f32[256,1536]{1,0:T(8,128)}) fusion(bf16[256,768]{1,0:T(8,128)(2,1)S(1)} %fusion.100, bf16[768,1536]{1,0:T(8,128)(2,1)S(1)} %copy-done), kind=kOutput, calls=%fused_computation.74 | convolution fusion | flops 605945856 | bytes 5111808 | tf_op jit(solution)/shard_map/dot_general | solution.py:117
  30.8 2.0 %multiply_convert_fusion.2 = (bf16[256,1536]{1,0:T(8,128)(2,1)S(1)}, f32[256,1536]{1,0:T(8,128)}) fusion(bf16[256,768]{1,0:T(8,128)(2,1)S(1)} %fusion.70, bf16[768,1536]{1,0:T(8,128)(2,1)S(1)} %copy-done), kind=kOutput, calls=%fused_computation.72 | convolution fusion | flops 605945856 | bytes 5111808 | tf_op jit(solution)/shard_map/dot_general | solution.py:117
  34.5 2.0 %multiply_convert_fusion.1 = (bf16[256,1536]{1,0:T(8,128)(2,1)S(1)}, f32[256,1536]{1,0:T(8,128)}) fusion(bf16[256,768]{1,0:T(8,128)(2,1)S(1)} %fusion.75, bf16[768,1536]{1,0:T(8,128)(2,1)S(1)} %copy-done), kind=kOutput, calls=%fused_computation.70 | convolution fusion | flops 605945856 | bytes 5111808 | tf_op jit(solution)/shard_map/dot_general | solution.py:117
  39.5 2.2 %multiply_convert_fusion = (bf16[256,1536]{1,0:T(8,128)(2,1)}, f32[256,1536]{1,0:T(8,128)}) fusion(bf16[256,768]{1,0:T(8,128)(2,1)S(1)} %fusion.80, bf16[768,1536]{1,0:T(8,128)(2,1)S(1)} %copy-done), kind=kOutput, calls=%fused_computation.68 | convolution fusion | flops 605945856 | bytes 5111808 | tf_op jit(solution)/shard_map/dot_general | solution.py:117
  42.8 3.1 %fusion.14 = bf16[256,1536]{1,0:T(8,128)(2,1)S(1)} fusion(bf16[768,1536]{1,0:T(8,128)(2,1)} %param.6, f32[256,1536]{1,0:T(8,128)} %get-tuple-element.46, bf16[256,384]{1,0:T(8,128)(2,1)S(1)} %bitcast.228, bf16[256,384]{1,0:T(8,128)(2,1)S(1)} %bitcast.225), kind=kOutput, calls=%fused_computation.20 | convolution fusion | flops 608698368 | bytes 5111808 | tf_op jit(solution)/shard_map/dot_general | solution.py:127
  57.0 4.1 %convolution_convert_fusion = bf16[768,1536]{1,0:T(8,128)(2,1)} fusion(bf16[256,1536]{1,0:T(8,128)(2,1)S(1)} %copy-done.18, bf16[256,1536]{1,0:T(8,128)(2,1)S(1)} %copy-done.20, bf16[256,1536]{1,0:T(8,128)(2,1)S(1)} %copy-done.22, bf16[256,1536]{1,0:T(8,128)(2,1)S(1)} %copy-done.16, bf16[256,768]{1,0:T(8,128)(2,1)S(1)} %maximum_bitcast_fusion, ...), kind=kOutput, calls=%fused_computation | convolution fusion | flops 2440691712 | bytes 7077888 | tf_op jit(solution)/shard_map/dot_general | solution.py:35
  61.1 5.2 %convert_element_type.288 = bf16[8,96,4,384]{3,2,1,0:T(4,128)(2,1)} reshape(bf16[768,1536]{1,0:T(8,128)(2,1)} %convolution_convert_fusion) | data formatting | bytes 4718592 | tf_op jit(solution)/shard_map/convert_element_type | solution.py:96
  66.3 2.1 %copy.15 = bf16[8,96,4,384]{3,1,0,2:T(8,128)(2,1)S(1)} copy(bf16[8,96,4,384]{3,2,1,0:T(4,128)(2,1)} %convert_element_type.288) | data formatting | bytes 4718592 | tf_op jit(solution)/shard_map/convert_element_type | solution.py:96
  73.3 4.1 %convolution_convert_fusion.1 = bf16[768,1536]{1,0:T(8,128)(2,1)} fusion(bf16[256,1536]{1,0:T(8,128)(2,1)S(1)} %fusion.17, bf16[256,1536]{1,0:T(8,128)(2,1)S(1)} %copy-done.39, bf16[256,1536]{1,0:T(8,128)(2,1)S(1)} %copy-done.37, bf16[256,1536]{1,0:T(8,128)(2,1)S(1)} %copy-done.35, bf16[256,768]{1,0:T(8,128)(2,1)S(1)} %copy-done.6, ...), kind=kOutput, calls=%fused_computation.1 | convolution fusion | flops 2435973120 | bytes 7077888 | tf_op jit(solution)/shard_map/dot_general | solution.py:35
  77.4 5.2 %convert_element_type.263 = bf16[8,96,4,384]{3,2,1,0:T(4,128)(2,1)} reshape(bf16[768,1536]{1,0:T(8,128)(2,1)} %convolution_convert_fusion.1) | data formatting | bytes 4718592 | tf_op jit(solution)/shard_map/convert_element_type | solution.py:96
  82.6 2.0 %copy.14 = bf16[8,96,4,384]{3,1,0,2:T(8,128)(2,1)S(1)} copy(bf16[8,96,4,384]{3,2,1,0:T(4,128)(2,1)} %convert_element_type.263) | data formatting | bytes 4718592 | tf_op jit(solution)/shard_map/convert_element_type | solution.py:96
  84.6 1.4 copy-done.2
  87.4 2.5 %fusion.59 = bf16[256,768]{1,0:T(8,128)(2,1)S(1)} fusion(bf16[256,1536]{1,0:T(8,128)(2,1)S(1)} %copy-done.16, bf16[768,1536]{1,0:T(8,128)(2,1)} %param.6, bf16[256,384]{1,0:T(8,128)(2,1)S(1)} %bitcast.189, bf16[256,384]{1,0:T(8,128)(2,1)S(1)} %bitcast.183), kind=kOutput, calls=%fused_computation.83 | convolution fusion | flops 605159424 | bytes 3932160 | tf_op jit(solution)/shard_map/dot_general | solution.py:29
  90.7 6.0 %all-to-all-start.1 = ((bf16[16,32,384]{2,1,0:T(8,128)(2,1)}), bf16[16,32,384]{2,1,0:T(8,128)(2,1)}, u32[]{:S(2)}, u32[]{:S(2)}) async-start(bf16[16,32,384]{2,1,0:T(8,128)(2,1)} %bitcast.28), calls=%async_computation.1 | async-start | bytes 786432 | tf_op jit(solution)/shard_map/all_to_all | solution.py:61
  96.7 2.1 %fusion.18 = bf16[2,2,2,2,96,384]{5,4,3,2,1,0:T(8,128)(2,1)S(1)} fusion(bf16[2,2,2,2,96,384]{5,4,3,2,1,0:T(8,128)(2,1)} %collective-permute-done.5, bf16[2,2,2,2,2,96,384]{6,5,4,3,2,1,0:T(8,128)(2,1)} %bitcast.175, s32[]{:T(128)S(6)} %select_n.98), kind=kLoop, calls=%fused_computation.29 | loop fusion | flops 2359296 | bytes 3538948 | tf_op jit(solution)/shard_map/convert_element_type | solution.py:84
  99.8 1.9 %collective-permute-start.6 = (bf16[2,2,2,96,384]{4,3,2,1,0:T(8,128)(2,1)}, bf16[2,2,2,96,384]{4,3,2,1,0:T(8,128)(2,1)}, u32[]{:S(2)}, u32[]{:S(2)}) collective-permute-start(bf16[2,2,2,96,384]{4,3,2,1,0:T(8,128)(2,1)} %dynamic-slice_bitcast_fusion.2), channel_id=1, source_target_pairs={{0,4},{4,0},{8,12},{12,8},{16,20},{20,16},{24,28},{28,24},{1,5},{5... | collective-permute-start | bytes 1769480 | tf_op jit(solution)/shard_map/ppermute | solution.py:83
  101.7 1.6 %fusion.19 = bf16[2,2,2,2,96,384]{5,4,3,2,1,0:T(8,128)(2,1)S(1)} fusion(bf16[2,2,2,2,96,384]{5,4,3,2,1,0:T(8,128)(2,1)} %collective-permute-done, bf16[2,2,2,2,2,96,384]{6,5,4,3,2,1,0:T(8,128)(2,1)S(1)} %bitcast.177, s32[]{:T(128)S(6)} %select_n.98), kind=kLoop, calls=%fused_computation.31 | loop fusion | flops 2359296 | bytes 3538948 | tf_op jit(solution)/shard_map/convert_element_type | solution.py:84
  104.2 1.5 %collective-permute-start.1 = (bf16[2,2,2,96,384]{4,3,2,1,0:T(8,128)(2,1)}, bf16[2,2,2,96,384]{4,3,2,1,0:T(8,128)(2,1)}, u32[]{:S(2)}, u32[]{:S(2)}) collective-permute-start(bf16[2,2,2,96,384]{4,3,2,1,0:T(8,128)(2,1)} %dynamic-slice_bitcast_fusion.3), channel_id=1, source_target_pairs={{0,2},{1,3},{2,0},{3,1},{4,6},{5,7},{6,4},{7,5},{8,10},{9,11},{10,... | collective-permute-start | bytes 1769480 | tf_op jit(solution)/shard_map/ppermute | solution.py:83
  105.6 4.5 %all-to-all-done.1 = bf16[16,32,384]{2,1,0:T(8,128)(2,1)} async-done(((bf16[16,32,384]{2,1,0:T(8,128)(2,1)}), bf16[16,32,384]{2,1,0:T(8,128)(2,1)}, u32[]{:S(2)}, u32[]{:S(2)}) %all-to-all-start.1) | async-done | bytes 393248 | tf_op jit(solution)/shard_map/all_to_all | solution.py:61
  110.1 7.6 %collective-permute-done.6 = bf16[2,2,2,96,384]{4,3,2,1,0:T(8,128)(2,1)} collective-permute-done((bf16[2,2,2,96,384]{4,3,2,1,0:T(8,128)(2,1)}, bf16[2,2,2,96,384]{4,3,2,1,0:T(8,128)(2,1)}, u32[]{:S(2)}, u32[]{:S(2)}) %collective-permute-start.6) | collective-permute-done | bytes 589856 | tf_op jit(solution)/shard_map/ppermute | solution.py:83
  117.7 1.4 fusion.61
  119.1 1.7 %collective-permute-start.7 = (bf16[2,2,96,384]{3,2,1,0:T(8,128)(2,1)S(1)}, bf16[2,2,96,384]{3,2,1,0:T(8,128)(2,1)S(1)}, u32[]{:S(2)}, u32[]{:S(2)}) collective-permute-start(bf16[2,2,96,384]{3,2,1,0:T(8,128)(2,1)S(1)} %dynamic-slice_bitcast_fusion.4), channel_id=1, source_target_pairs={{0,2},{1,3},{2,0},{3,1},{4,6},{5,7},{6,4},{7,5},{8,10},{9,11},{10,... | collective-permute-start | bytes 884744 | tf_op jit(solution)/shard_map/ppermute | solution.py:83
  122.1 1.6 %collective-permute-start.2 = (bf16[2,2,96,384]{3,2,1,0:T(8,128)(2,1)S(1)}, bf16[2,2,96,384]{3,2,1,0:T(8,128)(2,1)S(1)}, u32[]{:S(2)}, u32[]{:S(2)}) collective-permute-start(bf16[2,2,96,384]{3,2,1,0:T(8,128)(2,1)S(1)} %dynamic-slice_bitcast_fusion.5), channel_id=1, source_target_pairs={{0,4},{4,0},{8,12},{12,8},{16,20},{20,16},{24,28},{28,24},{1,5},{5... | collective-permute-start | bytes 884744 | tf_op jit(solution)/shard_map/ppermute | solution.py:83
  123.7 3.9 %collective-permute-done.7 = bf16[2,2,96,384]{3,2,1,0:T(8,128)(2,1)S(1)} collective-permute-done((bf16[2,2,96,384]{3,2,1,0:T(8,128)(2,1)S(1)}, bf16[2,2,96,384]{3,2,1,0:T(8,128)(2,1)S(1)}, u32[]{:S(2)}, u32[]{:S(2)}) %collective-permute-start.7) | collective-permute-done | bytes 294944 | tf_op jit(solution)/shard_map/ppermute | solution.py:83
  127.8 2.6 %collective-permute-done.2 = bf16[2,2,96,384]{3,2,1,0:T(8,128)(2,1)S(1)} collective-permute-done((bf16[2,2,96,384]{3,2,1,0:T(8,128)(2,1)S(1)}, bf16[2,2,96,384]{3,2,1,0:T(8,128)(2,1)S(1)}, u32[]{:S(2)}, u32[]{:S(2)}) %collective-permute-start.2) | collective-permute-done | bytes 294944 | tf_op jit(solution)/shard_map/ppermute | solution.py:83
  130.6 4.5 %collective-permute-done.8 = bf16[2,96,384]{2,1,0:T(8,128)(2,1)S(1)} collective-permute-done((bf16[2,96,384]{2,1,0:T(8,128)(2,1)S(1)}, bf16[2,96,384]{2,1,0:T(8,128)(2,1)S(1)}, u32[]{:S(2)}, u32[]{:S(2)}) %collective-permute-start.8) | collective-permute-done | bytes 147488 | tf_op jit(solution)/shard_map/ppermute | solution.py:83
  137.0 1.7 %collective-permute-start.4 = (bf16[96,384]{1,0:T(8,128)(2,1)S(1)}, bf16[96,384]{1,0:T(8,128)(2,1)S(1)}, u32[]{:S(2)}, u32[]{:S(2)}) collective-permute-start(bf16[96,384]{1,0:T(8,128)(2,1)S(1)} %dynamic-slice_bitcast_fusion.9), channel_id=1, source_target_pairs={{0,16},{4,20},{8,24},{12,28},{16,0},{20,4},{24,8},{28,12},{1,17},{... | collective-permute-start | bytes 221192 | tf_op jit(solution)/shard_map/ppermute | solution.py:83
  138.7 3.4 %collective-permute-done.9 = bf16[96,384]{1,0:T(8,128)(2,1)S(1)} collective-permute-done((bf16[96,384]{1,0:T(8,128)(2,1)S(1)}, bf16[96,384]{1,0:T(8,128)(2,1)S(1)}, u32[]{:S(2)}, u32[]{:S(2)}) %collective-permute-start.9) | collective-permute-done | bytes 73760 | tf_op jit(solution)/shard_map/ppermute | solution.py:83
  143.6 1.8 %copy.17 = bf16[512,384]{1,0:T(8,128)(2,1)} copy(bf16[512,384]{1,0:T(8,128)(2,1)} %bitcast.29) | data formatting | bytes 786432
  (167 shorter events, 32.5 us)
Async XLA Ops:
  0.6 26.6 %copy-start = (bf16[768,1536]{1,0:T(8,128)(2,1)S(1)}, bf16[768,1536]{1,0:T(8,128)(2,1)}, u32[]{:S(2)}) copy-start(bf16[768,1536]{1,0:T(8,128)(2,1)} %param.5) | copy-start | bytes 7077892
  0.6 21.7 %all-to-all-start = ((bf16[16,32,384]{2,1,0:T(8,128)(2,1)}), bf16[16,32,384]{2,1,0:T(8,128)(2,1)S(1)}, u32[]{:S(2)}, u32[]{:S(2)}) async-start(bf16[16,32,384]{2,1,0:T(8,128)(2,1)} %bitcast.243), calls=%async_computation | async-start | bytes 786432 | tf_op jit(solution)/shard_map/all_to_all | solution.py:61
  22.4 19.3 %all-to-all-start.2 = ((bf16[16,32,384]{2,1,0:T(8,128)(2,1)}), bf16[16,32,384]{2,1,0:T(8,128)(2,1)}, u32[]{:S(2)}, u32[]{:S(2)}) async-start(bf16[16,32,384]{2,1,0:T(8,128)(2,1)} %bitcast.244), calls=%async_computation.2 | async-start | bytes 786432 | tf_op jit(solution)/shard_map/all_to_all | solution.py:61
  27.2 2.0 %copy-start.5 = (bf16[256,768]{1,0:T(8,128)(2,1)}, bf16[256,768]{1,0:T(8,128)(2,1)S(1)}, u32[]{:S(2)}) copy-start(bf16[256,768]{1,0:T(8,128)(2,1)S(1)} %fusion.100) | copy-start | bytes 1179652
  27.3 2.0 %copy-start.31 = (bf16[768,1536]{1,0:T(8,128)(2,1)S(1)}, bf16[768,1536]{1,0:T(8,128)(2,1)}, u32[]{:S(2)}) copy-start(bf16[768,1536]{1,0:T(8,128)(2,1)} %param.6) | copy-start | bytes 7077892
  30.8 2.1 %copy-start.7 = (bf16[256,768]{1,0:T(8,128)(2,1)}, bf16[256,768]{1,0:T(8,128)(2,1)S(1)}, u32[]{:S(2)}) copy-start(bf16[256,768]{1,0:T(8,128)(2,1)S(1)} %fusion.70) | copy-start | bytes 1179652
  34.3 2.2 %copy-start.27 = (f32[256]{0:T(256)}, f32[256]{0:T(256)S(1)}, u32[]{:S(2)}) copy-start(f32[256]{0:T(256)S(1)} %add_rsqrt_fusion.1) | copy-start | bytes 3076
  34.5 2.0 %copy-start.9 = (bf16[256,768]{1,0:T(8,128)(2,1)}, bf16[256,768]{1,0:T(8,128)(2,1)S(1)}, u32[]{:S(2)}) copy-start(bf16[256,768]{1,0:T(8,128)(2,1)S(1)} %fusion.75) | copy-start | bytes 1179652
  42.8 3.1 %copy-start.30 = (f32[256]{0:T(256)S(1)}, f32[256]{0:T(256)}, u32[]{:S(2)}) copy-start(f32[256]{0:T(256)} %copy-done.29) | copy-start | bytes 3076
  46.8 1.7 %copy-start.32 = (bf16[768,1536]{1,0:T(8,128)(2,1)S(1)}, bf16[768,1536]{1,0:T(8,128)(2,1)}, u32[]{:S(2)}) copy-start(bf16[768,1536]{1,0:T(8,128)(2,1)} %param.6) | copy-start | bytes 7077892
  47.2 1.9 %copy-start.15 = (f32[256,1536]{1,0:T(8,128)S(1)}, f32[256,1536]{1,0:T(8,128)}, u32[]{:S(2)}) copy-start(f32[256,1536]{1,0:T(8,128)} %get-tuple-element.44) | copy-start | bytes 4718596
  55.0 1.7 %copy-start.20 = (bf16[256,1536]{1,0:T(8,128)(2,1)S(1)}, bf16[256,1536]{1,0:T(8,128)(2,1)}, u32[]{:S(2)}) copy-start(bf16[256,1536]{1,0:T(8,128)(2,1)} %copy-done.19) | copy-start | bytes 2359300
  55.0 2.0 %copy-start.22 = (bf16[256,1536]{1,0:T(8,128)(2,1)S(1)}, bf16[256,1536]{1,0:T(8,128)(2,1)}, u32[]{:S(2)}) copy-start(bf16[256,1536]{1,0:T(8,128)(2,1)} %copy-done.21) | copy-start | bytes 2359300
  66.3 4.9 %copy-start.33 = (bf16[768,1536]{1,0:T(8,128)(2,1)S(1)}, bf16[768,1536]{1,0:T(8,128)(2,1)}, u32[]{:S(2)}) copy-start(bf16[768,1536]{1,0:T(8,128)(2,1)} %param.6) | copy-start | bytes 7077892
  68.4 2.8 %copy-start.13 = (f32[256,1536]{1,0:T(8,128)S(1)}, f32[256,1536]{1,0:T(8,128)}, u32[]{:S(2)}) copy-start(f32[256,1536]{1,0:T(8,128)} %get-tuple-element.40) | copy-start | bytes 4718596
  68.4 2.8 %copy-start.24 = (bf16[1,256,384]{2,1,0:T(8,128)(2,1)S(1)}, bf16[1,256,384]{2,1,0:T(8,128)(2,1)}, u32[]{:S(2)}) copy-start(bf16[1,256,384]{2,1,0:T(8,128)(2,1)} %copy-done.23) | copy-start | bytes 589828
  68.4 2.7 %copy-start.26 = (bf16[1,256,384]{2,1,0:T(8,128)(2,1)S(1)}, bf16[1,256,384]{2,1,0:T(8,128)(2,1)}, u32[]{:S(2)}) copy-start(bf16[1,256,384]{2,1,0:T(8,128)(2,1)} %copy-done.25) | copy-start | bytes 589828
  70.9 25.8 %collective-permute-start.5 = (bf16[2,2,2,2,96,384]{5,4,3,2,1,0:T(8,128)(2,1)}, bf16[2,2,2,2,96,384]{5,4,3,2,1,0:T(8,128)(2,1)}, u32[]{:S(2)}, u32[]{:S(2)}) collective-permute-start(bf16[2,2,2,2,96,384]{5,4,3,2,1,0:T(8,128)(2,1)} %dynamic-slice_bitcast_fusion), channel_id=1, source_target_pairs={{0,1},{1,0},{2,3},{3,2},{4,5},{5,4},{6,7},{7,6},{8,9},{9,8},{10,11... | collective-permute-start | bytes 3538952 | tf_op jit(solution)/shard_map/ppermute | solution.py:83
  71.2 1.8 %copy-start.37 = (bf16[256,1536]{1,0:T(8,128)(2,1)S(1)}, bf16[256,1536]{1,0:T(8,128)(2,1)}, u32[]{:S(2)}) copy-start(bf16[256,1536]{1,0:T(8,128)(2,1)} %copy-done.36) | copy-start | bytes 2359300
  71.2 2.0 %copy-start.39 = (bf16[256,1536]{1,0:T(8,128)(2,1)S(1)}, bf16[256,1536]{1,0:T(8,128)(2,1)}, u32[]{:S(2)}) copy-start(bf16[256,1536]{1,0:T(8,128)(2,1)} %copy-done.38) | copy-start | bytes 2359300
  87.1 14.5 %collective-permute-start = (bf16[2,2,2,2,96,384]{5,4,3,2,1,0:T(8,128)(2,1)}, bf16[2,2,2,2,96,384]{5,4,3,2,1,0:T(8,128)(2,1)}, u32[]{:S(2)}, u32[]{:S(2)}) collective-permute-start(bf16[2,2,2,2,96,384]{5,4,3,2,1,0:T(8,128)(2,1)} %dynamic-slice_bitcast_fusion.1), channel_id=1, source_target_pairs={{0,1},{1,0},{2,3},{3,2},{4,5},{5,4},{6,7},{7,6},{8,9},{9,8},{10,11... | collective-permute-start | bytes 3538952 | tf_op jit(solution)/shard_map/ppermute | solution.py:83
  90.7 19.4 %all-to-all-start.1 = ((bf16[16,32,384]{2,1,0:T(8,128)(2,1)}), bf16[16,32,384]{2,1,0:T(8,128)(2,1)}, u32[]{:S(2)}, u32[]{:S(2)}) async-start(bf16[16,32,384]{2,1,0:T(8,128)(2,1)} %bitcast.28), calls=%async_computation.1 | async-start | bytes 786432 | tf_op jit(solution)/shard_map/all_to_all | solution.py:61
  96.7 5.0 %copy-start.3 = (bf16[8,96,4,384]{3,1,0,2:T(8,128)(2,1)S(1)}, bf16[8,96,4,384]{3,1,0,2:T(8,128)(2,1)}, u32[]{:S(2)}) copy-start(bf16[8,96,4,384]{3,1,0,2:T(8,128)(2,1)} %copy-done.2) | copy-start | bytes 7077892
  98.8 4.4 %copy-start.4 = (bf16[2,2,2,2,96,384]{5,4,3,2,1,0:T(8,128)(2,1)}, bf16[2,2,2,2,96,384]{5,4,3,2,1,0:T(8,128)(2,1)S(1)}, u32[]{:S(2)}) copy-start(bf16[2,2,2,2,96,384]{5,4,3,2,1,0:T(8,128)(2,1)S(1)} %fusion.18) | copy-start | bytes 3538948
  99.8 17.9 %collective-permute-start.6 = (bf16[2,2,2,96,384]{4,3,2,1,0:T(8,128)(2,1)}, bf16[2,2,2,96,384]{4,3,2,1,0:T(8,128)(2,1)}, u32[]{:S(2)}, u32[]{:S(2)}) collective-permute-start(bf16[2,2,2,96,384]{4,3,2,1,0:T(8,128)(2,1)} %dynamic-slice_bitcast_fusion.2), channel_id=1, source_target_pairs={{0,4},{4,0},{8,12},{12,8},{16,20},{20,16},{24,28},{28,24},{1,5},{5... | collective-permute-start | bytes 1769480 | tf_op jit(solution)/shard_map/ppermute | solution.py:83
  104.2 16.7 %collective-permute-start.1 = (bf16[2,2,2,96,384]{4,3,2,1,0:T(8,128)(2,1)}, bf16[2,2,2,96,384]{4,3,2,1,0:T(8,128)(2,1)}, u32[]{:S(2)}, u32[]{:S(2)}) collective-permute-start(bf16[2,2,2,96,384]{4,3,2,1,0:T(8,128)(2,1)} %dynamic-slice_bitcast_fusion.3), channel_id=1, source_target_pairs={{0,2},{1,3},{2,0},{3,1},{4,6},{5,7},{6,4},{7,5},{8,10},{9,11},{10,... | collective-permute-start | bytes 1769480 | tf_op jit(solution)/shard_map/ppermute | solution.py:83
  119.1 8.5 %collective-permute-start.7 = (bf16[2,2,96,384]{3,2,1,0:T(8,128)(2,1)S(1)}, bf16[2,2,96,384]{3,2,1,0:T(8,128)(2,1)S(1)}, u32[]{:S(2)}, u32[]{:S(2)}) collective-permute-start(bf16[2,2,96,384]{3,2,1,0:T(8,128)(2,1)S(1)} %dynamic-slice_bitcast_fusion.4), channel_id=1, source_target_pairs={{0,2},{1,3},{2,0},{3,1},{4,6},{5,7},{6,4},{7,5},{8,10},{9,11},{10,... | collective-permute-start | bytes 884744 | tf_op jit(solution)/shard_map/ppermute | solution.py:83
  122.1 8.3 %collective-permute-start.2 = (bf16[2,2,96,384]{3,2,1,0:T(8,128)(2,1)S(1)}, bf16[2,2,96,384]{3,2,1,0:T(8,128)(2,1)S(1)}, u32[]{:S(2)}, u32[]{:S(2)}) collective-permute-start(bf16[2,2,96,384]{3,2,1,0:T(8,128)(2,1)S(1)} %dynamic-slice_bitcast_fusion.5), channel_id=1, source_target_pairs={{0,4},{4,0},{8,12},{12,8},{16,20},{20,16},{24,28},{28,24},{1,5},{5... | collective-permute-start | bytes 884744 | tf_op jit(solution)/shard_map/ppermute | solution.py:83
  127.8 7.4 %collective-permute-start.8 = (bf16[2,96,384]{2,1,0:T(8,128)(2,1)S(1)}, bf16[2,96,384]{2,1,0:T(8,128)(2,1)S(1)}, u32[]{:S(2)}, u32[]{:S(2)}) collective-permute-start(bf16[2,96,384]{2,1,0:T(8,128)(2,1)S(1)} %dynamic-slice_bitcast_fusion.6), channel_id=1, source_target_pairs={{0,8},{4,12},{8,0},{12,4},{16,24},{20,28},{24,16},{28,20},{1,9},{5... | collective-permute-start | bytes 442376 | tf_op jit(solution)/shard_map/ppermute | solution.py:83
  130.5 6.4 %collective-permute-start.3 = (bf16[2,96,384]{2,1,0:T(8,128)(2,1)S(1)}, bf16[2,96,384]{2,1,0:T(8,128)(2,1)S(1)}, u32[]{:S(2)}, u32[]{:S(2)}) collective-permute-start(bf16[2,96,384]{2,1,0:T(8,128)(2,1)S(1)} %dynamic-slice_bitcast_fusion.7), channel_id=1, source_target_pairs={{0,8},{4,12},{8,0},{12,4},{16,24},{20,28},{24,16},{28,20},{1,9},{5... | collective-permute-start | bytes 442376 | tf_op jit(solution)/shard_map/ppermute | solution.py:83
  135.2 6.9 %collective-permute-start.9 = (bf16[96,384]{1,0:T(8,128)(2,1)S(1)}, bf16[96,384]{1,0:T(8,128)(2,1)S(1)}, u32[]{:S(2)}, u32[]{:S(2)}) collective-permute-start(bf16[96,384]{1,0:T(8,128)(2,1)S(1)} %dynamic-slice_bitcast_fusion.8), channel_id=1, source_target_pairs={{0,16},{4,20},{8,24},{12,28},{16,0},{20,4},{24,8},{28,12},{1,17},{... | collective-permute-start | bytes 221192 | tf_op jit(solution)/shard_map/ppermute | solution.py:83
  137.0 5.9 %collective-permute-start.4 = (bf16[96,384]{1,0:T(8,128)(2,1)S(1)}, bf16[96,384]{1,0:T(8,128)(2,1)S(1)}, u32[]{:S(2)}, u32[]{:S(2)}) collective-permute-start(bf16[96,384]{1,0:T(8,128)(2,1)S(1)} %dynamic-slice_bitcast_fusion.9), channel_id=1, source_target_pairs={{0,16},{4,20},{8,24},{12,28},{16,0},{20,4},{24,8},{28,12},{1,17},{... | collective-permute-start | bytes 221192 | tf_op jit(solution)/shard_map/ppermute | solution.py:83
  (21 other events, 22.5 us)

commit v2 on v1

v2 whole, which is shorter than its diff:
```python
import functools
import math

import jax
import jax.numpy as jnp
from jax import lax
from jax.experimental import pallas as pl
from jax.experimental.pallas import tpu as pltpu
from jax.sharding import PartitionSpec as P

MEMBERS = 16
MASKS = (8, 4, 2, 1)
LANES = 128
CHUNK = 256
VMEM_BYTES = 40 * 1024 * 1024


def section_groups(span_x, span_y):
    bits_x = [span_x.bit_length() - 2, 0]
    bits_y = [span_y.bit_length() - 2, 0]
    mask_x = sum(1 << bit for bit in bits_x)
    mask_y = sum(1 << bit for bit in bits_y)
    groups = []
    for base_x in range(span_x):
        for base_y in range(span_y):
            if base_x & mask_x or base_y & mask_y:
                continue
            group = []
            for member in range(MEMBERS):
                at_x, at_y = base_x, base_y
                at_x |= (member >> 3 & 1) << bits_x[0] | (member >> 2 & 1) << bits_x[1]
                at_y |= (member >> 1 & 1) << bits_y[0] | (member & 1) << bits_y[1]
                group.append(at_x * span_y + at_y)
            groups.append(group)
    return groups


def exchange(block, groups):
    return lax.all_to_all(
        block, ("gx", "gy"), split_axis=0, concat_axis=0, axis_index_groups=groups, tiled=True
    )


def low_members(mask):
    return [member for member in range(MEMBERS) if not member & mask]


def read_pair(ref, mask):
    low = jnp.concatenate([ref[member] for member in low_members(mask)], 0)
    high = jnp.concatenate([ref[member | mask] for member in low_members(mask)], 0)
    return jnp.concatenate([low, high], 1).astype(jnp.float32)


def write_pair(ref, mask, pair):
    rows, width = ref.shape[1:]
    for place, member in enumerate(low_members(mask)):
        part = pair[place * rows : (place + 1) * rows]
        ref[member] = part[:, :width]
        ref[member | mask] = part[:, width:]


def forward_kernel(
    state_ref, up_ref, down_t_ref, out_ref, normed_ref, normed_t_ref, factor_ref, hidden_ref, slope_ref
):
    pairs = MEMBERS // 2 * state_ref.shape[1]
    hidden_units = up_ref.shape[1]
    for section, mask in enumerate(MASKS):
        at = pl.ds(section * pairs, pairs)
        pair = read_pair(state_ref if section == 0 else out_ref, mask)
        centre = jnp.mean(pair, axis=-1, keepdims=True)
        shifted = pair - centre
        spread = jnp.mean(shifted * shifted, axis=-1, keepdims=True)
        factor = lax.rsqrt(spread + 1e-05)
        normed = (shifted * factor).astype(jnp.bfloat16)
        normed_ref[at, :] = normed
        factor_ref[at, :] = jnp.broadcast_to(factor, (pairs, LANES))
        total = pair
        for start in range(0, hidden_units, CHUNK):
            units = pl.ds(start, CHUNK)
            pre = jnp.dot(normed, up_ref[:, units], preferred_element_type=jnp.float32)
            share = 0.5 * (1.0 + lax.erf(pre * (1.0 / math.sqrt(2.0))))
            hidden = (pre * share).astype(jnp.bfloat16)
            hidden_ref[at, units] = hidden
            bell = jnp.exp(-0.5 * pre * pre) * (1.0 / math.sqrt(2.0 * math.pi))
            slope_ref[at, units] = (share + pre * bell).astype(jnp.bfloat16)
            total = total + jnp.dot(hidden, down_t_ref[units, :], preferred_element_type=jnp.float32)
        write_pair(out_ref, mask, total.astype(jnp.bfloat16))
        normed_t_ref[:, at] = normed.T


def backward_kernel(
    grad_ref, normed_ref, factor_ref, slope_ref, down_ref, up_t_ref, grad_t_ref, d_pre_ref, work_ref
):
    pairs = MEMBERS // 2 * grad_ref.shape[1]
    hidden_units = down_ref.shape[1]
    last = len(MASKS) - 1
    for section in range(last, -1, -1):
        mask = MASKS[section]
        at = pl.ds(section * pairs, pairs)
        pair_grad = read_pair(grad_ref if section == last else work_ref, mask)
        pair_bf = pair_grad.astype(jnp.bfloat16)
        d_norm = jnp.zeros(pair_grad.shape, jnp.float32)
        for start in range(0, hidden_units, CHUNK):
            units = pl.ds(start, CHUNK)
            d_hidden = jnp.dot(pair_bf, down_ref[:, units], preferred_element_type=jnp.float32)
            d_pre = (d_hidden * slope_ref[at, units].astype(jnp.float32)).astype(jnp.bfloat16)
            d_pre_ref[at, units] = d_pre
            if section > 0:
                d_norm = d_norm + jnp.dot(d_pre, up_t_ref[units, :], preferred_element_type=jnp.float32)
        if section > 0:
            normed = normed_ref[at, :].astype(jnp.float32)
            d_pair = factor_ref[at, :][:, :1] * (
                d_norm
                - jnp.mean(d_norm, axis=-1, keepdims=True)
                - normed * jnp.mean(d_norm * normed, axis=-1, keepdims=True)
            )
            write_pair(work_ref, mask, (pair_grad + d_pair).astype(jnp.bfloat16))
        grad_t_ref[:, at] = pair_bf.T


def blocks_kernel(places, bit_ref, left_ref, right_ref, out_ref):
    rows, columns = out_ref.shape[1:]
    pieces = []
    for group in range(len(places[0])):
        base = (2 * group + bit_ref[0]) * columns
        for inner in range(0, columns, LANES):
            pieces.append((group, inner, pl.multiple_of(base + inner, LANES)))
    for first in range(0, len(pieces), 2):
        some = pieces[first : first + 2]
        right = jnp.concatenate([right_ref[:, pl.ds(start, LANES)] for _, _, start in some], 1)
        total = jnp.dot(left_ref[...], right, preferred_element_type=jnp.float32)
        total = total.astype(jnp.bfloat16)
        for which, (group, inner, _) in enumerate(some):
            for block in range(len(places)):
                out_ref[places[block][group], :, inner : inner + LANES] = total[
                    block * rows : (block + 1) * rows, which * LANES : (which + 1) * LANES
                ]


def call(kernel, outs, flops, *args, scalars=0, scratch=()):
    size = sum(math.prod(item.shape) * item.dtype.itemsize for item in list(args) + list(outs))
    whole = pl.BlockSpec(memory_space=pltpu.VMEM)
    return pl.pallas_call(
        kernel,
        out_shape=list(outs),
        in_specs=[pl.BlockSpec(memory_space=pltpu.SMEM)] * scalars + [whole] * (len(args) - scalars),
        out_specs=[whole] * len(outs),
        scratch_shapes=list(scratch),
        compiler_params=pltpu.CompilerParams(vmem_limit_bytes=VMEM_BYTES),
        cost_estimate=pl.CostEstimate(flops=flops, bytes_accessed=size, transcendentals=0),
    )(*args)


def forward(state, w_up, down_t):
    _, rows, width = state.shape
    total = len(MASKS) * (MEMBERS // 2) * rows
    depth, units = w_up.shape
    bf16, f32 = jnp.bfloat16, jnp.float32
    outs = [
        jax.ShapeDtypeStruct(state.shape, bf16),
        jax.ShapeDtypeStruct((total, depth), bf16),
        jax.ShapeDtypeStruct((depth, total), bf16),
        jax.ShapeDtypeStruct((total, LANES), f32),
        jax.ShapeDtypeStruct((total, units), bf16),
        jax.ShapeDtypeStruct((total, units), bf16),
    ]
    return call(forward_kernel, outs, 4 * total * depth * units, state, w_up, down_t)


def backward(grad, normed, factor, slope, w_down, up_t):
    total, units = slope.shape
    depth = normed.shape[1]
    outs = [
        jax.ShapeDtypeStruct((depth, total), jnp.bfloat16),
        jax.ShapeDtypeStruct((total, units), jnp.bfloat16),
    ]
    scratch = [pltpu.VMEM(grad.shape, jnp.bfloat16)]
    return call(
        backward_kernel, outs, 4 * total * depth * units, grad, normed, factor, slope, w_down, up_t,
        scratch=scratch,
    )


def gradient_blocks(left, right, bit, order, span_x, span_y):
    rows, columns = left.shape[0] // span_x, right.shape[1] // span_y
    places = []
    for at_x in range(span_x):
        line = []
        for group in range(span_y // 2):
            place = 0
            for axis, step in order:
                at = at_x if axis == "gx" else 2 * group
                place = 2 * place + (at >> step & 1)
            line.append(place)
        places.append(line)
    out = jax.ShapeDtypeStruct((span_x * span_y // 2, rows, columns), jnp.bfloat16)
    flops = left.shape[0] * left.shape[1] * right.shape[1]
    (blocks,) = call(
        functools.partial(blocks_kernel, places), [out], flops,
        bit.reshape(1).astype(jnp.int32), left, right, scalars=1,
    )
    return blocks


def pick(block, at):
    return lax.dynamic_index_in_dim(block, at, 0, keepdims=False).astype(jnp.float32)


def swap(block, axis, bit):
    pairs = [(source, source ^ (1 << bit)) for source in range(lax.axis_size(axis))]
    return lax.ppermute(block, axis, pairs)


def finish_sum(kept, taken, order):
    for axis, bit in order:
        mine = lax.axis_index(axis) // (1 << bit) % 2
        kept = kept.reshape((2, -1) + kept.shape[1:])
        taken = taken.reshape(kept.shape)
        give = (pick(kept, 1 - mine) + pick(taken, 1 - mine)).astype(jnp.bfloat16)
        kept = (pick(kept, mine) + pick(taken, mine)).astype(jnp.bfloat16)
        taken = swap(give, axis, bit)
    return (kept.astype(jnp.float32) + taken.astype(jnp.float32))[0]


def scatter_narrow(left, right, order, span_x, span_y):
    total = jnp.dot(left, right, preferred_element_type=jnp.float32).astype(jnp.bfloat16)
    rows, columns = left.shape[0] // span_x, right.shape[1] // span_y
    count_x, count_y = span_x.bit_length() - 1, span_y.bit_length() - 1
    dims = [("gx", bit) for bit in range(count_x)][::-1] + ["rows"]
    dims += [("gy", bit) for bit in range(count_y)][::-1] + ["columns"]
    blocks = total.reshape((2,) * count_x + (rows,) + (2,) * count_y + (columns,))
    blocks = blocks.transpose([dims.index(item) for item in list(order) + ["rows", "columns"]])
    blocks = blocks.reshape(-1, rows, columns)
    return finish_sum(blocks, jnp.zeros_like(blocks), order)


def local(signal, w_up, w_down, cotangent):
    span_x = lax.axis_size("gx")
    span_y = lax.axis_size("gy")
    groups = section_groups(span_x, span_y)
    rows, width = signal.shape
    state = exchange(signal.reshape(MEMBERS, rows // MEMBERS, width), groups)
    grad = exchange(cotangent.reshape(MEMBERS, rows // MEMBERS, width), groups)
    down_t, up_t = w_down.T, w_up.T
    state, normed, normed_t, factor, hidden, slope = forward(state, w_up, down_t)
    mixed_out = exchange(state, groups).reshape(rows, width)
    grad_t, d_pre = backward(grad, normed, factor, slope, w_down, up_t)

    rest_y = [("gy", bit) for bit in range(1, span_y.bit_length() - 1)]
    rest_x = [("gx", bit) for bit in range(1, span_x.bit_length() - 1)]
    core, across = ("gy", 0), ("gx", 0)
    order_down = [across] + rest_y + rest_x
    order_up = rest_y + [across] + rest_x
    if w_up.shape[1] // span_y % LANES:
        grad_down = scatter_narrow(grad_t, hidden, [core] + order_down, span_x, span_y)
        grad_up = scatter_narrow(normed_t, d_pre, [core] + order_up, span_x, span_y)
        return (mixed_out, grad_up, grad_down)

    mine = lax.axis_index("gy") % 2
    give_down = gradient_blocks(grad_t, hidden, 1 - mine, order_down, span_x, span_y)
    give_up = gradient_blocks(normed_t, d_pre, 1 - mine, order_up, span_x, span_y)
    take_down, take_up = swap(give_down, *core), swap(give_up, *core)
    keep_down = gradient_blocks(grad_t, hidden, mine, order_down, span_x, span_y)
    keep_up = gradient_blocks(normed_t, d_pre, mine, order_up, span_x, span_y)
    grad_down = finish_sum(keep_down, take_down, order_down)
    grad_up = finish_sum(keep_up, take_up, order_up)
    return (mixed_out, grad_up, grad_down)


def solution(mesh):
    return jax.shard_map(
        local,
        mesh=mesh,
        in_specs=(P(("gx", "gy"), None), P(), P(), P(("gx", "gy"), None)),
        out_specs=(P(("gx", "gy"), None), P("gx", "gy"), P("gx", "gy")),
        check_vma=False,
    )
```

time: 146 us -> 126 us (0.86)
  matrix products: 29.9 us -> 0 us
  Pallas kernels: 0 us -> 26.5 us
  blocking collectives: 0 us -> 21.7 us
  waiting for transfers between devices: 42 us -> 24 us
  local copies, waits for them, and re-layouts: 32.2 us -> 24.3 us
  starting transfers between devices: 27.2 us -> 20.6 us
  other arithmetic: 12.5 us -> 7.32 us
    dot_general x17 -> x0, matrix products: 29.9 us -> none  [the longest x4 8.19 us: local(): pre = jnp.dot(normed_bf, w_up, preferred_element_type=jnp.float32)]
    pallas_call x0 -> x6, Pallas kernels: none -> 26.5 us  [call(): pl.pallas_call(kernel, out_shape=list(outs), in_specs=[pl.BlockSpec(memor...]
    all_to_all x0 -> x1, blocking collectives: none -> 21.7 us  [exchange(): lax.all_to_all(block, ('gx', 'gy'), split_axis=0, concat_axis=0, axis_ind...]
    all_to_all x3 -> x2, waiting for transfers between devices: 18.7 us -> 0.01 us  [exchange(): lax.all_to_all(block, ('gx', 'gy'), split_axis=0, concat_axis=0, axis_ind...]
    convert_element_type x4 -> x0, local copies, waits for them, and re-layouts: 14.5 us -> none  [scatter_sum(): blocks.reshape((2,) * len(left) + (rows, columns)).astype(jnp.bfloat16)]
    unnamed x81 -> x37, local copies, waits for them, and re-layouts: 11.7 us -> 24.3 us
    all_to_all x3 -> x2, starting transfers between devices: 17.6 us -> 7.36 us  [exchange(): lax.all_to_all(block, ('gx', 'gy'), split_axis=0, concat_axis=0, axis_ind...]
    squeeze x12 -> x0, local copies, waits for them, and re-layouts: 4.4 us -> none  [the longest x10 4.32 us: halve(): lax.dynamic_index_in_dim(total, 1 - mine, dim, keepdims=False)]
  transfers between devices with their start and end apart: 13 -> 12, of which waited for: 9 -> 7; matrix products, arithmetic and copies ran while one was open for 27% -> 11% of each run, Pallas kernels for 0% -> 11%
where the time goes in v2:
time: 126 us; the launch traced here: 125 us
  Pallas kernels  26.5 us (21%)
  local copies, waits for them, and re-layouts  24.3 us (19%)
  waiting for transfers between devices  24 us (19%)
  blocking collectives  21.7 us (17%)
  starting transfers between devices  20.6 us (16%)
  other arithmetic  7.32 us (6%)
    pallas_call x6, Pallas kernels, call(): pl.pallas_call(kernel, out_shape=list(outs), in_specs=[pl.BlockSpec(memor...  26.5 us
    unnamed x37, local copies, waits for them, and re-layouts  24.3 us
    ppermute x10, waiting for transfers between devices, swap(): return lax.ppermute(block, axis, pairs)  24 us
    all_to_all x1, blocking collectives, exchange(): lax.all_to_all(block, ('gx', 'gy'), split_axis=0, concat_axis=0, axis_ind...  21.7 us
    ppermute x10, starting transfers between devices, swap(): return lax.ppermute(block, axis, pairs)  13.3 us
    all_to_all x2, starting transfers between devices, exchange(): lax.all_to_all(block, ('gx', 'gy'), split_axis=0, concat_axis=0, axis_ind...  7.36 us
    convert_element_type x6, other arithmetic, finish_sum(): kept = (pick(kept, mine) + pick(taken, mine)).astype(jnp.bfloat16)  5.91 us
  transfers between devices with their start and end apart: 12, of which 7 were waited for; matrix products, arithmetic and copies ran while one was open for 11% of the time, Pallas kernels for 11%

profile of v2, /device:TPU:0, one launch (start us, length us, event | category | flops | bytes accessed | tf_op | source)
XLA Modules:
  0.0 125.3 jit_solution(12186698848443056806)
XLA Ops:
  0.6 21.7 %all_to_all.15.state_ref = bf16[16,32,384]{2,1,0:T(8,128)(2,1)} all-to-all(bf16[16,32,384]{2,1,0:T(8,128)(2,1)} %bitcast.58), channel_id=1, replica_groups={{0,1,2,3,4,5,6,7,16,17,18,19,20,21,22,23},{8,9,10,11,12,13,14,15,24,25,..., dimensions={0} | all-to-all | bytes 786432 | tf_op jit(solution)/shard_map/all_to_all | solution.py:39
  22.3 3.6 %all-to-all-start.2 = ((bf16[16,32,384]{2,1,0:T(8,128)(2,1)}), bf16[16,32,384]{2,1,0:T(8,128)(2,1)S(1)}, u32[]{:S(2)}, u32[]{:S(2)}) async-start(bf16[16,32,384]{2,1,0:T(8,128)(2,1)} %bitcast.59), calls=%async_computation.2 | async-start | bytes 786432 | tf_op jit(solution)/shard_map/all_to_all | solution.py:39
  25.9 4.4 %copy.7 = bf16[768,1536]{0,1:T(8,128)(2,1)} copy(bf16[768,1536]{1,0:T(8,128)(2,1)} %down_ref.1) | data formatting | bytes 4718592 | tf_op args[2]
  30.3 2.5 %copy.8 = bf16[768,1536]{0,1:T(8,128)(2,1)} copy(bf16[768,1536]{1,0:T(8,128)(2,1)S(1)} %copy-done.7) | data formatting | bytes 4718592 | tf_op args[1]
  32.8 1.7 %copy-done.8 = bf16[768,1536]{1,0:T(8,128)(2,1)S(1)} copy-done((bf16[768,1536]{1,0:T(8,128)(2,1)S(1)}, bf16[768,1536]{1,0:T(8,128)(2,1)}, u32[]{:S(2)}) %copy-start.8) | copy-done | bytes 2359320
  34.4 1.7 %copy-done.10 = bf16[768,1536]{0,1:T(8,128)(2,1)S(1)} copy-done((bf16[768,1536]{0,1:T(8,128)(2,1)S(1)}, bf16[768,1536]{0,1:T(8,128)(2,1)}, u32[]{:S(2)}) %copy-start.10) | copy-done | bytes 2359320
  37.1 9.1 %shard_map.67 = (bf16[16,32,384]{2,1,0:T(8,128)(2,1)}, bf16[1024,768]{1,0:T(8,128)(2,1)S(1)}, bf16[768,1024]{1,0:T(8,128)(2,1)S(1)}, f32[1024,128]{1,0:T(8,128)S...) custom-call(bf16[16,32,384]{2,1,0:T(8,128)(2,1)S(1)} %copy-done.12, bf16[768,1536]{1,0:T(8,128)(2,1)S(1)} %copy-done.8, ...), custom_call_target="tpu_custom_call" | custom-call | flops 4831838208 | bytes 15466496 | tf_op jit(solution)/shard_map/pallas_call | solution.py:143
  47.4 1.2 copy-done.13
  49.4 1.7 %copy-done.9 = bf16[768,1536]{1,0:T(8,128)(2,1)S(1)} copy-done((bf16[768,1536]{1,0:T(8,128)(2,1)S(1)}, bf16[768,1536]{1,0:T(8,128)(2,1)}, u32[]{:S(2)}) %copy-start.9) | copy-done | bytes 2359320
  51.1 1.7 %copy-done.11 = bf16[768,1536]{0,1:T(8,128)(2,1)S(1)} copy-done((bf16[768,1536]{0,1:T(8,128)(2,1)S(1)}, bf16[768,1536]{0,1:T(8,128)(2,1)}, u32[]{:S(2)}) %copy-start.11) | copy-done | bytes 2359320
  52.7 1.4 %copy-done.14 = bf16[1024,768]{1,0:T(8,128)(2,1)S(1)} copy-done((bf16[1024,768]{1,0:T(8,128)(2,1)S(1)}, bf16[1024,768]{1,0:T(8,128)(2,1)}, u32[]{:S(2)}) %copy-start.14) | copy-done | bytes 1572888
  55.2 9.6 %shard_map.68 = (bf16[768,1024]{1,0:T(8,128)(2,1)S(1)}, bf16[1024,1536]{1,0:T(8,128)(2,1)S(1)}) custom-call(bf16[16,32,384]{2,1,0:T(8,128)(2,1)S(1)} %all-to-all-done.2.grad_ref, bf16[1024,768]{1,0:T(8,128)(2,1)S(1)} %copy-done.14, f32[1024,128]{1,0:T(8,128)S(1)} %copy-done.16, bf16[1024,1536]{1,0:T(8,128)(2,1)} %get-tuple-element.15.slope_ref, ...), custom_call_target="tpu_custom_call" | custom-call | flops 4831838208 | bytes 15073280 | tf_op jit(solution)/shard_map/pallas_call | solution.py:143
  64.8 2.6 %shard_map.70 = bf16[16,96,384]{2,1,0:T(8,128)(2,1)} custom-call(s32[1]{0:T(128)} %bitcast.7.bit_ref, bf16[768,1024]{1,0:T(8,128)(2,1)S(1)} %copy-done.3, bf16[1024,1536]{1,0:T(8,128)(2,1)S(1)} %get-tuple-element.16.right_ref), custom_call_target="tpu_custom_call" | custom-call | flops 1207959552 | bytes 5898244 | tf_op jit(solution)/shard_map/pallas_call | solution.py:143
  67.7 2.4 %shard_map.72 = bf16[16,96,384]{2,1,0:T(8,128)(2,1)} custom-call(s32[1]{0:T(128)} %bitcast.7.bit_ref, bf16[768,1024]{1,0:T(8,128)(2,1)S(1)} %get-tuple-element.17.left_ref, bf16[1024,1536]{1,0:T(8,128)(2,1)S(1)} %get-tuple-element.18.right_ref), custom_call_target="tpu_custom_call" | custom-call | flops 1207959552 | bytes 5898244 | tf_op jit(solution)/shard_map/pallas_call | solution.py:143
  70.4 1.9 %copy-done.1 = bf16[1024,1536]{1,0:T(8,128)(2,1)S(1)} copy-done((bf16[1024,1536]{1,0:T(8,128)(2,1)S(1)}, bf16[1024,1536]{1,0:T(8,128)(2,1)}, u32[]{:S(2)}) %copy-start.1) | copy-done | bytes 3145752
  72.3 1.4 %copy-done.4 = bf16[768,1024]{1,0:T(8,128)(2,1)S(1)} copy-done((bf16[768,1024]{1,0:T(8,128)(2,1)S(1)}, bf16[768,1024]{1,0:T(8,128)(2,1)}, u32[]{:S(2)}) %copy-start.4) | copy-done | bytes 1572888
  73.7 1.4 %shard_map.69 = bf16[16,96,384]{2,1,0:T(8,128)(2,1)S(1)} custom-call(s32[1]{0:T(128)} %bitcast.3.bit_ref, bf16[768,1024]{1,0:T(8,128)(2,1)S(1)} %copy-done.4, bf16[1024,1536]{1,0:T(8,128)(2,1)S(1)} %copy-done.1), custom_call_target="tpu_custom_call" | custom-call | flops 1207959552 | bytes 5898244 | tf_op jit(solution)/shard_map/pallas_call | solution.py:143
  75.1 1.4 %shard_map.71 = bf16[16,96,384]{2,1,0:T(8,128)(2,1)S(1)} custom-call(s32[1]{0:T(128)} %bitcast.3.bit_ref, bf16[768,1024]{1,0:T(8,128)(2,1)S(1)} %copy-done.6, bf16[1024,1536]{1,0:T(8,128)(2,1)S(1)} %get-tuple-element.18.right_ref), custom_call_target="tpu_custom_call" | custom-call | flops 1207959552 | bytes 5898244 | tf_op jit(solution)/shard_map/pallas_call | solution.py:143
  76.6 2.3 %add_convert_fusion.3 = (bf16[1,8,96,384]{3,2,1,0:T(8,128)(2,1)S(1)}, bf16[8,96,384]{2,1,0:T(8,128)(2,1)}) fusion(bf16[2,8,96,384]{3,2,1,0:T(8,128)(2,1)} %bitcast.8, s32[]{:T(128)S(6)} %select_n.101, bf16[2,8,96,384]{3,2,1,0:T(8,128)(2,1)S(1)} %bitcast.48, s32[]{:T(128)S(6)} %select_n.104), kind=kLoop, calls=%fused_computation.3 | loop fusion | flops 2359296 | bytes 3538952 | tf_op jit(solution)/shard_map/convert_element_type | solution.py:220
  78.9 1.8 %collective-permute-start.1 = (bf16[8,96,384]{2,1,0:T(8,128)(2,1)}, bf16[8,96,384]{2,1,0:T(8,128)(2,1)S(1)}, u32[]{:S(2)}, u32[]{:S(2)}) collective-permute-start(bf16[8,96,384]{2,1,0:T(8,128)(2,1)} %get-tuple-element.22), channel_id=1, source_target_pairs={{0,2},{1,3},{2,0},{3,1},{4,6},{5,7},{6,4},{7,5},{8,10},{9,11},{10,... | collective-permute-start | bytes 1769480 | tf_op jit(solution)/shard_map/ppermute | solution.py:211
  80.7 2.4 %add_convert_fusion.1 = (bf16[1,8,96,384]{3,2,1,0:T(8,128)(2,1)S(1)}, bf16[8,96,384]{2,1,0:T(8,128)(2,1)}) fusion(bf16[2,8,96,384]{3,2,1,0:T(8,128)(2,1)} %bitcast.20, s32[]{:T(128)S(6)} %select_n.103, bf16[2,8,96,384]{3,2,1,0:T(8,128)(2,1)S(1)} %bitcast.47, s32[]{:T(128)S(6)} %select_n.108), kind=kLoop, calls=%fused_computation.1 | loop fusion | flops 2359296 | bytes 3538952 | tf_op jit(solution)/shard_map/convert_element_type | solution.py:220
  83.1 1.5 %collective-permute-start.6 = (bf16[8,96,384]{2,1,0:T(8,128)(2,1)}, bf16[8,96,384]{2,1,0:T(8,128)(2,1)S(1)}, u32[]{:S(2)}, u32[]{:S(2)}) collective-permute-start(bf16[8,96,384]{2,1,0:T(8,128)(2,1)} %get-tuple-element.20), channel_id=1, source_target_pairs={{0,4},{4,0},{8,12},{12,8},{16,20},{20,16},{24,28},{28,24},{1,5},{5... | collective-permute-start | bytes 1769480 | tf_op jit(solution)/shard_map/ppermute | solution.py:211
  84.6 3.8 %all-to-all-start.1 = ((bf16[16,32,384]{2,1,0:T(8,128)(2,1)}), bf16[16,32,384]{2,1,0:T(8,128)(2,1)S(1)}, u32[]{:S(2)}, u32[]{:S(2)}) async-start(bf16[16,32,384]{2,1,0:T(8,128)(2,1)} %get-tuple-element.11), calls=%async_computation.1 | async-start | bytes 786432 | tf_op jit(solution)/shard_map/all_to_all | solution.py:39
  88.4 7.0 %collective-permute-done.1 = bf16[8,96,384]{2,1,0:T(8,128)(2,1)S(1)} collective-permute-done((bf16[8,96,384]{2,1,0:T(8,128)(2,1)}, bf16[8,96,384]{2,1,0:T(8,128)(2,1)S(1)}, u32[]{:S(2)}, u32[]{:S(2)}) %collective-permute-start.1) | collective-permute-done | bytes 589856 | tf_op jit(solution)/shard_map/ppermute | solution.py:211
  96.2 1.7 %collective-permute-start.2 = (bf16[4,96,384]{2,1,0:T(8,128)(2,1)}, bf16[4,96,384]{2,1,0:T(8,128)(2,1)S(1)}, u32[]{:S(2)}, u32[]{:S(2)}) collective-permute-start(bf16[4,96,384]{2,1,0:T(8,128)(2,1)} %get-tuple-element.26), channel_id=1, source_target_pairs={{0,4},{4,0},{8,12},{12,8},{16,20},{20,16},{24,28},{28,24},{1,5},{5... | collective-permute-start | bytes 884744 | tf_op jit(solution)/shard_map/ppermute | solution.py:211
  98.0 4.7 %collective-permute-done.6 = bf16[8,96,384]{2,1,0:T(8,128)(2,1)S(1)} collective-permute-done((bf16[8,96,384]{2,1,0:T(8,128)(2,1)}, bf16[8,96,384]{2,1,0:T(8,128)(2,1)S(1)}, u32[]{:S(2)}, u32[]{:S(2)}) %collective-permute-start.6) | collective-permute-done | bytes 589856 | tf_op jit(solution)/shard_map/ppermute | solution.py:211
  103.1 5.8 %collective-permute-done.2 = bf16[4,96,384]{2,1,0:T(8,128)(2,1)S(1)} collective-permute-done((bf16[4,96,384]{2,1,0:T(8,128)(2,1)}, bf16[4,96,384]{2,1,0:T(8,128)(2,1)S(1)}, u32[]{:S(2)}, u32[]{:S(2)}) %collective-permute-start.2) | collective-permute-done | bytes 294944 | tf_op jit(solution)/shard_map/ppermute | solution.py:211
  109.7 1.6 %collective-permute-start.8 = (bf16[2,96,384]{2,1,0:T(8,128)(2,1)S(1)}, bf16[2,96,384]{2,1,0:T(8,128)(2,1)S(1)}, u32[]{:S(2)}, u32[]{:S(2)}) collective-permute-start(bf16[2,96,384]{2,1,0:T(8,128)(2,1)S(1)} %get-tuple-element.28), channel_id=1, source_target_pairs={{0,8},{4,12},{8,0},{12,4},{16,24},{20,28},{24,16},{28,20},{1,9},{5... | collective-permute-start | bytes 442376 | tf_op jit(solution)/shard_map/ppermute | solution.py:211
  111.3 4.2 %collective-permute-done.3 = bf16[2,96,384]{2,1,0:T(8,128)(2,1)S(1)} collective-permute-done((bf16[2,96,384]{2,1,0:T(8,128)(2,1)S(1)}, bf16[2,96,384]{2,1,0:T(8,128)(2,1)S(1)}, u32[]{:S(2)}, u32[]{:S(2)}) %collective-permute-start.3) | collective-permute-done | bytes 147488 | tf_op jit(solution)/shard_map/ppermute | solution.py:211
  115.5 2.9 %collective-permute-start.4 = (bf16[1,96,384]{2,1,0:T(8,128)(2,1)S(1)}, bf16[1,96,384]{2,1,0:T(8,128)(2,1)S(1)}, u32[]{:S(2)}, u32[]{:S(2)}) collective-permute-start(bf16[1,96,384]{2,1,0:T(8,128)(2,1)S(1)} %fusion.8), channel_id=1, source_target_pairs={{0,16},{4,20},{8,24},{12,28},{16,0},{20,4},{24,8},{28,12},{1,17},{... | collective-permute-start | bytes 221192 | tf_op jit(solution)/shard_map/ppermute | solution.py:211
  118.4 2.7 %collective-permute-start.9 = (bf16[1,96,384]{2,1,0:T(8,128)(2,1)S(1)}, bf16[1,96,384]{2,1,0:T(8,128)(2,1)S(1)}, u32[]{:S(2)}, u32[]{:S(2)}) collective-permute-start(bf16[1,96,384]{2,1,0:T(8,128)(2,1)S(1)} %fusion.6), channel_id=1, source_target_pairs={{0,16},{4,20},{8,24},{12,28},{16,0},{20,4},{24,8},{28,12},{1,17},{... | collective-permute-start | bytes 221192 | tf_op jit(solution)/shard_map/ppermute | solution.py:211
  122.5 1.3 %collective-permute-done.9 = bf16[1,96,384]{2,1,0:T(8,128)(2,1)S(1)} collective-permute-done((bf16[1,96,384]{2,1,0:T(8,128)(2,1)S(1)}, bf16[1,96,384]{2,1,0:T(8,128)(2,1)S(1)}, u32[]{:S(2)}, u32[]{:S(2)}) %collective-permute-start.9) | collective-permute-done | bytes 73760 | tf_op jit(solution)/shard_map/ppermute | solution.py:211
  (46 shorter events, 9.5 us)
Async XLA Ops:
  22.3 27.1 %all-to-all-start.2 = ((bf16[16,32,384]{2,1,0:T(8,128)(2,1)}), bf16[16,32,384]{2,1,0:T(8,128)(2,1)S(1)}, u32[]{:S(2)}, u32[]{:S(2)}) async-start(bf16[16,32,384]{2,1,0:T(8,128)(2,1)} %bitcast.59), calls=%async_computation.2 | async-start | bytes 786432 | tf_op jit(solution)/shard_map/all_to_all | solution.py:39
  25.9 4.4 %copy-start.7 = (bf16[768,1536]{1,0:T(8,128)(2,1)S(1)}, bf16[768,1536]{1,0:T(8,128)(2,1)}, u32[]{:S(2)}) copy-start(bf16[768,1536]{1,0:T(8,128)(2,1)} %up_ref.1) | copy-start | bytes 7077892
  32.8 1.7 %copy-start.8 = (bf16[768,1536]{1,0:T(8,128)(2,1)S(1)}, bf16[768,1536]{1,0:T(8,128)(2,1)}, u32[]{:S(2)}) copy-start(bf16[768,1536]{1,0:T(8,128)(2,1)} %up_ref.1) | copy-start | bytes 7077892
  34.4 1.7 %copy-start.10 = (bf16[768,1536]{0,1:T(8,128)(2,1)S(1)}, bf16[768,1536]{0,1:T(8,128)(2,1)}, u32[]{:S(2)}) copy-start(bf16[768,1536]{0,1:T(8,128)(2,1)} %copy.7) | copy-start | bytes 7077892
  36.1 1.0 copy-start.12
  46.2 1.2 copy-start.2
  47.4 1.2 copy-start.13
  48.6 0.8 copy-start.15
  49.4 1.7 %copy-start.9 = (bf16[768,1536]{1,0:T(8,128)(2,1)S(1)}, bf16[768,1536]{1,0:T(8,128)(2,1)}, u32[]{:S(2)}) copy-start(bf16[768,1536]{1,0:T(8,128)(2,1)} %down_ref.1) | copy-start | bytes 7077892
  51.1 1.7 %copy-start.11 = (bf16[768,1536]{0,1:T(8,128)(2,1)S(1)}, bf16[768,1536]{0,1:T(8,128)(2,1)}, u32[]{:S(2)}) copy-start(bf16[768,1536]{0,1:T(8,128)(2,1)} %copy.8) | copy-start | bytes 7077892
  52.7 1.4 %copy-start.14 = (bf16[1024,768]{1,0:T(8,128)(2,1)S(1)}, bf16[1024,768]{1,0:T(8,128)(2,1)}, u32[]{:S(2)}) copy-start(bf16[1024,768]{1,0:T(8,128)(2,1)} %copy-done.13) | copy-start | bytes 4718596
  54.1 1.0 copy-start.16
  55.2 9.6 %copy-start.3 = (bf16[768,1024]{1,0:T(8,128)(2,1)S(1)}, bf16[768,1024]{1,0:T(8,128)(2,1)}, u32[]{:S(2)}) copy-start(bf16[768,1024]{1,0:T(8,128)(2,1)} %copy-done.2) | copy-start | bytes 4718596
  64.8 2.7 %copy-start = (bf16[1024,1536]{1,0:T(8,128)(2,1)}, bf16[1024,1536]{1,0:T(8,128)(2,1)S(1)}, u32[]{:S(2)}) copy-start(bf16[1024,1536]{1,0:T(8,128)(2,1)S(1)} %get-tuple-element.16.right_ref) | copy-start | bytes 9437188
  64.8 2.9 %copy-start.5 = (bf16[768,1024]{1,0:T(8,128)(2,1)}, bf16[768,1024]{1,0:T(8,128)(2,1)S(1)}, u32[]{:S(2)}) copy-start(bf16[768,1024]{1,0:T(8,128)(2,1)S(1)} %get-tuple-element.17.left_ref) | copy-start | bytes 4718596
  67.5 9.1 %collective-permute-start = (bf16[16,96,384]{2,1,0:T(8,128)(2,1)}, bf16[16,96,384]{2,1,0:T(8,128)(2,1)}, u32[]{:S(2)}, u32[]{:S(2)}) collective-permute-start(bf16[16,96,384]{2,1,0:T(8,128)(2,1)} %shard_map.70), channel_id=1, source_target_pairs={{0,1},{1,0},{2,3},{3,2},{4,5},{5,4},{6,7},{7,6},{8,9},{9,8},{10,11... | collective-permute-start | bytes 3538952 | tf_op jit(solution)/shard_map/ppermute | solution.py:211
  70.2 10.5 %collective-permute-start.5 = (bf16[16,96,384]{2,1,0:T(8,128)(2,1)}, bf16[16,96,384]{2,1,0:T(8,128)(2,1)}, u32[]{:S(2)}, u32[]{:S(2)}) collective-permute-start(bf16[16,96,384]{2,1,0:T(8,128)(2,1)} %shard_map.72), channel_id=1, source_target_pairs={{0,1},{1,0},{2,3},{3,2},{4,5},{5,4},{6,7},{7,6},{8,9},{9,8},{10,11... | collective-permute-start | bytes 3538952 | tf_op jit(solution)/shard_map/ppermute | solution.py:211
  70.4 1.9 %copy-start.1 = (bf16[1024,1536]{1,0:T(8,128)(2,1)S(1)}, bf16[1024,1536]{1,0:T(8,128)(2,1)}, u32[]{:S(2)}) copy-start(bf16[1024,1536]{1,0:T(8,128)(2,1)} %copy-done) | copy-start | bytes 9437188
  72.3 1.4 %copy-start.4 = (bf16[768,1024]{1,0:T(8,128)(2,1)S(1)}, bf16[768,1024]{1,0:T(8,128)(2,1)}, u32[]{:S(2)}) copy-start(bf16[768,1024]{1,0:T(8,128)(2,1)} %copy-done.2) | copy-start | bytes 4718596
  73.7 1.4 %copy-start.6 = (bf16[768,1024]{1,0:T(8,128)(2,1)S(1)}, bf16[768,1024]{1,0:T(8,128)(2,1)}, u32[]{:S(2)}) copy-start(bf16[768,1024]{1,0:T(8,128)(2,1)} %copy-done.5) | copy-start | bytes 4718596
  78.9 16.5 %collective-permute-start.1 = (bf16[8,96,384]{2,1,0:T(8,128)(2,1)}, bf16[8,96,384]{2,1,0:T(8,128)(2,1)S(1)}, u32[]{:S(2)}, u32[]{:S(2)}) collective-permute-start(bf16[8,96,384]{2,1,0:T(8,128)(2,1)} %get-tuple-element.22), channel_id=1, source_target_pairs={{0,2},{1,3},{2,0},{3,1},{4,6},{5,7},{6,4},{7,5},{8,10},{9,11},{10,... | collective-permute-start | bytes 1769480 | tf_op jit(solution)/shard_map/ppermute | solution.py:211
  83.1 19.6 %collective-permute-start.6 = (bf16[8,96,384]{2,1,0:T(8,128)(2,1)}, bf16[8,96,384]{2,1,0:T(8,128)(2,1)S(1)}, u32[]{:S(2)}, u32[]{:S(2)}) collective-permute-start(bf16[8,96,384]{2,1,0:T(8,128)(2,1)} %get-tuple-element.20), channel_id=1, source_target_pairs={{0,4},{4,0},{8,12},{12,8},{16,20},{20,16},{24,28},{28,24},{1,5},{5... | collective-permute-start | bytes 1769480 | tf_op jit(solution)/shard_map/ppermute | solution.py:211
  84.6 26.7 %all-to-all-start.1 = ((bf16[16,32,384]{2,1,0:T(8,128)(2,1)}), bf16[16,32,384]{2,1,0:T(8,128)(2,1)S(1)}, u32[]{:S(2)}, u32[]{:S(2)}) async-start(bf16[16,32,384]{2,1,0:T(8,128)(2,1)} %get-tuple-element.11), calls=%async_computation.1 | async-start | bytes 786432 | tf_op jit(solution)/shard_map/all_to_all | solution.py:39
  96.2 12.7 %collective-permute-start.2 = (bf16[4,96,384]{2,1,0:T(8,128)(2,1)}, bf16[4,96,384]{2,1,0:T(8,128)(2,1)S(1)}, u32[]{:S(2)}, u32[]{:S(2)}) collective-permute-start(bf16[4,96,384]{2,1,0:T(8,128)(2,1)} %get-tuple-element.26), channel_id=1, source_target_pairs={{0,4},{4,0},{8,12},{12,8},{16,20},{20,16},{24,28},{28,24},{1,5},{5... | collective-permute-start | bytes 884744 | tf_op jit(solution)/shard_map/ppermute | solution.py:211
  102.8 6.8 %collective-permute-start.7 = (bf16[4,96,384]{2,1,0:T(8,128)(2,1)S(1)}, bf16[4,96,384]{2,1,0:T(8,128)(2,1)S(1)}, u32[]{:S(2)}, u32[]{:S(2)}) collective-permute-start(bf16[4,96,384]{2,1,0:T(8,128)(2,1)S(1)} %get-tuple-element.24), channel_id=1, source_target_pairs={{0,2},{1,3},{2,0},{3,1},{4,6},{5,7},{6,4},{7,5},{8,10},{9,11},{10,... | collective-permute-start | bytes 884744 | tf_op jit(solution)/shard_map/ppermute | solution.py:211
  109.0 6.4 %collective-permute-start.3 = (bf16[2,96,384]{2,1,0:T(8,128)(2,1)S(1)}, bf16[2,96,384]{2,1,0:T(8,128)(2,1)S(1)}, u32[]{:S(2)}, u32[]{:S(2)}) collective-permute-start(bf16[2,96,384]{2,1,0:T(8,128)(2,1)S(1)} %get-tuple-element.30), channel_id=1, source_target_pairs={{0,8},{4,12},{8,0},{12,4},{16,24},{20,28},{24,16},{28,20},{1,9},{5... | collective-permute-start | bytes 442376 | tf_op jit(solution)/shard_map/ppermute | solution.py:211
  109.7 8.7 %collective-permute-start.8 = (bf16[2,96,384]{2,1,0:T(8,128)(2,1)S(1)}, bf16[2,96,384]{2,1,0:T(8,128)(2,1)S(1)}, u32[]{:S(2)}, u32[]{:S(2)}) collective-permute-start(bf16[2,96,384]{2,1,0:T(8,128)(2,1)S(1)} %get-tuple-element.28), channel_id=1, source_target_pairs={{0,8},{4,12},{8,0},{12,4},{16,24},{20,28},{24,16},{28,20},{1,9},{5... | collective-permute-start | bytes 442376 | tf_op jit(solution)/shard_map/ppermute | solution.py:211
  115.5 6.4 %collective-permute-start.4 = (bf16[1,96,384]{2,1,0:T(8,128)(2,1)S(1)}, bf16[1,96,384]{2,1,0:T(8,128)(2,1)S(1)}, u32[]{:S(2)}, u32[]{:S(2)}) collective-permute-start(bf16[1,96,384]{2,1,0:T(8,128)(2,1)S(1)} %fusion.8), channel_id=1, source_target_pairs={{0,16},{4,20},{8,24},{12,28},{16,0},{20,4},{24,8},{28,12},{1,17},{... | collective-permute-start | bytes 221192 | tf_op jit(solution)/shard_map/ppermute | solution.py:211
  118.4 5.4 %collective-permute-start.9 = (bf16[1,96,384]{2,1,0:T(8,128)(2,1)S(1)}, bf16[1,96,384]{2,1,0:T(8,128)(2,1)S(1)}, u32[]{:S(2)}, u32[]{:S(2)}) collective-permute-start(bf16[1,96,384]{2,1,0:T(8,128)(2,1)S(1)} %fusion.6), channel_id=1, source_target_pairs={{0,16},{4,20},{8,24},{12,28},{16,0},{20,4},{24,8},{28,12},{1,17},{... | collective-permute-start | bytes 221192 | tf_op jit(solution)/shard_map/ppermute | solution.py:211

commit v3 on v2

--- a/solution.py
+++ b/solution.py
@@ -12,7 +12,7 @@
 MASKS = (8, 4, 2, 1)
 LANES = 128
 CHUNK = 256
-VMEM_BYTES = 40 * 1024 * 1024
+VMEM_BYTES = 16 * 1024 * 1024
 
 
 def section_groups(span_x, span_y):
@@ -41,13 +41,20 @@
     )
 
 
+def contract_last(left, right):
+    return lax.dot_general(
+        left, right, (((1,), (1,)), ((), ())), preferred_element_type=jnp.float32
+    )
+
+
 def low_members(mask):
     return [member for member in range(MEMBERS) if not member & mask]
 
 
-def read_pair(ref, mask):
-    low = jnp.concatenate([ref[member] for member in low_members(mask)], 0)
-    high = jnp.concatenate([ref[member | mask] for member in low_members(mask)], 0)
+def read_pair(ref, mask, first, rows):
+    at = pl.ds(first, rows)
+    low = jnp.concatenate([ref[member, at] for member in low_members(mask)], 0)
+    high = jnp.concatenate([ref[member | mask, at] for member in low_members(mask)], 0)
     return jnp.concatenate([low, high], 1).astype(jnp.float32)
 
 
@@ -60,13 +67,14 @@
 
 
 def forward_kernel(
-    state_ref, up_ref, down_t_ref, out_ref, normed_ref, normed_t_ref, factor_ref, hidden_ref, slope_ref
+    both_ref, up_ref, down_ref, out_ref, normed_ref, normed_t_ref, factor_ref, hidden_ref, slope_ref
 ):
-    pairs = MEMBERS // 2 * state_ref.shape[1]
+    rows = out_ref.shape[1]
+    pairs = MEMBERS // 2 * rows
     hidden_units = up_ref.shape[1]
     for section, mask in enumerate(MASKS):
         at = pl.ds(section * pairs, pairs)
-        pair = read_pair(state_ref if section == 0 else out_ref, mask)
+        pair = read_pair(both_ref if section == 0 else out_ref, mask, 0, rows)
         centre = jnp.mean(pair, axis=-1, keepdims=True)
         shifted = pair - centre
         spread = jnp.mean(shifted * shifted, axis=-1, keepdims=True)
@@ -74,7 +82,6 @@
         normed = (shifted * factor).astype(jnp.bfloat16)
         normed_ref[at, :] = normed
         factor_ref[at, :] = jnp.broadcast_to(factor, (pairs, LANES))
-        total = pair
         for start in range(0, hidden_units, CHUNK):
             units = pl.ds(start, CHUNK)
             pre = jnp.dot(normed, up_ref[:, units], preferred_element_type=jnp.float32)
@@ -83,31 +90,33 @@
             hidden_ref[at, units] = hidden
             bell = jnp.exp(-0.5 * pre * pre) * (1.0 / math.sqrt(2.0 * math.pi))
             slope_ref[at, units] = (share + pre * bell).astype(jnp.bfloat16)
-            total = total + jnp.dot(hidden, down_t_ref[units, :], preferred_element_type=jnp.float32)
-        write_pair(out_ref, mask, total.astype(jnp.bfloat16))
+        mixed = pair + contract_last(hidden_ref[at, :], down_ref[...])
+        write_pair(out_ref, mask, mixed.astype(jnp.bfloat16))
         normed_t_ref[:, at] = normed.T
 
 
 def backward_kernel(
-    grad_ref, normed_ref, factor_ref, slope_ref, down_ref, up_t_ref, grad_t_ref, d_pre_ref, work_ref
+    both_ref, normed_ref, factor_ref, slope_ref, down_ref, up_ref, grad_t_ref, d_pre_ref, work_ref
 ):
-    pairs = MEMBERS // 2 * grad_ref.shape[1]
+    rows = work_ref.shape[1]
+    pairs = MEMBERS // 2 * rows
     hidden_units = down_ref.shape[1]
     last = len(MASKS) - 1
     for section in range(last, -1, -1):
         mask = MASKS[section]
         at = pl.ds(section * pairs, pairs)
-        pair_grad = read_pair(grad_ref if section == last else work_ref, mask)
+        if section == last:
+            pair_grad = read_pair(both_ref, mask, rows, rows)
+        else:
+            pair_grad = read_pair(work_ref, mask, 0, rows)
         pair_bf = pair_grad.astype(jnp.bfloat16)
-        d_norm = jnp.zeros(pair_grad.shape, jnp.float32)
         for start in range(0, hidden_units, CHUNK):
             units = pl.ds(start, CHUNK)
             d_hidden = jnp.dot(pair_bf, down_ref[:, units], preferred_element_type=jnp.float32)
             d_pre = (d_hidden * slope_ref[at, units].astype(jnp.float32)).astype(jnp.bfloat16)
             d_pre_ref[at, units] = d_pre
-            if section > 0:
-                d_norm = d_norm + jnp.dot(d_pre, up_t_ref[units, :], preferred_element_type=jnp.float32)
         if section > 0:
+            d_norm = contract_last(d_pre_ref[at, :], up_ref[...])
             normed = normed_ref[at, :].astype(jnp.float32)
             d_pair = factor_ref[at, :][:, :1] * (
                 d_norm
@@ -151,32 +160,32 @@
     )(*args)
 
 
-def forward(state, w_up, down_t):
-    _, rows, width = state.shape
+def forward(both, w_up, w_down):
+    rows, width = both.shape[1] // 2, both.shape[2]
     total = len(MASKS) * (MEMBERS // 2) * rows
     depth, units = w_up.shape
     bf16, f32 = jnp.bfloat16, jnp.float32
     outs = [
-        jax.ShapeDtypeStruct(state.shape, bf16),
+        jax.ShapeDtypeStruct((MEMBERS, rows, width), bf16),
         jax.ShapeDtypeStruct((total, depth), bf16),
         jax.ShapeDtypeStruct((depth, total), bf16),
         jax.ShapeDtypeStruct((total, LANES), f32),
         jax.ShapeDtypeStruct((total, units), bf16),
         jax.ShapeDtypeStruct((total, units), bf16),
     ]
-    return call(forward_kernel, outs, 4 * total * depth * units, state, w_up, down_t)
-
-
-def backward(grad, normed, factor, slope, w_down, up_t):
+    return call(forward_kernel, outs, 4 * total * depth * units, both, w_up, w_down)
+
+
+def backward(both, normed, factor, slope, w_down, w_up):
     total, units = slope.shape
     depth = normed.shape[1]
     outs = [
         jax.ShapeDtypeStruct((depth, total), jnp.bfloat16),
         jax.ShapeDtypeStruct((total, units), jnp.bfloat16),
     ]
-    scratch = [pltpu.VMEM(grad.shape, jnp.bfloat16)]
+    scratch = [pltpu.VMEM((MEMBERS, both.shape[1] // 2, both.shape[2]), jnp.bfloat16)]
     return call(
-        backward_kernel, outs, 4 * total * depth * units, grad, normed, factor, slope, w_down, up_t,
+        backward_kernel, outs, 4 * total * depth * units, both, normed, factor, slope, w_down, w_up,
         scratch=scratch,
     )
 
@@ -239,17 +248,17 @@
     span_y = lax.axis_size("gy")
     groups = section_groups(span_x, span_y)
     rows, width = signal.shape
-    state = exchange(signal.reshape(MEMBERS, rows // MEMBERS, width), groups)
-    grad = exchange(cotangent.reshape(MEMBERS, rows // MEMBERS, width), groups)
-    down_t, up_t = w_down.T, w_up.T
-    state, normed, normed_t, factor, hidden, slope = forward(state, w_up, down_t)
+    parts = (MEMBERS, rows // MEMBERS, width)
+    both = jnp.concatenate([signal.reshape(parts), cotangent.reshape(parts)], 1)
+    both = exchange(both, groups)
+    state, normed, normed_t, factor, hidden, slope = forward(both, w_up, w_down)
     mixed_out = exchange(state, groups).reshape(rows, width)
-    grad_t, d_pre = backward(grad, normed, factor, slope, w_down, up_t)
+    grad_t, d_pre = backward(both, normed, factor, slope, w_down, w_up)
 
     rest_y = [("gy", bit) for bit in range(1, span_y.bit_length() - 1)]
     rest_x = [("gx", bit) for bit in range(1, span_x.bit_length() - 1)]
     core, across = ("gy", 0), ("gx", 0)
-    order_down = [across] + rest_y + rest_x
+    order_down = [across] + rest_y + rest_x[::-1]
     order_up = rest_y + [across] + rest_x
     if w_up.shape[1] // span_y % LANES:
         grad_down = scatter_narrow(grad_t, hidden, [core] + order_down, span_x, span_y)

time: 126 us -> 113 us (0.90)
  waiting for transfers between devices: 24 us -> 53.6 us
  blocking collectives: 21.7 us -> 0 us
  local copies, waits for them, and re-layouts: 24.3 us -> 9.42 us
  Pallas kernels: 26.5 us -> 22.4 us
  starting transfers between devices: 20.6 us -> 17.2 us
  other arithmetic: 7.32 us -> 8.72 us
    all_to_all x2, waiting for transfers between devices: 0.01 us -> 22.7 us  [exchange(): lax.all_to_all(block, ('gx', 'gy'), split_axis=0, concat_axis=0, axis_ind...]
    all_to_all x1 -> x0, blocking collectives: 21.7 us -> none  [exchange(): lax.all_to_all(block, ('gx', 'gy'), split_axis=0, concat_axis=0, axis_ind...]
    unnamed x37 -> x21, local copies, waits for them, and re-layouts: 24.3 us -> 9.42 us
    ppermute x10, starting transfers between devices: 13.3 us -> 6.09 us  [swap(): return lax.ppermute(block, axis, pairs)]
    ppermute x10, waiting for transfers between devices: 24 us -> 30.9 us  [swap(): return lax.ppermute(block, axis, pairs)]
    pallas_call x6, Pallas kernels: 26.5 us -> 22.4 us  [call(): pl.pallas_call(kernel, out_shape=list(outs), in_specs=[pl.BlockSpec(memor...]
    all_to_all x2, starting transfers between devices: 7.36 us -> 11.1 us  [exchange(): lax.all_to_all(block, ('gx', 'gy'), split_axis=0, concat_axis=0, axis_ind...]
    concatenate x0 -> x1, other arithmetic: none -> 2.12 us  [local(): both = jnp.concatenate([signal.reshape(parts), cotangent.reshape(parts)], 1)]
  transfers between devices with their start and end apart: 12 -> 12, of which waited for: 7 -> 9; matrix products, arithmetic and copies ran while one was open for 11% -> 5% of each run, Pallas kernels for 11% -> 5%
where the time goes in v3:
time: 113 us; the launch traced here: 112 us
  waiting for transfers between devices  53.6 us (47%)
  Pallas kernels  22.4 us (20%)
  starting transfers between devices  17.2 us (15%)
  local copies, waits for them, and re-layouts  9.42 us (8%)
  other arithmetic  8.72 us (8%)
    ppermute x10, waiting for transfers between devices, swap(): return lax.ppermute(block, axis, pairs)  30.9 us
    all_to_all x2, waiting for transfers between devices, exchange(): lax.all_to_all(block, ('gx', 'gy'), split_axis=0, concat_axis=0, axis_ind...  22.7 us
    pallas_call x6, Pallas kernels, call(): pl.pallas_call(kernel, out_shape=list(outs), in_specs=[pl.BlockSpec(memor...  22.4 us
    all_to_all x2, starting transfers between devices, exchange(): lax.all_to_all(block, ('gx', 'gy'), split_axis=0, concat_axis=0, axis_ind...  11.1 us
    unnamed x21, local copies, waits for them, and re-layouts  9.42 us
    ppermute x10, starting transfers between devices, swap(): return lax.ppermute(block, axis, pairs)  6.09 us
    convert_element_type x6, other arithmetic, finish_sum(): kept = (pick(kept, mine) + pick(taken, mine)).astype(jnp.bfloat16)  5.18 us
  transfers between devices with their start and end apart: 12, of which 9 were waited for; matrix products, arithmetic and copies ran while one was open for 5% of the time, Pallas kernels for 5%

profile of v3, /device:TPU:0, one launch (start us, length us, event | category | flops | bytes accessed | tf_op | source)
XLA Modules:
  0.0 112.1 jit_solution(6207758463422485465)
XLA Ops:
  0.6 2.1 %pad_maximum_fusion = bf16[16,64,384]{2,1,0:T(8,128)(2,1)} fusion(bf16[16,32,384]{2,1,0:T(8,128)(2,1)} %bitcast.54, bf16[16,32,384]{2,1,0:T(8,128)(2,1)} %bitcast.55), kind=kLoop, calls=%fused_computation.4 | loop fusion | flops 1572864 | bytes 1572864 | tf_op jit(solution)/shard_map/concatenate | solution.py:252
  2.8 7.3 %all-to-all-start = ((bf16[16,64,384]{2,1,0:T(8,128)(2,1)}), bf16[16,64,384]{2,1,0:T(8,128)(2,1)S(1)}, u32[]{:S(2)}, u32[]{:S(2)}) async-start(bf16[16,64,384]{2,1,0:T(8,128)(2,1)} %pad_maximum_fusion), calls=%async_computation | async-start | bytes 1572864 | tf_op jit(solution)/shard_map/all_to_all | solution.py:39
  10.1 22.7 %all-to-all-done.both_ref = bf16[16,64,384]{2,1,0:T(8,128)(2,1)S(1)} async-done(((bf16[16,64,384]{2,1,0:T(8,128)(2,1)}), bf16[16,64,384]{2,1,0:T(8,128)(2,1)S(1)}, u32[]{:S(2)}, u32[]{:S(2)}) %all-to-all-start) | async-done | bytes 786464 | tf_op jit(solution)/shard_map/all_to_all | solution.py:39
  32.7 0.9 copy-done.6
  33.6 1.1 %copy-done.7 = bf16[16,64,384]{2,1,0:T(8,128)(2,1)S(1)} copy-done((bf16[16,64,384]{2,1,0:T(8,128)(2,1)S(1)}, bf16[16,64,384]{2,1,0:T(8,128)(2,1)}, u32[]{:S(2)}) %copy-start.7) | copy-done | bytes 786456
  34.8 1.7 %copy-done.8 = bf16[768,1536]{1,0:T(8,128)(2,1)S(1)} copy-done((bf16[768,1536]{1,0:T(8,128)(2,1)S(1)}, bf16[768,1536]{1,0:T(8,128)(2,1)}, u32[]{:S(2)}) %copy-start.8) | copy-done | bytes 2359320
  36.4 1.7 %copy-done.9 = bf16[768,1536]{1,0:T(8,128)(2,1)S(1)} copy-done((bf16[768,1536]{1,0:T(8,128)(2,1)S(1)}, bf16[768,1536]{1,0:T(8,128)(2,1)}, u32[]{:S(2)}) %copy-start.9) | copy-done | bytes 2359320
  38.1 8.5 %shard_map.67 = (bf16[16,32,384]{2,1,0:T(8,128)(2,1)}, bf16[1024,768]{1,0:T(8,128)(2,1)S(1)}, bf16[768,1024]{1,0:T(8,128)(2,1)S(1)}, f32[1024,128]{1,0:T(8,128)S...) custom-call(bf16[16,64,384]{2,1,0:T(8,128)(2,1)S(1)} %copy-done.7, bf16[768,1536]{1,0:T(8,128)(2,1)S(1)} %copy-done.8, ...), custom_call_target="tpu_custom_call" | custom-call | flops 4831838208 | bytes 15859712 | tf_op jit(solution)/shard_map/pallas_call | solution.py:152
  46.6 6.1 %shard_map.68 = (bf16[768,1024]{1,0:T(8,128)(2,1)S(1)}, bf16[1024,1536]{1,0:T(8,128)(2,1)S(1)}) custom-call(bf16[16,64,384]{2,1,0:T(8,128)(2,1)S(1)} %copy-done.7, bf16[1024,768]{1,0:T(8,128)(2,1)S(1)} %get-tuple-element.13.normed_ref, f32[1024,128]{1,0:T(8,128)S(1)} %get-tuple-element.14.factor_ref, bf16[1024,1536]{1,0:T(8,128)(2,1)S(1)} %get-tuple-element.15.slope_ref, ...), custom_call_target="tpu_custom_call" | custom-call | flops 4831838208 | bytes 15466496 | tf_op jit(solution)/shard_map/pallas_call | solution.py:152
  52.7 2.6 %shard_map.70 = bf16[16,96,384]{2,1,0:T(8,128)(2,1)} custom-call(s32[1]{0:T(128)} %bitcast.5.bit_ref, bf16[768,1024]{1,0:T(8,128)(2,1)S(1)} %get-tuple-element.12.left_ref, bf16[1024,1536]{1,0:T(8,128)(2,1)S(1)} %get-tuple-element.16.right_ref), custom_call_target="tpu_custom_call" | custom-call | flops 1207959552 | bytes 5898244 | tf_op jit(solution)/shard_map/pallas_call | solution.py:152
  55.3 2.4 %shard_map.72 = bf16[16,96,384]{2,1,0:T(8,128)(2,1)} custom-call(s32[1]{0:T(128)} %bitcast.5.bit_ref, bf16[768,1024]{1,0:T(8,128)(2,1)S(1)} %get-tuple-element.17.left_ref, bf16[1024,1536]{1,0:T(8,128)(2,1)S(1)} %get-tuple-element.18.right_ref), custom_call_target="tpu_custom_call" | custom-call | flops 1207959552 | bytes 5898244 | tf_op jit(solution)/shard_map/pallas_call | solution.py:152
  57.8 0.5 collective-permute-start.5
  58.3 1.9 %copy-done.1 = bf16[1024,1536]{1,0:T(8,128)(2,1)S(1)} copy-done((bf16[1024,1536]{1,0:T(8,128)(2,1)S(1)}, bf16[1024,1536]{1,0:T(8,128)(2,1)}, u32[]{:S(2)}) %copy-start.1) | copy-done | bytes 3145752
  60.1 1.4 %copy-done.3 = bf16[768,1024]{1,0:T(8,128)(2,1)S(1)} copy-done((bf16[768,1024]{1,0:T(8,128)(2,1)S(1)}, bf16[768,1024]{1,0:T(8,128)(2,1)}, u32[]{:S(2)}) %copy-start.3) | copy-done | bytes 1572888
  61.6 1.4 %shard_map.69 = bf16[16,96,384]{2,1,0:T(8,128)(2,1)S(1)} custom-call(s32[1]{0:T(128)} %bitcast.3.bit_ref, bf16[768,1024]{1,0:T(8,128)(2,1)S(1)} %copy-done.3, bf16[1024,1536]{1,0:T(8,128)(2,1)S(1)} %copy-done.1), custom_call_target="tpu_custom_call" | custom-call | flops 1207959552 | bytes 5898244 | tf_op jit(solution)/shard_map/pallas_call | solution.py:152
  63.0 1.4 %shard_map.71 = bf16[16,96,384]{2,1,0:T(8,128)(2,1)S(1)} custom-call(s32[1]{0:T(128)} %bitcast.3.bit_ref, bf16[768,1024]{1,0:T(8,128)(2,1)S(1)} %copy-done.5, bf16[1024,1536]{1,0:T(8,128)(2,1)S(1)} %get-tuple-element.18.right_ref), custom_call_target="tpu_custom_call" | custom-call | flops 1207959552 | bytes 5898244 | tf_op jit(solution)/shard_map/pallas_call | solution.py:152
  64.4 2.4 %add_convert_fusion.3 = (bf16[1,8,96,384]{3,2,1,0:T(8,128)(2,1)S(1)}, bf16[8,96,384]{2,1,0:T(8,128)(2,1)}) fusion(bf16[2,8,96,384]{3,2,1,0:T(8,128)(2,1)} %bitcast.6, s32[]{:T(128)S(6)} %select_n.101, bf16[2,8,96,384]{3,2,1,0:T(8,128)(2,1)S(1)} %bitcast.46, s32[]{:T(128)S(6)} %select_n.104), kind=kLoop, calls=%fused_computation.3 | loop fusion | flops 2359296 | bytes 3538952 | tf_op jit(solution)/shard_map/convert_element_type | solution.py:229
  66.8 2.4 %add_convert_fusion.1 = (bf16[1,8,96,384]{3,2,1,0:T(8,128)(2,1)S(1)}, bf16[8,96,384]{2,1,0:T(8,128)(2,1)}) fusion(bf16[2,8,96,384]{3,2,1,0:T(8,128)(2,1)} %bitcast.18, s32[]{:T(128)S(6)} %select_n.103, bf16[2,8,96,384]{3,2,1,0:T(8,128)(2,1)S(1)} %bitcast.45, s32[]{:T(128)S(6)} %select_n.108), kind=kLoop, calls=%fused_computation.1 | loop fusion | flops 2359296 | bytes 3538952 | tf_op jit(solution)/shard_map/convert_element_type | solution.py:229
  69.1 1.0 collective-permute-start.6
  70.2 3.8 %all-to-all-start.1 = ((bf16[16,32,384]{2,1,0:T(8,128)(2,1)}), bf16[16,32,384]{2,1,0:T(8,128)(2,1)S(1)}, u32[]{:S(2)}, u32[]{:S(2)}) async-start(bf16[16,32,384]{2,1,0:T(8,128)(2,1)} %get-tuple-element.11), calls=%async_computation.1 | async-start | bytes 786432 | tf_op jit(solution)/shard_map/all_to_all | solution.py:39
  74.0 9.9 %collective-permute-done.1 = bf16[8,96,384]{2,1,0:T(8,128)(2,1)S(1)} collective-permute-done((bf16[8,96,384]{2,1,0:T(8,128)(2,1)}, bf16[8,96,384]{2,1,0:T(8,128)(2,1)S(1)}, u32[]{:S(2)}, u32[]{:S(2)}) %collective-permute-start.1) | collective-permute-done | bytes 589856 | tf_op jit(solution)/shard_map/ppermute | solution.py:220
  84.1 4.6 %collective-permute-done.6 = bf16[8,96,384]{2,1,0:T(8,128)(2,1)S(1)} collective-permute-done((bf16[8,96,384]{2,1,0:T(8,128)(2,1)}, bf16[8,96,384]{2,1,0:T(8,128)(2,1)S(1)}, u32[]{:S(2)}, u32[]{:S(2)}) %collective-permute-start.6) | collective-permute-done | bytes 589856 | tf_op jit(solution)/shard_map/ppermute | solution.py:220
  88.9 2.1 %collective-permute-start.7 = (bf16[4,96,384]{2,1,0:T(8,128)(2,1)S(1)}, bf16[4,96,384]{2,1,0:T(8,128)(2,1)S(1)}, u32[]{:S(2)}, u32[]{:S(2)}) collective-permute-start(bf16[4,96,384]{2,1,0:T(8,128)(2,1)S(1)} %get-tuple-element.24), channel_id=1, source_target_pairs={{0,2},{1,3},{2,0},{3,1},{4,6},{5,7},{6,4},{7,5},{8,10},{9,11},{10,... | collective-permute-start | bytes 884744 | tf_op jit(solution)/shard_map/ppermute | solution.py:220
  91.0 4.1 %collective-permute-done.2 = bf16[4,96,384]{2,1,0:T(8,128)(2,1)S(1)} collective-permute-done((bf16[4,96,384]{2,1,0:T(8,128)(2,1)S(1)}, bf16[4,96,384]{2,1,0:T(8,128)(2,1)S(1)}, u32[]{:S(2)}, u32[]{:S(2)}) %collective-permute-start.2) | collective-permute-done | bytes 294944 | tf_op jit(solution)/shard_map/ppermute | solution.py:220
  95.8 1.7 %collective-permute-start.8 = (bf16[2,96,384]{2,1,0:T(8,128)(2,1)S(1)}, bf16[2,96,384]{2,1,0:T(8,128)(2,1)S(1)}, u32[]{:S(2)}, u32[]{:S(2)}) collective-permute-start(bf16[2,96,384]{2,1,0:T(8,128)(2,1)S(1)} %get-tuple-element.28), channel_id=1, source_target_pairs={{0,16},{4,20},{8,24},{12,28},{16,0},{20,4},{24,8},{28,12},{1,17},{... | collective-permute-start | bytes 442376 | tf_op jit(solution)/shard_map/ppermute | solution.py:220
  97.5 4.5 %collective-permute-done.3 = bf16[2,96,384]{2,1,0:T(8,128)(2,1)S(1)} collective-permute-done((bf16[2,96,384]{2,1,0:T(8,128)(2,1)S(1)}, bf16[2,96,384]{2,1,0:T(8,128)(2,1)S(1)}, u32[]{:S(2)}, u32[]{:S(2)}) %collective-permute-start.3) | collective-permute-done | bytes 147488 | tf_op jit(solution)/shard_map/ppermute | solution.py:220
  102.5 3.7 %collective-permute-done.8 = bf16[2,96,384]{2,1,0:T(8,128)(2,1)S(1)} collective-permute-done((bf16[2,96,384]{2,1,0:T(8,128)(2,1)S(1)}, bf16[2,96,384]{2,1,0:T(8,128)(2,1)S(1)}, u32[]{:S(2)}, u32[]{:S(2)}) %collective-permute-start.8) | collective-permute-done | bytes 147488 | tf_op jit(solution)/shard_map/ppermute | solution.py:220
  106.4 1.5 %collective-permute-done.4 = bf16[1,96,384]{2,1,0:T(8,128)(2,1)S(1)} collective-permute-done((bf16[1,96,384]{2,1,0:T(8,128)(2,1)S(1)}, bf16[1,96,384]{2,1,0:T(8,128)(2,1)S(1)}, u32[]{:S(2)}, u32[]{:S(2)}) %collective-permute-start.4) | collective-permute-done | bytes 73760 | tf_op jit(solution)/shard_map/ppermute | solution.py:220
  107.9 0.7 add_bitcast_fusion.1
  108.5 2.2 %collective-permute-done.9 = bf16[1,96,384]{2,1,0:T(8,128)(2,1)S(1)} collective-permute-done((bf16[1,96,384]{2,1,0:T(8,128)(2,1)S(1)}, bf16[1,96,384]{2,1,0:T(8,128)(2,1)S(1)}, u32[]{:S(2)}, u32[]{:S(2)}) %collective-permute-start.9) | collective-permute-done | bytes 73760 | tf_op jit(solution)/shard_map/ppermute | solution.py:220
  110.7 0.7 add_bitcast_fusion
  111.4 0.7 copy.8
  (30 shorter events, 1.6 us)
Async XLA Ops:
  2.8 30.0 %all-to-all-start = ((bf16[16,64,384]{2,1,0:T(8,128)(2,1)}), bf16[16,64,384]{2,1,0:T(8,128)(2,1)S(1)}, u32[]{:S(2)}, u32[]{:S(2)}) async-start(bf16[16,64,384]{2,1,0:T(8,128)(2,1)} %pad_maximum_fusion), calls=%async_computation | async-start | bytes 1572864 | tf_op jit(solution)/shard_map/all_to_all | solution.py:39
  32.7 0.9 copy-start.6
  33.6 1.1 %copy-start.7 = (bf16[16,64,384]{2,1,0:T(8,128)(2,1)S(1)}, bf16[16,64,384]{2,1,0:T(8,128)(2,1)}, u32[]{:S(2)}) copy-start(bf16[16,64,384]{2,1,0:T(8,128)(2,1)} %copy-done.6) | copy-start | bytes 2359300
  34.8 1.7 %copy-start.8 = (bf16[768,1536]{1,0:T(8,128)(2,1)S(1)}, bf16[768,1536]{1,0:T(8,128)(2,1)}, u32[]{:S(2)}) copy-start(bf16[768,1536]{1,0:T(8,128)(2,1)} %up_ref.3) | copy-start | bytes 7077892
  36.4 1.7 %copy-start.9 = (bf16[768,1536]{1,0:T(8,128)(2,1)S(1)}, bf16[768,1536]{1,0:T(8,128)(2,1)}, u32[]{:S(2)}) copy-start(bf16[768,1536]{1,0:T(8,128)(2,1)} %down_ref.3) | copy-start | bytes 7077892
  46.6 6.1 %copy-start.2 = (bf16[768,1024]{1,0:T(8,128)(2,1)}, bf16[768,1024]{1,0:T(8,128)(2,1)S(1)}, u32[]{:S(2)}) copy-start(bf16[768,1024]{1,0:T(8,128)(2,1)S(1)} %get-tuple-element.12.left_ref) | copy-start | bytes 4718596
  52.7 2.6 %copy-start = (bf16[1024,1536]{1,0:T(8,128)(2,1)}, bf16[1024,1536]{1,0:T(8,128)(2,1)S(1)}, u32[]{:S(2)}) copy-start(bf16[1024,1536]{1,0:T(8,128)(2,1)S(1)} %get-tuple-element.16.right_ref) | copy-start | bytes 9437188
  52.7 2.6 %copy-start.4 = (bf16[768,1024]{1,0:T(8,128)(2,1)}, bf16[768,1024]{1,0:T(8,128)(2,1)S(1)}, u32[]{:S(2)}) copy-start(bf16[768,1024]{1,0:T(8,128)(2,1)S(1)} %get-tuple-element.17.left_ref) | copy-start | bytes 4718596
  55.3 9.0 %collective-permute-start = (bf16[16,96,384]{2,1,0:T(8,128)(2,1)}, bf16[16,96,384]{2,1,0:T(8,128)(2,1)}, u32[]{:S(2)}, u32[]{:S(2)}) collective-permute-start(bf16[16,96,384]{2,1,0:T(8,128)(2,1)} %shard_map.70), channel_id=1, source_target_pairs={{0,1},{1,0},{2,3},{3,2},{4,5},{5,4},{6,7},{7,6},{8,9},{9,8},{10,11... | collective-permute-start | bytes 3538952 | tf_op jit(solution)/shard_map/ppermute | solution.py:220
  57.8 9.0 %collective-permute-start.5 = (bf16[16,96,384]{2,1,0:T(8,128)(2,1)}, bf16[16,96,384]{2,1,0:T(8,128)(2,1)}, u32[]{:S(2)}, u32[]{:S(2)}) collective-permute-start(bf16[16,96,384]{2,1,0:T(8,128)(2,1)} %shard_map.72), channel_id=1, source_target_pairs={{0,1},{1,0},{2,3},{3,2},{4,5},{5,4},{6,7},{7,6},{8,9},{9,8},{10,11... | collective-permute-start | bytes 3538952 | tf_op jit(solution)/shard_map/ppermute | solution.py:220
  58.3 1.9 %copy-start.1 = (bf16[1024,1536]{1,0:T(8,128)(2,1)S(1)}, bf16[1024,1536]{1,0:T(8,128)(2,1)}, u32[]{:S(2)}) copy-start(bf16[1024,1536]{1,0:T(8,128)(2,1)} %copy-done) | copy-start | bytes 9437188
  60.1 1.4 %copy-start.3 = (bf16[768,1024]{1,0:T(8,128)(2,1)S(1)}, bf16[768,1024]{1,0:T(8,128)(2,1)}, u32[]{:S(2)}) copy-start(bf16[768,1024]{1,0:T(8,128)(2,1)} %copy-done.2) | copy-start | bytes 4718596
  61.6 1.4 %copy-start.5 = (bf16[768,1024]{1,0:T(8,128)(2,1)S(1)}, bf16[768,1024]{1,0:T(8,128)(2,1)}, u32[]{:S(2)}) copy-start(bf16[768,1024]{1,0:T(8,128)(2,1)} %copy-done.4) | copy-start | bytes 4718596
  66.8 17.1 %collective-permute-start.1 = (bf16[8,96,384]{2,1,0:T(8,128)(2,1)}, bf16[8,96,384]{2,1,0:T(8,128)(2,1)S(1)}, u32[]{:S(2)}, u32[]{:S(2)}) collective-permute-start(bf16[8,96,384]{2,1,0:T(8,128)(2,1)} %get-tuple-element.22), channel_id=1, source_target_pairs={{0,2},{1,3},{2,0},{3,1},{4,6},{5,7},{6,4},{7,5},{8,10},{9,11},{10,... | collective-permute-start | bytes 1769480 | tf_op jit(solution)/shard_map/ppermute | solution.py:220
  69.1 19.6 %collective-permute-start.6 = (bf16[8,96,384]{2,1,0:T(8,128)(2,1)}, bf16[8,96,384]{2,1,0:T(8,128)(2,1)S(1)}, u32[]{:S(2)}, u32[]{:S(2)}) collective-permute-start(bf16[8,96,384]{2,1,0:T(8,128)(2,1)} %get-tuple-element.20), channel_id=1, source_target_pairs={{0,4},{4,0},{8,12},{12,8},{16,20},{20,16},{24,28},{28,24},{1,5},{5... | collective-permute-start | bytes 1769480 | tf_op jit(solution)/shard_map/ppermute | solution.py:220
  70.2 27.3 %all-to-all-start.1 = ((bf16[16,32,384]{2,1,0:T(8,128)(2,1)}), bf16[16,32,384]{2,1,0:T(8,128)(2,1)S(1)}, u32[]{:S(2)}, u32[]{:S(2)}) async-start(bf16[16,32,384]{2,1,0:T(8,128)(2,1)} %get-tuple-element.11), calls=%async_computation.1 | async-start | bytes 786432 | tf_op jit(solution)/shard_map/all_to_all | solution.py:39
  84.0 11.1 %collective-permute-start.2 = (bf16[4,96,384]{2,1,0:T(8,128)(2,1)S(1)}, bf16[4,96,384]{2,1,0:T(8,128)(2,1)S(1)}, u32[]{:S(2)}, u32[]{:S(2)}) collective-permute-start(bf16[4,96,384]{2,1,0:T(8,128)(2,1)S(1)} %get-tuple-element.26), channel_id=1, source_target_pairs={{0,4},{4,0},{8,12},{12,8},{16,20},{20,16},{24,28},{28,24},{1,5},{5... | collective-permute-start | bytes 884744 | tf_op jit(solution)/shard_map/ppermute | solution.py:220
  88.9 6.8 %collective-permute-start.7 = (bf16[4,96,384]{2,1,0:T(8,128)(2,1)S(1)}, bf16[4,96,384]{2,1,0:T(8,128)(2,1)S(1)}, u32[]{:S(2)}, u32[]{:S(2)}) collective-permute-start(bf16[4,96,384]{2,1,0:T(8,128)(2,1)S(1)} %get-tuple-element.24), channel_id=1, source_target_pairs={{0,2},{1,3},{2,0},{3,1},{4,6},{5,7},{6,4},{7,5},{8,10},{9,11},{10,... | collective-permute-start | bytes 884744 | tf_op jit(solution)/shard_map/ppermute | solution.py:220
  95.2 6.8 %collective-permute-start.3 = (bf16[2,96,384]{2,1,0:T(8,128)(2,1)S(1)}, bf16[2,96,384]{2,1,0:T(8,128)(2,1)S(1)}, u32[]{:S(2)}, u32[]{:S(2)}) collective-permute-start(bf16[2,96,384]{2,1,0:T(8,128)(2,1)S(1)} %get-tuple-element.30), channel_id=1, source_target_pairs={{0,8},{4,12},{8,0},{12,4},{16,24},{20,28},{24,16},{28,20},{1,9},{5... | collective-permute-start | bytes 442376 | tf_op jit(solution)/shard_map/ppermute | solution.py:220
  95.8 10.5 %collective-permute-start.8 = (bf16[2,96,384]{2,1,0:T(8,128)(2,1)S(1)}, bf16[2,96,384]{2,1,0:T(8,128)(2,1)S(1)}, u32[]{:S(2)}, u32[]{:S(2)}) collective-permute-start(bf16[2,96,384]{2,1,0:T(8,128)(2,1)S(1)} %get-tuple-element.28), channel_id=1, source_target_pairs={{0,16},{4,20},{8,24},{12,28},{16,0},{20,4},{24,8},{28,12},{1,17},{... | collective-permute-start | bytes 442376 | tf_op jit(solution)/shard_map/ppermute | solution.py:220
  102.1 5.8 %collective-permute-start.4 = (bf16[1,96,384]{2,1,0:T(8,128)(2,1)S(1)}, bf16[1,96,384]{2,1,0:T(8,128)(2,1)S(1)}, u32[]{:S(2)}, u32[]{:S(2)}) collective-permute-start(bf16[1,96,384]{2,1,0:T(8,128)(2,1)S(1)} %fusion.8), channel_id=1, source_target_pairs={{0,16},{4,20},{8,24},{12,28},{16,0},{20,4},{24,8},{28,12},{1,17},{... | collective-permute-start | bytes 221192 | tf_op jit(solution)/shard_map/ppermute | solution.py:220
  106.3 4.4 %collective-permute-start.9 = (bf16[1,96,384]{2,1,0:T(8,128)(2,1)S(1)}, bf16[1,96,384]{2,1,0:T(8,128)(2,1)S(1)}, u32[]{:S(2)}, u32[]{:S(2)}) collective-permute-start(bf16[1,96,384]{2,1,0:T(8,128)(2,1)S(1)} %fusion.6), channel_id=1, source_target_pairs={{0,8},{4,12},{8,0},{12,4},{16,24},{20,28},{24,16},{28,20},{1,9},{5... | collective-permute-start | bytes 221192 | tf_op jit(solution)/shard_map/ppermute | solution.py:220

commit v4 on v3

v4 whole, which is shorter than its diff:
```python
import functools
import math

import jax
import jax.numpy as jnp
from jax import lax
from jax.experimental import pallas as pl
from jax.experimental.pallas import tpu as pltpu
from jax.sharding import PartitionSpec as P

MEMBERS = 16
MASKS = (8, 4, 2, 1)
LANES = 128
CHUNK = 256
SECTIONS_BYTES = 20 * 1024 * 1024
KEEP_BYTES = 4 * 1024 * 1024


def section_groups(span_x, span_y):
    bits_x = [span_x.bit_length() - 2, 0]
    bits_y = [span_y.bit_length() - 2, 0]
    mask_x = sum(1 << bit for bit in bits_x)
    mask_y = sum(1 << bit for bit in bits_y)
    groups = []
    for base_x in range(span_x):
        for base_y in range(span_y):
            if base_x & mask_x or base_y & mask_y:
                continue
            group = []
            for member in range(MEMBERS):
                at_x, at_y = base_x, base_y
                at_x |= (member >> 3 & 1) << bits_x[0] | (member >> 2 & 1) << bits_x[1]
                at_y |= (member >> 1 & 1) << bits_y[0] | (member & 1) << bits_y[1]
                group.append(at_x * span_y + at_y)
            groups.append(group)
    return groups


def exchange(block, groups):
    return lax.all_to_all(
        block, ("gx", "gy"), split_axis=0, concat_axis=0, axis_index_groups=groups, tiled=True
    )


def contract_last(left, right):
    return lax.dot_general(
        left, right, (((1,), (1,)), ((), ())), preferred_element_type=jnp.float32
    )


def low_members(mask):
    return [member for member in range(MEMBERS) if not member & mask]


def read_pair(ref, mask, first, rows):
    at = pl.ds(first, rows)
    low = jnp.concatenate([ref[member, at] for member in low_members(mask)], 0)
    high = jnp.concatenate([ref[member | mask, at] for member in low_members(mask)], 0)
    return jnp.concatenate([low, high], 1).astype(jnp.float32)


def write_pair(ref, mask, pair, spots=range(MEMBERS), swapped=0):
    rows, width = ref.shape[1:]
    for place, member in enumerate(low_members(mask)):
        part = pair[place * rows : (place + 1) * rows]
        ref[spots[member] ^ swapped] = part[:, :width]
        ref[spots[member | mask] ^ swapped] = part[:, width:]


def write_blocks(places, bit, left_ref, right_ref, out_ref):
    rows, columns = out_ref.shape[1:]
    pieces = []
    for group in range(len(places[0])):
        base = (2 * group + bit) * columns
        for inner in range(0, columns, LANES):
            pieces.append((group, inner, pl.multiple_of(base + inner, LANES)))
    for first in range(0, len(pieces), 2):
        some = pieces[first : first + 2]
        right = jnp.concatenate([right_ref[:, pl.ds(start, LANES)] for _, _, start in some], 1)
        total = jnp.dot(left_ref[...], right, preferred_element_type=jnp.float32)
        total = total.astype(jnp.bfloat16)
        for which, (group, inner, _) in enumerate(some):
            for block in range(len(places)):
                out_ref[places[block][group], :, inner : inner + LANES] = total[
                    block * rows : (block + 1) * rows, which * LANES : (which + 1) * LANES
                ]


def sections_kernel(
    spots, places_down, places_up, place_ref, both_ref, up_hbm, down_hbm,
    out_ref, hidden_ref, d_pre_ref, normed_t_ref, grad_t_ref, *rest
):
    blocks, (up_ref, down_ref, normed_ref, factor_ref, slope_ref, work_ref, arrived) = rest[:-7], rest[-7:]
    fetch_up = pltpu.make_async_copy(up_hbm, up_ref, arrived.at[0])
    fetch_down = pltpu.make_async_copy(down_hbm, down_ref, arrived.at[1])
    fetch_up.start()
    fetch_down.start()
    rows = work_ref.shape[1]
    pairs = MEMBERS // 2 * rows
    hidden_units = up_ref.shape[1]
    last = len(MASKS) - 1

    for section, mask in enumerate(MASKS):
        at = pl.ds(section * pairs, pairs)
        pair = read_pair(both_ref if section == 0 else work_ref, mask, 0, rows)
        centre = jnp.mean(pair, axis=-1, keepdims=True)
        shifted = pair - centre
        spread = jnp.mean(shifted * shifted, axis=-1, keepdims=True)
        factor = lax.rsqrt(spread + 1e-05)
        normed = (shifted * factor).astype(jnp.bfloat16)
        normed_ref[at, :] = normed
        factor_ref[at, :] = jnp.broadcast_to(factor, (pairs, LANES))
        if section == 0:
            fetch_up.wait()
        for start in range(0, hidden_units, CHUNK):
            units = pl.ds(start, CHUNK)
            pre = jnp.dot(normed, up_ref[:, units], preferred_element_type=jnp.float32)
            share = 0.5 * (1.0 + lax.erf(pre * (1.0 / math.sqrt(2.0))))
            hidden_ref[at, units] = (pre * share).astype(jnp.bfloat16)
            bell = jnp.exp(-0.5 * pre * pre) * (1.0 / math.sqrt(2.0 * math.pi))
            slope_ref[at, units] = (share + pre * bell).astype(jnp.bfloat16)
        if section == 0:
            fetch_down.wait()
        mixed = (pair + contract_last(hidden_ref[at, :], down_ref[...])).astype(jnp.bfloat16)
        if section < last:
            write_pair(work_ref, mask, mixed)
        else:
            write_pair(out_ref, mask, mixed, spots, place_ref[2])
        normed_t_ref[:, at] = normed.T

    for section in range(last, -1, -1):
        mask = MASKS[section]
        at = pl.ds(section * pairs, pairs)
        if section == last:
            pair_grad = read_pair(both_ref, mask, rows, rows)
        else:
            pair_grad = read_pair(work_ref, mask, 0, rows)
        pair_bf = pair_grad.astype(jnp.bfloat16)
        for start in range(0, hidden_units, CHUNK):
            units = pl.ds(start, CHUNK)
            d_hidden = jnp.dot(pair_bf, down_ref[:, units], preferred_element_type=jnp.float32)
            d_pre_ref[at, units] = (d_hidden * slope_ref[at, units].astype(jnp.float32)).astype(jnp.bfloat16)
        if section > 0:
            d_norm = contract_last(d_pre_ref[at, :], up_ref[...])
            normed = normed_ref[at, :].astype(jnp.float32)
            d_pair = factor_ref[at, :][:, :1] * (
                d_norm
                - jnp.mean(d_norm, axis=-1, keepdims=True)
                - normed * jnp.mean(d_norm * normed, axis=-1, keepdims=True)
            )
            write_pair(work_ref, mask, (pair_grad + d_pair).astype(jnp.bfloat16))
        grad_t_ref[:, at] = pair_bf.T

    if blocks:
        write_blocks(places_down, place_ref[1], grad_t_ref, hidden_ref, blocks[0])
        write_blocks(places_up, place_ref[1], normed_t_ref, d_pre_ref, blocks[1])


def keep_kernel(
    places_down, places_up, place_ref, hidden_ref, d_pre_ref, normed_t_ref, grad_t_ref, down_ref, up_ref
):
    write_blocks(places_down, 1 - place_ref[1], grad_t_ref, hidden_ref, down_ref)
    write_blocks(places_up, 1 - place_ref[1], normed_t_ref, d_pre_ref, up_ref)


def join_kernel(first_ref, second_ref, out_ref, done):
    rows = first_ref.shape[1]
    copies = [
        pltpu.make_async_copy(ref, out_ref.at[:, pl.ds(place * rows, rows)], done.at[place])
        for place, ref in enumerate((first_ref, second_ref))
    ]
    for copy in copies:
        copy.start()
    for copy in copies:
        copy.wait()


def settle_kernel(sources, place_ref, blocks_ref, out_ref, done):
    rows = blocks_ref.shape[1]
    copies = []
    for index, source in enumerate(sources):
        first = pl.multiple_of((place_ref[0] ^ source) * rows, rows)
        copies.append(pltpu.make_async_copy(blocks_ref.at[index], out_ref.at[pl.ds(first, rows)], done.at[index]))
    for copy in copies:
        copy.start()
    for copy in copies:
        copy.wait()


def spec(space):
    return pl.BlockSpec(memory_space=space)


def join(first, second):
    members, rows, width = first.shape
    out = jax.ShapeDtypeStruct((members, 2 * rows, width), first.dtype)
    return pl.pallas_call(
        join_kernel,
        out_shape=out,
        in_specs=[spec(pltpu.HBM)] * 2,
        out_specs=spec(pltpu.HBM),
        scratch_shapes=[pltpu.SemaphoreType.DMA((2,))],
        cost_estimate=pl.CostEstimate(flops=0, bytes_accessed=4 * out.size, transcendentals=0),
    )(first, second)


def block_places(order, span_x, span_y):
    places = []
    for at_x in range(span_x):
        line = []
        for group in range(span_y // 2):
            place = 0
            for axis, step in order:
                at = at_x if axis == "gx" else 2 * group
                place = 2 * place + (at >> step & 1)
            line.append(place)
        places.append(line)
    return places


def sections(place, both, w_up, w_down, spots, places, block):
    rows, width = both.shape[1] // 2, both.shape[2]
    total = len(MASKS) * (MEMBERS // 2) * rows
    depth, units = w_up.shape
    bf16 = jnp.bfloat16
    outs = [
        jax.ShapeDtypeStruct((MEMBERS, rows, width), bf16),
        jax.ShapeDtypeStruct((total, units), bf16),
        jax.ShapeDtypeStruct((total, units), bf16),
        jax.ShapeDtypeStruct((depth, total), bf16),
        jax.ShapeDtypeStruct((depth, total), bf16),
    ]
    outs += [block] * 2 if block else []
    return pl.pallas_call(
        functools.partial(sections_kernel, spots, *places),
        out_shape=outs,
        in_specs=[spec(pltpu.SMEM), spec(pltpu.VMEM), spec(pltpu.HBM), spec(pltpu.HBM)],
        out_specs=[spec(pltpu.VMEM)] * len(outs),
        scratch_shapes=[
            pltpu.VMEM(w_up.shape, bf16),
            pltpu.VMEM(w_down.shape, bf16),
            pltpu.VMEM((total, depth), bf16),
            pltpu.VMEM((total, LANES), jnp.float32),
            pltpu.VMEM((total, units), bf16),
            pltpu.VMEM((MEMBERS, rows, width), bf16),
            pltpu.SemaphoreType.DMA((2,)),
        ],
        compiler_params=pltpu.CompilerParams(vmem_limit_bytes=SECTIONS_BYTES),
        cost_estimate=pl.CostEstimate(
            flops=10 * total * depth * units, bytes_accessed=16 * total * units, transcendentals=0
        ),
    )(place, both, w_up, w_down)


def keep_blocks(place, hidden, d_pre, normed_t, grad_t, places, block):
    total, units = hidden.shape
    depth = normed_t.shape[0]
    return pl.pallas_call(
        functools.partial(keep_kernel, *places),
        out_shape=[block] * 2,
        in_specs=[spec(pltpu.SMEM)] + [spec(pltpu.VMEM)] * 4,
        out_specs=[spec(pltpu.VMEM)] * 2,
        compiler_params=pltpu.CompilerParams(vmem_limit_bytes=KEEP_BYTES),
        cost_estimate=pl.CostEstimate(
            flops=2 * total * depth * units, bytes_accessed=8 * total * units, transcendentals=0
        ),
    )(place, hidden, d_pre, normed_t, grad_t)


def pick(block, at):
    return lax.dynamic_index_in_dim(block, at, 0, keepdims=False).astype(jnp.float32)


def swap(block, axis, bit):
    pairs = [(source, source ^ (1 << bit)) for source in range(lax.axis_size(axis))]
    return lax.ppermute(block, axis, pairs)


def halve(kept, taken, step):
    axis, bit = step
    mine = lax.axis_index(axis) // (1 << bit) % 2
    kept = kept.reshape((2, -1) + kept.shape[1:])
    taken = taken.reshape(kept.shape)
    give = (pick(kept, 1 - mine) + pick(taken, 1 - mine)).astype(jnp.bfloat16)
    keep = (pick(kept, mine) + pick(taken, mine)).astype(jnp.bfloat16)
    return keep, give


def finish_sum(kept, taken, order, beside=None):
    for phase, step in enumerate(order):
        kept, give = halve(kept, taken, step)
        if beside:
            give = beside(phase, give)
        taken = swap(give, *step)
    return (kept.astype(jnp.float32) + taken.astype(jnp.float32))[0]


def scatter_narrow(left, right, order, span_x, span_y):
    total = jnp.dot(left, right, preferred_element_type=jnp.float32).astype(jnp.bfloat16)
    rows, columns = left.shape[0] // span_x, right.shape[1] // span_y
    count_x, count_y = span_x.bit_length() - 1, span_y.bit_length() - 1
    dims = [("gx", bit) for bit in range(count_x)][::-1] + ["rows"]
    dims += [("gy", bit) for bit in range(count_y)][::-1] + ["columns"]
    blocks = total.reshape((2,) * count_x + (rows,) + (2,) * count_y + (columns,))
    blocks = blocks.transpose([dims.index(item) for item in list(order) + ["rows", "columns"]])
    blocks = blocks.reshape(-1, rows, columns)
    return finish_sum(blocks, jnp.zeros_like(blocks), order)


class Homeward:
    def __init__(self, state, steps):
        self.held = state[None]
        self.steps = list(steps)
        self.order = []

    def advance(self, other):
        if not self.steps:
            return other
        axis, bit, weight = self.steps.pop(0)
        self.order.append(weight)
        half = self.held.shape[1] // 2
        kept, given = self.held[:, :half], self.held[:, half:]
        given, other = lax.optimization_barrier((given, other))
        self.held = jnp.concatenate([kept, swap(given, axis, bit)], 0)
        return other

    def settle(self, place):
        blocks = self.held[:, 0]
        members, rows, width = blocks.shape
        sources = [sum(w for at, w in enumerate(self.order) if index >> at & 1) for index in range(members)]
        return pl.pallas_call(
            functools.partial(settle_kernel, sources),
            out_shape=jax.ShapeDtypeStruct((members * rows, width), blocks.dtype),
            in_specs=[spec(pltpu.SMEM), spec(pltpu.VMEM)],
            out_specs=spec(pltpu.HBM),
            scratch_shapes=[pltpu.SemaphoreType.DMA((members,))],
            cost_estimate=pl.CostEstimate(flops=0, bytes_accessed=4 * blocks.size, transcendentals=0),
        )(place, blocks)


def local(signal, w_up, w_down, cotangent):
    span_x = lax.axis_size("gx")
    span_y = lax.axis_size("gy")
    groups = section_groups(span_x, span_y)
    rows, width = signal.shape
    depth, units = w_up.shape
    steps = [("gx", span_x.bit_length() - 2), ("gx", 0), ("gy", span_y.bit_length() - 2), ("gy", 0)]
    bits = [lax.axis_index(axis) // (1 << bit) % 2 for axis, bit in steps]
    member = sum(bit * mask for bit, mask in zip(bits, MASKS))
    homeward = [0, 3, 2, 1]
    spots = [sum((m // MASKS[at] & 1) * mask for at, mask in zip(homeward, MASKS)) for m in range(MEMBERS)]
    spot = sum(bits[at] * mask for at, mask in zip(homeward, MASKS))
    place = jnp.stack([member, 1 - bits[3], spot]).astype(jnp.int32)

    rest_y = [("gy", bit) for bit in range(1, span_y.bit_length() - 1)]
    rest_x = [("gx", bit) for bit in range(1, span_x.bit_length() - 1)]
    core, across = ("gy", 0), ("gx", 0)
    order_down = [across] + rest_y + rest_x[::-1]
    order_up = rest_y + [across] + rest_x
    places = [block_places(order, span_x, span_y) for order in (order_down, order_up)]
    block = None
    if units // span_y % LANES == 0:
        block = jax.ShapeDtypeStruct(
            (span_x * span_y // 2, depth // span_x, units // span_y), jnp.bfloat16
        )

    parts = (MEMBERS, rows // MEMBERS, width)
    both = exchange(join(signal.reshape(parts), cotangent.reshape(parts)), groups)
    state, hidden, d_pre, normed_t, grad_t, *given = sections(
        place, both, w_up, w_down, spots, places, block
    )
    home = Homeward(state, [steps[at] + (MASKS[at],) for at in homeward])
    if not given:
        while home.steps:
            home.advance(place)
        mixed_out = home.settle(place)
        grad_down = scatter_narrow(grad_t, hidden, [core] + order_down, span_x, span_y)
        grad_up = scatter_narrow(normed_t, d_pre, [core] + order_up, span_x, span_y)
        return (mixed_out, grad_up, grad_down)
    given[0] = home.advance(given[0])
    take_down, take_up = [swap(part, *core) for part in given]
    keep_down, keep_up = keep_blocks(place, hidden, d_pre, normed_t, grad_t, places, block)
    grad_up = finish_sum(keep_up, take_up, order_up)
    beside = lambda phase, give: home.advance(give) if phase > 0 else give
    grad_down = finish_sum(keep_down, take_down, order_down, beside)
    while home.steps:
        home.advance(place)
    return (home.settle(place), grad_up, grad_down)


def solution(mesh):
    return jax.shard_map(
        local,
        mesh=mesh,
        in_specs=(P(("gx", "gy"), None), P(), P(), P(("gx", "gy"), None)),
        out_specs=(P(("gx", "gy"), None), P("gx", "gy"), P("gx", "gy")),
        check_vma=False,
    )
```

time: 113 us -> 140 us (1.24)
  Pallas kernels: 22.4 us -> 48.2 us
  local copies, waits for them, and re-layouts: 9.42 us -> 14.6 us
  other arithmetic: 8.72 us -> 6.01 us
  starting transfers between devices: 17.2 us -> 15.4 us
    pallas_call x6 -> x4, Pallas kernels: 22.4 us -> 48.2 us  [the longest x1 24.9 us: join(): pl.pallas_call(join_kernel, out_shape=out, in_specs=[spec(pltpu.HBM)] * 2...]
    unnamed x21 -> x22, local copies, waits for them, and re-layouts: 9.42 us -> 14.6 us
    all_to_all x2 -> x1, starting transfers between devices: 11.1 us -> 7.31 us  [exchange(): lax.all_to_all(block, ('gx', 'gy'), split_axis=0, concat_axis=0, axis_ind...]
    ppermute x10 -> x14, starting transfers between devices: 6.09 us -> 8.11 us  [swap(): return lax.ppermute(block, axis, pairs)]
    concatenate x1 -> x3, other arithmetic: 2.12 us -> 0.14 us  [advance(): self.held = jnp.concatenate([kept, swap(given, axis, bit)], 0)]
    convert_element_type x8, other arithmetic: 5.22 us -> 3.6 us  [the longest x6 3.56 us: halve(): keep = (pick(kept, mine) + pick(taken, mine)).astype(jnp.bfloat16)]
    ppermute x10 -> x14, waiting for transfers between devices: 30.9 us -> 31.7 us  [swap(): return lax.ppermute(block, axis, pairs)]
    all_to_all x2 -> x1, waiting for transfers between devices: 22.7 us -> 22.5 us  [exchange(): lax.all_to_all(block, ('gx', 'gy'), split_axis=0, concat_axis=0, axis_ind...]
  transfers between devices with their start and end apart: 12 -> 15, of which waited for: 9 -> 10; matrix products, arithmetic and copies ran while one was open for 5% -> 4% of each run, Pallas kernels for 5% -> 2%
where the time goes in v4:
time: 140 us
  waiting for transfers between devices  54.2 us (39%)
  Pallas kernels  48.2 us (34%)
  starting transfers between devices  15.4 us (11%)
  local copies, waits for them, and re-layouts  14.6 us (10%)
  other arithmetic  6.01 us (4%)
    ppermute x14, waiting for transfers between devices, swap(): return lax.ppermute(block, axis, pairs)  31.7 us
    pallas_call x1, Pallas kernels, join(): pl.pallas_call(join_kernel, out_shape=out, in_specs=[spec(pltpu.HBM)] * 2...  24.9 us
    all_to_all x1, waiting for transfers between devices, exchange(): lax.all_to_all(block, ('gx', 'gy'), split_axis=0, concat_axis=0, axis_ind...  22.5 us
    pallas_call x1, Pallas kernels, sections(): pl.pallas_call(functools.partial(sections_kernel, spots, *places), out_sh...  18.3 us
    unnamed x22, local copies, waits for them, and re-layouts  14.6 us
    ppermute x14, starting transfers between devices, swap(): return lax.ppermute(block, axis, pairs)  8.11 us
    all_to_all x1, starting transfers between devices, exchange(): lax.all_to_all(block, ('gx', 'gy'), split_axis=0, concat_axis=0, axis_ind...  7.31 us
    convert_element_type x6, other arithmetic, halve(): keep = (pick(kept, mine) + pick(taken, mine)).astype(jnp.bfloat16)  3.56 us
  transfers between devices with their start and end apart: 15, of which 10 were waited for; matrix products, arithmetic and copies ran while one was open for 4% of the time, Pallas kernels for 2%

profile of v4, /device:TPU:0, one launch (start us, length us, event | category | flops | bytes accessed | tf_op | source)
XLA Modules:
  0.0 139.6 jit_solution(13003005657200300569)
XLA Ops:
  0.6 24.9 %shard_map.67 = bf16[16,64,384]{2,1,0:T(8,128)(2,1)} custom-call(bf16[16,32,384]{2,1,0:T(8,128)(2,1)} %bitcast.57, bf16[16,32,384]{2,1,0:T(8,128)(2,1)} %bitcast.58), custom_call_target="tpu_custom_call" | custom-call | bytes 1572864 | tf_op jit(solution)/shard_map/pallas_call | solution.py:197
  25.6 7.3 %all-to-all-start = ((bf16[16,64,384]{2,1,0:T(8,128)(2,1)}), bf16[16,64,384]{2,1,0:T(8,128)(2,1)S(1)}, u32[]{:S(2)}, u32[]{:S(2)}) async-start(bf16[16,64,384]{2,1,0:T(8,128)(2,1)} %shard_map.67), calls=%async_computation | async-start | bytes 1572864 | tf_op jit(solution)/shard_map/all_to_all | solution.py:40
  33.1 22.5 %all-to-all-done.both_ref = bf16[16,64,384]{2,1,0:T(8,128)(2,1)S(1)} async-done(((bf16[16,64,384]{2,1,0:T(8,128)(2,1)}), bf16[16,64,384]{2,1,0:T(8,128)(2,1)S(1)}, u32[]{:S(2)}, u32[]{:S(2)}) %all-to-all-start) | async-done | bytes 786464 | tf_op jit(solution)/shard_map/all_to_all | solution.py:40
  55.6 0.9 copy-done.6
  56.5 1.1 copy-done.7
  57.6 1.7 %copy-done.9 = bf16[768,1536]{1,0:T(8,128)(2,1)S(1)} copy-done((bf16[768,1536]{1,0:T(8,128)(2,1)S(1)}, bf16[768,1536]{1,0:T(8,128)(2,1)}, u32[]{:S(2)}) %copy-start.9) | copy-done | bytes 2359320
  59.3 1.7 %copy-done.10 = bf16[768,1536]{1,0:T(8,128)(2,1)S(1)} copy-done((bf16[768,1536]{1,0:T(8,128)(2,1)S(1)}, bf16[768,1536]{1,0:T(8,128)(2,1)}, u32[]{:S(2)}) %copy-start.10) | copy-done | bytes 2359320
  60.9 18.3 %shard_map.68 = (bf16[16,32,384]{2,1,0:T(8,128)(2,1)S(1)}, bf16[1024,1536]{1,0:T(8,128)(2,1)S(1)}, bf16[1024,1536]{1,0:T(8,128)(2,1)S(1)}, bf16[768,1024]{1,0:T(...) custom-call(s32[3]{0:T(128)S(1)} %pad_add_fusion.place_ref, ...), custom_call_target="tpu_custom_call" | custom-call | flops 12079595520 | bytes 25165824 | tf_op jit(solution)/shard_map/pallas_call | solution.py:234
  79.2 1.6 %copy-done = bf16[1024,1536]{1,0:T(8,128)(2,1)} copy-done((bf16[1024,1536]{1,0:T(8,128)(2,1)}, bf16[1024,1536]{1,0:T(8,128)(2,1)S(1)}, u32[]{:S(2)}) %copy-start) | copy-done | bytes 3145752
  80.8 1.1 copy-done.2
  82.0 1.2 copy-done.4
  83.8 1.9 %copy-done.1 = bf16[1024,1536]{1,0:T(8,128)(2,1)S(1)} copy-done((bf16[1024,1536]{1,0:T(8,128)(2,1)S(1)}, bf16[1024,1536]{1,0:T(8,128)(2,1)}, u32[]{:S(2)}) %copy-start.1) | copy-done | bytes 3145752
  85.7 1.4 %copy-done.3 = bf16[768,1024]{1,0:T(8,128)(2,1)S(1)} copy-done((bf16[768,1024]{1,0:T(8,128)(2,1)S(1)}, bf16[768,1024]{1,0:T(8,128)(2,1)}, u32[]{:S(2)}) %copy-start.3) | copy-done | bytes 1572888
  87.1 1.4 %copy-done.5 = bf16[768,1024]{1,0:T(8,128)(2,1)S(1)} copy-done((bf16[768,1024]{1,0:T(8,128)(2,1)S(1)}, bf16[768,1024]{1,0:T(8,128)(2,1)}, u32[]{:S(2)}) %copy-start.5) | copy-done | bytes 1572888
  88.5 3.2 %shard_map.69 = (bf16[16,96,384]{2,1,0:T(8,128)(2,1)S(1)}, bf16[16,96,384]{2,1,0:T(8,128)(2,1)S(1)}) custom-call(s32[3]{0:T(128)S(1)} %pad_add_fusion.place_ref, bf16[1024,1536]{1,0:T(8,128)(2,1)S(1)} %get-tuple-element.23.hidden_ref, bf16[1024,1536]{1,0:T(8,128)(2,1)S(1)} %copy-done.1, bf16[768,1024]{1,0:T(8,128)(2,1)S(1)} %copy-done.3, ...), custom_call_target="tpu_custom_call" | custom-call | flops 2415919104 | bytes 12582912 | tf_op jit(solution)/shard_map/pallas_call | solution.py:258
  92.3 1.5 %add_convert_fusion.3 = (bf16[1,8,96,384]{3,2,1,0:T(8,128)(2,1)S(1)}, bf16[8,96,384]{2,1,0:T(8,128)(2,1)S(1)}) fusion(bf16[2,8,96,384]{3,2,1,0:T(8,128)(2,1)} %bitcast.7, s32[]{:T(128)S(6)} %select_n.114, bf16[2,8,96,384]{3,2,1,0:T(8,128)(2,1)S(1)} %bitcast.49, s32[]{:T(128)S(6)} %select_n.116), kind=kLoop, calls=%fused_computation.3 | loop fusion | flops 2359296 | bytes 3538952 | tf_op jit(solution)/shard_map/convert_element_type | solution.py:285
  93.9 1.6 %add_convert_fusion.1 = (bf16[1,8,96,384]{3,2,1,0:T(8,128)(2,1)S(1)}, bf16[8,96,384]{2,1,0:T(8,128)(2,1)S(1)}) fusion(bf16[2,8,96,384]{3,2,1,0:T(8,128)(2,1)} %bitcast.18, s32[]{:T(128)S(6)} %select_n.117, bf16[2,8,96,384]{3,2,1,0:T(8,128)(2,1)S(1)} %bitcast.48, s32[]{:T(128)S(6)} %select_n.115), kind=kLoop, calls=%fused_computation.1 | loop fusion | flops 2359296 | bytes 3538952 | tf_op jit(solution)/shard_map/convert_element_type | solution.py:285
  95.5 1.1 collective-permute-start.9
  96.6 11.1 %collective-permute-done = bf16[1,8,32,384]{3,2,0,1:T(8,128)(2,1)S(1)} collective-permute-done((bf16[1,8,32,384]{3,2,0,1:T(8,128)(2,1)S(1)}, bf16[1,8,32,384]{3,2,0,1:T(8,128)(2,1)S(1)}, u32[]{:S(2)}, u32[]{:S(2)}) %collective-permute-start) | collective-permute-done | bytes 196640 | tf_op jit(solution)/shard_map/ppermute | solution.py:276
  107.7 1.5 %collective-permute-done.2 = bf16[8,96,384]{2,1,0:T(8,128)(2,1)S(1)} collective-permute-done((bf16[8,96,384]{2,1,0:T(8,128)(2,1)S(1)}, bf16[8,96,384]{2,1,0:T(8,128)(2,1)S(1)}, u32[]{:S(2)}, u32[]{:S(2)}) %collective-permute-start.2) | collective-permute-done | bytes 589856 | tf_op jit(solution)/shard_map/ppermute | solution.py:276
  109.4 1.4 %collective-permute-done.9 = bf16[8,96,384]{2,1,0:T(8,128)(2,1)S(1)} collective-permute-done((bf16[8,96,384]{2,1,0:T(8,128)(2,1)S(1)}, bf16[8,96,384]{2,1,0:T(8,128)(2,1)S(1)}, u32[]{:S(2)}, u32[]{:S(2)}) %collective-permute-start.9) | collective-permute-done | bytes 589856 | tf_op jit(solution)/shard_map/ppermute | solution.py:276
  111.0 1.8 %collective-permute-start.10 = (bf16[4,96,384]{2,1,0:T(8,128)(2,1)S(1)}, bf16[4,96,384]{2,1,0:T(8,128)(2,1)S(1)}, u32[]{:S(2)}, u32[]{:S(2)}) collective-permute-start(bf16[4,96,384]{2,1,0:T(8,128)(2,1)S(1)} %get-tuple-element.42), channel_id=1, source_target_pairs={{0,4},{4,0},{8,12},{12,8},{16,20},{20,16},{24,28},{28,24},{1,5},{5... | collective-permute-start | bytes 884744 | tf_op jit(solution)/shard_map/ppermute | solution.py:276
  113.1 6.1 %collective-permute-done.10 = bf16[4,96,384]{2,1,0:T(8,128)(2,1)S(1)} collective-permute-done((bf16[4,96,384]{2,1,0:T(8,128)(2,1)S(1)}, bf16[4,96,384]{2,1,0:T(8,128)(2,1)S(1)}, u32[]{:S(2)}, u32[]{:S(2)}) %collective-permute-start.10) | collective-permute-done | bytes 294944 | tf_op jit(solution)/shard_map/ppermute | solution.py:276
  119.4 1.0 collective-permute-done.4
  120.4 1.1 collective-permute-start.6
  121.5 1.3 collective-permute-start.5
  122.8 2.4 %collective-permute-done.11 = bf16[2,96,384]{2,1,0:T(8,128)(2,1)S(1)} collective-permute-done((bf16[2,96,384]{2,1,0:T(8,128)(2,1)S(1)}, bf16[2,96,384]{2,1,0:T(8,128)(2,1)S(1)}, u32[]{:S(2)}, u32[]{:S(2)}) %collective-permute-start.11) | collective-permute-done | bytes 147488 | tf_op jit(solution)/shard_map/ppermute | solution.py:276
  125.2 0.8 collective-permute-start.12
  126.1 4.8 %collective-permute-done.6 = bf16[2,96,384]{2,1,0:T(8,128)(2,1)S(1)} collective-permute-done((bf16[2,96,384]{2,1,0:T(8,128)(2,1)S(1)}, bf16[2,96,384]{2,1,0:T(8,128)(2,1)S(1)}, u32[]{:S(2)}, u32[]{:S(2)}) %collective-permute-start.6) | collective-permute-done | bytes 147488 | tf_op jit(solution)/shard_map/ppermute | solution.py:276
  131.0 0.8 collective-permute-start.7
  132.5 2.8 %collective-permute-done.13 = bf16[1,96,384]{2,1,0:T(8,128)(2,1)S(1)} collective-permute-done((bf16[1,96,384]{2,1,0:T(8,128)(2,1)S(1)}, bf16[1,96,384]{2,1,0:T(8,128)(2,1)S(1)}, u32[]{:S(2)}, u32[]{:S(2)}) %collective-permute-start.13) | collective-permute-done | bytes 73760 | tf_op jit(solution)/shard_map/ppermute | solution.py:276
  137.6 1.9 %shard_map.70 = bf16[512,384]{1,0:T(8,128)(2,1)} custom-call(s32[3]{0:T(128)} %copy-done.8, bf16[16,32,384]{2,1,0:T(8,128)(2,1)} %maximum_bitcast_fusion.blocks_ref), custom_call_target="tpu_custom_call" | custom-call | bytes 786432 | tf_op jit(solution)/shard_map/pallas_call | solution.py:331
  (40 shorter events, 5.4 us)
Async XLA Ops:
  25.6 30.0 %all-to-all-start = ((bf16[16,64,384]{2,1,0:T(8,128)(2,1)}), bf16[16,64,384]{2,1,0:T(8,128)(2,1)S(1)}, u32[]{:S(2)}, u32[]{:S(2)}) async-start(bf16[16,64,384]{2,1,0:T(8,128)(2,1)} %shard_map.67), calls=%async_computation | async-start | bytes 1572864 | tf_op jit(solution)/shard_map/all_to_all | solution.py:40
  55.6 0.9 copy-start.6
  56.5 1.1 copy-start.7
  57.6 1.7 %copy-start.9 = (bf16[768,1536]{1,0:T(8,128)(2,1)S(1)}, bf16[768,1536]{1,0:T(8,128)(2,1)}, u32[]{:S(2)}) copy-start(bf16[768,1536]{1,0:T(8,128)(2,1)} %up_hbm.1) | copy-start | bytes 7077892
  59.3 1.7 %copy-start.10 = (bf16[768,1536]{1,0:T(8,128)(2,1)S(1)}, bf16[768,1536]{1,0:T(8,128)(2,1)}, u32[]{:S(2)}) copy-start(bf16[768,1536]{1,0:T(8,128)(2,1)} %down_hbm.1) | copy-start | bytes 7077892
  79.2 1.6 %copy-start = (bf16[1024,1536]{1,0:T(8,128)(2,1)}, bf16[1024,1536]{1,0:T(8,128)(2,1)S(1)}, u32[]{:S(2)}) copy-start(bf16[1024,1536]{1,0:T(8,128)(2,1)S(1)} %get-tuple-element.24.d_pre_ref) | copy-start | bytes 9437188
  80.8 1.1 copy-start.2
  82.0 1.2 copy-start.4
  83.2 9.1 %collective-permute-start.1 = (bf16[16,96,384]{2,1,0:T(8,128)(2,1)}, bf16[16,96,384]{2,1,0:T(8,128)(2,1)}, u32[]{:S(2)}, u32[]{:S(2)}) collective-permute-start(bf16[16,96,384]{2,1,0:T(8,128)(2,1)} %get-tuple-element.28), channel_id=1, source_target_pairs={{0,1},{1,0},{2,3},{3,2},{4,5},{5,4},{6,7},{7,6},{8,9},{9,8},{10,11... | collective-permute-start | bytes 3538952 | tf_op jit(solution)/shard_map/ppermute | solution.py:276
  83.3 10.6 %collective-permute-start.8 = (bf16[16,96,384]{2,1,0:T(8,128)(2,1)}, bf16[16,96,384]{2,1,0:T(8,128)(2,1)}, u32[]{:S(2)}, u32[]{:S(2)}) collective-permute-start(bf16[16,96,384]{2,1,0:T(8,128)(2,1)} %get-tuple-element.35), channel_id=1, source_target_pairs={{0,1},{1,0},{2,3},{3,2},{4,5},{5,4},{6,7},{7,6},{8,9},{9,8},{10,11... | collective-permute-start | bytes 3538952 | tf_op jit(solution)/shard_map/ppermute | solution.py:276
  83.8 1.9 %copy-start.1 = (bf16[1024,1536]{1,0:T(8,128)(2,1)S(1)}, bf16[1024,1536]{1,0:T(8,128)(2,1)}, u32[]{:S(2)}) copy-start(bf16[1024,1536]{1,0:T(8,128)(2,1)} %copy-done) | copy-start | bytes 9437188
  85.7 1.4 %copy-start.3 = (bf16[768,1024]{1,0:T(8,128)(2,1)S(1)}, bf16[768,1024]{1,0:T(8,128)(2,1)}, u32[]{:S(2)}) copy-start(bf16[768,1024]{1,0:T(8,128)(2,1)} %copy-done.2) | copy-start | bytes 4718596
  87.1 1.4 %copy-start.5 = (bf16[768,1024]{1,0:T(8,128)(2,1)S(1)}, bf16[768,1024]{1,0:T(8,128)(2,1)}, u32[]{:S(2)}) copy-start(bf16[768,1024]{1,0:T(8,128)(2,1)} %copy-done.4) | copy-start | bytes 4718596
  91.7 0.6 copy-start.8
  93.8 15.4 %collective-permute-start.2 = (bf16[8,96,384]{2,1,0:T(8,128)(2,1)S(1)}, bf16[8,96,384]{2,1,0:T(8,128)(2,1)S(1)}, u32[]{:S(2)}, u32[]{:S(2)}) collective-permute-start(bf16[8,96,384]{2,1,0:T(8,128)(2,1)S(1)} %get-tuple-element.40), channel_id=1, source_target_pairs={{0,4},{4,0},{8,12},{12,8},{16,20},{20,16},{24,28},{28,24},{1,5},{5... | collective-permute-start | bytes 1769480 | tf_op jit(solution)/shard_map/ppermute | solution.py:276
  95.5 15.4 %collective-permute-start.9 = (bf16[8,96,384]{2,1,0:T(8,128)(2,1)S(1)}, bf16[8,96,384]{2,1,0:T(8,128)(2,1)S(1)}, u32[]{:S(2)}, u32[]{:S(2)}) collective-permute-start(bf16[8,96,384]{2,1,0:T(8,128)(2,1)S(1)} %get-tuple-element.38), channel_id=1, source_target_pairs={{0,2},{1,3},{2,0},{3,1},{4,6},{5,7},{6,4},{7,5},{8,10},{9,11},{10,... | collective-permute-start | bytes 1769480 | tf_op jit(solution)/shard_map/ppermute | solution.py:276
  96.6 11.1 %collective-permute-start = (bf16[1,8,32,384]{3,2,0,1:T(8,128)(2,1)S(1)}, bf16[1,8,32,384]{3,2,0,1:T(8,128)(2,1)S(1)}, u32[]{:S(2)}, u32[]{:S(2)}) collective-permute-start(bf16[1,8,32,384]{3,2,0,1:T(8,128)(2,1)S(1)} %get-tuple-element.22), channel_id=1, source_target_pairs={{0,16},{4,20},{8,24},{12,28},{16,0},{20,4},{24,8},{28,12},{1,17},{... | collective-permute-start | bytes 589832 | tf_op jit(solution)/shard_map/ppermute | solution.py:276
  109.4 3.7 %collective-permute-start.3 = (bf16[2,4,32,384]{3,2,0,1:T(8,128)(2,1)S(1)}, bf16[2,4,32,384]{3,2,0,1:T(8,128)(2,1)S(1)}, u32[]{:S(2)}, u32[]{:S(2)}) collective-permute-start(bf16[2,4,32,384]{3,2,0,1:T(8,128)(2,1)S(1)} %get-tuple-element.29), channel_id=1, source_target_pairs={{0,1},{1,0},{2,3},{3,2},{4,5},{5,4},{6,7},{7,6},{8,9},{9,8},{10,11... | collective-permute-start | bytes 589832 | tf_op jit(solution)/shard_map/ppermute | solution.py:276
  111.0 8.2 %collective-permute-start.10 = (bf16[4,96,384]{2,1,0:T(8,128)(2,1)S(1)}, bf16[4,96,384]{2,1,0:T(8,128)(2,1)S(1)}, u32[]{:S(2)}, u32[]{:S(2)}) collective-permute-start(bf16[4,96,384]{2,1,0:T(8,128)(2,1)S(1)} %get-tuple-element.42), channel_id=1, source_target_pairs={{0,4},{4,0},{8,12},{12,8},{16,20},{20,16},{24,28},{28,24},{1,5},{5... | collective-permute-start | bytes 884744 | tf_op jit(solution)/shard_map/ppermute | solution.py:276
  112.8 7.6 %collective-permute-start.4 = (bf16[4,96,384]{2,1,0:T(8,128)(2,1)S(1)}, bf16[4,96,384]{2,1,0:T(8,128)(2,1)S(1)}, u32[]{:S(2)}, u32[]{:S(2)}) collective-permute-start(bf16[4,96,384]{2,1,0:T(8,128)(2,1)S(1)} %get-tuple-element.30), channel_id=1, source_target_pairs={{0,2},{1,3},{2,0},{3,1},{4,6},{5,7},{6,4},{7,5},{8,10},{9,11},{10,... | collective-permute-start | bytes 884744 | tf_op jit(solution)/shard_map/ppermute | solution.py:276
  119.3 5.9 %collective-permute-start.11 = (bf16[2,96,384]{2,1,0:T(8,128)(2,1)S(1)}, bf16[2,96,384]{2,1,0:T(8,128)(2,1)S(1)}, u32[]{:S(2)}, u32[]{:S(2)}) collective-permute-start(bf16[2,96,384]{2,1,0:T(8,128)(2,1)S(1)} %get-tuple-element.46), channel_id=1, source_target_pairs={{0,8},{4,12},{8,0},{12,4},{16,24},{20,28},{24,16},{28,20},{1,9},{5... | collective-permute-start | bytes 442376 | tf_op jit(solution)/shard_map/ppermute | solution.py:276
  120.4 10.4 %collective-permute-start.6 = (bf16[2,96,384]{2,1,0:T(8,128)(2,1)S(1)}, bf16[2,96,384]{2,1,0:T(8,128)(2,1)S(1)}, u32[]{:S(2)}, u32[]{:S(2)}) collective-permute-start(bf16[2,96,384]{2,1,0:T(8,128)(2,1)S(1)} %get-tuple-element.32), channel_id=1, source_target_pairs={{0,16},{4,20},{8,24},{12,28},{16,0},{20,4},{24,8},{28,12},{1,17},{... | collective-permute-start | bytes 442376 | tf_op jit(solution)/shard_map/ppermute | solution.py:276
  121.5 9.3 %collective-permute-start.5 = (bf16[4,2,32,384]{3,2,0,1:T(8,128)(2,1)S(1)}, bf16[4,2,32,384]{3,2,0,1:T(8,128)(2,1)S(1)}, u32[]{:S(2)}, u32[]{:S(2)}) collective-permute-start(bf16[4,2,32,384]{3,2,0,1:T(8,128)(2,1)S(1)} %get-tuple-element.31), channel_id=1, source_target_pairs={{0,2},{1,3},{2,0},{3,1},{4,6},{5,7},{6,4},{7,5},{8,10},{9,11},{10,... | collective-permute-start | bytes 589832 | tf_op jit(solution)/shard_map/ppermute | solution.py:276
  125.2 6.6 %collective-permute-start.12 = (bf16[1,96,384]{2,1,0:T(8,128)(2,1)S(1)}, bf16[1,96,384]{2,1,0:T(8,128)(2,1)S(1)}, u32[]{:S(2)}, u32[]{:S(2)}) collective-permute-start(bf16[1,96,384]{2,1,0:T(8,128)(2,1)S(1)} %fusion.10), channel_id=1, source_target_pairs={{0,16},{4,20},{8,24},{12,28},{16,0},{20,4},{24,8},{28,12},{1,17},{... | collective-permute-start | bytes 221192 | tf_op jit(solution)/shard_map/ppermute | solution.py:276
  130.9 4.4 %collective-permute-start.13 = (bf16[1,96,384]{2,1,0:T(8,128)(2,1)S(1)}, bf16[1,96,384]{2,1,0:T(8,128)(2,1)S(1)}, u32[]{:S(2)}, u32[]{:S(2)}) collective-permute-start(bf16[1,96,384]{2,1,0:T(8,128)(2,1)S(1)} %fusion.12), channel_id=1, source_target_pairs={{0,8},{4,12},{8,0},{12,4},{16,24},{20,28},{24,16},{28,20},{1,9},{5... | collective-permute-start | bytes 221192 | tf_op jit(solution)/shard_map/ppermute | solution.py:276
  131.0 5.7 %collective-permute-start.7 = (bf16[8,1,32,384]{3,2,0,1:T(8,128)(2,1)S(1)}, bf16[8,1,32,384]{3,2,0,1:T(8,128)(2,1)S(1)}, u32[]{:S(2)}, u32[]{:S(2)}) collective-permute-start(bf16[8,1,32,384]{3,2,0,1:T(8,128)(2,1)S(1)} %get-tuple-element.33), channel_id=1, source_target_pairs={{0,4},{4,0},{8,12},{12,8},{16,20},{20,16},{24,28},{28,24},{1,5},{5... | collective-permute-start | bytes 589832 | tf_op jit(solution)/shard_map/ppermute | solution.py:276

commit v5 on v4

--- a/solution.py
+++ b/solution.py
@@ -87,14 +87,18 @@
 
 
 def sections_kernel(
-    spots, places_down, places_up, place_ref, both_ref, up_hbm, down_hbm,
+    spots, places_down, places_up, place_ref, both_hbm, up_hbm, down_hbm,
     out_ref, hidden_ref, d_pre_ref, normed_t_ref, grad_t_ref, *rest
 ):
-    blocks, (up_ref, down_ref, normed_ref, factor_ref, slope_ref, work_ref, arrived) = rest[:-7], rest[-7:]
-    fetch_up = pltpu.make_async_copy(up_hbm, up_ref, arrived.at[0])
-    fetch_down = pltpu.make_async_copy(down_hbm, down_ref, arrived.at[1])
+    blocks = rest[:-8]
+    both_ref, up_ref, down_ref, normed_ref, factor_ref, slope_ref, work_ref, arrived = rest[-8:]
+    fetch_both = pltpu.make_async_copy(both_hbm, both_ref, arrived.at[0])
+    fetch_up = pltpu.make_async_copy(up_hbm, up_ref, arrived.at[1])
+    fetch_down = pltpu.make_async_copy(down_hbm, down_ref, arrived.at[2])
+    fetch_both.start()
     fetch_up.start()
     fetch_down.start()
+    fetch_both.wait()
     rows = work_ref.shape[1]
     pairs = MEMBERS // 2 * rows
     hidden_units = up_ref.shape[1]
@@ -163,18 +167,6 @@
     write_blocks(places_up, 1 - place_ref[1], normed_t_ref, d_pre_ref, up_ref)
 
 
-def join_kernel(first_ref, second_ref, out_ref, done):
-    rows = first_ref.shape[1]
-    copies = [
-        pltpu.make_async_copy(ref, out_ref.at[:, pl.ds(place * rows, rows)], done.at[place])
-        for place, ref in enumerate((first_ref, second_ref))
-    ]
-    for copy in copies:
-        copy.start()
-    for copy in copies:
-        copy.wait()
-
-
 def settle_kernel(sources, place_ref, blocks_ref, out_ref, done):
     rows = blocks_ref.shape[1]
     copies = []
@@ -189,19 +181,6 @@
 
 def spec(space):
     return pl.BlockSpec(memory_space=space)
-
-
-def join(first, second):
-    members, rows, width = first.shape
-    out = jax.ShapeDtypeStruct((members, 2 * rows, width), first.dtype)
-    return pl.pallas_call(
-        join_kernel,
-        out_shape=out,
-        in_specs=[spec(pltpu.HBM)] * 2,
-        out_specs=spec(pltpu.HBM),
-        scratch_shapes=[pltpu.SemaphoreType.DMA((2,))],
-        cost_estimate=pl.CostEstimate(flops=0, bytes_accessed=4 * out.size, transcendentals=0),
-    )(first, second)
 
 
 def block_places(order, span_x, span_y):
@@ -224,32 +203,33 @@
     depth, units = w_up.shape
     bf16 = jnp.bfloat16
     outs = [
-        jax.ShapeDtypeStruct((MEMBERS, rows, width), bf16),
-        jax.ShapeDtypeStruct((total, units), bf16),
-        jax.ShapeDtypeStruct((total, units), bf16),
-        jax.ShapeDtypeStruct((depth, total), bf16),
-        jax.ShapeDtypeStruct((depth, total), bf16),
+        pltpu.VMEM((MEMBERS, rows, width), bf16),
+        pltpu.VMEM((total, units), bf16),
+        pltpu.VMEM((total, units), bf16),
+        pltpu.VMEM((depth, total), bf16),
+        pltpu.VMEM((depth, total), bf16),
     ]
     outs += [block] * 2 if block else []
     return pl.pallas_call(
         functools.partial(sections_kernel, spots, *places),
         out_shape=outs,
-        in_specs=[spec(pltpu.SMEM), spec(pltpu.VMEM), spec(pltpu.HBM), spec(pltpu.HBM)],
+        in_specs=[spec(pltpu.SMEM)] + [spec(pltpu.HBM)] * 3,
         out_specs=[spec(pltpu.VMEM)] * len(outs),
         scratch_shapes=[
+            pltpu.VMEM(both.shape, bf16),
             pltpu.VMEM(w_up.shape, bf16),
             pltpu.VMEM(w_down.shape, bf16),
             pltpu.VMEM((total, depth), bf16),
             pltpu.VMEM((total, LANES), jnp.float32),
             pltpu.VMEM((total, units), bf16),
             pltpu.VMEM((MEMBERS, rows, width), bf16),
-            pltpu.SemaphoreType.DMA((2,)),
+            pltpu.SemaphoreType.DMA((3,)),
         ],
         compiler_params=pltpu.CompilerParams(vmem_limit_bytes=SECTIONS_BYTES),
         cost_estimate=pl.CostEstimate(
             flops=10 * total * depth * units, bytes_accessed=16 * total * units, transcendentals=0
         ),
-    )(place, both, w_up, w_down)
+    )(place, *[pltpu.with_memory_space_constraint(item, pltpu.HBM) for item in (both, w_up, w_down)])
 
 
 def keep_blocks(place, hidden, d_pre, normed_t, grad_t, places, block):
@@ -264,7 +244,7 @@
         cost_estimate=pl.CostEstimate(
             flops=2 * total * depth * units, bytes_accessed=8 * total * units, transcendentals=0
         ),
-    )(place, hidden, d_pre, normed_t, grad_t)
+    )(place, *[pltpu.with_memory_space_constraint(item, pltpu.VMEM) for item in (hidden, d_pre, normed_t, grad_t)])
 
 
 def pick(block, at):
@@ -347,7 +327,7 @@
     steps = [("gx", span_x.bit_length() - 2), ("gx", 0), ("gy", span_y.bit_length() - 2), ("gy", 0)]
     bits = [lax.axis_index(axis) // (1 << bit) % 2 for axis, bit in steps]
     member = sum(bit * mask for bit, mask in zip(bits, MASKS))
-    homeward = [0, 3, 2, 1]
+    homeward = [2, 0, 3, 1]
     spots = [sum((m // MASKS[at] & 1) * mask for at, mask in zip(homeward, MASKS)) for m in range(MEMBERS)]
     spot = sum(bits[at] * mask for at, mask in zip(homeward, MASKS))
     place = jnp.stack([member, 1 - bits[3], spot]).astype(jnp.int32)
@@ -360,12 +340,10 @@
     places = [block_places(order, span_x, span_y) for order in (order_down, order_up)]
     block = None
     if units // span_y % LANES == 0:
-        block = jax.ShapeDtypeStruct(
-            (span_x * span_y // 2, depth // span_x, units // span_y), jnp.bfloat16
-        )
+        block = pltpu.VMEM((span_x * span_y // 2, depth // span_x, units // span_y), jnp.bfloat16)
 
     parts = (MEMBERS, rows // MEMBERS, width)
-    both = exchange(join(signal.reshape(parts), cotangent.reshape(parts)), groups)
+    both = exchange(jnp.concatenate([signal.reshape(parts), cotangent.reshape(parts)], 1), groups)
     state, hidden, d_pre, normed_t, grad_t, *given = sections(
         place, both, w_up, w_down, spots, places, block
     )
@@ -381,7 +359,7 @@
     take_down, take_up = [swap(part, *core) for part in given]
     keep_down, keep_up = keep_blocks(place, hidden, d_pre, normed_t, grad_t, places, block)
     grad_up = finish_sum(keep_up, take_up, order_up)
-    beside = lambda phase, give: home.advance(give) if phase > 0 else give
+    beside = lambda phase, give: home.advance(give)
     grad_down = finish_sum(keep_down, take_down, order_down, beside)
     while home.steps:
         home.advance(place)

time: 140 us -> 110 us (0.79)
  Pallas kernels: 48.2 us -> 24.5 us
  waiting for transfers between devices: 54.2 us -> 48.8 us
  local copies, waits for them, and re-layouts: 14.6 us -> 9.76 us
  other arithmetic: 6.01 us -> 8.18 us
  starting transfers between devices: 15.4 us -> 17.1 us
    pallas_call x1 -> x0, Pallas kernels: 24.9 us -> none  [join(): pl.pallas_call(join_kernel, out_shape=out, in_specs=[spec(pltpu.HBM)] * 2...]
    ppermute x14, waiting for transfers between devices: 31.7 us -> 26.2 us  [swap(): return lax.ppermute(block, axis, pairs)]
    unnamed x22 -> x18, local copies, waits for them, and re-layouts: 14.6 us -> 9.72 us
    concatenate x0 -> x1, other arithmetic: none -> 2.12 us  [local(): jnp.concatenate([signal.reshape(parts), cotangent.reshape(parts)], 1)]
    ppermute x14, starting transfers between devices: 8.11 us -> 9.76 us  [swap(): return lax.ppermute(block, axis, pairs)]
  transfers between devices with their start and end apart: 15 -> 15, of which waited for: 10 -> 9; matrix products, arithmetic and copies ran while one was open for 4% -> 5% of each run, Pallas kernels for 2% -> 5%
where the time goes in v5:
time: 110 us; the launch traced here: 109 us
  waiting for transfers between devices  48.8 us (44%)
  Pallas kernels  24.5 us (22%)
  starting transfers between devices  17.1 us (16%)
  local copies, waits for them, and re-layouts  9.76 us (9%)
  other arithmetic  8.18 us (7%)
    ppermute x14, waiting for transfers between devices, swap(): return lax.ppermute(block, axis, pairs)  26.2 us
    all_to_all x1, waiting for transfers between devices, exchange(): lax.all_to_all(block, ('gx', 'gy'), split_axis=0, concat_axis=0, axis_ind...  22.6 us
    pallas_call x1, Pallas kernels, sections(): pl.pallas_call(functools.partial(sections_kernel, spots, *places), out_sh...  19.5 us
    ppermute x14, starting transfers between devices, swap(): return lax.ppermute(block, axis, pairs)  9.76 us
    unnamed x18, local copies, waits for them, and re-layouts  9.72 us
    all_to_all x1, starting transfers between devices, exchange(): lax.all_to_all(block, ('gx', 'gy'), split_axis=0, concat_axis=0, axis_ind...  7.34 us
    convert_element_type x6, other arithmetic, halve(): keep = (pick(kept, mine) + pick(taken, mine)).astype(jnp.bfloat16)  3.63 us
    pallas_call x1, Pallas kernels, keep_blocks(): pl.pallas_call(functools.partial(keep_kernel, *places), out_shape=[block]...  3.16 us
  transfers between devices with their start and end apart: 15, of which 9 were waited for; matrix products, arithmetic and copies ran while one was open for 5% of the time, Pallas kernels for 5%

profile of v5, /device:TPU:0, one launch (start us, length us, event | category | flops | bytes accessed | tf_op | source)
XLA Modules:
  0.0 109.3 jit_solution(13856930268946424308)
XLA Ops:
  0.6 2.1 %pad_maximum_fusion = bf16[16,64,384]{2,1,0:T(8,128)(2,1)} fusion(bf16[16,32,384]{2,1,0:T(8,128)(2,1)} %bitcast.57, bf16[16,32,384]{2,1,0:T(8,128)(2,1)} %bitcast.58), kind=kLoop, calls=%fused_computation.4 | loop fusion | flops 1572864 | bytes 1572864 | tf_op jit(solution)/shard_map/concatenate | solution.py:346
  2.7 7.3 %all-to-all-start = ((bf16[16,64,384]{2,1,0:T(8,128)(2,1)}), bf16[16,64,384]{2,1,0:T(8,128)(2,1)}, u32[]{:S(2)}, u32[]{:S(2)}) async-start(bf16[16,64,384]{2,1,0:T(8,128)(2,1)} %pad_maximum_fusion), calls=%async_computation | async-start | bytes 1572864 | tf_op jit(solution)/shard_map/all_to_all | solution.py:40
  10.3 22.6 %all-to-all-done.both_hbm = bf16[16,64,384]{2,1,0:T(8,128)(2,1)} async-done(((bf16[16,64,384]{2,1,0:T(8,128)(2,1)}), bf16[16,64,384]{2,1,0:T(8,128)(2,1)}, u32[]{:S(2)}, u32[]{:S(2)}) %all-to-all-start) | async-done | bytes 786464 | tf_op jit(solution)/shard_map/all_to_all | solution.py:40
  32.8 19.5 %shard_map.67 = (bf16[16,32,384]{2,1,0:T(8,128)(2,1)S(1)}, bf16[1024,1536]{1,0:T(8,128)(2,1)S(1)}, bf16[1024,1536]{1,0:T(8,128)(2,1)S(1)}, bf16[768,1024]{1,0:T(...) custom-call(s32[3]{0:T(128)S(1)} %pad_add_fusion.place_ref, ...), custom_call_target="tpu_custom_call" | custom-call | flops 12079595520 | bytes 25165824 | tf_op jit(solution)/shard_map/pallas_call | solution.py:213
  52.4 1.6 %copy-done = bf16[1024,1536]{1,0:T(8,128)(2,1)} copy-done((bf16[1024,1536]{1,0:T(8,128)(2,1)}, bf16[1024,1536]{1,0:T(8,128)(2,1)S(1)}, u32[]{:S(2)}) %copy-start) | copy-done | bytes 3145752
  54.0 1.2 %copy-done.2 = bf16[768,1024]{1,0:T(8,128)(2,1)} copy-done((bf16[768,1024]{1,0:T(8,128)(2,1)}, bf16[768,1024]{1,0:T(8,128)(2,1)S(1)}, u32[]{:S(2)}) %copy-start.2) | copy-done | bytes 1572888
  55.1 1.2 %copy-done.4 = bf16[768,1024]{1,0:T(8,128)(2,1)} copy-done((bf16[768,1024]{1,0:T(8,128)(2,1)}, bf16[768,1024]{1,0:T(8,128)(2,1)S(1)}, u32[]{:S(2)}) %copy-start.4) | copy-done | bytes 1572888
  57.0 1.9 %copy-done.1 = bf16[1024,1536]{1,0:T(8,128)(2,1)S(1)} copy-done((bf16[1024,1536]{1,0:T(8,128)(2,1)S(1)}, bf16[1024,1536]{1,0:T(8,128)(2,1)}, u32[]{:S(2)}) %copy-start.1) | copy-done | bytes 3145752
  58.9 1.4 %copy-done.3 = bf16[768,1024]{1,0:T(8,128)(2,1)S(1)} copy-done((bf16[768,1024]{1,0:T(8,128)(2,1)S(1)}, bf16[768,1024]{1,0:T(8,128)(2,1)}, u32[]{:S(2)}) %copy-start.3) | copy-done | bytes 1572888
  60.3 1.4 %copy-done.5 = bf16[768,1024]{1,0:T(8,128)(2,1)S(1)} copy-done((bf16[768,1024]{1,0:T(8,128)(2,1)S(1)}, bf16[768,1024]{1,0:T(8,128)(2,1)}, u32[]{:S(2)}) %copy-start.5) | copy-done | bytes 1572888
  61.7 3.2 %shard_map.68 = (bf16[16,96,384]{2,1,0:T(8,128)(2,1)S(1)}, bf16[16,96,384]{2,1,0:T(8,128)(2,1)S(1)}) custom-call(s32[3]{0:T(128)S(1)} %pad_add_fusion.place_ref, bf16[1024,1536]{1,0:T(8,128)(2,1)S(1)} %get-tuple-element.23.hidden_ref, bf16[1024,1536]{1,0:T(8,128)(2,1)S(1)} %copy-done.1, bf16[768,1024]{1,0:T(8,128)(2,1)S(1)} %copy-done.3, ...), custom_call_target="tpu_custom_call" | custom-call | flops 2415919104 | bytes 12582912 | tf_op jit(solution)/shard_map/pallas_call | solution.py:238
  64.9 1.0 copy-done.6
  66.0 1.6 %add_convert_fusion.2 = (bf16[1,8,96,384]{3,2,1,0:T(8,128)(2,1)S(1)}, bf16[8,96,384]{2,1,0:T(8,128)(2,1)S(1)}) fusion(bf16[2,8,96,384]{3,2,1,0:T(8,128)(2,1)} %bitcast.7, s32[]{:T(128)S(6)} %select_n.115, bf16[2,8,96,384]{3,2,1,0:T(8,128)(2,1)S(1)} %bitcast.49, s32[]{:T(128)S(6)} %select_n.114), kind=kLoop, calls=%fused_computation.2 | loop fusion | flops 2359296 | bytes 3538952 | tf_op jit(solution)/shard_map/convert_element_type | solution.py:265
  67.6 1.2 %collective-permute-start.3 = (bf16[8,96,384]{2,1,0:T(8,128)(2,1)S(1)}, bf16[8,96,384]{2,1,0:T(8,128)(2,1)S(1)}, u32[]{:S(2)}, u32[]{:S(2)}) collective-permute-start(bf16[8,96,384]{2,1,0:T(8,128)(2,1)S(1)} %get-tuple-element.30), channel_id=1, source_target_pairs={{0,4},{4,0},{8,12},{12,8},{16,20},{20,16},{24,28},{28,24},{1,5},{5... | collective-permute-start | bytes 1769480 | tf_op jit(solution)/shard_map/ppermute | solution.py:256
  68.8 1.5 %add_convert_fusion.1 = (bf16[1,8,96,384]{3,2,1,0:T(8,128)(2,1)S(1)}, bf16[8,96,384]{2,1,0:T(8,128)(2,1)S(1)}) fusion(bf16[2,8,96,384]{3,2,1,0:T(8,128)(2,1)} %bitcast.17, s32[]{:T(128)S(6)} %select_n.117, bf16[2,8,96,384]{3,2,1,0:T(8,128)(2,1)S(1)} %bitcast.48, s32[]{:T(128)S(6)} %select_n.116), kind=kLoop, calls=%fused_computation.1 | loop fusion | flops 2359296 | bytes 3538952 | tf_op jit(solution)/shard_map/convert_element_type | solution.py:265
  70.3 1.1 collective-permute-start.8
  71.4 10.2 %collective-permute-done.2 = bf16[2,4,32,384]{3,2,0,1:T(8,128)(2,1)S(1)} collective-permute-done((bf16[2,4,32,384]{3,2,0,1:T(8,128)(2,1)S(1)}, bf16[2,4,32,384]{3,2,0,1:T(8,128)(2,1)S(1)}, u32[]{:S(2)}, u32[]{:S(2)}) %collective-permute-start.2) | collective-permute-done | bytes 196640 | tf_op jit(solution)/shard_map/ppermute | solution.py:256
  81.7 1.3 %collective-permute-done.3 = bf16[8,96,384]{2,1,0:T(8,128)(2,1)S(1)} collective-permute-done((bf16[8,96,384]{2,1,0:T(8,128)(2,1)S(1)}, bf16[8,96,384]{2,1,0:T(8,128)(2,1)S(1)}, u32[]{:S(2)}, u32[]{:S(2)}) %collective-permute-start.3) | collective-permute-done | bytes 589856 | tf_op jit(solution)/shard_map/ppermute | solution.py:256
  83.2 1.8 %collective-permute-start.5 = (bf16[4,96,384]{2,1,0:T(8,128)(2,1)S(1)}, bf16[4,96,384]{2,1,0:T(8,128)(2,1)S(1)}, u32[]{:S(2)}, u32[]{:S(2)}) collective-permute-start(bf16[4,96,384]{2,1,0:T(8,128)(2,1)S(1)} %get-tuple-element.32), channel_id=1, source_target_pairs={{0,2},{1,3},{2,0},{3,1},{4,6},{5,7},{6,4},{7,5},{8,10},{9,11},{10,... | collective-permute-start | bytes 884744 | tf_op jit(solution)/shard_map/ppermute | solution.py:256
  85.7 0.9 collective-permute-start.9
  86.6 6.0 %collective-permute-done.5 = bf16[4,96,384]{2,1,0:T(8,128)(2,1)S(1)} collective-permute-done((bf16[4,96,384]{2,1,0:T(8,128)(2,1)S(1)}, bf16[4,96,384]{2,1,0:T(8,128)(2,1)S(1)}, u32[]{:S(2)}, u32[]{:S(2)}) %collective-permute-start.5) | collective-permute-done | bytes 294944 | tf_op jit(solution)/shard_map/ppermute | solution.py:256
  92.8 1.5 %collective-permute-done.9 = bf16[4,96,384]{2,1,0:T(8,128)(2,1)S(1)} collective-permute-done((bf16[4,96,384]{2,1,0:T(8,128)(2,1)S(1)}, bf16[4,96,384]{2,1,0:T(8,128)(2,1)S(1)}, u32[]{:S(2)}, u32[]{:S(2)}) %collective-permute-start.9) | collective-permute-done | bytes 294944 | tf_op jit(solution)/shard_map/ppermute | solution.py:256
  94.4 0.5 collective-permute-start.10
  95.0 1.6 %collective-permute-start.6 = (bf16[8,1,32,384]{3,2,0,1:T(8,128)(2,1)S(1)}, bf16[8,1,32,384]{3,2,0,1:T(8,128)(2,1)S(1)}, u32[]{:S(2)}, u32[]{:S(2)}) collective-permute-start(bf16[8,1,32,384]{3,2,0,1:T(8,128)(2,1)S(1)} %get-tuple-element.33), channel_id=1, source_target_pairs={{0,4},{4,0},{8,12},{12,8},{16,20},{20,16},{24,28},{28,24},{1,5},{5... | collective-permute-start | bytes 589832 | tf_op jit(solution)/shard_map/ppermute | solution.py:256
  96.6 4.6 %collective-permute-done.12 = bf16[2,96,384]{2,1,0:T(8,128)(2,1)S(1)} collective-permute-done((bf16[2,96,384]{2,1,0:T(8,128)(2,1)S(1)}, bf16[2,96,384]{2,1,0:T(8,128)(2,1)S(1)}, u32[]{:S(2)}, u32[]{:S(2)}) %collective-permute-start.12) | collective-permute-done | bytes 147488 | tf_op jit(solution)/shard_map/ppermute | solution.py:256
  101.3 1.1 %collective-permute-done.10 = bf16[2,96,384]{2,1,0:T(8,128)(2,1)S(1)} collective-permute-done((bf16[2,96,384]{2,1,0:T(8,128)(2,1)S(1)}, bf16[2,96,384]{2,1,0:T(8,128)(2,1)S(1)}, u32[]{:S(2)}, u32[]{:S(2)}) %collective-permute-start.10) | collective-permute-done | bytes 147488 | tf_op jit(solution)/shard_map/ppermute | solution.py:256
  102.5 1.8 %collective-permute-start.11 = (bf16[1,96,384]{2,1,0:T(8,128)(2,1)S(1)}, bf16[1,96,384]{2,1,0:T(8,128)(2,1)S(1)}, u32[]{:S(2)}, u32[]{:S(2)}) collective-permute-start(bf16[1,96,384]{2,1,0:T(8,128)(2,1)S(1)} %fusion.11), channel_id=1, source_target_pairs={{0,16},{4,20},{8,24},{12,28},{16,0},{20,4},{24,8},{28,12},{1,17},{... | collective-permute-start | bytes 221192 | tf_op jit(solution)/shard_map/ppermute | solution.py:256
  104.3 0.8 maximum_bitcast_fusion.blocks_ref
  105.1 1.9 %shard_map.69 = bf16[512,384]{1,0:T(8,128)(2,1)} custom-call(s32[3]{0:T(128)} %copy-done.8, bf16[16,32,384]{2,1,0:T(8,128)(2,1)} %maximum_bitcast_fusion.blocks_ref), custom_call_target="tpu_custom_call" | custom-call | bytes 786432 | tf_op jit(solution)/shard_map/pallas_call | solution.py:311
  107.0 0.7 add_bitcast_fusion
  107.7 0.9 collective-permute-done.11
  108.6 0.7 add_bitcast_fusion.1
  (36 shorter events, 2.0 us)
Async XLA Ops:
  2.7 30.1 %all-to-all-start = ((bf16[16,64,384]{2,1,0:T(8,128)(2,1)}), bf16[16,64,384]{2,1,0:T(8,128)(2,1)}, u32[]{:S(2)}, u32[]{:S(2)}) async-start(bf16[16,64,384]{2,1,0:T(8,128)(2,1)} %pad_maximum_fusion), calls=%async_computation | async-start | bytes 1572864 | tf_op jit(solution)/shard_map/all_to_all | solution.py:40
  10.3 46.7 %copy-start.8 = (s32[3]{0:T(128)}, s32[3]{0:T(128)S(1)}, u32[]{:S(2)}) copy-start(s32[3]{0:T(128)S(1)} %pad_add_fusion.place_ref) | copy-start | bytes 40
  52.4 1.6 %copy-start = (bf16[1024,1536]{1,0:T(8,128)(2,1)}, bf16[1024,1536]{1,0:T(8,128)(2,1)S(1)}, u32[]{:S(2)}) copy-start(bf16[1024,1536]{1,0:T(8,128)(2,1)S(1)} %get-tuple-element.24.d_pre_ref) | copy-start | bytes 9437188
  54.0 1.2 %copy-start.2 = (bf16[768,1024]{1,0:T(8,128)(2,1)}, bf16[768,1024]{1,0:T(8,128)(2,1)S(1)}, u32[]{:S(2)}) copy-start(bf16[768,1024]{1,0:T(8,128)(2,1)S(1)} %get-tuple-element.25.normed_t_ref) | copy-start | bytes 4718596
  55.1 1.2 %copy-start.4 = (bf16[768,1024]{1,0:T(8,128)(2,1)}, bf16[768,1024]{1,0:T(8,128)(2,1)S(1)}, u32[]{:S(2)}) copy-start(bf16[768,1024]{1,0:T(8,128)(2,1)S(1)} %get-tuple-element.26.grad_t_ref) | copy-start | bytes 4718596
  56.4 9.5 %collective-permute-start.1 = (bf16[16,96,384]{2,1,0:T(8,128)(2,1)}, bf16[16,96,384]{2,1,0:T(8,128)(2,1)}, u32[]{:S(2)}, u32[]{:S(2)}) collective-permute-start(bf16[16,96,384]{2,1,0:T(8,128)(2,1)} %get-tuple-element.28), channel_id=1, source_target_pairs={{0,1},{1,0},{2,3},{3,2},{4,5},{5,4},{6,7},{7,6},{8,9},{9,8},{10,11... | collective-permute-start | bytes 3538952 | tf_op jit(solution)/shard_map/ppermute | solution.py:256
  56.5 12.3 %collective-permute-start.7 = (bf16[16,96,384]{2,1,0:T(8,128)(2,1)}, bf16[16,96,384]{2,1,0:T(8,128)(2,1)}, u32[]{:S(2)}, u32[]{:S(2)}) collective-permute-start(bf16[16,96,384]{2,1,0:T(8,128)(2,1)} %get-tuple-element.35), channel_id=1, source_target_pairs={{0,1},{1,0},{2,3},{3,2},{4,5},{5,4},{6,7},{7,6},{8,9},{9,8},{10,11... | collective-permute-start | bytes 3538952 | tf_op jit(solution)/shard_map/ppermute | solution.py:256
  57.0 8.9 %collective-permute-start = (bf16[1,8,32,384]{3,2,0,1:T(8,128)(2,1)S(1)}, bf16[1,8,32,384]{3,2,0,1:T(8,128)(2,1)S(1)}, u32[]{:S(2)}, u32[]{:S(2)}) collective-permute-start(bf16[1,8,32,384]{3,2,0,1:T(8,128)(2,1)S(1)} %get-tuple-element.22), channel_id=1, source_target_pairs={{0,2},{1,3},{2,0},{3,1},{4,6},{5,7},{6,4},{7,5},{8,10},{9,11},{10,... | collective-permute-start | bytes 589832 | tf_op jit(solution)/shard_map/ppermute | solution.py:256
  57.0 1.9 %copy-start.1 = (bf16[1024,1536]{1,0:T(8,128)(2,1)S(1)}, bf16[1024,1536]{1,0:T(8,128)(2,1)}, u32[]{:S(2)}) copy-start(bf16[1024,1536]{1,0:T(8,128)(2,1)} %copy-done) | copy-start | bytes 9437188
  58.9 1.4 %copy-start.3 = (bf16[768,1024]{1,0:T(8,128)(2,1)S(1)}, bf16[768,1024]{1,0:T(8,128)(2,1)}, u32[]{:S(2)}) copy-start(bf16[768,1024]{1,0:T(8,128)(2,1)} %copy-done.2) | copy-start | bytes 4718596
  60.3 1.4 %copy-start.5 = (bf16[768,1024]{1,0:T(8,128)(2,1)S(1)}, bf16[768,1024]{1,0:T(8,128)(2,1)}, u32[]{:S(2)}) copy-start(bf16[768,1024]{1,0:T(8,128)(2,1)} %copy-done.4) | copy-start | bytes 4718596
  64.9 1.0 copy-start.6
  66.0 2.8 %copy-start.7 = (bf16[16,96,384]{2,1,0:T(8,128)(2,1)S(1)}, bf16[16,96,384]{2,1,0:T(8,128)(2,1)}, u32[]{:S(2)}) copy-start(bf16[16,96,384]{2,1,0:T(8,128)(2,1)} %copy-done.6) | copy-start | bytes 3538948
  67.6 15.4 %collective-permute-start.3 = (bf16[8,96,384]{2,1,0:T(8,128)(2,1)S(1)}, bf16[8,96,384]{2,1,0:T(8,128)(2,1)S(1)}, u32[]{:S(2)}, u32[]{:S(2)}) collective-permute-start(bf16[8,96,384]{2,1,0:T(8,128)(2,1)S(1)} %get-tuple-element.30), channel_id=1, source_target_pairs={{0,4},{4,0},{8,12},{12,8},{16,20},{20,16},{24,28},{28,24},{1,5},{5... | collective-permute-start | bytes 1769480 | tf_op jit(solution)/shard_map/ppermute | solution.py:256
  70.3 15.2 %collective-permute-start.8 = (bf16[8,96,384]{2,1,0:T(8,128)(2,1)S(1)}, bf16[8,96,384]{2,1,0:T(8,128)(2,1)S(1)}, u32[]{:S(2)}, u32[]{:S(2)}) collective-permute-start(bf16[8,96,384]{2,1,0:T(8,128)(2,1)S(1)} %get-tuple-element.38), channel_id=1, source_target_pairs={{0,2},{1,3},{2,0},{3,1},{4,6},{5,7},{6,4},{7,5},{8,10},{9,11},{10,... | collective-permute-start | bytes 1769480 | tf_op jit(solution)/shard_map/ppermute | solution.py:256
  71.4 10.3 %collective-permute-start.2 = (bf16[2,4,32,384]{3,2,0,1:T(8,128)(2,1)S(1)}, bf16[2,4,32,384]{3,2,0,1:T(8,128)(2,1)S(1)}, u32[]{:S(2)}, u32[]{:S(2)}) collective-permute-start(bf16[2,4,32,384]{3,2,0,1:T(8,128)(2,1)S(1)} %get-tuple-element.29), channel_id=1, source_target_pairs={{0,16},{4,20},{8,24},{12,28},{16,0},{20,4},{24,8},{28,12},{1,17},{... | collective-permute-start | bytes 589832 | tf_op jit(solution)/shard_map/ppermute | solution.py:256
  83.2 3.4 %collective-permute-start.4 = (bf16[4,2,32,384]{3,2,0,1:T(8,128)(2,1)S(1)}, bf16[4,2,32,384]{3,2,0,1:T(8,128)(2,1)S(1)}, u32[]{:S(2)}, u32[]{:S(2)}) collective-permute-start(bf16[4,2,32,384]{3,2,0,1:T(8,128)(2,1)S(1)} %get-tuple-element.31), channel_id=1, source_target_pairs={{0,1},{1,0},{2,3},{3,2},{4,5},{5,4},{6,7},{7,6},{8,9},{9,8},{10,11... | collective-permute-start | bytes 589832 | tf_op jit(solution)/shard_map/ppermute | solution.py:256
  83.2 9.4 %collective-permute-start.5 = (bf16[4,96,384]{2,1,0:T(8,128)(2,1)S(1)}, bf16[4,96,384]{2,1,0:T(8,128)(2,1)S(1)}, u32[]{:S(2)}, u32[]{:S(2)}) collective-permute-start(bf16[4,96,384]{2,1,0:T(8,128)(2,1)S(1)} %get-tuple-element.32), channel_id=1, source_target_pairs={{0,2},{1,3},{2,0},{3,1},{4,6},{5,7},{6,4},{7,5},{8,10},{9,11},{10,... | collective-permute-start | bytes 884744 | tf_op jit(solution)/shard_map/ppermute | solution.py:256
  85.7 8.7 %collective-permute-start.9 = (bf16[4,96,384]{2,1,0:T(8,128)(2,1)S(1)}, bf16[4,96,384]{2,1,0:T(8,128)(2,1)S(1)}, u32[]{:S(2)}, u32[]{:S(2)}) collective-permute-start(bf16[4,96,384]{2,1,0:T(8,128)(2,1)S(1)} %get-tuple-element.42), channel_id=1, source_target_pairs={{0,4},{4,0},{8,12},{12,8},{16,20},{20,16},{24,28},{28,24},{1,5},{5... | collective-permute-start | bytes 884744 | tf_op jit(solution)/shard_map/ppermute | solution.py:256
  92.7 8.5 %collective-permute-start.12 = (bf16[2,96,384]{2,1,0:T(8,128)(2,1)S(1)}, bf16[2,96,384]{2,1,0:T(8,128)(2,1)S(1)}, u32[]{:S(2)}, u32[]{:S(2)}) collective-permute-start(bf16[2,96,384]{2,1,0:T(8,128)(2,1)S(1)} %get-tuple-element.36), channel_id=1, source_target_pairs={{0,16},{4,20},{8,24},{12,28},{16,0},{20,4},{24,8},{28,12},{1,17},{... | collective-permute-start | bytes 442376 | tf_op jit(solution)/shard_map/ppermute | solution.py:256
  94.4 8.0 %collective-permute-start.10 = (bf16[2,96,384]{2,1,0:T(8,128)(2,1)S(1)}, bf16[2,96,384]{2,1,0:T(8,128)(2,1)S(1)}, u32[]{:S(2)}, u32[]{:S(2)}) collective-permute-start(bf16[2,96,384]{2,1,0:T(8,128)(2,1)S(1)} %get-tuple-element.48), channel_id=1, source_target_pairs={{0,8},{4,12},{8,0},{12,4},{16,24},{20,28},{24,16},{28,20},{1,9},{5... | collective-permute-start | bytes 442376 | tf_op jit(solution)/shard_map/ppermute | solution.py:256
  95.0 9.3 %collective-permute-start.6 = (bf16[8,1,32,384]{3,2,0,1:T(8,128)(2,1)S(1)}, bf16[8,1,32,384]{3,2,0,1:T(8,128)(2,1)S(1)}, u32[]{:S(2)}, u32[]{:S(2)}) collective-permute-start(bf16[8,1,32,384]{3,2,0,1:T(8,128)(2,1)S(1)} %get-tuple-element.33), channel_id=1, source_target_pairs={{0,4},{4,0},{8,12},{12,8},{16,20},{20,16},{24,28},{28,24},{1,5},{5... | collective-permute-start | bytes 589832 | tf_op jit(solution)/shard_map/ppermute | solution.py:256
  101.2 5.8 %collective-permute-start.13 = (bf16[1,96,384]{2,1,0:T(8,128)(2,1)S(1)}, bf16[1,96,384]{2,1,0:T(8,128)(2,1)S(1)}, u32[]{:S(2)}, u32[]{:S(2)}) collective-permute-start(bf16[1,96,384]{2,1,0:T(8,128)(2,1)S(1)} %fusion.9), channel_id=1, source_target_pairs={{0,8},{4,12},{8,0},{12,4},{16,24},{20,28},{24,16},{28,20},{1,9},{5... | collective-permute-start | bytes 221192 | tf_op jit(solution)/shard_map/ppermute | solution.py:256
  102.5 6.1 %collective-permute-start.11 = (bf16[1,96,384]{2,1,0:T(8,128)(2,1)S(1)}, bf16[1,96,384]{2,1,0:T(8,128)(2,1)S(1)}, u32[]{:S(2)}, u32[]{:S(2)}) collective-permute-start(bf16[1,96,384]{2,1,0:T(8,128)(2,1)S(1)} %fusion.11), channel_id=1, source_target_pairs={{0,16},{4,20},{8,24},{12,28},{16,0},{20,4},{24,8},{28,12},{1,17},{... | collective-permute-start | bytes 221192 | tf_op jit(solution)/shard_map/ppermute | solution.py:256

commit v6 on v5

--- a/solution.py
+++ b/solution.py
@@ -247,8 +247,11 @@
     )(place, *[pltpu.with_memory_space_constraint(item, pltpu.VMEM) for item in (hidden, d_pre, normed_t, grad_t)])
 
 
-def pick(block, at):
-    return lax.dynamic_index_in_dim(block, at, 0, keepdims=False).astype(jnp.float32)
+def halve_kernel(slot, place_ref, kept_ref, taken_ref, keep_ref, give_ref):
+    mine = place_ref[slot]
+    for out_ref, half in ((give_ref, 1 - mine), (keep_ref, mine)):
+        total = kept_ref[half].astype(jnp.float32) + taken_ref[half].astype(jnp.float32)
+        out_ref[...] = total.astype(out_ref.dtype)
 
 
 def swap(block, axis, bit):
@@ -256,26 +259,29 @@
     return lax.ppermute(block, axis, pairs)
 
 
-def halve(kept, taken, step):
-    axis, bit = step
-    mine = lax.axis_index(axis) // (1 << bit) % 2
-    kept = kept.reshape((2, -1) + kept.shape[1:])
-    taken = taken.reshape(kept.shape)
-    give = (pick(kept, 1 - mine) + pick(taken, 1 - mine)).astype(jnp.bfloat16)
-    keep = (pick(kept, mine) + pick(taken, mine)).astype(jnp.bfloat16)
-    return keep, give
-
-
-def finish_sum(kept, taken, order, beside=None):
+def halve(place, slot, kept, taken):
+    shape = (2, kept.shape[0] // 2) + kept.shape[1:]
+    kept, taken = kept.reshape(shape), taken.reshape(shape)
+    return pl.pallas_call(
+        functools.partial(halve_kernel, slot),
+        out_shape=[pltpu.VMEM(shape[1:], kept.dtype)] * 2,
+        in_specs=[spec(pltpu.SMEM)] + [spec(pltpu.VMEM)] * 2,
+        out_specs=[spec(pltpu.VMEM)] * 2,
+        compiler_params=pltpu.CompilerParams(vmem_limit_bytes=KEEP_BYTES),
+        cost_estimate=pl.CostEstimate(flops=kept.size, bytes_accessed=6 * kept.size, transcendentals=0),
+    )(place, *[pltpu.with_memory_space_constraint(item, pltpu.VMEM) for item in (kept, taken)])
+
+
+def finish_sum(place, slots, kept, taken, order, beside=None):
     for phase, step in enumerate(order):
-        kept, give = halve(kept, taken, step)
+        kept, give = halve(place, slots[step], kept, taken)
         if beside:
             give = beside(phase, give)
         taken = swap(give, *step)
     return (kept.astype(jnp.float32) + taken.astype(jnp.float32))[0]
 
 
-def scatter_narrow(left, right, order, span_x, span_y):
+def scatter_narrow(place, slots, left, right, order, span_x, span_y):
     total = jnp.dot(left, right, preferred_element_type=jnp.float32).astype(jnp.bfloat16)
     rows, columns = left.shape[0] // span_x, right.shape[1] // span_y
     count_x, count_y = span_x.bit_length() - 1, span_y.bit_length() - 1
@@ -284,7 +290,7 @@
     blocks = total.reshape((2,) * count_x + (rows,) + (2,) * count_y + (columns,))
     blocks = blocks.transpose([dims.index(item) for item in list(order) + ["rows", "columns"]])
     blocks = blocks.reshape(-1, rows, columns)
-    return finish_sum(blocks, jnp.zeros_like(blocks), order)
+    return finish_sum(place, slots, blocks, jnp.zeros_like(blocks), order)
 
 
 class Homeward:
@@ -327,16 +333,18 @@
     steps = [("gx", span_x.bit_length() - 2), ("gx", 0), ("gy", span_y.bit_length() - 2), ("gy", 0)]
     bits = [lax.axis_index(axis) // (1 << bit) % 2 for axis, bit in steps]
     member = sum(bit * mask for bit, mask in zip(bits, MASKS))
-    homeward = [2, 0, 3, 1]
+    homeward = [2, 0, 1, 3]
     spots = [sum((m // MASKS[at] & 1) * mask for at, mask in zip(homeward, MASKS)) for m in range(MEMBERS)]
     spot = sum(bits[at] * mask for at, mask in zip(homeward, MASKS))
-    place = jnp.stack([member, 1 - bits[3], spot]).astype(jnp.int32)
 
     rest_y = [("gy", bit) for bit in range(1, span_y.bit_length() - 1)]
     rest_x = [("gx", bit) for bit in range(1, span_x.bit_length() - 1)]
     core, across = ("gy", 0), ("gx", 0)
     order_down = [across] + rest_y + rest_x[::-1]
     order_up = rest_y + [across] + rest_x
+    slots = {step: 3 + at for at, step in enumerate([core] + order_up)}
+    owns = [lax.axis_index(axis) // (1 << bit) % 2 for axis, bit in slots]
+    place = jnp.stack([member, 1 - bits[3], spot] + owns).astype(jnp.int32)
     places = [block_places(order, span_x, span_y) for order in (order_down, order_up)]
     block = None
     if units // span_y % LANES == 0:
@@ -352,15 +360,15 @@
         while home.steps:
             home.advance(place)
         mixed_out = home.settle(place)
-        grad_down = scatter_narrow(grad_t, hidden, [core] + order_down, span_x, span_y)
-        grad_up = scatter_narrow(normed_t, d_pre, [core] + order_up, span_x, span_y)
+        grad_down = scatter_narrow(place, slots, grad_t, hidden, [core] + order_down, span_x, span_y)
+        grad_up = scatter_narrow(place, slots, normed_t, d_pre, [core] + order_up, span_x, span_y)
         return (mixed_out, grad_up, grad_down)
     given[0] = home.advance(given[0])
     take_down, take_up = [swap(part, *core) for part in given]
     keep_down, keep_up = keep_blocks(place, hidden, d_pre, normed_t, grad_t, places, block)
-    grad_up = finish_sum(keep_up, take_up, order_up)
-    beside = lambda phase, give: home.advance(give)
-    grad_down = finish_sum(keep_down, take_down, order_down, beside)
+    grad_up = finish_sum(place, slots, keep_up, take_up, order_up)
+    beside = lambda phase, give: give if phase == 1 else home.advance(give)
+    grad_down = finish_sum(place, slots, keep_down, take_down, order_down, beside)
     while home.steps:
         home.advance(place)
     return (home.settle(place), grad_up, grad_down)

time: 110 us -> 103 us (0.936)
  local copies, waits for them, and re-layouts: 9.76 us -> 1.03 us
  Pallas kernels: 24.5 us -> 28.8 us
  other arithmetic: 8.18 us -> 4.43 us
  waiting for transfers between devices: 48.8 us -> 51.6 us
  starting transfers between devices: 17.1 us -> 16 us
    unnamed x18 -> x4, local copies, waits for them, and re-layouts: 9.72 us -> 0.9 us
    pallas_call x0 -> x8, Pallas kernels: none -> 5.43 us  [halve(): pl.pallas_call(functools.partial(halve_kernel, slot), out_shape=[pltpu.VM...]
    convert_element_type x8 -> x0, other arithmetic: 3.67 us -> none  [the longest x6 3.63 us: halve(): keep = (pick(kept, mine) + pick(taken, mine)).astype(jnp.bfloat16)]
    ppermute x14, waiting for transfers between devices: 26.2 us -> 29.1 us  [swap(): return lax.ppermute(block, axis, pairs)]
    pallas_call x1, Pallas kernels: 19.5 us -> 18.3 us  [sections(): pl.pallas_call(functools.partial(sections_kernel, spots, *places), out_sh...]
  transfers between devices with their start and end apart: 15 -> 15, of which waited for: 9 -> 9; matrix products, arithmetic and copies ran while one was open for 5% -> 2% of each run, Pallas kernels for 5% -> 8%
where the time goes in v6:
time: 103 us
  waiting for transfers between devices  51.6 us (50%)
  Pallas kernels  28.8 us (28%)
  starting transfers between devices  16 us (16%)
  other arithmetic  4.43 us (4%)
  between operations  1.06 us (1%)
  local copies, waits for them, and re-layouts  1.03 us (1%)
    ppermute x14, waiting for transfers between devices, swap(): return lax.ppermute(block, axis, pairs)  29.1 us
    all_to_all x1, waiting for transfers between devices, exchange(): lax.all_to_all(block, ('gx', 'gy'), split_axis=0, concat_axis=0, axis_ind...  22.5 us
    pallas_call x1, Pallas kernels, sections(): pl.pallas_call(functools.partial(sections_kernel, spots, *places), out_sh...  18.3 us
    ppermute x14, starting transfers between devices, swap(): return lax.ppermute(block, axis, pairs)  8.7 us
    all_to_all x1, starting transfers between devices, exchange(): lax.all_to_all(block, ('gx', 'gy'), split_axis=0, concat_axis=0, axis_ind...  7.3 us
    pallas_call x8, Pallas kernels, halve(): pl.pallas_call(functools.partial(halve_kernel, slot), out_shape=[pltpu.VM...  5.43 us
    pallas_call x1, Pallas kernels, keep_blocks(): pl.pallas_call(functools.partial(keep_kernel, *places), out_shape=[block]...  3.17 us
    concatenate x1, other arithmetic, local(): jnp.concatenate([signal.reshape(parts), cotangent.reshape(parts)], 1)  2.12 us
  transfers between devices with their start and end apart: 15, of which 9 were waited for; matrix products, arithmetic and copies ran while one was open for 2% of the time, Pallas kernels for 8%

profile of v6, /device:TPU:0, one launch (start us, length us, event | category | flops | bytes accessed | tf_op | source)
XLA Modules:
  0.0 102.9 jit_solution(1257862906255875991)
XLA Ops:
  0.6 2.1 %pad_maximum_fusion = bf16[16,64,384]{2,1,0:T(8,128)(2,1)} fusion(bf16[16,32,384]{2,1,0:T(8,128)(2,1)} %bitcast.50, bf16[16,32,384]{2,1,0:T(8,128)(2,1)} %bitcast.51), kind=kLoop, calls=%fused_computation | loop fusion | flops 1572864 | bytes 1572864 | tf_op jit(solution)/shard_map/concatenate | solution.py:354
  2.8 7.3 %all-to-all-start = ((bf16[16,64,384]{2,1,0:T(8,128)(2,1)}), bf16[16,64,384]{2,1,0:T(8,128)(2,1)S(1)}, u32[]{:S(2)}, u32[]{:S(2)}) async-start(bf16[16,64,384]{2,1,0:T(8,128)(2,1)} %pad_maximum_fusion), calls=%async_computation | async-start | bytes 1572864 | tf_op jit(solution)/shard_map/all_to_all | solution.py:40
  10.2 22.5 %all-to-all-done.both_hbm = bf16[16,64,384]{2,1,0:T(8,128)(2,1)S(1)} async-done(((bf16[16,64,384]{2,1,0:T(8,128)(2,1)}), bf16[16,64,384]{2,1,0:T(8,128)(2,1)S(1)}, u32[]{:S(2)}, u32[]{:S(2)}) %all-to-all-start) | async-done | bytes 786464 | tf_op jit(solution)/shard_map/all_to_all | solution.py:40
  32.7 0.9 copy-done.1
  33.6 18.3 %shard_map.67 = (bf16[16,32,384]{2,1,0:T(8,128)(2,1)S(1)}, bf16[1024,1536]{1,0:T(8,128)(2,1)S(1)}, bf16[1024,1536]{1,0:T(8,128)(2,1)S(1)}, bf16[768,1024]{1,0:T(...) custom-call(s32[8]{0:T(128)S(1)} %stack.35.place_ref, ...), custom_call_target="tpu_custom_call" | custom-call | flops 12079595520 | bytes 25165824 | tf_op jit(solution)/shard_map/pallas_call | solution.py:213
  52.1 0.5 collective-permute-start.8
  52.6 3.2 %shard_map.68 = (bf16[16,96,384]{2,1,0:T(8,128)(2,1)S(1)}, bf16[16,96,384]{2,1,0:T(8,128)(2,1)S(1)}) custom-call(s32[8]{0:T(128)S(1)} %stack.35.place_ref, bf16[1024,1536]{1,0:T(8,128)(2,1)S(1)} %get-tuple-element.39.hidden_ref, bf16[1024,1536]{1,0:T(8,128)(2,1)S(1)} %get-tuple-element.40.d_pre_ref, bf16[768,1024]{1,0:T(8,128)(2,1)S(1)} %get-tuple-element.41.normed_t_ref, ...), custom_call_target="tpu_custom_call" | custom-call | flops 2415919104 | bytes 12582912 | tf_op jit(solution)/shard_map/pallas_call | solution.py:238
  55.8 3.7 %collective-permute-done = bf16[1,8,32,384]{3,2,0,1:T(8,128)(2,1)S(1)} collective-permute-done((bf16[1,8,32,384]{3,2,0,1:T(8,128)(2,1)S(1)}, bf16[1,8,32,384]{3,2,0,1:T(8,128)(2,1)S(1)}, u32[]{:S(2)}, u32[]{:S(2)}) %collective-permute-start) | collective-permute-done | bytes 196640 | tf_op jit(solution)/shard_map/ppermute | solution.py:259
  59.5 0.8 shard_map.69
  60.5 0.8 shard_map.74
  61.3 1.5 %collective-permute-start.9 = (bf16[8,96,384]{2,1,0:T(8,128)(2,1)S(1)}, bf16[8,96,384]{2,1,0:T(8,128)(2,1)S(1)}, u32[]{:S(2)}, u32[]{:S(2)}) collective-permute-start(bf16[8,96,384]{2,1,0:T(8,128)(2,1)S(1)} %get-tuple-element.60), channel_id=1, source_target_pairs={{0,2},{1,3},{2,0},{3,1},{4,6},{5,7},{6,4},{7,5},{8,10},{9,11},{10,... | collective-permute-start | bytes 1769480 | tf_op jit(solution)/shard_map/ppermute | solution.py:259
  62.8 12.1 %collective-permute-done.3 = bf16[8,96,384]{2,1,0:T(8,128)(2,1)S(1)} collective-permute-done((bf16[8,96,384]{2,1,0:T(8,128)(2,1)S(1)}, bf16[8,96,384]{2,1,0:T(8,128)(2,1)S(1)}, u32[]{:S(2)}, u32[]{:S(2)}) %collective-permute-start.3) | collective-permute-done | bytes 589856 | tf_op jit(solution)/shard_map/ppermute | solution.py:259
  74.9 0.7 shard_map.70
  75.6 0.7 collective-permute-start.4
  76.3 0.7 shard_map.75
  77.0 1.6 %collective-permute-start.10 = (bf16[4,96,384]{2,1,0:T(8,128)(2,1)S(1)}, bf16[4,96,384]{2,1,0:T(8,128)(2,1)S(1)}, u32[]{:S(2)}, u32[]{:S(2)}) collective-permute-start(bf16[4,96,384]{2,1,0:T(8,128)(2,1)S(1)} %get-tuple-element.62), channel_id=1, source_target_pairs={{0,4},{4,0},{8,12},{12,8},{16,20},{20,16},{24,28},{28,24},{1,5},{5... | collective-permute-start | bytes 884744 | tf_op jit(solution)/shard_map/ppermute | solution.py:259
  78.7 4.2 %collective-permute-done.4 = bf16[4,96,384]{2,1,0:T(8,128)(2,1)S(1)} collective-permute-done((bf16[4,96,384]{2,1,0:T(8,128)(2,1)S(1)}, bf16[4,96,384]{2,1,0:T(8,128)(2,1)S(1)}, u32[]{:S(2)}, u32[]{:S(2)}) %collective-permute-start.4) | collective-permute-done | bytes 294944 | tf_op jit(solution)/shard_map/ppermute | solution.py:259
  82.9 0.6 shard_map.71
  83.5 1.0 %collective-permute-start.5 = (bf16[4,2,32,384]{3,2,0,1:T(8,128)(2,1)S(1)}, bf16[4,2,32,384]{3,2,0,1:T(8,128)(2,1)S(1)}, u32[]{:S(2)}, u32[]{:S(2)}) collective-permute-start(bf16[4,2,32,384]{3,2,0,1:T(8,128)(2,1)S(1)} %get-tuple-element.52), channel_id=1, source_target_pairs={{0,4},{4,0},{8,12},{12,8},{16,20},{20,16},{24,28},{28,24},{1,5},{5... | collective-permute-start | bytes 589832 | tf_op jit(solution)/shard_map/ppermute | solution.py:259
  84.6 0.4 collective-permute-done.10
  85.0 0.6 shard_map.76
  85.7 2.0 %collective-permute-start.6 = (bf16[2,96,384]{2,1,0:T(8,128)(2,1)S(1)}, bf16[2,96,384]{2,1,0:T(8,128)(2,1)S(1)}, u32[]{:S(2)}, u32[]{:S(2)}) collective-permute-start(bf16[2,96,384]{2,1,0:T(8,128)(2,1)S(1)} %get-tuple-element.54), channel_id=1, source_target_pairs={{0,16},{4,20},{8,24},{12,28},{16,0},{20,4},{24,8},{28,12},{1,17},{... | collective-permute-start | bytes 442376 | tf_op jit(solution)/shard_map/ppermute | solution.py:259
  87.7 4.8 %collective-permute-done.11 = bf16[2,96,384]{2,1,0:T(8,128)(2,1)S(1)} collective-permute-done((bf16[2,96,384]{2,1,0:T(8,128)(2,1)S(1)}, bf16[2,96,384]{2,1,0:T(8,128)(2,1)S(1)}, u32[]{:S(2)}, u32[]{:S(2)}) %collective-permute-start.11) | collective-permute-done | bytes 147488 | tf_op jit(solution)/shard_map/ppermute | solution.py:259
  92.5 0.6 shard_map.77
  93.2 1.1 %collective-permute-done.6 = bf16[2,96,384]{2,1,0:T(8,128)(2,1)S(1)} collective-permute-done((bf16[2,96,384]{2,1,0:T(8,128)(2,1)S(1)}, bf16[2,96,384]{2,1,0:T(8,128)(2,1)S(1)}, u32[]{:S(2)}, u32[]{:S(2)}) %collective-permute-start.6) | collective-permute-done | bytes 147488 | tf_op jit(solution)/shard_map/ppermute | solution.py:259
  94.3 0.6 shard_map.72
  94.9 1.0 collective-permute-start.13
  96.0 2.4 %collective-permute-done.12 = bf16[1,96,384]{2,1,0:T(8,128)(2,1)S(1)} collective-permute-done((bf16[1,96,384]{2,1,0:T(8,128)(2,1)S(1)}, bf16[1,96,384]{2,1,0:T(8,128)(2,1)S(1)}, u32[]{:S(2)}, u32[]{:S(2)}) %collective-permute-start.12) | collective-permute-done | bytes 73760 | tf_op jit(solution)/shard_map/ppermute | solution.py:259
  98.4 0.7 add_bitcast_fusion.1
  99.4 0.7 add_bitcast_fusion
  100.0 0.8 maximum_bitcast_fusion.blocks_ref
  100.9 1.9 %shard_map.73 = bf16[512,384]{1,0:T(8,128)(2,1)} custom-call(s32[8]{0:T(128)} %copy-done, bf16[16,32,384]{2,1,0:T(8,128)(2,1)} %maximum_bitcast_fusion.blocks_ref), custom_call_target="tpu_custom_call" | custom-call | bytes 786432 | tf_op jit(solution)/shard_map/pallas_call | solution.py:317
  (22 shorter events, 0.9 us)
Async XLA Ops:
  2.8 30.0 %all-to-all-start = ((bf16[16,64,384]{2,1,0:T(8,128)(2,1)}), bf16[16,64,384]{2,1,0:T(8,128)(2,1)S(1)}, u32[]{:S(2)}, u32[]{:S(2)}) async-start(bf16[16,64,384]{2,1,0:T(8,128)(2,1)} %pad_maximum_fusion), calls=%async_computation | async-start | bytes 1572864 | tf_op jit(solution)/shard_map/all_to_all | solution.py:40
  10.2 84.0 %copy-start = (s32[8]{0:T(128)}, s32[8]{0:T(128)S(1)}, u32[]{:S(2)}) copy-start(s32[8]{0:T(128)S(1)} %stack.35.place_ref) | copy-start | bytes 100
  32.7 0.9 copy-start.1
  52.0 7.5 %collective-permute-start.1 = (bf16[16,96,384]{2,1,0:T(8,128)(2,1)S(1)}, bf16[16,96,384]{2,1,0:T(8,128)(2,1)S(1)}, u32[]{:S(2)}, u32[]{:S(2)}) collective-permute-start(bf16[16,96,384]{2,1,0:T(8,128)(2,1)S(1)} %get-tuple-element.44), channel_id=1, source_target_pairs={{0,1},{1,0},{2,3},{3,2},{4,5},{5,4},{6,7},{7,6},{8,9},{9,8},{10,11... | collective-permute-start | bytes 3538952 | tf_op jit(solution)/shard_map/ppermute | solution.py:259
  52.1 8.4 %collective-permute-start.8 = (bf16[16,96,384]{2,1,0:T(8,128)(2,1)S(1)}, bf16[16,96,384]{2,1,0:T(8,128)(2,1)S(1)}, u32[]{:S(2)}, u32[]{:S(2)}) collective-permute-start(bf16[16,96,384]{2,1,0:T(8,128)(2,1)S(1)} %get-tuple-element.58), channel_id=1, source_target_pairs={{0,1},{1,0},{2,3},{3,2},{4,5},{5,4},{6,7},{7,6},{8,9},{9,8},{10,11... | collective-permute-start | bytes 3538952 | tf_op jit(solution)/shard_map/ppermute | solution.py:259
  52.6 6.9 %collective-permute-start = (bf16[1,8,32,384]{3,2,0,1:T(8,128)(2,1)S(1)}, bf16[1,8,32,384]{3,2,0,1:T(8,128)(2,1)S(1)}, u32[]{:S(2)}, u32[]{:S(2)}) collective-permute-start(bf16[1,8,32,384]{3,2,0,1:T(8,128)(2,1)S(1)} %get-tuple-element.38), channel_id=1, source_target_pairs={{0,2},{1,3},{2,0},{3,1},{4,6},{5,7},{6,4},{7,5},{8,10},{9,11},{10,... | collective-permute-start | bytes 589832 | tf_op jit(solution)/shard_map/ppermute | solution.py:259
  60.4 14.5 %collective-permute-start.3 = (bf16[8,96,384]{2,1,0:T(8,128)(2,1)S(1)}, bf16[8,96,384]{2,1,0:T(8,128)(2,1)S(1)}, u32[]{:S(2)}, u32[]{:S(2)}) collective-permute-start(bf16[8,96,384]{2,1,0:T(8,128)(2,1)S(1)} %get-tuple-element.48), channel_id=1, source_target_pairs={{0,4},{4,0},{8,12},{12,8},{16,20},{20,16},{24,28},{28,24},{1,5},{5... | collective-permute-start | bytes 1769480 | tf_op jit(solution)/shard_map/ppermute | solution.py:259
  61.3 15.0 %collective-permute-start.9 = (bf16[8,96,384]{2,1,0:T(8,128)(2,1)S(1)}, bf16[8,96,384]{2,1,0:T(8,128)(2,1)S(1)}, u32[]{:S(2)}, u32[]{:S(2)}) collective-permute-start(bf16[8,96,384]{2,1,0:T(8,128)(2,1)S(1)} %get-tuple-element.60), channel_id=1, source_target_pairs={{0,2},{1,3},{2,0},{3,1},{4,6},{5,7},{6,4},{7,5},{8,10},{9,11},{10,... | collective-permute-start | bytes 1769480 | tf_op jit(solution)/shard_map/ppermute | solution.py:259
  62.8 15.8 %collective-permute-start.2 = (bf16[2,4,32,384]{3,2,0,1:T(8,128)(2,1)S(1)}, bf16[2,4,32,384]{3,2,0,1:T(8,128)(2,1)S(1)}, u32[]{:S(2)}, u32[]{:S(2)}) collective-permute-start(bf16[2,4,32,384]{3,2,0,1:T(8,128)(2,1)S(1)} %get-tuple-element.46), channel_id=1, source_target_pairs={{0,16},{4,20},{8,24},{12,28},{16,0},{20,4},{24,8},{28,12},{1,17},{... | collective-permute-start | bytes 589832 | tf_op jit(solution)/shard_map/ppermute | solution.py:259
  75.6 7.3 %collective-permute-start.4 = (bf16[4,96,384]{2,1,0:T(8,128)(2,1)S(1)}, bf16[4,96,384]{2,1,0:T(8,128)(2,1)S(1)}, u32[]{:S(2)}, u32[]{:S(2)}) collective-permute-start(bf16[4,96,384]{2,1,0:T(8,128)(2,1)S(1)} %get-tuple-element.50), channel_id=1, source_target_pairs={{0,2},{1,3},{2,0},{3,1},{4,6},{5,7},{6,4},{7,5},{8,10},{9,11},{10,... | collective-permute-start | bytes 884744 | tf_op jit(solution)/shard_map/ppermute | solution.py:259
  77.0 8.0 %collective-permute-start.10 = (bf16[4,96,384]{2,1,0:T(8,128)(2,1)S(1)}, bf16[4,96,384]{2,1,0:T(8,128)(2,1)S(1)}, u32[]{:S(2)}, u32[]{:S(2)}) collective-permute-start(bf16[4,96,384]{2,1,0:T(8,128)(2,1)S(1)} %get-tuple-element.62), channel_id=1, source_target_pairs={{0,4},{4,0},{8,12},{12,8},{16,20},{20,16},{24,28},{28,24},{1,5},{5... | collective-permute-start | bytes 884744 | tf_op jit(solution)/shard_map/ppermute | solution.py:259
  83.5 11.4 %collective-permute-start.5 = (bf16[4,2,32,384]{3,2,0,1:T(8,128)(2,1)S(1)}, bf16[4,2,32,384]{3,2,0,1:T(8,128)(2,1)S(1)}, u32[]{:S(2)}, u32[]{:S(2)}) collective-permute-start(bf16[4,2,32,384]{3,2,0,1:T(8,128)(2,1)S(1)} %get-tuple-element.52), channel_id=1, source_target_pairs={{0,4},{4,0},{8,12},{12,8},{16,20},{20,16},{24,28},{28,24},{1,5},{5... | collective-permute-start | bytes 589832 | tf_op jit(solution)/shard_map/ppermute | solution.py:259
  85.6 6.9 %collective-permute-start.11 = (bf16[2,96,384]{2,1,0:T(8,128)(2,1)S(1)}, bf16[2,96,384]{2,1,0:T(8,128)(2,1)S(1)}, u32[]{:S(2)}, u32[]{:S(2)}) collective-permute-start(bf16[2,96,384]{2,1,0:T(8,128)(2,1)S(1)} %get-tuple-element.64), channel_id=1, source_target_pairs={{0,8},{4,12},{8,0},{12,4},{16,24},{20,28},{24,16},{28,20},{1,9},{5... | collective-permute-start | bytes 442376 | tf_op jit(solution)/shard_map/ppermute | solution.py:259
  85.7 8.6 %collective-permute-start.6 = (bf16[2,96,384]{2,1,0:T(8,128)(2,1)S(1)}, bf16[2,96,384]{2,1,0:T(8,128)(2,1)S(1)}, u32[]{:S(2)}, u32[]{:S(2)}) collective-permute-start(bf16[2,96,384]{2,1,0:T(8,128)(2,1)S(1)} %get-tuple-element.54), channel_id=1, source_target_pairs={{0,16},{4,20},{8,24},{12,28},{16,0},{20,4},{24,8},{28,12},{1,17},{... | collective-permute-start | bytes 442376 | tf_op jit(solution)/shard_map/ppermute | solution.py:259
  93.1 5.3 %collective-permute-start.12 = (bf16[1,96,384]{2,1,0:T(8,128)(2,1)S(1)}, bf16[1,96,384]{2,1,0:T(8,128)(2,1)S(1)}, u32[]{:S(2)}, u32[]{:S(2)}) collective-permute-start(bf16[1,96,384]{2,1,0:T(8,128)(2,1)S(1)} %get-tuple-element.66), channel_id=1, source_target_pairs={{0,16},{4,20},{8,24},{12,28},{16,0},{20,4},{24,8},{28,12},{1,17},{... | collective-permute-start | bytes 221192 | tf_op jit(solution)/shard_map/ppermute | solution.py:259
  94.9 4.4 %collective-permute-start.13 = (bf16[1,96,384]{2,1,0:T(8,128)(2,1)S(1)}, bf16[1,96,384]{2,1,0:T(8,128)(2,1)S(1)}, u32[]{:S(2)}, u32[]{:S(2)}) collective-permute-start(bf16[1,96,384]{2,1,0:T(8,128)(2,1)S(1)} %get-tuple-element.68), channel_id=1, source_target_pairs={{0,8},{4,12},{8,0},{12,4},{16,24},{20,28},{24,16},{28,20},{1,9},{5... | collective-permute-start | bytes 221192 | tf_op jit(solution)/shard_map/ppermute | solution.py:259
  96.0 4.1 %collective-permute-start.7 = (bf16[8,1,32,384]{3,2,0,1:T(8,128)(2,1)S(1)}, bf16[8,1,32,384]{3,2,0,1:T(8,128)(2,1)S(1)}, u32[]{:S(2)}, u32[]{:S(2)}) collective-permute-start(bf16[8,1,32,384]{3,2,0,1:T(8,128)(2,1)S(1)} %get-tuple-element.56), channel_id=1, source_target_pairs={{0,1},{1,0},{2,3},{3,2},{4,5},{5,4},{6,7},{7,6},{8,9},{9,8},{10,11... | collective-permute-start | bytes 589832 | tf_op jit(solution)/shard_map/ppermute | solution.py:259

commit v7 on v5

--- a/solution.py
+++ b/solution.py
@@ -12,7 +12,7 @@
 MASKS = (8, 4, 2, 1)
 LANES = 128
 CHUNK = 256
-SECTIONS_BYTES = 20 * 1024 * 1024
+SECTIONS_BYTES = 8 * 1024 * 1024
 KEEP_BYTES = 4 * 1024 * 1024
 
 
@@ -52,10 +52,9 @@
     return [member for member in range(MEMBERS) if not member & mask]
 
 
-def read_pair(ref, mask, first, rows):
-    at = pl.ds(first, rows)
-    low = jnp.concatenate([ref[member, at] for member in low_members(mask)], 0)
-    high = jnp.concatenate([ref[member | mask, at] for member in low_members(mask)], 0)
+def read_pair(ref, mask, spots=range(MEMBERS), swapped=0):
+    low = jnp.concatenate([ref[spots[member] ^ swapped] for member in low_members(mask)], 0)
+    high = jnp.concatenate([ref[spots[member | mask] ^ swapped] for member in low_members(mask)], 0)
     return jnp.concatenate([low, high], 1).astype(jnp.float32)
 
 
@@ -86,27 +85,20 @@
                 ]
 
 
-def sections_kernel(
-    spots, places_down, places_up, place_ref, both_hbm, up_hbm, down_hbm,
-    out_ref, hidden_ref, d_pre_ref, normed_t_ref, grad_t_ref, *rest
+def forward_kernel(
+    spots, place_ref, state_ref, up_hbm, down_hbm,
+    out_ref, hidden_ref, slope_ref, normed_ref, normed_t_ref, factor_ref, up_ref, down_ref, work_ref, arrived
 ):
-    blocks = rest[:-8]
-    both_ref, up_ref, down_ref, normed_ref, factor_ref, slope_ref, work_ref, arrived = rest[-8:]
-    fetch_both = pltpu.make_async_copy(both_hbm, both_ref, arrived.at[0])
-    fetch_up = pltpu.make_async_copy(up_hbm, up_ref, arrived.at[1])
-    fetch_down = pltpu.make_async_copy(down_hbm, down_ref, arrived.at[2])
-    fetch_both.start()
+    fetch_up = pltpu.make_async_copy(up_hbm, up_ref, arrived.at[0])
+    fetch_down = pltpu.make_async_copy(down_hbm, down_ref, arrived.at[1])
     fetch_up.start()
     fetch_down.start()
-    fetch_both.wait()
-    rows = work_ref.shape[1]
-    pairs = MEMBERS // 2 * rows
+    pairs = MEMBERS // 2 * work_ref.shape[1]
     hidden_units = up_ref.shape[1]
     last = len(MASKS) - 1
-
     for section, mask in enumerate(MASKS):
         at = pl.ds(section * pairs, pairs)
-        pair = read_pair(both_ref if section == 0 else work_ref, mask, 0, rows)
+        pair = read_pair(state_ref if section == 0 else work_ref, mask)
         centre = jnp.mean(pair, axis=-1, keepdims=True)
         shifted = pair - centre
         spread = jnp.mean(shifted * shifted, axis=-1, keepdims=True)
@@ -132,13 +124,22 @@
             write_pair(out_ref, mask, mixed, spots, place_ref[2])
         normed_t_ref[:, at] = normed.T
 
+
+def backward_kernel(
+    places_down, places_up, place_ref, grad_ref, hidden_ref, slope_ref, normed_ref, normed_t_ref, factor_ref,
+    up_ref, down_ref, d_pre_ref, grad_t_ref, *rest
+):
+    blocks, work_ref = rest[:-1], rest[-1]
+    pairs = MEMBERS // 2 * work_ref.shape[1]
+    hidden_units = up_ref.shape[1]
+    last = len(MASKS) - 1
     for section in range(last, -1, -1):
         mask = MASKS[section]
         at = pl.ds(section * pairs, pairs)
         if section == last:
-            pair_grad = read_pair(both_ref, mask, rows, rows)
+            pair_grad = read_pair(grad_ref, mask, swapped=place_ref[0])
         else:
-            pair_grad = read_pair(work_ref, mask, 0, rows)
+            pair_grad = read_pair(work_ref, mask)
         pair_bf = pair_grad.astype(jnp.bfloat16)
         for start in range(0, hidden_units, CHUNK):
             units = pl.ds(start, CHUNK)
@@ -167,12 +168,19 @@
     write_blocks(places_up, 1 - place_ref[1], normed_t_ref, d_pre_ref, up_ref)
 
 
-def settle_kernel(sources, place_ref, blocks_ref, out_ref, done):
-    rows = blocks_ref.shape[1]
+def arrange_kernel(spots, place_ref, block_ref, out_ref):
+    rows = out_ref.shape[1]
+    for member, spot in enumerate(spots):
+        out_ref[spot ^ place_ref[3]] = block_ref[member * rows : (member + 1) * rows]
+
+
+def settle_kernel(sources, place_ref, kept_ref, taken_ref, out_ref, done):
+    half, rows = kept_ref.shape[:2]
     copies = []
     for index, source in enumerate(sources):
+        block = kept_ref.at[index] if index < half else taken_ref.at[index - half]
         first = pl.multiple_of((place_ref[0] ^ source) * rows, rows)
-        copies.append(pltpu.make_async_copy(blocks_ref.at[index], out_ref.at[pl.ds(first, rows)], done.at[index]))
+        copies.append(pltpu.make_async_copy(block, out_ref.at[pl.ds(first, rows)], done.at[index]))
     for copy in copies:
         copy.start()
     for copy in copies:
@@ -197,39 +205,67 @@
     return places
 
 
-def sections(place, both, w_up, w_down, spots, places, block):
-    rows, width = both.shape[1] // 2, both.shape[2]
-    total = len(MASKS) * (MEMBERS // 2) * rows
+def in_vmem(*items):
+    return [pltpu.with_memory_space_constraint(item, pltpu.VMEM) for item in items]
+
+
+def forward(place, state, w_up, w_down, spots):
+    members, rows, width = state.shape
+    total = len(MASKS) * (members // 2) * rows
     depth, units = w_up.shape
     bf16 = jnp.bfloat16
     outs = [
-        pltpu.VMEM((MEMBERS, rows, width), bf16),
+        pltpu.VMEM(state.shape, bf16),
         pltpu.VMEM((total, units), bf16),
         pltpu.VMEM((total, units), bf16),
+        pltpu.VMEM((total, depth), bf16),
         pltpu.VMEM((depth, total), bf16),
-        pltpu.VMEM((depth, total), bf16),
+        pltpu.VMEM((total, LANES), jnp.float32),
+        pltpu.VMEM(w_up.shape, bf16),
+        pltpu.VMEM(w_down.shape, bf16),
     ]
-    outs += [block] * 2 if block else []
     return pl.pallas_call(
-        functools.partial(sections_kernel, spots, *places),
+        functools.partial(forward_kernel, spots),
         out_shape=outs,
-        in_specs=[spec(pltpu.SMEM)] + [spec(pltpu.HBM)] * 3,
+        in_specs=[spec(pltpu.SMEM), spec(pltpu.VMEM)] + [spec(pltpu.HBM)] * 2,
         out_specs=[spec(pltpu.VMEM)] * len(outs),
-        scratch_shapes=[
-            pltpu.VMEM(both.shape, bf16),
-            pltpu.VMEM(w_up.shape, bf16),
-            pltpu.VMEM(w_down.shape, bf16),
-            pltpu.VMEM((total, depth), bf16),
-            pltpu.VMEM((total, LANES), jnp.float32),
-            pltpu.VMEM((total, units), bf16),
-            pltpu.VMEM((MEMBERS, rows, width), bf16),
-            pltpu.SemaphoreType.DMA((3,)),
-        ],
+        scratch_shapes=[pltpu.VMEM(state.shape, bf16), pltpu.SemaphoreType.DMA((2,))],
         compiler_params=pltpu.CompilerParams(vmem_limit_bytes=SECTIONS_BYTES),
         cost_estimate=pl.CostEstimate(
             flops=10 * total * depth * units, bytes_accessed=16 * total * units, transcendentals=0
         ),
-    )(place, *[pltpu.with_memory_space_constraint(item, pltpu.HBM) for item in (both, w_up, w_down)])
+    )(place, state, *[pltpu.with_memory_space_constraint(item, pltpu.HBM) for item in (w_up, w_down)])
+
+
+def backward(place, grad, kept, places, block):
+    total, units = kept[0].shape
+    depth = kept[2].shape[1]
+    bf16 = jnp.bfloat16
+    outs = [pltpu.VMEM((total, units), bf16), pltpu.VMEM((depth, total), bf16)]
+    outs += [block] * 2 if block else []
+    return pl.pallas_call(
+        functools.partial(backward_kernel, *places),
+        out_shape=outs,
+        in_specs=[spec(pltpu.SMEM)] + [spec(pltpu.VMEM)] * (1 + len(kept)),
+        out_specs=[spec(pltpu.VMEM)] * len(outs),
+        scratch_shapes=[pltpu.VMEM(grad.shape, bf16)],
+        compiler_params=pltpu.CompilerParams(vmem_limit_bytes=SECTIONS_BYTES),
+        cost_estimate=pl.CostEstimate(
+            flops=10 * total * depth * units, bytes_accessed=16 * total * units, transcendentals=0
+        ),
+    )(place, grad, *in_vmem(*kept))
+
+
+def arrange(place, block, spots):
+    rows, width = block.shape
+    return pl.pallas_call(
+        functools.partial(arrange_kernel, spots),
+        out_shape=jax.ShapeDtypeStruct((MEMBERS, rows // MEMBERS, width), block.dtype),
+        in_specs=[spec(pltpu.SMEM), spec(pltpu.VMEM)],
+        out_specs=spec(pltpu.VMEM),
+        compiler_params=pltpu.CompilerParams(vmem_limit_bytes=KEEP_BYTES),
+        cost_estimate=pl.CostEstimate(flops=0, bytes_accessed=4 * block.size, transcendentals=0),
+    )(place, block)
 
 
 def keep_blocks(place, hidden, d_pre, normed_t, grad_t, places, block):
@@ -244,11 +280,7 @@
         cost_estimate=pl.CostEstimate(
             flops=2 * total * depth * units, bytes_accessed=8 * total * units, transcendentals=0
         ),
-    )(place, *[pltpu.with_memory_space_constraint(item, pltpu.VMEM) for item in (hidden, d_pre, normed_t, grad_t)])
-
-
-def pick(block, at):
-    return lax.dynamic_index_in_dim(block, at, 0, keepdims=False).astype(jnp.float32)
+    )(place, *in_vmem(hidden, d_pre, normed_t, grad_t))
 
 
 def swap(block, axis, bit):
@@ -256,26 +288,26 @@
     return lax.ppermute(block, axis, pairs)
 
 
-def halve(kept, taken, step):
-    axis, bit = step
-    mine = lax.axis_index(axis) // (1 << bit) % 2
-    kept = kept.reshape((2, -1) + kept.shape[1:])
-    taken = taken.reshape(kept.shape)
-    give = (pick(kept, 1 - mine) + pick(taken, 1 - mine)).astype(jnp.bfloat16)
-    keep = (pick(kept, mine) + pick(taken, mine)).astype(jnp.bfloat16)
-    return keep, give
-
-
-def finish_sum(kept, taken, order, beside=None):
+def pick(block, at):
+    size = (1,) + block.shape[1:]
+    start = (at,) + (0,) * (block.ndim - 1)
+    return lax.dynamic_slice(block, start, size, allow_negative_indices=False)[0].astype(jnp.float32)
+
+
+def finish_sum(halves, kept, taken, order, beside=None):
     for phase, step in enumerate(order):
-        kept, give = halve(kept, taken, step)
+        mine, other = halves[step]
+        shape = (2, kept.shape[0] // 2) + kept.shape[1:]
+        kept, taken = kept.reshape(shape), taken.reshape(shape)
+        give = (pick(kept, other) + pick(taken, other)).astype(jnp.bfloat16)
+        kept = (pick(kept, mine) + pick(taken, mine)).astype(jnp.bfloat16)
         if beside:
             give = beside(phase, give)
         taken = swap(give, *step)
     return (kept.astype(jnp.float32) + taken.astype(jnp.float32))[0]
 
 
-def scatter_narrow(left, right, order, span_x, span_y):
+def scatter_narrow(halves, left, right, order, span_x, span_y):
     total = jnp.dot(left, right, preferred_element_type=jnp.float32).astype(jnp.bfloat16)
     rows, columns = left.shape[0] // span_x, right.shape[1] // span_y
     count_x, count_y = span_x.bit_length() - 1, span_y.bit_length() - 1
@@ -284,38 +316,46 @@
     blocks = total.reshape((2,) * count_x + (rows,) + (2,) * count_y + (columns,))
     blocks = blocks.transpose([dims.index(item) for item in list(order) + ["rows", "columns"]])
     blocks = blocks.reshape(-1, rows, columns)
-    return finish_sum(blocks, jnp.zeros_like(blocks), order)
-
-
-class Homeward:
-    def __init__(self, state, steps):
-        self.held = state[None]
+    return finish_sum(halves, blocks, jnp.zeros_like(blocks), order)
+
+
+class Journey:
+    def __init__(self, blocks, steps):
+        self.parts = [blocks[None]]
         self.steps = list(steps)
-        self.order = []
+        self.sources = [0]
 
     def advance(self, other):
         if not self.steps:
             return other
         axis, bit, weight = self.steps.pop(0)
-        self.order.append(weight)
-        half = self.held.shape[1] // 2
-        kept, given = self.held[:, :half], self.held[:, half:]
+        held = jnp.concatenate(self.parts, 0)
+        half = held.shape[1] // 2
+        kept, given = held[:, :half], held[:, half:]
         given, other = lax.optimization_barrier((given, other))
-        self.held = jnp.concatenate([kept, swap(given, axis, bit)], 0)
+        self.parts = [kept, swap(given, axis, bit)]
+        self.sources += [source | weight for source in self.sources]
         return other
 
-    def settle(self, place):
-        blocks = self.held[:, 0]
-        members, rows, width = blocks.shape
-        sources = [sum(w for at, w in enumerate(self.order) if index >> at & 1) for index in range(members)]
-        return pl.pallas_call(
-            functools.partial(settle_kernel, sources),
-            out_shape=jax.ShapeDtypeStruct((members * rows, width), blocks.dtype),
-            in_specs=[spec(pltpu.SMEM), spec(pltpu.VMEM)],
-            out_specs=spec(pltpu.HBM),
-            scratch_shapes=[pltpu.SemaphoreType.DMA((members,))],
-            cost_estimate=pl.CostEstimate(flops=0, bytes_accessed=4 * blocks.size, transcendentals=0),
-        )(place, blocks)
+    def arrived(self):
+        return [part[:, 0] for part in self.parts]
+
+
+def settle(place, journey):
+    kept, taken = journey.arrived()
+    half, rows, width = kept.shape
+    return pl.pallas_call(
+        functools.partial(settle_kernel, journey.sources),
+        out_shape=jax.ShapeDtypeStruct((2 * half * rows, width), kept.dtype),
+        in_specs=[spec(pltpu.SMEM)] + [spec(pltpu.VMEM)] * 2,
+        out_specs=spec(pltpu.HBM),
+        scratch_shapes=[pltpu.SemaphoreType.DMA((2 * half,))],
+        cost_estimate=pl.CostEstimate(flops=0, bytes_accessed=8 * kept.size, transcendentals=0),
+    )(place, kept, taken)
+
+
+def spots_of(order):
+    return [sum((m // MASKS[at] & 1) * mask for at, mask in zip(order, MASKS)) for m in range(MEMBERS)]
 
 
 def local(signal, w_up, w_down, cotangent):
@@ -327,43 +367,49 @@
     steps = [("gx", span_x.bit_length() - 2), ("gx", 0), ("gy", span_y.bit_length() - 2), ("gy", 0)]
     bits = [lax.axis_index(axis) // (1 << bit) % 2 for axis, bit in steps]
     member = sum(bit * mask for bit, mask in zip(bits, MASKS))
-    homeward = [2, 0, 3, 1]
-    spots = [sum((m // MASKS[at] & 1) * mask for at, mask in zip(homeward, MASKS)) for m in range(MEMBERS)]
-    spot = sum(bits[at] * mask for at, mask in zip(homeward, MASKS))
-    place = jnp.stack([member, 1 - bits[3], spot]).astype(jnp.int32)
-
     rest_y = [("gy", bit) for bit in range(1, span_y.bit_length() - 1)]
     rest_x = [("gx", bit) for bit in range(1, span_x.bit_length() - 1)]
     core, across = ("gy", 0), ("gx", 0)
     order_down = [across] + rest_y + rest_x[::-1]
     order_up = rest_y + [across] + rest_x
+    inbound, homeward = [3, 2, 1, 0], [0, 2, 3, 1]
+    spot_in, spot_home = [sum(bits[at] * mask for at, mask in zip(o, MASKS)) for o in (inbound, homeward)]
+    owns = [lax.axis_index(axis) // (1 << bit) % 2 for axis, bit in [core] + order_up]
+    place = jnp.stack([member, 1 - bits[3], spot_home, spot_in]).astype(jnp.int32)
+    place, owns, others = lax.optimization_barrier((place, owns, [1 - own for own in owns]))
+    halves = {step: (own, other) for step, own, other in zip([core] + order_up, owns, others)}
     places = [block_places(order, span_x, span_y) for order in (order_down, order_up)]
     block = None
     if units // span_y % LANES == 0:
         block = pltpu.VMEM((span_x * span_y // 2, depth // span_x, units // span_y), jnp.bfloat16)
 
-    parts = (MEMBERS, rows // MEMBERS, width)
-    both = exchange(jnp.concatenate([signal.reshape(parts), cotangent.reshape(parts)], 1), groups)
-    state, hidden, d_pre, normed_t, grad_t, *given = sections(
-        place, both, w_up, w_down, spots, places, block
-    )
-    home = Homeward(state, [steps[at] + (MASKS[at],) for at in homeward])
+    state = exchange(signal.reshape(MEMBERS, rows // MEMBERS, width), groups)
+    coming = Journey(arrange(place, cotangent, spots_of(inbound)), [steps[at] + (MASKS[at],) for at in inbound])
+    for _ in range(3):
+        place = coming.advance(place)
+    state = coming.advance(state)
+    state, *kept = forward(place, state, w_up, w_down, spots_of(homeward))
+    going = Journey(state, [steps[at] + (MASKS[at],) for at in homeward])
+    going.advance(place)
+    grad = jnp.concatenate(coming.arrived(), 0)
+    d_pre, grad_t, *given = backward(place, grad, kept, places, block)
+    hidden, normed_t = kept[0], kept[3]
     if not given:
-        while home.steps:
-            home.advance(place)
-        mixed_out = home.settle(place)
-        grad_down = scatter_narrow(grad_t, hidden, [core] + order_down, span_x, span_y)
-        grad_up = scatter_narrow(normed_t, d_pre, [core] + order_up, span_x, span_y)
+        while going.steps:
+            going.advance(place)
+        mixed_out = settle(place, going)
+        grad_down = scatter_narrow(halves, grad_t, hidden, [core] + order_down, span_x, span_y)
+        grad_up = scatter_narrow(halves, normed_t, d_pre, [core] + order_up, span_x, span_y)
         return (mixed_out, grad_up, grad_down)
-    given[0] = home.advance(given[0])
+    given[0] = going.advance(given[0])
     take_down, take_up = [swap(part, *core) for part in given]
     keep_down, keep_up = keep_blocks(place, hidden, d_pre, normed_t, grad_t, places, block)
-    grad_up = finish_sum(keep_up, take_up, order_up)
-    beside = lambda phase, give: home.advance(give)
-    grad_down = finish_sum(keep_down, take_down, order_down, beside)
-    while home.steps:
-        home.advance(place)
-    return (home.settle(place), grad_up, grad_down)
+    grad_up = finish_sum(halves, keep_up, take_up, order_up)
+    beside = lambda phase, give: going.advance(give) if phase in (0, 2) else give
+    grad_down = finish_sum(halves, keep_down, take_down, order_down, beside)
+    while going.steps:
+        going.advance(place)
+    return (settle(place, going), grad_up, grad_down)
 
 
 def solution(mesh):

time: 110 us -> 94.5 us (0.86)
  waiting for transfers between devices: 48.8 us -> 40.4 us
  local copies, waits for them, and re-layouts: 9.76 us -> 1.83 us
  starting transfers between devices: 17.1 us -> 22.1 us
  other arithmetic: 8.18 us -> 3.59 us
    all_to_all x1, waiting for transfers between devices: 22.6 us -> 4.17 us  [exchange(): lax.all_to_all(block, ('gx', 'gy'), split_axis=0, concat_axis=0, axis_ind...]
    ppermute x14 -> x18, waiting for transfers between devices: 26.2 us -> 36.3 us  [swap(): return lax.ppermute(block, axis, pairs)]
    unnamed x18 -> x6, local copies, waits for them, and re-layouts: 9.72 us -> 1.7 us
    ppermute x14 -> x18, starting transfers between devices: 9.76 us -> 17.2 us  [swap(): return lax.ppermute(block, axis, pairs)]
    convert_element_type x8, other arithmetic: 3.67 us -> 1.15 us  [the longest x6 1.11 us: finish_sum(): kept = (pick(kept, mine) + pick(taken, mine)).astype(jnp.bfloat16)]
    all_to_all x1, starting transfers between devices: 7.34 us -> 4.93 us  [exchange(): lax.all_to_all(block, ('gx', 'gy'), split_axis=0, concat_axis=0, axis_ind...]
    concatenate x4 -> x7, other arithmetic: 2.26 us -> 0.98 us  [the longest x6 0.93 us: advance(): held = jnp.concatenate(self.parts, 0)]
    pallas_call x2 -> x4, Pallas kernels: 21.4 us -> 22.2 us  [the longest x1 10.3 us: forward(): pl.pallas_call(functools.partial(forward_kernel, spots), out_shape=outs,...]
  transfers between devices with their start and end apart: 15 -> 19, of which waited for: 9 -> 11; matrix products, arithmetic and copies ran while one was open for 5% -> 3% of each run, Pallas kernels for 5% -> 26%
where the time goes in v7:
time: 94.5 us; the launch traced here: 94.3 us
  waiting for transfers between devices  40.4 us (43%)
  Pallas kernels  25.4 us (27%)
  starting transfers between devices  22.1 us (23%)
  other arithmetic  3.59 us (4%)
  local copies, waits for them, and re-layouts  1.83 us (2%)
    ppermute x18, waiting for transfers between devices, swap(): return lax.ppermute(block, axis, pairs)  36.3 us
    ppermute x18, starting transfers between devices, swap(): return lax.ppermute(block, axis, pairs)  17.2 us
    pallas_call x1, Pallas kernels, forward(): pl.pallas_call(functools.partial(forward_kernel, spots), out_shape=outs,...  10.3 us
    pallas_call x1, Pallas kernels, backward(): pl.pallas_call(functools.partial(backward_kernel, *places), out_shape=out...  9.43 us
    all_to_all x1, starting transfers between devices, exchange(): lax.all_to_all(block, ('gx', 'gy'), split_axis=0, concat_axis=0, axis_ind...  4.93 us
    all_to_all x1, waiting for transfers between devices, exchange(): lax.all_to_all(block, ('gx', 'gy'), split_axis=0, concat_axis=0, axis_ind...  4.17 us
    pallas_call x1, Pallas kernels, keep_blocks(): pl.pallas_call(functools.partial(keep_kernel, *places), out_shape=[block]...  3.17 us
    pallas_call x1, Pallas kernels, settle(): pl.pallas_call(functools.partial(settle_kernel, journey.sources), out_sha...  1.9 us
  transfers between devices with their start and end apart: 19, of which 11 were waited for; matrix products, arithmetic and copies ran while one was open for 3% of the time, Pallas kernels for 26%

profile of v7, /device:TPU:0, one launch (start us, length us, event | category | flops | bytes accessed | tf_op | source)
XLA Modules:
  0.0 94.3 jit_solution(6880667496618914633)
XLA Ops:
  0.8 1.0 %copy-done = bf16[512,384]{1,0:T(8,128)(2,1)S(1)} copy-done((bf16[512,384]{1,0:T(8,128)(2,1)S(1)}, bf16[512,384]{1,0:T(8,128)(2,1)}, u32[]{:S(2)}) %copy-start) | copy-done | bytes 393240
  1.8 0.6 shard_map.67
  2.4 0.5 collective-permute-start
  3.0 1.1 %collective-permute-done = bf16[1,8,32,384]{3,2,0,1:T(8,128)(2,1)S(1)} collective-permute-done((bf16[1,8,32,384]{3,2,0,1:T(8,128)(2,1)S(1)}, bf16[1,8,32,384]{3,2,0,1:T(8,128)(2,1)S(1)}, u32[]{:S(2)}, u32[]{:S(2)}) %collective-permute-start) | collective-permute-done | bytes 196640 | tf_op jit(solution)/shard_map/ppermute | solution.py:288
  4.1 2.9 %collective-permute-start.1 = (bf16[2,4,32,384]{3,2,0,1:T(8,128)(2,1)S(1)}, bf16[2,4,32,384]{3,2,0,1:T(8,128)(2,1)S(1)}, u32[]{:S(2)}, u32[]{:S(2)}) collective-permute-start(bf16[2,4,32,384]{3,2,0,1:T(8,128)(2,1)S(1)} %get-tuple-element.44), channel_id=1, source_target_pairs={{0,2},{1,3},{2,0},{3,1},{4,6},{5,7},{6,4},{7,5},{8,10},{9,11},{10,... | collective-permute-start | bytes 589832 | tf_op jit(solution)/shard_map/ppermute | solution.py:288
  7.0 4.9 %all-to-all-start = ((bf16[16,32,384]{2,1,0:T(8,128)(2,1)}), bf16[16,32,384]{2,1,0:T(8,128)(2,1)S(1)}, u32[]{:S(2)}, u32[]{:S(2)}) async-start(bf16[16,32,384]{2,1,0:T(8,128)(2,1)} %bitcast.5), calls=%async_computation | async-start | bytes 786432 | tf_op jit(solution)/shard_map/all_to_all | solution.py:40
  12.2 1.8 %collective-permute-start.2 = (bf16[4,2,32,384]{3,2,0,1:T(8,128)(2,1)S(1)}, bf16[4,2,32,384]{3,2,0,1:T(8,128)(2,1)S(1)}, u32[]{:S(2)}, u32[]{:S(2)}) collective-permute-start(bf16[4,2,32,384]{3,2,0,1:T(8,128)(2,1)S(1)} %fusion.9), channel_id=1, source_target_pairs={{0,4},{4,0},{8,12},{12,8},{16,20},{20,16},{24,28},{28,24},{1,5},{5... | collective-permute-start | bytes 589832 | tf_op jit(solution)/shard_map/ppermute | solution.py:288
  14.1 7.8 %collective-permute-done.2 = bf16[4,2,32,384]{3,2,0,1:T(8,128)(2,1)S(1)} collective-permute-done((bf16[4,2,32,384]{3,2,0,1:T(8,128)(2,1)S(1)}, bf16[4,2,32,384]{3,2,0,1:T(8,128)(2,1)S(1)}, u32[]{:S(2)}, u32[]{:S(2)}) %collective-permute-start.2) | collective-permute-done | bytes 196640 | tf_op jit(solution)/shard_map/ppermute | solution.py:288
  22.0 4.2 %all-to-all-done.state_ref = bf16[16,32,384]{2,1,0:T(8,128)(2,1)S(1)} async-done(((bf16[16,32,384]{2,1,0:T(8,128)(2,1)}), bf16[16,32,384]{2,1,0:T(8,128)(2,1)S(1)}, u32[]{:S(2)}, u32[]{:S(2)}) %all-to-all-start) | async-done | bytes 393248 | tf_op jit(solution)/shard_map/all_to_all | solution.py:40
  26.2 10.3 %shard_map.68 = (bf16[16,32,384]{2,1,0:T(8,128)(2,1)S(1)}, bf16[1024,1536]{1,0:T(8,128)(2,1)S(1)}, bf16[1024,1536]{1,0:T(8,128)(2,1)S(1)}, bf16[1024,768]{1,0:T(...) custom-call(s32[4]{0:T(128)S(1)} %pad_add_fusion.place_ref, ...), custom_call_target="tpu_custom_call" | custom-call | flops 12079595520 | bytes 25165824 | tf_op jit(solution)/shard_map/pallas_call | solution.py:227
  36.6 3.0 %collective-permute-start.3 = (bf16[1,8,32,384]{3,2,0,1:T(8,128)(2,1)S(1)}, bf16[1,8,32,384]{3,2,0,1:T(8,128)(2,1)S(1)}, u32[]{:S(2)}, u32[]{:S(2)}) collective-permute-start(bf16[1,8,32,384]{3,2,0,1:T(8,128)(2,1)S(1)} %get-tuple-element.50), channel_id=1, source_target_pairs={{0,16},{4,20},{8,24},{12,28},{16,0},{20,4},{24,8},{28,12},{1,17},{... | collective-permute-start | bytes 589832 | tf_op jit(solution)/shard_map/ppermute | solution.py:288
  39.6 9.4 %shard_map.69 = (bf16[1024,1536]{1,0:T(8,128)(2,1)S(1)}, bf16[768,1024]{1,0:T(8,128)(2,1)S(1)}, bf16[16,96,384]{2,1,0:T(8,128)(2,1)S(1)}, bf16[16,96,384]{2,1,0:T(8,128)(2,1)S(1)}) custom-call(s32[4]{0:T(128)S(1)} %pad_add_fusion.place_ref, bf16[16,32,384]{2,1,0:T(8,128)(2,1)S(1)} %pad_maximum_fusion.1.grad_ref, ...), custom_call_target="tpu_custom_call" | custom-call | flops 12079595520 | bytes 25165824 | tf_op jit(solution)/shard_map/pallas_call | solution.py:246
  49.2 0.5 collective-permute-start.11
  49.7 0.6 collective-permute-start.5
  50.3 3.2 %shard_map.70 = (bf16[16,96,384]{2,1,0:T(8,128)(2,1)S(1)}, bf16[16,96,384]{2,1,0:T(8,128)(2,1)S(1)}) custom-call(s32[4]{0:T(128)S(1)} %pad_add_fusion.place_ref, bf16[1024,1536]{1,0:T(8,128)(2,1)S(1)} %get-tuple-element.52.hidden_ref, bf16[1024,1536]{1,0:T(8,128)(2,1)S(1)} %get-tuple-element.61.d_pre_ref, ...), custom_call_target="tpu_custom_call" | custom-call | flops 2415919104 | bytes 12582912 | tf_op jit(solution)/shard_map/pallas_call | solution.py:274
  53.4 3.1 %collective-permute-done.5 = bf16[2,4,32,384]{3,2,0,1:T(8,128)(2,1)S(1)} collective-permute-done((bf16[2,4,32,384]{3,2,0,1:T(8,128)(2,1)S(1)}, bf16[2,4,32,384]{3,2,0,1:T(8,128)(2,1)S(1)}, u32[]{:S(2)}, u32[]{:S(2)}) %collective-permute-start.5) | collective-permute-done | bytes 196640 | tf_op jit(solution)/shard_map/ppermute | solution.py:288
  57.4 0.9 %collective-permute-start.12 = (bf16[8,96,384]{2,1,0:T(8,128)(2,1)S(1)}, bf16[8,96,384]{2,1,0:T(8,128)(2,1)S(1)}, u32[]{:S(2)}, u32[]{:S(2)}) collective-permute-start(bf16[8,96,384]{2,1,0:T(8,128)(2,1)S(1)} %get-tuple-element.80), channel_id=1, source_target_pairs={{0,2},{1,3},{2,0},{3,1},{4,6},{5,7},{6,4},{7,5},{8,10},{9,11},{10,... | collective-permute-start | bytes 1769480 | tf_op jit(solution)/shard_map/ppermute | solution.py:288
  58.3 13.2 %collective-permute-done.8 = bf16[8,96,384]{2,1,0:T(8,128)(2,1)S(1)} collective-permute-done((bf16[8,96,384]{2,1,0:T(8,128)(2,1)S(1)}, bf16[8,96,384]{2,1,0:T(8,128)(2,1)S(1)}, u32[]{:S(2)}, u32[]{:S(2)}) %collective-permute-start.8) | collective-permute-done | bytes 589856 | tf_op jit(solution)/shard_map/ppermute | solution.py:288
  71.7 0.6 collective-permute-start.9
  72.5 1.8 %collective-permute-start.13 = (bf16[4,96,384]{2,1,0:T(8,128)(2,1)S(1)}, bf16[4,96,384]{2,1,0:T(8,128)(2,1)S(1)}, u32[]{:S(2)}, u32[]{:S(2)}) collective-permute-start(bf16[4,96,384]{2,1,0:T(8,128)(2,1)S(1)} %get-tuple-element.84), channel_id=1, source_target_pairs={{0,4},{4,0},{8,12},{12,8},{16,20},{20,16},{24,28},{28,24},{1,5},{5... | collective-permute-start | bytes 884744 | tf_op jit(solution)/shard_map/ppermute | solution.py:288
  74.2 0.7 pad_maximum_fusion.2
  74.9 4.0 %collective-permute-done.9 = bf16[4,96,384]{2,1,0:T(8,128)(2,1)S(1)} collective-permute-done((bf16[4,96,384]{2,1,0:T(8,128)(2,1)S(1)}, bf16[4,96,384]{2,1,0:T(8,128)(2,1)S(1)}, u32[]{:S(2)}, u32[]{:S(2)}) %collective-permute-start.9) | collective-permute-done | bytes 294944 | tf_op jit(solution)/shard_map/ppermute | solution.py:288
  79.5 1.7 %collective-permute-start.14 = (bf16[2,96,384]{2,1,0:T(8,128)(2,1)S(1)}, bf16[2,96,384]{2,1,0:T(8,128)(2,1)S(1)}, u32[]{:S(2)}, u32[]{:S(2)}) collective-permute-start(bf16[2,96,384]{2,1,0:T(8,128)(2,1)S(1)} %get-tuple-element.90), channel_id=1, source_target_pairs={{0,8},{4,12},{8,0},{12,4},{16,24},{20,28},{24,16},{28,20},{1,9},{5... | collective-permute-start | bytes 442376 | tf_op jit(solution)/shard_map/ppermute | solution.py:288
  81.3 1.0 %collective-permute-start.10 = (bf16[8,1,32,384]{3,2,0,1:T(8,128)(2,1)S(1)}, bf16[8,1,32,384]{3,2,0,1:T(8,128)(2,1)S(1)}, u32[]{:S(2)}, u32[]{:S(2)}) collective-permute-start(bf16[8,1,32,384]{3,2,0,1:T(8,128)(2,1)S(1)} %get-tuple-element.72), channel_id=1, source_target_pairs={{0,4},{4,0},{8,12},{12,8},{16,20},{20,16},{24,28},{28,24},{1,5},{5... | collective-permute-start | bytes 589832 | tf_op jit(solution)/shard_map/ppermute | solution.py:288
  82.3 3.9 %collective-permute-done.16 = bf16[2,96,384]{2,1,0:T(8,128)(2,1)S(1)} collective-permute-done((bf16[2,96,384]{2,1,0:T(8,128)(2,1)S(1)}, bf16[2,96,384]{2,1,0:T(8,128)(2,1)S(1)}, u32[]{:S(2)}, u32[]{:S(2)}) %collective-permute-start.16) | collective-permute-done | bytes 147488 | tf_op jit(solution)/shard_map/ppermute | solution.py:288
  86.3 1.2 %collective-permute-done.14 = bf16[2,96,384]{2,1,0:T(8,128)(2,1)S(1)} collective-permute-done((bf16[2,96,384]{2,1,0:T(8,128)(2,1)S(1)}, bf16[2,96,384]{2,1,0:T(8,128)(2,1)S(1)}, u32[]{:S(2)}, u32[]{:S(2)}) %collective-permute-start.14) | collective-permute-done | bytes 147488 | tf_op jit(solution)/shard_map/ppermute | solution.py:288
  87.5 1.5 %collective-permute-start.15 = (bf16[1,96,384]{2,1,0:T(8,128)(2,1)S(1)}, bf16[1,96,384]{2,1,0:T(8,128)(2,1)S(1)}, u32[]{:S(2)}, u32[]{:S(2)}) collective-permute-start(bf16[1,96,384]{2,1,0:T(8,128)(2,1)S(1)} %fusion.15), channel_id=1, source_target_pairs={{0,16},{4,20},{8,24},{12,28},{16,0},{20,4},{24,8},{28,12},{1,17},{... | collective-permute-start | bytes 221192 | tf_op jit(solution)/shard_map/ppermute | solution.py:288
  88.9 0.7 copy-done.2
  89.6 1.9 %shard_map.71 = bf16[512,384]{1,0:T(8,128)(2,1)} custom-call(s32[4]{0:T(128)} %copy-done.1, bf16[8,32,384]{2,1,0:T(8,128)(2,1)} %get-tuple-element.92.kept_ref, bf16[8,32,384]{2,1,0:T(8,128)(2,1)} %bitcast.67), custom_call_target="tpu_custom_call" | custom-call | bytes 786432 | tf_op jit(solution)/shard_map/pallas_call | solution.py:347
  91.6 0.7 add_bitcast_fusion
  92.3 1.3 %collective-permute-done.15 = bf16[1,96,384]{2,1,0:T(8,128)(2,1)S(1)} collective-permute-done((bf16[1,96,384]{2,1,0:T(8,128)(2,1)S(1)}, bf16[1,96,384]{2,1,0:T(8,128)(2,1)S(1)}, u32[]{:S(2)}, u32[]{:S(2)}) %collective-permute-start.15) | collective-permute-done | bytes 73760 | tf_op jit(solution)/shard_map/ppermute | solution.py:288
  93.6 0.7 add_bitcast_fusion.1
  (38 shorter events, 2.6 us)
Async XLA Ops:
  0.8 1.0 %copy-start = (bf16[512,384]{1,0:T(8,128)(2,1)S(1)}, bf16[512,384]{1,0:T(8,128)(2,1)}, u32[]{:S(2)}) copy-start(bf16[512,384]{1,0:T(8,128)(2,1)} %block_ref.1) | copy-start | bytes 1179652
  1.8 48.5 %copy-start.1 = (s32[4]{0:T(128)}, s32[4]{0:T(128)S(1)}, u32[]{:S(2)}) copy-start(s32[4]{0:T(128)S(1)} %pad_add_fusion.place_ref) | copy-start | bytes 52
  2.4 1.6 %collective-permute-start = (bf16[1,8,32,384]{3,2,0,1:T(8,128)(2,1)S(1)}, bf16[1,8,32,384]{3,2,0,1:T(8,128)(2,1)S(1)}, u32[]{:S(2)}, u32[]{:S(2)}) collective-permute-start(bf16[1,8,32,384]{3,2,0,1:T(8,128)(2,1)S(1)} %get-tuple-element.42), channel_id=1, source_target_pairs={{0,1},{1,0},{2,3},{3,2},{4,5},{5,4},{6,7},{7,6},{8,9},{9,8},{10,11... | collective-permute-start | bytes 589832 | tf_op jit(solution)/shard_map/ppermute | solution.py:288
  4.1 8.1 %collective-permute-start.1 = (bf16[2,4,32,384]{3,2,0,1:T(8,128)(2,1)S(1)}, bf16[2,4,32,384]{3,2,0,1:T(8,128)(2,1)S(1)}, u32[]{:S(2)}, u32[]{:S(2)}) collective-permute-start(bf16[2,4,32,384]{3,2,0,1:T(8,128)(2,1)S(1)} %get-tuple-element.44), channel_id=1, source_target_pairs={{0,2},{1,3},{2,0},{3,1},{4,6},{5,7},{6,4},{7,5},{8,10},{9,11},{10,... | collective-permute-start | bytes 589832 | tf_op jit(solution)/shard_map/ppermute | solution.py:288
  7.0 19.2 %all-to-all-start = ((bf16[16,32,384]{2,1,0:T(8,128)(2,1)}), bf16[16,32,384]{2,1,0:T(8,128)(2,1)S(1)}, u32[]{:S(2)}, u32[]{:S(2)}) async-start(bf16[16,32,384]{2,1,0:T(8,128)(2,1)} %bitcast.5), calls=%async_computation | async-start | bytes 786432 | tf_op jit(solution)/shard_map/all_to_all | solution.py:40
  12.2 9.7 %collective-permute-start.2 = (bf16[4,2,32,384]{3,2,0,1:T(8,128)(2,1)S(1)}, bf16[4,2,32,384]{3,2,0,1:T(8,128)(2,1)S(1)}, u32[]{:S(2)}, u32[]{:S(2)}) collective-permute-start(bf16[4,2,32,384]{3,2,0,1:T(8,128)(2,1)S(1)} %fusion.9), channel_id=1, source_target_pairs={{0,4},{4,0},{8,12},{12,8},{16,20},{20,16},{24,28},{28,24},{1,5},{5... | collective-permute-start | bytes 589832 | tf_op jit(solution)/shard_map/ppermute | solution.py:288
  26.2 13.4 %collective-permute-start.4 = (bf16[8,1,32,384]{3,2,0,1:T(8,128)(2,1)S(1)}, bf16[8,1,32,384]{3,2,0,1:T(8,128)(2,1)S(1)}, u32[]{:S(2)}, u32[]{:S(2)}) collective-permute-start(bf16[8,1,32,384]{3,2,0,1:T(8,128)(2,1)S(1)} %get-tuple-element.51), channel_id=1, source_target_pairs={{0,16},{4,20},{8,24},{12,28},{16,0},{20,4},{24,8},{28,12},{1,17},{... | collective-permute-start | bytes 589832 | tf_op jit(solution)/shard_map/ppermute | solution.py:288
  36.6 12.5 %collective-permute-start.3 = (bf16[1,8,32,384]{3,2,0,1:T(8,128)(2,1)S(1)}, bf16[1,8,32,384]{3,2,0,1:T(8,128)(2,1)S(1)}, u32[]{:S(2)}, u32[]{:S(2)}) collective-permute-start(bf16[1,8,32,384]{3,2,0,1:T(8,128)(2,1)S(1)} %get-tuple-element.50), channel_id=1, source_target_pairs={{0,16},{4,20},{8,24},{12,28},{16,0},{20,4},{24,8},{28,12},{1,17},{... | collective-permute-start | bytes 589832 | tf_op jit(solution)/shard_map/ppermute | solution.py:288
  49.1 7.5 %collective-permute-start.6 = (bf16[16,96,384]{2,1,0:T(8,128)(2,1)S(1)}, bf16[16,96,384]{2,1,0:T(8,128)(2,1)S(1)}, u32[]{:S(2)}, u32[]{:S(2)}) collective-permute-start(bf16[16,96,384]{2,1,0:T(8,128)(2,1)S(1)} %get-tuple-element.65), channel_id=1, source_target_pairs={{0,1},{1,0},{2,3},{3,2},{4,5},{5,4},{6,7},{7,6},{8,9},{9,8},{10,11... | collective-permute-start | bytes 3538952 | tf_op jit(solution)/shard_map/ppermute | solution.py:288
  49.2 7.9 %collective-permute-start.11 = (bf16[16,96,384]{2,1,0:T(8,128)(2,1)S(1)}, bf16[16,96,384]{2,1,0:T(8,128)(2,1)S(1)}, u32[]{:S(2)}, u32[]{:S(2)}) collective-permute-start(bf16[16,96,384]{2,1,0:T(8,128)(2,1)S(1)} %get-tuple-element.74), channel_id=1, source_target_pairs={{0,1},{1,0},{2,3},{3,2},{4,5},{5,4},{6,7},{7,6},{8,9},{9,8},{10,11... | collective-permute-start | bytes 3538952 | tf_op jit(solution)/shard_map/ppermute | solution.py:288
  49.7 6.9 %collective-permute-start.5 = (bf16[2,4,32,384]{3,2,0,1:T(8,128)(2,1)S(1)}, bf16[2,4,32,384]{3,2,0,1:T(8,128)(2,1)S(1)}, u32[]{:S(2)}, u32[]{:S(2)}) collective-permute-start(bf16[2,4,32,384]{3,2,0,1:T(8,128)(2,1)S(1)} %get-tuple-element.60), channel_id=1, source_target_pairs={{0,2},{1,3},{2,0},{3,1},{4,6},{5,7},{6,4},{7,5},{8,10},{9,11},{10,... | collective-permute-start | bytes 589832 | tf_op jit(solution)/shard_map/ppermute | solution.py:288
  57.0 14.5 %collective-permute-start.8 = (bf16[8,96,384]{2,1,0:T(8,128)(2,1)S(1)}, bf16[8,96,384]{2,1,0:T(8,128)(2,1)S(1)}, u32[]{:S(2)}, u32[]{:S(2)}) collective-permute-start(bf16[8,96,384]{2,1,0:T(8,128)(2,1)S(1)} %get-tuple-element.69), channel_id=1, source_target_pairs={{0,4},{4,0},{8,12},{12,8},{16,20},{20,16},{24,28},{28,24},{1,5},{5... | collective-permute-start | bytes 1769480 | tf_op jit(solution)/shard_map/ppermute | solution.py:288
  57.4 14.9 %collective-permute-start.12 = (bf16[8,96,384]{2,1,0:T(8,128)(2,1)S(1)}, bf16[8,96,384]{2,1,0:T(8,128)(2,1)S(1)}, u32[]{:S(2)}, u32[]{:S(2)}) collective-permute-start(bf16[8,96,384]{2,1,0:T(8,128)(2,1)S(1)} %get-tuple-element.80), channel_id=1, source_target_pairs={{0,2},{1,3},{2,0},{3,1},{4,6},{5,7},{6,4},{7,5},{8,10},{9,11},{10,... | collective-permute-start | bytes 1769480 | tf_op jit(solution)/shard_map/ppermute | solution.py:288
  58.3 15.9 %collective-permute-start.7 = (bf16[4,2,32,384]{3,2,0,1:T(8,128)(2,1)S(1)}, bf16[4,2,32,384]{3,2,0,1:T(8,128)(2,1)S(1)}, u32[]{:S(2)}, u32[]{:S(2)}) collective-permute-start(bf16[4,2,32,384]{3,2,0,1:T(8,128)(2,1)S(1)} %get-tuple-element.66), channel_id=1, source_target_pairs={{0,1},{1,0},{2,3},{3,2},{4,5},{5,4},{6,7},{7,6},{8,9},{9,8},{10,11... | collective-permute-start | bytes 589832 | tf_op jit(solution)/shard_map/ppermute | solution.py:288
  71.7 7.3 %collective-permute-start.9 = (bf16[4,96,384]{2,1,0:T(8,128)(2,1)S(1)}, bf16[4,96,384]{2,1,0:T(8,128)(2,1)S(1)}, u32[]{:S(2)}, u32[]{:S(2)}) collective-permute-start(bf16[4,96,384]{2,1,0:T(8,128)(2,1)S(1)} %get-tuple-element.86), channel_id=1, source_target_pairs={{0,2},{1,3},{2,0},{3,1},{4,6},{5,7},{6,4},{7,5},{8,10},{9,11},{10,... | collective-permute-start | bytes 884744 | tf_op jit(solution)/shard_map/ppermute | solution.py:288
  72.5 7.0 %collective-permute-start.13 = (bf16[4,96,384]{2,1,0:T(8,128)(2,1)S(1)}, bf16[4,96,384]{2,1,0:T(8,128)(2,1)S(1)}, u32[]{:S(2)}, u32[]{:S(2)}) collective-permute-start(bf16[4,96,384]{2,1,0:T(8,128)(2,1)S(1)} %get-tuple-element.84), channel_id=1, source_target_pairs={{0,4},{4,0},{8,12},{12,8},{16,20},{20,16},{24,28},{28,24},{1,5},{5... | collective-permute-start | bytes 884744 | tf_op jit(solution)/shard_map/ppermute | solution.py:288
  79.0 7.1 %collective-permute-start.16 = (bf16[2,96,384]{2,1,0:T(8,128)(2,1)S(1)}, bf16[2,96,384]{2,1,0:T(8,128)(2,1)S(1)}, u32[]{:S(2)}, u32[]{:S(2)}) collective-permute-start(bf16[2,96,384]{2,1,0:T(8,128)(2,1)S(1)} %get-tuple-element.78), channel_id=1, source_target_pairs={{0,16},{4,20},{8,24},{12,28},{16,0},{20,4},{24,8},{28,12},{1,17},{... | collective-permute-start | bytes 442376 | tf_op jit(solution)/shard_map/ppermute | solution.py:288
  79.5 7.9 %collective-permute-start.14 = (bf16[2,96,384]{2,1,0:T(8,128)(2,1)S(1)}, bf16[2,96,384]{2,1,0:T(8,128)(2,1)S(1)}, u32[]{:S(2)}, u32[]{:S(2)}) collective-permute-start(bf16[2,96,384]{2,1,0:T(8,128)(2,1)S(1)} %get-tuple-element.90), channel_id=1, source_target_pairs={{0,8},{4,12},{8,0},{12,4},{16,24},{20,28},{24,16},{28,20},{1,9},{5... | collective-permute-start | bytes 442376 | tf_op jit(solution)/shard_map/ppermute | solution.py:288
  81.3 7.7 %collective-permute-start.10 = (bf16[8,1,32,384]{3,2,0,1:T(8,128)(2,1)S(1)}, bf16[8,1,32,384]{3,2,0,1:T(8,128)(2,1)S(1)}, u32[]{:S(2)}, u32[]{:S(2)}) collective-permute-start(bf16[8,1,32,384]{3,2,0,1:T(8,128)(2,1)S(1)} %get-tuple-element.72), channel_id=1, source_target_pairs={{0,4},{4,0},{8,12},{12,8},{16,20},{20,16},{24,28},{28,24},{1,5},{5... | collective-permute-start | bytes 589832 | tf_op jit(solution)/shard_map/ppermute | solution.py:288
  86.2 5.4 %collective-permute-start.17 = (bf16[1,96,384]{2,1,0:T(8,128)(2,1)S(1)}, bf16[1,96,384]{2,1,0:T(8,128)(2,1)S(1)}, u32[]{:S(2)}, u32[]{:S(2)}) collective-permute-start(bf16[1,96,384]{2,1,0:T(8,128)(2,1)S(1)} %fusion.13), channel_id=1, source_target_pairs={{0,8},{4,12},{8,0},{12,4},{16,24},{20,28},{24,16},{28,20},{1,9},{5... | collective-permute-start | bytes 221192 | tf_op jit(solution)/shard_map/ppermute | solution.py:288
  87.5 6.1 %collective-permute-start.15 = (bf16[1,96,384]{2,1,0:T(8,128)(2,1)S(1)}, bf16[1,96,384]{2,1,0:T(8,128)(2,1)S(1)}, u32[]{:S(2)}, u32[]{:S(2)}) collective-permute-start(bf16[1,96,384]{2,1,0:T(8,128)(2,1)S(1)} %fusion.15), channel_id=1, source_target_pairs={{0,16},{4,20},{8,24},{12,28},{16,0},{20,4},{24,8},{28,12},{1,17},{... | collective-permute-start | bytes 221192 | tf_op jit(solution)/shard_map/ppermute | solution.py:288
  88.9 0.7 copy-start.2

commit v8 on v7

--- a/solution.py
+++ b/solution.py
@@ -66,7 +66,7 @@
         ref[spots[member | mask] ^ swapped] = part[:, width:]
 
 
-def write_blocks(places, bit, left_ref, right_ref, out_ref):
+def write_blocks(places, bit, products, out_ref):
     rows, columns = out_ref.shape[1:]
     pieces = []
     for group in range(len(places[0])):
@@ -75,8 +75,10 @@
             pieces.append((group, inner, pl.multiple_of(base + inner, LANES)))
     for first in range(0, len(pieces), 2):
         some = pieces[first : first + 2]
-        right = jnp.concatenate([right_ref[:, pl.ds(start, LANES)] for _, _, start in some], 1)
-        total = jnp.dot(left_ref[...], right, preferred_element_type=jnp.float32)
+        total = 0.0
+        for left_ref, right_ref in products:
+            right = jnp.concatenate([right_ref[:, pl.ds(start, LANES)] for _, _, start in some], 1)
+            total += jnp.dot(left_ref[...], right, preferred_element_type=jnp.float32)
         total = total.astype(jnp.bfloat16)
         for which, (group, inner, _) in enumerate(some):
             for block in range(len(places)):
@@ -89,12 +91,16 @@
     spots, place_ref, state_ref, up_hbm, down_hbm,
     out_ref, hidden_ref, slope_ref, normed_ref, normed_t_ref, factor_ref, up_ref, down_ref, work_ref, arrived
 ):
-    fetch_up = pltpu.make_async_copy(up_hbm, up_ref, arrived.at[0])
-    fetch_down = pltpu.make_async_copy(down_hbm, down_ref, arrived.at[1])
-    fetch_up.start()
-    fetch_down.start()
     pairs = MEMBERS // 2 * work_ref.shape[1]
     hidden_units = up_ref.shape[1]
+    starts = range(0, hidden_units, CHUNK)
+    fetches = []
+    for which, (source, target) in enumerate(((up_hbm, up_ref), (down_hbm, down_ref))):
+        for place, start in enumerate(starts):
+            units = pl.ds(start, CHUNK)
+            copy = pltpu.make_async_copy(source.at[:, units], target.at[:, units], arrived.at[which, place])
+            copy.start()
+            fetches.append(copy)
     last = len(MASKS) - 1
     for section, mask in enumerate(MASKS):
         at = pl.ds(section * pairs, pairs)
@@ -106,17 +112,18 @@
         normed = (shifted * factor).astype(jnp.bfloat16)
         normed_ref[at, :] = normed
         factor_ref[at, :] = jnp.broadcast_to(factor, (pairs, LANES))
-        if section == 0:
-            fetch_up.wait()
-        for start in range(0, hidden_units, CHUNK):
+        for place, start in enumerate(starts):
             units = pl.ds(start, CHUNK)
+            if section == 0:
+                fetches[place].wait()
             pre = jnp.dot(normed, up_ref[:, units], preferred_element_type=jnp.float32)
             share = 0.5 * (1.0 + lax.erf(pre * (1.0 / math.sqrt(2.0))))
             hidden_ref[at, units] = (pre * share).astype(jnp.bfloat16)
             bell = jnp.exp(-0.5 * pre * pre) * (1.0 / math.sqrt(2.0 * math.pi))
             slope_ref[at, units] = (share + pre * bell).astype(jnp.bfloat16)
         if section == 0:
-            fetch_down.wait()
+            for copy in fetches[len(starts) :]:
+                copy.wait()
         mixed = (pair + contract_last(hidden_ref[at, :], down_ref[...])).astype(jnp.bfloat16)
         if section < last:
             write_pair(work_ref, mask, mixed)
@@ -126,46 +133,65 @@
 
 
 def backward_kernel(
-    places_down, places_up, place_ref, grad_ref, hidden_ref, slope_ref, normed_ref, normed_t_ref, factor_ref,
-    up_ref, down_ref, d_pre_ref, grad_t_ref, *rest
+    places, place_ref, grad_ref, hidden_ref, slope_ref, normed_ref, factor_ref, up_ref, down_ref,
+    d_pre_ref, grad_t_ref, last_ref, *rest
 ):
     blocks, work_ref = rest[:-1], rest[-1]
     pairs = MEMBERS // 2 * work_ref.shape[1]
-    hidden_units = up_ref.shape[1]
-    last = len(MASKS) - 1
-    for section in range(last, -1, -1):
+    for section in range(len(MASKS) - 1, 0, -1):
         mask = MASKS[section]
         at = pl.ds(section * pairs, pairs)
-        if section == last:
+        later = pl.ds((section - 1) * pairs, pairs)
+        if section == len(MASKS) - 1:
             pair_grad = read_pair(grad_ref, mask, swapped=place_ref[0])
         else:
             pair_grad = read_pair(work_ref, mask)
         pair_bf = pair_grad.astype(jnp.bfloat16)
-        for start in range(0, hidden_units, CHUNK):
+        for start in range(0, up_ref.shape[1], CHUNK):
             units = pl.ds(start, CHUNK)
             d_hidden = jnp.dot(pair_bf, down_ref[:, units], preferred_element_type=jnp.float32)
-            d_pre_ref[at, units] = (d_hidden * slope_ref[at, units].astype(jnp.float32)).astype(jnp.bfloat16)
-        if section > 0:
-            d_norm = contract_last(d_pre_ref[at, :], up_ref[...])
-            normed = normed_ref[at, :].astype(jnp.float32)
-            d_pair = factor_ref[at, :][:, :1] * (
-                d_norm
-                - jnp.mean(d_norm, axis=-1, keepdims=True)
-                - normed * jnp.mean(d_norm * normed, axis=-1, keepdims=True)
-            )
-            write_pair(work_ref, mask, (pair_grad + d_pair).astype(jnp.bfloat16))
+            d_pre_ref[later, units] = (d_hidden * slope_ref[at, units].astype(jnp.float32)).astype(jnp.bfloat16)
+        d_norm = contract_last(d_pre_ref[later, :], up_ref[...])
+        normed = normed_ref[at, :].astype(jnp.float32)
+        d_pair = factor_ref[at, :][:, :1] * (
+            d_norm
+            - jnp.mean(d_norm, axis=-1, keepdims=True)
+            - normed * jnp.mean(d_norm * normed, axis=-1, keepdims=True)
+        )
+        write_pair(work_ref, mask, (pair_grad + d_pair).astype(jnp.bfloat16))
         grad_t_ref[:, at] = pair_bf.T
-
+    pair_bf = read_pair(work_ref, MASKS[0]).astype(jnp.bfloat16)
+    last_ref[...] = pair_bf
+    grad_t_ref[:, pl.ds(0, pairs)] = pair_bf.T
     if blocks:
-        write_blocks(places_down, place_ref[1], grad_t_ref, hidden_ref, blocks[0])
-        write_blocks(places_up, place_ref[1], normed_t_ref, d_pre_ref, blocks[1])
-
-
-def keep_kernel(
-    places_down, places_up, place_ref, hidden_ref, d_pre_ref, normed_t_ref, grad_t_ref, down_ref, up_ref
-):
-    write_blocks(places_down, 1 - place_ref[1], grad_t_ref, hidden_ref, down_ref)
-    write_blocks(places_up, 1 - place_ref[1], normed_t_ref, d_pre_ref, up_ref)
+        write_blocks(places, place_ref[1], [(grad_t_ref, hidden_ref)], blocks[0])
+
+
+def first_section(normed_t_ref, later_ref, first_ref):
+    pairs = first_ref.shape[0]
+    return [
+        (normed_t_ref.at[:, pl.ds(pairs, later_ref.shape[0])], later_ref),
+        (normed_t_ref.at[:, pl.ds(0, pairs)], first_ref),
+    ]
+
+
+def last_kernel(places, place_ref, last_ref, slope_ref, down_ref, normed_t_ref, later_ref, d_pre_ref, *blocks):
+    pairs = last_ref.shape[0]
+    for start in range(0, down_ref.shape[1], CHUNK):
+        units = pl.ds(start, CHUNK)
+        d_hidden = jnp.dot(last_ref[...], down_ref[:, units], preferred_element_type=jnp.float32)
+        slope = slope_ref[pl.ds(0, pairs), units].astype(jnp.float32)
+        d_pre_ref[:, units] = (d_hidden * slope).astype(jnp.bfloat16)
+    if blocks:
+        write_blocks(places, place_ref[1], first_section(normed_t_ref, later_ref, d_pre_ref), blocks[0])
+
+
+def keep_down_kernel(places, place_ref, grad_t_ref, hidden_ref, out_ref):
+    write_blocks(places, 1 - place_ref[1], [(grad_t_ref, hidden_ref)], out_ref)
+
+
+def keep_up_kernel(places, place_ref, normed_t_ref, later_ref, first_ref, out_ref):
+    write_blocks(places, 1 - place_ref[1], first_section(normed_t_ref, later_ref, first_ref), out_ref)
 
 
 def arrange_kernel(spots, place_ref, block_ref, out_ref):
@@ -229,7 +255,7 @@
         out_shape=outs,
         in_specs=[spec(pltpu.SMEM), spec(pltpu.VMEM)] + [spec(pltpu.HBM)] * 2,
         out_specs=[spec(pltpu.VMEM)] * len(outs),
-        scratch_shapes=[pltpu.VMEM(state.shape, bf16), pltpu.SemaphoreType.DMA((2,))],
+        scratch_shapes=[pltpu.VMEM(state.shape, bf16), pltpu.SemaphoreType.DMA((2, units // CHUNK))],
         compiler_params=pltpu.CompilerParams(vmem_limit_bytes=SECTIONS_BYTES),
         cost_estimate=pl.CostEstimate(
             flops=10 * total * depth * units, bytes_accessed=16 * total * units, transcendentals=0
@@ -237,23 +263,17 @@
     )(place, state, *[pltpu.with_memory_space_constraint(item, pltpu.HBM) for item in (w_up, w_down)])
 
 
-def backward(place, grad, kept, places, block):
-    total, units = kept[0].shape
-    depth = kept[2].shape[1]
-    bf16 = jnp.bfloat16
-    outs = [pltpu.VMEM((total, units), bf16), pltpu.VMEM((depth, total), bf16)]
-    outs += [block] * 2 if block else []
+def call(kernel, outs, flops, place, *args, scratch=()):
+    size = sum(2 * math.prod(item.shape) for item in list(args) + list(outs))
     return pl.pallas_call(
-        functools.partial(backward_kernel, *places),
-        out_shape=outs,
-        in_specs=[spec(pltpu.SMEM)] + [spec(pltpu.VMEM)] * (1 + len(kept)),
+        kernel,
+        out_shape=list(outs),
+        in_specs=[spec(pltpu.SMEM)] + [spec(pltpu.VMEM)] * len(args),
         out_specs=[spec(pltpu.VMEM)] * len(outs),
-        scratch_shapes=[pltpu.VMEM(grad.shape, bf16)],
+        scratch_shapes=list(scratch),
         compiler_params=pltpu.CompilerParams(vmem_limit_bytes=SECTIONS_BYTES),
-        cost_estimate=pl.CostEstimate(
-            flops=10 * total * depth * units, bytes_accessed=16 * total * units, transcendentals=0
-        ),
-    )(place, grad, *in_vmem(*kept))
+        cost_estimate=pl.CostEstimate(flops=flops, bytes_accessed=size, transcendentals=0),
+    )(place, *in_vmem(*args))
 
 
 def arrange(place, block, spots):
@@ -266,21 +286,6 @@
         compiler_params=pltpu.CompilerParams(vmem_limit_bytes=KEEP_BYTES),
         cost_estimate=pl.CostEstimate(flops=0, bytes_accessed=4 * block.size, transcendentals=0),
     )(place, block)
-
-
-def keep_blocks(place, hidden, d_pre, normed_t, grad_t, places, block):
-    total, units = hidden.shape
-    depth = normed_t.shape[0]
-    return pl.pallas_call(
-        functools.partial(keep_kernel, *places),
-        out_shape=[block] * 2,
-        in_specs=[spec(pltpu.SMEM)] + [spec(pltpu.VMEM)] * 4,
-        out_specs=[spec(pltpu.VMEM)] * 2,
-        compiler_params=pltpu.CompilerParams(vmem_limit_bytes=KEEP_BYTES),
-        cost_estimate=pl.CostEstimate(
-            flops=2 * total * depth * units, bytes_accessed=8 * total * units, transcendentals=0
-        ),
-    )(place, *in_vmem(hidden, d_pre, normed_t, grad_t))
 
 
 def swap(block, axis, bit):
@@ -392,20 +397,42 @@
     going = Journey(state, [steps[at] + (MASKS[at],) for at in homeward])
     going.advance(place)
     grad = jnp.concatenate(coming.arrived(), 0)
-    d_pre, grad_t, *given = backward(place, grad, kept, places, block)
-    hidden, normed_t = kept[0], kept[3]
-    if not given:
+    hidden, slope, normed, normed_t, factor, up, down = kept
+    total, pairs, bf16 = hidden.shape[0], hidden.shape[0] // len(MASKS), jnp.bfloat16
+    matmul = 2 * depth * units
+    blocks = [block] if block else []
+    later, grad_t, last, *given_down = call(
+        functools.partial(backward_kernel, places[0]),
+        [pltpu.VMEM((total - pairs, units), bf16), pltpu.VMEM((depth, total), bf16), pltpu.VMEM((pairs, depth), bf16)]
+        + blocks,
+        3 * matmul * total,
+        place, grad, hidden, slope, normed, factor, up, down,
+        scratch=[pltpu.VMEM(state.shape, bf16)],
+    )
+    take_down = swap(given_down[0], *core) if blocks else None
+    first, *given_up = call(
+        functools.partial(last_kernel, places[1]),
+        [pltpu.VMEM((pairs, units), bf16)] + blocks,
+        matmul * (total // 2 + pairs),
+        place, last, slope, down, normed_t, later,
+    )
+    if not block:
         while going.steps:
             going.advance(place)
         mixed_out = settle(place, going)
+        d_pre = jnp.concatenate([first, later], 0)
         grad_down = scatter_narrow(halves, grad_t, hidden, [core] + order_down, span_x, span_y)
         grad_up = scatter_narrow(halves, normed_t, d_pre, [core] + order_up, span_x, span_y)
         return (mixed_out, grad_up, grad_down)
-    given[0] = going.advance(given[0])
-    take_down, take_up = [swap(part, *core) for part in given]
-    keep_down, keep_up = keep_blocks(place, hidden, d_pre, normed_t, grad_t, places, block)
+    take_up = swap(going.advance(given_up[0]), *core)
+    (keep_down,) = call(
+        functools.partial(keep_down_kernel, places[0]), blocks, matmul * total // 2, place, grad_t, hidden
+    )
+    (keep_up,) = call(
+        functools.partial(keep_up_kernel, places[1]), blocks, matmul * total // 2, place, normed_t, later, first
+    )
     grad_up = finish_sum(halves, keep_up, take_up, order_up)
-    beside = lambda phase, give: going.advance(give) if phase in (0, 2) else give
+    beside = lambda phase, give: going.advance(give) if phase in (1, 2) else give
     grad_down = finish_sum(halves, keep_down, take_down, order_down, beside)
     while going.steps:
         going.advance(place)

time: 94.5 us -> 104 us (1.10)
  waiting for transfers between devices: 40.4 us -> 48.4 us
  Pallas kernels: 25.4 us -> 27.4 us
    ppermute x18, waiting for transfers between devices: 36.3 us -> 44.3 us  [swap(): return lax.ppermute(block, axis, pairs)]
    pallas_call x2 -> x4, Pallas kernels: 12.6 us -> 13.9 us  [call(): pl.pallas_call(kernel, out_shape=list(outs), in_specs=[spec(pltpu.SMEM)]...]
  transfers between devices with their start and end apart: 19 -> 19, of which waited for: 11 -> 10; matrix products, arithmetic and copies ran while one was open for 3% -> 3% of each run, Pallas kernels for 26% -> 26%
where the time goes in v8:
time: 104 us; the launch traced here: 103 us
  waiting for transfers between devices  48.4 us (47%)
  Pallas kernels  27.4 us (26%)
  starting transfers between devices  21.2 us (20%)
  other arithmetic  3.62 us (3%)
  local copies, waits for them, and re-layouts  1.82 us (2%)
    ppermute x18, waiting for transfers between devices, swap(): return lax.ppermute(block, axis, pairs)  44.3 us
    ppermute x18, starting transfers between devices, swap(): return lax.ppermute(block, axis, pairs)  16.3 us
    pallas_call x4, Pallas kernels, call(): pl.pallas_call(kernel, out_shape=list(outs), in_specs=[spec(pltpu.SMEM)]...  13.9 us
    pallas_call x1, Pallas kernels, forward(): pl.pallas_call(functools.partial(forward_kernel, spots), out_shape=outs,...  11.1 us
    all_to_all x1, starting transfers between devices, exchange(): lax.all_to_all(block, ('gx', 'gy'), split_axis=0, concat_axis=0, axis_ind...  4.93 us
    all_to_all x1, waiting for transfers between devices, exchange(): lax.all_to_all(block, ('gx', 'gy'), split_axis=0, concat_axis=0, axis_ind...  4.17 us
  transfers between devices with their start and end apart: 19, of which 10 were waited for; matrix products, arithmetic and copies ran while one was open for 3% of the time, Pallas kernels for 26%

profile of v8, /device:TPU:0, one launch (start us, length us, event | category | flops | bytes accessed | tf_op | source)
XLA Modules:
  0.0 103.5 jit_solution(4500714483656520454)
XLA Ops:
  0.8 1.0 copy-done
  1.8 0.6 shard_map.67
  2.4 0.5 collective-permute-start
  3.0 1.1 %collective-permute-done = bf16[1,8,32,384]{3,2,0,1:T(8,128)(2,1)S(1)} collective-permute-done((bf16[1,8,32,384]{3,2,0,1:T(8,128)(2,1)S(1)}, bf16[1,8,32,384]{3,2,0,1:T(8,128)(2,1)S(1)}, u32[]{:S(2)}, u32[]{:S(2)}) %collective-permute-start) | collective-permute-done | bytes 196640 | tf_op jit(solution)/shard_map/ppermute | solution.py:293
  4.1 2.9 %collective-permute-start.1 = (bf16[2,4,32,384]{3,2,0,1:T(8,128)(2,1)S(1)}, bf16[2,4,32,384]{3,2,0,1:T(8,128)(2,1)S(1)}, u32[]{:S(2)}, u32[]{:S(2)}) collective-permute-start(bf16[2,4,32,384]{3,2,0,1:T(8,128)(2,1)S(1)} %get-tuple-element.44), channel_id=1, source_target_pairs={{0,2},{1,3},{2,0},{3,1},{4,6},{5,7},{6,4},{7,5},{8,10},{9,11},{10,... | collective-permute-start | bytes 589832 | tf_op jit(solution)/shard_map/ppermute | solution.py:293
  7.0 4.9 %all-to-all-start = ((bf16[16,32,384]{2,1,0:T(8,128)(2,1)}), bf16[16,32,384]{2,1,0:T(8,128)(2,1)S(1)}, u32[]{:S(2)}, u32[]{:S(2)}) async-start(bf16[16,32,384]{2,1,0:T(8,128)(2,1)} %bitcast.5), calls=%async_computation | async-start | bytes 786432 | tf_op jit(solution)/shard_map/all_to_all | solution.py:40
  12.2 1.8 %collective-permute-start.2 = (bf16[4,2,32,384]{3,2,0,1:T(8,128)(2,1)S(1)}, bf16[4,2,32,384]{3,2,0,1:T(8,128)(2,1)S(1)}, u32[]{:S(2)}, u32[]{:S(2)}) collective-permute-start(bf16[4,2,32,384]{3,2,0,1:T(8,128)(2,1)S(1)} %fusion.9), channel_id=1, source_target_pairs={{0,4},{4,0},{8,12},{12,8},{16,20},{20,16},{24,28},{28,24},{1,5},{5... | collective-permute-start | bytes 589832 | tf_op jit(solution)/shard_map/ppermute | solution.py:293
  14.1 7.8 %collective-permute-done.2 = bf16[4,2,32,384]{3,2,0,1:T(8,128)(2,1)S(1)} collective-permute-done((bf16[4,2,32,384]{3,2,0,1:T(8,128)(2,1)S(1)}, bf16[4,2,32,384]{3,2,0,1:T(8,128)(2,1)S(1)}, u32[]{:S(2)}, u32[]{:S(2)}) %collective-permute-start.2) | collective-permute-done | bytes 196640 | tf_op jit(solution)/shard_map/ppermute | solution.py:293
  22.0 4.2 %all-to-all-done.state_ref = bf16[16,32,384]{2,1,0:T(8,128)(2,1)S(1)} async-done(((bf16[16,32,384]{2,1,0:T(8,128)(2,1)}), bf16[16,32,384]{2,1,0:T(8,128)(2,1)S(1)}, u32[]{:S(2)}, u32[]{:S(2)}) %all-to-all-start) | async-done | bytes 393248 | tf_op jit(solution)/shard_map/all_to_all | solution.py:40
  26.2 11.1 %shard_map.68 = (bf16[16,32,384]{2,1,0:T(8,128)(2,1)S(1)}, bf16[1024,1536]{1,0:T(8,128)(2,1)S(1)}, bf16[1024,1536]{1,0:T(8,128)(2,1)S(1)}, bf16[1024,768]{1,0:T(...) custom-call(s32[4]{0:T(128)S(1)} %pad_add_fusion.place_ref, ...), custom_call_target="tpu_custom_call" | custom-call | flops 12079595520 | bytes 25165824 | tf_op jit(solution)/shard_map/pallas_call | solution.py:253
  37.3 3.0 %collective-permute-start.3 = (bf16[1,8,32,384]{3,2,0,1:T(8,128)(2,1)S(1)}, bf16[1,8,32,384]{3,2,0,1:T(8,128)(2,1)S(1)}, u32[]{:S(2)}, u32[]{:S(2)}) collective-permute-start(bf16[1,8,32,384]{3,2,0,1:T(8,128)(2,1)S(1)} %get-tuple-element.50), channel_id=1, source_target_pairs={{0,16},{4,20},{8,24},{12,28},{16,0},{20,4},{24,8},{28,12},{1,17},{... | collective-permute-start | bytes 589832 | tf_op jit(solution)/shard_map/ppermute | solution.py:293
  40.4 7.3 %shard_map.69 = (bf16[768,1536]{1,0:T(8,128)(2,1)S(1)}, bf16[768,1024]{1,0:T(8,128)(2,1)S(1)}, bf16[256,768]{1,0:T(8,128)(2,1)S(1)}, bf16[16,96,384]{2,1,0:T(8,128)(2,1)S(1)}) custom-call(s32[4]{0:T(128)S(1)} %pad_add_fusion.place_ref, bf16[16,32,384]{2,1,0:T(8,128)(2,1)S(1)} %pad_maximum_fusion.1.grad_ref, ...), custom_call_target="tpu_custom_call" | custom-call | flops 7247757312 | bytes 18743296 | tf_op jit(solution)/shard_map/pallas_call | solution.py:268
  47.7 2.7 %shard_map.70 = (bf16[256,1536]{1,0:T(8,128)(2,1)S(1)}, bf16[16,96,384]{2,1,0:T(8,128)(2,1)S(1)}) custom-call(s32[4]{0:T(128)S(1)} %pad_add_fusion.place_ref, bf16[256,768]{1,0:T(8,128)(2,1)S(1)} %get-tuple-element.58.last_ref, bf16[1024,1536]{1,0:T(8,128)(2,1)S(1)} %get-tuple-element.53.slope_ref, bf16[768,1536]{1,0:T(8,128)(2,1)S(1)} %get-tuple-element.57.down_ref, ...), custom_call_target="tpu_custom_call" | custom-call | flops 1811939328 | bytes 11796480 | tf_op jit(solution)/shard_map/pallas_call | solution.py:268
  50.5 0.6 collective-permute-start.11
  51.1 1.9 %shard_map.71 = bf16[16,96,384]{2,1,0:T(8,128)(2,1)S(1)} custom-call(s32[4]{0:T(128)S(1)} %pad_add_fusion.place_ref, bf16[768,1024]{1,0:T(8,128)(2,1)S(1)} %get-tuple-element.63.grad_t_ref, bf16[1024,1536]{1,0:T(8,128)(2,1)S(1)} %get-tuple-element.52.hidden_ref), custom_call_target="tpu_custom_call" | custom-call | flops 1207959552 | bytes 5898240 | tf_op jit(solution)/shard_map/pallas_call | solution.py:268
  53.0 1.9 %shard_map.73 = bf16[16,96,384]{2,1,0:T(8,128)(2,1)S(1)} custom-call(s32[4]{0:T(128)S(1)} %pad_add_fusion.place_ref, bf16[768,1024]{1,0:T(8,128)(2,1)S(1)} %get-tuple-element.59.normed_t_ref, bf16[768,1536]{1,0:T(8,128)(2,1)S(1)} %get-tuple-element.60.later_ref, bf16[256,1536]{1,0:T(8,128)(2,1)S(1)} %get-tuple-element.73.first_ref), custom_call_target="tpu_custom_call" | custom-call | flops 1207959552 | bytes 5898240 | tf_op jit(solution)/shard_map/pallas_call | solution.py:268
  55.8 0.7 collective-permute-start.12
  56.5 1.4 %collective-permute-start.5 = (bf16[2,4,32,384]{3,2,0,1:T(8,128)(2,1)S(1)}, bf16[2,4,32,384]{3,2,0,1:T(8,128)(2,1)S(1)}, u32[]{:S(2)}, u32[]{:S(2)}) collective-permute-start(bf16[2,4,32,384]{3,2,0,1:T(8,128)(2,1)S(1)} %get-tuple-element.62), channel_id=1, source_target_pairs={{0,2},{1,3},{2,0},{3,1},{4,6},{5,7},{6,4},{7,5},{8,10},{9,11},{10,... | collective-permute-start | bytes 589832 | tf_op jit(solution)/shard_map/ppermute | solution.py:293
  57.8 17.4 %collective-permute-done.5 = bf16[2,4,32,384]{3,2,0,1:T(8,128)(2,1)S(1)} collective-permute-done((bf16[2,4,32,384]{3,2,0,1:T(8,128)(2,1)S(1)}, bf16[2,4,32,384]{3,2,0,1:T(8,128)(2,1)S(1)}, u32[]{:S(2)}, u32[]{:S(2)}) %collective-permute-start.5) | collective-permute-done | bytes 196640 | tf_op jit(solution)/shard_map/ppermute | solution.py:293
  75.8 1.8 %collective-permute-start.13 = (bf16[4,96,384]{2,1,0:T(8,128)(2,1)S(1)}, bf16[4,96,384]{2,1,0:T(8,128)(2,1)S(1)}, u32[]{:S(2)}, u32[]{:S(2)}) collective-permute-start(bf16[4,96,384]{2,1,0:T(8,128)(2,1)S(1)} %get-tuple-element.84), channel_id=1, source_target_pairs={{0,4},{4,0},{8,12},{12,8},{16,20},{20,16},{24,28},{28,24},{1,5},{5... | collective-permute-start | bytes 884744 | tf_op jit(solution)/shard_map/ppermute | solution.py:293
  77.8 0.7 pad_maximum_fusion.2
  78.6 6.7 %collective-permute-done.13 = bf16[4,96,384]{2,1,0:T(8,128)(2,1)S(1)} collective-permute-done((bf16[4,96,384]{2,1,0:T(8,128)(2,1)S(1)}, bf16[4,96,384]{2,1,0:T(8,128)(2,1)S(1)}, u32[]{:S(2)}, u32[]{:S(2)}) %collective-permute-start.13) | collective-permute-done | bytes 294944 | tf_op jit(solution)/shard_map/ppermute | solution.py:293
  85.4 1.3 %collective-permute-done.9 = bf16[4,96,384]{2,1,0:T(8,128)(2,1)S(1)} collective-permute-done((bf16[4,96,384]{2,1,0:T(8,128)(2,1)S(1)}, bf16[4,96,384]{2,1,0:T(8,128)(2,1)S(1)}, u32[]{:S(2)}, u32[]{:S(2)}) %collective-permute-start.9) | collective-permute-done | bytes 294944 | tf_op jit(solution)/shard_map/ppermute | solution.py:293
  86.7 0.8 collective-permute-start.16
  87.5 1.7 %collective-permute-start.10 = (bf16[8,1,32,384]{3,2,0,1:T(8,128)(2,1)S(1)}, bf16[8,1,32,384]{3,2,0,1:T(8,128)(2,1)S(1)}, u32[]{:S(2)}, u32[]{:S(2)}) collective-permute-start(bf16[8,1,32,384]{3,2,0,1:T(8,128)(2,1)S(1)} %get-tuple-element.72), channel_id=1, source_target_pairs={{0,4},{4,0},{8,12},{12,8},{16,20},{20,16},{24,28},{28,24},{1,5},{5... | collective-permute-start | bytes 589832 | tf_op jit(solution)/shard_map/ppermute | solution.py:293
  89.3 2.5 %collective-permute-done.14 = bf16[2,96,384]{2,1,0:T(8,128)(2,1)S(1)} collective-permute-done((bf16[2,96,384]{2,1,0:T(8,128)(2,1)S(1)}, bf16[2,96,384]{2,1,0:T(8,128)(2,1)S(1)}, u32[]{:S(2)}, u32[]{:S(2)}) %collective-permute-start.14) | collective-permute-done | bytes 147488 | tf_op jit(solution)/shard_map/ppermute | solution.py:293
  92.2 6.1 %collective-permute-done.16 = bf16[2,96,384]{2,1,0:T(8,128)(2,1)S(1)} collective-permute-done((bf16[2,96,384]{2,1,0:T(8,128)(2,1)S(1)}, bf16[2,96,384]{2,1,0:T(8,128)(2,1)S(1)}, u32[]{:S(2)}, u32[]{:S(2)}) %collective-permute-start.16) | collective-permute-done | bytes 147488 | tf_op jit(solution)/shard_map/ppermute | solution.py:293
  98.5 0.7 copy-done.2
  99.2 1.9 %shard_map.72 = bf16[512,384]{1,0:T(8,128)(2,1)} custom-call(s32[4]{0:T(128)} %copy-done.1, bf16[8,32,384]{2,1,0:T(8,128)(2,1)} %get-tuple-element.92.kept_ref, bf16[8,32,384]{2,1,0:T(8,128)(2,1)} %bitcast.67), custom_call_target="tpu_custom_call" | custom-call | bytes 786432 | tf_op jit(solution)/shard_map/pallas_call | solution.py:352
  101.1 0.7 add_bitcast_fusion.1
  101.8 1.0 collective-permute-done.17
  102.8 0.7 add_bitcast_fusion
  (40 shorter events, 3.0 us)
Async XLA Ops:
  0.8 1.0 copy-start
  1.8 51.2 %copy-start.1 = (s32[4]{0:T(128)}, s32[4]{0:T(128)S(1)}, u32[]{:S(2)}) copy-start(s32[4]{0:T(128)S(1)} %pad_add_fusion.place_ref) | copy-start | bytes 52
  2.4 1.6 %collective-permute-start = (bf16[1,8,32,384]{3,2,0,1:T(8,128)(2,1)S(1)}, bf16[1,8,32,384]{3,2,0,1:T(8,128)(2,1)S(1)}, u32[]{:S(2)}, u32[]{:S(2)}) collective-permute-start(bf16[1,8,32,384]{3,2,0,1:T(8,128)(2,1)S(1)} %get-tuple-element.42), channel_id=1, source_target_pairs={{0,1},{1,0},{2,3},{3,2},{4,5},{5,4},{6,7},{7,6},{8,9},{9,8},{10,11... | collective-permute-start | bytes 589832 | tf_op jit(solution)/shard_map/ppermute | solution.py:293
  4.1 8.1 %collective-permute-start.1 = (bf16[2,4,32,384]{3,2,0,1:T(8,128)(2,1)S(1)}, bf16[2,4,32,384]{3,2,0,1:T(8,128)(2,1)S(1)}, u32[]{:S(2)}, u32[]{:S(2)}) collective-permute-start(bf16[2,4,32,384]{3,2,0,1:T(8,128)(2,1)S(1)} %get-tuple-element.44), channel_id=1, source_target_pairs={{0,2},{1,3},{2,0},{3,1},{4,6},{5,7},{6,4},{7,5},{8,10},{9,11},{10,... | collective-permute-start | bytes 589832 | tf_op jit(solution)/shard_map/ppermute | solution.py:293
  7.0 19.2 %all-to-all-start = ((bf16[16,32,384]{2,1,0:T(8,128)(2,1)}), bf16[16,32,384]{2,1,0:T(8,128)(2,1)S(1)}, u32[]{:S(2)}, u32[]{:S(2)}) async-start(bf16[16,32,384]{2,1,0:T(8,128)(2,1)} %bitcast.5), calls=%async_computation | async-start | bytes 786432 | tf_op jit(solution)/shard_map/all_to_all | solution.py:40
  12.2 9.7 %collective-permute-start.2 = (bf16[4,2,32,384]{3,2,0,1:T(8,128)(2,1)S(1)}, bf16[4,2,32,384]{3,2,0,1:T(8,128)(2,1)S(1)}, u32[]{:S(2)}, u32[]{:S(2)}) collective-permute-start(bf16[4,2,32,384]{3,2,0,1:T(8,128)(2,1)S(1)} %fusion.9), channel_id=1, source_target_pairs={{0,4},{4,0},{8,12},{12,8},{16,20},{20,16},{24,28},{28,24},{1,5},{5... | collective-permute-start | bytes 589832 | tf_op jit(solution)/shard_map/ppermute | solution.py:293
  26.2 14.1 %collective-permute-start.4 = (bf16[8,1,32,384]{3,2,0,1:T(8,128)(2,1)S(1)}, bf16[8,1,32,384]{3,2,0,1:T(8,128)(2,1)S(1)}, u32[]{:S(2)}, u32[]{:S(2)}) collective-permute-start(bf16[8,1,32,384]{3,2,0,1:T(8,128)(2,1)S(1)} %get-tuple-element.51), channel_id=1, source_target_pairs={{0,16},{4,20},{8,24},{12,28},{16,0},{20,4},{24,8},{28,12},{1,17},{... | collective-permute-start | bytes 589832 | tf_op jit(solution)/shard_map/ppermute | solution.py:293
  37.3 13.1 %collective-permute-start.3 = (bf16[1,8,32,384]{3,2,0,1:T(8,128)(2,1)S(1)}, bf16[1,8,32,384]{3,2,0,1:T(8,128)(2,1)S(1)}, u32[]{:S(2)}, u32[]{:S(2)}) collective-permute-start(bf16[1,8,32,384]{3,2,0,1:T(8,128)(2,1)S(1)} %get-tuple-element.50), channel_id=1, source_target_pairs={{0,16},{4,20},{8,24},{12,28},{16,0},{20,4},{24,8},{28,12},{1,17},{... | collective-permute-start | bytes 589832 | tf_op jit(solution)/shard_map/ppermute | solution.py:293
  47.6 7.3 %collective-permute-start.6 = (bf16[16,96,384]{2,1,0:T(8,128)(2,1)S(1)}, bf16[16,96,384]{2,1,0:T(8,128)(2,1)S(1)}, u32[]{:S(2)}, u32[]{:S(2)}) collective-permute-start(bf16[16,96,384]{2,1,0:T(8,128)(2,1)S(1)} %get-tuple-element.65), channel_id=1, source_target_pairs={{0,1},{1,0},{2,3},{3,2},{4,5},{5,4},{6,7},{7,6},{8,9},{9,8},{10,11... | collective-permute-start | bytes 3538952 | tf_op jit(solution)/shard_map/ppermute | solution.py:293
  50.5 4.9 %collective-permute-start.11 = (bf16[16,96,384]{2,1,0:T(8,128)(2,1)S(1)}, bf16[16,96,384]{2,1,0:T(8,128)(2,1)S(1)}, u32[]{:S(2)}, u32[]{:S(2)}) collective-permute-start(bf16[16,96,384]{2,1,0:T(8,128)(2,1)S(1)} %get-tuple-element.74), channel_id=1, source_target_pairs={{0,1},{1,0},{2,3},{3,2},{4,5},{5,4},{6,7},{7,6},{8,9},{9,8},{10,11... | collective-permute-start | bytes 3538952 | tf_op jit(solution)/shard_map/ppermute | solution.py:293
  55.3 20.0 %collective-permute-start.7 = (bf16[8,96,384]{2,1,0:T(8,128)(2,1)S(1)}, bf16[8,96,384]{2,1,0:T(8,128)(2,1)S(1)}, u32[]{:S(2)}, u32[]{:S(2)}) collective-permute-start(bf16[8,96,384]{2,1,0:T(8,128)(2,1)S(1)} %get-tuple-element.82), channel_id=1, source_target_pairs={{0,4},{4,0},{8,12},{12,8},{16,20},{20,16},{24,28},{28,24},{1,5},{5... | collective-permute-start | bytes 1769480 | tf_op jit(solution)/shard_map/ppermute | solution.py:293
  55.8 19.8 %collective-permute-start.12 = (bf16[8,96,384]{2,1,0:T(8,128)(2,1)S(1)}, bf16[8,96,384]{2,1,0:T(8,128)(2,1)S(1)}, u32[]{:S(2)}, u32[]{:S(2)}) collective-permute-start(bf16[8,96,384]{2,1,0:T(8,128)(2,1)S(1)} %get-tuple-element.80), channel_id=1, source_target_pairs={{0,2},{1,3},{2,0},{3,1},{4,6},{5,7},{6,4},{7,5},{8,10},{9,11},{10,... | collective-permute-start | bytes 1769480 | tf_op jit(solution)/shard_map/ppermute | solution.py:293
  56.5 18.8 %collective-permute-start.5 = (bf16[2,4,32,384]{3,2,0,1:T(8,128)(2,1)S(1)}, bf16[2,4,32,384]{3,2,0,1:T(8,128)(2,1)S(1)}, u32[]{:S(2)}, u32[]{:S(2)}) collective-permute-start(bf16[2,4,32,384]{3,2,0,1:T(8,128)(2,1)S(1)} %get-tuple-element.62), channel_id=1, source_target_pairs={{0,2},{1,3},{2,0},{3,1},{4,6},{5,7},{6,4},{7,5},{8,10},{9,11},{10,... | collective-permute-start | bytes 589832 | tf_op jit(solution)/shard_map/ppermute | solution.py:293
  75.5 2.3 %collective-permute-start.8 = (bf16[4,2,32,384]{3,2,0,1:T(8,128)(2,1)S(1)}, bf16[4,2,32,384]{3,2,0,1:T(8,128)(2,1)S(1)}, u32[]{:S(2)}, u32[]{:S(2)}) collective-permute-start(bf16[4,2,32,384]{3,2,0,1:T(8,128)(2,1)S(1)} %get-tuple-element.68), channel_id=1, source_target_pairs={{0,1},{1,0},{2,3},{3,2},{4,5},{5,4},{6,7},{7,6},{8,9},{9,8},{10,11... | collective-permute-start | bytes 589832 | tf_op jit(solution)/shard_map/ppermute | solution.py:293
  75.8 9.5 %collective-permute-start.13 = (bf16[4,96,384]{2,1,0:T(8,128)(2,1)S(1)}, bf16[4,96,384]{2,1,0:T(8,128)(2,1)S(1)}, u32[]{:S(2)}, u32[]{:S(2)}) collective-permute-start(bf16[4,96,384]{2,1,0:T(8,128)(2,1)S(1)} %get-tuple-element.84), channel_id=1, source_target_pairs={{0,4},{4,0},{8,12},{12,8},{16,20},{20,16},{24,28},{28,24},{1,5},{5... | collective-permute-start | bytes 884744 | tf_op jit(solution)/shard_map/ppermute | solution.py:293
  77.5 9.1 %collective-permute-start.9 = (bf16[4,96,384]{2,1,0:T(8,128)(2,1)S(1)}, bf16[4,96,384]{2,1,0:T(8,128)(2,1)S(1)}, u32[]{:S(2)}, u32[]{:S(2)}) collective-permute-start(bf16[4,96,384]{2,1,0:T(8,128)(2,1)S(1)} %get-tuple-element.71), channel_id=1, source_target_pairs={{0,2},{1,3},{2,0},{3,1},{4,6},{5,7},{6,4},{7,5},{8,10},{9,11},{10,... | collective-permute-start | bytes 884744 | tf_op jit(solution)/shard_map/ppermute | solution.py:293
  85.3 6.5 %collective-permute-start.14 = (bf16[2,96,384]{2,1,0:T(8,128)(2,1)S(1)}, bf16[2,96,384]{2,1,0:T(8,128)(2,1)S(1)}, u32[]{:S(2)}, u32[]{:S(2)}) collective-permute-start(bf16[2,96,384]{2,1,0:T(8,128)(2,1)S(1)} %get-tuple-element.90), channel_id=1, source_target_pairs={{0,8},{4,12},{8,0},{12,4},{16,24},{20,28},{24,16},{28,20},{1,9},{5... | collective-permute-start | bytes 442376 | tf_op jit(solution)/shard_map/ppermute | solution.py:293
  86.7 11.6 %collective-permute-start.16 = (bf16[2,96,384]{2,1,0:T(8,128)(2,1)S(1)}, bf16[2,96,384]{2,1,0:T(8,128)(2,1)S(1)}, u32[]{:S(2)}, u32[]{:S(2)}) collective-permute-start(bf16[2,96,384]{2,1,0:T(8,128)(2,1)S(1)} %get-tuple-element.78), channel_id=1, source_target_pairs={{0,16},{4,20},{8,24},{12,28},{16,0},{20,4},{24,8},{28,12},{1,17},{... | collective-permute-start | bytes 442376 | tf_op jit(solution)/shard_map/ppermute | solution.py:293
  87.5 10.9 %collective-permute-start.10 = (bf16[8,1,32,384]{3,2,0,1:T(8,128)(2,1)S(1)}, bf16[8,1,32,384]{3,2,0,1:T(8,128)(2,1)S(1)}, u32[]{:S(2)}, u32[]{:S(2)}) collective-permute-start(bf16[8,1,32,384]{3,2,0,1:T(8,128)(2,1)S(1)} %get-tuple-element.72), channel_id=1, source_target_pairs={{0,4},{4,0},{8,12},{12,8},{16,20},{20,16},{24,28},{28,24},{1,5},{5... | collective-permute-start | bytes 589832 | tf_op jit(solution)/shard_map/ppermute | solution.py:293
  91.8 9.3 %collective-permute-start.15 = (bf16[1,96,384]{2,1,0:T(8,128)(2,1)S(1)}, bf16[1,96,384]{2,1,0:T(8,128)(2,1)S(1)}, u32[]{:S(2)}, u32[]{:S(2)}) collective-permute-start(bf16[1,96,384]{2,1,0:T(8,128)(2,1)S(1)} %fusion.15), channel_id=1, source_target_pairs={{0,16},{4,20},{8,24},{12,28},{16,0},{20,4},{24,8},{28,12},{1,17},{... | collective-permute-start | bytes 221192 | tf_op jit(solution)/shard_map/ppermute | solution.py:293
  98.4 4.4 %collective-permute-start.17 = (bf16[1,96,384]{2,1,0:T(8,128)(2,1)S(1)}, bf16[1,96,384]{2,1,0:T(8,128)(2,1)S(1)}, u32[]{:S(2)}, u32[]{:S(2)}) collective-permute-start(bf16[1,96,384]{2,1,0:T(8,128)(2,1)S(1)} %fusion.13), channel_id=1, source_target_pairs={{0,8},{4,12},{8,0},{12,4},{16,24},{20,28},{24,16},{28,20},{1,9},{5... | collective-permute-start | bytes 221192 | tf_op jit(solution)/shard_map/ppermute | solution.py:293
  98.5 0.7 copy-start.2

commit v9 on v8

v9 whole, which is shorter than its diff:
```python
import functools
import math

import jax
import jax.numpy as jnp
from jax import lax
from jax.experimental import pallas as pl
from jax.experimental.pallas import tpu as pltpu
from jax.sharding import PartitionSpec as P

MEMBERS = 16
MASKS = (8, 4, 2, 1)
LANES = 128
CHUNK = 256
SECTIONS_BYTES = 8 * 1024 * 1024
KEEP_BYTES = 4 * 1024 * 1024


def contract_last(left, right):
    return lax.dot_general(
        left, right, (((1,), (1,)), ((), ())), preferred_element_type=jnp.float32
    )


def low_members(mask):
    return [member for member in range(MEMBERS) if not member & mask]


def join_pair(rows_of, mask):
    low = jnp.concatenate([rows_of(member) for member in low_members(mask)], 0)
    high = jnp.concatenate([rows_of(member | mask) for member in low_members(mask)], 0)
    return jnp.concatenate([low, high], 1).astype(jnp.float32)


def read_pair(ref, mask):
    return join_pair(lambda member: ref[member], mask)


def read_landed(refs, landings, spots, mask):
    return join_pair(
        lambda member: jnp.concatenate(
            [ref[landing[member] ^ spot] for ref, landing, spot in zip(refs, landings, spots)], 0
        ),
        mask,
    )


def write_pair(ref, mask, pair):
    rows, width = ref.shape[1:]
    for place, member in enumerate(low_members(mask)):
        part = pair[place * rows : (place + 1) * rows]
        ref[member] = part[:, :width]
        ref[member | mask] = part[:, width:]


def write_blocks(places, bit, products, out_ref):
    rows, columns = out_ref.shape[1:]
    pieces = []
    for group in range(len(places[0])):
        base = (2 * group + bit) * columns
        for inner in range(0, columns, LANES):
            pieces.append((group, inner, pl.multiple_of(base + inner, LANES)))
    for first in range(0, len(pieces), 2):
        some = pieces[first : first + 2]
        total = 0.0
        for left_ref, right_ref in products:
            right = jnp.concatenate([right_ref[:, pl.ds(start, LANES)] for _, _, start in some], 1)
            total += jnp.dot(left_ref[...], right, preferred_element_type=jnp.float32)
        total = total.astype(jnp.bfloat16)
        for which, (group, inner, _) in enumerate(some):
            for block in range(len(places)):
                out_ref[places[block][group], :, inner : inner + LANES] = total[
                    block * rows : (block + 1) * rows, which * LANES : (which + 1) * LANES
                ]


def load_kernel(place_ref, up_hbm, down_hbm, up_ref, down_ref, arrived):
    copies = [
        pltpu.make_async_copy(up_hbm, up_ref, arrived.at[0]),
        pltpu.make_async_copy(down_hbm, down_ref, arrived.at[1]),
    ]
    for copy in copies:
        copy.start()
    for copy in copies:
        copy.wait()


def forward_kernel(
    landings, place_ref, first_ref, second_ref, up_ref, down_ref,
    out_ref, hidden_ref, slope_ref, normed_ref, normed_t_ref, factor_ref, work_ref
):
    pairs = MEMBERS // 2 * work_ref.shape[1]
    last = len(MASKS) - 1
    for section, mask in enumerate(MASKS):
        at = pl.ds(section * pairs, pairs)
        if section == 0:
            pair = read_landed((first_ref, second_ref), landings, (place_ref[2], place_ref[3]), mask)
        else:
            pair = read_pair(work_ref, mask)
        centre = jnp.mean(pair, axis=-1, keepdims=True)
        shifted = pair - centre
        spread = jnp.mean(shifted * shifted, axis=-1, keepdims=True)
        factor = lax.rsqrt(spread + 1e-05)
        normed = (shifted * factor).astype(jnp.bfloat16)
        normed_ref[at, :] = normed
        factor_ref[at, :] = jnp.broadcast_to(factor, (pairs, LANES))
        for start in range(0, up_ref.shape[1], CHUNK):
            units = pl.ds(start, CHUNK)
            pre = jnp.dot(normed, up_ref[:, units], preferred_element_type=jnp.float32)
            share = 0.5 * (1.0 + lax.erf(pre * (1.0 / math.sqrt(2.0))))
            hidden_ref[at, units] = (pre * share).astype(jnp.bfloat16)
            bell = jnp.exp(-0.5 * pre * pre) * (1.0 / math.sqrt(2.0 * math.pi))
            slope_ref[at, units] = (share + pre * bell).astype(jnp.bfloat16)
        mixed = (pair + contract_last(hidden_ref[at, :], down_ref[...])).astype(jnp.bfloat16)
        write_pair(work_ref if section < last else out_ref, mask, mixed)
        normed_t_ref[:, at] = normed.T


def backward_kernel(
    places, place_ref, grad_ref, hidden_ref, slope_ref, normed_ref, factor_ref, up_ref, down_ref,
    d_pre_ref, grad_t_ref, last_ref, *rest
):
    blocks, work_ref = rest[:-1], rest[-1]
    pairs = MEMBERS // 2 * work_ref.shape[1]
    for section in range(len(MASKS) - 1, 0, -1):
        mask = MASKS[section]
        at = pl.ds(section * pairs, pairs)
        later = pl.ds((section - 1) * pairs, pairs)
        if section == len(MASKS) - 1:
            pair_grad = read_landed((grad_ref,), (range(MEMBERS),), (place_ref[0],), mask)
        else:
            pair_grad = read_pair(work_ref, mask)
        pair_bf = pair_grad.astype(jnp.bfloat16)
        for start in range(0, up_ref.shape[1], CHUNK):
            units = pl.ds(start, CHUNK)
            d_hidden = jnp.dot(pair_bf, down_ref[:, units], preferred_element_type=jnp.float32)
            d_pre_ref[later, units] = (d_hidden * slope_ref[at, units].astype(jnp.float32)).astype(jnp.bfloat16)
        d_norm = contract_last(d_pre_ref[later, :], up_ref[...])
        normed = normed_ref[at, :].astype(jnp.float32)
        d_pair = factor_ref[at, :][:, :1] * (
            d_norm
            - jnp.mean(d_norm, axis=-1, keepdims=True)
            - normed * jnp.mean(d_norm * normed, axis=-1, keepdims=True)
        )
        write_pair(work_ref, mask, (pair_grad + d_pair).astype(jnp.bfloat16))
        grad_t_ref[:, at] = pair_bf.T
    pair_bf = read_pair(work_ref, MASKS[0]).astype(jnp.bfloat16)
    last_ref[...] = pair_bf
    grad_t_ref[:, pl.ds(0, pairs)] = pair_bf.T
    if blocks:
        write_blocks(places, place_ref[1], [(grad_t_ref, hidden_ref)], blocks[0])


def first_section(normed_t_ref, later_ref, first_ref):
    pairs = first_ref.shape[0]
    return [
        (normed_t_ref.at[:, pl.ds(pairs, later_ref.shape[0])], later_ref),
        (normed_t_ref.at[:, pl.ds(0, pairs)], first_ref),
    ]


def last_kernel(places, place_ref, last_ref, slope_ref, down_ref, normed_t_ref, later_ref, d_pre_ref, *blocks):
    pairs = last_ref.shape[0]
    for start in range(0, down_ref.shape[1], CHUNK):
        units = pl.ds(start, CHUNK)
        d_hidden = jnp.dot(last_ref[...], down_ref[:, units], preferred_element_type=jnp.float32)
        slope = slope_ref[pl.ds(0, pairs), units].astype(jnp.float32)
        d_pre_ref[:, units] = (d_hidden * slope).astype(jnp.bfloat16)
    if blocks:
        write_blocks(places, place_ref[1], first_section(normed_t_ref, later_ref, d_pre_ref), blocks[0])


def keep_down_kernel(places, place_ref, grad_t_ref, hidden_ref, out_ref):
    write_blocks(places, 1 - place_ref[1], [(grad_t_ref, hidden_ref)], out_ref)


def keep_up_kernel(places, place_ref, normed_t_ref, later_ref, first_ref, out_ref):
    write_blocks(places, 1 - place_ref[1], first_section(normed_t_ref, later_ref, first_ref), out_ref)


def settle_kernel(sources, place_ref, kept_ref, taken_ref, out_ref, done):
    half, rows = kept_ref.shape[:2]
    copies = []
    for index, source in enumerate(sources):
        block = kept_ref.at[index] if index < half else taken_ref.at[index - half]
        first = pl.multiple_of((place_ref[0] ^ source) * rows, rows)
        copies.append(pltpu.make_async_copy(block, out_ref.at[pl.ds(first, rows)], done.at[index]))
    for copy in copies:
        copy.start()
    for copy in copies:
        copy.wait()


def spec(space):
    return pl.BlockSpec(memory_space=space)


def block_places(order, span_x, span_y):
    places = []
    for at_x in range(span_x):
        line = []
        for group in range(span_y // 2):
            place = 0
            for axis, step in order:
                at = at_x if axis == "gx" else 2 * group
                place = 2 * place + (at >> step & 1)
            line.append(place)
        places.append(line)
    return places


def in_vmem(*items):
    return [pltpu.with_memory_space_constraint(item, pltpu.VMEM) for item in items]


def load(place, *weights):
    return pl.pallas_call(
        load_kernel,
        out_shape=[pltpu.VMEM(item.shape, item.dtype) for item in weights],
        in_specs=[spec(pltpu.SMEM)] + [spec(pltpu.HBM)] * 2,
        out_specs=[spec(pltpu.VMEM)] * 2,
        scratch_shapes=[pltpu.SemaphoreType.DMA((2,))],
        compiler_params=pltpu.CompilerParams(vmem_limit_bytes=KEEP_BYTES),
        cost_estimate=pl.CostEstimate(flops=0, bytes_accessed=8 * weights[0].size, transcendentals=0),
    )(place, *[pltpu.with_memory_space_constraint(item, pltpu.HBM) for item in weights])


def call(kernel, outs, flops, place, *args, scratch=()):
    size = sum(2 * math.prod(item.shape) for item in list(args) + list(outs))
    return pl.pallas_call(
        kernel,
        out_shape=list(outs),
        in_specs=[spec(pltpu.SMEM)] + [spec(pltpu.VMEM)] * len(args),
        out_specs=[spec(pltpu.VMEM)] * len(outs),
        scratch_shapes=list(scratch),
        compiler_params=pltpu.CompilerParams(vmem_limit_bytes=SECTIONS_BYTES),
        cost_estimate=pl.CostEstimate(flops=flops, bytes_accessed=size, transcendentals=0),
    )(place, *in_vmem(*args))


def swap(block, axis, bit):
    pairs = [(source, source ^ (1 << bit)) for source in range(lax.axis_size(axis))]
    return lax.ppermute(block, axis, pairs)


def pick(block, at):
    return slice_at(block, 0, at).astype(jnp.float32)


def halve(halves, step, kept, taken):
    mine, other = halves[step]
    shape = (2, kept.shape[0] // 2) + kept.shape[1:]
    kept, taken = kept.reshape(shape), taken.reshape(shape)
    give = (pick(kept, other) + pick(taken, other)).astype(jnp.bfloat16)
    keep = (pick(kept, mine) + pick(taken, mine)).astype(jnp.bfloat16)
    return keep, give


def last_sum(kept, taken):
    return (kept.astype(jnp.float32) + taken.astype(jnp.float32))[0]


def finish_sum(halves, kept, taken, order):
    for step in order:
        kept, give = halve(halves, step, kept, taken)
        taken = swap(give, *step)
    return last_sum(kept, taken)


def scatter_narrow(halves, left, right, order, span_x, span_y):
    total = jnp.dot(left, right, preferred_element_type=jnp.float32).astype(jnp.bfloat16)
    rows, columns = left.shape[0] // span_x, right.shape[1] // span_y
    count_x, count_y = span_x.bit_length() - 1, span_y.bit_length() - 1
    dims = [("gx", bit) for bit in range(count_x)][::-1] + ["rows"]
    dims += [("gy", bit) for bit in range(count_y)][::-1] + ["columns"]
    blocks = total.reshape((2,) * count_x + (rows,) + (2,) * count_y + (columns,))
    blocks = blocks.transpose([dims.index(item) for item in list(order) + ["rows", "columns"]])
    blocks = blocks.reshape(-1, rows, columns)
    return finish_sum(halves, blocks, jnp.zeros_like(blocks), order)


class Journey:
    def __init__(self, held, bits=(0, 1, 2, 3), sources=(0,)):
        self.held = held
        self.bits = list(bits)
        self.sources = list(sources)
        self.parts = None

    def split(self):
        half = self.held.shape[-2] // 2
        return [Journey(part, self.bits, self.sources) for part in (self.held[..., :half, :], self.held[..., half:, :])]

    def hop(self, at, steps, halves, after=None):
        dim = self.bits.index(at)
        mine, other = halves[steps[at]]
        kept, given = [slice_at(self.held, dim, part) for part in (mine, other)]
        if after is not None:
            given, after = lax.optimization_barrier((given, after))
        self.parts = [kept, swap(given, *steps[at])]
        self.held = jnp.concatenate(self.parts, -3)
        self.bits.remove(at)
        self.sources += [source | MASKS[at] for source in self.sources]
        return after

    def landing(self):
        return [self.sources.index(member) for member in range(MEMBERS)]


def landing_of(order):
    return [sum(bool(member & MASKS[at]) << k for k, at in enumerate(order)) for member in range(MEMBERS)]


def slice_at(block, dim, at):
    start = [0] * block.ndim
    start[dim] = at
    size = list(block.shape)
    size[dim] = 1
    part = lax.dynamic_slice(block, start, size, allow_negative_indices=False)
    return lax.squeeze(part, (dim,))


def settle(place, journey):
    kept, taken = journey.parts
    half, rows, width = kept.shape
    return pl.pallas_call(
        functools.partial(settle_kernel, journey.sources),
        out_shape=jax.ShapeDtypeStruct((2 * half * rows, width), kept.dtype),
        in_specs=[spec(pltpu.SMEM)] + [spec(pltpu.VMEM)] * 2,
        out_specs=spec(pltpu.HBM),
        scratch_shapes=[pltpu.SemaphoreType.DMA((2 * half,))],
        cost_estimate=pl.CostEstimate(flops=0, bytes_accessed=8 * kept.size, transcendentals=0),
    )(place, kept, taken)


def local(signal, w_up, w_down, cotangent):
    span_x = lax.axis_size("gx")
    span_y = lax.axis_size("gy")
    rows, width = signal.shape
    depth, units = w_up.shape
    steps = [("gx", span_x.bit_length() - 2), ("gx", 0), ("gy", span_y.bit_length() - 2), ("gy", 0)]
    z, y, x, core = range(4)
    rest_y = [("gy", bit) for bit in range(1, span_y.bit_length() - 1)]
    rest_x = [("gx", bit) for bit in range(1, span_x.bit_length() - 1)]
    order_down = [steps[y]] + rest_y + rest_x[::-1]
    order_up = rest_y + [steps[y]] + rest_x
    orders = ((z, x, y, core), (z, y, x, core))
    landings = [landing_of(order) for order in orders]

    owns = [lax.axis_index(axis) // (1 << bit) % 2 for axis, bit in [steps[core]] + order_up]
    own = dict(zip([steps[core]] + order_up, owns))
    member = sum(own[step] * mask for step, mask in zip(steps, MASKS))
    spots = [sum(own[steps[at]] << k for k, at in enumerate(order)) for order in orders]
    place = jnp.stack([member, 1 - own[steps[core]]] + spots).astype(jnp.int32)
    place, owns, others = lax.optimization_barrier((place, owns, [1 - item for item in owns]))
    halves = {step: pair for step, pair in zip([steps[core]] + order_up, zip(owns, others))}
    places = [block_places(order, span_x, span_y) for order in (order_down, order_up)]
    block = None
    if units // span_y % LANES == 0:
        block = pltpu.VMEM((span_x * span_y // 2, depth // span_x, units // span_y), jnp.bfloat16)
    blocks = [block] if block else []

    parts = (2, 2, 2, 2, 1, rows // MEMBERS, width)
    whole, coming = Journey(signal.reshape(parts)), Journey(cotangent.reshape(parts))
    whole.hop(z, steps, halves)
    coming.hop(core, steps, halves)
    coming.hop(x, steps, halves)
    coming.hop(y, steps, halves)
    first, second = whole.split()
    first.hop(x, steps, halves)
    second.hop(y, steps, halves)
    first.hop(y, steps, halves)
    second.hop(x, steps, halves)
    first.hop(core, steps, halves)
    second.hop(core, steps, halves)
    first.held = coming.hop(z, steps, halves, first.held)
    up, down = load(place, w_up, w_down)

    total = len(MASKS) * (MEMBERS // 2) * (rows // MEMBERS)
    pairs, bf16 = total // len(MASKS), jnp.bfloat16
    matmul = 2 * depth * units
    state_type = (MEMBERS, rows // MEMBERS, width)
    state, hidden, slope, normed, normed_t, factor = call(
        functools.partial(forward_kernel, landings),
        [
            pltpu.VMEM(state_type, bf16),
            pltpu.VMEM((total, units), bf16),
            pltpu.VMEM((total, units), bf16),
            pltpu.VMEM((total, depth), bf16),
            pltpu.VMEM((depth, total), bf16),
            pltpu.VMEM((total, LANES), jnp.float32),
        ],
        4 * matmul * total,
        place, first.held, second.held, up, down,
        scratch=[pltpu.VMEM(state_type, bf16)],
    )
    going = Journey(state.reshape(parts))
    coming.held = going.hop(z, steps, halves, coming.held)
    later, grad_t, last, *given_down = call(
        functools.partial(backward_kernel, places[0]),
        [pltpu.VMEM((total - pairs, units), bf16), pltpu.VMEM((depth, total), bf16), pltpu.VMEM((pairs, depth), bf16)]
        + blocks,
        3 * matmul * total,
        place, coming.held, hidden, slope, normed, factor, up, down,
        scratch=[pltpu.VMEM(state_type, bf16)],
    )
    take_down = swap(given_down[0], *steps[core]) if blocks else None
    early, *given_up = call(
        functools.partial(last_kernel, places[1]),
        [pltpu.VMEM((pairs, units), bf16)] + blocks,
        matmul * (total // 2 + pairs),
        place, last, slope, down, normed_t, later,
    )
    if not block:
        for at in (x, core, y):
            going.hop(at, steps, halves)
        mixed_out = settle(place, going)
        d_pre = jnp.concatenate([early, later], 0)
        grad_down = scatter_narrow(halves, grad_t, hidden, [steps[core]] + order_down, span_x, span_y)
        grad_up = scatter_narrow(halves, normed_t, d_pre, [steps[core]] + order_up, span_x, span_y)
        return (mixed_out, grad_up, grad_down)
    take_up = swap(going.hop(x, steps, halves, given_up[0]), *steps[core])
    (keep_down,) = call(
        functools.partial(keep_down_kernel, places[0]), blocks, matmul * total // 2, place, grad_t, hidden
    )

    barrier = lax.optimization_barrier
    give_up = None
    for phase, (step_down, step_up) in enumerate(zip(order_down, order_up)):
        if phase > 0:
            keep_down, give_up = barrier((keep_down, give_up))
        keep_down, give_down = halve(halves, step_down, keep_down, take_down)
        if phase == 2:
            give_down = going.hop(y, steps, halves, give_down)
        take_down = swap(give_down, *step_down)
        if phase == 0:
            after, give_down = barrier((place, give_down))
            (keep_up,) = call(
                functools.partial(keep_up_kernel, places[1]), blocks, matmul * total // 2,
                after, normed_t, later, early,
            )
        else:
            keep_up, give_down = barrier((keep_up, give_down))
        keep_up, give_up = halve(halves, step_up, keep_up, take_up)
        if phase == 0:
            give_up = going.hop(core, steps, halves, give_up)
        take_up = swap(give_up, *step_up)
    return (settle(place, going), last_sum(keep_up, take_up), last_sum(keep_down, take_down))


def solution(mesh):
    return jax.shard_map(
        local,
        mesh=mesh,
        in_specs=(P(("gx", "gy"), None), P(), P(), P(("gx", "gy"), None)),
        out_specs=(P(("gx", "gy"), None), P("gx", "gy"), P("gx", "gy")),
        check_vma=False,
    )
```

time: 104 us -> 102 us (0.981)
  waiting for transfers between devices: 48.4 us -> 44.7 us
  starting transfers between devices: 21.2 us -> 22.9 us
    pallas_call x2 -> x1, Pallas kernels: 11.7 us -> 2.93 us  [load(): pl.pallas_call(load_kernel, out_shape=[pltpu.VMEM(item.shape, item.dtype)...]
    pallas_call x4 -> x5, Pallas kernels: 13.9 us -> 22.4 us  [call(): pl.pallas_call(kernel, out_shape=list(outs), in_specs=[spec(pltpu.SMEM)]...]
    ppermute x18 -> x25, starting transfers between devices: 16.3 us -> 22.9 us  [swap(): return lax.ppermute(block, axis, pairs)]
    all_to_all x1 -> x0, starting transfers between devices: 4.93 us -> none  [exchange(): lax.all_to_all(block, ('gx', 'gy'), split_axis=0, concat_axis=0, axis_ind...]
    all_to_all x1 -> x0, waiting for transfers between devices: 4.17 us -> none  [exchange(): lax.all_to_all(block, ('gx', 'gy'), split_axis=0, concat_axis=0, axis_ind...]
    squeeze x1 -> x3, local copies, waits for them, and re-layouts: 0.04 us -> 1.16 us  [slice_at(): return lax.squeeze(part, (dim,))]
    squeeze x2 -> x10, other arithmetic: 1.38 us -> 2.35 us  [the longest x2 1.38 us: last_sum(): return (kept.astype(jnp.float32) + taken.astype(jnp.float32))[0]]
    ppermute x18 -> x25, waiting for transfers between devices: 44.3 us -> 44.7 us  [swap(): return lax.ppermute(block, axis, pairs)]
  transfers between devices with their start and end apart: 19 -> 25, of which waited for: 10 -> 17; matrix products, arithmetic and copies ran while one was open for 3% -> 3% of each run, Pallas kernels for 26% -> 27%
where the time goes in v9:
time: 102 us
  waiting for transfers between devices  44.7 us (44%)
  Pallas kernels  27.2 us (27%)
  starting transfers between devices  22.9 us (22%)
  other arithmetic  3.85 us (4%)
  local copies, waits for them, and re-layouts  2.01 us (2%)
  between operations  1.11 us (1%)
    ppermute x25, waiting for transfers between devices, swap(): return lax.ppermute(block, axis, pairs)  44.7 us
    ppermute x25, starting transfers between devices, swap(): return lax.ppermute(block, axis, pairs)  22.9 us
    pallas_call x5, Pallas kernels, call(): pl.pallas_call(kernel, out_shape=list(outs), in_specs=[spec(pltpu.SMEM)]...  22.4 us
    pallas_call x1, Pallas kernels, load(): pl.pallas_call(load_kernel, out_shape=[pltpu.VMEM(item.shape, item.dtype)...  2.93 us
  transfers between devices with their start and end apart: 25, of which 17 were waited for; matrix products, arithmetic and copies ran while one was open for 3% of the time, Pallas kernels for 27%

profile of v9, /device:TPU:0, one launch (start us, length us, event | category | flops | bytes accessed | tf_op | source)
XLA Modules:
  0.0 101.8 jit_solution(8541647710297977755)
XLA Ops:
  0.8 1.1 %dynamic-slice_bitcast_fusion.4 = (bf16[2,2,2,1,32,384]{5,4,2,1,0,3:T(8,128)(2,1)S(1)}, bf16[2,2,2,1,32,384]{5,4,2,1,0,3:T(8,128)(2,1)S(1)}) fusion(bf16[2,2,2,2,1,32,384]{6,5,3,2,1,0,4:T(8,128)(2,1)} %bitcast.128, s32[]{:T(128)} %sub.30, s32[]{:T(128)S(6)} %select_n.40), kind=kLoop, calls=%fused_computation.94 | loop fusion | bytes 786440 | tf_op jit(solution)/shard_map/squeeze | solution.py:319
  2.5 3.7 %collective-permute-start.3 = (bf16[2,2,2,1,32,384]{5,4,2,1,0,3:T(8,128)(2,1)S(1)}, bf16[2,2,2,1,32,384]{5,4,2,1,0,3:T(8,128)(2,1)S(1)}, u32[]{:S(2)}, u32[]{:S(2)}) collective-permute-start(bf16[2,2,2,1,32,384]{5,4,2,1,0,3:T(8,128)(2,1)S(1)} %get-tuple-element.111), channel_id=1, source_target_pairs={{0,16},{4,20},{8,24},{12,28},{16,0},{20,4},{24,8},{28,12},{1,17},{... | collective-permute-start | bytes 589832 | tf_op jit(solution)/shard_map/ppermute | solution.py:243
  6.2 2.9 %shard_map.67 = (bf16[768,1536]{1,0:T(8,128)(2,1)S(1)}, bf16[768,1536]{1,0:T(8,128)(2,1)S(1)}) custom-call(s32[4]{0:T(128)S(1)} %pad_add_fusion.place_ref, bf16[768,1536]{1,0:T(8,128)(2,1)} %up_hbm.1, bf16[768,1536]{1,0:T(8,128)(2,1)} %down_hbm.1), custom_call_target="tpu_custom_call" | custom-call | bytes 9437184 | tf_op jit(solution)/shard_map/pallas_call | solution.py:217
  9.2 1.6 %collective-permute-start.1 = (bf16[2,2,2,32,384]{4,3,2,0,1:T(8,128)(2,1)S(1)}, bf16[2,2,2,32,384]{4,3,2,0,1:T(8,128)(2,1)S(1)}, u32[]{:S(2)}, u32[]{:S(2)}) collective-permute-start(bf16[2,2,2,32,384]{4,3,2,0,1:T(8,128)(2,1)S(1)} %bitcast.134), channel_id=1, source_target_pairs={{0,2},{1,3},{2,0},{3,1},{4,6},{5,7},{6,4},{7,5},{8,10},{9,11},{10,... | collective-permute-start | bytes 589832 | tf_op jit(solution)/shard_map/ppermute | solution.py:243
  10.8 5.1 %collective-permute-done.3 = bf16[2,2,2,1,32,384]{5,4,2,1,0,3:T(8,128)(2,1)S(1)} collective-permute-done((bf16[2,2,2,1,32,384]{5,4,2,1,0,3:T(8,128)(2,1)S(1)}, bf16[2,2,2,1,32,384]{5,4,2,1,0,3:T(8,128)(2,1)S(1)}, u32[]{:S(2)}, u32[]{:S(2)}) %collective-permute-start.3) | collective-permute-done | bytes 196640 | tf_op jit(solution)/shard_map/ppermute | solution.py:243
  16.0 1.6 %collective-permute-start.4 = (bf16[2,2,2,16,384]{4,3,2,1,0:T(8,128)(2,1)S(1)}, bf16[2,2,2,16,384]{4,3,2,1,0:T(8,128)(2,1)S(1)}, u32[]{:S(2)}, u32[]{:S(2)}) collective-permute-start(bf16[2,2,2,16,384]{4,3,2,1,0:T(8,128)(2,1)S(1)} %bitcast.137), channel_id=1, source_target_pairs={{0,2},{1,3},{2,0},{3,1},{4,6},{5,7},{6,4},{7,5},{8,10},{9,11},{10,... | collective-permute-start | bytes 294920 | tf_op jit(solution)/shard_map/ppermute | solution.py:243
  17.7 1.6 %collective-permute-start.7 = (bf16[2,2,2,16,384]{4,3,2,1,0:T(8,128)(2,1)S(1)}, bf16[2,2,2,16,384]{4,3,2,1,0:T(8,128)(2,1)S(1)}, u32[]{:S(2)}, u32[]{:S(2)}) collective-permute-start(bf16[2,2,2,16,384]{4,3,2,1,0:T(8,128)(2,1)S(1)} %bitcast.136), channel_id=1, source_target_pairs={{0,4},{4,0},{8,12},{12,8},{16,20},{20,16},{24,28},{28,24},{1,5},{5... | collective-permute-start | bytes 294920 | tf_op jit(solution)/shard_map/ppermute | solution.py:243
  19.3 1.4 %collective-permute-done.4 = bf16[2,2,2,16,384]{4,3,2,1,0:T(8,128)(2,1)S(1)} collective-permute-done((bf16[2,2,2,16,384]{4,3,2,1,0:T(8,128)(2,1)S(1)}, bf16[2,2,2,16,384]{4,3,2,1,0:T(8,128)(2,1)S(1)}, u32[]{:S(2)}, u32[]{:S(2)}) %collective-permute-start.4) | collective-permute-done | bytes 98336 | tf_op jit(solution)/shard_map/ppermute | solution.py:243
  20.7 1.6 %collective-permute-start.5 = (bf16[2,4,16,384]{3,2,1,0:T(8,128)(2,1)S(1)}, bf16[2,4,16,384]{3,2,1,0:T(8,128)(2,1)S(1)}, u32[]{:S(2)}, u32[]{:S(2)}) collective-permute-start(bf16[2,4,16,384]{3,2,1,0:T(8,128)(2,1)S(1)} %get-tuple-element.125), channel_id=1, source_target_pairs={{0,4},{4,0},{8,12},{12,8},{16,20},{20,16},{24,28},{28,24},{1,5},{5... | collective-permute-start | bytes 294920 | tf_op jit(solution)/shard_map/ppermute | solution.py:243
  22.7 1.3 %collective-permute-start.8 = (bf16[2,4,16,384]{3,2,1,0:T(8,128)(2,1)S(1)}, bf16[2,4,16,384]{3,2,1,0:T(8,128)(2,1)S(1)}, u32[]{:S(2)}, u32[]{:S(2)}) collective-permute-start(bf16[2,4,16,384]{3,2,1,0:T(8,128)(2,1)S(1)} %get-tuple-element.121), channel_id=1, source_target_pairs={{0,2},{1,3},{2,0},{3,1},{4,6},{5,7},{6,4},{7,5},{8,10},{9,11},{10,... | collective-permute-start | bytes 294920 | tf_op jit(solution)/shard_map/ppermute | solution.py:243
  24.6 1.5 %collective-permute-done.5 = bf16[2,4,16,384]{3,2,1,0:T(8,128)(2,1)S(1)} collective-permute-done((bf16[2,4,16,384]{3,2,1,0:T(8,128)(2,1)S(1)}, bf16[2,4,16,384]{3,2,1,0:T(8,128)(2,1)S(1)}, u32[]{:S(2)}, u32[]{:S(2)}) %collective-permute-start.5) | collective-permute-done | bytes 98336 | tf_op jit(solution)/shard_map/ppermute | solution.py:243
  26.3 1.1 %collective-permute-done.8 = bf16[2,4,16,384]{3,2,1,0:T(8,128)(2,1)S(1)} collective-permute-done((bf16[2,4,16,384]{3,2,1,0:T(8,128)(2,1)S(1)}, bf16[2,4,16,384]{3,2,1,0:T(8,128)(2,1)S(1)}, u32[]{:S(2)}, u32[]{:S(2)}) %collective-permute-start.8) | collective-permute-done | bytes 98336 | tf_op jit(solution)/shard_map/ppermute | solution.py:243
  27.6 1.2 %collective-permute-done.9 = bf16[8,16,384]{2,1,0:T(8,128)(2,1)S(1)} collective-permute-done((bf16[8,16,384]{2,1,0:T(8,128)(2,1)S(1)}, bf16[8,16,384]{2,1,0:T(8,128)(2,1)S(1)}, u32[]{:S(2)}, u32[]{:S(2)}) %collective-permute-start.9) | collective-permute-done | bytes 98336 | tf_op jit(solution)/shard_map/ppermute | solution.py:243
  28.8 0.9 collective-permute-done.2
  29.9 8.5 %shard_map.68 = (bf16[16,32,384]{2,1,0:T(8,128)(2,1)S(1)}, bf16[1024,1536]{1,0:T(8,128)(2,1)S(1)}, bf16[1024,1536]{1,0:T(8,128)(2,1)S(1)}, bf16[1024,768]{1,0:T(...) custom-call(s32[4]{0:T(128)S(1)} %pad_add_fusion.place_ref, ...), custom_call_target="tpu_custom_call" | custom-call | flops 9663676416 | bytes 15204352 | tf_op jit(solution)/shard_map/pallas_call | solution.py:230
  38.5 2.5 %collective-permute-done.10 = bf16[8,32,384]{2,1,0:T(8,128)(2,1)S(1)} collective-permute-done((bf16[8,32,384]{2,1,0:T(8,128)(2,1)S(1)}, bf16[8,32,384]{2,1,0:T(8,128)(2,1)S(1)}, u32[]{:S(2)}, u32[]{:S(2)}) %collective-permute-start.10) | collective-permute-done | bytes 196640 | tf_op jit(solution)/shard_map/ppermute | solution.py:243
  41.5 7.3 %shard_map.69 = (bf16[768,1536]{1,0:T(8,128)(2,1)S(1)}, bf16[768,1024]{1,0:T(8,128)(2,1)S(1)}, bf16[256,768]{1,0:T(8,128)(2,1)S(1)}, bf16[16,96,384]{2,1,0:T(8,128)(2,1)S(1)}) custom-call(s32[4]{0:T(128)S(1)} %pad_add_fusion.place_ref, bf16[16,32,384]{2,1,0:T(8,128)(2,1)S(1)} %pad_maximum_fusion.grad_ref, ...), custom_call_target="tpu_custom_call" | custom-call | flops 7247757312 | bytes 18743296 | tf_op jit(solution)/shard_map/pallas_call | solution.py:230
  48.8 2.7 %shard_map.70 = (bf16[256,1536]{1,0:T(8,128)(2,1)S(1)}, bf16[16,96,384]{2,1,0:T(8,128)(2,1)S(1)}) custom-call(s32[4]{0:T(128)S(1)} %pad_add_fusion.place_ref, bf16[256,768]{1,0:T(8,128)(2,1)S(1)} %get-tuple-element.65.last_ref, bf16[1024,1536]{1,0:T(8,128)(2,1)S(1)} %get-tuple-element.62.slope_ref, bf16[768,1536]{1,0:T(8,128)(2,1)S(1)} %get-tuple-element.56.down_ref, ...), custom_call_target="tpu_custom_call" | custom-call | flops 1811939328 | bytes 11796480 | tf_op jit(solution)/shard_map/pallas_call | solution.py:230
  52.4 1.0 collective-permute-start.12
  53.4 1.9 %shard_map.71 = bf16[16,96,384]{2,1,0:T(8,128)(2,1)S(1)} custom-call(s32[4]{0:T(128)S(1)} %pad_add_fusion.place_ref, bf16[768,1024]{1,0:T(8,128)(2,1)S(1)} %get-tuple-element.70.grad_t_ref, bf16[1024,1536]{1,0:T(8,128)(2,1)S(1)} %get-tuple-element.61.hidden_ref), custom_call_target="tpu_custom_call" | custom-call | flops 1207959552 | bytes 5898240 | tf_op jit(solution)/shard_map/pallas_call | solution.py:230
  55.4 4.4 %collective-permute-done.12 = bf16[2,2,2,32,384]{4,3,2,0,1:T(8,128)(2,1)S(1)} collective-permute-done((bf16[2,2,2,32,384]{4,3,2,0,1:T(8,128)(2,1)S(1)}, bf16[2,2,2,32,384]{4,3,2,0,1:T(8,128)(2,1)S(1)}, u32[]{:S(2)}, u32[]{:S(2)}) %collective-permute-start.12) | collective-permute-done | bytes 196640 | tf_op jit(solution)/shard_map/ppermute | solution.py:243
  60.1 2.0 %collective-permute-start.16 = (bf16[8,96,384]{2,1,0:T(8,128)(2,1)S(1)}, bf16[8,96,384]{2,1,0:T(8,128)(2,1)S(1)}, u32[]{:S(2)}, u32[]{:S(2)}) collective-permute-start(bf16[8,96,384]{2,1,0:T(8,128)(2,1)S(1)} %get-tuple-element.90), channel_id=1, source_target_pairs={{0,4},{4,0},{8,12},{12,8},{16,20},{20,16},{24,28},{28,24},{1,5},{5... | collective-permute-start | bytes 1769480 | tf_op jit(solution)/shard_map/ppermute | solution.py:243
  62.1 1.9 %shard_map.72 = bf16[16,96,384]{2,1,0:T(8,128)(2,1)S(1)} custom-call(s32[4]{0:T(128)S(1)} %pad_add_fusion.place_ref, bf16[768,1024]{1,0:T(8,128)(2,1)S(1)} %get-tuple-element.66.normed_t_ref, bf16[768,1536]{1,0:T(8,128)(2,1)S(1)} %get-tuple-element.67.later_ref, bf16[256,1536]{1,0:T(8,128)(2,1)S(1)} %get-tuple-element.73.first_ref), custom_call_target="tpu_custom_call" | custom-call | flops 1207959552 | bytes 5898240 | tf_op jit(solution)/shard_map/pallas_call | solution.py:230
  64.8 10.5 %collective-permute-done.16 = bf16[8,96,384]{2,1,0:T(8,128)(2,1)S(1)} collective-permute-done((bf16[8,96,384]{2,1,0:T(8,128)(2,1)S(1)}, bf16[8,96,384]{2,1,0:T(8,128)(2,1)S(1)}, u32[]{:S(2)}, u32[]{:S(2)}) %collective-permute-start.16) | collective-permute-done | bytes 589856 | tf_op jit(solution)/shard_map/ppermute | solution.py:243
  76.2 4.5 %collective-permute-done.17 = bf16[8,96,384]{2,1,0:T(8,128)(2,1)S(1)} collective-permute-done((bf16[8,96,384]{2,1,0:T(8,128)(2,1)S(1)}, bf16[8,96,384]{2,1,0:T(8,128)(2,1)S(1)}, u32[]{:S(2)}, u32[]{:S(2)}) %collective-permute-start.17) | collective-permute-done | bytes 589856 | tf_op jit(solution)/shard_map/ppermute | solution.py:243
  81.7 3.7 %collective-permute-done.18 = bf16[4,96,384]{2,1,0:T(8,128)(2,1)S(1)} collective-permute-done((bf16[4,96,384]{2,1,0:T(8,128)(2,1)S(1)}, bf16[4,96,384]{2,1,0:T(8,128)(2,1)S(1)}, u32[]{:S(2)}, u32[]{:S(2)}) %collective-permute-start.18) | collective-permute-done | bytes 294944 | tf_op jit(solution)/shard_map/ppermute | solution.py:243
  85.5 1.3 %collective-permute-start.21 = (bf16[2,96,384]{2,1,0:T(8,128)(2,1)S(1)}, bf16[2,96,384]{2,1,0:T(8,128)(2,1)S(1)}, u32[]{:S(2)}, u32[]{:S(2)}) collective-permute-start(bf16[2,96,384]{2,1,0:T(8,128)(2,1)S(1)} %get-tuple-element.81), channel_id=1, source_target_pairs={{0,16},{4,20},{8,24},{12,28},{16,0},{20,4},{24,8},{28,12},{1,17},{... | collective-permute-start | bytes 442376 | tf_op jit(solution)/shard_map/ppermute | solution.py:243
  87.2 1.0 collective-permute-done.20
  89.0 4.1 %collective-permute-done.21 = bf16[2,96,384]{2,1,0:T(8,128)(2,1)S(1)} collective-permute-done((bf16[2,96,384]{2,1,0:T(8,128)(2,1)S(1)}, bf16[2,96,384]{2,1,0:T(8,128)(2,1)S(1)}, u32[]{:S(2)}, u32[]{:S(2)}) %collective-permute-start.21) | collective-permute-done | bytes 147488 | tf_op jit(solution)/shard_map/ppermute | solution.py:243
  93.8 1.9 %shard_map.73 = bf16[512,384]{1,0:T(8,128)(2,1)} custom-call(s32[4]{0:T(128)} %copy-done, bf16[8,32,384]{2,1,0:T(8,128)(2,1)} %get-tuple-element.100.kept_ref, bf16[8,32,384]{2,1,0:T(8,128)(2,1)} %copy-done.2), custom_call_target="tpu_custom_call" | custom-call | bytes 786432 | tf_op jit(solution)/shard_map/pallas_call | solution.py:325
  95.8 3.0 %collective-permute-start.23 = (bf16[1,96,384]{2,1,0:T(8,128)(2,1)S(1)}, bf16[1,96,384]{2,1,0:T(8,128)(2,1)S(1)}, u32[]{:S(2)}, u32[]{:S(2)}) collective-permute-start(bf16[1,96,384]{2,1,0:T(8,128)(2,1)S(1)} %add_convert_fusion.13), channel_id=1, source_target_pairs={{0,16},{4,20},{8,24},{12,28},{16,0},{20,4},{24,8},{28,12},{1,17},{... | collective-permute-start | bytes 221192 | tf_op jit(solution)/shard_map/ppermute | solution.py:243
  99.5 1.6 %collective-permute-done.23 = bf16[1,96,384]{2,1,0:T(8,128)(2,1)S(1)} collective-permute-done((bf16[1,96,384]{2,1,0:T(8,128)(2,1)S(1)}, bf16[1,96,384]{2,1,0:T(8,128)(2,1)S(1)}, u32[]{:S(2)}, u32[]{:S(2)}) %collective-permute-start.23) | collective-permute-done | bytes 73760 | tf_op jit(solution)/shard_map/ppermute | solution.py:243
  (69 shorter events, 10.2 us)
Async XLA Ops:
  0.6 1.8 %copy-start.1 = (bf16[512,384]{1,0:T(8,128)(2,1)S(1)}, bf16[512,384]{1,0:T(8,128)(2,1)}, u32[]{:S(2)}) copy-start(bf16[512,384]{1,0:T(8,128)(2,1)} %param.4) | copy-start | bytes 1179652
  0.8 61.3 %copy-start = (s32[4]{0:T(128)}, s32[4]{0:T(128)S(1)}, u32[]{:S(2)}) copy-start(s32[4]{0:T(128)S(1)} %pad_add_fusion.place_ref) | copy-start | bytes 52
  1.9 7.2 %collective-permute-start = (bf16[2,2,2,1,32,384]{5,4,2,1,0,3:T(8,128)(2,1)S(1)}, bf16[2,2,2,1,32,384]{5,4,2,1,0,3:T(8,128)(2,1)S(1)}, u32[]{:S(2)}, u32[]{:S(2)}) collective-permute-start(bf16[2,2,2,1,32,384]{5,4,2,1,0,3:T(8,128)(2,1)S(1)} %get-tuple-element.117), channel_id=1, source_target_pairs={{0,1},{1,0},{2,3},{3,2},{4,5},{5,4},{6,7},{7,6},{8,9},{9,8},{10,11... | collective-permute-start | bytes 589832 | tf_op jit(solution)/shard_map/ppermute | solution.py:243
  2.5 13.4 %collective-permute-start.3 = (bf16[2,2,2,1,32,384]{5,4,2,1,0,3:T(8,128)(2,1)S(1)}, bf16[2,2,2,1,32,384]{5,4,2,1,0,3:T(8,128)(2,1)S(1)}, u32[]{:S(2)}, u32[]{:S(2)}) collective-permute-start(bf16[2,2,2,1,32,384]{5,4,2,1,0,3:T(8,128)(2,1)S(1)} %get-tuple-element.111), channel_id=1, source_target_pairs={{0,16},{4,20},{8,24},{12,28},{16,0},{20,4},{24,8},{28,12},{1,17},{... | collective-permute-start | bytes 589832 | tf_op jit(solution)/shard_map/ppermute | solution.py:243
  9.2 14.7 %collective-permute-start.1 = (bf16[2,2,2,32,384]{4,3,2,0,1:T(8,128)(2,1)S(1)}, bf16[2,2,2,32,384]{4,3,2,0,1:T(8,128)(2,1)S(1)}, u32[]{:S(2)}, u32[]{:S(2)}) collective-permute-start(bf16[2,2,2,32,384]{4,3,2,0,1:T(8,128)(2,1)S(1)} %bitcast.134), channel_id=1, source_target_pairs={{0,2},{1,3},{2,0},{3,1},{4,6},{5,7},{6,4},{7,5},{8,10},{9,11},{10,... | collective-permute-start | bytes 589832 | tf_op jit(solution)/shard_map/ppermute | solution.py:243
  16.0 4.7 %collective-permute-start.4 = (bf16[2,2,2,16,384]{4,3,2,1,0:T(8,128)(2,1)S(1)}, bf16[2,2,2,16,384]{4,3,2,1,0:T(8,128)(2,1)S(1)}, u32[]{:S(2)}, u32[]{:S(2)}) collective-permute-start(bf16[2,2,2,16,384]{4,3,2,1,0:T(8,128)(2,1)S(1)} %bitcast.137), channel_id=1, source_target_pairs={{0,2},{1,3},{2,0},{3,1},{4,6},{5,7},{6,4},{7,5},{8,10},{9,11},{10,... | collective-permute-start | bytes 294920 | tf_op jit(solution)/shard_map/ppermute | solution.py:243
  17.7 5.0 %collective-permute-start.7 = (bf16[2,2,2,16,384]{4,3,2,1,0:T(8,128)(2,1)S(1)}, bf16[2,2,2,16,384]{4,3,2,1,0:T(8,128)(2,1)S(1)}, u32[]{:S(2)}, u32[]{:S(2)}) collective-permute-start(bf16[2,2,2,16,384]{4,3,2,1,0:T(8,128)(2,1)S(1)} %bitcast.136), channel_id=1, source_target_pairs={{0,4},{4,0},{8,12},{12,8},{16,20},{20,16},{24,28},{28,24},{1,5},{5... | collective-permute-start | bytes 294920 | tf_op jit(solution)/shard_map/ppermute | solution.py:243
  20.7 5.4 %collective-permute-start.5 = (bf16[2,4,16,384]{3,2,1,0:T(8,128)(2,1)S(1)}, bf16[2,4,16,384]{3,2,1,0:T(8,128)(2,1)S(1)}, u32[]{:S(2)}, u32[]{:S(2)}) collective-permute-start(bf16[2,4,16,384]{3,2,1,0:T(8,128)(2,1)S(1)} %get-tuple-element.125), channel_id=1, source_target_pairs={{0,4},{4,0},{8,12},{12,8},{16,20},{20,16},{24,28},{28,24},{1,5},{5... | collective-permute-start | bytes 294920 | tf_op jit(solution)/shard_map/ppermute | solution.py:243
  22.7 4.7 %collective-permute-start.8 = (bf16[2,4,16,384]{3,2,1,0:T(8,128)(2,1)S(1)}, bf16[2,4,16,384]{3,2,1,0:T(8,128)(2,1)S(1)}, u32[]{:S(2)}, u32[]{:S(2)}) collective-permute-start(bf16[2,4,16,384]{3,2,1,0:T(8,128)(2,1)S(1)} %get-tuple-element.121), channel_id=1, source_target_pairs={{0,2},{1,3},{2,0},{3,1},{4,6},{5,7},{6,4},{7,5},{8,10},{9,11},{10,... | collective-permute-start | bytes 294920 | tf_op jit(solution)/shard_map/ppermute | solution.py:243
  24.0 5.7 %collective-permute-start.2 = (bf16[2,4,32,384]{3,2,1,0:T(8,128)(2,1)S(1)}, bf16[2,4,32,384]{3,2,1,0:T(8,128)(2,1)S(1)}, u32[]{:S(2)}, u32[]{:S(2)}) collective-permute-start(bf16[2,4,32,384]{3,2,1,0:T(8,128)(2,1)S(1)} %get-tuple-element.113), channel_id=1, source_target_pairs={{0,4},{4,0},{8,12},{12,8},{16,20},{20,16},{24,28},{28,24},{1,5},{5... | collective-permute-start | bytes 589832 | tf_op jit(solution)/shard_map/ppermute | solution.py:243
  26.2 1.4 %collective-permute-start.6 = (bf16[8,16,384]{2,1,0:T(8,128)(2,1)S(1)}, bf16[8,16,384]{2,1,0:T(8,128)(2,1)S(1)}, u32[]{:S(2)}, u32[]{:S(2)}) collective-permute-start(bf16[8,16,384]{2,1,0:T(8,128)(2,1)S(1)} %get-tuple-element.124), channel_id=1, source_target_pairs={{0,1},{1,0},{2,3},{3,2},{4,5},{5,4},{6,7},{7,6},{8,9},{9,8},{10,11... | collective-permute-start | bytes 294920 | tf_op jit(solution)/shard_map/ppermute | solution.py:243
  27.4 1.4 %collective-permute-start.9 = (bf16[8,16,384]{2,1,0:T(8,128)(2,1)S(1)}, bf16[8,16,384]{2,1,0:T(8,128)(2,1)S(1)}, u32[]{:S(2)}, u32[]{:S(2)}) collective-permute-start(bf16[8,16,384]{2,1,0:T(8,128)(2,1)S(1)} %get-tuple-element.120), channel_id=1, source_target_pairs={{0,1},{1,0},{2,3},{3,2},{4,5},{5,4},{6,7},{7,6},{8,9},{9,8},{10,11... | collective-permute-start | bytes 294920 | tf_op jit(solution)/shard_map/ppermute | solution.py:243
  29.8 11.2 %collective-permute-start.10 = (bf16[8,32,384]{2,1,0:T(8,128)(2,1)S(1)}, bf16[8,32,384]{2,1,0:T(8,128)(2,1)S(1)}, u32[]{:S(2)}, u32[]{:S(2)}) collective-permute-start(bf16[8,32,384]{2,1,0:T(8,128)(2,1)S(1)} %get-tuple-element.58), channel_id=1, source_target_pairs={{0,16},{4,20},{8,24},{12,28},{16,0},{20,4},{24,8},{28,12},{1,17},{... | collective-permute-start | bytes 589832 | tf_op jit(solution)/shard_map/ppermute | solution.py:243
  41.0 11.2 %collective-permute-start.11 = (bf16[2,2,2,1,32,384]{5,4,2,1,0,3:T(8,128)(2,1)S(1)}, bf16[2,2,2,1,32,384]{5,4,2,1,0,3:T(8,128)(2,1)S(1)}, u32[]{:S(2)}, u32[]{:S(2)}) collective-permute-start(bf16[2,2,2,1,32,384]{5,4,2,1,0,3:T(8,128)(2,1)S(1)} %get-tuple-element.59), channel_id=1, source_target_pairs={{0,16},{4,20},{8,24},{12,28},{16,0},{20,4},{24,8},{28,12},{1,17},{... | collective-permute-start | bytes 589832 | tf_op jit(solution)/shard_map/ppermute | solution.py:243
  48.8 11.0 %collective-permute-start.13 = (bf16[16,96,384]{2,1,0:T(8,128)(2,1)S(1)}, bf16[16,96,384]{2,1,0:T(8,128)(2,1)S(1)}, u32[]{:S(2)}, u32[]{:S(2)}) collective-permute-start(bf16[16,96,384]{2,1,0:T(8,128)(2,1)S(1)} %get-tuple-element.71), channel_id=1, source_target_pairs={{0,1},{1,0},{2,3},{3,2},{4,5},{5,4},{6,7},{7,6},{8,9},{9,8},{10,11... | collective-permute-start | bytes 3538952 | tf_op jit(solution)/shard_map/ppermute | solution.py:243
  52.3 11.7 %collective-permute-start.14 = (bf16[16,96,384]{2,1,0:T(8,128)(2,1)S(1)}, bf16[16,96,384]{2,1,0:T(8,128)(2,1)S(1)}, u32[]{:S(2)}, u32[]{:S(2)}) collective-permute-start(bf16[16,96,384]{2,1,0:T(8,128)(2,1)S(1)} %get-tuple-element.74), channel_id=1, source_target_pairs={{0,1},{1,0},{2,3},{3,2},{4,5},{5,4},{6,7},{7,6},{8,9},{9,8},{10,11... | collective-permute-start | bytes 3538952 | tf_op jit(solution)/shard_map/ppermute | solution.py:243
  52.4 7.3 %collective-permute-start.12 = (bf16[2,2,2,32,384]{4,3,2,0,1:T(8,128)(2,1)S(1)}, bf16[2,2,2,32,384]{4,3,2,0,1:T(8,128)(2,1)S(1)}, u32[]{:S(2)}, u32[]{:S(2)}) collective-permute-start(bf16[2,2,2,32,384]{4,3,2,0,1:T(8,128)(2,1)S(1)} %bitcast.135), channel_id=1, source_target_pairs={{0,2},{1,3},{2,0},{3,1},{4,6},{5,7},{6,4},{7,5},{8,10},{9,11},{10,... | collective-permute-start | bytes 589832 | tf_op jit(solution)/shard_map/ppermute | solution.py:243
  60.1 15.2 %collective-permute-start.16 = (bf16[8,96,384]{2,1,0:T(8,128)(2,1)S(1)}, bf16[8,96,384]{2,1,0:T(8,128)(2,1)S(1)}, u32[]{:S(2)}, u32[]{:S(2)}) collective-permute-start(bf16[8,96,384]{2,1,0:T(8,128)(2,1)S(1)} %get-tuple-element.90), channel_id=1, source_target_pairs={{0,4},{4,0},{8,12},{12,8},{16,20},{20,16},{24,28},{28,24},{1,5},{5... | collective-permute-start | bytes 1769480 | tf_op jit(solution)/shard_map/ppermute | solution.py:243
  64.4 16.3 %collective-permute-start.17 = (bf16[8,96,384]{2,1,0:T(8,128)(2,1)S(1)}, bf16[8,96,384]{2,1,0:T(8,128)(2,1)S(1)}, u32[]{:S(2)}, u32[]{:S(2)}) collective-permute-start(bf16[8,96,384]{2,1,0:T(8,128)(2,1)S(1)} %get-tuple-element.76), channel_id=1, source_target_pairs={{0,2},{1,3},{2,0},{3,1},{4,6},{5,7},{6,4},{7,5},{8,10},{9,11},{10,... | collective-permute-start | bytes 1769480 | tf_op jit(solution)/shard_map/ppermute | solution.py:243
  64.8 16.2 %collective-permute-start.15 = (bf16[2,4,32,384]{3,2,1,0:T(8,128)(2,1)S(1)}, bf16[2,4,32,384]{3,2,1,0:T(8,128)(2,1)S(1)}, u32[]{:S(2)}, u32[]{:S(2)}) collective-permute-start(bf16[2,4,32,384]{3,2,1,0:T(8,128)(2,1)S(1)} %get-tuple-element.75), channel_id=1, source_target_pairs={{0,1},{1,0},{2,3},{3,2},{4,5},{5,4},{6,7},{7,6},{8,9},{9,8},{10,11... | collective-permute-start | bytes 589832 | tf_op jit(solution)/shard_map/ppermute | solution.py:243
  75.4 10.0 %collective-permute-start.18 = (bf16[4,96,384]{2,1,0:T(8,128)(2,1)S(1)}, bf16[4,96,384]{2,1,0:T(8,128)(2,1)S(1)}, u32[]{:S(2)}, u32[]{:S(2)}) collective-permute-start(bf16[4,96,384]{2,1,0:T(8,128)(2,1)S(1)} %get-tuple-element.94), channel_id=1, source_target_pairs={{0,2},{1,3},{2,0},{3,1},{4,6},{5,7},{6,4},{7,5},{8,10},{9,11},{10,... | collective-permute-start | bytes 884744 | tf_op jit(solution)/shard_map/ppermute | solution.py:243
  80.9 7.3 %collective-permute-start.20 = (bf16[4,96,384]{2,1,0:T(8,128)(2,1)S(1)}, bf16[4,96,384]{2,1,0:T(8,128)(2,1)S(1)}, u32[]{:S(2)}, u32[]{:S(2)}) collective-permute-start(bf16[4,96,384]{2,1,0:T(8,128)(2,1)S(1)} %get-tuple-element.92), channel_id=1, source_target_pairs={{0,4},{4,0},{8,12},{12,8},{16,20},{20,16},{24,28},{28,24},{1,5},{5... | collective-permute-start | bytes 884744 | tf_op jit(solution)/shard_map/ppermute | solution.py:243
  85.5 7.5 %collective-permute-start.21 = (bf16[2,96,384]{2,1,0:T(8,128)(2,1)S(1)}, bf16[2,96,384]{2,1,0:T(8,128)(2,1)S(1)}, u32[]{:S(2)}, u32[]{:S(2)}) collective-permute-start(bf16[2,96,384]{2,1,0:T(8,128)(2,1)S(1)} %get-tuple-element.81), channel_id=1, source_target_pairs={{0,16},{4,20},{8,24},{12,28},{16,0},{20,4},{24,8},{28,12},{1,17},{... | collective-permute-start | bytes 442376 | tf_op jit(solution)/shard_map/ppermute | solution.py:243
  86.8 6.3 %collective-permute-start.19 = (bf16[8,32,384]{2,1,0:T(8,128)(2,1)S(1)}, bf16[8,32,384]{2,1,0:T(8,128)(2,1)S(1)}, u32[]{:S(2)}, u32[]{:S(2)}) collective-permute-start(bf16[8,32,384]{2,1,0:T(8,128)(2,1)S(1)} %get-tuple-element.80), channel_id=1, source_target_pairs={{0,4},{4,0},{8,12},{12,8},{16,20},{20,16},{24,28},{28,24},{1,5},{5... | collective-permute-start | bytes 589832 | tf_op jit(solution)/shard_map/ppermute | solution.py:243
  88.3 7.5 %collective-permute-start.22 = (bf16[2,96,384]{2,1,0:T(8,128)(2,1)S(1)}, bf16[2,96,384]{2,1,0:T(8,128)(2,1)S(1)}, u32[]{:S(2)}, u32[]{:S(2)}) collective-permute-start(bf16[2,96,384]{2,1,0:T(8,128)(2,1)S(1)} %get-tuple-element.98), channel_id=1, source_target_pairs={{0,8},{4,12},{8,0},{12,4},{16,24},{20,28},{24,16},{28,20},{1,9},{5... | collective-permute-start | bytes 442376 | tf_op jit(solution)/shard_map/ppermute | solution.py:243
  93.1 5.8 %collective-permute-start.24 = (bf16[1,96,384]{2,1,0:T(8,128)(2,1)S(1)}, bf16[1,96,384]{2,1,0:T(8,128)(2,1)S(1)}, u32[]{:S(2)}, u32[]{:S(2)}) collective-permute-start(bf16[1,96,384]{2,1,0:T(8,128)(2,1)S(1)} %add_convert_fusion.15), channel_id=1, source_target_pairs={{0,8},{4,12},{8,0},{12,4},{16,24},{20,28},{24,16},{28,20},{1,9},{5... | collective-permute-start | bytes 221192 | tf_op jit(solution)/shard_map/ppermute | solution.py:243
  93.2 0.7 copy-start.2
  95.8 5.3 %collective-permute-start.23 = (bf16[1,96,384]{2,1,0:T(8,128)(2,1)S(1)}, bf16[1,96,384]{2,1,0:T(8,128)(2,1)S(1)}, u32[]{:S(2)}, u32[]{:S(2)}) collective-permute-start(bf16[1,96,384]{2,1,0:T(8,128)(2,1)S(1)} %add_convert_fusion.13), channel_id=1, source_target_pairs={{0,16},{4,20},{8,24},{12,28},{16,0},{20,4},{24,8},{28,12},{1,17},{... | collective-permute-start | bytes 221192 | tf_op jit(solution)/shard_map/ppermute | solution.py:243

commit v10 on v7

--- a/solution.py
+++ b/solution.py
@@ -52,18 +52,18 @@
     return [member for member in range(MEMBERS) if not member & mask]
 
 
-def read_pair(ref, mask, spots=range(MEMBERS), swapped=0):
-    low = jnp.concatenate([ref[spots[member] ^ swapped] for member in low_members(mask)], 0)
-    high = jnp.concatenate([ref[spots[member | mask] ^ swapped] for member in low_members(mask)], 0)
+def read_pair(ref, mask, swapped=0):
+    low = jnp.concatenate([ref[member ^ swapped] for member in low_members(mask)], 0)
+    high = jnp.concatenate([ref[(member | mask) ^ swapped] for member in low_members(mask)], 0)
     return jnp.concatenate([low, high], 1).astype(jnp.float32)
 
 
-def write_pair(ref, mask, pair, spots=range(MEMBERS), swapped=0):
+def write_pair(ref, mask, pair):
     rows, width = ref.shape[1:]
     for place, member in enumerate(low_members(mask)):
         part = pair[place * rows : (place + 1) * rows]
-        ref[spots[member] ^ swapped] = part[:, :width]
-        ref[spots[member | mask] ^ swapped] = part[:, width:]
+        ref[member] = part[:, :width]
+        ref[member | mask] = part[:, width:]
 
 
 def write_blocks(places, bit, left_ref, right_ref, out_ref):
@@ -85,13 +85,17 @@
                 ]
 
 
+def load_kernel(place_ref, source, target, arrived):
+    copy = pltpu.make_async_copy(source, target, arrived)
+    copy.start()
+    copy.wait()
+
+
 def forward_kernel(
-    spots, place_ref, state_ref, up_hbm, down_hbm,
-    out_ref, hidden_ref, slope_ref, normed_ref, normed_t_ref, factor_ref, up_ref, down_ref, work_ref, arrived
+    state_ref, up_ref, down_hbm,
+    out_ref, hidden_ref, slope_ref, normed_ref, normed_t_ref, factor_ref, down_ref, work_ref, arrived
 ):
-    fetch_up = pltpu.make_async_copy(up_hbm, up_ref, arrived.at[0])
-    fetch_down = pltpu.make_async_copy(down_hbm, down_ref, arrived.at[1])
-    fetch_up.start()
+    fetch_down = pltpu.make_async_copy(down_hbm, down_ref, arrived)
     fetch_down.start()
     pairs = MEMBERS // 2 * work_ref.shape[1]
     hidden_units = up_ref.shape[1]
@@ -106,8 +110,6 @@
         normed = (shifted * factor).astype(jnp.bfloat16)
         normed_ref[at, :] = normed
         factor_ref[at, :] = jnp.broadcast_to(factor, (pairs, LANES))
-        if section == 0:
-            fetch_up.wait()
         for start in range(0, hidden_units, CHUNK):
             units = pl.ds(start, CHUNK)
             pre = jnp.dot(normed, up_ref[:, units], preferred_element_type=jnp.float32)
@@ -118,10 +120,7 @@
         if section == 0:
             fetch_down.wait()
         mixed = (pair + contract_last(hidden_ref[at, :], down_ref[...])).astype(jnp.bfloat16)
-        if section < last:
-            write_pair(work_ref, mask, mixed)
-        else:
-            write_pair(out_ref, mask, mixed, spots, place_ref[2])
+        write_pair(work_ref if section < last else out_ref, mask, mixed)
         normed_t_ref[:, at] = normed.T
 
 
@@ -168,17 +167,12 @@
     write_blocks(places_up, 1 - place_ref[1], normed_t_ref, d_pre_ref, up_ref)
 
 
-def arrange_kernel(spots, place_ref, block_ref, out_ref):
-    rows = out_ref.shape[1]
-    for member, spot in enumerate(spots):
-        out_ref[spot ^ place_ref[3]] = block_ref[member * rows : (member + 1) * rows]
-
-
-def settle_kernel(sources, place_ref, kept_ref, taken_ref, out_ref, done):
-    half, rows = kept_ref.shape[:2]
+def settle_kernel(sources, place_ref, *refs):
+    parts, out_ref, done = refs[:-2], refs[-2], refs[-1]
+    count, rows = parts[0].shape[:2]
     copies = []
     for index, source in enumerate(sources):
-        block = kept_ref.at[index] if index < half else taken_ref.at[index - half]
+        block = parts[index // count].at[index % count]
         first = pl.multiple_of((place_ref[0] ^ source) * rows, rows)
         copies.append(pltpu.make_async_copy(block, out_ref.at[pl.ds(first, rows)], done.at[index]))
     for copy in copies:
@@ -209,10 +203,22 @@
     return [pltpu.with_memory_space_constraint(item, pltpu.VMEM) for item in items]
 
 
-def forward(place, state, w_up, w_down, spots):
+def load(place, weight):
+    return pl.pallas_call(
+        load_kernel,
+        out_shape=pltpu.VMEM(weight.shape, weight.dtype),
+        in_specs=[spec(pltpu.SMEM), spec(pltpu.HBM)],
+        out_specs=spec(pltpu.VMEM),
+        scratch_shapes=[pltpu.SemaphoreType.DMA],
+        compiler_params=pltpu.CompilerParams(vmem_limit_bytes=KEEP_BYTES),
+        cost_estimate=pl.CostEstimate(flops=0, bytes_accessed=4 * weight.size, transcendentals=0),
+    )(place, pltpu.with_memory_space_constraint(weight, pltpu.HBM))
+
+
+def forward(state, up, w_down):
     members, rows, width = state.shape
     total = len(MASKS) * (members // 2) * rows
-    depth, units = w_up.shape
+    depth, units = up.shape
     bf16 = jnp.bfloat16
     outs = [
         pltpu.VMEM(state.shape, bf16),
@@ -221,20 +227,19 @@
         pltpu.VMEM((total, depth), bf16),
         pltpu.VMEM((depth, total), bf16),
         pltpu.VMEM((total, LANES), jnp.float32),
-        pltpu.VMEM(w_up.shape, bf16),
         pltpu.VMEM(w_down.shape, bf16),
     ]
     return pl.pallas_call(
-        functools.partial(forward_kernel, spots),
+        forward_kernel,
         out_shape=outs,
-        in_specs=[spec(pltpu.SMEM), spec(pltpu.VMEM)] + [spec(pltpu.HBM)] * 2,
+        in_specs=[spec(pltpu.VMEM)] * 2 + [spec(pltpu.HBM)],
         out_specs=[spec(pltpu.VMEM)] * len(outs),
-        scratch_shapes=[pltpu.VMEM(state.shape, bf16), pltpu.SemaphoreType.DMA((2,))],
+        scratch_shapes=[pltpu.VMEM(state.shape, bf16), pltpu.SemaphoreType.DMA],
         compiler_params=pltpu.CompilerParams(vmem_limit_bytes=SECTIONS_BYTES),
         cost_estimate=pl.CostEstimate(
             flops=10 * total * depth * units, bytes_accessed=16 * total * units, transcendentals=0
         ),
-    )(place, state, *[pltpu.with_memory_space_constraint(item, pltpu.HBM) for item in (w_up, w_down)])
+    )(state, *in_vmem(up), pltpu.with_memory_space_constraint(w_down, pltpu.HBM))
 
 
 def backward(place, grad, kept, places, block):
@@ -256,18 +261,6 @@
     )(place, grad, *in_vmem(*kept))
 
 
-def arrange(place, block, spots):
-    rows, width = block.shape
-    return pl.pallas_call(
-        functools.partial(arrange_kernel, spots),
-        out_shape=jax.ShapeDtypeStruct((MEMBERS, rows // MEMBERS, width), block.dtype),
-        in_specs=[spec(pltpu.SMEM), spec(pltpu.VMEM)],
-        out_specs=spec(pltpu.VMEM),
-        compiler_params=pltpu.CompilerParams(vmem_limit_bytes=KEEP_BYTES),
-        cost_estimate=pl.CostEstimate(flops=0, bytes_accessed=4 * block.size, transcendentals=0),
-    )(place, block)
-
-
 def keep_blocks(place, hidden, d_pre, normed_t, grad_t, places, block):
     total, units = hidden.shape
     depth = normed_t.shape[0]
@@ -289,9 +282,7 @@
 
 
 def pick(block, at):
-    size = (1,) + block.shape[1:]
-    start = (at,) + (0,) * (block.ndim - 1)
-    return lax.dynamic_slice(block, start, size, allow_negative_indices=False)[0].astype(jnp.float32)
+    return slice_at(block, 0, at).astype(jnp.float32)
 
 
 def finish_sum(halves, kept, taken, order, beside=None):
@@ -320,42 +311,76 @@
 
 
 class Journey:
-    def __init__(self, blocks, steps):
-        self.parts = [blocks[None]]
-        self.steps = list(steps)
-        self.sources = [0]
-
-    def advance(self, other):
-        if not self.steps:
-            return other
-        axis, bit, weight = self.steps.pop(0)
-        held = jnp.concatenate(self.parts, 0)
-        half = held.shape[1] // 2
-        kept, given = held[:, :half], held[:, half:]
-        given, other = lax.optimization_barrier((given, other))
-        self.parts = [kept, swap(given, axis, bit)]
-        self.sources += [source | weight for source in self.sources]
-        return other
-
-    def arrived(self):
-        return [part[:, 0] for part in self.parts]
+    def __init__(self, held, bits=(0, 1, 2, 3), sources=(0,)):
+        self.held = held
+        self.bits = list(bits)
+        self.sources = list(sources)
+        self.parts = None
+
+    def hop(self, at, steps, halves, after=None):
+        dim = self.bits.index(at)
+        mine, other = halves[steps[at]]
+        kept, given = [slice_at(self.held, dim, part) for part in (mine, other)]
+        if after is not None:
+            given, after = lax.optimization_barrier((given, after))
+        self.parts = [kept, swap(given, *steps[at])]
+        self.held = jnp.concatenate(self.parts, -3)
+        self.bits.remove(at)
+        self.sources += [source | MASKS[at] for source in self.sources]
+        return after
+
+    def hop_both(self, at, also, steps, halves, after=None):
+        dims = self.bits.index(at), self.bits.index(also)
+        parts = []
+        for theirs, beyond in ((0, 0), (1, 0), (0, 1), (1, 1)):
+            part = slice_at(self.held, dims[0], halves[steps[at]][theirs], keep=True)
+            part = slice_at(part, dims[1], halves[steps[also]][beyond], keep=True)
+            parts.append(lax.squeeze(part, dims))
+        if after is not None:
+            parts, after = lax.optimization_barrier((parts, after))
+        self.parts = [
+            parts[0],
+            swap(parts[1], *steps[at]),
+            swap(parts[2], *steps[also]),
+            swap_both(parts[3], steps[at], steps[also]),
+        ]
+        self.held = jnp.concatenate(self.parts, -3)
+        for bit in (at, also):
+            self.bits.remove(bit)
+            self.sources += [source | MASKS[bit] for source in self.sources]
+        return after
+
+
+def slice_at(block, dim, at, keep=False):
+    start = [0] * block.ndim
+    start[dim] = at
+    size = list(block.shape)
+    size[dim] = 1
+    part = lax.dynamic_slice(block, start, size, allow_negative_indices=False)
+    return part if keep else lax.squeeze(part, (dim,))
+
+
+def swap_both(block, step, also):
+    span_x, span_y = lax.axis_size("gx"), lax.axis_size("gy")
+    flips = {step[0]: 1 << step[1], also[0]: 1 << also[1]}
+    pairs = []
+    for at_x in range(span_x):
+        for at_y in range(span_y):
+            pairs.append((at_x * span_y + at_y, (at_x ^ flips["gx"]) * span_y + (at_y ^ flips["gy"])))
+    return lax.ppermute(block, ("gx", "gy"), pairs)
 
 
 def settle(place, journey):
-    kept, taken = journey.arrived()
-    half, rows, width = kept.shape
+    parts = journey.parts
+    rows, width = parts[0].shape[-2:]
     return pl.pallas_call(
         functools.partial(settle_kernel, journey.sources),
-        out_shape=jax.ShapeDtypeStruct((2 * half * rows, width), kept.dtype),
-        in_specs=[spec(pltpu.SMEM)] + [spec(pltpu.VMEM)] * 2,
+        out_shape=jax.ShapeDtypeStruct((MEMBERS * rows, width), parts[0].dtype),
+        in_specs=[spec(pltpu.SMEM)] + [spec(pltpu.VMEM)] * len(parts),
         out_specs=spec(pltpu.HBM),
-        scratch_shapes=[pltpu.SemaphoreType.DMA((2 * half,))],
-        cost_estimate=pl.CostEstimate(flops=0, bytes_accessed=8 * kept.size, transcendentals=0),
-    )(place, kept, taken)
-
-
-def spots_of(order):
-    return [sum((m // MASKS[at] & 1) * mask for at, mask in zip(order, MASKS)) for m in range(MEMBERS)]
+        scratch_shapes=[pltpu.SemaphoreType.DMA((MEMBERS,))],
+        cost_estimate=pl.CostEstimate(flops=0, bytes_accessed=4 * MEMBERS * rows * width, transcendentals=0),
+    )(place, *parts)
 
 
 def local(signal, w_up, w_down, cotangent):
@@ -365,50 +390,57 @@
     rows, width = signal.shape
     depth, units = w_up.shape
     steps = [("gx", span_x.bit_length() - 2), ("gx", 0), ("gy", span_y.bit_length() - 2), ("gy", 0)]
-    bits = [lax.axis_index(axis) // (1 << bit) % 2 for axis, bit in steps]
-    member = sum(bit * mask for bit, mask in zip(bits, MASKS))
+    z, y, x, core = range(4)
     rest_y = [("gy", bit) for bit in range(1, span_y.bit_length() - 1)]
     rest_x = [("gx", bit) for bit in range(1, span_x.bit_length() - 1)]
-    core, across = ("gy", 0), ("gx", 0)
-    order_down = [across] + rest_y + rest_x[::-1]
-    order_up = rest_y + [across] + rest_x
-    inbound, homeward = [3, 2, 1, 0], [0, 2, 3, 1]
-    spot_in, spot_home = [sum(bits[at] * mask for at, mask in zip(o, MASKS)) for o in (inbound, homeward)]
-    owns = [lax.axis_index(axis) // (1 << bit) % 2 for axis, bit in [core] + order_up]
-    place = jnp.stack([member, 1 - bits[3], spot_home, spot_in]).astype(jnp.int32)
-    place, owns, others = lax.optimization_barrier((place, owns, [1 - own for own in owns]))
-    halves = {step: (own, other) for step, own, other in zip([core] + order_up, owns, others)}
+    order_down = [steps[y]] + rest_y + rest_x[::-1]
+    order_up = rest_y + [steps[y]] + rest_x
+
+    owns = [lax.axis_index(axis) // (1 << bit) % 2 for axis, bit in [steps[core]] + order_up]
+    own = dict(zip([steps[core]] + order_up, owns))
+    member = sum(own[step] * mask for step, mask in zip(steps, MASKS))
+    place = jnp.stack([member, 1 - own[steps[core]]]).astype(jnp.int32)
+    place, owns, others = lax.optimization_barrier((place, owns, [1 - item for item in owns]))
+    halves = {step: pair for step, pair in zip([steps[core]] + order_up, zip(owns, others))}
     places = [block_places(order, span_x, span_y) for order in (order_down, order_up)]
     block = None
     if units // span_y % LANES == 0:
         block = pltpu.VMEM((span_x * span_y // 2, depth // span_x, units // span_y), jnp.bfloat16)
 
+    parts = (2, 2, 2, 2, 1, rows // MEMBERS, width)
     state = exchange(signal.reshape(MEMBERS, rows // MEMBERS, width), groups)
-    coming = Journey(arrange(place, cotangent, spots_of(inbound)), [steps[at] + (MASKS[at],) for at in inbound])
-    for _ in range(3):
-        place = coming.advance(place)
-    state = coming.advance(state)
-    state, *kept = forward(place, state, w_up, w_down, spots_of(homeward))
-    going = Journey(state, [steps[at] + (MASKS[at],) for at in homeward])
-    going.advance(place)
-    grad = jnp.concatenate(coming.arrived(), 0)
+    coming = Journey(cotangent.reshape(parts))
+    coming.hop(core, steps, halves)
+    coming.hop_both(x, y, steps, halves)
+    up = load(place, w_up)
+    state = coming.hop(z, steps, halves, state)
+    state, *kept, down = forward(state, up, w_down)
+    kept += [up, down]
+    going = Journey(state.reshape(parts))
+    grad = going.hop(z, steps, halves, coming.held)
     d_pre, grad_t, *given = backward(place, grad, kept, places, block)
     hidden, normed_t = kept[0], kept[3]
     if not given:
-        while going.steps:
-            going.advance(place)
+        going.hop(core, steps, halves)
+        going.hop_both(x, y, steps, halves)
         mixed_out = settle(place, going)
-        grad_down = scatter_narrow(halves, grad_t, hidden, [core] + order_down, span_x, span_y)
-        grad_up = scatter_narrow(halves, normed_t, d_pre, [core] + order_up, span_x, span_y)
+        grad_down = scatter_narrow(halves, grad_t, hidden, [steps[core]] + order_down, span_x, span_y)
+        grad_up = scatter_narrow(halves, normed_t, d_pre, [steps[core]] + order_up, span_x, span_y)
         return (mixed_out, grad_up, grad_down)
-    given[0] = going.advance(given[0])
-    take_down, take_up = [swap(part, *core) for part in given]
+    take_down, take_up = [swap(part, *steps[core]) for part in given]
     keep_down, keep_up = keep_blocks(place, hidden, d_pre, normed_t, grad_t, places, block)
+
+    def beside(phase, give):
+        if phase == 0:
+            return going.hop(core, steps, halves, give)
+        if phase == 2:
+            return going.hop_both(x, y, steps, halves, give)
+        if phase == len(order_down) - 1:
+            going.parts, give = lax.optimization_barrier((going.parts, give))
+        return give
+
     grad_up = finish_sum(halves, keep_up, take_up, order_up)
-    beside = lambda phase, give: going.advance(give) if phase in (0, 2) else give
     grad_down = finish_sum(halves, keep_down, take_down, order_down, beside)
-    while going.steps:
-        going.advance(place)
     return (settle(place, going), grad_up, grad_down)
 
 

time: 94.5 us -> 95.4 us (level)
  starting transfers between devices: 22.1 us -> 24.6 us
  local copies, waits for them, and re-layouts: 1.83 us -> 0.82 us
    ppermute x0 -> x2, starting transfers between devices: none -> 4.6 us  [swap_both(): return lax.ppermute(block, ('gx', 'gy'), pairs)]
    ppermute x18, starting transfers between devices: 17.2 us -> 12.6 us  [swap(): return lax.ppermute(block, axis, pairs)]
    all_to_all x1, starting transfers between devices: 4.93 us -> 7.44 us  [exchange(): lax.all_to_all(block, ('gx', 'gy'), split_axis=0, concat_axis=0, axis_ind...]
    unnamed x6 -> x10, local copies, waits for them, and re-layouts: 1.7 us -> 0.58 us
    ppermute x18, waiting for transfers between devices: 36.3 us -> 35.3 us  [swap(): return lax.ppermute(block, axis, pairs)]
  transfers between devices with their start and end apart: 19 -> 21, of which waited for: 11 -> 12; matrix products, arithmetic and copies ran while one was open for 3% -> 3% of each run, Pallas kernels for 26% -> 17%
where the time goes in v10:
time: 95.4 us; the launch traced here: 95.1 us
  waiting for transfers between devices  39.6 us (42%)
  Pallas kernels  25.5 us (27%)
  starting transfers between devices  24.6 us (26%)
  other arithmetic  3.53 us (4%)
  between operations  0.99 us (1%)
    ppermute x18, waiting for transfers between devices, swap(): return lax.ppermute(block, axis, pairs)  35.3 us
    ppermute x18, starting transfers between devices, swap(): return lax.ppermute(block, axis, pairs)  12.6 us
    pallas_call x1, Pallas kernels, backward(): pl.pallas_call(functools.partial(backward_kernel, *places), out_shape=out...  9.51 us
    pallas_call x1, Pallas kernels, forward(): pl.pallas_call(forward_kernel, out_shape=outs, in_specs=[spec(pltpu.VMEM)...  8.72 us
    all_to_all x1, starting transfers between devices, exchange(): lax.all_to_all(block, ('gx', 'gy'), split_axis=0, concat_axis=0, axis_ind...  7.44 us
    ppermute x2, starting transfers between devices, swap_both(): return lax.ppermute(block, ('gx', 'gy'), pairs)  4.6 us
    all_to_all x1, waiting for transfers between devices, exchange(): lax.all_to_all(block, ('gx', 'gy'), split_axis=0, concat_axis=0, axis_ind...  3.45 us
    pallas_call x1, Pallas kernels, keep_blocks(): pl.pallas_call(functools.partial(keep_kernel, *places), out_shape=[block]...  3.17 us
  transfers between devices with their start and end apart: 21, of which 12 were waited for; matrix products, arithmetic and copies ran while one was open for 3% of the time, Pallas kernels for 17%

profile of v10, /device:TPU:0, one launch (start us, length us, event | category | flops | bytes accessed | tf_op | source)
XLA Modules:
  0.0 95.1 jit_solution(7379733886885176946)
XLA Ops:
  0.6 7.4 %all-to-all-start = ((bf16[16,32,384]{2,1,0:T(8,128)(2,1)}), bf16[16,32,384]{2,1,0:T(8,128)(2,1)S(1)}, u32[]{:S(2)}, u32[]{:S(2)}) async-start(bf16[16,32,384]{2,1,0:T(8,128)(2,1)} %bitcast.98), calls=%async_computation | async-start | bytes 786432 | tf_op jit(solution)/shard_map/all_to_all | solution.py:40
  8.7 1.1 %collective-permute-done = bf16[2,2,2,1,32,384]{5,4,2,1,0,3:T(8,128)(2,1)S(1)} collective-permute-done((bf16[2,2,2,1,32,384]{5,4,2,1,0,3:T(8,128)(2,1)S(1)}, bf16[2,2,2,1,32,384]{5,4,2,1,0,3:T(8,128)(2,1)S(1)}, u32[]{:S(2)}, u32[]{:S(2)}) %collective-permute-start) | collective-permute-done | bytes 196640 | tf_op jit(solution)/shard_map/ppermute | solution.py:281
  9.9 2.8 %collective-permute-start.3 = (bf16[2,2,32,384]{3,2,1,0:T(8,128)(2,1)S(1)}, bf16[2,2,32,384]{3,2,1,0:T(8,128)(2,1)S(1)}, u32[]{:S(2)}, u32[]{:S(2)}) collective-permute-start(bf16[2,2,32,384]{3,2,1,0:T(8,128)(2,1)S(1)} %bitcast.103), channel_id=1, source_target_pairs={{0,6},{1,7},{2,4},{3,5},{4,2},{5,3},{6,0},{7,1},{8,14},{9,15},{10,... | collective-permute-start | bytes 294920 | tf_op jit(solution)/shard_map/ppermute | solution.py:370
  12.7 0.6 collective-permute-start.2
  13.6 2.2 %shard_map.67.up_ref = bf16[768,1536]{1,0:T(8,128)(2,1)S(1)} custom-call(s32[2]{0:T(128)S(1)} %pad_add_fusion.place_ref, bf16[768,1536]{1,0:T(8,128)(2,1)} %source.1), custom_call_target="tpu_custom_call" | custom-call | bytes 4718592 | tf_op jit(solution)/shard_map/pallas_call | solution.py:207
  15.9 0.9 collective-permute-done.3
  16.7 2.0 %collective-permute-done.2 = bf16[2,2,32,384]{3,2,1,0:T(8,128)(2,1)S(1)} collective-permute-done((bf16[2,2,32,384]{3,2,1,0:T(8,128)(2,1)S(1)}, bf16[2,2,32,384]{3,2,1,0:T(8,128)(2,1)S(1)}, u32[]{:S(2)}, u32[]{:S(2)}) %collective-permute-start.2) | collective-permute-done | bytes 98336 | tf_op jit(solution)/shard_map/ppermute | solution.py:281
  18.9 3.5 %all-to-all-done.state_ref = bf16[16,32,384]{2,1,0:T(8,128)(2,1)S(1)} async-done(((bf16[16,32,384]{2,1,0:T(8,128)(2,1)}), bf16[16,32,384]{2,1,0:T(8,128)(2,1)S(1)}, u32[]{:S(2)}, u32[]{:S(2)}) %all-to-all-start) | async-done | bytes 393248 | tf_op jit(solution)/shard_map/all_to_all | solution.py:40
  22.6 8.7 %shard_map.68 = (bf16[16,32,384]{2,1,0:T(8,128)(2,1)S(1)}, bf16[1024,1536]{1,0:T(8,128)(2,1)S(1)}, bf16[1024,1536]{1,0:T(8,128)(2,1)S(1)}, bf16[1024,768]{1,0:T(...) custom-call(bf16[16,32,384]{2,1,0:T(8,128)(2,1)S(1)} %all-to-all-done.state_r, ...), custom_call_target="tpu_custom_call" | custom-call | flops 12079595520 | bytes 25165824 | tf_op jit(solution)/shard_map/pallas_call | solution.py:232
  31.4 2.0 %collective-permute-done.4 = bf16[8,32,384]{2,1,0:T(8,128)(2,1)S(1)} collective-permute-done((bf16[8,32,384]{2,1,0:T(8,128)(2,1)S(1)}, bf16[8,32,384]{2,1,0:T(8,128)(2,1)S(1)}, u32[]{:S(2)}, u32[]{:S(2)}) %collective-permute-start.4) | collective-permute-done | bytes 196640 | tf_op jit(solution)/shard_map/ppermute | solution.py:281
  33.4 9.5 %shard_map.69 = (bf16[1024,1536]{1,0:T(8,128)(2,1)S(1)}, bf16[768,1024]{1,0:T(8,128)(2,1)S(1)}, bf16[16,96,384]{2,1,0:T(8,128)(2,1)S(1)}, bf16[16,96,384]{2,1,0:T(8,128)(2,1)S(1)}) custom-call(s32[2]{0:T(128)S(1)} %pad_add_fusion.place_ref, bf16[16,32,384]{2,1,0:T(8,128)(2,1)S(1)} %pad_maximum_fusion.1.grad_ref, ...), custom_call_target="tpu_custom_call" | custom-call | flops 12079595520 | bytes 25165824 | tf_op jit(solution)/shard_map/pallas_call | solution.py:251
  43.5 0.7 collective-permute-start.5
  44.2 3.2 %shard_map.70 = (bf16[16,96,384]{2,1,0:T(8,128)(2,1)S(1)}, bf16[16,96,384]{2,1,0:T(8,128)(2,1)S(1)}) custom-call(s32[2]{0:T(128)S(1)} %pad_add_fusion.place_ref, bf16[1024,1536]{1,0:T(8,128)(2,1)S(1)} %get-tuple-element.56.hidden_ref, bf16[1024,1536]{1,0:T(8,128)(2,1)S(1)} %get-tuple-element.63.d_pre_ref, ...), custom_call_target="tpu_custom_call" | custom-call | flops 2415919104 | bytes 12582912 | tf_op jit(solution)/shard_map/pallas_call | solution.py:267
  47.4 7.4 %collective-permute-done.5 = bf16[2,2,2,1,32,384]{5,4,2,1,0,3:T(8,128)(2,1)S(1)} collective-permute-done((bf16[2,2,2,1,32,384]{5,4,2,1,0,3:T(8,128)(2,1)S(1)}, bf16[2,2,2,1,32,384]{5,4,2,1,0,3:T(8,128)(2,1)S(1)}, u32[]{:S(2)}, u32[]{:S(2)}) %collective-permute-start.5) | collective-permute-done | bytes 196640 | tf_op jit(solution)/shard_map/ppermute | solution.py:281
  55.2 1.5 %collective-permute-start.15 = (bf16[8,96,384]{2,1,0:T(8,128)(2,1)S(1)}, bf16[8,96,384]{2,1,0:T(8,128)(2,1)S(1)}, u32[]{:S(2)}, u32[]{:S(2)}) collective-permute-start(bf16[8,96,384]{2,1,0:T(8,128)(2,1)S(1)} %get-tuple-element.84), channel_id=1, source_target_pairs={{0,2},{1,3},{2,0},{3,1},{4,6},{5,7},{6,4},{7,5},{8,10},{9,11},{10,... | collective-permute-start | bytes 1769480 | tf_op jit(solution)/shard_map/ppermute | solution.py:281
  57.0 1.1 %collective-permute-start.8 = (bf16[8,96,384]{2,1,0:T(8,128)(2,1)S(1)}, bf16[8,96,384]{2,1,0:T(8,128)(2,1)S(1)}, u32[]{:S(2)}, u32[]{:S(2)}) collective-permute-start(bf16[8,96,384]{2,1,0:T(8,128)(2,1)S(1)} %get-tuple-element.68), channel_id=1, source_target_pairs={{0,4},{4,0},{8,12},{12,8},{16,20},{20,16},{24,28},{28,24},{1,5},{5... | collective-permute-start | bytes 1769480 | tf_op jit(solution)/shard_map/ppermute | solution.py:281
  58.1 12.4 %collective-permute-done.15 = bf16[8,96,384]{2,1,0:T(8,128)(2,1)S(1)} collective-permute-done((bf16[8,96,384]{2,1,0:T(8,128)(2,1)S(1)}, bf16[8,96,384]{2,1,0:T(8,128)(2,1)S(1)}, u32[]{:S(2)}, u32[]{:S(2)}) %collective-permute-start.15) | collective-permute-done | bytes 589856 | tf_op jit(solution)/shard_map/ppermute | solution.py:281
  70.7 1.6 %collective-permute-start.16 = (bf16[4,96,384]{2,1,0:T(8,128)(2,1)S(1)}, bf16[4,96,384]{2,1,0:T(8,128)(2,1)S(1)}, u32[]{:S(2)}, u32[]{:S(2)}) collective-permute-start(bf16[4,96,384]{2,1,0:T(8,128)(2,1)S(1)} %get-tuple-element.88), channel_id=1, source_target_pairs={{0,4},{4,0},{8,12},{12,8},{16,20},{20,16},{24,28},{28,24},{1,5},{5... | collective-permute-start | bytes 884744 | tf_op jit(solution)/shard_map/ppermute | solution.py:281
  72.4 1.0 %collective-permute-start.9 = (bf16[4,96,384]{2,1,0:T(8,128)(2,1)S(1)}, bf16[4,96,384]{2,1,0:T(8,128)(2,1)S(1)}, u32[]{:S(2)}, u32[]{:S(2)}) collective-permute-start(bf16[4,96,384]{2,1,0:T(8,128)(2,1)S(1)} %get-tuple-element.90), channel_id=1, source_target_pairs={{0,2},{1,3},{2,0},{3,1},{4,6},{5,7},{6,4},{7,5},{8,10},{9,11},{10,... | collective-permute-start | bytes 884744 | tf_op jit(solution)/shard_map/ppermute | solution.py:281
  73.5 0.7 fusion.13
  74.2 4.7 %collective-permute-done.16 = bf16[4,96,384]{2,1,0:T(8,128)(2,1)S(1)} collective-permute-done((bf16[4,96,384]{2,1,0:T(8,128)(2,1)S(1)}, bf16[4,96,384]{2,1,0:T(8,128)(2,1)S(1)}, u32[]{:S(2)}, u32[]{:S(2)}) %collective-permute-start.16) | collective-permute-done | bytes 294944 | tf_op jit(solution)/shard_map/ppermute | solution.py:281
  79.0 1.3 %collective-permute-done.9 = bf16[4,96,384]{2,1,0:T(8,128)(2,1)S(1)} collective-permute-done((bf16[4,96,384]{2,1,0:T(8,128)(2,1)S(1)}, bf16[4,96,384]{2,1,0:T(8,128)(2,1)S(1)}, u32[]{:S(2)}, u32[]{:S(2)}) %collective-permute-start.9) | collective-permute-done | bytes 294944 | tf_op jit(solution)/shard_map/ppermute | solution.py:281
  80.4 1.7 %collective-permute-start.13 = (bf16[2,96,384]{2,1,0:T(8,128)(2,1)S(1)}, bf16[2,96,384]{2,1,0:T(8,128)(2,1)S(1)}, u32[]{:S(2)}, u32[]{:S(2)}) collective-permute-start(bf16[2,96,384]{2,1,0:T(8,128)(2,1)S(1)} %get-tuple-element.74), channel_id=1, source_target_pairs={{0,16},{4,20},{8,24},{12,28},{16,0},{20,4},{24,8},{28,12},{1,17},{... | collective-permute-start | bytes 442376 | tf_op jit(solution)/shard_map/ppermute | solution.py:281
  82.4 1.4 %collective-permute-start.11 = (bf16[4,32,384]{2,1,0:T(8,128)(2,1)S(1)}, bf16[4,32,384]{2,1,0:T(8,128)(2,1)S(1)}, u32[]{:S(2)}, u32[]{:S(2)}) collective-permute-start(bf16[4,32,384]{2,1,0:T(8,128)(2,1)S(1)} %get-tuple-element.71), channel_id=1, source_target_pairs={{0,4},{4,0},{8,12},{12,8},{16,20},{20,16},{24,28},{28,24},{1,5},{5... | collective-permute-start | bytes 294920 | tf_op jit(solution)/shard_map/ppermute | solution.py:281
  83.7 1.8 %collective-permute-start.12 = (bf16[4,32,384]{2,1,0:T(8,128)(2,1)S(1)}, bf16[4,32,384]{2,1,0:T(8,128)(2,1)S(1)}, u32[]{:S(2)}, u32[]{:S(2)}) collective-permute-start(bf16[4,32,384]{2,1,0:T(8,128)(2,1)S(1)} %get-tuple-element.72), channel_id=1, source_target_pairs={{0,6},{1,7},{2,4},{3,5},{4,2},{5,3},{6,0},{7,1},{8,14},{9,15},{10,... | collective-permute-start | bytes 294920 | tf_op jit(solution)/shard_map/ppermute | solution.py:370
  85.8 1.2 %collective-permute-start.18 = (bf16[1,96,384]{2,1,0:T(8,128)(2,1)S(1)}, bf16[1,96,384]{2,1,0:T(8,128)(2,1)S(1)}, u32[]{:S(2)}, u32[]{:S(2)}) collective-permute-start(bf16[1,96,384]{2,1,0:T(8,128)(2,1)S(1)} %fusion.9), channel_id=1, source_target_pairs={{0,16},{4,20},{8,24},{12,28},{16,0},{20,4},{24,8},{28,12},{1,17},{... | collective-permute-start | bytes 221192 | tf_op jit(solution)/shard_map/ppermute | solution.py:281
  87.0 3.0 %collective-permute-done.13 = bf16[2,96,384]{2,1,0:T(8,128)(2,1)S(1)} collective-permute-done((bf16[2,96,384]{2,1,0:T(8,128)(2,1)S(1)}, bf16[2,96,384]{2,1,0:T(8,128)(2,1)S(1)}, u32[]{:S(2)}, u32[]{:S(2)}) %collective-permute-start.13) | collective-permute-done | bytes 147488 | tf_op jit(solution)/shard_map/ppermute | solution.py:281
  90.1 0.5 copy-done.2
  90.7 1.9 %shard_map.71 = bf16[512,384]{1,0:T(8,128)(2,1)} custom-call(s32[2]{0:T(128)} %copy-done, bf16[4,32,384]{2,1,0:T(8,128)(2,1)} %get-tuple-element.75.refs_0_, bf16[4,32,384]{2,1,0:T(8,128)(2,1)} %copy-done.2, bf16[4,32,384]{2,1,0:T(8,128)(2,1)} %copy-done.3, bf16[4,32,384]{2,1,0:T(8,128)(2,1)} %copy-done.4), custom_call_target="tpu_custom_call" | custom-call | bytes 786432 | tf_op jit(solution)/shard_map/pallas_call | solution.py:376
  92.6 0.7 add_bitcast_fusion.1
  93.3 1.1 %collective-permute-done.19 = bf16[1,96,384]{2,1,0:T(8,128)(2,1)S(1)} collective-permute-done((bf16[1,96,384]{2,1,0:T(8,128)(2,1)S(1)}, bf16[1,96,384]{2,1,0:T(8,128)(2,1)S(1)}, u32[]{:S(2)}, u32[]{:S(2)}) %collective-permute-start.19) | collective-permute-done | bytes 73760 | tf_op jit(solution)/shard_map/ppermute | solution.py:281
  94.4 0.7 add_bitcast_fusion
  (50 shorter events, 3.9 us)
Async XLA Ops:
  0.6 7.6 %copy-start.1 = (bf16[512,384]{1,0:T(8,128)(2,1)S(1)}, bf16[512,384]{1,0:T(8,128)(2,1)}, u32[]{:S(2)}) copy-start(bf16[512,384]{1,0:T(8,128)(2,1)} %param.7) | copy-start | bytes 1179652
  0.6 21.7 %all-to-all-start = ((bf16[16,32,384]{2,1,0:T(8,128)(2,1)}), bf16[16,32,384]{2,1,0:T(8,128)(2,1)S(1)}, u32[]{:S(2)}, u32[]{:S(2)}) async-start(bf16[16,32,384]{2,1,0:T(8,128)(2,1)} %bitcast.98), calls=%async_computation | async-start | bytes 786432 | tf_op jit(solution)/shard_map/all_to_all | solution.py:40
  8.3 36.0 %copy-start = (s32[2]{0:T(128)}, s32[2]{0:T(128)S(1)}, u32[]{:S(2)}) copy-start(s32[2]{0:T(128)S(1)} %pad_add_fusion.place_ref) | copy-start | bytes 28
  8.3 1.5 %collective-permute-start = (bf16[2,2,2,1,32,384]{5,4,2,1,0,3:T(8,128)(2,1)S(1)}, bf16[2,2,2,1,32,384]{5,4,2,1,0,3:T(8,128)(2,1)S(1)}, u32[]{:S(2)}, u32[]{:S(2)}) collective-permute-start(bf16[2,2,2,1,32,384]{5,4,2,1,0,3:T(8,128)(2,1)S(1)} %get-tuple-element.109), channel_id=1, source_target_pairs={{0,1},{1,0},{2,3},{3,2},{4,5},{5,4},{6,7},{7,6},{8,9},{9,8},{10,11... | collective-permute-start | bytes 589832 | tf_op jit(solution)/shard_map/ppermute | solution.py:281
  9.9 6.8 %collective-permute-start.3 = (bf16[2,2,32,384]{3,2,1,0:T(8,128)(2,1)S(1)}, bf16[2,2,32,384]{3,2,1,0:T(8,128)(2,1)S(1)}, u32[]{:S(2)}, u32[]{:S(2)}) collective-permute-start(bf16[2,2,32,384]{3,2,1,0:T(8,128)(2,1)S(1)} %bitcast.103), channel_id=1, source_target_pairs={{0,6},{1,7},{2,4},{3,5},{4,2},{5,3},{6,0},{7,1},{8,14},{9,15},{10,... | collective-permute-start | bytes 294920 | tf_op jit(solution)/shard_map/ppermute | solution.py:370
  12.7 6.0 %collective-permute-start.2 = (bf16[2,2,32,384]{3,2,1,0:T(8,128)(2,1)S(1)}, bf16[2,2,32,384]{3,2,1,0:T(8,128)(2,1)S(1)}, u32[]{:S(2)}, u32[]{:S(2)}) collective-permute-start(bf16[2,2,32,384]{3,2,1,0:T(8,128)(2,1)S(1)} %bitcast.104), channel_id=1, source_target_pairs={{0,4},{4,0},{8,12},{12,8},{16,20},{20,16},{24,28},{28,24},{1,5},{5... | collective-permute-start | bytes 294920 | tf_op jit(solution)/shard_map/ppermute | solution.py:281
  13.4 5.4 %collective-permute-start.1 = (bf16[2,2,32,384]{3,2,1,0:T(8,128)(2,1)S(1)}, bf16[2,2,32,384]{3,2,1,0:T(8,128)(2,1)S(1)}, u32[]{:S(2)}, u32[]{:S(2)}) collective-permute-start(bf16[2,2,32,384]{3,2,1,0:T(8,128)(2,1)S(1)} %bitcast.105), channel_id=1, source_target_pairs={{0,2},{1,3},{2,0},{3,1},{4,6},{5,7},{6,4},{7,5},{8,10},{9,11},{10,... | collective-permute-start | bytes 294920 | tf_op jit(solution)/shard_map/ppermute | solution.py:281
  22.3 11.0 %collective-permute-start.4 = (bf16[8,32,384]{2,1,0:T(8,128)(2,1)S(1)}, bf16[8,32,384]{2,1,0:T(8,128)(2,1)S(1)}, u32[]{:S(2)}, u32[]{:S(2)}) collective-permute-start(bf16[8,32,384]{2,1,0:T(8,128)(2,1)S(1)} %get-tuple-element.54), channel_id=1, source_target_pairs={{0,16},{4,20},{8,24},{12,28},{16,0},{20,4},{24,8},{28,12},{1,17},{... | collective-permute-start | bytes 589832 | tf_op jit(solution)/shard_map/ppermute | solution.py:281
  42.9 12.0 %collective-permute-start.14 = (bf16[16,96,384]{2,1,0:T(8,128)(2,1)S(1)}, bf16[16,96,384]{2,1,0:T(8,128)(2,1)S(1)}, u32[]{:S(2)}, u32[]{:S(2)}) collective-permute-start(bf16[16,96,384]{2,1,0:T(8,128)(2,1)S(1)} %get-tuple-element.80), channel_id=1, source_target_pairs={{0,1},{1,0},{2,3},{3,2},{4,5},{5,4},{6,7},{7,6},{8,9},{9,8},{10,11... | collective-permute-start | bytes 3538952 | tf_op jit(solution)/shard_map/ppermute | solution.py:281
  43.0 13.7 %collective-permute-start.6 = (bf16[16,96,384]{2,1,0:T(8,128)(2,1)S(1)}, bf16[16,96,384]{2,1,0:T(8,128)(2,1)S(1)}, u32[]{:S(2)}, u32[]{:S(2)}) collective-permute-start(bf16[16,96,384]{2,1,0:T(8,128)(2,1)S(1)} %get-tuple-element.66), channel_id=1, source_target_pairs={{0,1},{1,0},{2,3},{3,2},{4,5},{5,4},{6,7},{7,6},{8,9},{9,8},{10,11... | collective-permute-start | bytes 3538952 | tf_op jit(solution)/shard_map/ppermute | solution.py:281
  43.5 11.3 %collective-permute-start.5 = (bf16[2,2,2,1,32,384]{5,4,2,1,0,3:T(8,128)(2,1)S(1)}, bf16[2,2,2,1,32,384]{5,4,2,1,0,3:T(8,128)(2,1)S(1)}, u32[]{:S(2)}, u32[]{:S(2)}) collective-permute-start(bf16[2,2,2,1,32,384]{5,4,2,1,0,3:T(8,128)(2,1)S(1)} %get-tuple-element.55), channel_id=1, source_target_pairs={{0,16},{4,20},{8,24},{12,28},{16,0},{20,4},{24,8},{28,12},{1,17},{... | collective-permute-start | bytes 589832 | tf_op jit(solution)/shard_map/ppermute | solution.py:281
  55.2 15.3 %collective-permute-start.15 = (bf16[8,96,384]{2,1,0:T(8,128)(2,1)S(1)}, bf16[8,96,384]{2,1,0:T(8,128)(2,1)S(1)}, u32[]{:S(2)}, u32[]{:S(2)}) collective-permute-start(bf16[8,96,384]{2,1,0:T(8,128)(2,1)S(1)} %get-tuple-element.84), channel_id=1, source_target_pairs={{0,2},{1,3},{2,0},{3,1},{4,6},{5,7},{6,4},{7,5},{8,10},{9,11},{10,... | collective-permute-start | bytes 1769480 | tf_op jit(solution)/shard_map/ppermute | solution.py:281
  57.0 15.2 %collective-permute-start.8 = (bf16[8,96,384]{2,1,0:T(8,128)(2,1)S(1)}, bf16[8,96,384]{2,1,0:T(8,128)(2,1)S(1)}, u32[]{:S(2)}, u32[]{:S(2)}) collective-permute-start(bf16[8,96,384]{2,1,0:T(8,128)(2,1)S(1)} %get-tuple-element.68), channel_id=1, source_target_pairs={{0,4},{4,0},{8,12},{12,8},{16,20},{20,16},{24,28},{28,24},{1,5},{5... | collective-permute-start | bytes 1769480 | tf_op jit(solution)/shard_map/ppermute | solution.py:281
  58.1 15.3 %collective-permute-start.7 = (bf16[2,2,2,32,384]{4,3,2,1,0:T(8,128)(2,1)S(1)}, bf16[2,2,2,32,384]{4,3,2,1,0:T(8,128)(2,1)S(1)}, u32[]{:S(2)}, u32[]{:S(2)}) collective-permute-start(bf16[2,2,2,32,384]{4,3,2,1,0:T(8,128)(2,1)S(1)} %bitcast.102), channel_id=1, source_target_pairs={{0,1},{1,0},{2,3},{3,2},{4,5},{5,4},{6,7},{7,6},{8,9},{9,8},{10,11... | collective-permute-start | bytes 589832 | tf_op jit(solution)/shard_map/ppermute | solution.py:281
  70.7 8.2 %collective-permute-start.16 = (bf16[4,96,384]{2,1,0:T(8,128)(2,1)S(1)}, bf16[4,96,384]{2,1,0:T(8,128)(2,1)S(1)}, u32[]{:S(2)}, u32[]{:S(2)}) collective-permute-start(bf16[4,96,384]{2,1,0:T(8,128)(2,1)S(1)} %get-tuple-element.88), channel_id=1, source_target_pairs={{0,4},{4,0},{8,12},{12,8},{16,20},{20,16},{24,28},{28,24},{1,5},{5... | collective-permute-start | bytes 884744 | tf_op jit(solution)/shard_map/ppermute | solution.py:281
  72.4 7.9 %collective-permute-start.9 = (bf16[4,96,384]{2,1,0:T(8,128)(2,1)S(1)}, bf16[4,96,384]{2,1,0:T(8,128)(2,1)S(1)}, u32[]{:S(2)}, u32[]{:S(2)}) collective-permute-start(bf16[4,96,384]{2,1,0:T(8,128)(2,1)S(1)} %get-tuple-element.90), channel_id=1, source_target_pairs={{0,2},{1,3},{2,0},{3,1},{4,6},{5,7},{6,4},{7,5},{8,10},{9,11},{10,... | collective-permute-start | bytes 884744 | tf_op jit(solution)/shard_map/ppermute | solution.py:281
  79.0 6.8 %collective-permute-start.17 = (bf16[2,96,384]{2,1,0:T(8,128)(2,1)S(1)}, bf16[2,96,384]{2,1,0:T(8,128)(2,1)S(1)}, u32[]{:S(2)}, u32[]{:S(2)}) collective-permute-start(bf16[2,96,384]{2,1,0:T(8,128)(2,1)S(1)} %get-tuple-element.92), channel_id=1, source_target_pairs={{0,8},{4,12},{8,0},{12,4},{16,24},{20,28},{24,16},{28,20},{1,9},{5... | collective-permute-start | bytes 442376 | tf_op jit(solution)/shard_map/ppermute | solution.py:281
  80.4 9.5 %collective-permute-start.13 = (bf16[2,96,384]{2,1,0:T(8,128)(2,1)S(1)}, bf16[2,96,384]{2,1,0:T(8,128)(2,1)S(1)}, u32[]{:S(2)}, u32[]{:S(2)}) collective-permute-start(bf16[2,96,384]{2,1,0:T(8,128)(2,1)S(1)} %get-tuple-element.74), channel_id=1, source_target_pairs={{0,16},{4,20},{8,24},{12,28},{16,0},{20,4},{24,8},{28,12},{1,17},{... | collective-permute-start | bytes 442376 | tf_op jit(solution)/shard_map/ppermute | solution.py:281
  82.0 7.9 %collective-permute-start.10 = (bf16[4,32,384]{2,1,0:T(8,128)(2,1)S(1)}, bf16[4,32,384]{2,1,0:T(8,128)(2,1)S(1)}, u32[]{:S(2)}, u32[]{:S(2)}) collective-permute-start(bf16[4,32,384]{2,1,0:T(8,128)(2,1)S(1)} %get-tuple-element.70), channel_id=1, source_target_pairs={{0,2},{1,3},{2,0},{3,1},{4,6},{5,7},{6,4},{7,5},{8,10},{9,11},{10,... | collective-permute-start | bytes 294920 | tf_op jit(solution)/shard_map/ppermute | solution.py:281
  82.4 7.6 %collective-permute-start.11 = (bf16[4,32,384]{2,1,0:T(8,128)(2,1)S(1)}, bf16[4,32,384]{2,1,0:T(8,128)(2,1)S(1)}, u32[]{:S(2)}, u32[]{:S(2)}) collective-permute-start(bf16[4,32,384]{2,1,0:T(8,128)(2,1)S(1)} %get-tuple-element.71), channel_id=1, source_target_pairs={{0,4},{4,0},{8,12},{12,8},{16,20},{20,16},{24,28},{28,24},{1,5},{5... | collective-permute-start | bytes 294920 | tf_op jit(solution)/shard_map/ppermute | solution.py:281
  83.7 6.3 %collective-permute-start.12 = (bf16[4,32,384]{2,1,0:T(8,128)(2,1)S(1)}, bf16[4,32,384]{2,1,0:T(8,128)(2,1)S(1)}, u32[]{:S(2)}, u32[]{:S(2)}) collective-permute-start(bf16[4,32,384]{2,1,0:T(8,128)(2,1)S(1)} %get-tuple-element.72), channel_id=1, source_target_pairs={{0,6},{1,7},{2,4},{3,5},{4,2},{5,3},{6,0},{7,1},{8,14},{9,15},{10,... | collective-permute-start | bytes 294920 | tf_op jit(solution)/shard_map/ppermute | solution.py:370
  85.8 6.8 %collective-permute-start.18 = (bf16[1,96,384]{2,1,0:T(8,128)(2,1)S(1)}, bf16[1,96,384]{2,1,0:T(8,128)(2,1)S(1)}, u32[]{:S(2)}, u32[]{:S(2)}) collective-permute-start(bf16[1,96,384]{2,1,0:T(8,128)(2,1)S(1)} %fusion.9), channel_id=1, source_target_pairs={{0,16},{4,20},{8,24},{12,28},{16,0},{20,4},{24,8},{28,12},{1,17},{... | collective-permute-start | bytes 221192 | tf_op jit(solution)/shard_map/ppermute | solution.py:281
  90.0 0.6 copy-start.2
  90.0 0.6 copy-start.3
  90.0 0.7 copy-start.4
  90.0 4.4 %collective-permute-start.19 = (bf16[1,96,384]{2,1,0:T(8,128)(2,1)S(1)}, bf16[1,96,384]{2,1,0:T(8,128)(2,1)S(1)}, u32[]{:S(2)}, u32[]{:S(2)}) collective-permute-start(bf16[1,96,384]{2,1,0:T(8,128)(2,1)S(1)} %fusion.11), channel_id=1, source_target_pairs={{0,8},{4,12},{8,0},{12,4},{16,24},{20,28},{24,16},{28,20},{1,9},{5... | collective-permute-start | bytes 221192 | tf_op jit(solution)/shard_map/ppermute | solution.py:281

commit v11 on v10

--- a/solution.py
+++ b/solution.py
@@ -431,7 +431,7 @@
     keep_down, keep_up = keep_blocks(place, hidden, d_pre, normed_t, grad_t, places, block)
 
     def beside(phase, give):
-        if phase == 0:
+        if phase == 1:
             return going.hop(core, steps, halves, give)
         if phase == 2:
             return going.hop_both(x, y, steps, halves, give)

time: 95.4 us -> 88.4 us (0.927)
  waiting for transfers between devices: 39.6 us -> 34.9 us
  starting transfers between devices: 24.6 us -> 22.8 us
    ppermute x18, waiting for transfers between devices: 35.3 us -> 30.5 us  [swap(): return lax.ppermute(block, axis, pairs)]
    ppermute x18, starting transfers between devices: 12.6 us -> 11.1 us  [swap(): return lax.ppermute(block, axis, pairs)]
  transfers between devices with their start and end apart: 21 -> 21, of which waited for: 12 -> 13; matrix products, arithmetic and copies ran while one was open for 3% -> 3% of each run, Pallas kernels for 17% -> 18%
where the time goes in v11:
time: 88.4 us; the launch traced here: 88.1 us
  waiting for transfers between devices  34.9 us (39%)
  Pallas kernels  25.5 us (29%)
  starting transfers between devices  22.8 us (26%)
  other arithmetic  3.52 us (4%)
  between operations  1 us (1%)
    ppermute x18, waiting for transfers between devices, swap(): return lax.ppermute(block, axis, pairs)  30.5 us
    ppermute x18, starting transfers between devices, swap(): return lax.ppermute(block, axis, pairs)  11.1 us
    pallas_call x1, Pallas kernels, backward(): pl.pallas_call(functools.partial(backward_kernel, *places), out_shape=out...  9.44 us
    pallas_call x1, Pallas kernels, forward(): pl.pallas_call(forward_kernel, out_shape=outs, in_specs=[spec(pltpu.VMEM)...  8.72 us
    all_to_all x1, starting transfers between devices, exchange(): lax.all_to_all(block, ('gx', 'gy'), split_axis=0, concat_axis=0, axis_ind...  7.44 us
    ppermute x2, starting transfers between devices, swap_both(): return lax.ppermute(block, ('gx', 'gy'), pairs)  4.21 us
    all_to_all x1, waiting for transfers between devices, exchange(): lax.all_to_all(block, ('gx', 'gy'), split_axis=0, concat_axis=0, axis_ind...  3.45 us
    pallas_call x1, Pallas kernels, keep_blocks(): pl.pallas_call(functools.partial(keep_kernel, *places), out_shape=[block]...  3.17 us
  transfers between devices with their start and end apart: 21, of which 13 were waited for; matrix products, arithmetic and copies ran while one was open for 3% of the time, Pallas kernels for 18%

profile of v11, /device:TPU:0, one launch (start us, length us, event | category | flops | bytes accessed | tf_op | source)
XLA Modules:
  0.0 88.1 jit_solution(10642469397785230345)
XLA Ops:
  0.6 7.4 %all-to-all-start = ((bf16[16,32,384]{2,1,0:T(8,128)(2,1)}), bf16[16,32,384]{2,1,0:T(8,128)(2,1)S(1)}, u32[]{:S(2)}, u32[]{:S(2)}) async-start(bf16[16,32,384]{2,1,0:T(8,128)(2,1)} %bitcast.98), calls=%async_computation | async-start | bytes 786432 | tf_op jit(solution)/shard_map/all_to_all | solution.py:40
  8.7 1.1 %collective-permute-done = bf16[2,2,2,1,32,384]{5,4,2,1,0,3:T(8,128)(2,1)S(1)} collective-permute-done((bf16[2,2,2,1,32,384]{5,4,2,1,0,3:T(8,128)(2,1)S(1)}, bf16[2,2,2,1,32,384]{5,4,2,1,0,3:T(8,128)(2,1)S(1)}, u32[]{:S(2)}, u32[]{:S(2)}) %collective-permute-start) | collective-permute-done | bytes 196640 | tf_op jit(solution)/shard_map/ppermute | solution.py:281
  9.9 2.8 %collective-permute-start.3 = (bf16[2,2,32,384]{3,2,1,0:T(8,128)(2,1)S(1)}, bf16[2,2,32,384]{3,2,1,0:T(8,128)(2,1)S(1)}, u32[]{:S(2)}, u32[]{:S(2)}) collective-permute-start(bf16[2,2,32,384]{3,2,1,0:T(8,128)(2,1)S(1)} %bitcast.103), channel_id=1, source_target_pairs={{0,6},{1,7},{2,4},{3,5},{4,2},{5,3},{6,0},{7,1},{8,14},{9,15},{10,... | collective-permute-start | bytes 294920 | tf_op jit(solution)/shard_map/ppermute | solution.py:370
  12.7 0.6 collective-permute-start.2
  13.6 2.2 %shard_map.67.up_ref = bf16[768,1536]{1,0:T(8,128)(2,1)S(1)} custom-call(s32[2]{0:T(128)S(1)} %pad_add_fusion.place_ref, bf16[768,1536]{1,0:T(8,128)(2,1)} %source.1), custom_call_target="tpu_custom_call" | custom-call | bytes 4718592 | tf_op jit(solution)/shard_map/pallas_call | solution.py:207
  15.9 0.9 collective-permute-done.3
  16.7 2.0 %collective-permute-done.2 = bf16[2,2,32,384]{3,2,1,0:T(8,128)(2,1)S(1)} collective-permute-done((bf16[2,2,32,384]{3,2,1,0:T(8,128)(2,1)S(1)}, bf16[2,2,32,384]{3,2,1,0:T(8,128)(2,1)S(1)}, u32[]{:S(2)}, u32[]{:S(2)}) %collective-permute-start.2) | collective-permute-done | bytes 98336 | tf_op jit(solution)/shard_map/ppermute | solution.py:281
  18.9 3.5 %all-to-all-done.state_ref = bf16[16,32,384]{2,1,0:T(8,128)(2,1)S(1)} async-done(((bf16[16,32,384]{2,1,0:T(8,128)(2,1)}), bf16[16,32,384]{2,1,0:T(8,128)(2,1)S(1)}, u32[]{:S(2)}, u32[]{:S(2)}) %all-to-all-start) | async-done | bytes 393248 | tf_op jit(solution)/shard_map/all_to_all | solution.py:40
  22.6 8.7 %shard_map.68 = (bf16[16,32,384]{2,1,0:T(8,128)(2,1)S(1)}, bf16[1024,1536]{1,0:T(8,128)(2,1)S(1)}, bf16[1024,1536]{1,0:T(8,128)(2,1)S(1)}, bf16[1024,768]{1,0:T(...) custom-call(bf16[16,32,384]{2,1,0:T(8,128)(2,1)S(1)} %all-to-all-done.state_r, ...), custom_call_target="tpu_custom_call" | custom-call | flops 12079595520 | bytes 25165824 | tf_op jit(solution)/shard_map/pallas_call | solution.py:232
  31.4 2.0 %collective-permute-done.4 = bf16[8,32,384]{2,1,0:T(8,128)(2,1)S(1)} collective-permute-done((bf16[8,32,384]{2,1,0:T(8,128)(2,1)S(1)}, bf16[8,32,384]{2,1,0:T(8,128)(2,1)S(1)}, u32[]{:S(2)}, u32[]{:S(2)}) %collective-permute-start.4) | collective-permute-done | bytes 196640 | tf_op jit(solution)/shard_map/ppermute | solution.py:281
  33.4 9.4 %shard_map.69 = (bf16[1024,1536]{1,0:T(8,128)(2,1)S(1)}, bf16[768,1024]{1,0:T(8,128)(2,1)S(1)}, bf16[16,96,384]{2,1,0:T(8,128)(2,1)S(1)}, bf16[16,96,384]{2,1,0:T(8,128)(2,1)S(1)}) custom-call(s32[2]{0:T(128)S(1)} %pad_add_fusion.place_ref, bf16[16,32,384]{2,1,0:T(8,128)(2,1)S(1)} %pad_maximum_fusion.1.grad_ref, ...), custom_call_target="tpu_custom_call" | custom-call | flops 12079595520 | bytes 25165824 | tf_op jit(solution)/shard_map/pallas_call | solution.py:251
  43.4 3.2 %shard_map.70 = (bf16[16,96,384]{2,1,0:T(8,128)(2,1)S(1)}, bf16[16,96,384]{2,1,0:T(8,128)(2,1)S(1)}) custom-call(s32[2]{0:T(128)S(1)} %pad_add_fusion.place_ref, bf16[1024,1536]{1,0:T(8,128)(2,1)S(1)} %get-tuple-element.56.hidden_ref, bf16[1024,1536]{1,0:T(8,128)(2,1)S(1)} %get-tuple-element.63.d_pre_ref, ...), custom_call_target="tpu_custom_call" | custom-call | flops 2415919104 | bytes 12582912 | tf_op jit(solution)/shard_map/pallas_call | solution.py:267
  46.9 1.1 %collective-permute-start.7 = (bf16[8,96,384]{2,1,0:T(8,128)(2,1)S(1)}, bf16[8,96,384]{2,1,0:T(8,128)(2,1)S(1)}, u32[]{:S(2)}, u32[]{:S(2)}) collective-permute-start(bf16[8,96,384]{2,1,0:T(8,128)(2,1)S(1)} %get-tuple-element.86), channel_id=1, source_target_pairs={{0,4},{4,0},{8,12},{12,8},{16,20},{20,16},{24,28},{28,24},{1,5},{5... | collective-permute-start | bytes 1769480 | tf_op jit(solution)/shard_map/ppermute | solution.py:281
  48.4 1.2 %collective-permute-start.15 = (bf16[8,96,384]{2,1,0:T(8,128)(2,1)S(1)}, bf16[8,96,384]{2,1,0:T(8,128)(2,1)S(1)}, u32[]{:S(2)}, u32[]{:S(2)}) collective-permute-start(bf16[8,96,384]{2,1,0:T(8,128)(2,1)S(1)} %get-tuple-element.84), channel_id=1, source_target_pairs={{0,2},{1,3},{2,0},{3,1},{4,6},{5,7},{6,4},{7,5},{8,10},{9,11},{10,... | collective-permute-start | bytes 1769480 | tf_op jit(solution)/shard_map/ppermute | solution.py:281
  49.5 11.0 %collective-permute-done.5 = bf16[2,2,2,1,32,384]{5,4,2,1,0,3:T(8,128)(2,1)S(1)} collective-permute-done((bf16[2,2,2,1,32,384]{5,4,2,1,0,3:T(8,128)(2,1)S(1)}, bf16[2,2,2,1,32,384]{5,4,2,1,0,3:T(8,128)(2,1)S(1)}, u32[]{:S(2)}, u32[]{:S(2)}) %collective-permute-start.5) | collective-permute-done | bytes 196640 | tf_op jit(solution)/shard_map/ppermute | solution.py:281
  60.6 1.7 %collective-permute-done.7 = bf16[8,96,384]{2,1,0:T(8,128)(2,1)S(1)} collective-permute-done((bf16[8,96,384]{2,1,0:T(8,128)(2,1)S(1)}, bf16[8,96,384]{2,1,0:T(8,128)(2,1)S(1)}, u32[]{:S(2)}, u32[]{:S(2)}) %collective-permute-start.7) | collective-permute-done | bytes 589856 | tf_op jit(solution)/shard_map/ppermute | solution.py:281
  62.6 0.9 %collective-permute-done.15 = bf16[8,96,384]{2,1,0:T(8,128)(2,1)S(1)} collective-permute-done((bf16[8,96,384]{2,1,0:T(8,128)(2,1)S(1)}, bf16[8,96,384]{2,1,0:T(8,128)(2,1)S(1)}, u32[]{:S(2)}, u32[]{:S(2)}) %collective-permute-start.15) | collective-permute-done | bytes 589856 | tf_op jit(solution)/shard_map/ppermute | solution.py:281
  63.6 1.1 %collective-permute-start.16 = (bf16[4,96,384]{2,1,0:T(8,128)(2,1)S(1)}, bf16[4,96,384]{2,1,0:T(8,128)(2,1)S(1)}, u32[]{:S(2)}, u32[]{:S(2)}) collective-permute-start(bf16[4,96,384]{2,1,0:T(8,128)(2,1)S(1)} %get-tuple-element.88), channel_id=1, source_target_pairs={{0,4},{4,0},{8,12},{12,8},{16,20},{20,16},{24,28},{28,24},{1,5},{5... | collective-permute-start | bytes 884744 | tf_op jit(solution)/shard_map/ppermute | solution.py:281
  64.7 0.9 collective-permute-start.9
  65.6 0.7 fusion.13
  66.3 5.9 %collective-permute-done.16 = bf16[4,96,384]{2,1,0:T(8,128)(2,1)S(1)} collective-permute-done((bf16[4,96,384]{2,1,0:T(8,128)(2,1)S(1)}, bf16[4,96,384]{2,1,0:T(8,128)(2,1)S(1)}, u32[]{:S(2)}, u32[]{:S(2)}) %collective-permute-start.16) | collective-permute-done | bytes 294944 | tf_op jit(solution)/shard_map/ppermute | solution.py:281
  72.3 0.6 collective-permute-done.9
  73.0 1.8 %collective-permute-start.13 = (bf16[2,96,384]{2,1,0:T(8,128)(2,1)S(1)}, bf16[2,96,384]{2,1,0:T(8,128)(2,1)S(1)}, u32[]{:S(2)}, u32[]{:S(2)}) collective-permute-start(bf16[2,96,384]{2,1,0:T(8,128)(2,1)S(1)} %get-tuple-element.74), channel_id=1, source_target_pairs={{0,16},{4,20},{8,24},{12,28},{16,0},{20,4},{24,8},{28,12},{1,17},{... | collective-permute-start | bytes 442376 | tf_op jit(solution)/shard_map/ppermute | solution.py:281
  74.8 1.5 %collective-permute-start.10 = (bf16[4,32,384]{2,1,0:T(8,128)(2,1)S(1)}, bf16[4,32,384]{2,1,0:T(8,128)(2,1)S(1)}, u32[]{:S(2)}, u32[]{:S(2)}) collective-permute-start(bf16[4,32,384]{2,1,0:T(8,128)(2,1)S(1)} %get-tuple-element.70), channel_id=1, source_target_pairs={{0,2},{1,3},{2,0},{3,1},{4,6},{5,7},{6,4},{7,5},{8,10},{9,11},{10,... | collective-permute-start | bytes 294920 | tf_op jit(solution)/shard_map/ppermute | solution.py:281
  76.3 0.6 collective-permute-start.11
  76.8 1.4 %collective-permute-start.12 = (bf16[4,32,384]{2,1,0:T(8,128)(2,1)S(1)}, bf16[4,32,384]{2,1,0:T(8,128)(2,1)S(1)}, u32[]{:S(2)}, u32[]{:S(2)}) collective-permute-start(bf16[4,32,384]{2,1,0:T(8,128)(2,1)S(1)} %get-tuple-element.72), channel_id=1, source_target_pairs={{0,6},{1,7},{2,4},{3,5},{4,2},{5,3},{6,0},{7,1},{8,14},{9,15},{10,... | collective-permute-start | bytes 294920 | tf_op jit(solution)/shard_map/ppermute | solution.py:370
  78.3 0.9 %collective-permute-done.17 = bf16[2,96,384]{2,1,0:T(8,128)(2,1)S(1)} collective-permute-done((bf16[2,96,384]{2,1,0:T(8,128)(2,1)S(1)}, bf16[2,96,384]{2,1,0:T(8,128)(2,1)S(1)}, u32[]{:S(2)}, u32[]{:S(2)}) %collective-permute-start.17) | collective-permute-done | bytes 147488 | tf_op jit(solution)/shard_map/ppermute | solution.py:281
  79.7 3.2 %collective-permute-done.13 = bf16[2,96,384]{2,1,0:T(8,128)(2,1)S(1)} collective-permute-done((bf16[2,96,384]{2,1,0:T(8,128)(2,1)S(1)}, bf16[2,96,384]{2,1,0:T(8,128)(2,1)S(1)}, u32[]{:S(2)}, u32[]{:S(2)}) %collective-permute-start.13) | collective-permute-done | bytes 147488 | tf_op jit(solution)/shard_map/ppermute | solution.py:281
  83.6 1.9 %shard_map.71 = bf16[512,384]{1,0:T(8,128)(2,1)} custom-call(s32[2]{0:T(128)} %copy-done, bf16[4,32,384]{2,1,0:T(8,128)(2,1)} %get-tuple-element.75.refs_0_, bf16[4,32,384]{2,1,0:T(8,128)(2,1)} %copy-done.2, bf16[4,32,384]{2,1,0:T(8,128)(2,1)} %copy-done.3, bf16[4,32,384]{2,1,0:T(8,128)(2,1)} %copy-done.4), custom_call_target="tpu_custom_call" | custom-call | bytes 786432 | tf_op jit(solution)/shard_map/pallas_call | solution.py:376
  85.5 0.7 add_bitcast_fusion.1
  86.2 1.1 %collective-permute-done.19 = bf16[1,96,384]{2,1,0:T(8,128)(2,1)S(1)} collective-permute-done((bf16[1,96,384]{2,1,0:T(8,128)(2,1)S(1)}, bf16[1,96,384]{2,1,0:T(8,128)(2,1)S(1)}, u32[]{:S(2)}, u32[]{:S(2)}) %collective-permute-start.19) | collective-permute-done | bytes 73760 | tf_op jit(solution)/shard_map/ppermute | solution.py:281
  87.4 0.7 add_bitcast_fusion
  (50 shorter events, 4.4 us)
Async XLA Ops:
  0.6 7.6 %copy-start.1 = (bf16[512,384]{1,0:T(8,128)(2,1)S(1)}, bf16[512,384]{1,0:T(8,128)(2,1)}, u32[]{:S(2)}) copy-start(bf16[512,384]{1,0:T(8,128)(2,1)} %param.7) | copy-start | bytes 1179652
  0.6 21.7 %all-to-all-start = ((bf16[16,32,384]{2,1,0:T(8,128)(2,1)}), bf16[16,32,384]{2,1,0:T(8,128)(2,1)S(1)}, u32[]{:S(2)}, u32[]{:S(2)}) async-start(bf16[16,32,384]{2,1,0:T(8,128)(2,1)} %bitcast.98), calls=%async_computation | async-start | bytes 786432 | tf_op jit(solution)/shard_map/all_to_all | solution.py:40
  8.3 35.2 %copy-start = (s32[2]{0:T(128)}, s32[2]{0:T(128)S(1)}, u32[]{:S(2)}) copy-start(s32[2]{0:T(128)S(1)} %pad_add_fusion.place_ref) | copy-start | bytes 28
  8.3 1.5 %collective-permute-start = (bf16[2,2,2,1,32,384]{5,4,2,1,0,3:T(8,128)(2,1)S(1)}, bf16[2,2,2,1,32,384]{5,4,2,1,0,3:T(8,128)(2,1)S(1)}, u32[]{:S(2)}, u32[]{:S(2)}) collective-permute-start(bf16[2,2,2,1,32,384]{5,4,2,1,0,3:T(8,128)(2,1)S(1)} %get-tuple-element.109), channel_id=1, source_target_pairs={{0,1},{1,0},{2,3},{3,2},{4,5},{5,4},{6,7},{7,6},{8,9},{9,8},{10,11... | collective-permute-start | bytes 589832 | tf_op jit(solution)/shard_map/ppermute | solution.py:281
  9.9 6.8 %collective-permute-start.3 = (bf16[2,2,32,384]{3,2,1,0:T(8,128)(2,1)S(1)}, bf16[2,2,32,384]{3,2,1,0:T(8,128)(2,1)S(1)}, u32[]{:S(2)}, u32[]{:S(2)}) collective-permute-start(bf16[2,2,32,384]{3,2,1,0:T(8,128)(2,1)S(1)} %bitcast.103), channel_id=1, source_target_pairs={{0,6},{1,7},{2,4},{3,5},{4,2},{5,3},{6,0},{7,1},{8,14},{9,15},{10,... | collective-permute-start | bytes 294920 | tf_op jit(solution)/shard_map/ppermute | solution.py:370
  12.7 6.0 %collective-permute-start.2 = (bf16[2,2,32,384]{3,2,1,0:T(8,128)(2,1)S(1)}, bf16[2,2,32,384]{3,2,1,0:T(8,128)(2,1)S(1)}, u32[]{:S(2)}, u32[]{:S(2)}) collective-permute-start(bf16[2,2,32,384]{3,2,1,0:T(8,128)(2,1)S(1)} %bitcast.104), channel_id=1, source_target_pairs={{0,4},{4,0},{8,12},{12,8},{16,20},{20,16},{24,28},{28,24},{1,5},{5... | collective-permute-start | bytes 294920 | tf_op jit(solution)/shard_map/ppermute | solution.py:281
  13.4 5.4 %collective-permute-start.1 = (bf16[2,2,32,384]{3,2,1,0:T(8,128)(2,1)S(1)}, bf16[2,2,32,384]{3,2,1,0:T(8,128)(2,1)S(1)}, u32[]{:S(2)}, u32[]{:S(2)}) collective-permute-start(bf16[2,2,32,384]{3,2,1,0:T(8,128)(2,1)S(1)} %bitcast.105), channel_id=1, source_target_pairs={{0,2},{1,3},{2,0},{3,1},{4,6},{5,7},{6,4},{7,5},{8,10},{9,11},{10,... | collective-permute-start | bytes 294920 | tf_op jit(solution)/shard_map/ppermute | solution.py:281
  22.3 11.0 %collective-permute-start.4 = (bf16[8,32,384]{2,1,0:T(8,128)(2,1)S(1)}, bf16[8,32,384]{2,1,0:T(8,128)(2,1)S(1)}, u32[]{:S(2)}, u32[]{:S(2)}) collective-permute-start(bf16[8,32,384]{2,1,0:T(8,128)(2,1)S(1)} %get-tuple-element.54), channel_id=1, source_target_pairs={{0,16},{4,20},{8,24},{12,28},{16,0},{20,4},{24,8},{28,12},{1,17},{... | collective-permute-start | bytes 589832 | tf_op jit(solution)/shard_map/ppermute | solution.py:281
  42.8 3.8 %collective-permute-start.6 = (bf16[16,96,384]{2,1,0:T(8,128)(2,1)S(1)}, bf16[16,96,384]{2,1,0:T(8,128)(2,1)S(1)}, u32[]{:S(2)}, u32[]{:S(2)}) collective-permute-start(bf16[16,96,384]{2,1,0:T(8,128)(2,1)S(1)} %get-tuple-element.66), channel_id=1, source_target_pairs={{0,1},{1,0},{2,3},{3,2},{4,5},{5,4},{6,7},{7,6},{8,9},{9,8},{10,11... | collective-permute-start | bytes 3538952 | tf_op jit(solution)/shard_map/ppermute | solution.py:281
  42.9 5.1 %collective-permute-start.14 = (bf16[16,96,384]{2,1,0:T(8,128)(2,1)S(1)}, bf16[16,96,384]{2,1,0:T(8,128)(2,1)S(1)}, u32[]{:S(2)}, u32[]{:S(2)}) collective-permute-start(bf16[16,96,384]{2,1,0:T(8,128)(2,1)S(1)} %get-tuple-element.80), channel_id=1, source_target_pairs={{0,1},{1,0},{2,3},{3,2},{4,5},{5,4},{6,7},{7,6},{8,9},{9,8},{10,11... | collective-permute-start | bytes 3538952 | tf_op jit(solution)/shard_map/ppermute | solution.py:281
  46.9 15.4 %collective-permute-start.7 = (bf16[8,96,384]{2,1,0:T(8,128)(2,1)S(1)}, bf16[8,96,384]{2,1,0:T(8,128)(2,1)S(1)}, u32[]{:S(2)}, u32[]{:S(2)}) collective-permute-start(bf16[8,96,384]{2,1,0:T(8,128)(2,1)S(1)} %get-tuple-element.86), channel_id=1, source_target_pairs={{0,4},{4,0},{8,12},{12,8},{16,20},{20,16},{24,28},{28,24},{1,5},{5... | collective-permute-start | bytes 1769480 | tf_op jit(solution)/shard_map/ppermute | solution.py:281
  48.4 15.1 %collective-permute-start.15 = (bf16[8,96,384]{2,1,0:T(8,128)(2,1)S(1)}, bf16[8,96,384]{2,1,0:T(8,128)(2,1)S(1)}, u32[]{:S(2)}, u32[]{:S(2)}) collective-permute-start(bf16[8,96,384]{2,1,0:T(8,128)(2,1)S(1)} %get-tuple-element.84), channel_id=1, source_target_pairs={{0,2},{1,3},{2,0},{3,1},{4,6},{5,7},{6,4},{7,5},{8,10},{9,11},{10,... | collective-permute-start | bytes 1769480 | tf_op jit(solution)/shard_map/ppermute | solution.py:281
  49.5 11.0 %collective-permute-start.5 = (bf16[2,2,2,1,32,384]{5,4,2,1,0,3:T(8,128)(2,1)S(1)}, bf16[2,2,2,1,32,384]{5,4,2,1,0,3:T(8,128)(2,1)S(1)}, u32[]{:S(2)}, u32[]{:S(2)}) collective-permute-start(bf16[2,2,2,1,32,384]{5,4,2,1,0,3:T(8,128)(2,1)S(1)} %get-tuple-element.55), channel_id=1, source_target_pairs={{0,16},{4,20},{8,24},{12,28},{16,0},{20,4},{24,8},{28,12},{1,17},{... | collective-permute-start | bytes 589832 | tf_op jit(solution)/shard_map/ppermute | solution.py:281
  62.5 3.1 %collective-permute-start.8 = (bf16[2,2,2,32,384]{4,3,2,1,0:T(8,128)(2,1)S(1)}, bf16[2,2,2,32,384]{4,3,2,1,0:T(8,128)(2,1)S(1)}, u32[]{:S(2)}, u32[]{:S(2)}) collective-permute-start(bf16[2,2,2,32,384]{4,3,2,1,0:T(8,128)(2,1)S(1)} %bitcast.102), channel_id=1, source_target_pairs={{0,1},{1,0},{2,3},{3,2},{4,5},{5,4},{6,7},{7,6},{8,9},{9,8},{10,11... | collective-permute-start | bytes 589832 | tf_op jit(solution)/shard_map/ppermute | solution.py:281
  63.6 8.6 %collective-permute-start.16 = (bf16[4,96,384]{2,1,0:T(8,128)(2,1)S(1)}, bf16[4,96,384]{2,1,0:T(8,128)(2,1)S(1)}, u32[]{:S(2)}, u32[]{:S(2)}) collective-permute-start(bf16[4,96,384]{2,1,0:T(8,128)(2,1)S(1)} %get-tuple-element.88), channel_id=1, source_target_pairs={{0,4},{4,0},{8,12},{12,8},{16,20},{20,16},{24,28},{28,24},{1,5},{5... | collective-permute-start | bytes 884744 | tf_op jit(solution)/shard_map/ppermute | solution.py:281
  64.7 8.3 %collective-permute-start.9 = (bf16[4,96,384]{2,1,0:T(8,128)(2,1)S(1)}, bf16[4,96,384]{2,1,0:T(8,128)(2,1)S(1)}, u32[]{:S(2)}, u32[]{:S(2)}) collective-permute-start(bf16[4,96,384]{2,1,0:T(8,128)(2,1)S(1)} %get-tuple-element.68), channel_id=1, source_target_pairs={{0,2},{1,3},{2,0},{3,1},{4,6},{5,7},{6,4},{7,5},{8,10},{9,11},{10,... | collective-permute-start | bytes 884744 | tf_op jit(solution)/shard_map/ppermute | solution.py:281
  72.3 6.9 %collective-permute-start.17 = (bf16[2,96,384]{2,1,0:T(8,128)(2,1)S(1)}, bf16[2,96,384]{2,1,0:T(8,128)(2,1)S(1)}, u32[]{:S(2)}, u32[]{:S(2)}) collective-permute-start(bf16[2,96,384]{2,1,0:T(8,128)(2,1)S(1)} %get-tuple-element.92), channel_id=1, source_target_pairs={{0,8},{4,12},{8,0},{12,4},{16,24},{20,28},{24,16},{28,20},{1,9},{5... | collective-permute-start | bytes 442376 | tf_op jit(solution)/shard_map/ppermute | solution.py:281
  73.0 9.8 %collective-permute-start.13 = (bf16[2,96,384]{2,1,0:T(8,128)(2,1)S(1)}, bf16[2,96,384]{2,1,0:T(8,128)(2,1)S(1)}, u32[]{:S(2)}, u32[]{:S(2)}) collective-permute-start(bf16[2,96,384]{2,1,0:T(8,128)(2,1)S(1)} %get-tuple-element.74), channel_id=1, source_target_pairs={{0,16},{4,20},{8,24},{12,28},{16,0},{20,4},{24,8},{28,12},{1,17},{... | collective-permute-start | bytes 442376 | tf_op jit(solution)/shard_map/ppermute | solution.py:281
  74.8 8.1 %collective-permute-start.10 = (bf16[4,32,384]{2,1,0:T(8,128)(2,1)S(1)}, bf16[4,32,384]{2,1,0:T(8,128)(2,1)S(1)}, u32[]{:S(2)}, u32[]{:S(2)}) collective-permute-start(bf16[4,32,384]{2,1,0:T(8,128)(2,1)S(1)} %get-tuple-element.70), channel_id=1, source_target_pairs={{0,2},{1,3},{2,0},{3,1},{4,6},{5,7},{6,4},{7,5},{8,10},{9,11},{10,... | collective-permute-start | bytes 294920 | tf_op jit(solution)/shard_map/ppermute | solution.py:281
  76.3 6.6 %collective-permute-start.11 = (bf16[4,32,384]{2,1,0:T(8,128)(2,1)S(1)}, bf16[4,32,384]{2,1,0:T(8,128)(2,1)S(1)}, u32[]{:S(2)}, u32[]{:S(2)}) collective-permute-start(bf16[4,32,384]{2,1,0:T(8,128)(2,1)S(1)} %get-tuple-element.71), channel_id=1, source_target_pairs={{0,4},{4,0},{8,12},{12,8},{16,20},{20,16},{24,28},{28,24},{1,5},{5... | collective-permute-start | bytes 294920 | tf_op jit(solution)/shard_map/ppermute | solution.py:281
  76.8 6.1 %collective-permute-start.12 = (bf16[4,32,384]{2,1,0:T(8,128)(2,1)S(1)}, bf16[4,32,384]{2,1,0:T(8,128)(2,1)S(1)}, u32[]{:S(2)}, u32[]{:S(2)}) collective-permute-start(bf16[4,32,384]{2,1,0:T(8,128)(2,1)S(1)} %get-tuple-element.72), channel_id=1, source_target_pairs={{0,6},{1,7},{2,4},{3,5},{4,2},{5,3},{6,0},{7,1},{8,14},{9,15},{10,... | collective-permute-start | bytes 294920 | tf_op jit(solution)/shard_map/ppermute | solution.py:370
  79.2 6.3 %collective-permute-start.18 = (bf16[1,96,384]{2,1,0:T(8,128)(2,1)S(1)}, bf16[1,96,384]{2,1,0:T(8,128)(2,1)S(1)}, u32[]{:S(2)}, u32[]{:S(2)}) collective-permute-start(bf16[1,96,384]{2,1,0:T(8,128)(2,1)S(1)} %fusion.9), channel_id=1, source_target_pairs={{0,16},{4,20},{8,24},{12,28},{16,0},{20,4},{24,8},{28,12},{1,17},{... | collective-permute-start | bytes 221192 | tf_op jit(solution)/shard_map/ppermute | solution.py:281
  82.9 0.6 copy-start.2
  82.9 0.6 copy-start.3
  82.9 0.7 copy-start.4
  82.9 4.4 %collective-permute-start.19 = (bf16[1,96,384]{2,1,0:T(8,128)(2,1)S(1)}, bf16[1,96,384]{2,1,0:T(8,128)(2,1)S(1)}, u32[]{:S(2)}, u32[]{:S(2)}) collective-permute-start(bf16[1,96,384]{2,1,0:T(8,128)(2,1)S(1)} %fusion.11), channel_id=1, source_target_pairs={{0,8},{4,12},{8,0},{12,4},{16,24},{20,28},{24,16},{28,20},{1,9},{5... | collective-permute-start | bytes 221192 | tf_op jit(solution)/shard_map/ppermute | solution.py:281

commit v12 on v11

--- a/solution.py
+++ b/solution.py
@@ -393,8 +393,8 @@
     z, y, x, core = range(4)
     rest_y = [("gy", bit) for bit in range(1, span_y.bit_length() - 1)]
     rest_x = [("gx", bit) for bit in range(1, span_x.bit_length() - 1)]
-    order_down = [steps[y]] + rest_y + rest_x[::-1]
-    order_up = rest_y + [steps[y]] + rest_x
+    order_down = [steps[y]] + rest_y + rest_x
+    order_up = rest_y + [steps[y]] + rest_x[::-1]
 
     owns = [lax.axis_index(axis) // (1 << bit) % 2 for axis, bit in [steps[core]] + order_up]
     own = dict(zip([steps[core]] + order_up, owns))
@@ -428,11 +428,10 @@
         grad_up = scatter_narrow(halves, normed_t, d_pre, [steps[core]] + order_up, span_x, span_y)
         return (mixed_out, grad_up, grad_down)
     take_down, take_up = [swap(part, *steps[core]) for part in given]
-    keep_down, keep_up = keep_blocks(place, hidden, d_pre, normed_t, grad_t, places, block)
+    after = going.hop(core, steps, halves, place)
+    keep_down, keep_up = keep_blocks(after, hidden, d_pre, normed_t, grad_t, places, block)
 
     def beside(phase, give):
-        if phase == 1:
-            return going.hop(core, steps, halves, give)
         if phase == 2:
             return going.hop_both(x, y, steps, halves, give)
         if phase == len(order_down) - 1:

time: 88.4 us -> 99.5 us (1.13)
  waiting for transfers between devices: 34.9 us -> 44.6 us
  starting transfers between devices: 22.8 us -> 24.3 us
    ppermute x18, waiting for transfers between devices: 30.5 us -> 38.4 us  [swap(): return lax.ppermute(block, axis, pairs)]
    ppermute x2, waiting for transfers between devices: 0.88 us -> 2.7 us  [swap_both(): return lax.ppermute(block, ('gx', 'gy'), pairs)]
    ppermute x18, starting transfers between devices: 11.1 us -> 12.2 us  [swap(): return lax.ppermute(block, axis, pairs)]
  transfers between devices with their start and end apart: 21 -> 21, of which waited for: 13 -> 13; matrix products, arithmetic and copies ran while one was open for 3% -> 3% of each run, Pallas kernels for 18% -> 16%
where the time goes in v12:
time: 99.5 us; the launch traced here: 99.1 us
  waiting for transfers between devices  44.6 us (45%)
  Pallas kernels  25.5 us (26%)
  starting transfers between devices  24.3 us (24%)
  other arithmetic  3.53 us (4%)
    ppermute x18, waiting for transfers between devices, swap(): return lax.ppermute(block, axis, pairs)  38.4 us
    ppermute x18, starting transfers between devices, swap(): return lax.ppermute(block, axis, pairs)  12.2 us
    pallas_call x1, Pallas kernels, backward(): pl.pallas_call(functools.partial(backward_kernel, *places), out_shape=out...  9.46 us
    pallas_call x1, Pallas kernels, forward(): pl.pallas_call(forward_kernel, out_shape=outs, in_specs=[spec(pltpu.VMEM)...  8.72 us
    all_to_all x1, starting transfers between devices, exchange(): lax.all_to_all(block, ('gx', 'gy'), split_axis=0, concat_axis=0, axis_ind...  7.44 us
    ppermute x2, starting transfers between devices, swap_both(): return lax.ppermute(block, ('gx', 'gy'), pairs)  4.6 us
    all_to_all x1, waiting for transfers between devices, exchange(): lax.all_to_all(block, ('gx', 'gy'), split_axis=0, concat_axis=0, axis_ind...  3.45 us
    pallas_call x1, Pallas kernels, keep_blocks(): pl.pallas_call(functools.partial(keep_kernel, *places), out_shape=[block]...  3.17 us
  transfers between devices with their start and end apart: 21, of which 13 were waited for; matrix products, arithmetic and copies ran while one was open for 3% of the time, Pallas kernels for 16%

profile of v12, /device:TPU:0, one launch (start us, length us, event | category | flops | bytes accessed | tf_op | source)
XLA Modules:
  0.0 99.1 jit_solution(7296294886812498318)
XLA Ops:
  0.6 7.4 %all-to-all-start = ((bf16[16,32,384]{2,1,0:T(8,128)(2,1)}), bf16[16,32,384]{2,1,0:T(8,128)(2,1)S(1)}, u32[]{:S(2)}, u32[]{:S(2)}) async-start(bf16[16,32,384]{2,1,0:T(8,128)(2,1)} %bitcast.98), calls=%async_computation | async-start | bytes 786432 | tf_op jit(solution)/shard_map/all_to_all | solution.py:40
  8.7 1.1 %collective-permute-done = bf16[2,2,2,1,32,384]{5,4,2,1,0,3:T(8,128)(2,1)S(1)} collective-permute-done((bf16[2,2,2,1,32,384]{5,4,2,1,0,3:T(8,128)(2,1)S(1)}, bf16[2,2,2,1,32,384]{5,4,2,1,0,3:T(8,128)(2,1)S(1)}, u32[]{:S(2)}, u32[]{:S(2)}) %collective-permute-start) | collective-permute-done | bytes 196640 | tf_op jit(solution)/shard_map/ppermute | solution.py:281
  9.9 2.8 %collective-permute-start.3 = (bf16[2,2,32,384]{3,2,1,0:T(8,128)(2,1)S(1)}, bf16[2,2,32,384]{3,2,1,0:T(8,128)(2,1)S(1)}, u32[]{:S(2)}, u32[]{:S(2)}) collective-permute-start(bf16[2,2,32,384]{3,2,1,0:T(8,128)(2,1)S(1)} %bitcast.103), channel_id=1, source_target_pairs={{0,6},{1,7},{2,4},{3,5},{4,2},{5,3},{6,0},{7,1},{8,14},{9,15},{10,... | collective-permute-start | bytes 294920 | tf_op jit(solution)/shard_map/ppermute | solution.py:370
  12.7 0.6 collective-permute-start.2
  13.6 2.2 %shard_map.67.up_ref = bf16[768,1536]{1,0:T(8,128)(2,1)S(1)} custom-call(s32[2]{0:T(128)S(1)} %pad_add_fusion.place_ref, bf16[768,1536]{1,0:T(8,128)(2,1)} %source.1), custom_call_target="tpu_custom_call" | custom-call | bytes 4718592 | tf_op jit(solution)/shard_map/pallas_call | solution.py:207
  15.9 0.9 collective-permute-done.3
  16.7 2.0 %collective-permute-done.2 = bf16[2,2,32,384]{3,2,1,0:T(8,128)(2,1)S(1)} collective-permute-done((bf16[2,2,32,384]{3,2,1,0:T(8,128)(2,1)S(1)}, bf16[2,2,32,384]{3,2,1,0:T(8,128)(2,1)S(1)}, u32[]{:S(2)}, u32[]{:S(2)}) %collective-permute-start.2) | collective-permute-done | bytes 98336 | tf_op jit(solution)/shard_map/ppermute | solution.py:281
  18.9 3.5 %all-to-all-done.state_ref = bf16[16,32,384]{2,1,0:T(8,128)(2,1)S(1)} async-done(((bf16[16,32,384]{2,1,0:T(8,128)(2,1)}), bf16[16,32,384]{2,1,0:T(8,128)(2,1)S(1)}, u32[]{:S(2)}, u32[]{:S(2)}) %all-to-all-start) | async-done | bytes 393248 | tf_op jit(solution)/shard_map/all_to_all | solution.py:40
  22.6 8.7 %shard_map.68 = (bf16[16,32,384]{2,1,0:T(8,128)(2,1)S(1)}, bf16[1024,1536]{1,0:T(8,128)(2,1)S(1)}, bf16[1024,1536]{1,0:T(8,128)(2,1)S(1)}, bf16[1024,768]{1,0:T(...) custom-call(bf16[16,32,384]{2,1,0:T(8,128)(2,1)S(1)} %all-to-all-done.state_r, ...), custom_call_target="tpu_custom_call" | custom-call | flops 12079595520 | bytes 25165824 | tf_op jit(solution)/shard_map/pallas_call | solution.py:232
  31.4 2.0 %collective-permute-done.4 = bf16[8,32,384]{2,1,0:T(8,128)(2,1)S(1)} collective-permute-done((bf16[8,32,384]{2,1,0:T(8,128)(2,1)S(1)}, bf16[8,32,384]{2,1,0:T(8,128)(2,1)S(1)}, u32[]{:S(2)}, u32[]{:S(2)}) %collective-permute-start.4) | collective-permute-done | bytes 196640 | tf_op jit(solution)/shard_map/ppermute | solution.py:281
  33.4 9.5 %shard_map.69 = (bf16[1024,1536]{1,0:T(8,128)(2,1)S(1)}, bf16[768,1024]{1,0:T(8,128)(2,1)S(1)}, bf16[16,96,384]{2,1,0:T(8,128)(2,1)S(1)}, bf16[16,96,384]{2,1,0:T(8,128)(2,1)S(1)}) custom-call(s32[2]{0:T(128)S(1)} %pad_add_fusion.place_ref, bf16[16,32,384]{2,1,0:T(8,128)(2,1)S(1)} %pad_maximum_fusion.1.grad_ref, ...), custom_call_target="tpu_custom_call" | custom-call | flops 12079595520 | bytes 25165824 | tf_op jit(solution)/shard_map/pallas_call | solution.py:251
  43.4 0.7 collective-permute-start.5
  44.2 10.6 %collective-permute-done.5 = bf16[2,2,2,1,32,384]{5,4,2,1,0,3:T(8,128)(2,1)S(1)} collective-permute-done((bf16[2,2,2,1,32,384]{5,4,2,1,0,3:T(8,128)(2,1)S(1)}, bf16[2,2,2,1,32,384]{5,4,2,1,0,3:T(8,128)(2,1)S(1)}, u32[]{:S(2)}, u32[]{:S(2)}) %collective-permute-start.5) | collective-permute-done | bytes 196640 | tf_op jit(solution)/shard_map/ppermute | solution.py:281
  54.9 3.2 %shard_map.70 = (bf16[16,96,384]{2,1,0:T(8,128)(2,1)S(1)}, bf16[16,96,384]{2,1,0:T(8,128)(2,1)S(1)}) custom-call(s32[2]{0:T(128)S(1)} %pad_add_fusion.place_ref, bf16[1024,1536]{1,0:T(8,128)(2,1)S(1)} %get-tuple-element.58.hidden_ref, bf16[1024,1536]{1,0:T(8,128)(2,1)S(1)} %get-tuple-element.65.d_pre_ref, ...), custom_call_target="tpu_custom_call" | custom-call | flops 2415919104 | bytes 12582912 | tf_op jit(solution)/shard_map/pallas_call | solution.py:267
  58.4 1.5 %collective-permute-start.15 = (bf16[8,96,384]{2,1,0:T(8,128)(2,1)S(1)}, bf16[8,96,384]{2,1,0:T(8,128)(2,1)S(1)}, u32[]{:S(2)}, u32[]{:S(2)}) collective-permute-start(bf16[8,96,384]{2,1,0:T(8,128)(2,1)S(1)} %get-tuple-element.84), channel_id=1, source_target_pairs={{0,2},{1,3},{2,0},{3,1},{4,6},{5,7},{6,4},{7,5},{8,10},{9,11},{10,... | collective-permute-start | bytes 1769480 | tf_op jit(solution)/shard_map/ppermute | solution.py:281
  60.2 1.1 %collective-permute-start.8 = (bf16[8,96,384]{2,1,0:T(8,128)(2,1)S(1)}, bf16[8,96,384]{2,1,0:T(8,128)(2,1)S(1)}, u32[]{:S(2)}, u32[]{:S(2)}) collective-permute-start(bf16[8,96,384]{2,1,0:T(8,128)(2,1)S(1)} %get-tuple-element.86), channel_id=1, source_target_pairs={{0,4},{4,0},{8,12},{12,8},{16,20},{20,16},{24,28},{28,24},{1,5},{5... | collective-permute-start | bytes 1769480 | tf_op jit(solution)/shard_map/ppermute | solution.py:281
  61.2 12.5 %collective-permute-done.15 = bf16[8,96,384]{2,1,0:T(8,128)(2,1)S(1)} collective-permute-done((bf16[8,96,384]{2,1,0:T(8,128)(2,1)S(1)}, bf16[8,96,384]{2,1,0:T(8,128)(2,1)S(1)}, u32[]{:S(2)}, u32[]{:S(2)}) %collective-permute-start.15) | collective-permute-done | bytes 589856 | tf_op jit(solution)/shard_map/ppermute | solution.py:281
  73.9 1.6 %collective-permute-start.16 = (bf16[4,96,384]{2,1,0:T(8,128)(2,1)S(1)}, bf16[4,96,384]{2,1,0:T(8,128)(2,1)S(1)}, u32[]{:S(2)}, u32[]{:S(2)}) collective-permute-start(bf16[4,96,384]{2,1,0:T(8,128)(2,1)S(1)} %get-tuple-element.88), channel_id=1, source_target_pairs={{0,4},{4,0},{8,12},{12,8},{16,20},{20,16},{24,28},{28,24},{1,5},{5... | collective-permute-start | bytes 884744 | tf_op jit(solution)/shard_map/ppermute | solution.py:281
  75.6 1.0 collective-permute-start.9
  76.6 0.7 fusion.13
  77.3 4.7 %collective-permute-done.16 = bf16[4,96,384]{2,1,0:T(8,128)(2,1)S(1)} collective-permute-done((bf16[4,96,384]{2,1,0:T(8,128)(2,1)S(1)}, bf16[4,96,384]{2,1,0:T(8,128)(2,1)S(1)}, u32[]{:S(2)}, u32[]{:S(2)}) %collective-permute-start.16) | collective-permute-done | bytes 294944 | tf_op jit(solution)/shard_map/ppermute | solution.py:281
  82.2 1.3 %collective-permute-done.9 = bf16[4,96,384]{2,1,0:T(8,128)(2,1)S(1)} collective-permute-done((bf16[4,96,384]{2,1,0:T(8,128)(2,1)S(1)}, bf16[4,96,384]{2,1,0:T(8,128)(2,1)S(1)}, u32[]{:S(2)}, u32[]{:S(2)}) %collective-permute-start.9) | collective-permute-done | bytes 294944 | tf_op jit(solution)/shard_map/ppermute | solution.py:281
  83.5 1.7 %collective-permute-start.13 = (bf16[2,96,384]{2,1,0:T(8,128)(2,1)S(1)}, bf16[2,96,384]{2,1,0:T(8,128)(2,1)S(1)}, u32[]{:S(2)}, u32[]{:S(2)}) collective-permute-start(bf16[2,96,384]{2,1,0:T(8,128)(2,1)S(1)} %get-tuple-element.75), channel_id=1, source_target_pairs={{0,8},{4,12},{8,0},{12,4},{16,24},{20,28},{24,16},{28,20},{1,9},{5... | collective-permute-start | bytes 442376 | tf_op jit(solution)/shard_map/ppermute | solution.py:281
  85.5 1.4 %collective-permute-start.11 = (bf16[4,32,384]{2,1,0:T(8,128)(2,1)S(1)}, bf16[4,32,384]{2,1,0:T(8,128)(2,1)S(1)}, u32[]{:S(2)}, u32[]{:S(2)}) collective-permute-start(bf16[4,32,384]{2,1,0:T(8,128)(2,1)S(1)} %get-tuple-element.72), channel_id=1, source_target_pairs={{0,4},{4,0},{8,12},{12,8},{16,20},{20,16},{24,28},{28,24},{1,5},{5... | collective-permute-start | bytes 294920 | tf_op jit(solution)/shard_map/ppermute | solution.py:281
  86.9 1.8 %collective-permute-start.12 = (bf16[4,32,384]{2,1,0:T(8,128)(2,1)S(1)}, bf16[4,32,384]{2,1,0:T(8,128)(2,1)S(1)}, u32[]{:S(2)}, u32[]{:S(2)}) collective-permute-start(bf16[4,32,384]{2,1,0:T(8,128)(2,1)S(1)} %get-tuple-element.73), channel_id=1, source_target_pairs={{0,6},{1,7},{2,4},{3,5},{4,2},{5,3},{6,0},{7,1},{8,14},{9,15},{10,... | collective-permute-start | bytes 294920 | tf_op jit(solution)/shard_map/ppermute | solution.py:370
  88.7 1.3 %collective-permute-done.17 = bf16[2,96,384]{2,1,0:T(8,128)(2,1)S(1)} collective-permute-done((bf16[2,96,384]{2,1,0:T(8,128)(2,1)S(1)}, bf16[2,96,384]{2,1,0:T(8,128)(2,1)S(1)}, u32[]{:S(2)}, u32[]{:S(2)}) %collective-permute-start.17) | collective-permute-done | bytes 147488 | tf_op jit(solution)/shard_map/ppermute | solution.py:281
  90.6 1.8 %collective-permute-done.12.refs_3_ = bf16[4,32,384]{2,1,0:T(8,128)(2,1)S(1)} collective-permute-done((bf16[4,32,384]{2,1,0:T(8,128)(2,1)S(1)}, bf16[4,32,384]{2,1,0:T(8,128)(2,1)S(1)}, u32[]{:S(2)}, u32[]{:S(2)}) %collective-permute-start.12) | collective-permute-done | bytes 98336 | tf_op jit(solution)/shard_map/ppermute | solution.py:370
  92.4 0.9 collective-permute-start.19
  93.3 1.9 %shard_map.71 = bf16[512,384]{1,0:T(8,128)(2,1)} custom-call(s32[2]{0:T(128)} %copy-done, bf16[4,32,384]{2,1,0:T(8,128)(2,1)} %get-tuple-element.76.refs_0_, bf16[4,32,384]{2,1,0:T(8,128)(2,1)} %copy-done.2, bf16[4,32,384]{2,1,0:T(8,128)(2,1)} %copy-done.3, bf16[4,32,384]{2,1,0:T(8,128)(2,1)} %copy-done.4), custom_call_target="tpu_custom_call" | custom-call | bytes 786432 | tf_op jit(solution)/shard_map/pallas_call | solution.py:376
  95.2 0.7 add_bitcast_fusion.1
  95.9 2.5 %collective-permute-done.19 = bf16[1,96,384]{2,1,0:T(8,128)(2,1)S(1)} collective-permute-done((bf16[1,96,384]{2,1,0:T(8,128)(2,1)S(1)}, bf16[1,96,384]{2,1,0:T(8,128)(2,1)S(1)}, u32[]{:S(2)}, u32[]{:S(2)}) %collective-permute-start.19) | collective-permute-done | bytes 73760 | tf_op jit(solution)/shard_map/ppermute | solution.py:281
  98.4 0.7 add_bitcast_fusion
  (50 shorter events, 4.0 us)
Async XLA Ops:
  0.6 7.6 %copy-start.1 = (bf16[512,384]{1,0:T(8,128)(2,1)S(1)}, bf16[512,384]{1,0:T(8,128)(2,1)}, u32[]{:S(2)}) copy-start(bf16[512,384]{1,0:T(8,128)(2,1)} %param.7) | copy-start | bytes 1179652
  0.6 21.7 %all-to-all-start = ((bf16[16,32,384]{2,1,0:T(8,128)(2,1)}), bf16[16,32,384]{2,1,0:T(8,128)(2,1)S(1)}, u32[]{:S(2)}, u32[]{:S(2)}) async-start(bf16[16,32,384]{2,1,0:T(8,128)(2,1)} %bitcast.98), calls=%async_computation | async-start | bytes 786432 | tf_op jit(solution)/shard_map/all_to_all | solution.py:40
  8.3 46.6 %copy-start = (s32[2]{0:T(128)}, s32[2]{0:T(128)S(1)}, u32[]{:S(2)}) copy-start(s32[2]{0:T(128)S(1)} %pad_add_fusion.place_ref) | copy-start | bytes 28
  8.3 1.5 %collective-permute-start = (bf16[2,2,2,1,32,384]{5,4,2,1,0,3:T(8,128)(2,1)S(1)}, bf16[2,2,2,1,32,384]{5,4,2,1,0,3:T(8,128)(2,1)S(1)}, u32[]{:S(2)}, u32[]{:S(2)}) collective-permute-start(bf16[2,2,2,1,32,384]{5,4,2,1,0,3:T(8,128)(2,1)S(1)} %get-tuple-element.109), channel_id=1, source_target_pairs={{0,1},{1,0},{2,3},{3,2},{4,5},{5,4},{6,7},{7,6},{8,9},{9,8},{10,11... | collective-permute-start | bytes 589832 | tf_op jit(solution)/shard_map/ppermute | solution.py:281
  9.9 6.8 %collective-permute-start.3 = (bf16[2,2,32,384]{3,2,1,0:T(8,128)(2,1)S(1)}, bf16[2,2,32,384]{3,2,1,0:T(8,128)(2,1)S(1)}, u32[]{:S(2)}, u32[]{:S(2)}) collective-permute-start(bf16[2,2,32,384]{3,2,1,0:T(8,128)(2,1)S(1)} %bitcast.103), channel_id=1, source_target_pairs={{0,6},{1,7},{2,4},{3,5},{4,2},{5,3},{6,0},{7,1},{8,14},{9,15},{10,... | collective-permute-start | bytes 294920 | tf_op jit(solution)/shard_map/ppermute | solution.py:370
  12.7 6.0 %collective-permute-start.2 = (bf16[2,2,32,384]{3,2,1,0:T(8,128)(2,1)S(1)}, bf16[2,2,32,384]{3,2,1,0:T(8,128)(2,1)S(1)}, u32[]{:S(2)}, u32[]{:S(2)}) collective-permute-start(bf16[2,2,32,384]{3,2,1,0:T(8,128)(2,1)S(1)} %bitcast.104), channel_id=1, source_target_pairs={{0,4},{4,0},{8,12},{12,8},{16,20},{20,16},{24,28},{28,24},{1,5},{5... | collective-permute-start | bytes 294920 | tf_op jit(solution)/shard_map/ppermute | solution.py:281
  13.4 5.4 %collective-permute-start.1 = (bf16[2,2,32,384]{3,2,1,0:T(8,128)(2,1)S(1)}, bf16[2,2,32,384]{3,2,1,0:T(8,128)(2,1)S(1)}, u32[]{:S(2)}, u32[]{:S(2)}) collective-permute-start(bf16[2,2,32,384]{3,2,1,0:T(8,128)(2,1)S(1)} %bitcast.105), channel_id=1, source_target_pairs={{0,2},{1,3},{2,0},{3,1},{4,6},{5,7},{6,4},{7,5},{8,10},{9,11},{10,... | collective-permute-start | bytes 294920 | tf_op jit(solution)/shard_map/ppermute | solution.py:281
  22.3 11.0 %collective-permute-start.4 = (bf16[8,32,384]{2,1,0:T(8,128)(2,1)S(1)}, bf16[8,32,384]{2,1,0:T(8,128)(2,1)S(1)}, u32[]{:S(2)}, u32[]{:S(2)}) collective-permute-start(bf16[8,32,384]{2,1,0:T(8,128)(2,1)S(1)} %get-tuple-element.54), channel_id=1, source_target_pairs={{0,16},{4,20},{8,24},{12,28},{16,0},{20,4},{24,8},{28,12},{1,17},{... | collective-permute-start | bytes 589832 | tf_op jit(solution)/shard_map/ppermute | solution.py:281
  42.9 15.2 %collective-permute-start.14 = (bf16[16,96,384]{2,1,0:T(8,128)(2,1)S(1)}, bf16[16,96,384]{2,1,0:T(8,128)(2,1)S(1)}, u32[]{:S(2)}, u32[]{:S(2)}) collective-permute-start(bf16[16,96,384]{2,1,0:T(8,128)(2,1)S(1)} %get-tuple-element.81), channel_id=1, source_target_pairs={{0,1},{1,0},{2,3},{3,2},{4,5},{5,4},{6,7},{7,6},{8,9},{9,8},{10,11... | collective-permute-start | bytes 3538952 | tf_op jit(solution)/shard_map/ppermute | solution.py:281
  42.9 16.9 %collective-permute-start.7 = (bf16[16,96,384]{2,1,0:T(8,128)(2,1)S(1)}, bf16[16,96,384]{2,1,0:T(8,128)(2,1)S(1)}, u32[]{:S(2)}, u32[]{:S(2)}) collective-permute-start(bf16[16,96,384]{2,1,0:T(8,128)(2,1)S(1)} %get-tuple-element.68), channel_id=1, source_target_pairs={{0,1},{1,0},{2,3},{3,2},{4,5},{5,4},{6,7},{7,6},{8,9},{9,8},{10,11... | collective-permute-start | bytes 3538952 | tf_op jit(solution)/shard_map/ppermute | solution.py:281
  43.4 11.3 %collective-permute-start.5 = (bf16[2,2,2,1,32,384]{5,4,2,1,0,3:T(8,128)(2,1)S(1)}, bf16[2,2,2,1,32,384]{5,4,2,1,0,3:T(8,128)(2,1)S(1)}, u32[]{:S(2)}, u32[]{:S(2)}) collective-permute-start(bf16[2,2,2,1,32,384]{5,4,2,1,0,3:T(8,128)(2,1)S(1)} %get-tuple-element.55), channel_id=1, source_target_pairs={{0,16},{4,20},{8,24},{12,28},{16,0},{20,4},{24,8},{28,12},{1,17},{... | collective-permute-start | bytes 589832 | tf_op jit(solution)/shard_map/ppermute | solution.py:281
  58.4 15.3 %collective-permute-start.15 = (bf16[8,96,384]{2,1,0:T(8,128)(2,1)S(1)}, bf16[8,96,384]{2,1,0:T(8,128)(2,1)S(1)}, u32[]{:S(2)}, u32[]{:S(2)}) collective-permute-start(bf16[8,96,384]{2,1,0:T(8,128)(2,1)S(1)} %get-tuple-element.84), channel_id=1, source_target_pairs={{0,2},{1,3},{2,0},{3,1},{4,6},{5,7},{6,4},{7,5},{8,10},{9,11},{10,... | collective-permute-start | bytes 1769480 | tf_op jit(solution)/shard_map/ppermute | solution.py:281
  60.2 15.2 %collective-permute-start.8 = (bf16[8,96,384]{2,1,0:T(8,128)(2,1)S(1)}, bf16[8,96,384]{2,1,0:T(8,128)(2,1)S(1)}, u32[]{:S(2)}, u32[]{:S(2)}) collective-permute-start(bf16[8,96,384]{2,1,0:T(8,128)(2,1)S(1)} %get-tuple-element.86), channel_id=1, source_target_pairs={{0,4},{4,0},{8,12},{12,8},{16,20},{20,16},{24,28},{28,24},{1,5},{5... | collective-permute-start | bytes 1769480 | tf_op jit(solution)/shard_map/ppermute | solution.py:281
  61.2 15.4 %collective-permute-start.6 = (bf16[2,2,2,32,384]{4,3,2,1,0:T(8,128)(2,1)S(1)}, bf16[2,2,2,32,384]{4,3,2,1,0:T(8,128)(2,1)S(1)}, u32[]{:S(2)}, u32[]{:S(2)}) collective-permute-start(bf16[2,2,2,32,384]{4,3,2,1,0:T(8,128)(2,1)S(1)} %bitcast.102), channel_id=1, source_target_pairs={{0,1},{1,0},{2,3},{3,2},{4,5},{5,4},{6,7},{7,6},{8,9},{9,8},{10,11... | collective-permute-start | bytes 589832 | tf_op jit(solution)/shard_map/ppermute | solution.py:281
  73.9 8.2 %collective-permute-start.16 = (bf16[4,96,384]{2,1,0:T(8,128)(2,1)S(1)}, bf16[4,96,384]{2,1,0:T(8,128)(2,1)S(1)}, u32[]{:S(2)}, u32[]{:S(2)}) collective-permute-start(bf16[4,96,384]{2,1,0:T(8,128)(2,1)S(1)} %get-tuple-element.88), channel_id=1, source_target_pairs={{0,4},{4,0},{8,12},{12,8},{16,20},{20,16},{24,28},{28,24},{1,5},{5... | collective-permute-start | bytes 884744 | tf_op jit(solution)/shard_map/ppermute | solution.py:281
  75.6 7.9 %collective-permute-start.9 = (bf16[4,96,384]{2,1,0:T(8,128)(2,1)S(1)}, bf16[4,96,384]{2,1,0:T(8,128)(2,1)S(1)}, u32[]{:S(2)}, u32[]{:S(2)}) collective-permute-start(bf16[4,96,384]{2,1,0:T(8,128)(2,1)S(1)} %get-tuple-element.90), channel_id=1, source_target_pairs={{0,2},{1,3},{2,0},{3,1},{4,6},{5,7},{6,4},{7,5},{8,10},{9,11},{10,... | collective-permute-start | bytes 884744 | tf_op jit(solution)/shard_map/ppermute | solution.py:281
  82.1 7.9 %collective-permute-start.17 = (bf16[2,96,384]{2,1,0:T(8,128)(2,1)S(1)}, bf16[2,96,384]{2,1,0:T(8,128)(2,1)S(1)}, u32[]{:S(2)}, u32[]{:S(2)}) collective-permute-start(bf16[2,96,384]{2,1,0:T(8,128)(2,1)S(1)} %get-tuple-element.92), channel_id=1, source_target_pairs={{0,16},{4,20},{8,24},{12,28},{16,0},{20,4},{24,8},{28,12},{1,17},{... | collective-permute-start | bytes 442376 | tf_op jit(solution)/shard_map/ppermute | solution.py:281
  83.5 7.0 %collective-permute-start.13 = (bf16[2,96,384]{2,1,0:T(8,128)(2,1)S(1)}, bf16[2,96,384]{2,1,0:T(8,128)(2,1)S(1)}, u32[]{:S(2)}, u32[]{:S(2)}) collective-permute-start(bf16[2,96,384]{2,1,0:T(8,128)(2,1)S(1)} %get-tuple-element.75), channel_id=1, source_target_pairs={{0,8},{4,12},{8,0},{12,4},{16,24},{20,28},{24,16},{28,20},{1,9},{5... | collective-permute-start | bytes 442376 | tf_op jit(solution)/shard_map/ppermute | solution.py:281
  85.2 5.3 %collective-permute-start.10 = (bf16[4,32,384]{2,1,0:T(8,128)(2,1)S(1)}, bf16[4,32,384]{2,1,0:T(8,128)(2,1)S(1)}, u32[]{:S(2)}, u32[]{:S(2)}) collective-permute-start(bf16[4,32,384]{2,1,0:T(8,128)(2,1)S(1)} %get-tuple-element.71), channel_id=1, source_target_pairs={{0,2},{1,3},{2,0},{3,1},{4,6},{5,7},{6,4},{7,5},{8,10},{9,11},{10,... | collective-permute-start | bytes 294920 | tf_op jit(solution)/shard_map/ppermute | solution.py:281
  85.5 5.0 %collective-permute-start.11 = (bf16[4,32,384]{2,1,0:T(8,128)(2,1)S(1)}, bf16[4,32,384]{2,1,0:T(8,128)(2,1)S(1)}, u32[]{:S(2)}, u32[]{:S(2)}) collective-permute-start(bf16[4,32,384]{2,1,0:T(8,128)(2,1)S(1)} %get-tuple-element.72), channel_id=1, source_target_pairs={{0,4},{4,0},{8,12},{12,8},{16,20},{20,16},{24,28},{28,24},{1,5},{5... | collective-permute-start | bytes 294920 | tf_op jit(solution)/shard_map/ppermute | solution.py:281
  86.9 5.5 %collective-permute-start.12 = (bf16[4,32,384]{2,1,0:T(8,128)(2,1)S(1)}, bf16[4,32,384]{2,1,0:T(8,128)(2,1)S(1)}, u32[]{:S(2)}, u32[]{:S(2)}) collective-permute-start(bf16[4,32,384]{2,1,0:T(8,128)(2,1)S(1)} %get-tuple-element.73), channel_id=1, source_target_pairs={{0,6},{1,7},{2,4},{3,5},{4,2},{5,3},{6,0},{7,1},{8,14},{9,15},{10,... | collective-permute-start | bytes 294920 | tf_op jit(solution)/shard_map/ppermute | solution.py:370
  90.1 5.1 %collective-permute-start.18 = (bf16[1,96,384]{2,1,0:T(8,128)(2,1)S(1)}, bf16[1,96,384]{2,1,0:T(8,128)(2,1)S(1)}, u32[]{:S(2)}, u32[]{:S(2)}) collective-permute-start(bf16[1,96,384]{2,1,0:T(8,128)(2,1)S(1)} %fusion.9), channel_id=1, source_target_pairs={{0,8},{4,12},{8,0},{12,4},{16,24},{20,28},{24,16},{28,20},{1,9},{5... | collective-permute-start | bytes 221192 | tf_op jit(solution)/shard_map/ppermute | solution.py:281
  90.5 2.7 %copy-start.2 = (bf16[4,32,384]{2,1,0:T(8,128)(2,1)}, bf16[4,32,384]{2,1,0:T(8,128)(2,1)S(1)}, u32[]{:S(2)}) copy-start(bf16[4,32,384]{2,1,0:T(8,128)(2,1)S(1)} %collective-permute-done.10.refs_1_) | copy-start | bytes 294916
  90.6 2.7 %copy-start.3 = (bf16[4,32,384]{2,1,0:T(8,128)(2,1)}, bf16[4,32,384]{2,1,0:T(8,128)(2,1)S(1)}, u32[]{:S(2)}) copy-start(bf16[4,32,384]{2,1,0:T(8,128)(2,1)S(1)} %collective-permute-done.11.refs_2_) | copy-start | bytes 294916
  92.4 0.9 copy-start.4
  92.4 6.0 %collective-permute-start.19 = (bf16[1,96,384]{2,1,0:T(8,128)(2,1)S(1)}, bf16[1,96,384]{2,1,0:T(8,128)(2,1)S(1)}, u32[]{:S(2)}, u32[]{:S(2)}) collective-permute-start(bf16[1,96,384]{2,1,0:T(8,128)(2,1)S(1)} %fusion.11), channel_id=1, source_target_pairs={{0,16},{4,20},{8,24},{12,28},{16,0},{20,4},{24,8},{28,12},{1,17},{... | collective-permute-start | bytes 221192 | tf_op jit(solution)/shard_map/ppermute | solution.py:281

commit v13 on v12

--- a/solution.py
+++ b/solution.py
@@ -427,9 +427,9 @@
         grad_down = scatter_narrow(halves, grad_t, hidden, [steps[core]] + order_down, span_x, span_y)
         grad_up = scatter_narrow(halves, normed_t, d_pre, [steps[core]] + order_up, span_x, span_y)
         return (mixed_out, grad_up, grad_down)
+    given[0] = going.hop(core, steps, halves, given[0])
     take_down, take_up = [swap(part, *steps[core]) for part in given]
-    after = going.hop(core, steps, halves, place)
-    keep_down, keep_up = keep_blocks(after, hidden, d_pre, normed_t, grad_t, places, block)
+    keep_down, keep_up = keep_blocks(place, hidden, d_pre, normed_t, grad_t, places, block)
 
     def beside(phase, give):
         if phase == 2:

time: 99.5 us -> 95.2 us (0.957)
  waiting for transfers between devices: 44.6 us -> 39.1 us
  starting transfers between devices: 24.3 us -> 25.6 us
    ppermute x18, waiting for transfers between devices: 38.4 us -> 33.7 us  [swap(): return lax.ppermute(block, axis, pairs)]
    ppermute x18, starting transfers between devices: 12.2 us -> 14 us  [swap(): return lax.ppermute(block, axis, pairs)]
  transfers between devices with their start and end apart: 21 -> 21, of which waited for: 13 -> 14; matrix products, arithmetic and copies ran while one was open for 3% -> 3% of each run, Pallas kernels for 16% -> 27%
where the time goes in v13:
time: 95.2 us; the launch traced here: 94.9 us
  waiting for transfers between devices  39.1 us (41%)
  starting transfers between devices  25.6 us (27%)
  Pallas kernels  25.5 us (27%)
  other arithmetic  3.52 us (4%)
    ppermute x18, waiting for transfers between devices, swap(): return lax.ppermute(block, axis, pairs)  33.7 us
    ppermute x18, starting transfers between devices, swap(): return lax.ppermute(block, axis, pairs)  14 us
    pallas_call x1, Pallas kernels, backward(): pl.pallas_call(functools.partial(backward_kernel, *places), out_shape=out...  9.47 us
    pallas_call x1, Pallas kernels, forward(): pl.pallas_call(forward_kernel, out_shape=outs, in_specs=[spec(pltpu.VMEM)...  8.72 us
    all_to_all x1, starting transfers between devices, exchange(): lax.all_to_all(block, ('gx', 'gy'), split_axis=0, concat_axis=0, axis_ind...  7.44 us
    ppermute x2, starting transfers between devices, swap_both(): return lax.ppermute(block, ('gx', 'gy'), pairs)  4.17 us
    all_to_all x1, waiting for transfers between devices, exchange(): lax.all_to_all(block, ('gx', 'gy'), split_axis=0, concat_axis=0, axis_ind...  3.45 us
    pallas_call x1, Pallas kernels, keep_blocks(): pl.pallas_call(functools.partial(keep_kernel, *places), out_shape=[block]...  3.17 us
  transfers between devices with their start and end apart: 21, of which 14 were waited for; matrix products, arithmetic and copies ran while one was open for 3% of the time, Pallas kernels for 27%

profile of v13, /device:TPU:0, one launch (start us, length us, event | category | flops | bytes accessed | tf_op | source)
XLA Modules:
  0.0 94.9 jit_solution(9700515573015609067)
XLA Ops:
  0.6 7.4 %all-to-all-start = ((bf16[16,32,384]{2,1,0:T(8,128)(2,1)}), bf16[16,32,384]{2,1,0:T(8,128)(2,1)S(1)}, u32[]{:S(2)}, u32[]{:S(2)}) async-start(bf16[16,32,384]{2,1,0:T(8,128)(2,1)} %bitcast.98), calls=%async_computation | async-start | bytes 786432 | tf_op jit(solution)/shard_map/all_to_all | solution.py:40
  8.7 1.1 %collective-permute-done = bf16[2,2,2,1,32,384]{5,4,2,1,0,3:T(8,128)(2,1)S(1)} collective-permute-done((bf16[2,2,2,1,32,384]{5,4,2,1,0,3:T(8,128)(2,1)S(1)}, bf16[2,2,2,1,32,384]{5,4,2,1,0,3:T(8,128)(2,1)S(1)}, u32[]{:S(2)}, u32[]{:S(2)}) %collective-permute-start) | collective-permute-done | bytes 196640 | tf_op jit(solution)/shard_map/ppermute | solution.py:281
  9.9 2.8 %collective-permute-start.3 = (bf16[2,2,32,384]{3,2,1,0:T(8,128)(2,1)S(1)}, bf16[2,2,32,384]{3,2,1,0:T(8,128)(2,1)S(1)}, u32[]{:S(2)}, u32[]{:S(2)}) collective-permute-start(bf16[2,2,32,384]{3,2,1,0:T(8,128)(2,1)S(1)} %bitcast.103), channel_id=1, source_target_pairs={{0,6},{1,7},{2,4},{3,5},{4,2},{5,3},{6,0},{7,1},{8,14},{9,15},{10,... | collective-permute-start | bytes 294920 | tf_op jit(solution)/shard_map/ppermute | solution.py:370
  13.6 2.2 %shard_map.67.up_ref = bf16[768,1536]{1,0:T(8,128)(2,1)S(1)} custom-call(s32[2]{0:T(128)S(1)} %pad_add_fusion.place_ref, bf16[768,1536]{1,0:T(8,128)(2,1)} %source.1), custom_call_target="tpu_custom_call" | custom-call | bytes 4718592 | tf_op jit(solution)/shard_map/pallas_call | solution.py:207
  15.9 0.9 collective-permute-done.3
  16.7 2.0 %collective-permute-done.2 = bf16[2,2,32,384]{3,2,1,0:T(8,128)(2,1)S(1)} collective-permute-done((bf16[2,2,32,384]{3,2,1,0:T(8,128)(2,1)S(1)}, bf16[2,2,32,384]{3,2,1,0:T(8,128)(2,1)S(1)}, u32[]{:S(2)}, u32[]{:S(2)}) %collective-permute-start.2) | collective-permute-done | bytes 98336 | tf_op jit(solution)/shard_map/ppermute | solution.py:281
  18.9 3.5 %all-to-all-done.state_ref = bf16[16,32,384]{2,1,0:T(8,128)(2,1)S(1)} async-done(((bf16[16,32,384]{2,1,0:T(8,128)(2,1)}), bf16[16,32,384]{2,1,0:T(8,128)(2,1)S(1)}, u32[]{:S(2)}, u32[]{:S(2)}) %all-to-all-start) | async-done | bytes 393248 | tf_op jit(solution)/shard_map/all_to_all | solution.py:40
  22.6 8.7 %shard_map.68 = (bf16[16,32,384]{2,1,0:T(8,128)(2,1)S(1)}, bf16[1024,1536]{1,0:T(8,128)(2,1)S(1)}, bf16[1024,1536]{1,0:T(8,128)(2,1)S(1)}, bf16[1024,768]{1,0:T(...) custom-call(bf16[16,32,384]{2,1,0:T(8,128)(2,1)S(1)} %all-to-all-done.state_r, ...), custom_call_target="tpu_custom_call" | custom-call | flops 12079595520 | bytes 25165824 | tf_op jit(solution)/shard_map/pallas_call | solution.py:232
  31.4 2.0 %collective-permute-done.4 = bf16[8,32,384]{2,1,0:T(8,128)(2,1)S(1)} collective-permute-done((bf16[8,32,384]{2,1,0:T(8,128)(2,1)S(1)}, bf16[8,32,384]{2,1,0:T(8,128)(2,1)S(1)}, u32[]{:S(2)}, u32[]{:S(2)}) %collective-permute-start.4) | collective-permute-done | bytes 196640 | tf_op jit(solution)/shard_map/ppermute | solution.py:281
  33.4 0.8 collective-permute-start.5
  34.2 9.5 %shard_map.69 = (bf16[1024,1536]{1,0:T(8,128)(2,1)S(1)}, bf16[768,1024]{1,0:T(8,128)(2,1)S(1)}, bf16[16,96,384]{2,1,0:T(8,128)(2,1)S(1)}, bf16[16,96,384]{2,1,0:T(8,128)(2,1)S(1)}) custom-call(s32[2]{0:T(128)S(1)} %pad_add_fusion.place_ref, bf16[16,32,384]{2,1,0:T(8,128)(2,1)S(1)} %pad_maximum_fusion.1.grad_ref, ...), custom_call_target="tpu_custom_call" | custom-call | flops 12079595520 | bytes 25165824 | tf_op jit(solution)/shard_map/pallas_call | solution.py:251
  43.8 0.7 collective-permute-done.5
  44.7 3.2 %shard_map.70 = (bf16[16,96,384]{2,1,0:T(8,128)(2,1)S(1)}, bf16[16,96,384]{2,1,0:T(8,128)(2,1)S(1)}) custom-call(s32[2]{0:T(128)S(1)} %pad_add_fusion.place_ref, bf16[1024,1536]{1,0:T(8,128)(2,1)S(1)} %get-tuple-element.57.hidden_ref, bf16[1024,1536]{1,0:T(8,128)(2,1)S(1)} %get-tuple-element.65.d_pre_ref, ...), custom_call_target="tpu_custom_call" | custom-call | flops 2415919104 | bytes 12582912 | tf_op jit(solution)/shard_map/pallas_call | solution.py:267
  48.2 1.5 %collective-permute-start.15 = (bf16[8,96,384]{2,1,0:T(8,128)(2,1)S(1)}, bf16[8,96,384]{2,1,0:T(8,128)(2,1)S(1)}, u32[]{:S(2)}, u32[]{:S(2)}) collective-permute-start(bf16[8,96,384]{2,1,0:T(8,128)(2,1)S(1)} %get-tuple-element.84), channel_id=1, source_target_pairs={{0,2},{1,3},{2,0},{3,1},{4,6},{5,7},{6,4},{7,5},{8,10},{9,11},{10,... | collective-permute-start | bytes 1769480 | tf_op jit(solution)/shard_map/ppermute | solution.py:281
  50.7 13.3 %collective-permute-done.15 = bf16[8,96,384]{2,1,0:T(8,128)(2,1)S(1)} collective-permute-done((bf16[8,96,384]{2,1,0:T(8,128)(2,1)S(1)}, bf16[8,96,384]{2,1,0:T(8,128)(2,1)S(1)}, u32[]{:S(2)}, u32[]{:S(2)}) %collective-permute-start.15) | collective-permute-done | bytes 589856 | tf_op jit(solution)/shard_map/ppermute | solution.py:281
  64.1 1.5 %collective-permute-start.16 = (bf16[4,96,384]{2,1,0:T(8,128)(2,1)S(1)}, bf16[4,96,384]{2,1,0:T(8,128)(2,1)S(1)}, u32[]{:S(2)}, u32[]{:S(2)}) collective-permute-start(bf16[4,96,384]{2,1,0:T(8,128)(2,1)S(1)} %get-tuple-element.88), channel_id=1, source_target_pairs={{0,4},{4,0},{8,12},{12,8},{16,20},{20,16},{24,28},{28,24},{1,5},{5... | collective-permute-start | bytes 884744 | tf_op jit(solution)/shard_map/ppermute | solution.py:281
  65.8 0.7 collective-permute-start.9
  66.5 0.7 fusion.13
  67.2 5.6 %collective-permute-done.16 = bf16[4,96,384]{2,1,0:T(8,128)(2,1)S(1)} collective-permute-done((bf16[4,96,384]{2,1,0:T(8,128)(2,1)S(1)}, bf16[4,96,384]{2,1,0:T(8,128)(2,1)S(1)}, u32[]{:S(2)}, u32[]{:S(2)}) %collective-permute-start.16) | collective-permute-done | bytes 294944 | tf_op jit(solution)/shard_map/ppermute | solution.py:281
  72.9 1.0 %collective-permute-start.17 = (bf16[2,96,384]{2,1,0:T(8,128)(2,1)S(1)}, bf16[2,96,384]{2,1,0:T(8,128)(2,1)S(1)}, u32[]{:S(2)}, u32[]{:S(2)}) collective-permute-start(bf16[2,96,384]{2,1,0:T(8,128)(2,1)S(1)} %get-tuple-element.92), channel_id=1, source_target_pairs={{0,16},{4,20},{8,24},{12,28},{16,0},{20,4},{24,8},{28,12},{1,17},{... | collective-permute-start | bytes 442376 | tf_op jit(solution)/shard_map/ppermute | solution.py:281
  74.3 1.5 %collective-permute-start.13 = (bf16[2,96,384]{2,1,0:T(8,128)(2,1)S(1)}, bf16[2,96,384]{2,1,0:T(8,128)(2,1)S(1)}, u32[]{:S(2)}, u32[]{:S(2)}) collective-permute-start(bf16[2,96,384]{2,1,0:T(8,128)(2,1)S(1)} %get-tuple-element.75), channel_id=1, source_target_pairs={{0,8},{4,12},{8,0},{12,4},{16,24},{20,28},{24,16},{28,20},{1,9},{5... | collective-permute-start | bytes 442376 | tf_op jit(solution)/shard_map/ppermute | solution.py:281
  75.8 5.4 %collective-permute-done.17 = bf16[2,96,384]{2,1,0:T(8,128)(2,1)S(1)} collective-permute-done((bf16[2,96,384]{2,1,0:T(8,128)(2,1)S(1)}, bf16[2,96,384]{2,1,0:T(8,128)(2,1)S(1)}, u32[]{:S(2)}, u32[]{:S(2)}) %collective-permute-start.17) | collective-permute-done | bytes 147488 | tf_op jit(solution)/shard_map/ppermute | solution.py:281
  81.3 1.3 %collective-permute-start.10 = (bf16[4,32,384]{2,1,0:T(8,128)(2,1)S(1)}, bf16[4,32,384]{2,1,0:T(8,128)(2,1)S(1)}, u32[]{:S(2)}, u32[]{:S(2)}) collective-permute-start(bf16[4,32,384]{2,1,0:T(8,128)(2,1)S(1)} %get-tuple-element.71), channel_id=1, source_target_pairs={{0,2},{1,3},{2,0},{3,1},{4,6},{5,7},{6,4},{7,5},{8,10},{9,11},{10,... | collective-permute-start | bytes 294920 | tf_op jit(solution)/shard_map/ppermute | solution.py:281
  82.6 0.9 collective-permute-start.11
  83.4 1.4 %collective-permute-start.12 = (bf16[4,32,384]{2,1,0:T(8,128)(2,1)S(1)}, bf16[4,32,384]{2,1,0:T(8,128)(2,1)S(1)}, u32[]{:S(2)}, u32[]{:S(2)}) collective-permute-start(bf16[4,32,384]{2,1,0:T(8,128)(2,1)S(1)} %get-tuple-element.73), channel_id=1, source_target_pairs={{0,6},{1,7},{2,4},{3,5},{4,2},{5,3},{6,0},{7,1},{8,14},{9,15},{10,... | collective-permute-start | bytes 294920 | tf_op jit(solution)/shard_map/ppermute | solution.py:370
  84.9 1.5 %collective-permute-done.10.refs_1_ = bf16[4,32,384]{2,1,0:T(8,128)(2,1)S(1)} collective-permute-done((bf16[4,32,384]{2,1,0:T(8,128)(2,1)S(1)}, bf16[4,32,384]{2,1,0:T(8,128)(2,1)S(1)}, u32[]{:S(2)}, u32[]{:S(2)}) %collective-permute-start.10) | collective-permute-done | bytes 98336 | tf_op jit(solution)/shard_map/ppermute | solution.py:281
  86.3 1.5 %collective-permute-done.11.refs_2_ = bf16[4,32,384]{2,1,0:T(8,128)(2,1)S(1)} collective-permute-done((bf16[4,32,384]{2,1,0:T(8,128)(2,1)S(1)}, bf16[4,32,384]{2,1,0:T(8,128)(2,1)S(1)}, u32[]{:S(2)}, u32[]{:S(2)}) %collective-permute-start.11) | collective-permute-done | bytes 98336 | tf_op jit(solution)/shard_map/ppermute | solution.py:281
  87.9 1.1 %collective-permute-done.12.refs_3_ = bf16[4,32,384]{2,1,0:T(8,128)(2,1)S(1)} collective-permute-done((bf16[4,32,384]{2,1,0:T(8,128)(2,1)S(1)}, bf16[4,32,384]{2,1,0:T(8,128)(2,1)S(1)}, u32[]{:S(2)}, u32[]{:S(2)}) %collective-permute-start.12) | collective-permute-done | bytes 98336 | tf_op jit(solution)/shard_map/ppermute | solution.py:370
  89.0 2.4 %collective-permute-start.19 = (bf16[1,96,384]{2,1,0:T(8,128)(2,1)S(1)}, bf16[1,96,384]{2,1,0:T(8,128)(2,1)S(1)}, u32[]{:S(2)}, u32[]{:S(2)}) collective-permute-start(bf16[1,96,384]{2,1,0:T(8,128)(2,1)S(1)} %fusion.11), channel_id=1, source_target_pairs={{0,16},{4,20},{8,24},{12,28},{16,0},{20,4},{24,8},{28,12},{1,17},{... | collective-permute-start | bytes 221192 | tf_op jit(solution)/shard_map/ppermute | solution.py:281
  91.4 0.7 add_bitcast_fusion.1
  92.1 1.9 %shard_map.71 = bf16[512,384]{1,0:T(8,128)(2,1)} custom-call(s32[2]{0:T(128)} %copy-done, bf16[4,32,384]{2,1,0:T(8,128)(2,1)} %get-tuple-element.76.refs_0_, bf16[4,32,384]{2,1,0:T(8,128)(2,1)} %copy-done.2, bf16[4,32,384]{2,1,0:T(8,128)(2,1)} %copy-done.3, bf16[4,32,384]{2,1,0:T(8,128)(2,1)} %copy-done.4), custom_call_target="tpu_custom_call" | custom-call | bytes 786432 | tf_op jit(solution)/shard_map/pallas_call | solution.py:376
  94.2 0.7 add_bitcast_fusion
  (50 shorter events, 4.6 us)
Async XLA Ops:
  0.6 7.6 %copy-start.1 = (bf16[512,384]{1,0:T(8,128)(2,1)S(1)}, bf16[512,384]{1,0:T(8,128)(2,1)}, u32[]{:S(2)}) copy-start(bf16[512,384]{1,0:T(8,128)(2,1)} %param.7) | copy-start | bytes 1179652
  0.6 21.7 %all-to-all-start = ((bf16[16,32,384]{2,1,0:T(8,128)(2,1)}), bf16[16,32,384]{2,1,0:T(8,128)(2,1)S(1)}, u32[]{:S(2)}, u32[]{:S(2)}) async-start(bf16[16,32,384]{2,1,0:T(8,128)(2,1)} %bitcast.98), calls=%async_computation | async-start | bytes 786432 | tf_op jit(solution)/shard_map/all_to_all | solution.py:40
  8.3 36.4 %copy-start = (s32[2]{0:T(128)}, s32[2]{0:T(128)S(1)}, u32[]{:S(2)}) copy-start(s32[2]{0:T(128)S(1)} %pad_add_fusion.place_ref) | copy-start | bytes 28
  8.3 1.5 %collective-permute-start = (bf16[2,2,2,1,32,384]{5,4,2,1,0,3:T(8,128)(2,1)S(1)}, bf16[2,2,2,1,32,384]{5,4,2,1,0,3:T(8,128)(2,1)S(1)}, u32[]{:S(2)}, u32[]{:S(2)}) collective-permute-start(bf16[2,2,2,1,32,384]{5,4,2,1,0,3:T(8,128)(2,1)S(1)} %get-tuple-element.109), channel_id=1, source_target_pairs={{0,1},{1,0},{2,3},{3,2},{4,5},{5,4},{6,7},{7,6},{8,9},{9,8},{10,11... | collective-permute-start | bytes 589832 | tf_op jit(solution)/shard_map/ppermute | solution.py:281
  9.9 6.8 %collective-permute-start.3 = (bf16[2,2,32,384]{3,2,1,0:T(8,128)(2,1)S(1)}, bf16[2,2,32,384]{3,2,1,0:T(8,128)(2,1)S(1)}, u32[]{:S(2)}, u32[]{:S(2)}) collective-permute-start(bf16[2,2,32,384]{3,2,1,0:T(8,128)(2,1)S(1)} %bitcast.103), channel_id=1, source_target_pairs={{0,6},{1,7},{2,4},{3,5},{4,2},{5,3},{6,0},{7,1},{8,14},{9,15},{10,... | collective-permute-start | bytes 294920 | tf_op jit(solution)/shard_map/ppermute | solution.py:370
  12.7 6.0 %collective-permute-start.2 = (bf16[2,2,32,384]{3,2,1,0:T(8,128)(2,1)S(1)}, bf16[2,2,32,384]{3,2,1,0:T(8,128)(2,1)S(1)}, u32[]{:S(2)}, u32[]{:S(2)}) collective-permute-start(bf16[2,2,32,384]{3,2,1,0:T(8,128)(2,1)S(1)} %bitcast.104), channel_id=1, source_target_pairs={{0,4},{4,0},{8,12},{12,8},{16,20},{20,16},{24,28},{28,24},{1,5},{5... | collective-permute-start | bytes 294920 | tf_op jit(solution)/shard_map/ppermute | solution.py:281
  13.4 5.4 %collective-permute-start.1 = (bf16[2,2,32,384]{3,2,1,0:T(8,128)(2,1)S(1)}, bf16[2,2,32,384]{3,2,1,0:T(8,128)(2,1)S(1)}, u32[]{:S(2)}, u32[]{:S(2)}) collective-permute-start(bf16[2,2,32,384]{3,2,1,0:T(8,128)(2,1)S(1)} %bitcast.105), channel_id=1, source_target_pairs={{0,2},{1,3},{2,0},{3,1},{4,6},{5,7},{6,4},{7,5},{8,10},{9,11},{10,... | collective-permute-start | bytes 294920 | tf_op jit(solution)/shard_map/ppermute | solution.py:281
  22.3 11.0 %collective-permute-start.4 = (bf16[8,32,384]{2,1,0:T(8,128)(2,1)S(1)}, bf16[8,32,384]{2,1,0:T(8,128)(2,1)S(1)}, u32[]{:S(2)}, u32[]{:S(2)}) collective-permute-start(bf16[8,32,384]{2,1,0:T(8,128)(2,1)S(1)} %get-tuple-element.54), channel_id=1, source_target_pairs={{0,16},{4,20},{8,24},{12,28},{16,0},{20,4},{24,8},{28,12},{1,17},{... | collective-permute-start | bytes 589832 | tf_op jit(solution)/shard_map/ppermute | solution.py:281
  33.4 11.1 %collective-permute-start.5 = (bf16[2,2,2,1,32,384]{5,4,2,1,0,3:T(8,128)(2,1)S(1)}, bf16[2,2,2,1,32,384]{5,4,2,1,0,3:T(8,128)(2,1)S(1)}, u32[]{:S(2)}, u32[]{:S(2)}) collective-permute-start(bf16[2,2,2,1,32,384]{5,4,2,1,0,3:T(8,128)(2,1)S(1)} %get-tuple-element.55), channel_id=1, source_target_pairs={{0,16},{4,20},{8,24},{12,28},{16,0},{20,4},{24,8},{28,12},{1,17},{... | collective-permute-start | bytes 589832 | tf_op jit(solution)/shard_map/ppermute | solution.py:281
  43.7 4.2 %collective-permute-start.14 = (bf16[16,96,384]{2,1,0:T(8,128)(2,1)S(1)}, bf16[16,96,384]{2,1,0:T(8,128)(2,1)S(1)}, u32[]{:S(2)}, u32[]{:S(2)}) collective-permute-start(bf16[16,96,384]{2,1,0:T(8,128)(2,1)S(1)} %get-tuple-element.81), channel_id=1, source_target_pairs={{0,1},{1,0},{2,3},{3,2},{4,5},{5,4},{6,7},{7,6},{8,9},{9,8},{10,11... | collective-permute-start | bytes 3538952 | tf_op jit(solution)/shard_map/ppermute | solution.py:281
  44.6 5.2 %collective-permute-start.7 = (bf16[16,96,384]{2,1,0:T(8,128)(2,1)S(1)}, bf16[16,96,384]{2,1,0:T(8,128)(2,1)S(1)}, u32[]{:S(2)}, u32[]{:S(2)}) collective-permute-start(bf16[16,96,384]{2,1,0:T(8,128)(2,1)S(1)} %get-tuple-element.68), channel_id=1, source_target_pairs={{0,1},{1,0},{2,3},{3,2},{4,5},{5,4},{6,7},{7,6},{8,9},{9,8},{10,11... | collective-permute-start | bytes 3538952 | tf_op jit(solution)/shard_map/ppermute | solution.py:281
  48.2 15.8 %collective-permute-start.15 = (bf16[8,96,384]{2,1,0:T(8,128)(2,1)S(1)}, bf16[8,96,384]{2,1,0:T(8,128)(2,1)S(1)}, u32[]{:S(2)}, u32[]{:S(2)}) collective-permute-start(bf16[8,96,384]{2,1,0:T(8,128)(2,1)S(1)} %get-tuple-element.84), channel_id=1, source_target_pairs={{0,2},{1,3},{2,0},{3,1},{4,6},{5,7},{6,4},{7,5},{8,10},{9,11},{10,... | collective-permute-start | bytes 1769480 | tf_op jit(solution)/shard_map/ppermute | solution.py:281
  50.1 15.6 %collective-permute-start.8 = (bf16[8,96,384]{2,1,0:T(8,128)(2,1)S(1)}, bf16[8,96,384]{2,1,0:T(8,128)(2,1)S(1)}, u32[]{:S(2)}, u32[]{:S(2)}) collective-permute-start(bf16[8,96,384]{2,1,0:T(8,128)(2,1)S(1)} %get-tuple-element.86), channel_id=1, source_target_pairs={{0,4},{4,0},{8,12},{12,8},{16,20},{20,16},{24,28},{28,24},{1,5},{5... | collective-permute-start | bytes 1769480 | tf_op jit(solution)/shard_map/ppermute | solution.py:281
  50.7 15.8 %collective-permute-start.6 = (bf16[2,2,2,32,384]{4,3,2,1,0:T(8,128)(2,1)S(1)}, bf16[2,2,2,32,384]{4,3,2,1,0:T(8,128)(2,1)S(1)}, u32[]{:S(2)}, u32[]{:S(2)}) collective-permute-start(bf16[2,2,2,32,384]{4,3,2,1,0:T(8,128)(2,1)S(1)} %bitcast.102), channel_id=1, source_target_pairs={{0,1},{1,0},{2,3},{3,2},{4,5},{5,4},{6,7},{7,6},{8,9},{9,8},{10,11... | collective-permute-start | bytes 589832 | tf_op jit(solution)/shard_map/ppermute | solution.py:281
  64.1 8.7 %collective-permute-start.16 = (bf16[4,96,384]{2,1,0:T(8,128)(2,1)S(1)}, bf16[4,96,384]{2,1,0:T(8,128)(2,1)S(1)}, u32[]{:S(2)}, u32[]{:S(2)}) collective-permute-start(bf16[4,96,384]{2,1,0:T(8,128)(2,1)S(1)} %get-tuple-element.88), channel_id=1, source_target_pairs={{0,4},{4,0},{8,12},{12,8},{16,20},{20,16},{24,28},{28,24},{1,5},{5... | collective-permute-start | bytes 884744 | tf_op jit(solution)/shard_map/ppermute | solution.py:281
  65.8 8.4 %collective-permute-start.9 = (bf16[4,96,384]{2,1,0:T(8,128)(2,1)S(1)}, bf16[4,96,384]{2,1,0:T(8,128)(2,1)S(1)}, u32[]{:S(2)}, u32[]{:S(2)}) collective-permute-start(bf16[4,96,384]{2,1,0:T(8,128)(2,1)S(1)} %get-tuple-element.90), channel_id=1, source_target_pairs={{0,2},{1,3},{2,0},{3,1},{4,6},{5,7},{6,4},{7,5},{8,10},{9,11},{10,... | collective-permute-start | bytes 884744 | tf_op jit(solution)/shard_map/ppermute | solution.py:281
  72.9 8.3 %collective-permute-start.17 = (bf16[2,96,384]{2,1,0:T(8,128)(2,1)S(1)}, bf16[2,96,384]{2,1,0:T(8,128)(2,1)S(1)}, u32[]{:S(2)}, u32[]{:S(2)}) collective-permute-start(bf16[2,96,384]{2,1,0:T(8,128)(2,1)S(1)} %get-tuple-element.92), channel_id=1, source_target_pairs={{0,16},{4,20},{8,24},{12,28},{16,0},{20,4},{24,8},{28,12},{1,17},{... | collective-permute-start | bytes 442376 | tf_op jit(solution)/shard_map/ppermute | solution.py:281
  74.3 10.5 %collective-permute-start.13 = (bf16[2,96,384]{2,1,0:T(8,128)(2,1)S(1)}, bf16[2,96,384]{2,1,0:T(8,128)(2,1)S(1)}, u32[]{:S(2)}, u32[]{:S(2)}) collective-permute-start(bf16[2,96,384]{2,1,0:T(8,128)(2,1)S(1)} %get-tuple-element.75), channel_id=1, source_target_pairs={{0,8},{4,12},{8,0},{12,4},{16,24},{20,28},{24,16},{28,20},{1,9},{5... | collective-permute-start | bytes 442376 | tf_op jit(solution)/shard_map/ppermute | solution.py:281
  81.2 10.2 %collective-permute-start.18 = (bf16[1,96,384]{2,1,0:T(8,128)(2,1)S(1)}, bf16[1,96,384]{2,1,0:T(8,128)(2,1)S(1)}, u32[]{:S(2)}, u32[]{:S(2)}) collective-permute-start(bf16[1,96,384]{2,1,0:T(8,128)(2,1)S(1)} %fusion.9), channel_id=1, source_target_pairs={{0,8},{4,12},{8,0},{12,4},{16,24},{20,28},{24,16},{28,20},{1,9},{5... | collective-permute-start | bytes 221192 | tf_op jit(solution)/shard_map/ppermute | solution.py:281
  81.3 5.1 %collective-permute-start.10 = (bf16[4,32,384]{2,1,0:T(8,128)(2,1)S(1)}, bf16[4,32,384]{2,1,0:T(8,128)(2,1)S(1)}, u32[]{:S(2)}, u32[]{:S(2)}) collective-permute-start(bf16[4,32,384]{2,1,0:T(8,128)(2,1)S(1)} %get-tuple-element.71), channel_id=1, source_target_pairs={{0,2},{1,3},{2,0},{3,1},{4,6},{5,7},{6,4},{7,5},{8,10},{9,11},{10,... | collective-permute-start | bytes 294920 | tf_op jit(solution)/shard_map/ppermute | solution.py:281
  82.6 5.3 %collective-permute-start.11 = (bf16[4,32,384]{2,1,0:T(8,128)(2,1)S(1)}, bf16[4,32,384]{2,1,0:T(8,128)(2,1)S(1)}, u32[]{:S(2)}, u32[]{:S(2)}) collective-permute-start(bf16[4,32,384]{2,1,0:T(8,128)(2,1)S(1)} %get-tuple-element.72), channel_id=1, source_target_pairs={{0,4},{4,0},{8,12},{12,8},{16,20},{20,16},{24,28},{28,24},{1,5},{5... | collective-permute-start | bytes 294920 | tf_op jit(solution)/shard_map/ppermute | solution.py:281
  83.4 5.5 %collective-permute-start.12 = (bf16[4,32,384]{2,1,0:T(8,128)(2,1)S(1)}, bf16[4,32,384]{2,1,0:T(8,128)(2,1)S(1)}, u32[]{:S(2)}, u32[]{:S(2)}) collective-permute-start(bf16[4,32,384]{2,1,0:T(8,128)(2,1)S(1)} %get-tuple-element.73), channel_id=1, source_target_pairs={{0,6},{1,7},{2,4},{3,5},{4,2},{5,3},{6,0},{7,1},{8,14},{9,15},{10,... | collective-permute-start | bytes 294920 | tf_op jit(solution)/shard_map/ppermute | solution.py:370
  86.3 5.7 %copy-start.2 = (bf16[4,32,384]{2,1,0:T(8,128)(2,1)}, bf16[4,32,384]{2,1,0:T(8,128)(2,1)S(1)}, u32[]{:S(2)}) copy-start(bf16[4,32,384]{2,1,0:T(8,128)(2,1)S(1)} %collective-permute-done.10.refs_1_) | copy-start | bytes 294916
  87.9 4.2 %copy-start.3 = (bf16[4,32,384]{2,1,0:T(8,128)(2,1)}, bf16[4,32,384]{2,1,0:T(8,128)(2,1)S(1)}, u32[]{:S(2)}) copy-start(bf16[4,32,384]{2,1,0:T(8,128)(2,1)S(1)} %collective-permute-done.11.refs_2_) | copy-start | bytes 294916
  89.0 3.1 %copy-start.4 = (bf16[4,32,384]{2,1,0:T(8,128)(2,1)}, bf16[4,32,384]{2,1,0:T(8,128)(2,1)S(1)}, u32[]{:S(2)}) copy-start(bf16[4,32,384]{2,1,0:T(8,128)(2,1)S(1)} %collective-permute-done.12.refs_3_) | copy-start | bytes 294916
  89.0 5.3 %collective-permute-start.19 = (bf16[1,96,384]{2,1,0:T(8,128)(2,1)S(1)}, bf16[1,96,384]{2,1,0:T(8,128)(2,1)S(1)}, u32[]{:S(2)}, u32[]{:S(2)}) collective-permute-start(bf16[1,96,384]{2,1,0:T(8,128)(2,1)S(1)} %fusion.11), channel_id=1, source_target_pairs={{0,16},{4,20},{8,24},{12,28},{16,0},{20,4},{24,8},{28,12},{1,17},{... | collective-permute-start | bytes 221192 | tf_op jit(solution)/shard_map/ppermute | solution.py:281

commit v14 on v13

--- a/solution.py
+++ b/solution.py
@@ -427,11 +427,12 @@
         grad_down = scatter_narrow(halves, grad_t, hidden, [steps[core]] + order_down, span_x, span_y)
         grad_up = scatter_narrow(halves, normed_t, d_pre, [steps[core]] + order_up, span_x, span_y)
         return (mixed_out, grad_up, grad_down)
-    given[0] = going.hop(core, steps, halves, given[0])
     take_down, take_up = [swap(part, *steps[core]) for part in given]
     keep_down, keep_up = keep_blocks(place, hidden, d_pre, normed_t, grad_t, places, block)
 
     def beside(phase, give):
+        if phase == 1:
+            return going.hop(core, steps, halves, give)
         if phase == 2:
             return going.hop_both(x, y, steps, halves, give)
         if phase == len(order_down) - 1:

time: 95.2 us -> 88.9 us (0.934)
  waiting for transfers between devices: 39.1 us -> 34.8 us
  starting transfers between devices: 25.6 us -> 23.6 us
    ppermute x18, waiting for transfers between devices: 33.7 us -> 29.8 us  [swap(): return lax.ppermute(block, axis, pairs)]
    ppermute x18, starting transfers between devices: 14 us -> 11.9 us  [swap(): return lax.ppermute(block, axis, pairs)]
  transfers between devices with their start and end apart: 21 -> 21, of which waited for: 14 -> 13; matrix products, arithmetic and copies ran while one was open for 3% -> 3% of each run, Pallas kernels for 27% -> 18%
where the time goes in v14:
time: 88.9 us; the launch traced here: 88.6 us
  waiting for transfers between devices  34.8 us (39%)
  Pallas kernels  25.5 us (29%)
  starting transfers between devices  23.6 us (27%)
  other arithmetic  3.52 us (4%)
  between operations  0.98 us (1%)
    ppermute x18, waiting for transfers between devices, swap(): return lax.ppermute(block, axis, pairs)  29.8 us
    ppermute x18, starting transfers between devices, swap(): return lax.ppermute(block, axis, pairs)  11.9 us
    pallas_call x1, Pallas kernels, backward(): pl.pallas_call(functools.partial(backward_kernel, *places), out_shape=out...  9.44 us
    pallas_call x1, Pallas kernels, forward(): pl.pallas_call(forward_kernel, out_shape=outs, in_specs=[spec(pltpu.VMEM)...  8.72 us
    all_to_all x1, starting transfers between devices, exchange(): lax.all_to_all(block, ('gx', 'gy'), split_axis=0, concat_axis=0, axis_ind...  7.44 us
    ppermute x2, starting transfers between devices, swap_both(): return lax.ppermute(block, ('gx', 'gy'), pairs)  4.21 us
    all_to_all x1, waiting for transfers between devices, exchange(): lax.all_to_all(block, ('gx', 'gy'), split_axis=0, concat_axis=0, axis_ind...  3.45 us
    pallas_call x1, Pallas kernels, keep_blocks(): pl.pallas_call(functools.partial(keep_kernel, *places), out_shape=[block]...  3.17 us
  transfers between devices with their start and end apart: 21, of which 13 were waited for; matrix products, arithmetic and copies ran while one was open for 3% of the time, Pallas kernels for 18%

profile of v14, /device:TPU:0, one launch (start us, length us, event | category | flops | bytes accessed | tf_op | source)
XLA Modules:
  0.0 88.6 jit_solution(1993775976388519310)
XLA Ops:
  0.6 7.4 %all-to-all-start = ((bf16[16,32,384]{2,1,0:T(8,128)(2,1)}), bf16[16,32,384]{2,1,0:T(8,128)(2,1)S(1)}, u32[]{:S(2)}, u32[]{:S(2)}) async-start(bf16[16,32,384]{2,1,0:T(8,128)(2,1)} %bitcast.98), calls=%async_computation | async-start | bytes 786432 | tf_op jit(solution)/shard_map/all_to_all | solution.py:40
  8.7 1.1 %collective-permute-done = bf16[2,2,2,1,32,384]{5,4,2,1,0,3:T(8,128)(2,1)S(1)} collective-permute-done((bf16[2,2,2,1,32,384]{5,4,2,1,0,3:T(8,128)(2,1)S(1)}, bf16[2,2,2,1,32,384]{5,4,2,1,0,3:T(8,128)(2,1)S(1)}, u32[]{:S(2)}, u32[]{:S(2)}) %collective-permute-start) | collective-permute-done | bytes 196640 | tf_op jit(solution)/shard_map/ppermute | solution.py:281
  9.9 2.8 %collective-permute-start.3 = (bf16[2,2,32,384]{3,2,1,0:T(8,128)(2,1)S(1)}, bf16[2,2,32,384]{3,2,1,0:T(8,128)(2,1)S(1)}, u32[]{:S(2)}, u32[]{:S(2)}) collective-permute-start(bf16[2,2,32,384]{3,2,1,0:T(8,128)(2,1)S(1)} %bitcast.103), channel_id=1, source_target_pairs={{0,6},{1,7},{2,4},{3,5},{4,2},{5,3},{6,0},{7,1},{8,14},{9,15},{10,... | collective-permute-start | bytes 294920 | tf_op jit(solution)/shard_map/ppermute | solution.py:370
  13.6 2.2 %shard_map.67.up_ref = bf16[768,1536]{1,0:T(8,128)(2,1)S(1)} custom-call(s32[2]{0:T(128)S(1)} %pad_add_fusion.place_ref, bf16[768,1536]{1,0:T(8,128)(2,1)} %source.1), custom_call_target="tpu_custom_call" | custom-call | bytes 4718592 | tf_op jit(solution)/shard_map/pallas_call | solution.py:207
  15.9 0.9 collective-permute-done.3
  16.7 2.0 %collective-permute-done.2 = bf16[2,2,32,384]{3,2,1,0:T(8,128)(2,1)S(1)} collective-permute-done((bf16[2,2,32,384]{3,2,1,0:T(8,128)(2,1)S(1)}, bf16[2,2,32,384]{3,2,1,0:T(8,128)(2,1)S(1)}, u32[]{:S(2)}, u32[]{:S(2)}) %collective-permute-start.2) | collective-permute-done | bytes 98336 | tf_op jit(solution)/shard_map/ppermute | solution.py:281
  18.9 3.5 %all-to-all-done.state_ref = bf16[16,32,384]{2,1,0:T(8,128)(2,1)S(1)} async-done(((bf16[16,32,384]{2,1,0:T(8,128)(2,1)}), bf16[16,32,384]{2,1,0:T(8,128)(2,1)S(1)}, u32[]{:S(2)}, u32[]{:S(2)}) %all-to-all-start) | async-done | bytes 393248 | tf_op jit(solution)/shard_map/all_to_all | solution.py:40
  22.6 8.7 %shard_map.68 = (bf16[16,32,384]{2,1,0:T(8,128)(2,1)S(1)}, bf16[1024,1536]{1,0:T(8,128)(2,1)S(1)}, bf16[1024,1536]{1,0:T(8,128)(2,1)S(1)}, bf16[1024,768]{1,0:T(...) custom-call(bf16[16,32,384]{2,1,0:T(8,128)(2,1)S(1)} %all-to-all-done.state_r, ...), custom_call_target="tpu_custom_call" | custom-call | flops 12079595520 | bytes 25165824 | tf_op jit(solution)/shard_map/pallas_call | solution.py:232
  31.4 2.0 %collective-permute-done.4 = bf16[8,32,384]{2,1,0:T(8,128)(2,1)S(1)} collective-permute-done((bf16[8,32,384]{2,1,0:T(8,128)(2,1)S(1)}, bf16[8,32,384]{2,1,0:T(8,128)(2,1)S(1)}, u32[]{:S(2)}, u32[]{:S(2)}) %collective-permute-start.4) | collective-permute-done | bytes 196640 | tf_op jit(solution)/shard_map/ppermute | solution.py:281
  33.4 9.4 %shard_map.69 = (bf16[1024,1536]{1,0:T(8,128)(2,1)S(1)}, bf16[768,1024]{1,0:T(8,128)(2,1)S(1)}, bf16[16,96,384]{2,1,0:T(8,128)(2,1)S(1)}, bf16[16,96,384]{2,1,0:T(8,128)(2,1)S(1)}) custom-call(s32[2]{0:T(128)S(1)} %pad_add_fusion.place_ref, bf16[16,32,384]{2,1,0:T(8,128)(2,1)S(1)} %pad_maximum_fusion.1.grad_ref, ...), custom_call_target="tpu_custom_call" | custom-call | flops 12079595520 | bytes 25165824 | tf_op jit(solution)/shard_map/pallas_call | solution.py:251
  43.4 3.2 %shard_map.70 = (bf16[16,96,384]{2,1,0:T(8,128)(2,1)S(1)}, bf16[16,96,384]{2,1,0:T(8,128)(2,1)S(1)}) custom-call(s32[2]{0:T(128)S(1)} %pad_add_fusion.place_ref, bf16[1024,1536]{1,0:T(8,128)(2,1)S(1)} %get-tuple-element.56.hidden_ref, bf16[1024,1536]{1,0:T(8,128)(2,1)S(1)} %get-tuple-element.63.d_pre_ref, ...), custom_call_target="tpu_custom_call" | custom-call | flops 2415919104 | bytes 12582912 | tf_op jit(solution)/shard_map/pallas_call | solution.py:267
  46.9 1.1 %collective-permute-start.7 = (bf16[8,96,384]{2,1,0:T(8,128)(2,1)S(1)}, bf16[8,96,384]{2,1,0:T(8,128)(2,1)S(1)}, u32[]{:S(2)}, u32[]{:S(2)}) collective-permute-start(bf16[8,96,384]{2,1,0:T(8,128)(2,1)S(1)} %get-tuple-element.86), channel_id=1, source_target_pairs={{0,4},{4,0},{8,12},{12,8},{16,20},{20,16},{24,28},{28,24},{1,5},{5... | collective-permute-start | bytes 1769480 | tf_op jit(solution)/shard_map/ppermute | solution.py:281
  48.4 1.2 %collective-permute-start.15 = (bf16[8,96,384]{2,1,0:T(8,128)(2,1)S(1)}, bf16[8,96,384]{2,1,0:T(8,128)(2,1)S(1)}, u32[]{:S(2)}, u32[]{:S(2)}) collective-permute-start(bf16[8,96,384]{2,1,0:T(8,128)(2,1)S(1)} %get-tuple-element.84), channel_id=1, source_target_pairs={{0,2},{1,3},{2,0},{3,1},{4,6},{5,7},{6,4},{7,5},{8,10},{9,11},{10,... | collective-permute-start | bytes 1769480 | tf_op jit(solution)/shard_map/ppermute | solution.py:281
  49.5 11.0 %collective-permute-done.5 = bf16[2,2,2,1,32,384]{5,4,2,1,0,3:T(8,128)(2,1)S(1)} collective-permute-done((bf16[2,2,2,1,32,384]{5,4,2,1,0,3:T(8,128)(2,1)S(1)}, bf16[2,2,2,1,32,384]{5,4,2,1,0,3:T(8,128)(2,1)S(1)}, u32[]{:S(2)}, u32[]{:S(2)}) %collective-permute-start.5) | collective-permute-done | bytes 196640 | tf_op jit(solution)/shard_map/ppermute | solution.py:281
  60.6 1.7 %collective-permute-done.7 = bf16[8,96,384]{2,1,0:T(8,128)(2,1)S(1)} collective-permute-done((bf16[8,96,384]{2,1,0:T(8,128)(2,1)S(1)}, bf16[8,96,384]{2,1,0:T(8,128)(2,1)S(1)}, u32[]{:S(2)}, u32[]{:S(2)}) %collective-permute-start.7) | collective-permute-done | bytes 589856 | tf_op jit(solution)/shard_map/ppermute | solution.py:281
  62.6 0.9 %collective-permute-done.15 = bf16[8,96,384]{2,1,0:T(8,128)(2,1)S(1)} collective-permute-done((bf16[8,96,384]{2,1,0:T(8,128)(2,1)S(1)}, bf16[8,96,384]{2,1,0:T(8,128)(2,1)S(1)}, u32[]{:S(2)}, u32[]{:S(2)}) %collective-permute-start.15) | collective-permute-done | bytes 589856 | tf_op jit(solution)/shard_map/ppermute | solution.py:281
  63.6 1.1 %collective-permute-start.16 = (bf16[4,96,384]{2,1,0:T(8,128)(2,1)S(1)}, bf16[4,96,384]{2,1,0:T(8,128)(2,1)S(1)}, u32[]{:S(2)}, u32[]{:S(2)}) collective-permute-start(bf16[4,96,384]{2,1,0:T(8,128)(2,1)S(1)} %get-tuple-element.88), channel_id=1, source_target_pairs={{0,4},{4,0},{8,12},{12,8},{16,20},{20,16},{24,28},{28,24},{1,5},{5... | collective-permute-start | bytes 884744 | tf_op jit(solution)/shard_map/ppermute | solution.py:281
  64.7 0.9 collective-permute-start.9
  65.6 0.7 fusion.13
  66.3 5.9 %collective-permute-done.16 = bf16[4,96,384]{2,1,0:T(8,128)(2,1)S(1)} collective-permute-done((bf16[4,96,384]{2,1,0:T(8,128)(2,1)S(1)}, bf16[4,96,384]{2,1,0:T(8,128)(2,1)S(1)}, u32[]{:S(2)}, u32[]{:S(2)}) %collective-permute-start.16) | collective-permute-done | bytes 294944 | tf_op jit(solution)/shard_map/ppermute | solution.py:281
  72.3 0.8 collective-permute-start.17
  73.2 1.6 %collective-permute-start.13 = (bf16[2,96,384]{2,1,0:T(8,128)(2,1)S(1)}, bf16[2,96,384]{2,1,0:T(8,128)(2,1)S(1)}, u32[]{:S(2)}, u32[]{:S(2)}) collective-permute-start(bf16[2,96,384]{2,1,0:T(8,128)(2,1)S(1)} %get-tuple-element.75), channel_id=1, source_target_pairs={{0,8},{4,12},{8,0},{12,4},{16,24},{20,28},{24,16},{28,20},{1,9},{5... | collective-permute-start | bytes 442376 | tf_op jit(solution)/shard_map/ppermute | solution.py:281
  74.8 1.5 %collective-permute-start.10 = (bf16[4,32,384]{2,1,0:T(8,128)(2,1)S(1)}, bf16[4,32,384]{2,1,0:T(8,128)(2,1)S(1)}, u32[]{:S(2)}, u32[]{:S(2)}) collective-permute-start(bf16[4,32,384]{2,1,0:T(8,128)(2,1)S(1)} %get-tuple-element.71), channel_id=1, source_target_pairs={{0,2},{1,3},{2,0},{3,1},{4,6},{5,7},{6,4},{7,5},{8,10},{9,11},{10,... | collective-permute-start | bytes 294920 | tf_op jit(solution)/shard_map/ppermute | solution.py:281
  76.8 1.4 %collective-permute-start.12 = (bf16[4,32,384]{2,1,0:T(8,128)(2,1)S(1)}, bf16[4,32,384]{2,1,0:T(8,128)(2,1)S(1)}, u32[]{:S(2)}, u32[]{:S(2)}) collective-permute-start(bf16[4,32,384]{2,1,0:T(8,128)(2,1)S(1)} %get-tuple-element.73), channel_id=1, source_target_pairs={{0,6},{1,7},{2,4},{3,5},{4,2},{5,3},{6,0},{7,1},{8,14},{9,15},{10,... | collective-permute-start | bytes 294920 | tf_op jit(solution)/shard_map/ppermute | solution.py:370
  78.3 1.5 %collective-permute-done.17 = bf16[2,96,384]{2,1,0:T(8,128)(2,1)S(1)} collective-permute-done((bf16[2,96,384]{2,1,0:T(8,128)(2,1)S(1)}, bf16[2,96,384]{2,1,0:T(8,128)(2,1)S(1)}, u32[]{:S(2)}, u32[]{:S(2)}) %collective-permute-start.17) | collective-permute-done | bytes 147488 | tf_op jit(solution)/shard_map/ppermute | solution.py:281
  79.9 1.7 %collective-permute-done.13 = bf16[2,96,384]{2,1,0:T(8,128)(2,1)S(1)} collective-permute-done((bf16[2,96,384]{2,1,0:T(8,128)(2,1)S(1)}, bf16[2,96,384]{2,1,0:T(8,128)(2,1)S(1)}, u32[]{:S(2)}, u32[]{:S(2)}) %collective-permute-start.13) | collective-permute-done | bytes 147488 | tf_op jit(solution)/shard_map/ppermute | solution.py:281
  81.7 0.7 collective-permute-done.12.refs_3_
  82.4 1.0 %collective-permute-start.19 = (bf16[1,96,384]{2,1,0:T(8,128)(2,1)S(1)}, bf16[1,96,384]{2,1,0:T(8,128)(2,1)S(1)}, u32[]{:S(2)}, u32[]{:S(2)}) collective-permute-start(bf16[1,96,384]{2,1,0:T(8,128)(2,1)S(1)} %fusion.11), channel_id=1, source_target_pairs={{0,16},{4,20},{8,24},{12,28},{16,0},{20,4},{24,8},{28,12},{1,17},{... | collective-permute-start | bytes 221192 | tf_op jit(solution)/shard_map/ppermute | solution.py:281
  83.4 1.9 %shard_map.71 = bf16[512,384]{1,0:T(8,128)(2,1)} custom-call(s32[2]{0:T(128)} %copy-done, bf16[4,32,384]{2,1,0:T(8,128)(2,1)} %get-tuple-element.76.refs_0_, bf16[4,32,384]{2,1,0:T(8,128)(2,1)} %copy-done.2, bf16[4,32,384]{2,1,0:T(8,128)(2,1)} %copy-done.3, bf16[4,32,384]{2,1,0:T(8,128)(2,1)} %copy-done.4), custom_call_target="tpu_custom_call" | custom-call | bytes 786432 | tf_op jit(solution)/shard_map/pallas_call | solution.py:376
  85.3 0.7 add_bitcast_fusion.1
  86.0 1.9 %collective-permute-done.19 = bf16[1,96,384]{2,1,0:T(8,128)(2,1)S(1)} collective-permute-done((bf16[1,96,384]{2,1,0:T(8,128)(2,1)S(1)}, bf16[1,96,384]{2,1,0:T(8,128)(2,1)S(1)}, u32[]{:S(2)}, u32[]{:S(2)}) %collective-permute-start.19) | collective-permute-done | bytes 73760 | tf_op jit(solution)/shard_map/ppermute | solution.py:281
  87.9 0.7 add_bitcast_fusion
  (50 shorter events, 4.5 us)
Async XLA Ops:
  0.6 7.6 %copy-start.1 = (bf16[512,384]{1,0:T(8,128)(2,1)S(1)}, bf16[512,384]{1,0:T(8,128)(2,1)}, u32[]{:S(2)}) copy-start(bf16[512,384]{1,0:T(8,128)(2,1)} %param.7) | copy-start | bytes 1179652
  0.6 21.7 %all-to-all-start = ((bf16[16,32,384]{2,1,0:T(8,128)(2,1)}), bf16[16,32,384]{2,1,0:T(8,128)(2,1)S(1)}, u32[]{:S(2)}, u32[]{:S(2)}) async-start(bf16[16,32,384]{2,1,0:T(8,128)(2,1)} %bitcast.98), calls=%async_computation | async-start | bytes 786432 | tf_op jit(solution)/shard_map/all_to_all | solution.py:40
  8.3 35.2 %copy-start = (s32[2]{0:T(128)}, s32[2]{0:T(128)S(1)}, u32[]{:S(2)}) copy-start(s32[2]{0:T(128)S(1)} %pad_add_fusion.place_ref) | copy-start | bytes 28
  8.3 1.5 %collective-permute-start = (bf16[2,2,2,1,32,384]{5,4,2,1,0,3:T(8,128)(2,1)S(1)}, bf16[2,2,2,1,32,384]{5,4,2,1,0,3:T(8,128)(2,1)S(1)}, u32[]{:S(2)}, u32[]{:S(2)}) collective-permute-start(bf16[2,2,2,1,32,384]{5,4,2,1,0,3:T(8,128)(2,1)S(1)} %get-tuple-element.109), channel_id=1, source_target_pairs={{0,1},{1,0},{2,3},{3,2},{4,5},{5,4},{6,7},{7,6},{8,9},{9,8},{10,11... | collective-permute-start | bytes 589832 | tf_op jit(solution)/shard_map/ppermute | solution.py:281
  9.9 6.8 %collective-permute-start.3 = (bf16[2,2,32,384]{3,2,1,0:T(8,128)(2,1)S(1)}, bf16[2,2,32,384]{3,2,1,0:T(8,128)(2,1)S(1)}, u32[]{:S(2)}, u32[]{:S(2)}) collective-permute-start(bf16[2,2,32,384]{3,2,1,0:T(8,128)(2,1)S(1)} %bitcast.103), channel_id=1, source_target_pairs={{0,6},{1,7},{2,4},{3,5},{4,2},{5,3},{6,0},{7,1},{8,14},{9,15},{10,... | collective-permute-start | bytes 294920 | tf_op jit(solution)/shard_map/ppermute | solution.py:370
  12.7 6.0 %collective-permute-start.2 = (bf16[2,2,32,384]{3,2,1,0:T(8,128)(2,1)S(1)}, bf16[2,2,32,384]{3,2,1,0:T(8,128)(2,1)S(1)}, u32[]{:S(2)}, u32[]{:S(2)}) collective-permute-start(bf16[2,2,32,384]{3,2,1,0:T(8,128)(2,1)S(1)} %bitcast.104), channel_id=1, source_target_pairs={{0,4},{4,0},{8,12},{12,8},{16,20},{20,16},{24,28},{28,24},{1,5},{5... | collective-permute-start | bytes 294920 | tf_op jit(solution)/shard_map/ppermute | solution.py:281
  13.4 5.4 %collective-permute-start.1 = (bf16[2,2,32,384]{3,2,1,0:T(8,128)(2,1)S(1)}, bf16[2,2,32,384]{3,2,1,0:T(8,128)(2,1)S(1)}, u32[]{:S(2)}, u32[]{:S(2)}) collective-permute-start(bf16[2,2,32,384]{3,2,1,0:T(8,128)(2,1)S(1)} %bitcast.105), channel_id=1, source_target_pairs={{0,2},{1,3},{2,0},{3,1},{4,6},{5,7},{6,4},{7,5},{8,10},{9,11},{10,... | collective-permute-start | bytes 294920 | tf_op jit(solution)/shard_map/ppermute | solution.py:281
  22.3 11.0 %collective-permute-start.4 = (bf16[8,32,384]{2,1,0:T(8,128)(2,1)S(1)}, bf16[8,32,384]{2,1,0:T(8,128)(2,1)S(1)}, u32[]{:S(2)}, u32[]{:S(2)}) collective-permute-start(bf16[8,32,384]{2,1,0:T(8,128)(2,1)S(1)} %get-tuple-element.54), channel_id=1, source_target_pairs={{0,16},{4,20},{8,24},{12,28},{16,0},{20,4},{24,8},{28,12},{1,17},{... | collective-permute-start | bytes 589832 | tf_op jit(solution)/shard_map/ppermute | solution.py:281
  42.8 3.8 %collective-permute-start.6 = (bf16[16,96,384]{2,1,0:T(8,128)(2,1)S(1)}, bf16[16,96,384]{2,1,0:T(8,128)(2,1)S(1)}, u32[]{:S(2)}, u32[]{:S(2)}) collective-permute-start(bf16[16,96,384]{2,1,0:T(8,128)(2,1)S(1)} %get-tuple-element.66), channel_id=1, source_target_pairs={{0,1},{1,0},{2,3},{3,2},{4,5},{5,4},{6,7},{7,6},{8,9},{9,8},{10,11... | collective-permute-start | bytes 3538952 | tf_op jit(solution)/shard_map/ppermute | solution.py:281
  42.9 5.1 %collective-permute-start.14 = (bf16[16,96,384]{2,1,0:T(8,128)(2,1)S(1)}, bf16[16,96,384]{2,1,0:T(8,128)(2,1)S(1)}, u32[]{:S(2)}, u32[]{:S(2)}) collective-permute-start(bf16[16,96,384]{2,1,0:T(8,128)(2,1)S(1)} %get-tuple-element.81), channel_id=1, source_target_pairs={{0,1},{1,0},{2,3},{3,2},{4,5},{5,4},{6,7},{7,6},{8,9},{9,8},{10,11... | collective-permute-start | bytes 3538952 | tf_op jit(solution)/shard_map/ppermute | solution.py:281
  46.9 15.4 %collective-permute-start.7 = (bf16[8,96,384]{2,1,0:T(8,128)(2,1)S(1)}, bf16[8,96,384]{2,1,0:T(8,128)(2,1)S(1)}, u32[]{:S(2)}, u32[]{:S(2)}) collective-permute-start(bf16[8,96,384]{2,1,0:T(8,128)(2,1)S(1)} %get-tuple-element.86), channel_id=1, source_target_pairs={{0,4},{4,0},{8,12},{12,8},{16,20},{20,16},{24,28},{28,24},{1,5},{5... | collective-permute-start | bytes 1769480 | tf_op jit(solution)/shard_map/ppermute | solution.py:281
  48.4 15.1 %collective-permute-start.15 = (bf16[8,96,384]{2,1,0:T(8,128)(2,1)S(1)}, bf16[8,96,384]{2,1,0:T(8,128)(2,1)S(1)}, u32[]{:S(2)}, u32[]{:S(2)}) collective-permute-start(bf16[8,96,384]{2,1,0:T(8,128)(2,1)S(1)} %get-tuple-element.84), channel_id=1, source_target_pairs={{0,2},{1,3},{2,0},{3,1},{4,6},{5,7},{6,4},{7,5},{8,10},{9,11},{10,... | collective-permute-start | bytes 1769480 | tf_op jit(solution)/shard_map/ppermute | solution.py:281
  49.5 11.0 %collective-permute-start.5 = (bf16[2,2,2,1,32,384]{5,4,2,1,0,3:T(8,128)(2,1)S(1)}, bf16[2,2,2,1,32,384]{5,4,2,1,0,3:T(8,128)(2,1)S(1)}, u32[]{:S(2)}, u32[]{:S(2)}) collective-permute-start(bf16[2,2,2,1,32,384]{5,4,2,1,0,3:T(8,128)(2,1)S(1)} %get-tuple-element.55), channel_id=1, source_target_pairs={{0,16},{4,20},{8,24},{12,28},{16,0},{20,4},{24,8},{28,12},{1,17},{... | collective-permute-start | bytes 589832 | tf_op jit(solution)/shard_map/ppermute | solution.py:281
  62.5 3.1 %collective-permute-start.8 = (bf16[2,2,2,32,384]{4,3,2,1,0:T(8,128)(2,1)S(1)}, bf16[2,2,2,32,384]{4,3,2,1,0:T(8,128)(2,1)S(1)}, u32[]{:S(2)}, u32[]{:S(2)}) collective-permute-start(bf16[2,2,2,32,384]{4,3,2,1,0:T(8,128)(2,1)S(1)} %bitcast.102), channel_id=1, source_target_pairs={{0,1},{1,0},{2,3},{3,2},{4,5},{5,4},{6,7},{7,6},{8,9},{9,8},{10,11... | collective-permute-start | bytes 589832 | tf_op jit(solution)/shard_map/ppermute | solution.py:281
  63.6 8.6 %collective-permute-start.16 = (bf16[4,96,384]{2,1,0:T(8,128)(2,1)S(1)}, bf16[4,96,384]{2,1,0:T(8,128)(2,1)S(1)}, u32[]{:S(2)}, u32[]{:S(2)}) collective-permute-start(bf16[4,96,384]{2,1,0:T(8,128)(2,1)S(1)} %get-tuple-element.88), channel_id=1, source_target_pairs={{0,4},{4,0},{8,12},{12,8},{16,20},{20,16},{24,28},{28,24},{1,5},{5... | collective-permute-start | bytes 884744 | tf_op jit(solution)/shard_map/ppermute | solution.py:281
  64.7 8.4 %collective-permute-start.9 = (bf16[4,96,384]{2,1,0:T(8,128)(2,1)S(1)}, bf16[4,96,384]{2,1,0:T(8,128)(2,1)S(1)}, u32[]{:S(2)}, u32[]{:S(2)}) collective-permute-start(bf16[4,96,384]{2,1,0:T(8,128)(2,1)S(1)} %get-tuple-element.69), channel_id=1, source_target_pairs={{0,2},{1,3},{2,0},{3,1},{4,6},{5,7},{6,4},{7,5},{8,10},{9,11},{10,... | collective-permute-start | bytes 884744 | tf_op jit(solution)/shard_map/ppermute | solution.py:281
  72.3 7.5 %collective-permute-start.17 = (bf16[2,96,384]{2,1,0:T(8,128)(2,1)S(1)}, bf16[2,96,384]{2,1,0:T(8,128)(2,1)S(1)}, u32[]{:S(2)}, u32[]{:S(2)}) collective-permute-start(bf16[2,96,384]{2,1,0:T(8,128)(2,1)S(1)} %get-tuple-element.92), channel_id=1, source_target_pairs={{0,16},{4,20},{8,24},{12,28},{16,0},{20,4},{24,8},{28,12},{1,17},{... | collective-permute-start | bytes 442376 | tf_op jit(solution)/shard_map/ppermute | solution.py:281
  73.2 8.5 %collective-permute-start.13 = (bf16[2,96,384]{2,1,0:T(8,128)(2,1)S(1)}, bf16[2,96,384]{2,1,0:T(8,128)(2,1)S(1)}, u32[]{:S(2)}, u32[]{:S(2)}) collective-permute-start(bf16[2,96,384]{2,1,0:T(8,128)(2,1)S(1)} %get-tuple-element.75), channel_id=1, source_target_pairs={{0,8},{4,12},{8,0},{12,4},{16,24},{20,28},{24,16},{28,20},{1,9},{5... | collective-permute-start | bytes 442376 | tf_op jit(solution)/shard_map/ppermute | solution.py:281
  74.8 6.9 %collective-permute-start.10 = (bf16[4,32,384]{2,1,0:T(8,128)(2,1)S(1)}, bf16[4,32,384]{2,1,0:T(8,128)(2,1)S(1)}, u32[]{:S(2)}, u32[]{:S(2)}) collective-permute-start(bf16[4,32,384]{2,1,0:T(8,128)(2,1)S(1)} %get-tuple-element.71), channel_id=1, source_target_pairs={{0,2},{1,3},{2,0},{3,1},{4,6},{5,7},{6,4},{7,5},{8,10},{9,11},{10,... | collective-permute-start | bytes 294920 | tf_op jit(solution)/shard_map/ppermute | solution.py:281
  76.3 5.4 %collective-permute-start.11 = (bf16[4,32,384]{2,1,0:T(8,128)(2,1)S(1)}, bf16[4,32,384]{2,1,0:T(8,128)(2,1)S(1)}, u32[]{:S(2)}, u32[]{:S(2)}) collective-permute-start(bf16[4,32,384]{2,1,0:T(8,128)(2,1)S(1)} %get-tuple-element.72), channel_id=1, source_target_pairs={{0,4},{4,0},{8,12},{12,8},{16,20},{20,16},{24,28},{28,24},{1,5},{5... | collective-permute-start | bytes 294920 | tf_op jit(solution)/shard_map/ppermute | solution.py:281
  76.8 5.5 %collective-permute-start.12 = (bf16[4,32,384]{2,1,0:T(8,128)(2,1)S(1)}, bf16[4,32,384]{2,1,0:T(8,128)(2,1)S(1)}, u32[]{:S(2)}, u32[]{:S(2)}) collective-permute-start(bf16[4,32,384]{2,1,0:T(8,128)(2,1)S(1)} %get-tuple-element.73), channel_id=1, source_target_pairs={{0,6},{1,7},{2,4},{3,5},{4,2},{5,3},{6,0},{7,1},{8,14},{9,15},{10,... | collective-permute-start | bytes 294920 | tf_op jit(solution)/shard_map/ppermute | solution.py:370
  79.8 5.5 %collective-permute-start.18 = (bf16[1,96,384]{2,1,0:T(8,128)(2,1)S(1)}, bf16[1,96,384]{2,1,0:T(8,128)(2,1)S(1)}, u32[]{:S(2)}, u32[]{:S(2)}) collective-permute-start(bf16[1,96,384]{2,1,0:T(8,128)(2,1)S(1)} %fusion.9), channel_id=1, source_target_pairs={{0,8},{4,12},{8,0},{12,4},{16,24},{20,28},{24,16},{28,20},{1,9},{5... | collective-permute-start | bytes 221192 | tf_op jit(solution)/shard_map/ppermute | solution.py:281
  81.7 1.7 %copy-start.2 = (bf16[4,32,384]{2,1,0:T(8,128)(2,1)}, bf16[4,32,384]{2,1,0:T(8,128)(2,1)S(1)}, u32[]{:S(2)}) copy-start(bf16[4,32,384]{2,1,0:T(8,128)(2,1)S(1)} %collective-permute-done.10.refs_1_) | copy-start | bytes 294916
  81.7 1.7 %copy-start.3 = (bf16[4,32,384]{2,1,0:T(8,128)(2,1)}, bf16[4,32,384]{2,1,0:T(8,128)(2,1)S(1)}, u32[]{:S(2)}) copy-start(bf16[4,32,384]{2,1,0:T(8,128)(2,1)S(1)} %collective-permute-done.11.refs_2_) | copy-start | bytes 294916
  82.4 1.0 %copy-start.4 = (bf16[4,32,384]{2,1,0:T(8,128)(2,1)}, bf16[4,32,384]{2,1,0:T(8,128)(2,1)S(1)}, u32[]{:S(2)}) copy-start(bf16[4,32,384]{2,1,0:T(8,128)(2,1)S(1)} %collective-permute-done.12.refs_3_) | copy-start | bytes 294916
  82.4 5.6 %collective-permute-start.19 = (bf16[1,96,384]{2,1,0:T(8,128)(2,1)S(1)}, bf16[1,96,384]{2,1,0:T(8,128)(2,1)S(1)}, u32[]{:S(2)}, u32[]{:S(2)}) collective-permute-start(bf16[1,96,384]{2,1,0:T(8,128)(2,1)S(1)} %fusion.11), channel_id=1, source_target_pairs={{0,16},{4,20},{8,24},{12,28},{16,0},{20,4},{24,8},{28,12},{1,17},{... | collective-permute-start | bytes 221192 | tf_op jit(solution)/shard_map/ppermute | solution.py:281

commit v15 on v14

--- a/solution.py
+++ b/solution.py
@@ -52,9 +52,9 @@
     return [member for member in range(MEMBERS) if not member & mask]
 
 
-def read_pair(ref, mask, swapped=0):
-    low = jnp.concatenate([ref[member ^ swapped] for member in low_members(mask)], 0)
-    high = jnp.concatenate([ref[(member | mask) ^ swapped] for member in low_members(mask)], 0)
+def read_pair(ref, mask, spots=range(MEMBERS), swapped=0):
+    low = jnp.concatenate([ref[spots[member] ^ swapped] for member in low_members(mask)], 0)
+    high = jnp.concatenate([ref[spots[member | mask] ^ swapped] for member in low_members(mask)], 0)
     return jnp.concatenate([low, high], 1).astype(jnp.float32)
 
 
@@ -125,7 +125,7 @@
 
 
 def backward_kernel(
-    places_down, places_up, place_ref, grad_ref, hidden_ref, slope_ref, normed_ref, normed_t_ref, factor_ref,
+    spots, places_down, places_up, place_ref, grad_ref, hidden_ref, slope_ref, normed_ref, normed_t_ref, factor_ref,
     up_ref, down_ref, d_pre_ref, grad_t_ref, *rest
 ):
     blocks, work_ref = rest[:-1], rest[-1]
@@ -136,7 +136,7 @@
         mask = MASKS[section]
         at = pl.ds(section * pairs, pairs)
         if section == last:
-            pair_grad = read_pair(grad_ref, mask, swapped=place_ref[0])
+            pair_grad = read_pair(grad_ref, mask, spots, place_ref[2])
         else:
             pair_grad = read_pair(work_ref, mask)
         pair_bf = pair_grad.astype(jnp.bfloat16)
@@ -242,14 +242,14 @@
     )(state, *in_vmem(up), pltpu.with_memory_space_constraint(w_down, pltpu.HBM))
 
 
-def backward(place, grad, kept, places, block):
+def backward(place, grad, kept, spots, places, block):
     total, units = kept[0].shape
     depth = kept[2].shape[1]
     bf16 = jnp.bfloat16
     outs = [pltpu.VMEM((total, units), bf16), pltpu.VMEM((depth, total), bf16)]
     outs += [block] * 2 if block else []
     return pl.pallas_call(
-        functools.partial(backward_kernel, *places),
+        functools.partial(backward_kernel, spots, *places),
         out_shape=outs,
         in_specs=[spec(pltpu.SMEM)] + [spec(pltpu.VMEM)] * (1 + len(kept)),
         out_specs=[spec(pltpu.VMEM)] * len(outs),
@@ -399,7 +399,10 @@
     owns = [lax.axis_index(axis) // (1 << bit) % 2 for axis, bit in [steps[core]] + order_up]
     own = dict(zip([steps[core]] + order_up, owns))
     member = sum(own[step] * mask for step, mask in zip(steps, MASKS))
-    place = jnp.stack([member, 1 - own[steps[core]]]).astype(jnp.int32)
+    inbound = (z, core, x, y)
+    spots = [sum(bool(m & MASKS[at]) << k for k, at in enumerate(inbound)) for m in range(MEMBERS)]
+    spot = sum(own[steps[at]] << k for k, at in enumerate(inbound))
+    place = jnp.stack([member, 1 - own[steps[core]], spot]).astype(jnp.int32)
     place, owns, others = lax.optimization_barrier((place, owns, [1 - item for item in owns]))
     halves = {step: pair for step, pair in zip([steps[core]] + order_up, zip(owns, others))}
     places = [block_places(order, span_x, span_y) for order in (order_down, order_up)]
@@ -410,15 +413,16 @@
     parts = (2, 2, 2, 2, 1, rows // MEMBERS, width)
     state = exchange(signal.reshape(MEMBERS, rows // MEMBERS, width), groups)
     coming = Journey(cotangent.reshape(parts))
+    coming.hop(z, steps, halves)
     coming.hop(core, steps, halves)
     coming.hop_both(x, y, steps, halves)
     up = load(place, w_up)
-    state = coming.hop(z, steps, halves, state)
+    coming.held, state = lax.optimization_barrier((coming.held, state))
     state, *kept, down = forward(state, up, w_down)
     kept += [up, down]
     going = Journey(state.reshape(parts))
     grad = going.hop(z, steps, halves, coming.held)
-    d_pre, grad_t, *given = backward(place, grad, kept, places, block)
+    d_pre, grad_t, *given = backward(place, grad, kept, spots, places, block)
     hidden, normed_t = kept[0], kept[3]
     if not given:
         going.hop(core, steps, halves)

time: 88.9 us -> 95.4 us (1.073)
  waiting for transfers between devices: 34.8 us -> 40.3 us
  local copies, waits for them, and re-layouts: 0.26 us -> 1.22 us
    ppermute x18, waiting for transfers between devices: 29.8 us -> 38.3 us  [swap(): return lax.ppermute(block, axis, pairs)]
    all_to_all x1, starting transfers between devices: 7.44 us -> 3.83 us  [exchange(): lax.all_to_all(block, ('gx', 'gy'), split_axis=0, concat_axis=0, axis_ind...]
    all_to_all x1, waiting for transfers between devices: 3.45 us -> 0.01 us  [exchange(): lax.all_to_all(block, ('gx', 'gy'), split_axis=0, concat_axis=0, axis_ind...]
    ppermute x18, starting transfers between devices: 11.9 us -> 15.3 us  [swap(): return lax.ppermute(block, axis, pairs)]
    squeeze x3 -> x2, local copies, waits for them, and re-layouts: 0.15 us -> 1.12 us  [slice_at(): return part if keep else lax.squeeze(part, (dim,))]
  transfers between devices with their start and end apart: 21 -> 21, of which waited for: 13 -> 16; matrix products, arithmetic and copies ran while one was open for 3% -> 3% of each run, Pallas kernels for 18% -> 8%
where the time goes in v15:
time: 95.4 us; the launch traced here: 95.1 us
  waiting for transfers between devices  40.3 us (42%)
  Pallas kernels  25.5 us (27%)
  starting transfers between devices  23.6 us (25%)
  other arithmetic  3.53 us (4%)
  local copies, waits for them, and re-layouts  1.22 us (1%)
  between operations  0.98 us (1%)
    ppermute x18, waiting for transfers between devices, swap(): return lax.ppermute(block, axis, pairs)  38.3 us
    ppermute x18, starting transfers between devices, swap(): return lax.ppermute(block, axis, pairs)  15.3 us
    pallas_call x1, Pallas kernels, backward(): pl.pallas_call(functools.partial(backward_kernel, spots, *places), out_sh...  9.44 us
    pallas_call x1, Pallas kernels, forward(): pl.pallas_call(forward_kernel, out_shape=outs, in_specs=[spec(pltpu.VMEM)...  8.73 us
    ppermute x2, starting transfers between devices, swap_both(): return lax.ppermute(block, ('gx', 'gy'), pairs)  4.56 us
    all_to_all x1, starting transfers between devices, exchange(): lax.all_to_all(block, ('gx', 'gy'), split_axis=0, concat_axis=0, axis_ind...  3.83 us
    pallas_call x1, Pallas kernels, keep_blocks(): pl.pallas_call(functools.partial(keep_kernel, *places), out_shape=[block]...  3.17 us
    pallas_call x1, Pallas kernels, load(): pl.pallas_call(load_kernel, out_shape=pltpu.VMEM(weight.shape, weight.dty...  2.21 us
  transfers between devices with their start and end apart: 21, of which 16 were waited for; matrix products, arithmetic and copies ran while one was open for 3% of the time, Pallas kernels for 8%

profile of v15, /device:TPU:0, one launch (start us, length us, event | category | flops | bytes accessed | tf_op | source)
XLA Modules:
  0.0 95.1 jit_solution(808588342795675830)
XLA Ops:
  0.8 1.1 %dynamic-slice_bitcast_fusion.2 = (bf16[2,2,2,1,32,384]{5,4,2,1,0,3:T(8,128)(2,1)S(1)}, bf16[2,2,2,1,32,384]{5,4,2,1,0,3:T(8,128)(2,1)S(1)}) fusion(bf16[2,2,2,2,1,32,384]{6,5,3,2,1,4,0:T(8,128)(2,1)} %bitcast.97, s32[]{:T(128)S(6)} %sub.34, s32[]{:T(128)S(6)} %select_n.36), kind=kLoop, calls=%fused_computation.51 | loop fusion | bytes 786440 | tf_op jit(solution)/shard_map/squeeze | solution.py:360
  1.9 4.1 %collective-permute-start = (bf16[2,2,2,1,32,384]{5,4,2,1,0,3:T(8,128)(2,1)S(1)}, bf16[2,2,2,1,32,384]{5,4,2,1,0,3:T(8,128)(2,1)S(1)}, u32[]{:S(2)}, u32[]{:S(2)}) collective-permute-start(bf16[2,2,2,1,32,384]{5,4,2,1,0,3:T(8,128)(2,1)S(1)} %get-tuple-element.109), channel_id=1, source_target_pairs={{0,16},{4,20},{8,24},{12,28},{16,0},{20,4},{24,8},{28,12},{1,17},{... | collective-permute-start | bytes 589832 | tf_op jit(solution)/shard_map/ppermute | solution.py:281
  6.0 3.8 %all-to-all-start = ((bf16[16,32,384]{2,1,0:T(8,128)(2,1)}), bf16[16,32,384]{2,1,0:T(8,128)(2,1)S(1)}, u32[]{:S(2)}, u32[]{:S(2)}) async-start(bf16[16,32,384]{2,1,0:T(8,128)(2,1)} %bitcast.98), calls=%async_computation | async-start | bytes 786432 | tf_op jit(solution)/shard_map/all_to_all | solution.py:40
  9.8 10.3 %collective-permute-done = bf16[2,2,2,1,32,384]{5,4,2,1,0,3:T(8,128)(2,1)S(1)} collective-permute-done((bf16[2,2,2,1,32,384]{5,4,2,1,0,3:T(8,128)(2,1)S(1)}, bf16[2,2,2,1,32,384]{5,4,2,1,0,3:T(8,128)(2,1)S(1)}, u32[]{:S(2)}, u32[]{:S(2)}) %collective-permute-start) | collective-permute-done | bytes 196640 | tf_op jit(solution)/shard_map/ppermute | solution.py:281
  20.4 1.4 %collective-permute-done.1 = bf16[2,2,2,32,384]{4,3,2,1,0:T(8,128)(2,1)S(1)} collective-permute-done((bf16[2,2,2,32,384]{4,3,2,1,0:T(8,128)(2,1)S(1)}, bf16[2,2,2,32,384]{4,3,2,1,0:T(8,128)(2,1)S(1)}, u32[]{:S(2)}, u32[]{:S(2)}) %collective-permute-start.1) | collective-permute-done | bytes 196640 | tf_op jit(solution)/shard_map/ppermute | solution.py:281
  21.8 2.9 %collective-permute-start.4 = (bf16[4,32,384]{2,1,0:T(8,128)(2,1)S(1)}, bf16[4,32,384]{2,1,0:T(8,128)(2,1)S(1)}, u32[]{:S(2)}, u32[]{:S(2)}) collective-permute-start(bf16[4,32,384]{2,1,0:T(8,128)(2,1)S(1)} %get-tuple-element.104), channel_id=1, source_target_pairs={{0,6},{1,7},{2,4},{3,5},{4,2},{5,3},{6,0},{7,1},{8,14},{9,15},{10,... | collective-permute-start | bytes 294920 | tf_op jit(solution)/shard_map/ppermute | solution.py:370
  25.3 2.2 %shard_map.67.up_ref = bf16[768,1536]{1,0:T(8,128)(2,1)S(1)} custom-call(s32[3]{0:T(128)S(1)} %pad_add_fusion.place_ref, bf16[768,1536]{1,0:T(8,128)(2,1)} %source.1), custom_call_target="tpu_custom_call" | custom-call | bytes 4718592 | tf_op jit(solution)/shard_map/pallas_call | solution.py:207
  27.8 2.0 %collective-permute-done.3 = bf16[4,32,384]{2,1,0:T(8,128)(2,1)S(1)} collective-permute-done((bf16[4,32,384]{2,1,0:T(8,128)(2,1)S(1)}, bf16[4,32,384]{2,1,0:T(8,128)(2,1)S(1)}, u32[]{:S(2)}, u32[]{:S(2)}) %collective-permute-start.3) | collective-permute-done | bytes 98336 | tf_op jit(solution)/shard_map/ppermute | solution.py:281
  30.2 8.7 %shard_map.68 = (bf16[16,32,384]{2,1,0:T(8,128)(2,1)S(1)}, bf16[1024,1536]{1,0:T(8,128)(2,1)S(1)}, bf16[1024,1536]{1,0:T(8,128)(2,1)S(1)}, bf16[1024,768]{1,0:T(...) custom-call(bf16[16,32,384]{2,1,0:T(8,128)(2,1)S(1)} %all-to-all-done.state_r, ...), custom_call_target="tpu_custom_call" | custom-call | flops 12079595520 | bytes 25165824 | tf_op jit(solution)/shard_map/pallas_call | solution.py:232
  39.0 9.4 %shard_map.69 = (bf16[1024,1536]{1,0:T(8,128)(2,1)S(1)}, bf16[768,1024]{1,0:T(8,128)(2,1)S(1)}, bf16[16,96,384]{2,1,0:T(8,128)(2,1)S(1)}, bf16[16,96,384]{2,1,0:T(8,128)(2,1)S(1)}) custom-call(s32[3]{0:T(128)S(1)} %pad_add_fusion.place_ref, bf16[16,32,384]{2,1,0:T(8,128)(2,1)S(1)} %pad_maximum_fusion.grad_ref, ...), custom_call_target="tpu_custom_call" | custom-call | flops 12079595520 | bytes 25165824 | tf_op jit(solution)/shard_map/pallas_call | solution.py:251
  49.0 3.2 %shard_map.70 = (bf16[16,96,384]{2,1,0:T(8,128)(2,1)S(1)}, bf16[16,96,384]{2,1,0:T(8,128)(2,1)S(1)}) custom-call(s32[3]{0:T(128)S(1)} %pad_add_fusion.place_ref, bf16[1024,1536]{1,0:T(8,128)(2,1)S(1)} %get-tuple-element.56.hidden_ref, bf16[1024,1536]{1,0:T(8,128)(2,1)S(1)} %get-tuple-element.63.d_pre_ref, ...), custom_call_target="tpu_custom_call" | custom-call | flops 2415919104 | bytes 12582912 | tf_op jit(solution)/shard_map/pallas_call | solution.py:267
  52.5 1.5 %collective-permute-start.7 = (bf16[8,96,384]{2,1,0:T(8,128)(2,1)S(1)}, bf16[8,96,384]{2,1,0:T(8,128)(2,1)S(1)}, u32[]{:S(2)}, u32[]{:S(2)}) collective-permute-start(bf16[8,96,384]{2,1,0:T(8,128)(2,1)S(1)} %get-tuple-element.86), channel_id=1, source_target_pairs={{0,4},{4,0},{8,12},{12,8},{16,20},{20,16},{24,28},{28,24},{1,5},{5... | collective-permute-start | bytes 1769480 | tf_op jit(solution)/shard_map/ppermute | solution.py:281
  54.4 0.7 collective-permute-start.15
  55.1 11.4 %collective-permute-done.5 = bf16[2,2,2,1,32,384]{5,4,2,1,0,3:T(8,128)(2,1)S(1)} collective-permute-done((bf16[2,2,2,1,32,384]{5,4,2,1,0,3:T(8,128)(2,1)S(1)}, bf16[2,2,2,1,32,384]{5,4,2,1,0,3:T(8,128)(2,1)S(1)}, u32[]{:S(2)}, u32[]{:S(2)}) %collective-permute-start.5) | collective-permute-done | bytes 196640 | tf_op jit(solution)/shard_map/ppermute | solution.py:281
  66.6 1.3 %collective-permute-done.7 = bf16[8,96,384]{2,1,0:T(8,128)(2,1)S(1)} collective-permute-done((bf16[8,96,384]{2,1,0:T(8,128)(2,1)S(1)}, bf16[8,96,384]{2,1,0:T(8,128)(2,1)S(1)}, u32[]{:S(2)}, u32[]{:S(2)}) %collective-permute-start.7) | collective-permute-done | bytes 589856 | tf_op jit(solution)/shard_map/ppermute | solution.py:281
  68.1 1.3 %collective-permute-done.15 = bf16[8,96,384]{2,1,0:T(8,128)(2,1)S(1)} collective-permute-done((bf16[8,96,384]{2,1,0:T(8,128)(2,1)S(1)}, bf16[8,96,384]{2,1,0:T(8,128)(2,1)S(1)}, u32[]{:S(2)}, u32[]{:S(2)}) %collective-permute-start.15) | collective-permute-done | bytes 589856 | tf_op jit(solution)/shard_map/ppermute | solution.py:281
  69.6 0.8 collective-permute-start.16
  70.5 1.3 %collective-permute-start.9 = (bf16[4,96,384]{2,1,0:T(8,128)(2,1)S(1)}, bf16[4,96,384]{2,1,0:T(8,128)(2,1)S(1)}, u32[]{:S(2)}, u32[]{:S(2)}) collective-permute-start(bf16[4,96,384]{2,1,0:T(8,128)(2,1)S(1)} %get-tuple-element.69), channel_id=1, source_target_pairs={{0,2},{1,3},{2,0},{3,1},{4,6},{5,7},{6,4},{7,5},{8,10},{9,11},{10,... | collective-permute-start | bytes 884744 | tf_op jit(solution)/shard_map/ppermute | solution.py:281
  71.8 0.7 fusion.15
  72.5 5.2 %collective-permute-done.16 = bf16[4,96,384]{2,1,0:T(8,128)(2,1)S(1)} collective-permute-done((bf16[4,96,384]{2,1,0:T(8,128)(2,1)S(1)}, bf16[4,96,384]{2,1,0:T(8,128)(2,1)S(1)}, u32[]{:S(2)}, u32[]{:S(2)}) %collective-permute-start.16) | collective-permute-done | bytes 294944 | tf_op jit(solution)/shard_map/ppermute | solution.py:281
  77.9 1.0 %collective-permute-done.9 = bf16[4,96,384]{2,1,0:T(8,128)(2,1)S(1)} collective-permute-done((bf16[4,96,384]{2,1,0:T(8,128)(2,1)S(1)}, bf16[4,96,384]{2,1,0:T(8,128)(2,1)S(1)}, u32[]{:S(2)}, u32[]{:S(2)}) %collective-permute-start.9) | collective-permute-done | bytes 294944 | tf_op jit(solution)/shard_map/ppermute | solution.py:281
  79.0 2.5 %collective-permute-start.13 = (bf16[2,96,384]{2,1,0:T(8,128)(2,1)S(1)}, bf16[2,96,384]{2,1,0:T(8,128)(2,1)S(1)}, u32[]{:S(2)}, u32[]{:S(2)}) collective-permute-start(bf16[2,96,384]{2,1,0:T(8,128)(2,1)S(1)} %get-tuple-element.75), channel_id=1, source_target_pairs={{0,8},{4,12},{8,0},{12,4},{16,24},{20,28},{24,16},{28,20},{1,9},{5... | collective-permute-start | bytes 442376 | tf_op jit(solution)/shard_map/ppermute | solution.py:281
  81.6 1.0 %collective-permute-start.10 = (bf16[4,32,384]{2,1,0:T(8,128)(2,1)S(1)}, bf16[4,32,384]{2,1,0:T(8,128)(2,1)S(1)}, u32[]{:S(2)}, u32[]{:S(2)}) collective-permute-start(bf16[4,32,384]{2,1,0:T(8,128)(2,1)S(1)} %get-tuple-element.71), channel_id=1, source_target_pairs={{0,2},{1,3},{2,0},{3,1},{4,6},{5,7},{6,4},{7,5},{8,10},{9,11},{10,... | collective-permute-start | bytes 294920 | tf_op jit(solution)/shard_map/ppermute | solution.py:281
  82.6 0.7 collective-permute-start.11
  83.3 1.7 %collective-permute-start.12 = (bf16[4,32,384]{2,1,0:T(8,128)(2,1)S(1)}, bf16[4,32,384]{2,1,0:T(8,128)(2,1)S(1)}, u32[]{:S(2)}, u32[]{:S(2)}) collective-permute-start(bf16[4,32,384]{2,1,0:T(8,128)(2,1)S(1)} %get-tuple-element.73), channel_id=1, source_target_pairs={{0,6},{1,7},{2,4},{3,5},{4,2},{5,3},{6,0},{7,1},{8,14},{9,15},{10,... | collective-permute-start | bytes 294920 | tf_op jit(solution)/shard_map/ppermute | solution.py:370
  85.1 1.0 %collective-permute-done.17 = bf16[2,96,384]{2,1,0:T(8,128)(2,1)S(1)} collective-permute-done((bf16[2,96,384]{2,1,0:T(8,128)(2,1)S(1)}, bf16[2,96,384]{2,1,0:T(8,128)(2,1)S(1)}, u32[]{:S(2)}, u32[]{:S(2)}) %collective-permute-start.17) | collective-permute-done | bytes 147488 | tf_op jit(solution)/shard_map/ppermute | solution.py:281
  87.2 1.6 %collective-permute-done.12.refs_3_ = bf16[4,32,384]{2,1,0:T(8,128)(2,1)S(1)} collective-permute-done((bf16[4,32,384]{2,1,0:T(8,128)(2,1)S(1)}, bf16[4,32,384]{2,1,0:T(8,128)(2,1)S(1)}, u32[]{:S(2)}, u32[]{:S(2)}) %collective-permute-start.12) | collective-permute-done | bytes 98336 | tf_op jit(solution)/shard_map/ppermute | solution.py:370
  88.9 0.9 collective-permute-start.19
  89.7 1.9 %shard_map.71 = bf16[512,384]{1,0:T(8,128)(2,1)} custom-call(s32[3]{0:T(128)} %copy-done, bf16[4,32,384]{2,1,0:T(8,128)(2,1)} %get-tuple-element.76.refs_0_, bf16[4,32,384]{2,1,0:T(8,128)(2,1)} %copy-done.1, bf16[4,32,384]{2,1,0:T(8,128)(2,1)} %copy-done.2, bf16[4,32,384]{2,1,0:T(8,128)(2,1)} %copy-done.3), custom_call_target="tpu_custom_call" | custom-call | bytes 786432 | tf_op jit(solution)/shard_map/pallas_call | solution.py:376
  91.7 0.7 add_bitcast_fusion.1
  92.4 2.1 %collective-permute-done.19 = bf16[1,96,384]{2,1,0:T(8,128)(2,1)S(1)} collective-permute-done((bf16[1,96,384]{2,1,0:T(8,128)(2,1)S(1)}, bf16[1,96,384]{2,1,0:T(8,128)(2,1)S(1)}, u32[]{:S(2)}, u32[]{:S(2)}) %collective-permute-start.19) | collective-permute-done | bytes 73760 | tf_op jit(solution)/shard_map/ppermute | solution.py:281
  94.4 0.7 add_bitcast_fusion
  (45 shorter events, 4.7 us)
Async XLA Ops:
  0.8 48.2 %copy-start = (s32[3]{0:T(128)}, s32[3]{0:T(128)S(1)}, u32[]{:S(2)}) copy-start(s32[3]{0:T(128)S(1)} %pad_add_fusion.place_ref) | copy-start | bytes 40
  1.9 18.3 %collective-permute-start = (bf16[2,2,2,1,32,384]{5,4,2,1,0,3:T(8,128)(2,1)S(1)}, bf16[2,2,2,1,32,384]{5,4,2,1,0,3:T(8,128)(2,1)S(1)}, u32[]{:S(2)}, u32[]{:S(2)}) collective-permute-start(bf16[2,2,2,1,32,384]{5,4,2,1,0,3:T(8,128)(2,1)S(1)} %get-tuple-element.109), channel_id=1, source_target_pairs={{0,16},{4,20},{8,24},{12,28},{16,0},{20,4},{24,8},{28,12},{1,17},{... | collective-permute-start | bytes 589832 | tf_op jit(solution)/shard_map/ppermute | solution.py:281
  6.0 24.2 %all-to-all-start = ((bf16[16,32,384]{2,1,0:T(8,128)(2,1)}), bf16[16,32,384]{2,1,0:T(8,128)(2,1)S(1)}, u32[]{:S(2)}, u32[]{:S(2)}) async-start(bf16[16,32,384]{2,1,0:T(8,128)(2,1)} %bitcast.98), calls=%async_computation | async-start | bytes 786432 | tf_op jit(solution)/shard_map/all_to_all | solution.py:40
  20.2 1.5 %collective-permute-start.1 = (bf16[2,2,2,32,384]{4,3,2,1,0:T(8,128)(2,1)S(1)}, bf16[2,2,2,32,384]{4,3,2,1,0:T(8,128)(2,1)S(1)}, u32[]{:S(2)}, u32[]{:S(2)}) collective-permute-start(bf16[2,2,2,32,384]{4,3,2,1,0:T(8,128)(2,1)S(1)} %bitcast.102), channel_id=1, source_target_pairs={{0,1},{1,0},{2,3},{3,2},{4,5},{5,4},{6,7},{7,6},{8,9},{9,8},{10,11... | collective-permute-start | bytes 589832 | tf_op jit(solution)/shard_map/ppermute | solution.py:281
  21.8 6.1 %collective-permute-start.4 = (bf16[4,32,384]{2,1,0:T(8,128)(2,1)S(1)}, bf16[4,32,384]{2,1,0:T(8,128)(2,1)S(1)}, u32[]{:S(2)}, u32[]{:S(2)}) collective-permute-start(bf16[4,32,384]{2,1,0:T(8,128)(2,1)S(1)} %get-tuple-element.104), channel_id=1, source_target_pairs={{0,6},{1,7},{2,4},{3,5},{4,2},{5,3},{6,0},{7,1},{8,14},{9,15},{10,... | collective-permute-start | bytes 294920 | tf_op jit(solution)/shard_map/ppermute | solution.py:370
  24.6 5.2 %collective-permute-start.3 = (bf16[4,32,384]{2,1,0:T(8,128)(2,1)S(1)}, bf16[4,32,384]{2,1,0:T(8,128)(2,1)S(1)}, u32[]{:S(2)}, u32[]{:S(2)}) collective-permute-start(bf16[4,32,384]{2,1,0:T(8,128)(2,1)S(1)} %get-tuple-element.105), channel_id=1, source_target_pairs={{0,4},{4,0},{8,12},{12,8},{16,20},{20,16},{24,28},{28,24},{1,5},{5... | collective-permute-start | bytes 294920 | tf_op jit(solution)/shard_map/ppermute | solution.py:281
  25.1 4.9 %collective-permute-start.2 = (bf16[4,32,384]{2,1,0:T(8,128)(2,1)S(1)}, bf16[4,32,384]{2,1,0:T(8,128)(2,1)S(1)}, u32[]{:S(2)}, u32[]{:S(2)}) collective-permute-start(bf16[4,32,384]{2,1,0:T(8,128)(2,1)S(1)} %get-tuple-element.106), channel_id=1, source_target_pairs={{0,2},{1,3},{2,0},{3,1},{4,6},{5,7},{6,4},{7,5},{8,10},{9,11},{10,... | collective-permute-start | bytes 294920 | tf_op jit(solution)/shard_map/ppermute | solution.py:281
  48.4 3.8 %collective-permute-start.6 = (bf16[16,96,384]{2,1,0:T(8,128)(2,1)S(1)}, bf16[16,96,384]{2,1,0:T(8,128)(2,1)S(1)}, u32[]{:S(2)}, u32[]{:S(2)}) collective-permute-start(bf16[16,96,384]{2,1,0:T(8,128)(2,1)S(1)} %get-tuple-element.66), channel_id=1, source_target_pairs={{0,1},{1,0},{2,3},{3,2},{4,5},{5,4},{6,7},{7,6},{8,9},{9,8},{10,11... | collective-permute-start | bytes 3538952 | tf_op jit(solution)/shard_map/ppermute | solution.py:281
  48.5 5.6 %collective-permute-start.14 = (bf16[16,96,384]{2,1,0:T(8,128)(2,1)S(1)}, bf16[16,96,384]{2,1,0:T(8,128)(2,1)S(1)}, u32[]{:S(2)}, u32[]{:S(2)}) collective-permute-start(bf16[16,96,384]{2,1,0:T(8,128)(2,1)S(1)} %get-tuple-element.81), channel_id=1, source_target_pairs={{0,1},{1,0},{2,3},{3,2},{4,5},{5,4},{6,7},{7,6},{8,9},{9,8},{10,11... | collective-permute-start | bytes 3538952 | tf_op jit(solution)/shard_map/ppermute | solution.py:281
  52.5 15.4 %collective-permute-start.7 = (bf16[8,96,384]{2,1,0:T(8,128)(2,1)S(1)}, bf16[8,96,384]{2,1,0:T(8,128)(2,1)S(1)}, u32[]{:S(2)}, u32[]{:S(2)}) collective-permute-start(bf16[8,96,384]{2,1,0:T(8,128)(2,1)S(1)} %get-tuple-element.86), channel_id=1, source_target_pairs={{0,4},{4,0},{8,12},{12,8},{16,20},{20,16},{24,28},{28,24},{1,5},{5... | collective-permute-start | bytes 1769480 | tf_op jit(solution)/shard_map/ppermute | solution.py:281
  54.4 15.1 %collective-permute-start.15 = (bf16[8,96,384]{2,1,0:T(8,128)(2,1)S(1)}, bf16[8,96,384]{2,1,0:T(8,128)(2,1)S(1)}, u32[]{:S(2)}, u32[]{:S(2)}) collective-permute-start(bf16[8,96,384]{2,1,0:T(8,128)(2,1)S(1)} %get-tuple-element.84), channel_id=1, source_target_pairs={{0,2},{1,3},{2,0},{3,1},{4,6},{5,7},{6,4},{7,5},{8,10},{9,11},{10,... | collective-permute-start | bytes 1769480 | tf_op jit(solution)/shard_map/ppermute | solution.py:281
  55.1 11.4 %collective-permute-start.5 = (bf16[2,2,2,1,32,384]{5,4,2,1,0,3:T(8,128)(2,1)S(1)}, bf16[2,2,2,1,32,384]{5,4,2,1,0,3:T(8,128)(2,1)S(1)}, u32[]{:S(2)}, u32[]{:S(2)}) collective-permute-start(bf16[2,2,2,1,32,384]{5,4,2,1,0,3:T(8,128)(2,1)S(1)} %get-tuple-element.55), channel_id=1, source_target_pairs={{0,16},{4,20},{8,24},{12,28},{16,0},{20,4},{24,8},{28,12},{1,17},{... | collective-permute-start | bytes 589832 | tf_op jit(solution)/shard_map/ppermute | solution.py:281
  68.1 3.8 %collective-permute-start.8 = (bf16[2,2,2,32,384]{4,3,2,1,0:T(8,128)(2,1)S(1)}, bf16[2,2,2,32,384]{4,3,2,1,0:T(8,128)(2,1)S(1)}, u32[]{:S(2)}, u32[]{:S(2)}) collective-permute-start(bf16[2,2,2,32,384]{4,3,2,1,0:T(8,128)(2,1)S(1)} %bitcast.101), channel_id=1, source_target_pairs={{0,1},{1,0},{2,3},{3,2},{4,5},{5,4},{6,7},{7,6},{8,9},{9,8},{10,11... | collective-permute-start | bytes 589832 | tf_op jit(solution)/shard_map/ppermute | solution.py:281
  69.6 8.1 %collective-permute-start.16 = (bf16[4,96,384]{2,1,0:T(8,128)(2,1)S(1)}, bf16[4,96,384]{2,1,0:T(8,128)(2,1)S(1)}, u32[]{:S(2)}, u32[]{:S(2)}) collective-permute-start(bf16[4,96,384]{2,1,0:T(8,128)(2,1)S(1)} %get-tuple-element.88), channel_id=1, source_target_pairs={{0,4},{4,0},{8,12},{12,8},{16,20},{20,16},{24,28},{28,24},{1,5},{5... | collective-permute-start | bytes 884744 | tf_op jit(solution)/shard_map/ppermute | solution.py:281
  70.5 8.5 %collective-permute-start.9 = (bf16[4,96,384]{2,1,0:T(8,128)(2,1)S(1)}, bf16[4,96,384]{2,1,0:T(8,128)(2,1)S(1)}, u32[]{:S(2)}, u32[]{:S(2)}) collective-permute-start(bf16[4,96,384]{2,1,0:T(8,128)(2,1)S(1)} %get-tuple-element.69), channel_id=1, source_target_pairs={{0,2},{1,3},{2,0},{3,1},{4,6},{5,7},{6,4},{7,5},{8,10},{9,11},{10,... | collective-permute-start | bytes 884744 | tf_op jit(solution)/shard_map/ppermute | solution.py:281
  77.9 8.2 %collective-permute-start.17 = (bf16[2,96,384]{2,1,0:T(8,128)(2,1)S(1)}, bf16[2,96,384]{2,1,0:T(8,128)(2,1)S(1)}, u32[]{:S(2)}, u32[]{:S(2)}) collective-permute-start(bf16[2,96,384]{2,1,0:T(8,128)(2,1)S(1)} %get-tuple-element.92), channel_id=1, source_target_pairs={{0,16},{4,20},{8,24},{12,28},{16,0},{20,4},{24,8},{28,12},{1,17},{... | collective-permute-start | bytes 442376 | tf_op jit(solution)/shard_map/ppermute | solution.py:281
  79.0 7.3 %collective-permute-start.13 = (bf16[2,96,384]{2,1,0:T(8,128)(2,1)S(1)}, bf16[2,96,384]{2,1,0:T(8,128)(2,1)S(1)}, u32[]{:S(2)}, u32[]{:S(2)}) collective-permute-start(bf16[2,96,384]{2,1,0:T(8,128)(2,1)S(1)} %get-tuple-element.75), channel_id=1, source_target_pairs={{0,8},{4,12},{8,0},{12,4},{16,24},{20,28},{24,16},{28,20},{1,9},{5... | collective-permute-start | bytes 442376 | tf_op jit(solution)/shard_map/ppermute | solution.py:281
  81.6 5.1 %collective-permute-start.10 = (bf16[4,32,384]{2,1,0:T(8,128)(2,1)S(1)}, bf16[4,32,384]{2,1,0:T(8,128)(2,1)S(1)}, u32[]{:S(2)}, u32[]{:S(2)}) collective-permute-start(bf16[4,32,384]{2,1,0:T(8,128)(2,1)S(1)} %get-tuple-element.71), channel_id=1, source_target_pairs={{0,2},{1,3},{2,0},{3,1},{4,6},{5,7},{6,4},{7,5},{8,10},{9,11},{10,... | collective-permute-start | bytes 294920 | tf_op jit(solution)/shard_map/ppermute | solution.py:281
  82.6 4.6 %collective-permute-start.11 = (bf16[4,32,384]{2,1,0:T(8,128)(2,1)S(1)}, bf16[4,32,384]{2,1,0:T(8,128)(2,1)S(1)}, u32[]{:S(2)}, u32[]{:S(2)}) collective-permute-start(bf16[4,32,384]{2,1,0:T(8,128)(2,1)S(1)} %get-tuple-element.72), channel_id=1, source_target_pairs={{0,4},{4,0},{8,12},{12,8},{16,20},{20,16},{24,28},{28,24},{1,5},{5... | collective-permute-start | bytes 294920 | tf_op jit(solution)/shard_map/ppermute | solution.py:281
  83.3 5.5 %collective-permute-start.12 = (bf16[4,32,384]{2,1,0:T(8,128)(2,1)S(1)}, bf16[4,32,384]{2,1,0:T(8,128)(2,1)S(1)}, u32[]{:S(2)}, u32[]{:S(2)}) collective-permute-start(bf16[4,32,384]{2,1,0:T(8,128)(2,1)S(1)} %get-tuple-element.73), channel_id=1, source_target_pairs={{0,6},{1,7},{2,4},{3,5},{4,2},{5,3},{6,0},{7,1},{8,14},{9,15},{10,... | collective-permute-start | bytes 294920 | tf_op jit(solution)/shard_map/ppermute | solution.py:370
  86.1 5.6 %collective-permute-start.18 = (bf16[1,96,384]{2,1,0:T(8,128)(2,1)S(1)}, bf16[1,96,384]{2,1,0:T(8,128)(2,1)S(1)}, u32[]{:S(2)}, u32[]{:S(2)}) collective-permute-start(bf16[1,96,384]{2,1,0:T(8,128)(2,1)S(1)} %fusion.11), channel_id=1, source_target_pairs={{0,8},{4,12},{8,0},{12,4},{16,24},{20,28},{24,16},{28,20},{1,9},{5... | collective-permute-start | bytes 221192 | tf_op jit(solution)/shard_map/ppermute | solution.py:281
  86.6 3.1 %copy-start.1 = (bf16[4,32,384]{2,1,0:T(8,128)(2,1)}, bf16[4,32,384]{2,1,0:T(8,128)(2,1)S(1)}, u32[]{:S(2)}) copy-start(bf16[4,32,384]{2,1,0:T(8,128)(2,1)S(1)} %collective-permute-done.10.refs_1_) | copy-start | bytes 294916
  87.2 2.5 %copy-start.2 = (bf16[4,32,384]{2,1,0:T(8,128)(2,1)}, bf16[4,32,384]{2,1,0:T(8,128)(2,1)S(1)}, u32[]{:S(2)}) copy-start(bf16[4,32,384]{2,1,0:T(8,128)(2,1)S(1)} %collective-permute-done.11.refs_2_) | copy-start | bytes 294916
  88.9 0.9 copy-start.3
  88.9 5.6 %collective-permute-start.19 = (bf16[1,96,384]{2,1,0:T(8,128)(2,1)S(1)}, bf16[1,96,384]{2,1,0:T(8,128)(2,1)S(1)}, u32[]{:S(2)}, u32[]{:S(2)}) collective-permute-start(bf16[1,96,384]{2,1,0:T(8,128)(2,1)S(1)} %fusion.13), channel_id=1, source_target_pairs={{0,16},{4,20},{8,24},{12,28},{16,0},{20,4},{24,8},{28,12},{1,17},{... | collective-permute-start | bytes 221192 | tf_op jit(solution)/shard_map/ppermute | solution.py:281

commit v16 on v14

--- a/solution.py
+++ b/solution.py
@@ -140,8 +140,8 @@
         else:
             pair_grad = read_pair(work_ref, mask)
         pair_bf = pair_grad.astype(jnp.bfloat16)
-        for start in range(0, hidden_units, CHUNK):
-            units = pl.ds(start, CHUNK)
+        for start in range(0, hidden_units, 2 * CHUNK):
+            units = pl.ds(start, 2 * CHUNK)
             d_hidden = jnp.dot(pair_bf, down_ref[:, units], preferred_element_type=jnp.float32)
             d_pre_ref[at, units] = (d_hidden * slope_ref[at, units].astype(jnp.float32)).astype(jnp.bfloat16)
         if section > 0:
@@ -285,17 +285,24 @@
     return slice_at(block, 0, at).astype(jnp.float32)
 
 
-def finish_sum(halves, kept, taken, order, beside=None):
-    for phase, step in enumerate(order):
-        mine, other = halves[step]
-        shape = (2, kept.shape[0] // 2) + kept.shape[1:]
-        kept, taken = kept.reshape(shape), taken.reshape(shape)
-        give = (pick(kept, other) + pick(taken, other)).astype(jnp.bfloat16)
-        kept = (pick(kept, mine) + pick(taken, mine)).astype(jnp.bfloat16)
-        if beside:
-            give = beside(phase, give)
+def halve(halves, step, kept, taken):
+    mine, other = halves[step]
+    shape = (2, kept.shape[0] // 2) + kept.shape[1:]
+    kept, taken = kept.reshape(shape), taken.reshape(shape)
+    give = (pick(kept, other) + pick(taken, other)).astype(jnp.bfloat16)
+    keep = (pick(kept, mine) + pick(taken, mine)).astype(jnp.bfloat16)
+    return keep, give
+
+
+def last_sum(kept, taken):
+    return (kept.astype(jnp.float32) + taken.astype(jnp.float32))[0]
+
+
+def finish_sum(halves, kept, taken, order):
+    for step in order:
+        kept, give = halve(halves, step, kept, taken)
         taken = swap(give, *step)
-    return (kept.astype(jnp.float32) + taken.astype(jnp.float32))[0]
+    return last_sum(kept, taken)
 
 
 def scatter_narrow(halves, left, right, order, span_x, span_y):
@@ -430,18 +437,24 @@
     take_down, take_up = [swap(part, *steps[core]) for part in given]
     keep_down, keep_up = keep_blocks(place, hidden, d_pre, normed_t, grad_t, places, block)
 
-    def beside(phase, give):
+    barrier = lax.optimization_barrier
+    for phase, (step_down, step_up) in enumerate(zip(order_down, order_up)):
+        ending = phase == len(order_down) - 1
+        if not ending:
+            keep_up, give_up = halve(halves, step_up, keep_up, take_up)
+            take_up = swap(give_up, *step_up)
+        keep_down, give_down = halve(halves, step_down, keep_down, take_down)
         if phase == 1:
-            return going.hop(core, steps, halves, give)
+            give_down = going.hop(core, steps, halves, give_down)
         if phase == 2:
-            return going.hop_both(x, y, steps, halves, give)
-        if phase == len(order_down) - 1:
-            going.parts, give = lax.optimization_barrier((going.parts, give))
-        return give
-
-    grad_up = finish_sum(halves, keep_up, take_up, order_up)
-    grad_down = finish_sum(halves, keep_down, take_down, order_down, beside)
-    return (settle(place, going), grad_up, grad_down)
+            give_down = going.hop_both(x, y, steps, halves, give_down)
+        take_down = swap(give_down, *step_down)
+        if ending:
+            take_up, give_down = barrier((take_up, give_down))
+            keep_up, give_up = halve(halves, step_up, keep_up, take_up)
+            going.parts, give_up = barrier((going.parts, give_up))
+            take_up = swap(give_up, *step_up)
+    return (settle(place, going), last_sum(keep_up, take_up), last_sum(keep_down, take_down))
 
 
 def solution(mesh):

time: 88.9 us -> 90.2 us (1.015)
  starting transfers between devices: 23.6 us -> 25.1 us
    ppermute x18, starting transfers between devices: 11.9 us -> 13.5 us  [swap(): return lax.ppermute(block, axis, pairs)]
  transfers between devices with their start and end apart: 21 -> 21, of which waited for: 13 -> 14; matrix products, arithmetic and copies ran while one was open for 3% -> 3% of each run, Pallas kernels for 18% -> 18%
where the time goes in v16:
time: 90.2 us; the launch traced here: 89.9 us
  waiting for transfers between devices  34.5 us (38%)
  Pallas kernels  25.5 us (28%)
  starting transfers between devices  25.1 us (28%)
  other arithmetic  3.52 us (4%)
  between operations  0.98 us (1%)
    ppermute x18, waiting for transfers between devices, swap(): return lax.ppermute(block, axis, pairs)  29.9 us
    ppermute x18, starting transfers between devices, swap(): return lax.ppermute(block, axis, pairs)  13.5 us
    pallas_call x1, Pallas kernels, backward(): pl.pallas_call(functools.partial(backward_kernel, *places), out_shape=out...  9.44 us
    pallas_call x1, Pallas kernels, forward(): pl.pallas_call(forward_kernel, out_shape=outs, in_specs=[spec(pltpu.VMEM)...  8.72 us
    all_to_all x1, starting transfers between devices, exchange(): lax.all_to_all(block, ('gx', 'gy'), split_axis=0, concat_axis=0, axis_ind...  7.44 us
    ppermute x2, starting transfers between devices, swap_both(): return lax.ppermute(block, ('gx', 'gy'), pairs)  4.21 us
    all_to_all x1, waiting for transfers between devices, exchange(): lax.all_to_all(block, ('gx', 'gy'), split_axis=0, concat_axis=0, axis_ind...  3.45 us
    pallas_call x1, Pallas kernels, keep_blocks(): pl.pallas_call(functools.partial(keep_kernel, *places), out_shape=[block]...  3.17 us
  transfers between devices with their start and end apart: 21, of which 14 were waited for; matrix products, arithmetic and copies ran while one was open for 3% of the time, Pallas kernels for 18%

profile of v16, /device:TPU:0, one launch (start us, length us, event | category | flops | bytes accessed | tf_op | source)
XLA Modules:
  0.0 89.9 jit_solution(6811471403119276839)
XLA Ops:
  0.6 7.4 %all-to-all-start = ((bf16[16,32,384]{2,1,0:T(8,128)(2,1)}), bf16[16,32,384]{2,1,0:T(8,128)(2,1)S(1)}, u32[]{:S(2)}, u32[]{:S(2)}) async-start(bf16[16,32,384]{2,1,0:T(8,128)(2,1)} %bitcast.98), calls=%async_computation | async-start | bytes 786432 | tf_op jit(solution)/shard_map/all_to_all | solution.py:40
  8.7 1.1 %collective-permute-done = bf16[2,2,2,1,32,384]{5,4,2,1,0,3:T(8,128)(2,1)S(1)} collective-permute-done((bf16[2,2,2,1,32,384]{5,4,2,1,0,3:T(8,128)(2,1)S(1)}, bf16[2,2,2,1,32,384]{5,4,2,1,0,3:T(8,128)(2,1)S(1)}, u32[]{:S(2)}, u32[]{:S(2)}) %collective-permute-start) | collective-permute-done | bytes 196640 | tf_op jit(solution)/shard_map/ppermute | solution.py:281
  9.9 2.8 %collective-permute-start.3 = (bf16[2,2,32,384]{3,2,1,0:T(8,128)(2,1)S(1)}, bf16[2,2,32,384]{3,2,1,0:T(8,128)(2,1)S(1)}, u32[]{:S(2)}, u32[]{:S(2)}) collective-permute-start(bf16[2,2,32,384]{3,2,1,0:T(8,128)(2,1)S(1)} %bitcast.103), channel_id=1, source_target_pairs={{0,6},{1,7},{2,4},{3,5},{4,2},{5,3},{6,0},{7,1},{8,14},{9,15},{10,... | collective-permute-start | bytes 294920 | tf_op jit(solution)/shard_map/ppermute | solution.py:377
  12.7 0.6 collective-permute-start.2
  13.6 2.2 %shard_map.67.up_ref = bf16[768,1536]{1,0:T(8,128)(2,1)S(1)} custom-call(s32[2]{0:T(128)S(1)} %pad_add_fusion.place_ref, bf16[768,1536]{1,0:T(8,128)(2,1)} %source.1), custom_call_target="tpu_custom_call" | custom-call | bytes 4718592 | tf_op jit(solution)/shard_map/pallas_call | solution.py:207
  15.9 0.9 collective-permute-done.3
  16.7 2.0 %collective-permute-done.2 = bf16[2,2,32,384]{3,2,1,0:T(8,128)(2,1)S(1)} collective-permute-done((bf16[2,2,32,384]{3,2,1,0:T(8,128)(2,1)S(1)}, bf16[2,2,32,384]{3,2,1,0:T(8,128)(2,1)S(1)}, u32[]{:S(2)}, u32[]{:S(2)}) %collective-permute-start.2) | collective-permute-done | bytes 98336 | tf_op jit(solution)/shard_map/ppermute | solution.py:281
  18.9 3.5 %all-to-all-done.state_ref = bf16[16,32,384]{2,1,0:T(8,128)(2,1)S(1)} async-done(((bf16[16,32,384]{2,1,0:T(8,128)(2,1)}), bf16[16,32,384]{2,1,0:T(8,128)(2,1)S(1)}, u32[]{:S(2)}, u32[]{:S(2)}) %all-to-all-start) | async-done | bytes 393248 | tf_op jit(solution)/shard_map/all_to_all | solution.py:40
  22.6 8.7 %shard_map.68 = (bf16[16,32,384]{2,1,0:T(8,128)(2,1)S(1)}, bf16[1024,1536]{1,0:T(8,128)(2,1)S(1)}, bf16[1024,1536]{1,0:T(8,128)(2,1)S(1)}, bf16[1024,768]{1,0:T(...) custom-call(bf16[16,32,384]{2,1,0:T(8,128)(2,1)S(1)} %all-to-all-done.state_r, ...), custom_call_target="tpu_custom_call" | custom-call | flops 12079595520 | bytes 25165824 | tf_op jit(solution)/shard_map/pallas_call | solution.py:232
  31.4 2.0 %collective-permute-done.4 = bf16[8,32,384]{2,1,0:T(8,128)(2,1)S(1)} collective-permute-done((bf16[8,32,384]{2,1,0:T(8,128)(2,1)S(1)}, bf16[8,32,384]{2,1,0:T(8,128)(2,1)S(1)}, u32[]{:S(2)}, u32[]{:S(2)}) %collective-permute-start.4) | collective-permute-done | bytes 196640 | tf_op jit(solution)/shard_map/ppermute | solution.py:281
  33.4 9.4 %shard_map.69 = (bf16[1024,1536]{1,0:T(8,128)(2,1)S(1)}, bf16[768,1024]{1,0:T(8,128)(2,1)S(1)}, bf16[16,96,384]{2,1,0:T(8,128)(2,1)S(1)}, bf16[16,96,384]{2,1,0:T(8,128)(2,1)S(1)}) custom-call(s32[2]{0:T(128)S(1)} %pad_add_fusion.place_ref, bf16[16,32,384]{2,1,0:T(8,128)(2,1)S(1)} %pad_maximum_fusion.1.grad_ref, ...), custom_call_target="tpu_custom_call" | custom-call | flops 12079595520 | bytes 25165824 | tf_op jit(solution)/shard_map/pallas_call | solution.py:251
  43.4 3.2 %shard_map.70 = (bf16[16,96,384]{2,1,0:T(8,128)(2,1)S(1)}, bf16[16,96,384]{2,1,0:T(8,128)(2,1)S(1)}) custom-call(s32[2]{0:T(128)S(1)} %pad_add_fusion.place_ref, bf16[1024,1536]{1,0:T(8,128)(2,1)S(1)} %get-tuple-element.57.hidden_ref, bf16[1024,1536]{1,0:T(8,128)(2,1)S(1)} %get-tuple-element.64.d_pre_ref, ...), custom_call_target="tpu_custom_call" | custom-call | flops 2415919104 | bytes 12582912 | tf_op jit(solution)/shard_map/pallas_call | solution.py:267
  46.9 1.1 %collective-permute-start.7 = (bf16[8,96,384]{2,1,0:T(8,128)(2,1)S(1)}, bf16[8,96,384]{2,1,0:T(8,128)(2,1)S(1)}, u32[]{:S(2)}, u32[]{:S(2)}) collective-permute-start(bf16[8,96,384]{2,1,0:T(8,128)(2,1)S(1)} %get-tuple-element.88), channel_id=1, source_target_pairs={{0,4},{4,0},{8,12},{12,8},{16,20},{20,16},{24,28},{28,24},{1,5},{5... | collective-permute-start | bytes 1769480 | tf_op jit(solution)/shard_map/ppermute | solution.py:281
  48.4 1.2 %collective-permute-start.14 = (bf16[8,96,384]{2,1,0:T(8,128)(2,1)S(1)}, bf16[8,96,384]{2,1,0:T(8,128)(2,1)S(1)}, u32[]{:S(2)}, u32[]{:S(2)}) collective-permute-start(bf16[8,96,384]{2,1,0:T(8,128)(2,1)S(1)} %get-tuple-element.86), channel_id=1, source_target_pairs={{0,2},{1,3},{2,0},{3,1},{4,6},{5,7},{6,4},{7,5},{8,10},{9,11},{10,... | collective-permute-start | bytes 1769480 | tf_op jit(solution)/shard_map/ppermute | solution.py:281
  49.5 11.0 %collective-permute-done.5 = bf16[2,2,2,1,32,384]{5,4,2,1,0,3:T(8,128)(2,1)S(1)} collective-permute-done((bf16[2,2,2,1,32,384]{5,4,2,1,0,3:T(8,128)(2,1)S(1)}, bf16[2,2,2,1,32,384]{5,4,2,1,0,3:T(8,128)(2,1)S(1)}, u32[]{:S(2)}, u32[]{:S(2)}) %collective-permute-start.5) | collective-permute-done | bytes 196640 | tf_op jit(solution)/shard_map/ppermute | solution.py:281
  60.6 1.7 %collective-permute-done.7 = bf16[8,96,384]{2,1,0:T(8,128)(2,1)S(1)} collective-permute-done((bf16[8,96,384]{2,1,0:T(8,128)(2,1)S(1)}, bf16[8,96,384]{2,1,0:T(8,128)(2,1)S(1)}, u32[]{:S(2)}, u32[]{:S(2)}) %collective-permute-start.7) | collective-permute-done | bytes 589856 | tf_op jit(solution)/shard_map/ppermute | solution.py:281
  62.6 0.8 collective-permute-start.9
  63.6 1.4 %collective-permute-start.15 = (bf16[4,96,384]{2,1,0:T(8,128)(2,1)S(1)}, bf16[4,96,384]{2,1,0:T(8,128)(2,1)S(1)}, u32[]{:S(2)}, u32[]{:S(2)}) collective-permute-start(bf16[4,96,384]{2,1,0:T(8,128)(2,1)S(1)} %get-tuple-element.90), channel_id=1, source_target_pairs={{0,4},{4,0},{8,12},{12,8},{16,20},{20,16},{24,28},{28,24},{1,5},{5... | collective-permute-start | bytes 884744 | tf_op jit(solution)/shard_map/ppermute | solution.py:281
  65.0 0.7 fusion.13
  65.7 6.3 %collective-permute-done.9 = bf16[4,96,384]{2,1,0:T(8,128)(2,1)S(1)} collective-permute-done((bf16[4,96,384]{2,1,0:T(8,128)(2,1)S(1)}, bf16[4,96,384]{2,1,0:T(8,128)(2,1)S(1)}, u32[]{:S(2)}, u32[]{:S(2)}) %collective-permute-start.9) | collective-permute-done | bytes 294944 | tf_op jit(solution)/shard_map/ppermute | solution.py:281
  72.7 1.8 %collective-permute-start.16 = (bf16[2,96,384]{2,1,0:T(8,128)(2,1)S(1)}, bf16[2,96,384]{2,1,0:T(8,128)(2,1)S(1)}, u32[]{:S(2)}, u32[]{:S(2)}) collective-permute-start(bf16[2,96,384]{2,1,0:T(8,128)(2,1)S(1)} %get-tuple-element.94), channel_id=1, source_target_pairs={{0,16},{4,20},{8,24},{12,28},{16,0},{20,4},{24,8},{28,12},{1,17},{... | collective-permute-start | bytes 442376 | tf_op jit(solution)/shard_map/ppermute | solution.py:281
  74.6 1.5 %collective-permute-start.10 = (bf16[4,32,384]{2,1,0:T(8,128)(2,1)S(1)}, bf16[4,32,384]{2,1,0:T(8,128)(2,1)S(1)}, u32[]{:S(2)}, u32[]{:S(2)}) collective-permute-start(bf16[4,32,384]{2,1,0:T(8,128)(2,1)S(1)} %get-tuple-element.72), channel_id=1, source_target_pairs={{0,2},{1,3},{2,0},{3,1},{4,6},{5,7},{6,4},{7,5},{8,10},{9,11},{10,... | collective-permute-start | bytes 294920 | tf_op jit(solution)/shard_map/ppermute | solution.py:281
  76.1 0.6 collective-permute-start.11
  76.6 1.4 %collective-permute-start.12 = (bf16[4,32,384]{2,1,0:T(8,128)(2,1)S(1)}, bf16[4,32,384]{2,1,0:T(8,128)(2,1)S(1)}, u32[]{:S(2)}, u32[]{:S(2)}) collective-permute-start(bf16[4,32,384]{2,1,0:T(8,128)(2,1)S(1)} %get-tuple-element.74), channel_id=1, source_target_pairs={{0,6},{1,7},{2,4},{3,5},{4,2},{5,3},{6,0},{7,1},{8,14},{9,15},{10,... | collective-permute-start | bytes 294920 | tf_op jit(solution)/shard_map/ppermute | solution.py:377
  78.1 1.7 %collective-permute-done.17 = bf16[2,96,384]{2,1,0:T(8,128)(2,1)S(1)} collective-permute-done((bf16[2,96,384]{2,1,0:T(8,128)(2,1)S(1)}, bf16[2,96,384]{2,1,0:T(8,128)(2,1)S(1)}, u32[]{:S(2)}, u32[]{:S(2)}) %collective-permute-start.17) | collective-permute-done | bytes 147488 | tf_op jit(solution)/shard_map/ppermute | solution.py:281
  79.7 2.1 %collective-permute-done.16 = bf16[2,96,384]{2,1,0:T(8,128)(2,1)S(1)} collective-permute-done((bf16[2,96,384]{2,1,0:T(8,128)(2,1)S(1)}, bf16[2,96,384]{2,1,0:T(8,128)(2,1)S(1)}, u32[]{:S(2)}, u32[]{:S(2)}) %collective-permute-start.16) | collective-permute-done | bytes 147488 | tf_op jit(solution)/shard_map/ppermute | solution.py:281
  82.2 0.9 %collective-permute-start.18 = (bf16[1,96,384]{2,1,0:T(8,128)(2,1)S(1)}, bf16[1,96,384]{2,1,0:T(8,128)(2,1)S(1)}, u32[]{:S(2)}, u32[]{:S(2)}) collective-permute-start(bf16[1,96,384]{2,1,0:T(8,128)(2,1)S(1)} %fusion.11), channel_id=1, source_target_pairs={{0,8},{4,12},{8,0},{12,4},{16,24},{20,28},{24,16},{28,20},{1,9},{5... | collective-permute-start | bytes 221192 | tf_op jit(solution)/shard_map/ppermute | solution.py:281
  83.1 2.0 %collective-permute-start.19 = (bf16[1,96,384]{2,1,0:T(8,128)(2,1)S(1)}, bf16[1,96,384]{2,1,0:T(8,128)(2,1)S(1)}, u32[]{:S(2)}, u32[]{:S(2)}) collective-permute-start(bf16[1,96,384]{2,1,0:T(8,128)(2,1)S(1)} %fusion.10), channel_id=1, source_target_pairs={{0,16},{4,20},{8,24},{12,28},{16,0},{20,4},{24,8},{28,12},{1,17},{... | collective-permute-start | bytes 221192 | tf_op jit(solution)/shard_map/ppermute | solution.py:281
  85.2 1.9 %shard_map.71 = bf16[512,384]{1,0:T(8,128)(2,1)} custom-call(s32[2]{0:T(128)} %copy-done, bf16[4,32,384]{2,1,0:T(8,128)(2,1)} %get-tuple-element.80.refs_0_, bf16[4,32,384]{2,1,0:T(8,128)(2,1)} %copy-done.2, bf16[4,32,384]{2,1,0:T(8,128)(2,1)} %copy-done.3, bf16[4,32,384]{2,1,0:T(8,128)(2,1)} %copy-done.4), custom_call_target="tpu_custom_call" | custom-call | bytes 786432 | tf_op jit(solution)/shard_map/pallas_call | solution.py:383
  87.1 0.7 add_bitcast_fusion.1
  87.8 1.4 %collective-permute-done.19 = bf16[1,96,384]{2,1,0:T(8,128)(2,1)S(1)} collective-permute-done((bf16[1,96,384]{2,1,0:T(8,128)(2,1)S(1)}, bf16[1,96,384]{2,1,0:T(8,128)(2,1)S(1)}, u32[]{:S(2)}, u32[]{:S(2)}) %collective-permute-start.19) | collective-permute-done | bytes 73760 | tf_op jit(solution)/shard_map/ppermute | solution.py:281
  89.2 0.7 add_bitcast_fusion
  (50 shorter events, 4.2 us)
Async XLA Ops:
  0.6 7.6 %copy-start.1 = (bf16[512,384]{1,0:T(8,128)(2,1)S(1)}, bf16[512,384]{1,0:T(8,128)(2,1)}, u32[]{:S(2)}) copy-start(bf16[512,384]{1,0:T(8,128)(2,1)} %param.7) | copy-start | bytes 1179652
  0.6 21.7 %all-to-all-start = ((bf16[16,32,384]{2,1,0:T(8,128)(2,1)}), bf16[16,32,384]{2,1,0:T(8,128)(2,1)S(1)}, u32[]{:S(2)}, u32[]{:S(2)}) async-start(bf16[16,32,384]{2,1,0:T(8,128)(2,1)} %bitcast.98), calls=%async_computation | async-start | bytes 786432 | tf_op jit(solution)/shard_map/all_to_all | solution.py:40
  8.3 35.2 %copy-start = (s32[2]{0:T(128)}, s32[2]{0:T(128)S(1)}, u32[]{:S(2)}) copy-start(s32[2]{0:T(128)S(1)} %pad_add_fusion.place_ref) | copy-start | bytes 28
  8.3 1.5 %collective-permute-start = (bf16[2,2,2,1,32,384]{5,4,2,1,0,3:T(8,128)(2,1)S(1)}, bf16[2,2,2,1,32,384]{5,4,2,1,0,3:T(8,128)(2,1)S(1)}, u32[]{:S(2)}, u32[]{:S(2)}) collective-permute-start(bf16[2,2,2,1,32,384]{5,4,2,1,0,3:T(8,128)(2,1)S(1)} %get-tuple-element.111), channel_id=1, source_target_pairs={{0,1},{1,0},{2,3},{3,2},{4,5},{5,4},{6,7},{7,6},{8,9},{9,8},{10,11... | collective-permute-start | bytes 589832 | tf_op jit(solution)/shard_map/ppermute | solution.py:281
  9.9 6.8 %collective-permute-start.3 = (bf16[2,2,32,384]{3,2,1,0:T(8,128)(2,1)S(1)}, bf16[2,2,32,384]{3,2,1,0:T(8,128)(2,1)S(1)}, u32[]{:S(2)}, u32[]{:S(2)}) collective-permute-start(bf16[2,2,32,384]{3,2,1,0:T(8,128)(2,1)S(1)} %bitcast.103), channel_id=1, source_target_pairs={{0,6},{1,7},{2,4},{3,5},{4,2},{5,3},{6,0},{7,1},{8,14},{9,15},{10,... | collective-permute-start | bytes 294920 | tf_op jit(solution)/shard_map/ppermute | solution.py:377
  12.7 6.0 %collective-permute-start.2 = (bf16[2,2,32,384]{3,2,1,0:T(8,128)(2,1)S(1)}, bf16[2,2,32,384]{3,2,1,0:T(8,128)(2,1)S(1)}, u32[]{:S(2)}, u32[]{:S(2)}) collective-permute-start(bf16[2,2,32,384]{3,2,1,0:T(8,128)(2,1)S(1)} %bitcast.104), channel_id=1, source_target_pairs={{0,4},{4,0},{8,12},{12,8},{16,20},{20,16},{24,28},{28,24},{1,5},{5... | collective-permute-start | bytes 294920 | tf_op jit(solution)/shard_map/ppermute | solution.py:281
  13.4 5.4 %collective-permute-start.1 = (bf16[2,2,32,384]{3,2,1,0:T(8,128)(2,1)S(1)}, bf16[2,2,32,384]{3,2,1,0:T(8,128)(2,1)S(1)}, u32[]{:S(2)}, u32[]{:S(2)}) collective-permute-start(bf16[2,2,32,384]{3,2,1,0:T(8,128)(2,1)S(1)} %bitcast.105), channel_id=1, source_target_pairs={{0,2},{1,3},{2,0},{3,1},{4,6},{5,7},{6,4},{7,5},{8,10},{9,11},{10,... | collective-permute-start | bytes 294920 | tf_op jit(solution)/shard_map/ppermute | solution.py:281
  22.3 11.0 %collective-permute-start.4 = (bf16[8,32,384]{2,1,0:T(8,128)(2,1)S(1)}, bf16[8,32,384]{2,1,0:T(8,128)(2,1)S(1)}, u32[]{:S(2)}, u32[]{:S(2)}) collective-permute-start(bf16[8,32,384]{2,1,0:T(8,128)(2,1)S(1)} %get-tuple-element.55), channel_id=1, source_target_pairs={{0,16},{4,20},{8,24},{12,28},{16,0},{20,4},{24,8},{28,12},{1,17},{... | collective-permute-start | bytes 589832 | tf_op jit(solution)/shard_map/ppermute | solution.py:281
  42.8 3.8 %collective-permute-start.6 = (bf16[16,96,384]{2,1,0:T(8,128)(2,1)S(1)}, bf16[16,96,384]{2,1,0:T(8,128)(2,1)S(1)}, u32[]{:S(2)}, u32[]{:S(2)}) collective-permute-start(bf16[16,96,384]{2,1,0:T(8,128)(2,1)S(1)} %get-tuple-element.67), channel_id=1, source_target_pairs={{0,1},{1,0},{2,3},{3,2},{4,5},{5,4},{6,7},{7,6},{8,9},{9,8},{10,11... | collective-permute-start | bytes 3538952 | tf_op jit(solution)/shard_map/ppermute | solution.py:281
  42.9 5.1 %collective-permute-start.13 = (bf16[16,96,384]{2,1,0:T(8,128)(2,1)S(1)}, bf16[16,96,384]{2,1,0:T(8,128)(2,1)S(1)}, u32[]{:S(2)}, u32[]{:S(2)}) collective-permute-start(bf16[16,96,384]{2,1,0:T(8,128)(2,1)S(1)} %get-tuple-element.76), channel_id=1, source_target_pairs={{0,1},{1,0},{2,3},{3,2},{4,5},{5,4},{6,7},{7,6},{8,9},{9,8},{10,11... | collective-permute-start | bytes 3538952 | tf_op jit(solution)/shard_map/ppermute | solution.py:281
  46.9 15.4 %collective-permute-start.7 = (bf16[8,96,384]{2,1,0:T(8,128)(2,1)S(1)}, bf16[8,96,384]{2,1,0:T(8,128)(2,1)S(1)}, u32[]{:S(2)}, u32[]{:S(2)}) collective-permute-start(bf16[8,96,384]{2,1,0:T(8,128)(2,1)S(1)} %get-tuple-element.88), channel_id=1, source_target_pairs={{0,4},{4,0},{8,12},{12,8},{16,20},{20,16},{24,28},{28,24},{1,5},{5... | collective-permute-start | bytes 1769480 | tf_op jit(solution)/shard_map/ppermute | solution.py:281
  48.4 15.1 %collective-permute-start.14 = (bf16[8,96,384]{2,1,0:T(8,128)(2,1)S(1)}, bf16[8,96,384]{2,1,0:T(8,128)(2,1)S(1)}, u32[]{:S(2)}, u32[]{:S(2)}) collective-permute-start(bf16[8,96,384]{2,1,0:T(8,128)(2,1)S(1)} %get-tuple-element.86), channel_id=1, source_target_pairs={{0,2},{1,3},{2,0},{3,1},{4,6},{5,7},{6,4},{7,5},{8,10},{9,11},{10,... | collective-permute-start | bytes 1769480 | tf_op jit(solution)/shard_map/ppermute | solution.py:281
  49.5 11.0 %collective-permute-start.5 = (bf16[2,2,2,1,32,384]{5,4,2,1,0,3:T(8,128)(2,1)S(1)}, bf16[2,2,2,1,32,384]{5,4,2,1,0,3:T(8,128)(2,1)S(1)}, u32[]{:S(2)}, u32[]{:S(2)}) collective-permute-start(bf16[2,2,2,1,32,384]{5,4,2,1,0,3:T(8,128)(2,1)S(1)} %get-tuple-element.56), channel_id=1, source_target_pairs={{0,16},{4,20},{8,24},{12,28},{16,0},{20,4},{24,8},{28,12},{1,17},{... | collective-permute-start | bytes 589832 | tf_op jit(solution)/shard_map/ppermute | solution.py:281
  62.5 2.5 %collective-permute-start.8 = (bf16[2,2,2,32,384]{4,3,2,1,0:T(8,128)(2,1)S(1)}, bf16[2,2,2,32,384]{4,3,2,1,0:T(8,128)(2,1)S(1)}, u32[]{:S(2)}, u32[]{:S(2)}) collective-permute-start(bf16[2,2,2,32,384]{4,3,2,1,0:T(8,128)(2,1)S(1)} %bitcast.102), channel_id=1, source_target_pairs={{0,1},{1,0},{2,3},{3,2},{4,5},{5,4},{6,7},{7,6},{8,9},{9,8},{10,11... | collective-permute-start | bytes 589832 | tf_op jit(solution)/shard_map/ppermute | solution.py:281
  62.6 9.4 %collective-permute-start.9 = (bf16[4,96,384]{2,1,0:T(8,128)(2,1)S(1)}, bf16[4,96,384]{2,1,0:T(8,128)(2,1)S(1)}, u32[]{:S(2)}, u32[]{:S(2)}) collective-permute-start(bf16[4,96,384]{2,1,0:T(8,128)(2,1)S(1)} %get-tuple-element.70), channel_id=1, source_target_pairs={{0,2},{1,3},{2,0},{3,1},{4,6},{5,7},{6,4},{7,5},{8,10},{9,11},{10,... | collective-permute-start | bytes 884744 | tf_op jit(solution)/shard_map/ppermute | solution.py:281
  63.6 9.0 %collective-permute-start.15 = (bf16[4,96,384]{2,1,0:T(8,128)(2,1)S(1)}, bf16[4,96,384]{2,1,0:T(8,128)(2,1)S(1)}, u32[]{:S(2)}, u32[]{:S(2)}) collective-permute-start(bf16[4,96,384]{2,1,0:T(8,128)(2,1)S(1)} %get-tuple-element.90), channel_id=1, source_target_pairs={{0,4},{4,0},{8,12},{12,8},{16,20},{20,16},{24,28},{28,24},{1,5},{5... | collective-permute-start | bytes 884744 | tf_op jit(solution)/shard_map/ppermute | solution.py:281
  72.1 7.7 %collective-permute-start.17 = (bf16[2,96,384]{2,1,0:T(8,128)(2,1)S(1)}, bf16[2,96,384]{2,1,0:T(8,128)(2,1)S(1)}, u32[]{:S(2)}, u32[]{:S(2)}) collective-permute-start(bf16[2,96,384]{2,1,0:T(8,128)(2,1)S(1)} %get-tuple-element.78), channel_id=1, source_target_pairs={{0,8},{4,12},{8,0},{12,4},{16,24},{20,28},{24,16},{28,20},{1,9},{5... | collective-permute-start | bytes 442376 | tf_op jit(solution)/shard_map/ppermute | solution.py:281
  72.7 9.1 %collective-permute-start.16 = (bf16[2,96,384]{2,1,0:T(8,128)(2,1)S(1)}, bf16[2,96,384]{2,1,0:T(8,128)(2,1)S(1)}, u32[]{:S(2)}, u32[]{:S(2)}) collective-permute-start(bf16[2,96,384]{2,1,0:T(8,128)(2,1)S(1)} %get-tuple-element.94), channel_id=1, source_target_pairs={{0,16},{4,20},{8,24},{12,28},{16,0},{20,4},{24,8},{28,12},{1,17},{... | collective-permute-start | bytes 442376 | tf_op jit(solution)/shard_map/ppermute | solution.py:281
  74.6 7.3 %collective-permute-start.10 = (bf16[4,32,384]{2,1,0:T(8,128)(2,1)S(1)}, bf16[4,32,384]{2,1,0:T(8,128)(2,1)S(1)}, u32[]{:S(2)}, u32[]{:S(2)}) collective-permute-start(bf16[4,32,384]{2,1,0:T(8,128)(2,1)S(1)} %get-tuple-element.72), channel_id=1, source_target_pairs={{0,2},{1,3},{2,0},{3,1},{4,6},{5,7},{6,4},{7,5},{8,10},{9,11},{10,... | collective-permute-start | bytes 294920 | tf_op jit(solution)/shard_map/ppermute | solution.py:281
  76.1 5.9 %collective-permute-start.11 = (bf16[4,32,384]{2,1,0:T(8,128)(2,1)S(1)}, bf16[4,32,384]{2,1,0:T(8,128)(2,1)S(1)}, u32[]{:S(2)}, u32[]{:S(2)}) collective-permute-start(bf16[4,32,384]{2,1,0:T(8,128)(2,1)S(1)} %get-tuple-element.73), channel_id=1, source_target_pairs={{0,4},{4,0},{8,12},{12,8},{16,20},{20,16},{24,28},{28,24},{1,5},{5... | collective-permute-start | bytes 294920 | tf_op jit(solution)/shard_map/ppermute | solution.py:281
  76.6 5.6 %collective-permute-start.12 = (bf16[4,32,384]{2,1,0:T(8,128)(2,1)S(1)}, bf16[4,32,384]{2,1,0:T(8,128)(2,1)S(1)}, u32[]{:S(2)}, u32[]{:S(2)}) collective-permute-start(bf16[4,32,384]{2,1,0:T(8,128)(2,1)S(1)} %get-tuple-element.74), channel_id=1, source_target_pairs={{0,6},{1,7},{2,4},{3,5},{4,2},{5,3},{6,0},{7,1},{8,14},{9,15},{10,... | collective-permute-start | bytes 294920 | tf_op jit(solution)/shard_map/ppermute | solution.py:377
  81.9 3.3 %copy-start.2 = (bf16[4,32,384]{2,1,0:T(8,128)(2,1)}, bf16[4,32,384]{2,1,0:T(8,128)(2,1)S(1)}, u32[]{:S(2)}) copy-start(bf16[4,32,384]{2,1,0:T(8,128)(2,1)S(1)} %collective-permute-done.10.refs_1_) | copy-start | bytes 294916
  81.9 3.2 %copy-start.3 = (bf16[4,32,384]{2,1,0:T(8,128)(2,1)}, bf16[4,32,384]{2,1,0:T(8,128)(2,1)S(1)}, u32[]{:S(2)}) copy-start(bf16[4,32,384]{2,1,0:T(8,128)(2,1)S(1)} %collective-permute-done.11.refs_2_) | copy-start | bytes 294916
  82.2 2.9 %copy-start.4 = (bf16[4,32,384]{2,1,0:T(8,128)(2,1)}, bf16[4,32,384]{2,1,0:T(8,128)(2,1)S(1)}, u32[]{:S(2)}) copy-start(bf16[4,32,384]{2,1,0:T(8,128)(2,1)S(1)} %collective-permute-done.12.refs_3_) | copy-start | bytes 294916
  82.2 4.9 %collective-permute-start.18 = (bf16[1,96,384]{2,1,0:T(8,128)(2,1)S(1)}, bf16[1,96,384]{2,1,0:T(8,128)(2,1)S(1)}, u32[]{:S(2)}, u32[]{:S(2)}) collective-permute-start(bf16[1,96,384]{2,1,0:T(8,128)(2,1)S(1)} %fusion.11), channel_id=1, source_target_pairs={{0,8},{4,12},{8,0},{12,4},{16,24},{20,28},{24,16},{28,20},{1,9},{5... | collective-permute-start | bytes 221192 | tf_op jit(solution)/shard_map/ppermute | solution.py:281
  83.1 6.0 %collective-permute-start.19 = (bf16[1,96,384]{2,1,0:T(8,128)(2,1)S(1)}, bf16[1,96,384]{2,1,0:T(8,128)(2,1)S(1)}, u32[]{:S(2)}, u32[]{:S(2)}) collective-permute-start(bf16[1,96,384]{2,1,0:T(8,128)(2,1)S(1)} %fusion.10), channel_id=1, source_target_pairs={{0,16},{4,20},{8,24},{12,28},{16,0},{20,4},{24,8},{28,12},{1,17},{... | collective-permute-start | bytes 221192 | tf_op jit(solution)/shard_map/ppermute | solution.py:281

commit v17 on v16

--- a/solution.py
+++ b/solution.py
@@ -140,8 +140,8 @@
         else:
             pair_grad = read_pair(work_ref, mask)
         pair_bf = pair_grad.astype(jnp.bfloat16)
-        for start in range(0, hidden_units, 2 * CHUNK):
-            units = pl.ds(start, 2 * CHUNK)
+        for start in range(0, hidden_units, CHUNK):
+            units = pl.ds(start, CHUNK)
             d_hidden = jnp.dot(pair_bf, down_ref[:, units], preferred_element_type=jnp.float32)
             d_pre_ref[at, units] = (d_hidden * slope_ref[at, units].astype(jnp.float32)).astype(jnp.bfloat16)
         if section > 0:
@@ -437,23 +437,17 @@
     take_down, take_up = [swap(part, *steps[core]) for part in given]
     keep_down, keep_up = keep_blocks(place, hidden, d_pre, normed_t, grad_t, places, block)
 
-    barrier = lax.optimization_barrier
     for phase, (step_down, step_up) in enumerate(zip(order_down, order_up)):
-        ending = phase == len(order_down) - 1
-        if not ending:
-            keep_up, give_up = halve(halves, step_up, keep_up, take_up)
-            take_up = swap(give_up, *step_up)
+        if phase == 2:
+            keep_up = going.hop_both(x, y, steps, halves, keep_up)
+        keep_up, give_up = halve(halves, step_up, keep_up, take_up)
+        take_up = swap(give_up, *step_up)
         keep_down, give_down = halve(halves, step_down, keep_down, take_down)
         if phase == 1:
             give_down = going.hop(core, steps, halves, give_down)
-        if phase == 2:
-            give_down = going.hop_both(x, y, steps, halves, give_down)
+        if phase == len(order_down) - 1:
+            going.parts, give_down = lax.optimization_barrier((going.parts, give_down))
         take_down = swap(give_down, *step_down)
-        if ending:
-            take_up, give_down = barrier((take_up, give_down))
-            keep_up, give_up = halve(halves, step_up, keep_up, take_up)
-            going.parts, give_up = barrier((going.parts, give_up))
-            take_up = swap(give_up, *step_up)
     return (settle(place, going), last_sum(keep_up, take_up), last_sum(keep_down, take_down))
 
 

time: 90.2 us -> 88.9 us (0.986)
  starting transfers between devices: 25.1 us -> 23.6 us
    ppermute x18, starting transfers between devices: 13.5 us -> 11.9 us  [swap(): return lax.ppermute(block, axis, pairs)]
  transfers between devices with their start and end apart: 21 -> 21, of which waited for: 14 -> 13; matrix products, arithmetic and copies ran while one was open for 3% -> 3% of each run, Pallas kernels for 18% -> 18%
where the time goes in v17:
time: 88.9 us; the launch traced here: 88.6 us
  waiting for transfers between devices  34.8 us (39%)
  Pallas kernels  25.5 us (29%)
  starting transfers between devices  23.6 us (27%)
  other arithmetic  3.52 us (4%)
  between operations  0.98 us (1%)
    ppermute x18, waiting for transfers between devices, swap(): return lax.ppermute(block, axis, pairs)  29.8 us
    ppermute x18, starting transfers between devices, swap(): return lax.ppermute(block, axis, pairs)  11.9 us
    pallas_call x1, Pallas kernels, backward(): pl.pallas_call(functools.partial(backward_kernel, *places), out_shape=out...  9.44 us
    pallas_call x1, Pallas kernels, forward(): pl.pallas_call(forward_kernel, out_shape=outs, in_specs=[spec(pltpu.VMEM)...  8.72 us
    all_to_all x1, starting transfers between devices, exchange(): lax.all_to_all(block, ('gx', 'gy'), split_axis=0, concat_axis=0, axis_ind...  7.44 us
    ppermute x2, starting transfers between devices, swap_both(): return lax.ppermute(block, ('gx', 'gy'), pairs)  4.21 us
    all_to_all x1, waiting for transfers between devices, exchange(): lax.all_to_all(block, ('gx', 'gy'), split_axis=0, concat_axis=0, axis_ind...  3.45 us
    pallas_call x1, Pallas kernels, keep_blocks(): pl.pallas_call(functools.partial(keep_kernel, *places), out_shape=[block]...  3.17 us
  transfers between devices with their start and end apart: 21, of which 13 were waited for; matrix products, arithmetic and copies ran while one was open for 3% of the time, Pallas kernels for 18%

profile of v17, /device:TPU:0, one launch (start us, length us, event | category | flops | bytes accessed | tf_op | source)
XLA Modules:
  0.0 88.6 jit_solution(16345613773906607403)
XLA Ops:
  0.6 7.4 %all-to-all-start = ((bf16[16,32,384]{2,1,0:T(8,128)(2,1)}), bf16[16,32,384]{2,1,0:T(8,128)(2,1)S(1)}, u32[]{:S(2)}, u32[]{:S(2)}) async-start(bf16[16,32,384]{2,1,0:T(8,128)(2,1)} %bitcast.100), calls=%async_computation | async-start | bytes 786432 | tf_op jit(solution)/shard_map/all_to_all | solution.py:40
  8.7 1.1 %collective-permute-done = bf16[2,2,2,1,32,384]{5,4,2,1,0,3:T(8,128)(2,1)S(1)} collective-permute-done((bf16[2,2,2,1,32,384]{5,4,2,1,0,3:T(8,128)(2,1)S(1)}, bf16[2,2,2,1,32,384]{5,4,2,1,0,3:T(8,128)(2,1)S(1)}, u32[]{:S(2)}, u32[]{:S(2)}) %collective-permute-start) | collective-permute-done | bytes 196640 | tf_op jit(solution)/shard_map/ppermute | solution.py:281
  9.9 2.8 %collective-permute-start.3 = (bf16[2,2,32,384]{3,2,1,0:T(8,128)(2,1)S(1)}, bf16[2,2,32,384]{3,2,1,0:T(8,128)(2,1)S(1)}, u32[]{:S(2)}, u32[]{:S(2)}) collective-permute-start(bf16[2,2,32,384]{3,2,1,0:T(8,128)(2,1)S(1)} %bitcast.105), channel_id=1, source_target_pairs={{0,6},{1,7},{2,4},{3,5},{4,2},{5,3},{6,0},{7,1},{8,14},{9,15},{10,... | collective-permute-start | bytes 294920 | tf_op jit(solution)/shard_map/ppermute | solution.py:377
  13.6 2.2 %shard_map.67.up_ref = bf16[768,1536]{1,0:T(8,128)(2,1)S(1)} custom-call(s32[2]{0:T(128)S(1)} %pad_add_fusion.place_ref, bf16[768,1536]{1,0:T(8,128)(2,1)} %source.1), custom_call_target="tpu_custom_call" | custom-call | bytes 4718592 | tf_op jit(solution)/shard_map/pallas_call | solution.py:207
  15.9 0.9 collective-permute-done.3
  16.7 2.0 %collective-permute-done.2 = bf16[2,2,32,384]{3,2,1,0:T(8,128)(2,1)S(1)} collective-permute-done((bf16[2,2,32,384]{3,2,1,0:T(8,128)(2,1)S(1)}, bf16[2,2,32,384]{3,2,1,0:T(8,128)(2,1)S(1)}, u32[]{:S(2)}, u32[]{:S(2)}) %collective-permute-start.2) | collective-permute-done | bytes 98336 | tf_op jit(solution)/shard_map/ppermute | solution.py:281
  18.9 3.5 %all-to-all-done.state_ref = bf16[16,32,384]{2,1,0:T(8,128)(2,1)S(1)} async-done(((bf16[16,32,384]{2,1,0:T(8,128)(2,1)}), bf16[16,32,384]{2,1,0:T(8,128)(2,1)S(1)}, u32[]{:S(2)}, u32[]{:S(2)}) %all-to-all-start) | async-done | bytes 393248 | tf_op jit(solution)/shard_map/all_to_all | solution.py:40
  22.6 8.7 %shard_map.68 = (bf16[16,32,384]{2,1,0:T(8,128)(2,1)S(1)}, bf16[1024,1536]{1,0:T(8,128)(2,1)S(1)}, bf16[1024,1536]{1,0:T(8,128)(2,1)S(1)}, bf16[1024,768]{1,0:T(...) custom-call(bf16[16,32,384]{2,1,0:T(8,128)(2,1)S(1)} %all-to-all-done.state_r, ...), custom_call_target="tpu_custom_call" | custom-call | flops 12079595520 | bytes 25165824 | tf_op jit(solution)/shard_map/pallas_call | solution.py:232
  31.4 2.0 %collective-permute-done.4 = bf16[8,32,384]{2,1,0:T(8,128)(2,1)S(1)} collective-permute-done((bf16[8,32,384]{2,1,0:T(8,128)(2,1)S(1)}, bf16[8,32,384]{2,1,0:T(8,128)(2,1)S(1)}, u32[]{:S(2)}, u32[]{:S(2)}) %collective-permute-start.4) | collective-permute-done | bytes 196640 | tf_op jit(solution)/shard_map/ppermute | solution.py:281
  33.4 9.4 %shard_map.69 = (bf16[1024,1536]{1,0:T(8,128)(2,1)S(1)}, bf16[768,1024]{1,0:T(8,128)(2,1)S(1)}, bf16[16,96,384]{2,1,0:T(8,128)(2,1)S(1)}, bf16[16,96,384]{2,1,0:T(8,128)(2,1)S(1)}) custom-call(s32[2]{0:T(128)S(1)} %pad_add_fusion.place_ref, bf16[16,32,384]{2,1,0:T(8,128)(2,1)S(1)} %pad_maximum_fusion.1.grad_ref, ...), custom_call_target="tpu_custom_call" | custom-call | flops 12079595520 | bytes 25165824 | tf_op jit(solution)/shard_map/pallas_call | solution.py:251
  43.4 3.2 %shard_map.70 = (bf16[16,96,384]{2,1,0:T(8,128)(2,1)S(1)}, bf16[16,96,384]{2,1,0:T(8,128)(2,1)S(1)}) custom-call(s32[2]{0:T(128)S(1)} %pad_add_fusion.place_ref, bf16[1024,1536]{1,0:T(8,128)(2,1)S(1)} %get-tuple-element.56.hidden_ref, bf16[1024,1536]{1,0:T(8,128)(2,1)S(1)} %get-tuple-element.63.d_pre_ref, ...), custom_call_target="tpu_custom_call" | custom-call | flops 2415919104 | bytes 12582912 | tf_op jit(solution)/shard_map/pallas_call | solution.py:267
  46.9 1.1 %collective-permute-start.7 = (bf16[8,96,384]{2,1,0:T(8,128)(2,1)S(1)}, bf16[8,96,384]{2,1,0:T(8,128)(2,1)S(1)}, u32[]{:S(2)}, u32[]{:S(2)}) collective-permute-start(bf16[8,96,384]{2,1,0:T(8,128)(2,1)S(1)} %get-tuple-element.86), channel_id=1, source_target_pairs={{0,4},{4,0},{8,12},{12,8},{16,20},{20,16},{24,28},{28,24},{1,5},{5... | collective-permute-start | bytes 1769480 | tf_op jit(solution)/shard_map/ppermute | solution.py:281
  48.4 1.2 %collective-permute-start.10 = (bf16[8,96,384]{2,1,0:T(8,128)(2,1)S(1)}, bf16[8,96,384]{2,1,0:T(8,128)(2,1)S(1)}, u32[]{:S(2)}, u32[]{:S(2)}) collective-permute-start(bf16[8,96,384]{2,1,0:T(8,128)(2,1)S(1)} %get-tuple-element.84), channel_id=1, source_target_pairs={{0,2},{1,3},{2,0},{3,1},{4,6},{5,7},{6,4},{7,5},{8,10},{9,11},{10,... | collective-permute-start | bytes 1769480 | tf_op jit(solution)/shard_map/ppermute | solution.py:281
  49.5 11.0 %collective-permute-done.5 = bf16[2,2,2,1,32,384]{5,4,2,1,0,3:T(8,128)(2,1)S(1)} collective-permute-done((bf16[2,2,2,1,32,384]{5,4,2,1,0,3:T(8,128)(2,1)S(1)}, bf16[2,2,2,1,32,384]{5,4,2,1,0,3:T(8,128)(2,1)S(1)}, u32[]{:S(2)}, u32[]{:S(2)}) %collective-permute-start.5) | collective-permute-done | bytes 196640 | tf_op jit(solution)/shard_map/ppermute | solution.py:281
  60.6 1.7 %collective-permute-done.7 = bf16[8,96,384]{2,1,0:T(8,128)(2,1)S(1)} collective-permute-done((bf16[8,96,384]{2,1,0:T(8,128)(2,1)S(1)}, bf16[8,96,384]{2,1,0:T(8,128)(2,1)S(1)}, u32[]{:S(2)}, u32[]{:S(2)}) %collective-permute-start.7) | collective-permute-done | bytes 589856 | tf_op jit(solution)/shard_map/ppermute | solution.py:281
  62.6 0.9 %collective-permute-done.10 = bf16[8,96,384]{2,1,0:T(8,128)(2,1)S(1)} collective-permute-done((bf16[8,96,384]{2,1,0:T(8,128)(2,1)S(1)}, bf16[8,96,384]{2,1,0:T(8,128)(2,1)S(1)}, u32[]{:S(2)}, u32[]{:S(2)}) %collective-permute-start.10) | collective-permute-done | bytes 589856 | tf_op jit(solution)/shard_map/ppermute | solution.py:281
  63.6 1.1 %collective-permute-start.16 = (bf16[4,96,384]{2,1,0:T(8,128)(2,1)S(1)}, bf16[4,96,384]{2,1,0:T(8,128)(2,1)S(1)}, u32[]{:S(2)}, u32[]{:S(2)}) collective-permute-start(bf16[4,96,384]{2,1,0:T(8,128)(2,1)S(1)} %get-tuple-element.87), channel_id=1, source_target_pairs={{0,4},{4,0},{8,12},{12,8},{16,20},{20,16},{24,28},{28,24},{1,5},{5... | collective-permute-start | bytes 884744 | tf_op jit(solution)/shard_map/ppermute | solution.py:281
  64.7 0.9 collective-permute-start.14
  65.6 0.7 fusion.14
  66.3 5.9 %collective-permute-done.16 = bf16[4,96,384]{2,1,0:T(8,128)(2,1)S(1)} collective-permute-done((bf16[4,96,384]{2,1,0:T(8,128)(2,1)S(1)}, bf16[4,96,384]{2,1,0:T(8,128)(2,1)S(1)}, u32[]{:S(2)}, u32[]{:S(2)}) %collective-permute-start.16) | collective-permute-done | bytes 294944 | tf_op jit(solution)/shard_map/ppermute | solution.py:281
  72.3 0.8 collective-permute-start.17
  73.2 1.6 %collective-permute-start.15 = (bf16[2,96,384]{2,1,0:T(8,128)(2,1)S(1)}, bf16[2,96,384]{2,1,0:T(8,128)(2,1)S(1)}, u32[]{:S(2)}, u32[]{:S(2)}) collective-permute-start(bf16[2,96,384]{2,1,0:T(8,128)(2,1)S(1)} %get-tuple-element.94), channel_id=1, source_target_pairs={{0,8},{4,12},{8,0},{12,4},{16,24},{20,28},{24,16},{28,20},{1,9},{5... | collective-permute-start | bytes 442376 | tf_op jit(solution)/shard_map/ppermute | solution.py:281
  74.8 1.5 %collective-permute-start.11 = (bf16[4,32,384]{2,1,0:T(8,128)(2,1)S(1)}, bf16[4,32,384]{2,1,0:T(8,128)(2,1)S(1)}, u32[]{:S(2)}, u32[]{:S(2)}) collective-permute-start(bf16[4,32,384]{2,1,0:T(8,128)(2,1)S(1)} %get-tuple-element.71), channel_id=1, source_target_pairs={{0,2},{1,3},{2,0},{3,1},{4,6},{5,7},{6,4},{7,5},{8,10},{9,11},{10,... | collective-permute-start | bytes 294920 | tf_op jit(solution)/shard_map/ppermute | solution.py:281
  76.8 1.4 %collective-permute-start.13 = (bf16[4,32,384]{2,1,0:T(8,128)(2,1)S(1)}, bf16[4,32,384]{2,1,0:T(8,128)(2,1)S(1)}, u32[]{:S(2)}, u32[]{:S(2)}) collective-permute-start(bf16[4,32,384]{2,1,0:T(8,128)(2,1)S(1)} %get-tuple-element.73), channel_id=1, source_target_pairs={{0,6},{1,7},{2,4},{3,5},{4,2},{5,3},{6,0},{7,1},{8,14},{9,15},{10,... | collective-permute-start | bytes 294920 | tf_op jit(solution)/shard_map/ppermute | solution.py:377
  78.3 1.5 %collective-permute-done.17 = bf16[2,96,384]{2,1,0:T(8,128)(2,1)S(1)} collective-permute-done((bf16[2,96,384]{2,1,0:T(8,128)(2,1)S(1)}, bf16[2,96,384]{2,1,0:T(8,128)(2,1)S(1)}, u32[]{:S(2)}, u32[]{:S(2)}) %collective-permute-start.17) | collective-permute-done | bytes 147488 | tf_op jit(solution)/shard_map/ppermute | solution.py:281
  79.9 1.7 %collective-permute-done.15 = bf16[2,96,384]{2,1,0:T(8,128)(2,1)S(1)} collective-permute-done((bf16[2,96,384]{2,1,0:T(8,128)(2,1)S(1)}, bf16[2,96,384]{2,1,0:T(8,128)(2,1)S(1)}, u32[]{:S(2)}, u32[]{:S(2)}) %collective-permute-start.15) | collective-permute-done | bytes 147488 | tf_op jit(solution)/shard_map/ppermute | solution.py:281
  81.7 0.7 collective-permute-done.13.refs_3_
  82.4 1.0 %collective-permute-start.19 = (bf16[1,96,384]{2,1,0:T(8,128)(2,1)S(1)}, bf16[1,96,384]{2,1,0:T(8,128)(2,1)S(1)}, u32[]{:S(2)}, u32[]{:S(2)}) collective-permute-start(bf16[1,96,384]{2,1,0:T(8,128)(2,1)S(1)} %fusion.12), channel_id=1, source_target_pairs={{0,16},{4,20},{8,24},{12,28},{16,0},{20,4},{24,8},{28,12},{1,17},{... | collective-permute-start | bytes 221192 | tf_op jit(solution)/shard_map/ppermute | solution.py:281
  83.4 1.9 %shard_map.71 = bf16[512,384]{1,0:T(8,128)(2,1)} custom-call(s32[2]{0:T(128)} %copy-done, bf16[4,32,384]{2,1,0:T(8,128)(2,1)} %get-tuple-element.77.refs_0_, bf16[4,32,384]{2,1,0:T(8,128)(2,1)} %copy-done.2, bf16[4,32,384]{2,1,0:T(8,128)(2,1)} %copy-done.3, bf16[4,32,384]{2,1,0:T(8,128)(2,1)} %copy-done.4), custom_call_target="tpu_custom_call" | custom-call | bytes 786432 | tf_op jit(solution)/shard_map/pallas_call | solution.py:383
  85.3 0.7 add_bitcast_fusion.1
  86.0 1.9 %collective-permute-done.19 = bf16[1,96,384]{2,1,0:T(8,128)(2,1)S(1)} collective-permute-done((bf16[1,96,384]{2,1,0:T(8,128)(2,1)S(1)}, bf16[1,96,384]{2,1,0:T(8,128)(2,1)S(1)}, u32[]{:S(2)}, u32[]{:S(2)}) %collective-permute-start.19) | collective-permute-done | bytes 73760 | tf_op jit(solution)/shard_map/ppermute | solution.py:281
  87.9 0.7 add_bitcast_fusion
  (50 shorter events, 4.5 us)
Async XLA Ops:
  0.6 7.6 %copy-start.1 = (bf16[512,384]{1,0:T(8,128)(2,1)S(1)}, bf16[512,384]{1,0:T(8,128)(2,1)}, u32[]{:S(2)}) copy-start(bf16[512,384]{1,0:T(8,128)(2,1)} %param.7) | copy-start | bytes 1179652
  0.6 21.7 %all-to-all-start = ((bf16[16,32,384]{2,1,0:T(8,128)(2,1)}), bf16[16,32,384]{2,1,0:T(8,128)(2,1)S(1)}, u32[]{:S(2)}, u32[]{:S(2)}) async-start(bf16[16,32,384]{2,1,0:T(8,128)(2,1)} %bitcast.100), calls=%async_computation | async-start | bytes 786432 | tf_op jit(solution)/shard_map/all_to_all | solution.py:40
  8.3 35.2 %copy-start = (s32[2]{0:T(128)}, s32[2]{0:T(128)S(1)}, u32[]{:S(2)}) copy-start(s32[2]{0:T(128)S(1)} %pad_add_fusion.place_ref) | copy-start | bytes 28
  8.3 1.5 %collective-permute-start = (bf16[2,2,2,1,32,384]{5,4,2,1,0,3:T(8,128)(2,1)S(1)}, bf16[2,2,2,1,32,384]{5,4,2,1,0,3:T(8,128)(2,1)S(1)}, u32[]{:S(2)}, u32[]{:S(2)}) collective-permute-start(bf16[2,2,2,1,32,384]{5,4,2,1,0,3:T(8,128)(2,1)S(1)} %get-tuple-element.109), channel_id=1, source_target_pairs={{0,1},{1,0},{2,3},{3,2},{4,5},{5,4},{6,7},{7,6},{8,9},{9,8},{10,11... | collective-permute-start | bytes 589832 | tf_op jit(solution)/shard_map/ppermute | solution.py:281
  9.9 6.8 %collective-permute-start.3 = (bf16[2,2,32,384]{3,2,1,0:T(8,128)(2,1)S(1)}, bf16[2,2,32,384]{3,2,1,0:T(8,128)(2,1)S(1)}, u32[]{:S(2)}, u32[]{:S(2)}) collective-permute-start(bf16[2,2,32,384]{3,2,1,0:T(8,128)(2,1)S(1)} %bitcast.105), channel_id=1, source_target_pairs={{0,6},{1,7},{2,4},{3,5},{4,2},{5,3},{6,0},{7,1},{8,14},{9,15},{10,... | collective-permute-start | bytes 294920 | tf_op jit(solution)/shard_map/ppermute | solution.py:377
  12.7 6.0 %collective-permute-start.2 = (bf16[2,2,32,384]{3,2,1,0:T(8,128)(2,1)S(1)}, bf16[2,2,32,384]{3,2,1,0:T(8,128)(2,1)S(1)}, u32[]{:S(2)}, u32[]{:S(2)}) collective-permute-start(bf16[2,2,32,384]{3,2,1,0:T(8,128)(2,1)S(1)} %bitcast.106), channel_id=1, source_target_pairs={{0,4},{4,0},{8,12},{12,8},{16,20},{20,16},{24,28},{28,24},{1,5},{5... | collective-permute-start | bytes 294920 | tf_op jit(solution)/shard_map/ppermute | solution.py:281
  13.4 5.4 %collective-permute-start.1 = (bf16[2,2,32,384]{3,2,1,0:T(8,128)(2,1)S(1)}, bf16[2,2,32,384]{3,2,1,0:T(8,128)(2,1)S(1)}, u32[]{:S(2)}, u32[]{:S(2)}) collective-permute-start(bf16[2,2,32,384]{3,2,1,0:T(8,128)(2,1)S(1)} %bitcast.107), channel_id=1, source_target_pairs={{0,2},{1,3},{2,0},{3,1},{4,6},{5,7},{6,4},{7,5},{8,10},{9,11},{10,... | collective-permute-start | bytes 294920 | tf_op jit(solution)/shard_map/ppermute | solution.py:281
  22.3 11.0 %collective-permute-start.4 = (bf16[8,32,384]{2,1,0:T(8,128)(2,1)S(1)}, bf16[8,32,384]{2,1,0:T(8,128)(2,1)S(1)}, u32[]{:S(2)}, u32[]{:S(2)}) collective-permute-start(bf16[8,32,384]{2,1,0:T(8,128)(2,1)S(1)} %get-tuple-element.54), channel_id=1, source_target_pairs={{0,16},{4,20},{8,24},{12,28},{16,0},{20,4},{24,8},{28,12},{1,17},{... | collective-permute-start | bytes 589832 | tf_op jit(solution)/shard_map/ppermute | solution.py:281
  42.8 3.8 %collective-permute-start.6 = (bf16[16,96,384]{2,1,0:T(8,128)(2,1)S(1)}, bf16[16,96,384]{2,1,0:T(8,128)(2,1)S(1)}, u32[]{:S(2)}, u32[]{:S(2)}) collective-permute-start(bf16[16,96,384]{2,1,0:T(8,128)(2,1)S(1)} %get-tuple-element.66), channel_id=1, source_target_pairs={{0,1},{1,0},{2,3},{3,2},{4,5},{5,4},{6,7},{7,6},{8,9},{9,8},{10,11... | collective-permute-start | bytes 3538952 | tf_op jit(solution)/shard_map/ppermute | solution.py:281
  42.9 5.1 %collective-permute-start.9 = (bf16[16,96,384]{2,1,0:T(8,128)(2,1)S(1)}, bf16[16,96,384]{2,1,0:T(8,128)(2,1)S(1)}, u32[]{:S(2)}, u32[]{:S(2)}) collective-permute-start(bf16[16,96,384]{2,1,0:T(8,128)(2,1)S(1)} %get-tuple-element.69), channel_id=1, source_target_pairs={{0,1},{1,0},{2,3},{3,2},{4,5},{5,4},{6,7},{7,6},{8,9},{9,8},{10,11... | collective-permute-start | bytes 3538952 | tf_op jit(solution)/shard_map/ppermute | solution.py:281
  46.9 15.4 %collective-permute-start.7 = (bf16[8,96,384]{2,1,0:T(8,128)(2,1)S(1)}, bf16[8,96,384]{2,1,0:T(8,128)(2,1)S(1)}, u32[]{:S(2)}, u32[]{:S(2)}) collective-permute-start(bf16[8,96,384]{2,1,0:T(8,128)(2,1)S(1)} %get-tuple-element.86), channel_id=1, source_target_pairs={{0,4},{4,0},{8,12},{12,8},{16,20},{20,16},{24,28},{28,24},{1,5},{5... | collective-permute-start | bytes 1769480 | tf_op jit(solution)/shard_map/ppermute | solution.py:281
  48.4 15.1 %collective-permute-start.10 = (bf16[8,96,384]{2,1,0:T(8,128)(2,1)S(1)}, bf16[8,96,384]{2,1,0:T(8,128)(2,1)S(1)}, u32[]{:S(2)}, u32[]{:S(2)}) collective-permute-start(bf16[8,96,384]{2,1,0:T(8,128)(2,1)S(1)} %get-tuple-element.84), channel_id=1, source_target_pairs={{0,2},{1,3},{2,0},{3,1},{4,6},{5,7},{6,4},{7,5},{8,10},{9,11},{10,... | collective-permute-start | bytes 1769480 | tf_op jit(solution)/shard_map/ppermute | solution.py:281
  49.5 11.0 %collective-permute-start.5 = (bf16[2,2,2,1,32,384]{5,4,2,1,0,3:T(8,128)(2,1)S(1)}, bf16[2,2,2,1,32,384]{5,4,2,1,0,3:T(8,128)(2,1)S(1)}, u32[]{:S(2)}, u32[]{:S(2)}) collective-permute-start(bf16[2,2,2,1,32,384]{5,4,2,1,0,3:T(8,128)(2,1)S(1)} %get-tuple-element.55), channel_id=1, source_target_pairs={{0,16},{4,20},{8,24},{12,28},{16,0},{20,4},{24,8},{28,12},{1,17},{... | collective-permute-start | bytes 589832 | tf_op jit(solution)/shard_map/ppermute | solution.py:281
  62.5 3.1 %collective-permute-start.8 = (bf16[2,2,2,32,384]{4,3,2,1,0:T(8,128)(2,1)S(1)}, bf16[2,2,2,32,384]{4,3,2,1,0:T(8,128)(2,1)S(1)}, u32[]{:S(2)}, u32[]{:S(2)}) collective-permute-start(bf16[2,2,2,32,384]{4,3,2,1,0:T(8,128)(2,1)S(1)} %bitcast.104), channel_id=1, source_target_pairs={{0,1},{1,0},{2,3},{3,2},{4,5},{5,4},{6,7},{7,6},{8,9},{9,8},{10,11... | collective-permute-start | bytes 589832 | tf_op jit(solution)/shard_map/ppermute | solution.py:281
  63.6 8.6 %collective-permute-start.16 = (bf16[4,96,384]{2,1,0:T(8,128)(2,1)S(1)}, bf16[4,96,384]{2,1,0:T(8,128)(2,1)S(1)}, u32[]{:S(2)}, u32[]{:S(2)}) collective-permute-start(bf16[4,96,384]{2,1,0:T(8,128)(2,1)S(1)} %get-tuple-element.87), channel_id=1, source_target_pairs={{0,4},{4,0},{8,12},{12,8},{16,20},{20,16},{24,28},{28,24},{1,5},{5... | collective-permute-start | bytes 884744 | tf_op jit(solution)/shard_map/ppermute | solution.py:281
  64.7 8.4 %collective-permute-start.14 = (bf16[4,96,384]{2,1,0:T(8,128)(2,1)S(1)}, bf16[4,96,384]{2,1,0:T(8,128)(2,1)S(1)}, u32[]{:S(2)}, u32[]{:S(2)}) collective-permute-start(bf16[4,96,384]{2,1,0:T(8,128)(2,1)S(1)} %get-tuple-element.75), channel_id=1, source_target_pairs={{0,2},{1,3},{2,0},{3,1},{4,6},{5,7},{6,4},{7,5},{8,10},{9,11},{10,... | collective-permute-start | bytes 884744 | tf_op jit(solution)/shard_map/ppermute | solution.py:281
  72.3 7.5 %collective-permute-start.17 = (bf16[2,96,384]{2,1,0:T(8,128)(2,1)S(1)}, bf16[2,96,384]{2,1,0:T(8,128)(2,1)S(1)}, u32[]{:S(2)}, u32[]{:S(2)}) collective-permute-start(bf16[2,96,384]{2,1,0:T(8,128)(2,1)S(1)} %get-tuple-element.92), channel_id=1, source_target_pairs={{0,16},{4,20},{8,24},{12,28},{16,0},{20,4},{24,8},{28,12},{1,17},{... | collective-permute-start | bytes 442376 | tf_op jit(solution)/shard_map/ppermute | solution.py:281
  73.2 8.5 %collective-permute-start.15 = (bf16[2,96,384]{2,1,0:T(8,128)(2,1)S(1)}, bf16[2,96,384]{2,1,0:T(8,128)(2,1)S(1)}, u32[]{:S(2)}, u32[]{:S(2)}) collective-permute-start(bf16[2,96,384]{2,1,0:T(8,128)(2,1)S(1)} %get-tuple-element.94), channel_id=1, source_target_pairs={{0,8},{4,12},{8,0},{12,4},{16,24},{20,28},{24,16},{28,20},{1,9},{5... | collective-permute-start | bytes 442376 | tf_op jit(solution)/shard_map/ppermute | solution.py:281
  74.8 6.9 %collective-permute-start.11 = (bf16[4,32,384]{2,1,0:T(8,128)(2,1)S(1)}, bf16[4,32,384]{2,1,0:T(8,128)(2,1)S(1)}, u32[]{:S(2)}, u32[]{:S(2)}) collective-permute-start(bf16[4,32,384]{2,1,0:T(8,128)(2,1)S(1)} %get-tuple-element.71), channel_id=1, source_target_pairs={{0,2},{1,3},{2,0},{3,1},{4,6},{5,7},{6,4},{7,5},{8,10},{9,11},{10,... | collective-permute-start | bytes 294920 | tf_op jit(solution)/shard_map/ppermute | solution.py:281
  76.3 5.4 %collective-permute-start.12 = (bf16[4,32,384]{2,1,0:T(8,128)(2,1)S(1)}, bf16[4,32,384]{2,1,0:T(8,128)(2,1)S(1)}, u32[]{:S(2)}, u32[]{:S(2)}) collective-permute-start(bf16[4,32,384]{2,1,0:T(8,128)(2,1)S(1)} %get-tuple-element.72), channel_id=1, source_target_pairs={{0,4},{4,0},{8,12},{12,8},{16,20},{20,16},{24,28},{28,24},{1,5},{5... | collective-permute-start | bytes 294920 | tf_op jit(solution)/shard_map/ppermute | solution.py:281
  76.8 5.5 %collective-permute-start.13 = (bf16[4,32,384]{2,1,0:T(8,128)(2,1)S(1)}, bf16[4,32,384]{2,1,0:T(8,128)(2,1)S(1)}, u32[]{:S(2)}, u32[]{:S(2)}) collective-permute-start(bf16[4,32,384]{2,1,0:T(8,128)(2,1)S(1)} %get-tuple-element.73), channel_id=1, source_target_pairs={{0,6},{1,7},{2,4},{3,5},{4,2},{5,3},{6,0},{7,1},{8,14},{9,15},{10,... | collective-permute-start | bytes 294920 | tf_op jit(solution)/shard_map/ppermute | solution.py:377
  79.8 5.5 %collective-permute-start.18 = (bf16[1,96,384]{2,1,0:T(8,128)(2,1)S(1)}, bf16[1,96,384]{2,1,0:T(8,128)(2,1)S(1)}, u32[]{:S(2)}, u32[]{:S(2)}) collective-permute-start(bf16[1,96,384]{2,1,0:T(8,128)(2,1)S(1)} %fusion.10), channel_id=1, source_target_pairs={{0,8},{4,12},{8,0},{12,4},{16,24},{20,28},{24,16},{28,20},{1,9},{5... | collective-permute-start | bytes 221192 | tf_op jit(solution)/shard_map/ppermute | solution.py:281
  81.7 1.7 %copy-start.2 = (bf16[4,32,384]{2,1,0:T(8,128)(2,1)}, bf16[4,32,384]{2,1,0:T(8,128)(2,1)S(1)}, u32[]{:S(2)}) copy-start(bf16[4,32,384]{2,1,0:T(8,128)(2,1)S(1)} %collective-permute-done.11.refs_1_) | copy-start | bytes 294916
  81.7 1.7 %copy-start.3 = (bf16[4,32,384]{2,1,0:T(8,128)(2,1)}, bf16[4,32,384]{2,1,0:T(8,128)(2,1)S(1)}, u32[]{:S(2)}) copy-start(bf16[4,32,384]{2,1,0:T(8,128)(2,1)S(1)} %collective-permute-done.12.refs_2_) | copy-start | bytes 294916
  82.4 1.0 %copy-start.4 = (bf16[4,32,384]{2,1,0:T(8,128)(2,1)}, bf16[4,32,384]{2,1,0:T(8,128)(2,1)S(1)}, u32[]{:S(2)}) copy-start(bf16[4,32,384]{2,1,0:T(8,128)(2,1)S(1)} %collective-permute-done.13.refs_3_) | copy-start | bytes 294916
  82.4 5.6 %collective-permute-start.19 = (bf16[1,96,384]{2,1,0:T(8,128)(2,1)S(1)}, bf16[1,96,384]{2,1,0:T(8,128)(2,1)S(1)}, u32[]{:S(2)}, u32[]{:S(2)}) collective-permute-start(bf16[1,96,384]{2,1,0:T(8,128)(2,1)S(1)} %fusion.12), channel_id=1, source_target_pairs={{0,16},{4,20},{8,24},{12,28},{16,0},{20,4},{24,8},{28,12},{1,17},{... | collective-permute-start | bytes 221192 | tf_op jit(solution)/shard_map/ppermute | solution.py:281

commit v18 on v11

--- a/solution.py
+++ b/solution.py
@@ -93,7 +93,7 @@
 
 def forward_kernel(
     state_ref, up_ref, down_hbm,
-    out_ref, hidden_ref, slope_ref, normed_ref, normed_t_ref, factor_ref, down_ref, work_ref, arrived
+    out_ref, hidden_ref, slope_ref, normed_ref, normed_t_ref, factor_ref, up_t_ref, down_ref, work_ref, arrived
 ):
     fetch_down = pltpu.make_async_copy(down_hbm, down_ref, arrived)
     fetch_down.start()
@@ -122,15 +122,17 @@
         mixed = (pair + contract_last(hidden_ref[at, :], down_ref[...])).astype(jnp.bfloat16)
         write_pair(work_ref if section < last else out_ref, mask, mixed)
         normed_t_ref[:, at] = normed.T
+        quarter = pl.ds(section * (hidden_units // len(MASKS)), hidden_units // len(MASKS))
+        up_t_ref[quarter, :] = up_ref[:, quarter].T
 
 
 def backward_kernel(
     places_down, places_up, place_ref, grad_ref, hidden_ref, slope_ref, normed_ref, normed_t_ref, factor_ref,
-    up_ref, down_ref, d_pre_ref, grad_t_ref, *rest
+    up_t_ref, down_ref, d_pre_ref, grad_t_ref, *rest
 ):
     blocks, work_ref = rest[:-1], rest[-1]
     pairs = MEMBERS // 2 * work_ref.shape[1]
-    hidden_units = up_ref.shape[1]
+    hidden_units = down_ref.shape[1]
     last = len(MASKS) - 1
     for section in range(last, -1, -1):
         mask = MASKS[section]
@@ -145,7 +147,7 @@
             d_hidden = jnp.dot(pair_bf, down_ref[:, units], preferred_element_type=jnp.float32)
             d_pre_ref[at, units] = (d_hidden * slope_ref[at, units].astype(jnp.float32)).astype(jnp.bfloat16)
         if section > 0:
-            d_norm = contract_last(d_pre_ref[at, :], up_ref[...])
+            d_norm = jnp.dot(d_pre_ref[at, :], up_t_ref[...], preferred_element_type=jnp.float32)
             normed = normed_ref[at, :].astype(jnp.float32)
             d_pair = factor_ref[at, :][:, :1] * (
                 d_norm
@@ -227,6 +229,7 @@
         pltpu.VMEM((total, depth), bf16),
         pltpu.VMEM((depth, total), bf16),
         pltpu.VMEM((total, LANES), jnp.float32),
+        pltpu.VMEM((units, depth), bf16),
         pltpu.VMEM(w_down.shape, bf16),
     ]
     return pl.pallas_call(
@@ -414,8 +417,7 @@
     coming.hop_both(x, y, steps, halves)
     up = load(place, w_up)
     state = coming.hop(z, steps, halves, state)
-    state, *kept, down = forward(state, up, w_down)
-    kept += [up, down]
+    state, *kept = forward(state, up, w_down)
     going = Journey(state.reshape(parts))
     grad = going.hop(z, steps, halves, coming.held)
     d_pre, grad_t, *given = backward(place, grad, kept, places, block)

time: 88.4 us -> 88.4 us (level)
  no operation moved by 1% of the time
where the time goes in v18:
time: 88.4 us; the launch traced here: 88.1 us
  waiting for transfers between devices  34.8 us (39%)
  Pallas kernels  25.5 us (29%)
  starting transfers between devices  22.7 us (26%)
  other arithmetic  3.53 us (4%)
  between operations  1 us (1%)
    ppermute x18, waiting for transfers between devices, swap(): return lax.ppermute(block, axis, pairs)  30.5 us
    ppermute x18, starting transfers between devices, swap(): return lax.ppermute(block, axis, pairs)  11.1 us
    pallas_call x1, Pallas kernels, backward(): pl.pallas_call(functools.partial(backward_kernel, *places), out_shape=out...  9.44 us
    pallas_call x1, Pallas kernels, forward(): pl.pallas_call(forward_kernel, out_shape=outs, in_specs=[spec(pltpu.VMEM)...  8.78 us
    all_to_all x1, starting transfers between devices, exchange(): lax.all_to_all(block, ('gx', 'gy'), split_axis=0, concat_axis=0, axis_ind...  7.44 us
    ppermute x2, starting transfers between devices, swap_both(): return lax.ppermute(block, ('gx', 'gy'), pairs)  4.21 us
    all_to_all x1, waiting for transfers between devices, exchange(): lax.all_to_all(block, ('gx', 'gy'), split_axis=0, concat_axis=0, axis_ind...  3.45 us
    pallas_call x1, Pallas kernels, keep_blocks(): pl.pallas_call(functools.partial(keep_kernel, *places), out_shape=[block]...  3.17 us
  transfers between devices with their start and end apart: 21, of which 13 were waited for; matrix products, arithmetic and copies ran while one was open for 3% of the time, Pallas kernels for 18%

profile of v18, /device:TPU:0, one launch (start us, length us, event | category | flops | bytes accessed | tf_op | source)
XLA Modules:
  0.0 88.1 jit_solution(1540796206632406207)
XLA Ops:
  0.6 7.4 %all-to-all-start = ((bf16[16,32,384]{2,1,0:T(8,128)(2,1)}), bf16[16,32,384]{2,1,0:T(8,128)(2,1)S(1)}, u32[]{:S(2)}, u32[]{:S(2)}) async-start(bf16[16,32,384]{2,1,0:T(8,128)(2,1)} %bitcast.98), calls=%async_computation | async-start | bytes 786432 | tf_op jit(solution)/shard_map/all_to_all | solution.py:40
  8.7 1.1 %collective-permute-done = bf16[2,2,2,1,32,384]{5,4,2,1,0,3:T(8,128)(2,1)S(1)} collective-permute-done((bf16[2,2,2,1,32,384]{5,4,2,1,0,3:T(8,128)(2,1)S(1)}, bf16[2,2,2,1,32,384]{5,4,2,1,0,3:T(8,128)(2,1)S(1)}, u32[]{:S(2)}, u32[]{:S(2)}) %collective-permute-start) | collective-permute-done | bytes 196640 | tf_op jit(solution)/shard_map/ppermute | solution.py:284
  9.9 2.8 %collective-permute-start.3 = (bf16[2,2,32,384]{3,2,1,0:T(8,128)(2,1)S(1)}, bf16[2,2,32,384]{3,2,1,0:T(8,128)(2,1)S(1)}, u32[]{:S(2)}, u32[]{:S(2)}) collective-permute-start(bf16[2,2,32,384]{3,2,1,0:T(8,128)(2,1)S(1)} %bitcast.103), channel_id=1, source_target_pairs={{0,6},{1,7},{2,4},{3,5},{4,2},{5,3},{6,0},{7,1},{8,14},{9,15},{10,... | collective-permute-start | bytes 294920 | tf_op jit(solution)/shard_map/ppermute | solution.py:373
  12.7 0.6 collective-permute-start.2
  13.6 2.2 %shard_map.67.up_ref = bf16[768,1536]{1,0:T(8,128)(2,1)S(1)} custom-call(s32[2]{0:T(128)S(1)} %pad_add_fusion.place_ref, bf16[768,1536]{1,0:T(8,128)(2,1)} %source.1), custom_call_target="tpu_custom_call" | custom-call | bytes 4718592 | tf_op jit(solution)/shard_map/pallas_call | solution.py:209
  15.9 0.9 collective-permute-done.3
  16.7 2.0 %collective-permute-done.2 = bf16[2,2,32,384]{3,2,1,0:T(8,128)(2,1)S(1)} collective-permute-done((bf16[2,2,32,384]{3,2,1,0:T(8,128)(2,1)S(1)}, bf16[2,2,32,384]{3,2,1,0:T(8,128)(2,1)S(1)}, u32[]{:S(2)}, u32[]{:S(2)}) %collective-permute-start.2) | collective-permute-done | bytes 98336 | tf_op jit(solution)/shard_map/ppermute | solution.py:284
  18.9 3.5 %all-to-all-done.state_ref = bf16[16,32,384]{2,1,0:T(8,128)(2,1)S(1)} async-done(((bf16[16,32,384]{2,1,0:T(8,128)(2,1)}), bf16[16,32,384]{2,1,0:T(8,128)(2,1)S(1)}, u32[]{:S(2)}, u32[]{:S(2)}) %all-to-all-start) | async-done | bytes 393248 | tf_op jit(solution)/shard_map/all_to_all | solution.py:40
  22.6 8.8 %shard_map.68 = (bf16[16,32,384]{2,1,0:T(8,128)(2,1)S(1)}, bf16[1024,1536]{1,0:T(8,128)(2,1)S(1)}, bf16[1024,1536]{1,0:T(8,128)(2,1)S(1)}, bf16[1024,768]{1,0:T(...) custom-call(bf16[16,32,384]{2,1,0:T(8,128)(2,1)S(1)} %all-to-all-don, ...), custom_call_target="tpu_custom_call" | custom-call | flops 12079595520 | bytes 25165824 | tf_op jit(solution)/shard_map/pallas_call | solution.py:235
  31.4 1.9 %collective-permute-done.4 = bf16[8,32,384]{2,1,0:T(8,128)(2,1)S(1)} collective-permute-done((bf16[8,32,384]{2,1,0:T(8,128)(2,1)S(1)}, bf16[8,32,384]{2,1,0:T(8,128)(2,1)S(1)}, u32[]{:S(2)}, u32[]{:S(2)}) %collective-permute-start.4) | collective-permute-done | bytes 196640 | tf_op jit(solution)/shard_map/ppermute | solution.py:284
  33.4 9.4 %shard_map.69 = (bf16[1024,1536]{1,0:T(8,128)(2,1)S(1)}, bf16[768,1024]{1,0:T(8,128)(2,1)S(1)}, bf16[16,96,384]{2,1,0:T(8,128)(2,1)S(1)}, bf16[16,96,384]{2,1,0:T(8,128)(2,1)S(1)}) custom-call(s32[2]{0:T(128)S(1)} %pad_add_fusion.place_ref, bf16[16,32,384]{2,1,0:T(8,128)(2,1)S(1)} %pad_maximum_fusion.1.grad_ref, ...), custom_call_target="tpu_custom_call" | custom-call | flops 12079595520 | bytes 25165824 | tf_op jit(solution)/shard_map/pallas_call | solution.py:254
  43.4 3.2 %shard_map.70 = (bf16[16,96,384]{2,1,0:T(8,128)(2,1)S(1)}, bf16[16,96,384]{2,1,0:T(8,128)(2,1)S(1)}) custom-call(s32[2]{0:T(128)S(1)} %pad_add_fusion.place_ref, bf16[1024,1536]{1,0:T(8,128)(2,1)S(1)} %get-tuple-element.57.hidden_ref, bf16[1024,1536]{1,0:T(8,128)(2,1)S(1)} %get-tuple-element.65.d_pre_ref, ...), custom_call_target="tpu_custom_call" | custom-call | flops 2415919104 | bytes 12582912 | tf_op jit(solution)/shard_map/pallas_call | solution.py:270
  46.9 1.1 %collective-permute-start.7 = (bf16[8,96,384]{2,1,0:T(8,128)(2,1)S(1)}, bf16[8,96,384]{2,1,0:T(8,128)(2,1)S(1)}, u32[]{:S(2)}, u32[]{:S(2)}) collective-permute-start(bf16[8,96,384]{2,1,0:T(8,128)(2,1)S(1)} %get-tuple-element.88), channel_id=1, source_target_pairs={{0,4},{4,0},{8,12},{12,8},{16,20},{20,16},{24,28},{28,24},{1,5},{5... | collective-permute-start | bytes 1769480 | tf_op jit(solution)/shard_map/ppermute | solution.py:284
  48.4 1.2 %collective-permute-start.15 = (bf16[8,96,384]{2,1,0:T(8,128)(2,1)S(1)}, bf16[8,96,384]{2,1,0:T(8,128)(2,1)S(1)}, u32[]{:S(2)}, u32[]{:S(2)}) collective-permute-start(bf16[8,96,384]{2,1,0:T(8,128)(2,1)S(1)} %get-tuple-element.86), channel_id=1, source_target_pairs={{0,2},{1,3},{2,0},{3,1},{4,6},{5,7},{6,4},{7,5},{8,10},{9,11},{10,... | collective-permute-start | bytes 1769480 | tf_op jit(solution)/shard_map/ppermute | solution.py:284
  49.5 11.1 %collective-permute-done.5 = bf16[2,2,2,1,32,384]{5,4,2,1,0,3:T(8,128)(2,1)S(1)} collective-permute-done((bf16[2,2,2,1,32,384]{5,4,2,1,0,3:T(8,128)(2,1)S(1)}, bf16[2,2,2,1,32,384]{5,4,2,1,0,3:T(8,128)(2,1)S(1)}, u32[]{:S(2)}, u32[]{:S(2)}) %collective-permute-start.5) | collective-permute-done | bytes 196640 | tf_op jit(solution)/shard_map/ppermute | solution.py:284
  60.7 1.6 %collective-permute-done.7 = bf16[8,96,384]{2,1,0:T(8,128)(2,1)S(1)} collective-permute-done((bf16[8,96,384]{2,1,0:T(8,128)(2,1)S(1)}, bf16[8,96,384]{2,1,0:T(8,128)(2,1)S(1)}, u32[]{:S(2)}, u32[]{:S(2)}) %collective-permute-start.7) | collective-permute-done | bytes 589856 | tf_op jit(solution)/shard_map/ppermute | solution.py:284
  62.6 0.9 %collective-permute-done.15 = bf16[8,96,384]{2,1,0:T(8,128)(2,1)S(1)} collective-permute-done((bf16[8,96,384]{2,1,0:T(8,128)(2,1)S(1)}, bf16[8,96,384]{2,1,0:T(8,128)(2,1)S(1)}, u32[]{:S(2)}, u32[]{:S(2)}) %collective-permute-start.15) | collective-permute-done | bytes 589856 | tf_op jit(solution)/shard_map/ppermute | solution.py:284
  63.6 1.1 %collective-permute-start.16 = (bf16[4,96,384]{2,1,0:T(8,128)(2,1)S(1)}, bf16[4,96,384]{2,1,0:T(8,128)(2,1)S(1)}, u32[]{:S(2)}, u32[]{:S(2)}) collective-permute-start(bf16[4,96,384]{2,1,0:T(8,128)(2,1)S(1)} %get-tuple-element.90), channel_id=1, source_target_pairs={{0,4},{4,0},{8,12},{12,8},{16,20},{20,16},{24,28},{28,24},{1,5},{5... | collective-permute-start | bytes 884744 | tf_op jit(solution)/shard_map/ppermute | solution.py:284
  64.7 0.9 collective-permute-start.9
  65.6 0.7 fusion.13
  66.3 5.9 %collective-permute-done.16 = bf16[4,96,384]{2,1,0:T(8,128)(2,1)S(1)} collective-permute-done((bf16[4,96,384]{2,1,0:T(8,128)(2,1)S(1)}, bf16[4,96,384]{2,1,0:T(8,128)(2,1)S(1)}, u32[]{:S(2)}, u32[]{:S(2)}) %collective-permute-start.16) | collective-permute-done | bytes 294944 | tf_op jit(solution)/shard_map/ppermute | solution.py:284
  72.4 0.6 collective-permute-done.9
  73.0 1.8 %collective-permute-start.13 = (bf16[2,96,384]{2,1,0:T(8,128)(2,1)S(1)}, bf16[2,96,384]{2,1,0:T(8,128)(2,1)S(1)}, u32[]{:S(2)}, u32[]{:S(2)}) collective-permute-start(bf16[2,96,384]{2,1,0:T(8,128)(2,1)S(1)} %get-tuple-element.76), channel_id=1, source_target_pairs={{0,16},{4,20},{8,24},{12,28},{16,0},{20,4},{24,8},{28,12},{1,17},{... | collective-permute-start | bytes 442376 | tf_op jit(solution)/shard_map/ppermute | solution.py:284
  74.8 1.5 %collective-permute-start.10 = (bf16[4,32,384]{2,1,0:T(8,128)(2,1)S(1)}, bf16[4,32,384]{2,1,0:T(8,128)(2,1)S(1)}, u32[]{:S(2)}, u32[]{:S(2)}) collective-permute-start(bf16[4,32,384]{2,1,0:T(8,128)(2,1)S(1)} %get-tuple-element.72), channel_id=1, source_target_pairs={{0,2},{1,3},{2,0},{3,1},{4,6},{5,7},{6,4},{7,5},{8,10},{9,11},{10,... | collective-permute-start | bytes 294920 | tf_op jit(solution)/shard_map/ppermute | solution.py:284
  76.3 0.6 collective-permute-start.11
  76.9 1.4 %collective-permute-start.12 = (bf16[4,32,384]{2,1,0:T(8,128)(2,1)S(1)}, bf16[4,32,384]{2,1,0:T(8,128)(2,1)S(1)}, u32[]{:S(2)}, u32[]{:S(2)}) collective-permute-start(bf16[4,32,384]{2,1,0:T(8,128)(2,1)S(1)} %get-tuple-element.74), channel_id=1, source_target_pairs={{0,6},{1,7},{2,4},{3,5},{4,2},{5,3},{6,0},{7,1},{8,14},{9,15},{10,... | collective-permute-start | bytes 294920 | tf_op jit(solution)/shard_map/ppermute | solution.py:373
  78.3 0.9 %collective-permute-done.17 = bf16[2,96,384]{2,1,0:T(8,128)(2,1)S(1)} collective-permute-done((bf16[2,96,384]{2,1,0:T(8,128)(2,1)S(1)}, bf16[2,96,384]{2,1,0:T(8,128)(2,1)S(1)}, u32[]{:S(2)}, u32[]{:S(2)}) %collective-permute-start.17) | collective-permute-done | bytes 147488 | tf_op jit(solution)/shard_map/ppermute | solution.py:284
  79.7 3.3 %collective-permute-done.13 = bf16[2,96,384]{2,1,0:T(8,128)(2,1)S(1)} collective-permute-done((bf16[2,96,384]{2,1,0:T(8,128)(2,1)S(1)}, bf16[2,96,384]{2,1,0:T(8,128)(2,1)S(1)}, u32[]{:S(2)}, u32[]{:S(2)}) %collective-permute-start.13) | collective-permute-done | bytes 147488 | tf_op jit(solution)/shard_map/ppermute | solution.py:284
  83.6 1.9 %shard_map.71 = bf16[512,384]{1,0:T(8,128)(2,1)} custom-call(s32[2]{0:T(128)} %copy-done, bf16[4,32,384]{2,1,0:T(8,128)(2,1)} %get-tuple-element.77.refs_0_, bf16[4,32,384]{2,1,0:T(8,128)(2,1)} %copy-done.2, bf16[4,32,384]{2,1,0:T(8,128)(2,1)} %copy-done.3, bf16[4,32,384]{2,1,0:T(8,128)(2,1)} %copy-done.4), custom_call_target="tpu_custom_call" | custom-call | bytes 786432 | tf_op jit(solution)/shard_map/pallas_call | solution.py:379
  85.6 0.7 add_bitcast_fusion.1
  86.3 1.1 %collective-permute-done.19 = bf16[1,96,384]{2,1,0:T(8,128)(2,1)S(1)} collective-permute-done((bf16[1,96,384]{2,1,0:T(8,128)(2,1)S(1)}, bf16[1,96,384]{2,1,0:T(8,128)(2,1)S(1)}, u32[]{:S(2)}, u32[]{:S(2)}) %collective-permute-start.19) | collective-permute-done | bytes 73760 | tf_op jit(solution)/shard_map/ppermute | solution.py:284
  87.4 0.7 add_bitcast_fusion
  (50 shorter events, 4.4 us)
Async XLA Ops:
  0.6 7.6 %copy-start.1 = (bf16[512,384]{1,0:T(8,128)(2,1)S(1)}, bf16[512,384]{1,0:T(8,128)(2,1)}, u32[]{:S(2)}) copy-start(bf16[512,384]{1,0:T(8,128)(2,1)} %param.7) | copy-start | bytes 1179652
  0.6 21.7 %all-to-all-start = ((bf16[16,32,384]{2,1,0:T(8,128)(2,1)}), bf16[16,32,384]{2,1,0:T(8,128)(2,1)S(1)}, u32[]{:S(2)}, u32[]{:S(2)}) async-start(bf16[16,32,384]{2,1,0:T(8,128)(2,1)} %bitcast.98), calls=%async_computation | async-start | bytes 786432 | tf_op jit(solution)/shard_map/all_to_all | solution.py:40
  8.3 35.2 %copy-start = (s32[2]{0:T(128)}, s32[2]{0:T(128)S(1)}, u32[]{:S(2)}) copy-start(s32[2]{0:T(128)S(1)} %pad_add_fusion.place_ref) | copy-start | bytes 28
  8.3 1.5 %collective-permute-start = (bf16[2,2,2,1,32,384]{5,4,2,1,0,3:T(8,128)(2,1)S(1)}, bf16[2,2,2,1,32,384]{5,4,2,1,0,3:T(8,128)(2,1)S(1)}, u32[]{:S(2)}, u32[]{:S(2)}) collective-permute-start(bf16[2,2,2,1,32,384]{5,4,2,1,0,3:T(8,128)(2,1)S(1)} %get-tuple-element.111), channel_id=1, source_target_pairs={{0,1},{1,0},{2,3},{3,2},{4,5},{5,4},{6,7},{7,6},{8,9},{9,8},{10,11... | collective-permute-start | bytes 589832 | tf_op jit(solution)/shard_map/ppermute | solution.py:284
  9.9 6.8 %collective-permute-start.3 = (bf16[2,2,32,384]{3,2,1,0:T(8,128)(2,1)S(1)}, bf16[2,2,32,384]{3,2,1,0:T(8,128)(2,1)S(1)}, u32[]{:S(2)}, u32[]{:S(2)}) collective-permute-start(bf16[2,2,32,384]{3,2,1,0:T(8,128)(2,1)S(1)} %bitcast.103), channel_id=1, source_target_pairs={{0,6},{1,7},{2,4},{3,5},{4,2},{5,3},{6,0},{7,1},{8,14},{9,15},{10,... | collective-permute-start | bytes 294920 | tf_op jit(solution)/shard_map/ppermute | solution.py:373
  12.7 6.0 %collective-permute-start.2 = (bf16[2,2,32,384]{3,2,1,0:T(8,128)(2,1)S(1)}, bf16[2,2,32,384]{3,2,1,0:T(8,128)(2,1)S(1)}, u32[]{:S(2)}, u32[]{:S(2)}) collective-permute-start(bf16[2,2,32,384]{3,2,1,0:T(8,128)(2,1)S(1)} %bitcast.104), channel_id=1, source_target_pairs={{0,4},{4,0},{8,12},{12,8},{16,20},{20,16},{24,28},{28,24},{1,5},{5... | collective-permute-start | bytes 294920 | tf_op jit(solution)/shard_map/ppermute | solution.py:284
  13.4 5.4 %collective-permute-start.1 = (bf16[2,2,32,384]{3,2,1,0:T(8,128)(2,1)S(1)}, bf16[2,2,32,384]{3,2,1,0:T(8,128)(2,1)S(1)}, u32[]{:S(2)}, u32[]{:S(2)}) collective-permute-start(bf16[2,2,32,384]{3,2,1,0:T(8,128)(2,1)S(1)} %bitcast.105), channel_id=1, source_target_pairs={{0,2},{1,3},{2,0},{3,1},{4,6},{5,7},{6,4},{7,5},{8,10},{9,11},{10,... | collective-permute-start | bytes 294920 | tf_op jit(solution)/shard_map/ppermute | solution.py:284
  22.3 11.0 %collective-permute-start.4 = (bf16[8,32,384]{2,1,0:T(8,128)(2,1)S(1)}, bf16[8,32,384]{2,1,0:T(8,128)(2,1)S(1)}, u32[]{:S(2)}, u32[]{:S(2)}) collective-permute-start(bf16[8,32,384]{2,1,0:T(8,128)(2,1)S(1)} %get-tuple-element.55), channel_id=1, source_target_pairs={{0,16},{4,20},{8,24},{12,28},{16,0},{20,4},{24,8},{28,12},{1,17},{... | collective-permute-start | bytes 589832 | tf_op jit(solution)/shard_map/ppermute | solution.py:284
  42.8 3.8 %collective-permute-start.6 = (bf16[16,96,384]{2,1,0:T(8,128)(2,1)S(1)}, bf16[16,96,384]{2,1,0:T(8,128)(2,1)S(1)}, u32[]{:S(2)}, u32[]{:S(2)}) collective-permute-start(bf16[16,96,384]{2,1,0:T(8,128)(2,1)S(1)} %get-tuple-element.68), channel_id=1, source_target_pairs={{0,1},{1,0},{2,3},{3,2},{4,5},{5,4},{6,7},{7,6},{8,9},{9,8},{10,11... | collective-permute-start | bytes 3538952 | tf_op jit(solution)/shard_map/ppermute | solution.py:284
  42.9 5.1 %collective-permute-start.14 = (bf16[16,96,384]{2,1,0:T(8,128)(2,1)S(1)}, bf16[16,96,384]{2,1,0:T(8,128)(2,1)S(1)}, u32[]{:S(2)}, u32[]{:S(2)}) collective-permute-start(bf16[16,96,384]{2,1,0:T(8,128)(2,1)S(1)} %get-tuple-element.82), channel_id=1, source_target_pairs={{0,1},{1,0},{2,3},{3,2},{4,5},{5,4},{6,7},{7,6},{8,9},{9,8},{10,11... | collective-permute-start | bytes 3538952 | tf_op jit(solution)/shard_map/ppermute | solution.py:284
  46.9 15.4 %collective-permute-start.7 = (bf16[8,96,384]{2,1,0:T(8,128)(2,1)S(1)}, bf16[8,96,384]{2,1,0:T(8,128)(2,1)S(1)}, u32[]{:S(2)}, u32[]{:S(2)}) collective-permute-start(bf16[8,96,384]{2,1,0:T(8,128)(2,1)S(1)} %get-tuple-element.88), channel_id=1, source_target_pairs={{0,4},{4,0},{8,12},{12,8},{16,20},{20,16},{24,28},{28,24},{1,5},{5... | collective-permute-start | bytes 1769480 | tf_op jit(solution)/shard_map/ppermute | solution.py:284
  48.4 15.1 %collective-permute-start.15 = (bf16[8,96,384]{2,1,0:T(8,128)(2,1)S(1)}, bf16[8,96,384]{2,1,0:T(8,128)(2,1)S(1)}, u32[]{:S(2)}, u32[]{:S(2)}) collective-permute-start(bf16[8,96,384]{2,1,0:T(8,128)(2,1)S(1)} %get-tuple-element.86), channel_id=1, source_target_pairs={{0,2},{1,3},{2,0},{3,1},{4,6},{5,7},{6,4},{7,5},{8,10},{9,11},{10,... | collective-permute-start | bytes 1769480 | tf_op jit(solution)/shard_map/ppermute | solution.py:284
  49.5 11.1 %collective-permute-start.5 = (bf16[2,2,2,1,32,384]{5,4,2,1,0,3:T(8,128)(2,1)S(1)}, bf16[2,2,2,1,32,384]{5,4,2,1,0,3:T(8,128)(2,1)S(1)}, u32[]{:S(2)}, u32[]{:S(2)}) collective-permute-start(bf16[2,2,2,1,32,384]{5,4,2,1,0,3:T(8,128)(2,1)S(1)} %get-tuple-element.56), channel_id=1, source_target_pairs={{0,16},{4,20},{8,24},{12,28},{16,0},{20,4},{24,8},{28,12},{1,17},{... | collective-permute-start | bytes 589832 | tf_op jit(solution)/shard_map/ppermute | solution.py:284
  62.5 3.1 %collective-permute-start.8 = (bf16[2,2,2,32,384]{4,3,2,1,0:T(8,128)(2,1)S(1)}, bf16[2,2,2,32,384]{4,3,2,1,0:T(8,128)(2,1)S(1)}, u32[]{:S(2)}, u32[]{:S(2)}) collective-permute-start(bf16[2,2,2,32,384]{4,3,2,1,0:T(8,128)(2,1)S(1)} %bitcast.102), channel_id=1, source_target_pairs={{0,1},{1,0},{2,3},{3,2},{4,5},{5,4},{6,7},{7,6},{8,9},{9,8},{10,11... | collective-permute-start | bytes 589832 | tf_op jit(solution)/shard_map/ppermute | solution.py:284
  63.6 8.6 %collective-permute-start.16 = (bf16[4,96,384]{2,1,0:T(8,128)(2,1)S(1)}, bf16[4,96,384]{2,1,0:T(8,128)(2,1)S(1)}, u32[]{:S(2)}, u32[]{:S(2)}) collective-permute-start(bf16[4,96,384]{2,1,0:T(8,128)(2,1)S(1)} %get-tuple-element.90), channel_id=1, source_target_pairs={{0,4},{4,0},{8,12},{12,8},{16,20},{20,16},{24,28},{28,24},{1,5},{5... | collective-permute-start | bytes 884744 | tf_op jit(solution)/shard_map/ppermute | solution.py:284
  64.7 8.3 %collective-permute-start.9 = (bf16[4,96,384]{2,1,0:T(8,128)(2,1)S(1)}, bf16[4,96,384]{2,1,0:T(8,128)(2,1)S(1)}, u32[]{:S(2)}, u32[]{:S(2)}) collective-permute-start(bf16[4,96,384]{2,1,0:T(8,128)(2,1)S(1)} %get-tuple-element.70), channel_id=1, source_target_pairs={{0,2},{1,3},{2,0},{3,1},{4,6},{5,7},{6,4},{7,5},{8,10},{9,11},{10,... | collective-permute-start | bytes 884744 | tf_op jit(solution)/shard_map/ppermute | solution.py:284
  72.3 6.9 %collective-permute-start.17 = (bf16[2,96,384]{2,1,0:T(8,128)(2,1)S(1)}, bf16[2,96,384]{2,1,0:T(8,128)(2,1)S(1)}, u32[]{:S(2)}, u32[]{:S(2)}) collective-permute-start(bf16[2,96,384]{2,1,0:T(8,128)(2,1)S(1)} %get-tuple-element.94), channel_id=1, source_target_pairs={{0,8},{4,12},{8,0},{12,4},{16,24},{20,28},{24,16},{28,20},{1,9},{5... | collective-permute-start | bytes 442376 | tf_op jit(solution)/shard_map/ppermute | solution.py:284
  73.0 9.9 %collective-permute-start.13 = (bf16[2,96,384]{2,1,0:T(8,128)(2,1)S(1)}, bf16[2,96,384]{2,1,0:T(8,128)(2,1)S(1)}, u32[]{:S(2)}, u32[]{:S(2)}) collective-permute-start(bf16[2,96,384]{2,1,0:T(8,128)(2,1)S(1)} %get-tuple-element.76), channel_id=1, source_target_pairs={{0,16},{4,20},{8,24},{12,28},{16,0},{20,4},{24,8},{28,12},{1,17},{... | collective-permute-start | bytes 442376 | tf_op jit(solution)/shard_map/ppermute | solution.py:284
  74.8 8.1 %collective-permute-start.10 = (bf16[4,32,384]{2,1,0:T(8,128)(2,1)S(1)}, bf16[4,32,384]{2,1,0:T(8,128)(2,1)S(1)}, u32[]{:S(2)}, u32[]{:S(2)}) collective-permute-start(bf16[4,32,384]{2,1,0:T(8,128)(2,1)S(1)} %get-tuple-element.72), channel_id=1, source_target_pairs={{0,2},{1,3},{2,0},{3,1},{4,6},{5,7},{6,4},{7,5},{8,10},{9,11},{10,... | collective-permute-start | bytes 294920 | tf_op jit(solution)/shard_map/ppermute | solution.py:284
  76.3 6.7 %collective-permute-start.11 = (bf16[4,32,384]{2,1,0:T(8,128)(2,1)S(1)}, bf16[4,32,384]{2,1,0:T(8,128)(2,1)S(1)}, u32[]{:S(2)}, u32[]{:S(2)}) collective-permute-start(bf16[4,32,384]{2,1,0:T(8,128)(2,1)S(1)} %get-tuple-element.73), channel_id=1, source_target_pairs={{0,4},{4,0},{8,12},{12,8},{16,20},{20,16},{24,28},{28,24},{1,5},{5... | collective-permute-start | bytes 294920 | tf_op jit(solution)/shard_map/ppermute | solution.py:284
  76.9 6.1 %collective-permute-start.12 = (bf16[4,32,384]{2,1,0:T(8,128)(2,1)S(1)}, bf16[4,32,384]{2,1,0:T(8,128)(2,1)S(1)}, u32[]{:S(2)}, u32[]{:S(2)}) collective-permute-start(bf16[4,32,384]{2,1,0:T(8,128)(2,1)S(1)} %get-tuple-element.74), channel_id=1, source_target_pairs={{0,6},{1,7},{2,4},{3,5},{4,2},{5,3},{6,0},{7,1},{8,14},{9,15},{10,... | collective-permute-start | bytes 294920 | tf_op jit(solution)/shard_map/ppermute | solution.py:373
  79.2 6.4 %collective-permute-start.18 = (bf16[1,96,384]{2,1,0:T(8,128)(2,1)S(1)}, bf16[1,96,384]{2,1,0:T(8,128)(2,1)S(1)}, u32[]{:S(2)}, u32[]{:S(2)}) collective-permute-start(bf16[1,96,384]{2,1,0:T(8,128)(2,1)S(1)} %fusion.9), channel_id=1, source_target_pairs={{0,16},{4,20},{8,24},{12,28},{16,0},{20,4},{24,8},{28,12},{1,17},{... | collective-permute-start | bytes 221192 | tf_op jit(solution)/shard_map/ppermute | solution.py:284
  82.9 0.6 copy-start.2
  83.0 0.6 copy-start.3
  83.0 0.7 copy-start.4
  83.0 4.4 %collective-permute-start.19 = (bf16[1,96,384]{2,1,0:T(8,128)(2,1)S(1)}, bf16[1,96,384]{2,1,0:T(8,128)(2,1)S(1)}, u32[]{:S(2)}, u32[]{:S(2)}) collective-permute-start(bf16[1,96,384]{2,1,0:T(8,128)(2,1)S(1)} %fusion.11), channel_id=1, source_target_pairs={{0,8},{4,12},{8,0},{12,4},{16,24},{20,28},{24,16},{28,20},{1,9},{5... | collective-permute-start | bytes 221192 | tf_op jit(solution)/shard_map/ppermute | solution.py:284

commit v19 on v16

--- a/solution.py
+++ b/solution.py
@@ -140,8 +140,8 @@
         else:
             pair_grad = read_pair(work_ref, mask)
         pair_bf = pair_grad.astype(jnp.bfloat16)
-        for start in range(0, hidden_units, 2 * CHUNK):
-            units = pl.ds(start, 2 * CHUNK)
+        for start in range(0, hidden_units, CHUNK):
+            units = pl.ds(start, CHUNK)
             d_hidden = jnp.dot(pair_bf, down_ref[:, units], preferred_element_type=jnp.float32)
             d_pre_ref[at, units] = (d_hidden * slope_ref[at, units].astype(jnp.float32)).astype(jnp.bfloat16)
         if section > 0:
@@ -270,9 +270,7 @@
         in_specs=[spec(pltpu.SMEM)] + [spec(pltpu.VMEM)] * 4,
         out_specs=[spec(pltpu.VMEM)] * 2,
         compiler_params=pltpu.CompilerParams(vmem_limit_bytes=KEEP_BYTES),
-        cost_estimate=pl.CostEstimate(
-            flops=2 * total * depth * units, bytes_accessed=8 * total * units, transcendentals=0
-        ),
+        cost_estimate=pl.CostEstimate(flops=0, bytes_accessed=0, transcendentals=0),
     )(place, *in_vmem(hidden, d_pre, normed_t, grad_t))
 
 
@@ -386,7 +384,7 @@
         in_specs=[spec(pltpu.SMEM)] + [spec(pltpu.VMEM)] * len(parts),
         out_specs=spec(pltpu.HBM),
         scratch_shapes=[pltpu.SemaphoreType.DMA((MEMBERS,))],
-        cost_estimate=pl.CostEstimate(flops=0, bytes_accessed=4 * MEMBERS * rows * width, transcendentals=0),
+        cost_estimate=pl.CostEstimate(flops=0, bytes_accessed=0, transcendentals=0),
     )(place, *parts)
 
 

time: 90.2 us -> 90.2 us (level)
  no operation moved by 1% of the time
where the time goes in v19:
time: 90.2 us; the launch traced here: 89.9 us
  waiting for transfers between devices  34.5 us (38%)
  Pallas kernels  25.5 us (28%)
  starting transfers between devices  25.1 us (28%)
  other arithmetic  3.52 us (4%)
  between operations  0.98 us (1%)
    ppermute x18, waiting for transfers between devices, swap(): return lax.ppermute(block, axis, pairs)  29.9 us
    ppermute x18, starting transfers between devices, swap(): return lax.ppermute(block, axis, pairs)  13.5 us
    pallas_call x1, Pallas kernels, backward(): pl.pallas_call(functools.partial(backward_kernel, *places), out_shape=out...  9.44 us
    pallas_call x1, Pallas kernels, forward(): pl.pallas_call(forward_kernel, out_shape=outs, in_specs=[spec(pltpu.VMEM)...  8.72 us
    all_to_all x1, starting transfers between devices, exchange(): lax.all_to_all(block, ('gx', 'gy'), split_axis=0, concat_axis=0, axis_ind...  7.44 us
    ppermute x2, starting transfers between devices, swap_both(): return lax.ppermute(block, ('gx', 'gy'), pairs)  4.21 us
    all_to_all x1, waiting for transfers between devices, exchange(): lax.all_to_all(block, ('gx', 'gy'), split_axis=0, concat_axis=0, axis_ind...  3.45 us
    pallas_call x1, Pallas kernels, keep_blocks(): pl.pallas_call(functools.partial(keep_kernel, *places), out_shape=[block]...  3.17 us
  transfers between devices with their start and end apart: 21, of which 14 were waited for; matrix products, arithmetic and copies ran while one was open for 3% of the time, Pallas kernels for 18%

profile of v19, /device:TPU:0, one launch (start us, length us, event | category | flops | bytes accessed | tf_op | source)
XLA Modules:
  0.0 89.9 jit_solution(6811471403119276839)
XLA Ops:
  0.6 7.4 %all-to-all-start = ((bf16[16,32,384]{2,1,0:T(8,128)(2,1)}), bf16[16,32,384]{2,1,0:T(8,128)(2,1)S(1)}, u32[]{:S(2)}, u32[]{:S(2)}) async-start(bf16[16,32,384]{2,1,0:T(8,128)(2,1)} %bitcast.98), calls=%async_computation | async-start | bytes 786432 | tf_op jit(solution)/shard_map/all_to_all | solution.py:40
  8.7 1.1 %collective-permute-done = bf16[2,2,2,1,32,384]{5,4,2,1,0,3:T(8,128)(2,1)S(1)} collective-permute-done((bf16[2,2,2,1,32,384]{5,4,2,1,0,3:T(8,128)(2,1)S(1)}, bf16[2,2,2,1,32,384]{5,4,2,1,0,3:T(8,128)(2,1)S(1)}, u32[]{:S(2)}, u32[]{:S(2)}) %collective-permute-start) | collective-permute-done | bytes 196640 | tf_op jit(solution)/shard_map/ppermute | solution.py:279
  9.9 2.8 %collective-permute-start.3 = (bf16[2,2,32,384]{3,2,1,0:T(8,128)(2,1)S(1)}, bf16[2,2,32,384]{3,2,1,0:T(8,128)(2,1)S(1)}, u32[]{:S(2)}, u32[]{:S(2)}) collective-permute-start(bf16[2,2,32,384]{3,2,1,0:T(8,128)(2,1)S(1)} %bitcast.103), channel_id=1, source_target_pairs={{0,6},{1,7},{2,4},{3,5},{4,2},{5,3},{6,0},{7,1},{8,14},{9,15},{10,... | collective-permute-start | bytes 294920 | tf_op jit(solution)/shard_map/ppermute | solution.py:375
  12.7 0.6 collective-permute-start.2
  13.6 2.2 %shard_map.67.up_ref = bf16[768,1536]{1,0:T(8,128)(2,1)S(1)} custom-call(s32[2]{0:T(128)S(1)} %pad_add_fusion.place_ref, bf16[768,1536]{1,0:T(8,128)(2,1)} %source.1), custom_call_target="tpu_custom_call" | custom-call | bytes 4718592 | tf_op jit(solution)/shard_map/pallas_call | solution.py:207
  15.9 0.9 collective-permute-done.3
  16.7 2.0 %collective-permute-done.2 = bf16[2,2,32,384]{3,2,1,0:T(8,128)(2,1)S(1)} collective-permute-done((bf16[2,2,32,384]{3,2,1,0:T(8,128)(2,1)S(1)}, bf16[2,2,32,384]{3,2,1,0:T(8,128)(2,1)S(1)}, u32[]{:S(2)}, u32[]{:S(2)}) %collective-permute-start.2) | collective-permute-done | bytes 98336 | tf_op jit(solution)/shard_map/ppermute | solution.py:279
  18.9 3.5 %all-to-all-done.state_ref = bf16[16,32,384]{2,1,0:T(8,128)(2,1)S(1)} async-done(((bf16[16,32,384]{2,1,0:T(8,128)(2,1)}), bf16[16,32,384]{2,1,0:T(8,128)(2,1)S(1)}, u32[]{:S(2)}, u32[]{:S(2)}) %all-to-all-start) | async-done | bytes 393248 | tf_op jit(solution)/shard_map/all_to_all | solution.py:40
  22.6 8.7 %shard_map.68 = (bf16[16,32,384]{2,1,0:T(8,128)(2,1)S(1)}, bf16[1024,1536]{1,0:T(8,128)(2,1)S(1)}, bf16[1024,1536]{1,0:T(8,128)(2,1)S(1)}, bf16[1024,768]{1,0:T(...) custom-call(bf16[16,32,384]{2,1,0:T(8,128)(2,1)S(1)} %all-to-all-done.state_r, ...), custom_call_target="tpu_custom_call" | custom-call | flops 12079595520 | bytes 25165824 | tf_op jit(solution)/shard_map/pallas_call | solution.py:232
  31.4 2.0 %collective-permute-done.4 = bf16[8,32,384]{2,1,0:T(8,128)(2,1)S(1)} collective-permute-done((bf16[8,32,384]{2,1,0:T(8,128)(2,1)S(1)}, bf16[8,32,384]{2,1,0:T(8,128)(2,1)S(1)}, u32[]{:S(2)}, u32[]{:S(2)}) %collective-permute-start.4) | collective-permute-done | bytes 196640 | tf_op jit(solution)/shard_map/ppermute | solution.py:279
  33.4 9.4 %shard_map.69 = (bf16[1024,1536]{1,0:T(8,128)(2,1)S(1)}, bf16[768,1024]{1,0:T(8,128)(2,1)S(1)}, bf16[16,96,384]{2,1,0:T(8,128)(2,1)S(1)}, bf16[16,96,384]{2,1,0:T(8,128)(2,1)S(1)}) custom-call(s32[2]{0:T(128)S(1)} %pad_add_fusion.place_ref, bf16[16,32,384]{2,1,0:T(8,128)(2,1)S(1)} %pad_maximum_fusion.1.grad_ref, ...), custom_call_target="tpu_custom_call" | custom-call | flops 12079595520 | bytes 25165824 | tf_op jit(solution)/shard_map/pallas_call | solution.py:251
  43.4 3.2 %shard_map.70 = (bf16[16,96,384]{2,1,0:T(8,128)(2,1)S(1)}, bf16[16,96,384]{2,1,0:T(8,128)(2,1)S(1)}) custom-call(s32[2]{0:T(128)S(1)} %pad_add_fusion.place_ref, bf16[1024,1536]{1,0:T(8,128)(2,1)S(1)} %get-tuple-element.57.hidden_ref, bf16[1024,1536]{1,0:T(8,128)(2,1)S(1)} %get-tuple-element.64.d_pre_ref, ...), custom_call_target="tpu_custom_call" | custom-call | tf_op jit(solution)/shard_map/pallas_call | solution.py:267
  46.9 1.1 %collective-permute-start.7 = (bf16[8,96,384]{2,1,0:T(8,128)(2,1)S(1)}, bf16[8,96,384]{2,1,0:T(8,128)(2,1)S(1)}, u32[]{:S(2)}, u32[]{:S(2)}) collective-permute-start(bf16[8,96,384]{2,1,0:T(8,128)(2,1)S(1)} %get-tuple-element.88), channel_id=1, source_target_pairs={{0,4},{4,0},{8,12},{12,8},{16,20},{20,16},{24,28},{28,24},{1,5},{5... | collective-permute-start | bytes 1769480 | tf_op jit(solution)/shard_map/ppermute | solution.py:279
  48.4 1.2 %collective-permute-start.14 = (bf16[8,96,384]{2,1,0:T(8,128)(2,1)S(1)}, bf16[8,96,384]{2,1,0:T(8,128)(2,1)S(1)}, u32[]{:S(2)}, u32[]{:S(2)}) collective-permute-start(bf16[8,96,384]{2,1,0:T(8,128)(2,1)S(1)} %get-tuple-element.86), channel_id=1, source_target_pairs={{0,2},{1,3},{2,0},{3,1},{4,6},{5,7},{6,4},{7,5},{8,10},{9,11},{10,... | collective-permute-start | bytes 1769480 | tf_op jit(solution)/shard_map/ppermute | solution.py:279
  49.5 11.0 %collective-permute-done.5 = bf16[2,2,2,1,32,384]{5,4,2,1,0,3:T(8,128)(2,1)S(1)} collective-permute-done((bf16[2,2,2,1,32,384]{5,4,2,1,0,3:T(8,128)(2,1)S(1)}, bf16[2,2,2,1,32,384]{5,4,2,1,0,3:T(8,128)(2,1)S(1)}, u32[]{:S(2)}, u32[]{:S(2)}) %collective-permute-start.5) | collective-permute-done | bytes 196640 | tf_op jit(solution)/shard_map/ppermute | solution.py:279
  60.6 1.7 %collective-permute-done.7 = bf16[8,96,384]{2,1,0:T(8,128)(2,1)S(1)} collective-permute-done((bf16[8,96,384]{2,1,0:T(8,128)(2,1)S(1)}, bf16[8,96,384]{2,1,0:T(8,128)(2,1)S(1)}, u32[]{:S(2)}, u32[]{:S(2)}) %collective-permute-start.7) | collective-permute-done | bytes 589856 | tf_op jit(solution)/shard_map/ppermute | solution.py:279
  62.6 0.8 collective-permute-start.9
  63.6 1.4 %collective-permute-start.15 = (bf16[4,96,384]{2,1,0:T(8,128)(2,1)S(1)}, bf16[4,96,384]{2,1,0:T(8,128)(2,1)S(1)}, u32[]{:S(2)}, u32[]{:S(2)}) collective-permute-start(bf16[4,96,384]{2,1,0:T(8,128)(2,1)S(1)} %get-tuple-element.90), channel_id=1, source_target_pairs={{0,4},{4,0},{8,12},{12,8},{16,20},{20,16},{24,28},{28,24},{1,5},{5... | collective-permute-start | bytes 884744 | tf_op jit(solution)/shard_map/ppermute | solution.py:279
  65.0 0.7 fusion.13
  65.7 6.3 %collective-permute-done.9 = bf16[4,96,384]{2,1,0:T(8,128)(2,1)S(1)} collective-permute-done((bf16[4,96,384]{2,1,0:T(8,128)(2,1)S(1)}, bf16[4,96,384]{2,1,0:T(8,128)(2,1)S(1)}, u32[]{:S(2)}, u32[]{:S(2)}) %collective-permute-start.9) | collective-permute-done | bytes 294944 | tf_op jit(solution)/shard_map/ppermute | solution.py:279
  72.7 1.8 %collective-permute-start.16 = (bf16[2,96,384]{2,1,0:T(8,128)(2,1)S(1)}, bf16[2,96,384]{2,1,0:T(8,128)(2,1)S(1)}, u32[]{:S(2)}, u32[]{:S(2)}) collective-permute-start(bf16[2,96,384]{2,1,0:T(8,128)(2,1)S(1)} %get-tuple-element.94), channel_id=1, source_target_pairs={{0,16},{4,20},{8,24},{12,28},{16,0},{20,4},{24,8},{28,12},{1,17},{... | collective-permute-start | bytes 442376 | tf_op jit(solution)/shard_map/ppermute | solution.py:279
  74.6 1.5 %collective-permute-start.10 = (bf16[4,32,384]{2,1,0:T(8,128)(2,1)S(1)}, bf16[4,32,384]{2,1,0:T(8,128)(2,1)S(1)}, u32[]{:S(2)}, u32[]{:S(2)}) collective-permute-start(bf16[4,32,384]{2,1,0:T(8,128)(2,1)S(1)} %get-tuple-element.72), channel_id=1, source_target_pairs={{0,2},{1,3},{2,0},{3,1},{4,6},{5,7},{6,4},{7,5},{8,10},{9,11},{10,... | collective-permute-start | bytes 294920 | tf_op jit(solution)/shard_map/ppermute | solution.py:279
  76.1 0.6 collective-permute-start.11
  76.6 1.4 %collective-permute-start.12 = (bf16[4,32,384]{2,1,0:T(8,128)(2,1)S(1)}, bf16[4,32,384]{2,1,0:T(8,128)(2,1)S(1)}, u32[]{:S(2)}, u32[]{:S(2)}) collective-permute-start(bf16[4,32,384]{2,1,0:T(8,128)(2,1)S(1)} %get-tuple-element.74), channel_id=1, source_target_pairs={{0,6},{1,7},{2,4},{3,5},{4,2},{5,3},{6,0},{7,1},{8,14},{9,15},{10,... | collective-permute-start | bytes 294920 | tf_op jit(solution)/shard_map/ppermute | solution.py:375
  78.1 1.7 %collective-permute-done.17 = bf16[2,96,384]{2,1,0:T(8,128)(2,1)S(1)} collective-permute-done((bf16[2,96,384]{2,1,0:T(8,128)(2,1)S(1)}, bf16[2,96,384]{2,1,0:T(8,128)(2,1)S(1)}, u32[]{:S(2)}, u32[]{:S(2)}) %collective-permute-start.17) | collective-permute-done | bytes 147488 | tf_op jit(solution)/shard_map/ppermute | solution.py:279
  79.7 2.1 %collective-permute-done.16 = bf16[2,96,384]{2,1,0:T(8,128)(2,1)S(1)} collective-permute-done((bf16[2,96,384]{2,1,0:T(8,128)(2,1)S(1)}, bf16[2,96,384]{2,1,0:T(8,128)(2,1)S(1)}, u32[]{:S(2)}, u32[]{:S(2)}) %collective-permute-start.16) | collective-permute-done | bytes 147488 | tf_op jit(solution)/shard_map/ppermute | solution.py:279
  82.2 0.9 %collective-permute-start.18 = (bf16[1,96,384]{2,1,0:T(8,128)(2,1)S(1)}, bf16[1,96,384]{2,1,0:T(8,128)(2,1)S(1)}, u32[]{:S(2)}, u32[]{:S(2)}) collective-permute-start(bf16[1,96,384]{2,1,0:T(8,128)(2,1)S(1)} %fusion.11), channel_id=1, source_target_pairs={{0,8},{4,12},{8,0},{12,4},{16,24},{20,28},{24,16},{28,20},{1,9},{5... | collective-permute-start | bytes 221192 | tf_op jit(solution)/shard_map/ppermute | solution.py:279
  83.1 2.0 %collective-permute-start.19 = (bf16[1,96,384]{2,1,0:T(8,128)(2,1)S(1)}, bf16[1,96,384]{2,1,0:T(8,128)(2,1)S(1)}, u32[]{:S(2)}, u32[]{:S(2)}) collective-permute-start(bf16[1,96,384]{2,1,0:T(8,128)(2,1)S(1)} %fusion.10), channel_id=1, source_target_pairs={{0,16},{4,20},{8,24},{12,28},{16,0},{20,4},{24,8},{28,12},{1,17},{... | collective-permute-start | bytes 221192 | tf_op jit(solution)/shard_map/ppermute | solution.py:279
  85.2 1.9 %shard_map.71 = bf16[512,384]{1,0:T(8,128)(2,1)} custom-call(s32[2]{0:T(128)} %copy-done, bf16[4,32,384]{2,1,0:T(8,128)(2,1)} %get-tuple-element.80.refs_0_, bf16[4,32,384]{2,1,0:T(8,128)(2,1)} %copy-done.2, bf16[4,32,384]{2,1,0:T(8,128)(2,1)} %copy-done.3, bf16[4,32,384]{2,1,0:T(8,128)(2,1)} %copy-done.4), custom_call_target="tpu_custom_call" | custom-call | tf_op jit(solution)/shard_map/pallas_call | solution.py:381
  87.1 0.7 add_bitcast_fusion.1
  87.8 1.4 %collective-permute-done.19 = bf16[1,96,384]{2,1,0:T(8,128)(2,1)S(1)} collective-permute-done((bf16[1,96,384]{2,1,0:T(8,128)(2,1)S(1)}, bf16[1,96,384]{2,1,0:T(8,128)(2,1)S(1)}, u32[]{:S(2)}, u32[]{:S(2)}) %collective-permute-start.19) | collective-permute-done | bytes 73760 | tf_op jit(solution)/shard_map/ppermute | solution.py:279
  89.2 0.7 add_bitcast_fusion
  (50 shorter events, 4.2 us)
Async XLA Ops:
  0.6 7.6 %copy-start.1 = (bf16[512,384]{1,0:T(8,128)(2,1)S(1)}, bf16[512,384]{1,0:T(8,128)(2,1)}, u32[]{:S(2)}) copy-start(bf16[512,384]{1,0:T(8,128)(2,1)} %param.7) | copy-start | bytes 1179652
  0.6 21.7 %all-to-all-start = ((bf16[16,32,384]{2,1,0:T(8,128)(2,1)}), bf16[16,32,384]{2,1,0:T(8,128)(2,1)S(1)}, u32[]{:S(2)}, u32[]{:S(2)}) async-start(bf16[16,32,384]{2,1,0:T(8,128)(2,1)} %bitcast.98), calls=%async_computation | async-start | bytes 786432 | tf_op jit(solution)/shard_map/all_to_all | solution.py:40
  8.3 35.2 %copy-start = (s32[2]{0:T(128)}, s32[2]{0:T(128)S(1)}, u32[]{:S(2)}) copy-start(s32[2]{0:T(128)S(1)} %pad_add_fusion.place_ref) | copy-start | bytes 28
  8.3 1.5 %collective-permute-start = (bf16[2,2,2,1,32,384]{5,4,2,1,0,3:T(8,128)(2,1)S(1)}, bf16[2,2,2,1,32,384]{5,4,2,1,0,3:T(8,128)(2,1)S(1)}, u32[]{:S(2)}, u32[]{:S(2)}) collective-permute-start(bf16[2,2,2,1,32,384]{5,4,2,1,0,3:T(8,128)(2,1)S(1)} %get-tuple-element.111), channel_id=1, source_target_pairs={{0,1},{1,0},{2,3},{3,2},{4,5},{5,4},{6,7},{7,6},{8,9},{9,8},{10,11... | collective-permute-start | bytes 589832 | tf_op jit(solution)/shard_map/ppermute | solution.py:279
  9.9 6.8 %collective-permute-start.3 = (bf16[2,2,32,384]{3,2,1,0:T(8,128)(2,1)S(1)}, bf16[2,2,32,384]{3,2,1,0:T(8,128)(2,1)S(1)}, u32[]{:S(2)}, u32[]{:S(2)}) collective-permute-start(bf16[2,2,32,384]{3,2,1,0:T(8,128)(2,1)S(1)} %bitcast.103), channel_id=1, source_target_pairs={{0,6},{1,7},{2,4},{3,5},{4,2},{5,3},{6,0},{7,1},{8,14},{9,15},{10,... | collective-permute-start | bytes 294920 | tf_op jit(solution)/shard_map/ppermute | solution.py:375
  12.7 6.0 %collective-permute-start.2 = (bf16[2,2,32,384]{3,2,1,0:T(8,128)(2,1)S(1)}, bf16[2,2,32,384]{3,2,1,0:T(8,128)(2,1)S(1)}, u32[]{:S(2)}, u32[]{:S(2)}) collective-permute-start(bf16[2,2,32,384]{3,2,1,0:T(8,128)(2,1)S(1)} %bitcast.104), channel_id=1, source_target_pairs={{0,4},{4,0},{8,12},{12,8},{16,20},{20,16},{24,28},{28,24},{1,5},{5... | collective-permute-start | bytes 294920 | tf_op jit(solution)/shard_map/ppermute | solution.py:279
  13.4 5.4 %collective-permute-start.1 = (bf16[2,2,32,384]{3,2,1,0:T(8,128)(2,1)S(1)}, bf16[2,2,32,384]{3,2,1,0:T(8,128)(2,1)S(1)}, u32[]{:S(2)}, u32[]{:S(2)}) collective-permute-start(bf16[2,2,32,384]{3,2,1,0:T(8,128)(2,1)S(1)} %bitcast.105), channel_id=1, source_target_pairs={{0,2},{1,3},{2,0},{3,1},{4,6},{5,7},{6,4},{7,5},{8,10},{9,11},{10,... | collective-permute-start | bytes 294920 | tf_op jit(solution)/shard_map/ppermute | solution.py:279
  22.3 11.0 %collective-permute-start.4 = (bf16[8,32,384]{2,1,0:T(8,128)(2,1)S(1)}, bf16[8,32,384]{2,1,0:T(8,128)(2,1)S(1)}, u32[]{:S(2)}, u32[]{:S(2)}) collective-permute-start(bf16[8,32,384]{2,1,0:T(8,128)(2,1)S(1)} %get-tuple-element.55), channel_id=1, source_target_pairs={{0,16},{4,20},{8,24},{12,28},{16,0},{20,4},{24,8},{28,12},{1,17},{... | collective-permute-start | bytes 589832 | tf_op jit(solution)/shard_map/ppermute | solution.py:279
  42.8 3.8 %collective-permute-start.6 = (bf16[16,96,384]{2,1,0:T(8,128)(2,1)S(1)}, bf16[16,96,384]{2,1,0:T(8,128)(2,1)S(1)}, u32[]{:S(2)}, u32[]{:S(2)}) collective-permute-start(bf16[16,96,384]{2,1,0:T(8,128)(2,1)S(1)} %get-tuple-element.67), channel_id=1, source_target_pairs={{0,1},{1,0},{2,3},{3,2},{4,5},{5,4},{6,7},{7,6},{8,9},{9,8},{10,11... | collective-permute-start | bytes 3538952 | tf_op jit(solution)/shard_map/ppermute | solution.py:279
  42.9 5.1 %collective-permute-start.13 = (bf16[16,96,384]{2,1,0:T(8,128)(2,1)S(1)}, bf16[16,96,384]{2,1,0:T(8,128)(2,1)S(1)}, u32[]{:S(2)}, u32[]{:S(2)}) collective-permute-start(bf16[16,96,384]{2,1,0:T(8,128)(2,1)S(1)} %get-tuple-element.76), channel_id=1, source_target_pairs={{0,1},{1,0},{2,3},{3,2},{4,5},{5,4},{6,7},{7,6},{8,9},{9,8},{10,11... | collective-permute-start | bytes 3538952 | tf_op jit(solution)/shard_map/ppermute | solution.py:279
  46.9 15.4 %collective-permute-start.7 = (bf16[8,96,384]{2,1,0:T(8,128)(2,1)S(1)}, bf16[8,96,384]{2,1,0:T(8,128)(2,1)S(1)}, u32[]{:S(2)}, u32[]{:S(2)}) collective-permute-start(bf16[8,96,384]{2,1,0:T(8,128)(2,1)S(1)} %get-tuple-element.88), channel_id=1, source_target_pairs={{0,4},{4,0},{8,12},{12,8},{16,20},{20,16},{24,28},{28,24},{1,5},{5... | collective-permute-start | bytes 1769480 | tf_op jit(solution)/shard_map/ppermute | solution.py:279
  48.4 15.1 %collective-permute-start.14 = (bf16[8,96,384]{2,1,0:T(8,128)(2,1)S(1)}, bf16[8,96,384]{2,1,0:T(8,128)(2,1)S(1)}, u32[]{:S(2)}, u32[]{:S(2)}) collective-permute-start(bf16[8,96,384]{2,1,0:T(8,128)(2,1)S(1)} %get-tuple-element.86), channel_id=1, source_target_pairs={{0,2},{1,3},{2,0},{3,1},{4,6},{5,7},{6,4},{7,5},{8,10},{9,11},{10,... | collective-permute-start | bytes 1769480 | tf_op jit(solution)/shard_map/ppermute | solution.py:279
  49.5 11.0 %collective-permute-start.5 = (bf16[2,2,2,1,32,384]{5,4,2,1,0,3:T(8,128)(2,1)S(1)}, bf16[2,2,2,1,32,384]{5,4,2,1,0,3:T(8,128)(2,1)S(1)}, u32[]{:S(2)}, u32[]{:S(2)}) collective-permute-start(bf16[2,2,2,1,32,384]{5,4,2,1,0,3:T(8,128)(2,1)S(1)} %get-tuple-element.56), channel_id=1, source_target_pairs={{0,16},{4,20},{8,24},{12,28},{16,0},{20,4},{24,8},{28,12},{1,17},{... | collective-permute-start | bytes 589832 | tf_op jit(solution)/shard_map/ppermute | solution.py:279
  62.5 2.5 %collective-permute-start.8 = (bf16[2,2,2,32,384]{4,3,2,1,0:T(8,128)(2,1)S(1)}, bf16[2,2,2,32,384]{4,3,2,1,0:T(8,128)(2,1)S(1)}, u32[]{:S(2)}, u32[]{:S(2)}) collective-permute-start(bf16[2,2,2,32,384]{4,3,2,1,0:T(8,128)(2,1)S(1)} %bitcast.102), channel_id=1, source_target_pairs={{0,1},{1,0},{2,3},{3,2},{4,5},{5,4},{6,7},{7,6},{8,9},{9,8},{10,11... | collective-permute-start | bytes 589832 | tf_op jit(solution)/shard_map/ppermute | solution.py:279
  62.6 9.4 %collective-permute-start.9 = (bf16[4,96,384]{2,1,0:T(8,128)(2,1)S(1)}, bf16[4,96,384]{2,1,0:T(8,128)(2,1)S(1)}, u32[]{:S(2)}, u32[]{:S(2)}) collective-permute-start(bf16[4,96,384]{2,1,0:T(8,128)(2,1)S(1)} %get-tuple-element.70), channel_id=1, source_target_pairs={{0,2},{1,3},{2,0},{3,1},{4,6},{5,7},{6,4},{7,5},{8,10},{9,11},{10,... | collective-permute-start | bytes 884744 | tf_op jit(solution)/shard_map/ppermute | solution.py:279
  63.6 9.0 %collective-permute-start.15 = (bf16[4,96,384]{2,1,0:T(8,128)(2,1)S(1)}, bf16[4,96,384]{2,1,0:T(8,128)(2,1)S(1)}, u32[]{:S(2)}, u32[]{:S(2)}) collective-permute-start(bf16[4,96,384]{2,1,0:T(8,128)(2,1)S(1)} %get-tuple-element.90), channel_id=1, source_target_pairs={{0,4},{4,0},{8,12},{12,8},{16,20},{20,16},{24,28},{28,24},{1,5},{5... | collective-permute-start | bytes 884744 | tf_op jit(solution)/shard_map/ppermute | solution.py:279
  72.1 7.7 %collective-permute-start.17 = (bf16[2,96,384]{2,1,0:T(8,128)(2,1)S(1)}, bf16[2,96,384]{2,1,0:T(8,128)(2,1)S(1)}, u32[]{:S(2)}, u32[]{:S(2)}) collective-permute-start(bf16[2,96,384]{2,1,0:T(8,128)(2,1)S(1)} %get-tuple-element.78), channel_id=1, source_target_pairs={{0,8},{4,12},{8,0},{12,4},{16,24},{20,28},{24,16},{28,20},{1,9},{5... | collective-permute-start | bytes 442376 | tf_op jit(solution)/shard_map/ppermute | solution.py:279
  72.7 9.1 %collective-permute-start.16 = (bf16[2,96,384]{2,1,0:T(8,128)(2,1)S(1)}, bf16[2,96,384]{2,1,0:T(8,128)(2,1)S(1)}, u32[]{:S(2)}, u32[]{:S(2)}) collective-permute-start(bf16[2,96,384]{2,1,0:T(8,128)(2,1)S(1)} %get-tuple-element.94), channel_id=1, source_target_pairs={{0,16},{4,20},{8,24},{12,28},{16,0},{20,4},{24,8},{28,12},{1,17},{... | collective-permute-start | bytes 442376 | tf_op jit(solution)/shard_map/ppermute | solution.py:279
  74.6 7.3 %collective-permute-start.10 = (bf16[4,32,384]{2,1,0:T(8,128)(2,1)S(1)}, bf16[4,32,384]{2,1,0:T(8,128)(2,1)S(1)}, u32[]{:S(2)}, u32[]{:S(2)}) collective-permute-start(bf16[4,32,384]{2,1,0:T(8,128)(2,1)S(1)} %get-tuple-element.72), channel_id=1, source_target_pairs={{0,2},{1,3},{2,0},{3,1},{4,6},{5,7},{6,4},{7,5},{8,10},{9,11},{10,... | collective-permute-start | bytes 294920 | tf_op jit(solution)/shard_map/ppermute | solution.py:279
  76.1 5.9 %collective-permute-start.11 = (bf16[4,32,384]{2,1,0:T(8,128)(2,1)S(1)}, bf16[4,32,384]{2,1,0:T(8,128)(2,1)S(1)}, u32[]{:S(2)}, u32[]{:S(2)}) collective-permute-start(bf16[4,32,384]{2,1,0:T(8,128)(2,1)S(1)} %get-tuple-element.73), channel_id=1, source_target_pairs={{0,4},{4,0},{8,12},{12,8},{16,20},{20,16},{24,28},{28,24},{1,5},{5... | collective-permute-start | bytes 294920 | tf_op jit(solution)/shard_map/ppermute | solution.py:279
  76.6 5.6 %collective-permute-start.12 = (bf16[4,32,384]{2,1,0:T(8,128)(2,1)S(1)}, bf16[4,32,384]{2,1,0:T(8,128)(2,1)S(1)}, u32[]{:S(2)}, u32[]{:S(2)}) collective-permute-start(bf16[4,32,384]{2,1,0:T(8,128)(2,1)S(1)} %get-tuple-element.74), channel_id=1, source_target_pairs={{0,6},{1,7},{2,4},{3,5},{4,2},{5,3},{6,0},{7,1},{8,14},{9,15},{10,... | collective-permute-start | bytes 294920 | tf_op jit(solution)/shard_map/ppermute | solution.py:375
  81.9 3.3 %copy-start.2 = (bf16[4,32,384]{2,1,0:T(8,128)(2,1)}, bf16[4,32,384]{2,1,0:T(8,128)(2,1)S(1)}, u32[]{:S(2)}) copy-start(bf16[4,32,384]{2,1,0:T(8,128)(2,1)S(1)} %collective-permute-done.10.refs_1_) | copy-start | bytes 294916
  81.9 3.2 %copy-start.3 = (bf16[4,32,384]{2,1,0:T(8,128)(2,1)}, bf16[4,32,384]{2,1,0:T(8,128)(2,1)S(1)}, u32[]{:S(2)}) copy-start(bf16[4,32,384]{2,1,0:T(8,128)(2,1)S(1)} %collective-permute-done.11.refs_2_) | copy-start | bytes 294916
  82.2 2.9 %copy-start.4 = (bf16[4,32,384]{2,1,0:T(8,128)(2,1)}, bf16[4,32,384]{2,1,0:T(8,128)(2,1)S(1)}, u32[]{:S(2)}) copy-start(bf16[4,32,384]{2,1,0:T(8,128)(2,1)S(1)} %collective-permute-done.12.refs_3_) | copy-start | bytes 294916
  82.2 4.9 %collective-permute-start.18 = (bf16[1,96,384]{2,1,0:T(8,128)(2,1)S(1)}, bf16[1,96,384]{2,1,0:T(8,128)(2,1)S(1)}, u32[]{:S(2)}, u32[]{:S(2)}) collective-permute-start(bf16[1,96,384]{2,1,0:T(8,128)(2,1)S(1)} %fusion.11), channel_id=1, source_target_pairs={{0,8},{4,12},{8,0},{12,4},{16,24},{20,28},{24,16},{28,20},{1,9},{5... | collective-permute-start | bytes 221192 | tf_op jit(solution)/shard_map/ppermute | solution.py:279
  83.1 6.0 %collective-permute-start.19 = (bf16[1,96,384]{2,1,0:T(8,128)(2,1)S(1)}, bf16[1,96,384]{2,1,0:T(8,128)(2,1)S(1)}, u32[]{:S(2)}, u32[]{:S(2)}) collective-permute-start(bf16[1,96,384]{2,1,0:T(8,128)(2,1)S(1)} %fusion.10), channel_id=1, source_target_pairs={{0,16},{4,20},{8,24},{12,28},{16,0},{20,4},{24,8},{28,12},{1,17},{... | collective-permute-start | bytes 221192 | tf_op jit(solution)/shard_map/ppermute | solution.py:279

commit v20 on v18

--- a/solution.py
+++ b/solution.py
@@ -419,16 +419,17 @@
     state = coming.hop(z, steps, halves, state)
     state, *kept = forward(state, up, w_down)
     going = Journey(state.reshape(parts))
-    grad = going.hop(z, steps, halves, coming.held)
+    grad = going.hop_both(x, y, steps, halves, coming.held)
     d_pre, grad_t, *given = backward(place, grad, kept, places, block)
     hidden, normed_t = kept[0], kept[3]
     if not given:
+        going.hop(z, steps, halves)
         going.hop(core, steps, halves)
-        going.hop_both(x, y, steps, halves)
         mixed_out = settle(place, going)
         grad_down = scatter_narrow(halves, grad_t, hidden, [steps[core]] + order_down, span_x, span_y)
         grad_up = scatter_narrow(halves, normed_t, d_pre, [steps[core]] + order_up, span_x, span_y)
         return (mixed_out, grad_up, grad_down)
+    given[0] = going.hop(z, steps, halves, given[0])
     take_down, take_up = [swap(part, *steps[core]) for part in given]
     keep_down, keep_up = keep_blocks(place, hidden, d_pre, normed_t, grad_t, places, block)
 
@@ -436,8 +437,6 @@
         if phase == 1:
             return going.hop(core, steps, halves, give)
         if phase == 2:
-            return going.hop_both(x, y, steps, halves, give)
-        if phase == len(order_down) - 1:
             going.parts, give = lax.optimization_barrier((going.parts, give))
         return give
 

time: 88.4 us -> 89.8 us (1.016)
  starting transfers between devices: 22.7 us -> 23.8 us
    ppermute x18, starting transfers between devices: 11.1 us -> 14.6 us  [swap(): return lax.ppermute(block, axis, pairs)]
    ppermute x2, starting transfers between devices: 4.21 us -> 1.73 us  [swap_both(): return lax.ppermute(block, ('gx', 'gy'), pairs)]
  transfers between devices with their start and end apart: 21 -> 21, of which waited for: 13 -> 13; matrix products, arithmetic and copies ran while one was open for 3% -> 3% of each run, Pallas kernels for 18% -> 29%
where the time goes in v20:
time: 89.8 us; the launch traced here: 89.4 us
  waiting for transfers between devices  35.4 us (39%)
  Pallas kernels  25.5 us (28%)
  starting transfers between devices  23.8 us (27%)
  other arithmetic  3.48 us (4%)
  between operations  0.99 us (1%)
    ppermute x18, waiting for transfers between devices, swap(): return lax.ppermute(block, axis, pairs)  31 us
    ppermute x18, starting transfers between devices, swap(): return lax.ppermute(block, axis, pairs)  14.6 us
    pallas_call x1, Pallas kernels, backward(): pl.pallas_call(functools.partial(backward_kernel, *places), out_shape=out...  9.46 us
    pallas_call x1, Pallas kernels, forward(): pl.pallas_call(forward_kernel, out_shape=outs, in_specs=[spec(pltpu.VMEM)...  8.78 us
    all_to_all x1, starting transfers between devices, exchange(): lax.all_to_all(block, ('gx', 'gy'), split_axis=0, concat_axis=0, axis_ind...  7.44 us
    all_to_all x1, waiting for transfers between devices, exchange(): lax.all_to_all(block, ('gx', 'gy'), split_axis=0, concat_axis=0, axis_ind...  3.4 us
    pallas_call x1, Pallas kernels, keep_blocks(): pl.pallas_call(functools.partial(keep_kernel, *places), out_shape=[block]...  3.17 us
    pallas_call x1, Pallas kernels, load(): pl.pallas_call(load_kernel, out_shape=pltpu.VMEM(weight.shape, weight.dty...  2.21 us
  transfers between devices with their start and end apart: 21, of which 13 were waited for; matrix products, arithmetic and copies ran while one was open for 3% of the time, Pallas kernels for 29%

profile of v20, /device:TPU:0, one launch (start us, length us, event | category | flops | bytes accessed | tf_op | source)
XLA Modules:
  0.0 89.4 jit_solution(458075520119064080)
XLA Ops:
  0.6 7.4 %all-to-all-start = ((bf16[16,32,384]{2,1,0:T(8,128)(2,1)}), bf16[16,32,384]{2,1,0:T(8,128)(2,1)S(1)}, u32[]{:S(2)}, u32[]{:S(2)}) async-start(bf16[16,32,384]{2,1,0:T(8,128)(2,1)} %bitcast.93), calls=%async_computation | async-start | bytes 786432 | tf_op jit(solution)/shard_map/all_to_all | solution.py:40
  8.7 1.1 %collective-permute-done = bf16[2,2,2,1,32,384]{5,4,2,1,0,3:T(8,128)(2,1)S(1)} collective-permute-done((bf16[2,2,2,1,32,384]{5,4,2,1,0,3:T(8,128)(2,1)S(1)}, bf16[2,2,2,1,32,384]{5,4,2,1,0,3:T(8,128)(2,1)S(1)}, u32[]{:S(2)}, u32[]{:S(2)}) %collective-permute-start) | collective-permute-done | bytes 196640 | tf_op jit(solution)/shard_map/ppermute | solution.py:284
  10.0 1.9 %collective-permute-start.1 = (bf16[2,2,32,384]{3,2,1,0:T(8,128)(2,1)S(1)}, bf16[2,2,32,384]{3,2,1,0:T(8,128)(2,1)S(1)}, u32[]{:S(2)}, u32[]{:S(2)}) collective-permute-start(bf16[2,2,32,384]{3,2,1,0:T(8,128)(2,1)S(1)} %bitcast.99), channel_id=1, source_target_pairs={{0,2},{1,3},{2,0},{3,1},{4,6},{5,7},{6,4},{7,5},{8,10},{9,11},{10,... | collective-permute-start | bytes 294920 | tf_op jit(solution)/shard_map/ppermute | solution.py:284
  11.8 1.5 %collective-permute-start.2 = (bf16[2,2,32,384]{3,2,1,0:T(8,128)(2,1)S(1)}, bf16[2,2,32,384]{3,2,1,0:T(8,128)(2,1)S(1)}, u32[]{:S(2)}, u32[]{:S(2)}) collective-permute-start(bf16[2,2,32,384]{3,2,1,0:T(8,128)(2,1)S(1)} %bitcast.98), channel_id=1, source_target_pairs={{0,4},{4,0},{8,12},{12,8},{16,20},{20,16},{24,28},{28,24},{1,5},{5... | collective-permute-start | bytes 294920 | tf_op jit(solution)/shard_map/ppermute | solution.py:284
  13.5 2.2 %shard_map.67.up_ref = bf16[768,1536]{1,0:T(8,128)(2,1)S(1)} custom-call(s32[2]{0:T(128)S(1)} %pad_add_fusion.place_ref, bf16[768,1536]{1,0:T(8,128)(2,1)} %source.1), custom_call_target="tpu_custom_call" | custom-call | bytes 4718592 | tf_op jit(solution)/shard_map/pallas_call | solution.py:209
  15.7 0.9 collective-permute-done.1
  16.6 1.3 %collective-permute-done.2 = bf16[2,2,32,384]{3,2,1,0:T(8,128)(2,1)S(1)} collective-permute-done((bf16[2,2,32,384]{3,2,1,0:T(8,128)(2,1)S(1)}, bf16[2,2,32,384]{3,2,1,0:T(8,128)(2,1)S(1)}, u32[]{:S(2)}, u32[]{:S(2)}) %collective-permute-start.2) | collective-permute-done | bytes 98336 | tf_op jit(solution)/shard_map/ppermute | solution.py:284
  17.9 0.9 %collective-permute-done.3 = bf16[2,2,32,384]{3,2,1,0:T(8,128)(2,1)S(1)} collective-permute-done((bf16[2,2,32,384]{3,2,1,0:T(8,128)(2,1)S(1)}, bf16[2,2,32,384]{3,2,1,0:T(8,128)(2,1)S(1)}, u32[]{:S(2)}, u32[]{:S(2)}) %collective-permute-start.3) | collective-permute-done | bytes 98336 | tf_op jit(solution)/shard_map/ppermute | solution.py:373
  18.9 3.4 %all-to-all-done.state_ref = bf16[16,32,384]{2,1,0:T(8,128)(2,1)S(1)} async-done(((bf16[16,32,384]{2,1,0:T(8,128)(2,1)}), bf16[16,32,384]{2,1,0:T(8,128)(2,1)S(1)}, u32[]{:S(2)}, u32[]{:S(2)}) %all-to-all-start) | async-done | bytes 393248 | tf_op jit(solution)/shard_map/all_to_all | solution.py:40
  22.3 0.8 collective-permute-start.4
  23.1 8.8 %shard_map.68 = (bf16[16,32,384]{2,1,0:T(8,128)(2,1)S(1)}, bf16[1024,1536]{1,0:T(8,128)(2,1)S(1)}, bf16[1024,1536]{1,0:T(8,128)(2,1)S(1)}, bf16[1024,768]{1,0:T(...) custom-call(bf16[16,32,384]{2,1,0:T(8,128)(2,1)S(1)} %all-to-all-don, ...), custom_call_target="tpu_custom_call" | custom-call | flops 12079595520 | bytes 25165824 | tf_op jit(solution)/shard_map/pallas_call | solution.py:235
  32.0 1.5 %collective-permute-done.4 = bf16[8,32,384]{2,1,0:T(8,128)(2,1)S(1)} collective-permute-done((bf16[8,32,384]{2,1,0:T(8,128)(2,1)S(1)}, bf16[8,32,384]{2,1,0:T(8,128)(2,1)S(1)}, u32[]{:S(2)}, u32[]{:S(2)}) %collective-permute-start.4) | collective-permute-done | bytes 196640 | tf_op jit(solution)/shard_map/ppermute | solution.py:284
  33.5 0.7 collective-permute-start.5
  34.2 1.4 %collective-permute-start.6 = (bf16[2,2,1,32,384]{4,3,2,1,0:T(8,128)(2,1)S(1)}, bf16[2,2,1,32,384]{4,3,2,1,0:T(8,128)(2,1)S(1)}, u32[]{:S(2)}, u32[]{:S(2)}) collective-permute-start(bf16[2,2,1,32,384]{4,3,2,1,0:T(8,128)(2,1)S(1)} %get-tuple-element.56), channel_id=1, source_target_pairs={{0,4},{4,0},{8,12},{12,8},{16,20},{20,16},{24,28},{28,24},{1,5},{5... | collective-permute-start | bytes 294920 | tf_op jit(solution)/shard_map/ppermute | solution.py:284
  35.5 1.5 %collective-permute-start.7 = (bf16[2,2,1,32,384]{4,3,2,1,0:T(8,128)(2,1)S(1)}, bf16[2,2,1,32,384]{4,3,2,1,0:T(8,128)(2,1)S(1)}, u32[]{:S(2)}, u32[]{:S(2)}) collective-permute-start(bf16[2,2,1,32,384]{4,3,2,1,0:T(8,128)(2,1)S(1)} %get-tuple-element.57), channel_id=1, source_target_pairs={{0,6},{1,7},{2,4},{3,5},{4,2},{5,3},{6,0},{7,1},{8,14},{9,15},{10,... | collective-permute-start | bytes 294920 | tf_op jit(solution)/shard_map/ppermute | solution.py:373
  37.1 9.5 %shard_map.69 = (bf16[1024,1536]{1,0:T(8,128)(2,1)S(1)}, bf16[768,1024]{1,0:T(8,128)(2,1)S(1)}, bf16[16,96,384]{2,1,0:T(8,128)(2,1)S(1)}, bf16[16,96,384]{2,1,0:T(8,128)(2,1)S(1)}) custom-call(s32[2]{0:T(128)S(1)} %pad_add_fusion.place_ref, bf16[16,32,384]{2,1,0:T(8,128)(2,1)S(1)} %pad_maximum_fusion.1.grad_ref, ...), custom_call_target="tpu_custom_call" | custom-call | flops 12079595520 | bytes 25165824 | tf_op jit(solution)/shard_map/pallas_call | solution.py:254
  47.4 3.2 %shard_map.70 = (bf16[16,96,384]{2,1,0:T(8,128)(2,1)S(1)}, bf16[16,96,384]{2,1,0:T(8,128)(2,1)S(1)}) custom-call(s32[2]{0:T(128)S(1)} %pad_add_fusion.place_ref, bf16[1024,1536]{1,0:T(8,128)(2,1)S(1)} %get-tuple-element.59.hidden_ref, bf16[1024,1536]{1,0:T(8,128)(2,1)S(1)} %get-tuple-element.68.d_pre_ref, ...), custom_call_target="tpu_custom_call" | custom-call | flops 2415919104 | bytes 12582912 | tf_op jit(solution)/shard_map/pallas_call | solution.py:270
  50.9 0.7 collective-permute-start.14
  51.9 1.4 %collective-permute-start.10 = (bf16[8,96,384]{2,1,0:T(8,128)(2,1)S(1)}, bf16[8,96,384]{2,1,0:T(8,128)(2,1)S(1)}, u32[]{:S(2)}, u32[]{:S(2)}) collective-permute-start(bf16[8,96,384]{2,1,0:T(8,128)(2,1)S(1)} %get-tuple-element.84), channel_id=1, source_target_pairs={{0,4},{4,0},{8,12},{12,8},{16,20},{20,16},{24,28},{28,24},{1,5},{5... | collective-permute-start | bytes 1769480 | tf_op jit(solution)/shard_map/ppermute | solution.py:284
  53.3 11.3 %collective-permute-done.8 = bf16[2,4,32,384]{3,2,1,0:T(8,128)(2,1)S(1)} collective-permute-done((bf16[2,4,32,384]{3,2,1,0:T(8,128)(2,1)S(1)}, bf16[2,4,32,384]{3,2,1,0:T(8,128)(2,1)S(1)}, u32[]{:S(2)}, u32[]{:S(2)}) %collective-permute-start.8) | collective-permute-done | bytes 196640 | tf_op jit(solution)/shard_map/ppermute | solution.py:284
  64.6 0.7 fusion.5
  65.3 0.9 %collective-permute-done.14 = bf16[8,96,384]{2,1,0:T(8,128)(2,1)S(1)} collective-permute-done((bf16[8,96,384]{2,1,0:T(8,128)(2,1)S(1)}, bf16[8,96,384]{2,1,0:T(8,128)(2,1)S(1)}, u32[]{:S(2)}, u32[]{:S(2)}) %collective-permute-start.14) | collective-permute-done | bytes 589856 | tf_op jit(solution)/shard_map/ppermute | solution.py:284
  67.1 1.5 %collective-permute-start.12 = (bf16[4,96,384]{2,1,0:T(8,128)(2,1)S(1)}, bf16[4,96,384]{2,1,0:T(8,128)(2,1)S(1)}, u32[]{:S(2)}, u32[]{:S(2)}) collective-permute-start(bf16[4,96,384]{2,1,0:T(8,128)(2,1)S(1)} %get-tuple-element.73), channel_id=1, source_target_pairs={{0,2},{1,3},{2,0},{3,1},{4,6},{5,7},{6,4},{7,5},{8,10},{9,11},{10,... | collective-permute-start | bytes 884744 | tf_op jit(solution)/shard_map/ppermute | solution.py:284
  68.6 5.9 %collective-permute-done.15 = bf16[4,96,384]{2,1,0:T(8,128)(2,1)S(1)} collective-permute-done((bf16[4,96,384]{2,1,0:T(8,128)(2,1)S(1)}, bf16[4,96,384]{2,1,0:T(8,128)(2,1)S(1)}, u32[]{:S(2)}, u32[]{:S(2)}) %collective-permute-start.15) | collective-permute-done | bytes 294944 | tf_op jit(solution)/shard_map/ppermute | solution.py:284
  75.1 2.6 %collective-permute-start.18 = (bf16[2,96,384]{2,1,0:T(8,128)(2,1)S(1)}, bf16[2,96,384]{2,1,0:T(8,128)(2,1)S(1)}, u32[]{:S(2)}, u32[]{:S(2)}) collective-permute-start(bf16[2,96,384]{2,1,0:T(8,128)(2,1)S(1)} %get-tuple-element.80), channel_id=1, source_target_pairs={{0,16},{4,20},{8,24},{12,28},{16,0},{20,4},{24,8},{28,12},{1,17},{... | collective-permute-start | bytes 442376 | tf_op jit(solution)/shard_map/ppermute | solution.py:284
  77.7 1.9 %shard_map.71 = bf16[512,384]{1,0:T(8,128)(2,1)} custom-call(s32[2]{0:T(128)} %copy-done, bf16[8,32,384]{2,1,0:T(8,128)(2,1)} %get-tuple-element.74.refs_0_, bf16[8,32,384]{2,1,0:T(8,128)(2,1)} %copy-done.2), custom_call_target="tpu_custom_call" | custom-call | bytes 786432 | tf_op jit(solution)/shard_map/pallas_call | solution.py:379
  79.6 1.8 %collective-permute-done.16 = bf16[2,96,384]{2,1,0:T(8,128)(2,1)S(1)} collective-permute-done((bf16[2,96,384]{2,1,0:T(8,128)(2,1)S(1)}, bf16[2,96,384]{2,1,0:T(8,128)(2,1)S(1)}, u32[]{:S(2)}, u32[]{:S(2)}) %collective-permute-start.16) | collective-permute-done | bytes 147488 | tf_op jit(solution)/shard_map/ppermute | solution.py:284
  81.6 2.7 %collective-permute-done.18 = bf16[2,96,384]{2,1,0:T(8,128)(2,1)S(1)} collective-permute-done((bf16[2,96,384]{2,1,0:T(8,128)(2,1)S(1)}, bf16[2,96,384]{2,1,0:T(8,128)(2,1)S(1)}, u32[]{:S(2)}, u32[]{:S(2)}) %collective-permute-start.18) | collective-permute-done | bytes 147488 | tf_op jit(solution)/shard_map/ppermute | solution.py:284
  84.4 2.6 %collective-permute-done.17 = bf16[1,96,384]{2,1,0:T(8,128)(2,1)S(1)} collective-permute-done((bf16[1,96,384]{2,1,0:T(8,128)(2,1)S(1)}, bf16[1,96,384]{2,1,0:T(8,128)(2,1)S(1)}, u32[]{:S(2)}, u32[]{:S(2)}) %collective-permute-start.17) | collective-permute-done | bytes 73760 | tf_op jit(solution)/shard_map/ppermute | solution.py:284
  87.0 0.7 add_bitcast_fusion.1
  87.7 1.1 %collective-permute-done.19 = bf16[1,96,384]{2,1,0:T(8,128)(2,1)S(1)} collective-permute-done((bf16[1,96,384]{2,1,0:T(8,128)(2,1)S(1)}, bf16[1,96,384]{2,1,0:T(8,128)(2,1)S(1)}, u32[]{:S(2)}, u32[]{:S(2)}) %collective-permute-start.19) | collective-permute-done | bytes 73760 | tf_op jit(solution)/shard_map/ppermute | solution.py:284
  88.8 0.7 add_bitcast_fusion
  (48 shorter events, 4.2 us)
Async XLA Ops:
  0.6 7.6 %copy-start.1 = (bf16[512,384]{1,0:T(8,128)(2,1)S(1)}, bf16[512,384]{1,0:T(8,128)(2,1)}, u32[]{:S(2)}) copy-start(bf16[512,384]{1,0:T(8,128)(2,1)} %param.7) | copy-start | bytes 1179652
  0.6 21.7 %all-to-all-start = ((bf16[16,32,384]{2,1,0:T(8,128)(2,1)}), bf16[16,32,384]{2,1,0:T(8,128)(2,1)S(1)}, u32[]{:S(2)}, u32[]{:S(2)}) async-start(bf16[16,32,384]{2,1,0:T(8,128)(2,1)} %bitcast.93), calls=%async_computation | async-start | bytes 786432 | tf_op jit(solution)/shard_map/all_to_all | solution.py:40
  8.3 39.1 %copy-start = (s32[2]{0:T(128)}, s32[2]{0:T(128)S(1)}, u32[]{:S(2)}) copy-start(s32[2]{0:T(128)S(1)} %pad_add_fusion.place_ref) | copy-start | bytes 28
  8.3 1.5 %collective-permute-start = (bf16[2,2,2,1,32,384]{5,4,2,1,0,3:T(8,128)(2,1)S(1)}, bf16[2,2,2,1,32,384]{5,4,2,1,0,3:T(8,128)(2,1)S(1)}, u32[]{:S(2)}, u32[]{:S(2)}) collective-permute-start(bf16[2,2,2,1,32,384]{5,4,2,1,0,3:T(8,128)(2,1)S(1)} %get-tuple-element.107), channel_id=1, source_target_pairs={{0,1},{1,0},{2,3},{3,2},{4,5},{5,4},{6,7},{7,6},{8,9},{9,8},{10,11... | collective-permute-start | bytes 589832 | tf_op jit(solution)/shard_map/ppermute | solution.py:284
  10.0 6.7 %collective-permute-start.1 = (bf16[2,2,32,384]{3,2,1,0:T(8,128)(2,1)S(1)}, bf16[2,2,32,384]{3,2,1,0:T(8,128)(2,1)S(1)}, u32[]{:S(2)}, u32[]{:S(2)}) collective-permute-start(bf16[2,2,32,384]{3,2,1,0:T(8,128)(2,1)S(1)} %bitcast.99), channel_id=1, source_target_pairs={{0,2},{1,3},{2,0},{3,1},{4,6},{5,7},{6,4},{7,5},{8,10},{9,11},{10,... | collective-permute-start | bytes 294920 | tf_op jit(solution)/shard_map/ppermute | solution.py:284
  11.8 6.1 %collective-permute-start.2 = (bf16[2,2,32,384]{3,2,1,0:T(8,128)(2,1)S(1)}, bf16[2,2,32,384]{3,2,1,0:T(8,128)(2,1)S(1)}, u32[]{:S(2)}, u32[]{:S(2)}) collective-permute-start(bf16[2,2,32,384]{3,2,1,0:T(8,128)(2,1)S(1)} %bitcast.98), channel_id=1, source_target_pairs={{0,4},{4,0},{8,12},{12,8},{16,20},{20,16},{24,28},{28,24},{1,5},{5... | collective-permute-start | bytes 294920 | tf_op jit(solution)/shard_map/ppermute | solution.py:284
  13.3 5.5 %collective-permute-start.3 = (bf16[2,2,32,384]{3,2,1,0:T(8,128)(2,1)S(1)}, bf16[2,2,32,384]{3,2,1,0:T(8,128)(2,1)S(1)}, u32[]{:S(2)}, u32[]{:S(2)}) collective-permute-start(bf16[2,2,32,384]{3,2,1,0:T(8,128)(2,1)S(1)} %bitcast.97), channel_id=1, source_target_pairs={{0,6},{1,7},{2,4},{3,5},{4,2},{5,3},{6,0},{7,1},{8,14},{9,15},{10,... | collective-permute-start | bytes 294920 | tf_op jit(solution)/shard_map/ppermute | solution.py:373
  22.3 11.1 %collective-permute-start.4 = (bf16[8,32,384]{2,1,0:T(8,128)(2,1)S(1)}, bf16[8,32,384]{2,1,0:T(8,128)(2,1)S(1)}, u32[]{:S(2)}, u32[]{:S(2)}) collective-permute-start(bf16[8,32,384]{2,1,0:T(8,128)(2,1)S(1)} %get-tuple-element.53), channel_id=1, source_target_pairs={{0,16},{4,20},{8,24},{12,28},{16,0},{20,4},{24,8},{28,12},{1,17},{... | collective-permute-start | bytes 589832 | tf_op jit(solution)/shard_map/ppermute | solution.py:284
  33.5 13.1 %collective-permute-start.5 = (bf16[2,2,1,32,384]{4,3,2,1,0:T(8,128)(2,1)S(1)}, bf16[2,2,1,32,384]{4,3,2,1,0:T(8,128)(2,1)S(1)}, u32[]{:S(2)}, u32[]{:S(2)}) collective-permute-start(bf16[2,2,1,32,384]{4,3,2,1,0:T(8,128)(2,1)S(1)} %get-tuple-element.55), channel_id=1, source_target_pairs={{0,2},{1,3},{2,0},{3,1},{4,6},{5,7},{6,4},{7,5},{8,10},{9,11},{10,... | collective-permute-start | bytes 294920 | tf_op jit(solution)/shard_map/ppermute | solution.py:284
  34.2 12.5 %collective-permute-start.6 = (bf16[2,2,1,32,384]{4,3,2,1,0:T(8,128)(2,1)S(1)}, bf16[2,2,1,32,384]{4,3,2,1,0:T(8,128)(2,1)S(1)}, u32[]{:S(2)}, u32[]{:S(2)}) collective-permute-start(bf16[2,2,1,32,384]{4,3,2,1,0:T(8,128)(2,1)S(1)} %get-tuple-element.56), channel_id=1, source_target_pairs={{0,4},{4,0},{8,12},{12,8},{16,20},{20,16},{24,28},{28,24},{1,5},{5... | collective-permute-start | bytes 294920 | tf_op jit(solution)/shard_map/ppermute | solution.py:284
  35.5 11.2 %collective-permute-start.7 = (bf16[2,2,1,32,384]{4,3,2,1,0:T(8,128)(2,1)S(1)}, bf16[2,2,1,32,384]{4,3,2,1,0:T(8,128)(2,1)S(1)}, u32[]{:S(2)}, u32[]{:S(2)}) collective-permute-start(bf16[2,2,1,32,384]{4,3,2,1,0:T(8,128)(2,1)S(1)} %get-tuple-element.57), channel_id=1, source_target_pairs={{0,6},{1,7},{2,4},{3,5},{4,2},{5,3},{6,0},{7,1},{8,14},{9,15},{10,... | collective-permute-start | bytes 294920 | tf_op jit(solution)/shard_map/ppermute | solution.py:373
  46.5 4.0 %collective-permute-start.13 = (bf16[16,96,384]{2,1,0:T(8,128)(2,1)S(1)}, bf16[16,96,384]{2,1,0:T(8,128)(2,1)S(1)}, u32[]{:S(2)}, u32[]{:S(2)}) collective-permute-start(bf16[16,96,384]{2,1,0:T(8,128)(2,1)S(1)} %get-tuple-element.77), channel_id=1, source_target_pairs={{0,1},{1,0},{2,3},{3,2},{4,5},{5,4},{6,7},{7,6},{8,9},{9,8},{10,11... | collective-permute-start | bytes 3538952 | tf_op jit(solution)/shard_map/ppermute | solution.py:284
  46.8 4.8 %collective-permute-start.9 = (bf16[16,96,384]{2,1,0:T(8,128)(2,1)S(1)}, bf16[16,96,384]{2,1,0:T(8,128)(2,1)S(1)}, u32[]{:S(2)}, u32[]{:S(2)}) collective-permute-start(bf16[16,96,384]{2,1,0:T(8,128)(2,1)S(1)} %get-tuple-element.71), channel_id=1, source_target_pairs={{0,1},{1,0},{2,3},{3,2},{4,5},{5,4},{6,7},{7,6},{8,9},{9,8},{10,11... | collective-permute-start | bytes 3538952 | tf_op jit(solution)/shard_map/ppermute | solution.py:284
  50.9 15.3 %collective-permute-start.14 = (bf16[8,96,384]{2,1,0:T(8,128)(2,1)S(1)}, bf16[8,96,384]{2,1,0:T(8,128)(2,1)S(1)}, u32[]{:S(2)}, u32[]{:S(2)}) collective-permute-start(bf16[8,96,384]{2,1,0:T(8,128)(2,1)S(1)} %get-tuple-element.82), channel_id=1, source_target_pairs={{0,2},{1,3},{2,0},{3,1},{4,6},{5,7},{6,4},{7,5},{8,10},{9,11},{10,... | collective-permute-start | bytes 1769480 | tf_op jit(solution)/shard_map/ppermute | solution.py:284
  51.9 15.0 %collective-permute-start.10 = (bf16[8,96,384]{2,1,0:T(8,128)(2,1)S(1)}, bf16[8,96,384]{2,1,0:T(8,128)(2,1)S(1)}, u32[]{:S(2)}, u32[]{:S(2)}) collective-permute-start(bf16[8,96,384]{2,1,0:T(8,128)(2,1)S(1)} %get-tuple-element.84), channel_id=1, source_target_pairs={{0,4},{4,0},{8,12},{12,8},{16,20},{20,16},{24,28},{28,24},{1,5},{5... | collective-permute-start | bytes 1769480 | tf_op jit(solution)/shard_map/ppermute | solution.py:284
  53.3 11.3 %collective-permute-start.8 = (bf16[2,4,32,384]{3,2,1,0:T(8,128)(2,1)S(1)}, bf16[2,4,32,384]{3,2,1,0:T(8,128)(2,1)S(1)}, u32[]{:S(2)}, u32[]{:S(2)}) collective-permute-start(bf16[2,4,32,384]{3,2,1,0:T(8,128)(2,1)S(1)} %get-tuple-element.67), channel_id=1, source_target_pairs={{0,16},{4,20},{8,24},{12,28},{16,0},{20,4},{24,8},{28,12},{1,17},{... | collective-permute-start | bytes 589832 | tf_op jit(solution)/shard_map/ppermute | solution.py:284
  66.4 8.2 %collective-permute-start.15 = (bf16[4,96,384]{2,1,0:T(8,128)(2,1)S(1)}, bf16[4,96,384]{2,1,0:T(8,128)(2,1)S(1)}, u32[]{:S(2)}, u32[]{:S(2)}) collective-permute-start(bf16[4,96,384]{2,1,0:T(8,128)(2,1)S(1)} %get-tuple-element.86), channel_id=1, source_target_pairs={{0,4},{4,0},{8,12},{12,8},{16,20},{20,16},{24,28},{28,24},{1,5},{5... | collective-permute-start | bytes 884744 | tf_op jit(solution)/shard_map/ppermute | solution.py:284
  67.1 7.9 %collective-permute-start.12 = (bf16[4,96,384]{2,1,0:T(8,128)(2,1)S(1)}, bf16[4,96,384]{2,1,0:T(8,128)(2,1)S(1)}, u32[]{:S(2)}, u32[]{:S(2)}) collective-permute-start(bf16[4,96,384]{2,1,0:T(8,128)(2,1)S(1)} %get-tuple-element.73), channel_id=1, source_target_pairs={{0,2},{1,3},{2,0},{3,1},{4,6},{5,7},{6,4},{7,5},{8,10},{9,11},{10,... | collective-permute-start | bytes 884744 | tf_op jit(solution)/shard_map/ppermute | solution.py:284
  68.6 6.5 %collective-permute-start.11 = (bf16[8,32,384]{2,1,0:T(8,128)(2,1)S(1)}, bf16[8,32,384]{2,1,0:T(8,128)(2,1)S(1)}, u32[]{:S(2)}, u32[]{:S(2)}) collective-permute-start(bf16[8,32,384]{2,1,0:T(8,128)(2,1)S(1)} %get-tuple-element.72), channel_id=1, source_target_pairs={{0,1},{1,0},{2,3},{3,2},{4,5},{5,4},{6,7},{7,6},{8,9},{9,8},{10,11... | collective-permute-start | bytes 589832 | tf_op jit(solution)/shard_map/ppermute | solution.py:284
  74.6 6.7 %collective-permute-start.16 = (bf16[2,96,384]{2,1,0:T(8,128)(2,1)S(1)}, bf16[2,96,384]{2,1,0:T(8,128)(2,1)S(1)}, u32[]{:S(2)}, u32[]{:S(2)}) collective-permute-start(bf16[2,96,384]{2,1,0:T(8,128)(2,1)S(1)} %get-tuple-element.92), channel_id=1, source_target_pairs={{0,8},{4,12},{8,0},{12,4},{16,24},{20,28},{24,16},{28,20},{1,9},{5... | collective-permute-start | bytes 442376 | tf_op jit(solution)/shard_map/ppermute | solution.py:284
  75.1 2.6 %copy-start.2 = (bf16[8,32,384]{2,1,0:T(8,128)(2,1)}, bf16[8,32,384]{2,1,0:T(8,128)(2,1)S(1)}, u32[]{:S(2)}) copy-start(bf16[8,32,384]{2,1,0:T(8,128)(2,1)S(1)} %collective-permute-done.11.refs_1_) | copy-start | bytes 589828
  75.1 9.2 %collective-permute-start.18 = (bf16[2,96,384]{2,1,0:T(8,128)(2,1)S(1)}, bf16[2,96,384]{2,1,0:T(8,128)(2,1)S(1)}, u32[]{:S(2)}, u32[]{:S(2)}) collective-permute-start(bf16[2,96,384]{2,1,0:T(8,128)(2,1)S(1)} %get-tuple-element.80), channel_id=1, source_target_pairs={{0,16},{4,20},{8,24},{12,28},{16,0},{20,4},{24,8},{28,12},{1,17},{... | collective-permute-start | bytes 442376 | tf_op jit(solution)/shard_map/ppermute | solution.py:284
  81.4 5.6 %collective-permute-start.17 = (bf16[1,96,384]{2,1,0:T(8,128)(2,1)S(1)}, bf16[1,96,384]{2,1,0:T(8,128)(2,1)S(1)}, u32[]{:S(2)}, u32[]{:S(2)}) collective-permute-start(bf16[1,96,384]{2,1,0:T(8,128)(2,1)S(1)} %fusion.12), channel_id=1, source_target_pairs={{0,16},{4,20},{8,24},{12,28},{16,0},{20,4},{24,8},{28,12},{1,17},{... | collective-permute-start | bytes 221192 | tf_op jit(solution)/shard_map/ppermute | solution.py:284
  84.3 4.4 %collective-permute-start.19 = (bf16[1,96,384]{2,1,0:T(8,128)(2,1)S(1)}, bf16[1,96,384]{2,1,0:T(8,128)(2,1)S(1)}, u32[]{:S(2)}, u32[]{:S(2)}) collective-permute-start(bf16[1,96,384]{2,1,0:T(8,128)(2,1)S(1)} %fusion.10), channel_id=1, source_target_pairs={{0,8},{4,12},{8,0},{12,4},{16,24},{20,28},{24,16},{28,20},{1,9},{5... | collective-permute-start | bytes 221192 | tf_op jit(solution)/shard_map/ppermute | solution.py:284

commit v21 on v20

--- a/solution.py
+++ b/solution.py
@@ -419,8 +419,8 @@
     state = coming.hop(z, steps, halves, state)
     state, *kept = forward(state, up, w_down)
     going = Journey(state.reshape(parts))
-    grad = going.hop_both(x, y, steps, halves, coming.held)
-    d_pre, grad_t, *given = backward(place, grad, kept, places, block)
+    going.hop_both(x, y, steps, halves)
+    d_pre, grad_t, *given = backward(place, coming.held, kept, places, block)
     hidden, normed_t = kept[0], kept[3]
     if not given:
         going.hop(z, steps, halves)

time: 89.8 us -> 97 us (1.080)
  waiting for transfers between devices: 35.4 us -> 41.8 us
    ppermute x18, waiting for transfers between devices: 31 us -> 35.4 us  [swap(): return lax.ppermute(block, axis, pairs)]
    ppermute x18, starting transfers between devices: 14.6 us -> 16.8 us  [swap(): return lax.ppermute(block, axis, pairs)]
    ppermute x2, waiting for transfers between devices: 0.93 us -> 3.09 us  [swap_both(): return lax.ppermute(block, ('gx', 'gy'), pairs)]
    ppermute x2, starting transfers between devices: 1.73 us -> 0.36 us  [swap_both(): return lax.ppermute(block, ('gx', 'gy'), pairs)]
  transfers between devices with their start and end apart: 21 -> 21, of which waited for: 13 -> 16; matrix products, arithmetic and copies ran while one was open for 3% -> 3% of each run, Pallas kernels for 29% -> 8%
where the time goes in v21:
time: 97 us; the launch traced here: 96.7 us
  waiting for transfers between devices  41.8 us (43%)
  Pallas kernels  25.5 us (26%)
  starting transfers between devices  24.6 us (25%)
  other arithmetic  3.54 us (4%)
    ppermute x18, waiting for transfers between devices, swap(): return lax.ppermute(block, axis, pairs)  35.4 us
    ppermute x18, starting transfers between devices, swap(): return lax.ppermute(block, axis, pairs)  16.8 us
    pallas_call x1, Pallas kernels, backward(): pl.pallas_call(functools.partial(backward_kernel, *places), out_shape=out...  9.44 us
    pallas_call x1, Pallas kernels, forward(): pl.pallas_call(forward_kernel, out_shape=outs, in_specs=[spec(pltpu.VMEM)...  8.77 us
    all_to_all x1, starting transfers between devices, exchange(): lax.all_to_all(block, ('gx', 'gy'), split_axis=0, concat_axis=0, axis_ind...  7.44 us
    all_to_all x1, waiting for transfers between devices, exchange(): lax.all_to_all(block, ('gx', 'gy'), split_axis=0, concat_axis=0, axis_ind...  3.4 us
    pallas_call x1, Pallas kernels, keep_blocks(): pl.pallas_call(functools.partial(keep_kernel, *places), out_shape=[block]...  3.17 us
    ppermute x2, waiting for transfers between devices, swap_both(): return lax.ppermute(block, ('gx', 'gy'), pairs)  3.09 us
  transfers between devices with their start and end apart: 21, of which 16 were waited for; matrix products, arithmetic and copies ran while one was open for 3% of the time, Pallas kernels for 8%

profile of v21, /device:TPU:0, one launch (start us, length us, event | category | flops | bytes accessed | tf_op | source)
XLA Modules:
  0.0 96.7 jit_solution(4450787474529906563)
XLA Ops:
  0.6 7.4 %all-to-all-start = ((bf16[16,32,384]{2,1,0:T(8,128)(2,1)}), bf16[16,32,384]{2,1,0:T(8,128)(2,1)S(1)}, u32[]{:S(2)}, u32[]{:S(2)}) async-start(bf16[16,32,384]{2,1,0:T(8,128)(2,1)} %bitcast.93), calls=%async_computation | async-start | bytes 786432 | tf_op jit(solution)/shard_map/all_to_all | solution.py:40
  8.7 1.1 %collective-permute-done = bf16[2,2,2,1,32,384]{5,4,2,1,0,3:T(8,128)(2,1)S(1)} collective-permute-done((bf16[2,2,2,1,32,384]{5,4,2,1,0,3:T(8,128)(2,1)S(1)}, bf16[2,2,2,1,32,384]{5,4,2,1,0,3:T(8,128)(2,1)S(1)}, u32[]{:S(2)}, u32[]{:S(2)}) %collective-permute-start) | collective-permute-done | bytes 196640 | tf_op jit(solution)/shard_map/ppermute | solution.py:284
  10.0 1.9 %collective-permute-start.1 = (bf16[2,2,32,384]{3,2,1,0:T(8,128)(2,1)S(1)}, bf16[2,2,32,384]{3,2,1,0:T(8,128)(2,1)S(1)}, u32[]{:S(2)}, u32[]{:S(2)}) collective-permute-start(bf16[2,2,32,384]{3,2,1,0:T(8,128)(2,1)S(1)} %bitcast.99), channel_id=1, source_target_pairs={{0,2},{1,3},{2,0},{3,1},{4,6},{5,7},{6,4},{7,5},{8,10},{9,11},{10,... | collective-permute-start | bytes 294920 | tf_op jit(solution)/shard_map/ppermute | solution.py:284
  11.8 1.5 %collective-permute-start.2 = (bf16[2,2,32,384]{3,2,1,0:T(8,128)(2,1)S(1)}, bf16[2,2,32,384]{3,2,1,0:T(8,128)(2,1)S(1)}, u32[]{:S(2)}, u32[]{:S(2)}) collective-permute-start(bf16[2,2,32,384]{3,2,1,0:T(8,128)(2,1)S(1)} %bitcast.98), channel_id=1, source_target_pairs={{0,4},{4,0},{8,12},{12,8},{16,20},{20,16},{24,28},{28,24},{1,5},{5... | collective-permute-start | bytes 294920 | tf_op jit(solution)/shard_map/ppermute | solution.py:284
  13.5 2.2 %shard_map.67.up_ref = bf16[768,1536]{1,0:T(8,128)(2,1)S(1)} custom-call(s32[2]{0:T(128)S(1)} %pad_add_fusion.place_ref, bf16[768,1536]{1,0:T(8,128)(2,1)} %source.1), custom_call_target="tpu_custom_call" | custom-call | bytes 4718592 | tf_op jit(solution)/shard_map/pallas_call | solution.py:209
  15.7 0.9 collective-permute-done.1
  16.6 1.3 %collective-permute-done.2 = bf16[2,2,32,384]{3,2,1,0:T(8,128)(2,1)S(1)} collective-permute-done((bf16[2,2,32,384]{3,2,1,0:T(8,128)(2,1)S(1)}, bf16[2,2,32,384]{3,2,1,0:T(8,128)(2,1)S(1)}, u32[]{:S(2)}, u32[]{:S(2)}) %collective-permute-start.2) | collective-permute-done | bytes 98336 | tf_op jit(solution)/shard_map/ppermute | solution.py:284
  17.9 0.9 collective-permute-done.3
  18.9 3.4 %all-to-all-done.state_ref = bf16[16,32,384]{2,1,0:T(8,128)(2,1)S(1)} async-done(((bf16[16,32,384]{2,1,0:T(8,128)(2,1)}), bf16[16,32,384]{2,1,0:T(8,128)(2,1)S(1)}, u32[]{:S(2)}, u32[]{:S(2)}) %all-to-all-start) | async-done | bytes 393248 | tf_op jit(solution)/shard_map/all_to_all | solution.py:40
  22.3 8.8 %shard_map.68 = (bf16[16,32,384]{2,1,0:T(8,128)(2,1)S(1)}, bf16[1024,1536]{1,0:T(8,128)(2,1)S(1)}, bf16[1024,1536]{1,0:T(8,128)(2,1)S(1)}, bf16[1024,768]{1,0:T(...) custom-call(bf16[16,32,384]{2,1,0:T(8,128)(2,1)S(1)} %all-to-all-don, ...), custom_call_target="tpu_custom_call" | custom-call | flops 12079595520 | bytes 25165824 | tf_op jit(solution)/shard_map/pallas_call | solution.py:235
  31.8 3.0 %collective-permute-start.4 = (bf16[2,2,1,32,384]{4,3,2,1,0:T(8,128)(2,1)S(1)}, bf16[2,2,1,32,384]{4,3,2,1,0:T(8,128)(2,1)S(1)}, u32[]{:S(2)}, u32[]{:S(2)}) collective-permute-start(bf16[2,2,1,32,384]{4,3,2,1,0:T(8,128)(2,1)S(1)} %get-tuple-element.92), channel_id=1, source_target_pairs={{0,2},{1,3},{2,0},{3,1},{4,6},{5,7},{6,4},{7,5},{8,10},{9,11},{10,... | collective-permute-start | bytes 294920 | tf_op jit(solution)/shard_map/ppermute | solution.py:284
  34.7 0.7 collective-permute-start.7
  35.4 2.2 %collective-permute-done.6 = bf16[2,2,1,32,384]{4,3,2,1,0:T(8,128)(2,1)S(1)} collective-permute-done((bf16[2,2,1,32,384]{4,3,2,1,0:T(8,128)(2,1)S(1)}, bf16[2,2,1,32,384]{4,3,2,1,0:T(8,128)(2,1)S(1)}, u32[]{:S(2)}, u32[]{:S(2)}) %collective-permute-start.6) | collective-permute-done | bytes 98336 | tf_op jit(solution)/shard_map/ppermute | solution.py:373
  37.6 0.7 collective-permute-done.5
  38.4 6.5 %collective-permute-done.7 = bf16[8,32,384]{2,1,0:T(8,128)(2,1)S(1)} collective-permute-done((bf16[8,32,384]{2,1,0:T(8,128)(2,1)S(1)}, bf16[8,32,384]{2,1,0:T(8,128)(2,1)S(1)}, u32[]{:S(2)}, u32[]{:S(2)}) %collective-permute-start.7) | collective-permute-done | bytes 196640 | tf_op jit(solution)/shard_map/ppermute | solution.py:284
  45.0 9.4 %shard_map.69 = (bf16[1024,1536]{1,0:T(8,128)(2,1)S(1)}, bf16[768,1024]{1,0:T(8,128)(2,1)S(1)}, bf16[16,96,384]{2,1,0:T(8,128)(2,1)S(1)}, bf16[16,96,384]{2,1,0:T(8,128)(2,1)S(1)}) custom-call(s32[2]{0:T(128)S(1)} %pad_add_fusion.place_ref, bf16[16,32,384]{2,1,0:T(8,128)(2,1)S(1)} %pad_maximum_fusion.2.grad_ref, ...), custom_call_target="tpu_custom_call" | custom-call | flops 12079595520 | bytes 25165824 | tf_op jit(solution)/shard_map/pallas_call | solution.py:254
  55.0 3.2 %shard_map.70 = (bf16[16,96,384]{2,1,0:T(8,128)(2,1)S(1)}, bf16[16,96,384]{2,1,0:T(8,128)(2,1)S(1)}) custom-call(s32[2]{0:T(128)S(1)} %pad_add_fusion.place_ref, bf16[1024,1536]{1,0:T(8,128)(2,1)S(1)} %get-tuple-element.49.hidden_ref, bf16[1024,1536]{1,0:T(8,128)(2,1)S(1)} %get-tuple-element.58.d_pre_ref, ...), custom_call_target="tpu_custom_call" | custom-call | flops 2415919104 | bytes 12582912 | tf_op jit(solution)/shard_map/pallas_call | solution.py:270
  59.5 1.5 %collective-permute-start.14 = (bf16[8,96,384]{2,1,0:T(8,128)(2,1)S(1)}, bf16[8,96,384]{2,1,0:T(8,128)(2,1)S(1)}, u32[]{:S(2)}, u32[]{:S(2)}) collective-permute-start(bf16[8,96,384]{2,1,0:T(8,128)(2,1)S(1)} %get-tuple-element.72), channel_id=1, source_target_pairs={{0,2},{1,3},{2,0},{3,1},{4,6},{5,7},{6,4},{7,5},{8,10},{9,11},{10,... | collective-permute-start | bytes 1769480 | tf_op jit(solution)/shard_map/ppermute | solution.py:284
  61.0 10.4 %collective-permute-done.8 = bf16[2,4,32,384]{3,2,1,0:T(8,128)(2,1)S(1)} collective-permute-done((bf16[2,4,32,384]{3,2,1,0:T(8,128)(2,1)S(1)}, bf16[2,4,32,384]{3,2,1,0:T(8,128)(2,1)S(1)}, u32[]{:S(2)}, u32[]{:S(2)}) %collective-permute-start.8) | collective-permute-done | bytes 196640 | tf_op jit(solution)/shard_map/ppermute | solution.py:284
  71.4 0.7 fusion.5
  72.1 1.8 %collective-permute-done.10 = bf16[8,96,384]{2,1,0:T(8,128)(2,1)S(1)} collective-permute-done((bf16[8,96,384]{2,1,0:T(8,128)(2,1)S(1)}, bf16[8,96,384]{2,1,0:T(8,128)(2,1)S(1)}, u32[]{:S(2)}, u32[]{:S(2)}) %collective-permute-start.10) | collective-permute-done | bytes 589856 | tf_op jit(solution)/shard_map/ppermute | solution.py:284
  74.1 0.7 collective-permute-start.12
  75.0 1.4 %collective-permute-start.15 = (bf16[4,96,384]{2,1,0:T(8,128)(2,1)S(1)}, bf16[4,96,384]{2,1,0:T(8,128)(2,1)S(1)}, u32[]{:S(2)}, u32[]{:S(2)}) collective-permute-start(bf16[4,96,384]{2,1,0:T(8,128)(2,1)S(1)} %get-tuple-element.76), channel_id=1, source_target_pairs={{0,4},{4,0},{8,12},{12,8},{16,20},{20,16},{24,28},{28,24},{1,5},{5... | collective-permute-start | bytes 884744 | tf_op jit(solution)/shard_map/ppermute | solution.py:284
  76.4 6.0 %collective-permute-done.12 = bf16[4,96,384]{2,1,0:T(8,128)(2,1)S(1)} collective-permute-done((bf16[4,96,384]{2,1,0:T(8,128)(2,1)S(1)}, bf16[4,96,384]{2,1,0:T(8,128)(2,1)S(1)}, u32[]{:S(2)}, u32[]{:S(2)}) %collective-permute-start.12) | collective-permute-done | bytes 294944 | tf_op jit(solution)/shard_map/ppermute | solution.py:284
  82.5 0.7 collective-permute-done.15
  83.3 2.2 %collective-permute-start.16 = (bf16[2,96,384]{2,1,0:T(8,128)(2,1)S(1)}, bf16[2,96,384]{2,1,0:T(8,128)(2,1)S(1)}, u32[]{:S(2)}, u32[]{:S(2)}) collective-permute-start(bf16[2,96,384]{2,1,0:T(8,128)(2,1)S(1)} %get-tuple-element.82), channel_id=1, source_target_pairs={{0,8},{4,12},{8,0},{12,4},{16,24},{20,28},{24,16},{28,20},{1,9},{5... | collective-permute-start | bytes 442376 | tf_op jit(solution)/shard_map/ppermute | solution.py:284
  85.5 1.9 %shard_map.71 = bf16[512,384]{1,0:T(8,128)(2,1)} custom-call(s32[2]{0:T(128)} %copy-done, bf16[8,32,384]{2,1,0:T(8,128)(2,1)} %get-tuple-element.64.refs_0_, bf16[8,32,384]{2,1,0:T(8,128)(2,1)} %copy-done.2), custom_call_target="tpu_custom_call" | custom-call | bytes 786432 | tf_op jit(solution)/shard_map/pallas_call | solution.py:379
  87.4 3.0 %collective-permute-done.18 = bf16[2,96,384]{2,1,0:T(8,128)(2,1)S(1)} collective-permute-done((bf16[2,96,384]{2,1,0:T(8,128)(2,1)S(1)}, bf16[2,96,384]{2,1,0:T(8,128)(2,1)S(1)}, u32[]{:S(2)}, u32[]{:S(2)}) %collective-permute-start.18) | collective-permute-done | bytes 147488 | tf_op jit(solution)/shard_map/ppermute | solution.py:284
  90.7 1.9 %collective-permute-start.17 = (bf16[1,96,384]{2,1,0:T(8,128)(2,1)S(1)}, bf16[1,96,384]{2,1,0:T(8,128)(2,1)S(1)}, u32[]{:S(2)}, u32[]{:S(2)}) collective-permute-start(bf16[1,96,384]{2,1,0:T(8,128)(2,1)S(1)} %fusion.12), channel_id=1, source_target_pairs={{0,16},{4,20},{8,24},{12,28},{16,0},{20,4},{24,8},{28,12},{1,17},{... | collective-permute-start | bytes 221192 | tf_op jit(solution)/shard_map/ppermute | solution.py:284
  92.6 2.2 %collective-permute-done.19 = bf16[1,96,384]{2,1,0:T(8,128)(2,1)S(1)} collective-permute-done((bf16[1,96,384]{2,1,0:T(8,128)(2,1)S(1)}, bf16[1,96,384]{2,1,0:T(8,128)(2,1)S(1)}, u32[]{:S(2)}, u32[]{:S(2)}) %collective-permute-start.19) | collective-permute-done | bytes 73760 | tf_op jit(solution)/shard_map/ppermute | solution.py:284
  94.8 0.7 add_bitcast_fusion
  96.0 0.7 add_bitcast_fusion.1
  (45 shorter events, 4.9 us)
Async XLA Ops:
  0.6 7.6 %copy-start.1 = (bf16[512,384]{1,0:T(8,128)(2,1)S(1)}, bf16[512,384]{1,0:T(8,128)(2,1)}, u32[]{:S(2)}) copy-start(bf16[512,384]{1,0:T(8,128)(2,1)} %param.7) | copy-start | bytes 1179652
  0.6 21.7 %all-to-all-start = ((bf16[16,32,384]{2,1,0:T(8,128)(2,1)}), bf16[16,32,384]{2,1,0:T(8,128)(2,1)S(1)}, u32[]{:S(2)}, u32[]{:S(2)}) async-start(bf16[16,32,384]{2,1,0:T(8,128)(2,1)} %bitcast.93), calls=%async_computation | async-start | bytes 786432 | tf_op jit(solution)/shard_map/all_to_all | solution.py:40
  8.3 46.8 %copy-start = (s32[2]{0:T(128)}, s32[2]{0:T(128)S(1)}, u32[]{:S(2)}) copy-start(s32[2]{0:T(128)S(1)} %pad_add_fusion.place_ref) | copy-start | bytes 28
  8.3 1.5 %collective-permute-start = (bf16[2,2,2,1,32,384]{5,4,2,1,0,3:T(8,128)(2,1)S(1)}, bf16[2,2,2,1,32,384]{5,4,2,1,0,3:T(8,128)(2,1)S(1)}, u32[]{:S(2)}, u32[]{:S(2)}) collective-permute-start(bf16[2,2,2,1,32,384]{5,4,2,1,0,3:T(8,128)(2,1)S(1)} %get-tuple-element.97), channel_id=1, source_target_pairs={{0,1},{1,0},{2,3},{3,2},{4,5},{5,4},{6,7},{7,6},{8,9},{9,8},{10,11... | collective-permute-start | bytes 589832 | tf_op jit(solution)/shard_map/ppermute | solution.py:284
  10.0 6.7 %collective-permute-start.1 = (bf16[2,2,32,384]{3,2,1,0:T(8,128)(2,1)S(1)}, bf16[2,2,32,384]{3,2,1,0:T(8,128)(2,1)S(1)}, u32[]{:S(2)}, u32[]{:S(2)}) collective-permute-start(bf16[2,2,32,384]{3,2,1,0:T(8,128)(2,1)S(1)} %bitcast.99), channel_id=1, source_target_pairs={{0,2},{1,3},{2,0},{3,1},{4,6},{5,7},{6,4},{7,5},{8,10},{9,11},{10,... | collective-permute-start | bytes 294920 | tf_op jit(solution)/shard_map/ppermute | solution.py:284
  11.8 6.1 %collective-permute-start.2 = (bf16[2,2,32,384]{3,2,1,0:T(8,128)(2,1)S(1)}, bf16[2,2,32,384]{3,2,1,0:T(8,128)(2,1)S(1)}, u32[]{:S(2)}, u32[]{:S(2)}) collective-permute-start(bf16[2,2,32,384]{3,2,1,0:T(8,128)(2,1)S(1)} %bitcast.98), channel_id=1, source_target_pairs={{0,4},{4,0},{8,12},{12,8},{16,20},{20,16},{24,28},{28,24},{1,5},{5... | collective-permute-start | bytes 294920 | tf_op jit(solution)/shard_map/ppermute | solution.py:284
  13.3 5.5 %collective-permute-start.3 = (bf16[2,2,32,384]{3,2,1,0:T(8,128)(2,1)S(1)}, bf16[2,2,32,384]{3,2,1,0:T(8,128)(2,1)S(1)}, u32[]{:S(2)}, u32[]{:S(2)}) collective-permute-start(bf16[2,2,32,384]{3,2,1,0:T(8,128)(2,1)S(1)} %bitcast.97), channel_id=1, source_target_pairs={{0,6},{1,7},{2,4},{3,5},{4,2},{5,3},{6,0},{7,1},{8,14},{9,15},{10,... | collective-permute-start | bytes 294920 | tf_op jit(solution)/shard_map/ppermute | solution.py:373
  31.2 6.4 %collective-permute-start.6 = (bf16[2,2,1,32,384]{4,3,2,1,0:T(8,128)(2,1)S(1)}, bf16[2,2,1,32,384]{4,3,2,1,0:T(8,128)(2,1)S(1)}, u32[]{:S(2)}, u32[]{:S(2)}) collective-permute-start(bf16[2,2,1,32,384]{4,3,2,1,0:T(8,128)(2,1)S(1)} %get-tuple-element.90), channel_id=1, source_target_pairs={{0,6},{1,7},{2,4},{3,5},{4,2},{5,3},{6,0},{7,1},{8,14},{9,15},{10,... | collective-permute-start | bytes 294920 | tf_op jit(solution)/shard_map/ppermute | solution.py:373
  31.3 7.0 %collective-permute-start.5 = (bf16[2,2,1,32,384]{4,3,2,1,0:T(8,128)(2,1)S(1)}, bf16[2,2,1,32,384]{4,3,2,1,0:T(8,128)(2,1)S(1)}, u32[]{:S(2)}, u32[]{:S(2)}) collective-permute-start(bf16[2,2,1,32,384]{4,3,2,1,0:T(8,128)(2,1)S(1)} %get-tuple-element.91), channel_id=1, source_target_pairs={{0,4},{4,0},{8,12},{12,8},{16,20},{20,16},{24,28},{28,24},{1,5},{5... | collective-permute-start | bytes 294920 | tf_op jit(solution)/shard_map/ppermute | solution.py:284
  31.8 6.6 %collective-permute-start.4 = (bf16[2,2,1,32,384]{4,3,2,1,0:T(8,128)(2,1)S(1)}, bf16[2,2,1,32,384]{4,3,2,1,0:T(8,128)(2,1)S(1)}, u32[]{:S(2)}, u32[]{:S(2)}) collective-permute-start(bf16[2,2,1,32,384]{4,3,2,1,0:T(8,128)(2,1)S(1)} %get-tuple-element.92), channel_id=1, source_target_pairs={{0,2},{1,3},{2,0},{3,1},{4,6},{5,7},{6,4},{7,5},{8,10},{9,11},{10,... | collective-permute-start | bytes 294920 | tf_op jit(solution)/shard_map/ppermute | solution.py:284
  34.7 10.2 %collective-permute-start.7 = (bf16[8,32,384]{2,1,0:T(8,128)(2,1)S(1)}, bf16[8,32,384]{2,1,0:T(8,128)(2,1)S(1)}, u32[]{:S(2)}, u32[]{:S(2)}) collective-permute-start(bf16[8,32,384]{2,1,0:T(8,128)(2,1)S(1)} %get-tuple-element.48), channel_id=1, source_target_pairs={{0,16},{4,20},{8,24},{12,28},{16,0},{20,4},{24,8},{28,12},{1,17},{... | collective-permute-start | bytes 589832 | tf_op jit(solution)/shard_map/ppermute | solution.py:284
  54.5 3.8 %collective-permute-start.9 = (bf16[16,96,384]{2,1,0:T(8,128)(2,1)S(1)}, bf16[16,96,384]{2,1,0:T(8,128)(2,1)S(1)}, u32[]{:S(2)}, u32[]{:S(2)}) collective-permute-start(bf16[16,96,384]{2,1,0:T(8,128)(2,1)S(1)} %get-tuple-element.61), channel_id=1, source_target_pairs={{0,1},{1,0},{2,3},{3,2},{4,5},{5,4},{6,7},{7,6},{8,9},{9,8},{10,11... | collective-permute-start | bytes 3538952 | tf_op jit(solution)/shard_map/ppermute | solution.py:284
  54.5 4.6 %collective-permute-start.13 = (bf16[16,96,384]{2,1,0:T(8,128)(2,1)S(1)}, bf16[16,96,384]{2,1,0:T(8,128)(2,1)S(1)}, u32[]{:S(2)}, u32[]{:S(2)}) collective-permute-start(bf16[16,96,384]{2,1,0:T(8,128)(2,1)S(1)} %get-tuple-element.67), channel_id=1, source_target_pairs={{0,1},{1,0},{2,3},{3,2},{4,5},{5,4},{6,7},{7,6},{8,9},{9,8},{10,11... | collective-permute-start | bytes 3538952 | tf_op jit(solution)/shard_map/ppermute | solution.py:284
  58.6 15.4 %collective-permute-start.10 = (bf16[8,96,384]{2,1,0:T(8,128)(2,1)S(1)}, bf16[8,96,384]{2,1,0:T(8,128)(2,1)S(1)}, u32[]{:S(2)}, u32[]{:S(2)}) collective-permute-start(bf16[8,96,384]{2,1,0:T(8,128)(2,1)S(1)} %get-tuple-element.74), channel_id=1, source_target_pairs={{0,4},{4,0},{8,12},{12,8},{16,20},{20,16},{24,28},{28,24},{1,5},{5... | collective-permute-start | bytes 1769480 | tf_op jit(solution)/shard_map/ppermute | solution.py:284
  59.5 15.4 %collective-permute-start.14 = (bf16[8,96,384]{2,1,0:T(8,128)(2,1)S(1)}, bf16[8,96,384]{2,1,0:T(8,128)(2,1)S(1)}, u32[]{:S(2)}, u32[]{:S(2)}) collective-permute-start(bf16[8,96,384]{2,1,0:T(8,128)(2,1)S(1)} %get-tuple-element.72), channel_id=1, source_target_pairs={{0,2},{1,3},{2,0},{3,1},{4,6},{5,7},{6,4},{7,5},{8,10},{9,11},{10,... | collective-permute-start | bytes 1769480 | tf_op jit(solution)/shard_map/ppermute | solution.py:284
  61.0 10.4 %collective-permute-start.8 = (bf16[2,4,32,384]{3,2,1,0:T(8,128)(2,1)S(1)}, bf16[2,4,32,384]{3,2,1,0:T(8,128)(2,1)S(1)}, u32[]{:S(2)}, u32[]{:S(2)}) collective-permute-start(bf16[2,4,32,384]{3,2,1,0:T(8,128)(2,1)S(1)} %get-tuple-element.57), channel_id=1, source_target_pairs={{0,16},{4,20},{8,24},{12,28},{16,0},{20,4},{24,8},{28,12},{1,17},{... | collective-permute-start | bytes 589832 | tf_op jit(solution)/shard_map/ppermute | solution.py:284
  74.1 8.2 %collective-permute-start.12 = (bf16[4,96,384]{2,1,0:T(8,128)(2,1)S(1)}, bf16[4,96,384]{2,1,0:T(8,128)(2,1)S(1)}, u32[]{:S(2)}, u32[]{:S(2)}) collective-permute-start(bf16[4,96,384]{2,1,0:T(8,128)(2,1)S(1)} %get-tuple-element.63), channel_id=1, source_target_pairs={{0,2},{1,3},{2,0},{3,1},{4,6},{5,7},{6,4},{7,5},{8,10},{9,11},{10,... | collective-permute-start | bytes 884744 | tf_op jit(solution)/shard_map/ppermute | solution.py:284
  75.0 8.2 %collective-permute-start.15 = (bf16[4,96,384]{2,1,0:T(8,128)(2,1)S(1)}, bf16[4,96,384]{2,1,0:T(8,128)(2,1)S(1)}, u32[]{:S(2)}, u32[]{:S(2)}) collective-permute-start(bf16[4,96,384]{2,1,0:T(8,128)(2,1)S(1)} %get-tuple-element.76), channel_id=1, source_target_pairs={{0,4},{4,0},{8,12},{12,8},{16,20},{20,16},{24,28},{28,24},{1,5},{5... | collective-permute-start | bytes 884744 | tf_op jit(solution)/shard_map/ppermute | solution.py:284
  76.3 6.0 %collective-permute-start.11 = (bf16[8,32,384]{2,1,0:T(8,128)(2,1)S(1)}, bf16[8,32,384]{2,1,0:T(8,128)(2,1)S(1)}, u32[]{:S(2)}, u32[]{:S(2)}) collective-permute-start(bf16[8,32,384]{2,1,0:T(8,128)(2,1)S(1)} %get-tuple-element.62), channel_id=1, source_target_pairs={{0,1},{1,0},{2,3},{3,2},{4,5},{5,4},{6,7},{7,6},{8,9},{9,8},{10,11... | collective-permute-start | bytes 589832 | tf_op jit(solution)/shard_map/ppermute | solution.py:284
  82.4 3.1 %copy-start.2 = (bf16[8,32,384]{2,1,0:T(8,128)(2,1)}, bf16[8,32,384]{2,1,0:T(8,128)(2,1)S(1)}, u32[]{:S(2)}) copy-start(bf16[8,32,384]{2,1,0:T(8,128)(2,1)S(1)} %collective-permute-done.11.refs_1_) | copy-start | bytes 589828
  82.4 7.9 %collective-permute-start.18 = (bf16[2,96,384]{2,1,0:T(8,128)(2,1)S(1)}, bf16[2,96,384]{2,1,0:T(8,128)(2,1)S(1)}, u32[]{:S(2)}, u32[]{:S(2)}) collective-permute-start(bf16[2,96,384]{2,1,0:T(8,128)(2,1)S(1)} %get-tuple-element.70), channel_id=1, source_target_pairs={{0,16},{4,20},{8,24},{12,28},{16,0},{20,4},{24,8},{28,12},{1,17},{... | collective-permute-start | bytes 442376 | tf_op jit(solution)/shard_map/ppermute | solution.py:284
  83.3 7.4 %collective-permute-start.16 = (bf16[2,96,384]{2,1,0:T(8,128)(2,1)S(1)}, bf16[2,96,384]{2,1,0:T(8,128)(2,1)S(1)}, u32[]{:S(2)}, u32[]{:S(2)}) collective-permute-start(bf16[2,96,384]{2,1,0:T(8,128)(2,1)S(1)} %get-tuple-element.82), channel_id=1, source_target_pairs={{0,8},{4,12},{8,0},{12,4},{16,24},{20,28},{24,16},{28,20},{1,9},{5... | collective-permute-start | bytes 442376 | tf_op jit(solution)/shard_map/ppermute | solution.py:284
  90.4 4.4 %collective-permute-start.19 = (bf16[1,96,384]{2,1,0:T(8,128)(2,1)S(1)}, bf16[1,96,384]{2,1,0:T(8,128)(2,1)S(1)}, u32[]{:S(2)}, u32[]{:S(2)}) collective-permute-start(bf16[1,96,384]{2,1,0:T(8,128)(2,1)S(1)} %fusion.10), channel_id=1, source_target_pairs={{0,8},{4,12},{8,0},{12,4},{16,24},{20,28},{24,16},{28,20},{1,9},{5... | collective-permute-start | bytes 221192 | tf_op jit(solution)/shard_map/ppermute | solution.py:284
  90.7 5.3 %collective-permute-start.17 = (bf16[1,96,384]{2,1,0:T(8,128)(2,1)S(1)}, bf16[1,96,384]{2,1,0:T(8,128)(2,1)S(1)}, u32[]{:S(2)}, u32[]{:S(2)}) collective-permute-start(bf16[1,96,384]{2,1,0:T(8,128)(2,1)S(1)} %fusion.12), channel_id=1, source_target_pairs={{0,16},{4,20},{8,24},{12,28},{16,0},{20,4},{24,8},{28,12},{1,17},{... | collective-permute-start | bytes 221192 | tf_op jit(solution)/shard_map/ppermute | solution.py:284

commit v22 on v21

--- a/solution.py
+++ b/solution.py
@@ -419,25 +419,23 @@
     state = coming.hop(z, steps, halves, state)
     state, *kept = forward(state, up, w_down)
     going = Journey(state.reshape(parts))
-    going.hop_both(x, y, steps, halves)
     d_pre, grad_t, *given = backward(place, coming.held, kept, places, block)
     hidden, normed_t = kept[0], kept[3]
     if not given:
-        going.hop(z, steps, halves)
-        going.hop(core, steps, halves)
+        for at in (x, z, core, y):
+            going.hop(at, steps, halves)
         mixed_out = settle(place, going)
         grad_down = scatter_narrow(halves, grad_t, hidden, [steps[core]] + order_down, span_x, span_y)
         grad_up = scatter_narrow(halves, normed_t, d_pre, [steps[core]] + order_up, span_x, span_y)
         return (mixed_out, grad_up, grad_down)
-    given[0] = going.hop(z, steps, halves, given[0])
+    given[1] = going.hop(x, steps, halves, given[1])
     take_down, take_up = [swap(part, *steps[core]) for part in given]
     keep_down, keep_up = keep_blocks(place, hidden, d_pre, normed_t, grad_t, places, block)
 
     def beside(phase, give):
-        if phase == 1:
-            return going.hop(core, steps, halves, give)
-        if phase == 2:
-            going.parts, give = lax.optimization_barrier((going.parts, give))
+        if phase < 3:
+            return going.hop((z, core, y)[phase], steps, halves, give)
+        going.parts, give = lax.optimization_barrier((going.parts, give))
         return give
 
     grad_up = finish_sum(halves, keep_up, take_up, order_up)

time: 97 us -> 91.6 us (0.944)
  starting transfers between devices: 24.6 us -> 21.3 us
  waiting for transfers between devices: 41.8 us -> 39 us
    ppermute x18, starting transfers between devices: 16.8 us -> 13.7 us  [swap(): return lax.ppermute(block, axis, pairs)]
    ppermute x2 -> x1, waiting for transfers between devices: 3.09 us -> 0.93 us  [swap_both(): return lax.ppermute(block, ('gx', 'gy'), pairs)]
  transfers between devices with their start and end apart: 21 -> 20, of which waited for: 16 -> 14; matrix products, arithmetic and copies ran while one was open for 3% -> 3% of each run, Pallas kernels for 8% -> 18%
where the time goes in v22:
time: 91.6 us; the launch traced here: 91.2 us
  waiting for transfers between devices  39 us (43%)
  Pallas kernels  25.5 us (28%)
  starting transfers between devices  21.3 us (23%)
  other arithmetic  3.58 us (4%)
  between operations  0.98 us (1%)
    ppermute x18, waiting for transfers between devices, swap(): return lax.ppermute(block, axis, pairs)  34.6 us
    ppermute x18, starting transfers between devices, swap(): return lax.ppermute(block, axis, pairs)  13.7 us
    pallas_call x1, Pallas kernels, backward(): pl.pallas_call(functools.partial(backward_kernel, *places), out_shape=out...  9.48 us
    pallas_call x1, Pallas kernels, forward(): pl.pallas_call(forward_kernel, out_shape=outs, in_specs=[spec(pltpu.VMEM)...  8.78 us
    all_to_all x1, starting transfers between devices, exchange(): lax.all_to_all(block, ('gx', 'gy'), split_axis=0, concat_axis=0, axis_ind...  7.44 us
    all_to_all x1, waiting for transfers between devices, exchange(): lax.all_to_all(block, ('gx', 'gy'), split_axis=0, concat_axis=0, axis_ind...  3.4 us
    pallas_call x1, Pallas kernels, keep_blocks(): pl.pallas_call(functools.partial(keep_kernel, *places), out_shape=[block]...  3.17 us
    pallas_call x1, Pallas kernels, load(): pl.pallas_call(load_kernel, out_shape=pltpu.VMEM(weight.shape, weight.dty...  2.21 us
  transfers between devices with their start and end apart: 20, of which 14 were waited for; matrix products, arithmetic and copies ran while one was open for 3% of the time, Pallas kernels for 18%

profile of v22, /device:TPU:0, one launch (start us, length us, event | category | flops | bytes accessed | tf_op | source)
XLA Modules:
  0.0 91.2 jit_solution(12542958242964305384)
XLA Ops:
  0.6 7.4 %all-to-all-start = ((bf16[16,32,384]{2,1,0:T(8,128)(2,1)}), bf16[16,32,384]{2,1,0:T(8,128)(2,1)S(1)}, u32[]{:S(2)}, u32[]{:S(2)}) async-start(bf16[16,32,384]{2,1,0:T(8,128)(2,1)} %bitcast.96), calls=%async_computation | async-start | bytes 786432 | tf_op jit(solution)/shard_map/all_to_all | solution.py:40
  8.7 1.1 %collective-permute-done = bf16[2,2,2,1,32,384]{5,4,2,1,0,3:T(8,128)(2,1)S(1)} collective-permute-done((bf16[2,2,2,1,32,384]{5,4,2,1,0,3:T(8,128)(2,1)S(1)}, bf16[2,2,2,1,32,384]{5,4,2,1,0,3:T(8,128)(2,1)S(1)}, u32[]{:S(2)}, u32[]{:S(2)}) %collective-permute-start) | collective-permute-done | bytes 196640 | tf_op jit(solution)/shard_map/ppermute | solution.py:284
  10.0 1.9 %collective-permute-start.1 = (bf16[2,2,32,384]{3,2,1,0:T(8,128)(2,1)S(1)}, bf16[2,2,32,384]{3,2,1,0:T(8,128)(2,1)S(1)}, u32[]{:S(2)}, u32[]{:S(2)}) collective-permute-start(bf16[2,2,32,384]{3,2,1,0:T(8,128)(2,1)S(1)} %bitcast.103), channel_id=1, source_target_pairs={{0,2},{1,3},{2,0},{3,1},{4,6},{5,7},{6,4},{7,5},{8,10},{9,11},{10,... | collective-permute-start | bytes 294920 | tf_op jit(solution)/shard_map/ppermute | solution.py:284
  11.8 1.5 %collective-permute-start.2 = (bf16[2,2,32,384]{3,2,1,0:T(8,128)(2,1)S(1)}, bf16[2,2,32,384]{3,2,1,0:T(8,128)(2,1)S(1)}, u32[]{:S(2)}, u32[]{:S(2)}) collective-permute-start(bf16[2,2,32,384]{3,2,1,0:T(8,128)(2,1)S(1)} %bitcast.102), channel_id=1, source_target_pairs={{0,4},{4,0},{8,12},{12,8},{16,20},{20,16},{24,28},{28,24},{1,5},{5... | collective-permute-start | bytes 294920 | tf_op jit(solution)/shard_map/ppermute | solution.py:284
  13.5 2.2 %shard_map.67.up_ref = bf16[768,1536]{1,0:T(8,128)(2,1)S(1)} custom-call(s32[2]{0:T(128)S(1)} %pad_add_fusion.place_ref, bf16[768,1536]{1,0:T(8,128)(2,1)} %source.1), custom_call_target="tpu_custom_call" | custom-call | bytes 4718592 | tf_op jit(solution)/shard_map/pallas_call | solution.py:209
  15.7 0.9 collective-permute-done.1
  16.6 1.3 %collective-permute-done.2 = bf16[2,2,32,384]{3,2,1,0:T(8,128)(2,1)S(1)} collective-permute-done((bf16[2,2,32,384]{3,2,1,0:T(8,128)(2,1)S(1)}, bf16[2,2,32,384]{3,2,1,0:T(8,128)(2,1)S(1)}, u32[]{:S(2)}, u32[]{:S(2)}) %collective-permute-start.2) | collective-permute-done | bytes 98336 | tf_op jit(solution)/shard_map/ppermute | solution.py:284
  17.9 0.9 %collective-permute-done.3 = bf16[2,2,32,384]{3,2,1,0:T(8,128)(2,1)S(1)} collective-permute-done((bf16[2,2,32,384]{3,2,1,0:T(8,128)(2,1)S(1)}, bf16[2,2,32,384]{3,2,1,0:T(8,128)(2,1)S(1)}, u32[]{:S(2)}, u32[]{:S(2)}) %collective-permute-start.3) | collective-permute-done | bytes 98336 | tf_op jit(solution)/shard_map/ppermute | solution.py:373
  18.9 3.4 %all-to-all-done.state_ref = bf16[16,32,384]{2,1,0:T(8,128)(2,1)S(1)} async-done(((bf16[16,32,384]{2,1,0:T(8,128)(2,1)}), bf16[16,32,384]{2,1,0:T(8,128)(2,1)S(1)}, u32[]{:S(2)}, u32[]{:S(2)}) %all-to-all-start) | async-done | bytes 393248 | tf_op jit(solution)/shard_map/all_to_all | solution.py:40
  22.3 0.8 collective-permute-start.4
  23.1 8.8 %shard_map.68 = (bf16[16,32,384]{2,1,0:T(8,128)(2,1)S(1)}, bf16[1024,1536]{1,0:T(8,128)(2,1)S(1)}, bf16[1024,1536]{1,0:T(8,128)(2,1)S(1)}, bf16[1024,768]{1,0:T(...) custom-call(bf16[16,32,384]{2,1,0:T(8,128)(2,1)S(1)} %all-to-all-don, ...), custom_call_target="tpu_custom_call" | custom-call | flops 12079595520 | bytes 25165824 | tf_op jit(solution)/shard_map/pallas_call | solution.py:235
  31.9 1.6 %collective-permute-done.4 = bf16[8,32,384]{2,1,0:T(8,128)(2,1)S(1)} collective-permute-done((bf16[8,32,384]{2,1,0:T(8,128)(2,1)S(1)}, bf16[8,32,384]{2,1,0:T(8,128)(2,1)S(1)}, u32[]{:S(2)}, u32[]{:S(2)}) %collective-permute-start.4) | collective-permute-done | bytes 196640 | tf_op jit(solution)/shard_map/ppermute | solution.py:284
  33.5 9.5 %shard_map.69 = (bf16[1024,1536]{1,0:T(8,128)(2,1)S(1)}, bf16[768,1024]{1,0:T(8,128)(2,1)S(1)}, bf16[16,96,384]{2,1,0:T(8,128)(2,1)S(1)}, bf16[16,96,384]{2,1,0:T(8,128)(2,1)S(1)}) custom-call(s32[2]{0:T(128)S(1)} %pad_add_fusion.place_ref, bf16[16,32,384]{2,1,0:T(8,128)(2,1)S(1)} %pad_maximum_fusion.1.grad_ref, ...), custom_call_target="tpu_custom_call" | custom-call | flops 12079595520 | bytes 25165824 | tf_op jit(solution)/shard_map/pallas_call | solution.py:254
  43.7 0.6 collective-permute-start.5
  44.3 3.2 %shard_map.70 = (bf16[16,96,384]{2,1,0:T(8,128)(2,1)S(1)}, bf16[16,96,384]{2,1,0:T(8,128)(2,1)S(1)}) custom-call(s32[2]{0:T(128)S(1)} %pad_add_fusion.place_ref, bf16[1024,1536]{1,0:T(8,128)(2,1)S(1)} %get-tuple-element.53.hidden_ref, bf16[1024,1536]{1,0:T(8,128)(2,1)S(1)} %get-tuple-element.62.d_pre_ref, ...), custom_call_target="tpu_custom_call" | custom-call | flops 2415919104 | bytes 12582912 | tf_op jit(solution)/shard_map/pallas_call | solution.py:270
  47.5 3.1 %collective-permute-done.5 = bf16[2,2,2,1,32,384]{5,4,2,1,0,3:T(8,128)(2,1)S(1)} collective-permute-done((bf16[2,2,2,1,32,384]{5,4,2,1,0,3:T(8,128)(2,1)S(1)}, bf16[2,2,2,1,32,384]{5,4,2,1,0,3:T(8,128)(2,1)S(1)}, u32[]{:S(2)}, u32[]{:S(2)}) %collective-permute-start.5) | collective-permute-done | bytes 196640 | tf_op jit(solution)/shard_map/ppermute | solution.py:284
  51.0 0.6 collective-permute-start.8
  51.9 1.5 %collective-permute-start.14 = (bf16[8,96,384]{2,1,0:T(8,128)(2,1)S(1)}, bf16[8,96,384]{2,1,0:T(8,128)(2,1)S(1)}, u32[]{:S(2)}, u32[]{:S(2)}) collective-permute-start(bf16[8,96,384]{2,1,0:T(8,128)(2,1)S(1)} %get-tuple-element.80), channel_id=1, source_target_pairs={{0,2},{1,3},{2,0},{3,1},{4,6},{5,7},{6,4},{7,5},{8,10},{9,11},{10,... | collective-permute-start | bytes 1769480 | tf_op jit(solution)/shard_map/ppermute | solution.py:284
  53.5 10.4 %collective-permute-done.7 = bf16[2,2,2,32,384]{4,3,2,0,1:T(8,128)(2,1)S(1)} collective-permute-done((bf16[2,2,2,32,384]{4,3,2,0,1:T(8,128)(2,1)S(1)}, bf16[2,2,2,32,384]{4,3,2,0,1:T(8,128)(2,1)S(1)}, u32[]{:S(2)}, u32[]{:S(2)}) %collective-permute-start.7) | collective-permute-done | bytes 196640 | tf_op jit(solution)/shard_map/ppermute | solution.py:284
  63.9 1.6 %collective-permute-done.8 = bf16[8,96,384]{2,1,0:T(8,128)(2,1)S(1)} collective-permute-done((bf16[8,96,384]{2,1,0:T(8,128)(2,1)S(1)}, bf16[8,96,384]{2,1,0:T(8,128)(2,1)S(1)}, u32[]{:S(2)}, u32[]{:S(2)}) %collective-permute-start.8) | collective-permute-done | bytes 589856 | tf_op jit(solution)/shard_map/ppermute | solution.py:284
  66.3 1.6 %collective-permute-start.15 = (bf16[4,96,384]{2,1,0:T(8,128)(2,1)S(1)}, bf16[4,96,384]{2,1,0:T(8,128)(2,1)S(1)}, u32[]{:S(2)}, u32[]{:S(2)}) collective-permute-start(bf16[4,96,384]{2,1,0:T(8,128)(2,1)S(1)} %get-tuple-element.84), channel_id=1, source_target_pairs={{0,4},{4,0},{8,12},{12,8},{16,20},{20,16},{24,28},{28,24},{1,5},{5... | collective-permute-start | bytes 884744 | tf_op jit(solution)/shard_map/ppermute | solution.py:284
  67.9 0.6 collective-permute-start.10
  68.5 0.7 fusion.5
  69.2 6.2 %collective-permute-done.15 = bf16[4,96,384]{2,1,0:T(8,128)(2,1)S(1)} collective-permute-done((bf16[4,96,384]{2,1,0:T(8,128)(2,1)S(1)}, bf16[4,96,384]{2,1,0:T(8,128)(2,1)S(1)}, u32[]{:S(2)}, u32[]{:S(2)}) %collective-permute-start.15) | collective-permute-done | bytes 294944 | tf_op jit(solution)/shard_map/ppermute | solution.py:284
  75.9 2.6 %collective-permute-start.12 = (bf16[2,96,384]{2,1,0:T(8,128)(2,1)S(1)}, bf16[2,96,384]{2,1,0:T(8,128)(2,1)S(1)}, u32[]{:S(2)}, u32[]{:S(2)}) collective-permute-start(bf16[2,96,384]{2,1,0:T(8,128)(2,1)S(1)} %get-tuple-element.72), channel_id=1, source_target_pairs={{0,16},{4,20},{8,24},{12,28},{16,0},{20,4},{24,8},{28,12},{1,17},{... | collective-permute-start | bytes 442376 | tf_op jit(solution)/shard_map/ppermute | solution.py:284
  79.1 4.2 %collective-permute-done.16 = bf16[2,96,384]{2,1,0:T(8,128)(2,1)S(1)} collective-permute-done((bf16[2,96,384]{2,1,0:T(8,128)(2,1)S(1)}, bf16[2,96,384]{2,1,0:T(8,128)(2,1)S(1)}, u32[]{:S(2)}, u32[]{:S(2)}) %collective-permute-start.16) | collective-permute-done | bytes 147488 | tf_op jit(solution)/shard_map/ppermute | solution.py:284
  83.3 2.7 %collective-permute-done.12 = bf16[2,96,384]{2,1,0:T(8,128)(2,1)S(1)} collective-permute-done((bf16[2,96,384]{2,1,0:T(8,128)(2,1)S(1)}, bf16[2,96,384]{2,1,0:T(8,128)(2,1)S(1)}, u32[]{:S(2)}, u32[]{:S(2)}) %collective-permute-start.12) | collective-permute-done | bytes 147488 | tf_op jit(solution)/shard_map/ppermute | solution.py:284
  86.2 0.6 copy-done.2
  86.8 1.9 %shard_map.71 = bf16[512,384]{1,0:T(8,128)(2,1)} custom-call(s32[2]{0:T(128)} %copy-done, bf16[8,32,384]{2,1,0:T(8,128)(2,1)} %get-tuple-element.73.refs_0_, bf16[8,32,384]{2,1,0:T(8,128)(2,1)} %copy-done.2), custom_call_target="tpu_custom_call" | custom-call | bytes 786432 | tf_op jit(solution)/shard_map/pallas_call | solution.py:379
  88.7 0.7 add_bitcast_fusion.1
  89.4 1.1 %collective-permute-done.18 = bf16[1,96,384]{2,1,0:T(8,128)(2,1)S(1)} collective-permute-done((bf16[1,96,384]{2,1,0:T(8,128)(2,1)S(1)}, bf16[1,96,384]{2,1,0:T(8,128)(2,1)S(1)}, u32[]{:S(2)}, u32[]{:S(2)}) %collective-permute-start.18) | collective-permute-done | bytes 73760 | tf_op jit(solution)/shard_map/ppermute | solution.py:284
  90.6 0.7 add_bitcast_fusion
  (45 shorter events, 4.4 us)
Async XLA Ops:
  0.6 7.6 %copy-start.1 = (bf16[512,384]{1,0:T(8,128)(2,1)S(1)}, bf16[512,384]{1,0:T(8,128)(2,1)}, u32[]{:S(2)}) copy-start(bf16[512,384]{1,0:T(8,128)(2,1)} %param.7) | copy-start | bytes 1179652
  0.6 21.7 %all-to-all-start = ((bf16[16,32,384]{2,1,0:T(8,128)(2,1)}), bf16[16,32,384]{2,1,0:T(8,128)(2,1)S(1)}, u32[]{:S(2)}, u32[]{:S(2)}) async-start(bf16[16,32,384]{2,1,0:T(8,128)(2,1)} %bitcast.96), calls=%async_computation | async-start | bytes 786432 | tf_op jit(solution)/shard_map/all_to_all | solution.py:40
  8.3 36.0 %copy-start = (s32[2]{0:T(128)}, s32[2]{0:T(128)S(1)}, u32[]{:S(2)}) copy-start(s32[2]{0:T(128)S(1)} %pad_add_fusion.place_ref) | copy-start | bytes 28
  8.3 1.5 %collective-permute-start = (bf16[2,2,2,1,32,384]{5,4,2,1,0,3:T(8,128)(2,1)S(1)}, bf16[2,2,2,1,32,384]{5,4,2,1,0,3:T(8,128)(2,1)S(1)}, u32[]{:S(2)}, u32[]{:S(2)}) collective-permute-start(bf16[2,2,2,1,32,384]{5,4,2,1,0,3:T(8,128)(2,1)S(1)} %get-tuple-element.105), channel_id=1, source_target_pairs={{0,1},{1,0},{2,3},{3,2},{4,5},{5,4},{6,7},{7,6},{8,9},{9,8},{10,11... | collective-permute-start | bytes 589832 | tf_op jit(solution)/shard_map/ppermute | solution.py:284
  10.0 6.7 %collective-permute-start.1 = (bf16[2,2,32,384]{3,2,1,0:T(8,128)(2,1)S(1)}, bf16[2,2,32,384]{3,2,1,0:T(8,128)(2,1)S(1)}, u32[]{:S(2)}, u32[]{:S(2)}) collective-permute-start(bf16[2,2,32,384]{3,2,1,0:T(8,128)(2,1)S(1)} %bitcast.103), channel_id=1, source_target_pairs={{0,2},{1,3},{2,0},{3,1},{4,6},{5,7},{6,4},{7,5},{8,10},{9,11},{10,... | collective-permute-start | bytes 294920 | tf_op jit(solution)/shard_map/ppermute | solution.py:284
  11.8 6.1 %collective-permute-start.2 = (bf16[2,2,32,384]{3,2,1,0:T(8,128)(2,1)S(1)}, bf16[2,2,32,384]{3,2,1,0:T(8,128)(2,1)S(1)}, u32[]{:S(2)}, u32[]{:S(2)}) collective-permute-start(bf16[2,2,32,384]{3,2,1,0:T(8,128)(2,1)S(1)} %bitcast.102), channel_id=1, source_target_pairs={{0,4},{4,0},{8,12},{12,8},{16,20},{20,16},{24,28},{28,24},{1,5},{5... | collective-permute-start | bytes 294920 | tf_op jit(solution)/shard_map/ppermute | solution.py:284
  13.3 5.5 %collective-permute-start.3 = (bf16[2,2,32,384]{3,2,1,0:T(8,128)(2,1)S(1)}, bf16[2,2,32,384]{3,2,1,0:T(8,128)(2,1)S(1)}, u32[]{:S(2)}, u32[]{:S(2)}) collective-permute-start(bf16[2,2,32,384]{3,2,1,0:T(8,128)(2,1)S(1)} %bitcast.101), channel_id=1, source_target_pairs={{0,6},{1,7},{2,4},{3,5},{4,2},{5,3},{6,0},{7,1},{8,14},{9,15},{10,... | collective-permute-start | bytes 294920 | tf_op jit(solution)/shard_map/ppermute | solution.py:373
  22.3 11.1 %collective-permute-start.4 = (bf16[8,32,384]{2,1,0:T(8,128)(2,1)S(1)}, bf16[8,32,384]{2,1,0:T(8,128)(2,1)S(1)}, u32[]{:S(2)}, u32[]{:S(2)}) collective-permute-start(bf16[8,32,384]{2,1,0:T(8,128)(2,1)S(1)} %get-tuple-element.52), channel_id=1, source_target_pairs={{0,16},{4,20},{8,24},{12,28},{16,0},{20,4},{24,8},{28,12},{1,17},{... | collective-permute-start | bytes 589832 | tf_op jit(solution)/shard_map/ppermute | solution.py:284
  43.0 7.7 %collective-permute-start.6 = (bf16[16,96,384]{2,1,0:T(8,128)(2,1)S(1)}, bf16[16,96,384]{2,1,0:T(8,128)(2,1)S(1)}, u32[]{:S(2)}, u32[]{:S(2)}) collective-permute-start(bf16[16,96,384]{2,1,0:T(8,128)(2,1)S(1)} %get-tuple-element.65), channel_id=1, source_target_pairs={{0,1},{1,0},{2,3},{3,2},{4,5},{5,4},{6,7},{7,6},{8,9},{9,8},{10,11... | collective-permute-start | bytes 3538952 | tf_op jit(solution)/shard_map/ppermute | solution.py:284
  43.1 8.4 %collective-permute-start.13 = (bf16[16,96,384]{2,1,0:T(8,128)(2,1)S(1)}, bf16[16,96,384]{2,1,0:T(8,128)(2,1)S(1)}, u32[]{:S(2)}, u32[]{:S(2)}) collective-permute-start(bf16[16,96,384]{2,1,0:T(8,128)(2,1)S(1)} %get-tuple-element.76), channel_id=1, source_target_pairs={{0,1},{1,0},{2,3},{3,2},{4,5},{5,4},{6,7},{7,6},{8,9},{9,8},{10,11... | collective-permute-start | bytes 3538952 | tf_op jit(solution)/shard_map/ppermute | solution.py:284
  43.7 6.9 %collective-permute-start.5 = (bf16[2,2,2,1,32,384]{5,4,2,1,0,3:T(8,128)(2,1)S(1)}, bf16[2,2,2,1,32,384]{5,4,2,1,0,3:T(8,128)(2,1)S(1)}, u32[]{:S(2)}, u32[]{:S(2)}) collective-permute-start(bf16[2,2,2,1,32,384]{5,4,2,1,0,3:T(8,128)(2,1)S(1)} %get-tuple-element.61), channel_id=1, source_target_pairs={{0,2},{1,3},{2,0},{3,1},{4,6},{5,7},{6,4},{7,5},{8,10},{9,11},{10,... | collective-permute-start | bytes 589832 | tf_op jit(solution)/shard_map/ppermute | solution.py:284
  51.0 14.5 %collective-permute-start.8 = (bf16[8,96,384]{2,1,0:T(8,128)(2,1)S(1)}, bf16[8,96,384]{2,1,0:T(8,128)(2,1)S(1)}, u32[]{:S(2)}, u32[]{:S(2)}) collective-permute-start(bf16[8,96,384]{2,1,0:T(8,128)(2,1)S(1)} %get-tuple-element.67), channel_id=1, source_target_pairs={{0,4},{4,0},{8,12},{12,8},{16,20},{20,16},{24,28},{28,24},{1,5},{5... | collective-permute-start | bytes 1769480 | tf_op jit(solution)/shard_map/ppermute | solution.py:284
  51.9 14.3 %collective-permute-start.14 = (bf16[8,96,384]{2,1,0:T(8,128)(2,1)S(1)}, bf16[8,96,384]{2,1,0:T(8,128)(2,1)S(1)}, u32[]{:S(2)}, u32[]{:S(2)}) collective-permute-start(bf16[8,96,384]{2,1,0:T(8,128)(2,1)S(1)} %get-tuple-element.80), channel_id=1, source_target_pairs={{0,2},{1,3},{2,0},{3,1},{4,6},{5,7},{6,4},{7,5},{8,10},{9,11},{10,... | collective-permute-start | bytes 1769480 | tf_op jit(solution)/shard_map/ppermute | solution.py:284
  53.4 10.4 %collective-permute-start.7 = (bf16[2,2,2,32,384]{4,3,2,0,1:T(8,128)(2,1)S(1)}, bf16[2,2,2,32,384]{4,3,2,0,1:T(8,128)(2,1)S(1)}, u32[]{:S(2)}, u32[]{:S(2)}) collective-permute-start(bf16[2,2,2,32,384]{4,3,2,0,1:T(8,128)(2,1)S(1)} %bitcast.100), channel_id=1, source_target_pairs={{0,16},{4,20},{8,24},{12,28},{16,0},{20,4},{24,8},{28,12},{1,17},{... | collective-permute-start | bytes 589832 | tf_op jit(solution)/shard_map/ppermute | solution.py:284
  65.7 2.8 %collective-permute-start.9 = (bf16[2,4,32,384]{3,2,1,0:T(8,128)(2,1)S(1)}, bf16[2,4,32,384]{3,2,1,0:T(8,128)(2,1)S(1)}, u32[]{:S(2)}, u32[]{:S(2)}) collective-permute-start(bf16[2,4,32,384]{3,2,1,0:T(8,128)(2,1)S(1)} %get-tuple-element.68), channel_id=1, source_target_pairs={{0,1},{1,0},{2,3},{3,2},{4,5},{5,4},{6,7},{7,6},{8,9},{9,8},{10,11... | collective-permute-start | bytes 589832 | tf_op jit(solution)/shard_map/ppermute | solution.py:284
  66.3 9.1 %collective-permute-start.15 = (bf16[4,96,384]{2,1,0:T(8,128)(2,1)S(1)}, bf16[4,96,384]{2,1,0:T(8,128)(2,1)S(1)}, u32[]{:S(2)}, u32[]{:S(2)}) collective-permute-start(bf16[4,96,384]{2,1,0:T(8,128)(2,1)S(1)} %get-tuple-element.84), channel_id=1, source_target_pairs={{0,4},{4,0},{8,12},{12,8},{16,20},{20,16},{24,28},{28,24},{1,5},{5... | collective-permute-start | bytes 884744 | tf_op jit(solution)/shard_map/ppermute | solution.py:284
  67.9 7.9 %collective-permute-start.10 = (bf16[4,96,384]{2,1,0:T(8,128)(2,1)S(1)}, bf16[4,96,384]{2,1,0:T(8,128)(2,1)S(1)}, u32[]{:S(2)}, u32[]{:S(2)}) collective-permute-start(bf16[4,96,384]{2,1,0:T(8,128)(2,1)S(1)} %get-tuple-element.69), channel_id=1, source_target_pairs={{0,2},{1,3},{2,0},{3,1},{4,6},{5,7},{6,4},{7,5},{8,10},{9,11},{10,... | collective-permute-start | bytes 884744 | tf_op jit(solution)/shard_map/ppermute | solution.py:284
  75.5 7.7 %collective-permute-start.16 = (bf16[2,96,384]{2,1,0:T(8,128)(2,1)S(1)}, bf16[2,96,384]{2,1,0:T(8,128)(2,1)S(1)}, u32[]{:S(2)}, u32[]{:S(2)}) collective-permute-start(bf16[2,96,384]{2,1,0:T(8,128)(2,1)S(1)} %get-tuple-element.88), channel_id=1, source_target_pairs={{0,8},{4,12},{8,0},{12,4},{16,24},{20,28},{24,16},{28,20},{1,9},{5... | collective-permute-start | bytes 442376 | tf_op jit(solution)/shard_map/ppermute | solution.py:284
  75.9 10.2 %collective-permute-start.12 = (bf16[2,96,384]{2,1,0:T(8,128)(2,1)S(1)}, bf16[2,96,384]{2,1,0:T(8,128)(2,1)S(1)}, u32[]{:S(2)}, u32[]{:S(2)}) collective-permute-start(bf16[2,96,384]{2,1,0:T(8,128)(2,1)S(1)} %get-tuple-element.72), channel_id=1, source_target_pairs={{0,16},{4,20},{8,24},{12,28},{16,0},{20,4},{24,8},{28,12},{1,17},{... | collective-permute-start | bytes 442376 | tf_op jit(solution)/shard_map/ppermute | solution.py:284
  78.5 7.6 %collective-permute-start.11 = (bf16[8,32,384]{2,1,0:T(8,128)(2,1)S(1)}, bf16[8,32,384]{2,1,0:T(8,128)(2,1)S(1)}, u32[]{:S(2)}, u32[]{:S(2)}) collective-permute-start(bf16[8,32,384]{2,1,0:T(8,128)(2,1)S(1)} %get-tuple-element.70), channel_id=1, source_target_pairs={{0,4},{4,0},{8,12},{12,8},{16,20},{20,16},{24,28},{28,24},{1,5},{5... | collective-permute-start | bytes 589832 | tf_op jit(solution)/shard_map/ppermute | solution.py:284
  83.3 5.5 %collective-permute-start.17 = (bf16[1,96,384]{2,1,0:T(8,128)(2,1)S(1)}, bf16[1,96,384]{2,1,0:T(8,128)(2,1)S(1)}, u32[]{:S(2)}, u32[]{:S(2)}) collective-permute-start(bf16[1,96,384]{2,1,0:T(8,128)(2,1)S(1)} %fusion.17), channel_id=1, source_target_pairs={{0,16},{4,20},{8,24},{12,28},{16,0},{20,4},{24,8},{28,12},{1,17},{... | collective-permute-start | bytes 221192 | tf_op jit(solution)/shard_map/ppermute | solution.py:284
  86.1 0.7 copy-start.2
  86.1 4.4 %collective-permute-start.18 = (bf16[1,96,384]{2,1,0:T(8,128)(2,1)S(1)}, bf16[1,96,384]{2,1,0:T(8,128)(2,1)S(1)}, u32[]{:S(2)}, u32[]{:S(2)}) collective-permute-start(bf16[1,96,384]{2,1,0:T(8,128)(2,1)S(1)} %fusion.19), channel_id=1, source_target_pairs={{0,8},{4,12},{8,0},{12,4},{16,24},{20,28},{24,16},{28,20},{1,9},{5... | collective-permute-start | bytes 221192 | tf_op jit(solution)/shard_map/ppermute | solution.py:284

commit v23 on v21

--- a/solution.py
+++ b/solution.py
@@ -419,7 +419,7 @@
     state = coming.hop(z, steps, halves, state)
     state, *kept = forward(state, up, w_down)
     going = Journey(state.reshape(parts))
-    going.hop_both(x, y, steps, halves)
+    kept[4] = going.hop_both(x, y, steps, halves, kept[4])
     d_pre, grad_t, *given = backward(place, coming.held, kept, places, block)
     hidden, normed_t = kept[0], kept[3]
     if not given:

time: 97 us -> 93 us (0.959)
  waiting for transfers between devices: 41.8 us -> 30.9 us
  starting transfers between devices: 24.6 us -> 31.4 us
    ppermute x18, waiting for transfers between devices: 35.4 us -> 26.6 us  [swap(): return lax.ppermute(block, axis, pairs)]
    ppermute x18, starting transfers between devices: 16.8 us -> 21.5 us  [swap(): return lax.ppermute(block, axis, pairs)]
    ppermute x2, waiting for transfers between devices: 3.09 us -> 0.93 us  [swap_both(): return lax.ppermute(block, ('gx', 'gy'), pairs)]
    ppermute x2, starting transfers between devices: 0.36 us -> 2.49 us  [swap_both(): return lax.ppermute(block, ('gx', 'gy'), pairs)]
  transfers between devices with their start and end apart: 21 -> 21, of which waited for: 16 -> 13; matrix products, arithmetic and copies ran while one was open for 3% -> 3% of each run, Pallas kernels for 8% -> 17%
where the time goes in v23:
time: 93 us; the launch traced here: 92.7 us
  starting transfers between devices  31.4 us (34%)
  waiting for transfers between devices  30.9 us (33%)
  Pallas kernels  25.5 us (27%)
  other arithmetic  3.48 us (4%)
  between operations  0.97 us (1%)
    ppermute x18, waiting for transfers between devices, swap(): return lax.ppermute(block, axis, pairs)  26.6 us
    ppermute x18, starting transfers between devices, swap(): return lax.ppermute(block, axis, pairs)  21.5 us
    pallas_call x1, Pallas kernels, backward(): pl.pallas_call(functools.partial(backward_kernel, *places), out_shape=out...  9.44 us
    pallas_call x1, Pallas kernels, forward(): pl.pallas_call(forward_kernel, out_shape=outs, in_specs=[spec(pltpu.VMEM)...  8.78 us
    all_to_all x1, starting transfers between devices, exchange(): lax.all_to_all(block, ('gx', 'gy'), split_axis=0, concat_axis=0, axis_ind...  7.44 us
    all_to_all x1, waiting for transfers between devices, exchange(): lax.all_to_all(block, ('gx', 'gy'), split_axis=0, concat_axis=0, axis_ind...  3.4 us
    pallas_call x1, Pallas kernels, keep_blocks(): pl.pallas_call(functools.partial(keep_kernel, *places), out_shape=[block]...  3.17 us
    ppermute x2, starting transfers between devices, swap_both(): return lax.ppermute(block, ('gx', 'gy'), pairs)  2.49 us
  transfers between devices with their start and end apart: 21, of which 13 were waited for; matrix products, arithmetic and copies ran while one was open for 3% of the time, Pallas kernels for 17%

profile of v23, /device:TPU:0, one launch (start us, length us, event | category | flops | bytes accessed | tf_op | source)
XLA Modules:
  0.0 92.7 jit_solution(7570870722086396858)
XLA Ops:
  0.6 7.4 %all-to-all-start = ((bf16[16,32,384]{2,1,0:T(8,128)(2,1)}), bf16[16,32,384]{2,1,0:T(8,128)(2,1)S(1)}, u32[]{:S(2)}, u32[]{:S(2)}) async-start(bf16[16,32,384]{2,1,0:T(8,128)(2,1)} %bitcast.93), calls=%async_computation | async-start | bytes 786432 | tf_op jit(solution)/shard_map/all_to_all | solution.py:40
  8.7 1.1 %collective-permute-done = bf16[2,2,2,1,32,384]{5,4,2,1,0,3:T(8,128)(2,1)S(1)} collective-permute-done((bf16[2,2,2,1,32,384]{5,4,2,1,0,3:T(8,128)(2,1)S(1)}, bf16[2,2,2,1,32,384]{5,4,2,1,0,3:T(8,128)(2,1)S(1)}, u32[]{:S(2)}, u32[]{:S(2)}) %collective-permute-start) | collective-permute-done | bytes 196640 | tf_op jit(solution)/shard_map/ppermute | solution.py:284
  10.0 1.9 %collective-permute-start.1 = (bf16[2,2,32,384]{3,2,1,0:T(8,128)(2,1)S(1)}, bf16[2,2,32,384]{3,2,1,0:T(8,128)(2,1)S(1)}, u32[]{:S(2)}, u32[]{:S(2)}) collective-permute-start(bf16[2,2,32,384]{3,2,1,0:T(8,128)(2,1)S(1)} %bitcast.99), channel_id=1, source_target_pairs={{0,2},{1,3},{2,0},{3,1},{4,6},{5,7},{6,4},{7,5},{8,10},{9,11},{10,... | collective-permute-start | bytes 294920 | tf_op jit(solution)/shard_map/ppermute | solution.py:284
  11.8 1.5 %collective-permute-start.2 = (bf16[2,2,32,384]{3,2,1,0:T(8,128)(2,1)S(1)}, bf16[2,2,32,384]{3,2,1,0:T(8,128)(2,1)S(1)}, u32[]{:S(2)}, u32[]{:S(2)}) collective-permute-start(bf16[2,2,32,384]{3,2,1,0:T(8,128)(2,1)S(1)} %bitcast.98), channel_id=1, source_target_pairs={{0,4},{4,0},{8,12},{12,8},{16,20},{20,16},{24,28},{28,24},{1,5},{5... | collective-permute-start | bytes 294920 | tf_op jit(solution)/shard_map/ppermute | solution.py:284
  13.5 2.2 %shard_map.67.up_ref = bf16[768,1536]{1,0:T(8,128)(2,1)S(1)} custom-call(s32[2]{0:T(128)S(1)} %pad_add_fusion.place_ref, bf16[768,1536]{1,0:T(8,128)(2,1)} %source.1), custom_call_target="tpu_custom_call" | custom-call | bytes 4718592 | tf_op jit(solution)/shard_map/pallas_call | solution.py:209
  15.7 0.9 collective-permute-done.1
  16.6 1.3 %collective-permute-done.2 = bf16[2,2,32,384]{3,2,1,0:T(8,128)(2,1)S(1)} collective-permute-done((bf16[2,2,32,384]{3,2,1,0:T(8,128)(2,1)S(1)}, bf16[2,2,32,384]{3,2,1,0:T(8,128)(2,1)S(1)}, u32[]{:S(2)}, u32[]{:S(2)}) %collective-permute-start.2) | collective-permute-done | bytes 98336 | tf_op jit(solution)/shard_map/ppermute | solution.py:284
  17.9 0.9 collective-permute-done.3
  18.9 3.4 %all-to-all-done.state_ref = bf16[16,32,384]{2,1,0:T(8,128)(2,1)S(1)} async-done(((bf16[16,32,384]{2,1,0:T(8,128)(2,1)}), bf16[16,32,384]{2,1,0:T(8,128)(2,1)S(1)}, u32[]{:S(2)}, u32[]{:S(2)}) %all-to-all-start) | async-done | bytes 393248 | tf_op jit(solution)/shard_map/all_to_all | solution.py:40
  22.3 0.8 collective-permute-start.7
  23.1 8.8 %shard_map.68 = (bf16[16,32,384]{2,1,0:T(8,128)(2,1)S(1)}, bf16[1024,1536]{1,0:T(8,128)(2,1)S(1)}, bf16[1024,1536]{1,0:T(8,128)(2,1)S(1)}, bf16[1024,768]{1,0:T(...) custom-call(bf16[16,32,384]{2,1,0:T(8,128)(2,1)S(1)} %all-to-all-don, ...), custom_call_target="tpu_custom_call" | custom-call | flops 12079595520 | bytes 25165824 | tf_op jit(solution)/shard_map/pallas_call | solution.py:235
  33.2 2.3 %collective-permute-start.6 = (bf16[2,2,1,32,384]{4,3,2,1,0:T(8,128)(2,1)S(1)}, bf16[2,2,1,32,384]{4,3,2,1,0:T(8,128)(2,1)S(1)}, u32[]{:S(2)}, u32[]{:S(2)}) collective-permute-start(bf16[2,2,1,32,384]{4,3,2,1,0:T(8,128)(2,1)S(1)} %get-tuple-element.56), channel_id=1, source_target_pairs={{0,6},{1,7},{2,4},{3,5},{4,2},{5,3},{6,0},{7,1},{8,14},{9,15},{10,... | collective-permute-start | bytes 294920 | tf_op jit(solution)/shard_map/ppermute | solution.py:373
  35.5 2.1 %collective-permute-done.4 = bf16[2,2,1,32,384]{4,3,2,1,0:T(8,128)(2,1)S(1)} collective-permute-done((bf16[2,2,1,32,384]{4,3,2,1,0:T(8,128)(2,1)S(1)}, bf16[2,2,1,32,384]{4,3,2,1,0:T(8,128)(2,1)S(1)}, u32[]{:S(2)}, u32[]{:S(2)}) %collective-permute-start.4) | collective-permute-done | bytes 98336 | tf_op jit(solution)/shard_map/ppermute | solution.py:284
  37.7 1.4 %collective-permute-done.5 = bf16[2,2,1,32,384]{4,3,2,1,0:T(8,128)(2,1)S(1)} collective-permute-done((bf16[2,2,1,32,384]{4,3,2,1,0:T(8,128)(2,1)S(1)}, bf16[2,2,1,32,384]{4,3,2,1,0:T(8,128)(2,1)S(1)}, u32[]{:S(2)}, u32[]{:S(2)}) %collective-permute-start.5) | collective-permute-done | bytes 98336 | tf_op jit(solution)/shard_map/ppermute | solution.py:284
  39.2 9.4 %shard_map.69 = (bf16[1024,1536]{1,0:T(8,128)(2,1)S(1)}, bf16[768,1024]{1,0:T(8,128)(2,1)S(1)}, bf16[16,96,384]{2,1,0:T(8,128)(2,1)S(1)}, bf16[16,96,384]{2,1,0:T(8,128)(2,1)S(1)}) custom-call(s32[2]{0:T(128)S(1)} %pad_add_fusion.place_ref, bf16[16,32,384]{2,1,0:T(8,128)(2,1)S(1)} %pad_maximum_fusion.1.grad_ref, ...), custom_call_target="tpu_custom_call" | custom-call | flops 12079595520 | bytes 25165824 | tf_op jit(solution)/shard_map/pallas_call | solution.py:254
  49.3 3.2 %shard_map.70 = (bf16[16,96,384]{2,1,0:T(8,128)(2,1)S(1)}, bf16[16,96,384]{2,1,0:T(8,128)(2,1)S(1)}) custom-call(s32[2]{0:T(128)S(1)} %pad_add_fusion.place_ref, bf16[1024,1536]{1,0:T(8,128)(2,1)S(1)} %get-tuple-element.59.hidden_ref, bf16[1024,1536]{1,0:T(8,128)(2,1)S(1)} %get-tuple-element.68.d_pre_ref, ...), custom_call_target="tpu_custom_call" | custom-call | flops 2415919104 | bytes 12582912 | tf_op jit(solution)/shard_map/pallas_call | solution.py:270
  52.8 1.2 %collective-permute-start.10 = (bf16[8,96,384]{2,1,0:T(8,128)(2,1)S(1)}, bf16[8,96,384]{2,1,0:T(8,128)(2,1)S(1)}, u32[]{:S(2)}, u32[]{:S(2)}) collective-permute-start(bf16[8,96,384]{2,1,0:T(8,128)(2,1)S(1)} %get-tuple-element.84), channel_id=1, source_target_pairs={{0,4},{4,0},{8,12},{12,8},{16,20},{20,16},{24,28},{28,24},{1,5},{5... | collective-permute-start | bytes 1769480 | tf_op jit(solution)/shard_map/ppermute | solution.py:284
  54.3 1.4 %collective-permute-start.14 = (bf16[8,96,384]{2,1,0:T(8,128)(2,1)S(1)}, bf16[8,96,384]{2,1,0:T(8,128)(2,1)S(1)}, u32[]{:S(2)}, u32[]{:S(2)}) collective-permute-start(bf16[8,96,384]{2,1,0:T(8,128)(2,1)S(1)} %get-tuple-element.82), channel_id=1, source_target_pairs={{0,2},{1,3},{2,0},{3,1},{4,6},{5,7},{6,4},{7,5},{8,10},{9,11},{10,... | collective-permute-start | bytes 1769480 | tf_op jit(solution)/shard_map/ppermute | solution.py:284
  55.7 2.2 %collective-permute-start.8 = (bf16[2,4,32,384]{3,2,1,0:T(8,128)(2,1)S(1)}, bf16[2,4,32,384]{3,2,1,0:T(8,128)(2,1)S(1)}, u32[]{:S(2)}, u32[]{:S(2)}) collective-permute-start(bf16[2,4,32,384]{3,2,1,0:T(8,128)(2,1)S(1)} %get-tuple-element.67), channel_id=1, source_target_pairs={{0,16},{4,20},{8,24},{12,28},{16,0},{20,4},{24,8},{28,12},{1,17},{... | collective-permute-start | bytes 589832 | tf_op jit(solution)/shard_map/ppermute | solution.py:284
  57.9 9.3 %collective-permute-done.8 = bf16[2,4,32,384]{3,2,1,0:T(8,128)(2,1)S(1)} collective-permute-done((bf16[2,4,32,384]{3,2,1,0:T(8,128)(2,1)S(1)}, bf16[2,4,32,384]{3,2,1,0:T(8,128)(2,1)S(1)}, u32[]{:S(2)}, u32[]{:S(2)}) %collective-permute-start.8) | collective-permute-done | bytes 196640 | tf_op jit(solution)/shard_map/ppermute | solution.py:284
  67.2 0.7 fusion.5
  68.3 1.4 %collective-permute-start.12 = (bf16[4,96,384]{2,1,0:T(8,128)(2,1)S(1)}, bf16[4,96,384]{2,1,0:T(8,128)(2,1)S(1)}, u32[]{:S(2)}, u32[]{:S(2)}) collective-permute-start(bf16[4,96,384]{2,1,0:T(8,128)(2,1)S(1)} %get-tuple-element.73), channel_id=1, source_target_pairs={{0,2},{1,3},{2,0},{3,1},{4,6},{5,7},{6,4},{7,5},{8,10},{9,11},{10,... | collective-permute-start | bytes 884744 | tf_op jit(solution)/shard_map/ppermute | solution.py:284
  69.9 1.2 %collective-permute-start.15 = (bf16[4,96,384]{2,1,0:T(8,128)(2,1)S(1)}, bf16[4,96,384]{2,1,0:T(8,128)(2,1)S(1)}, u32[]{:S(2)}, u32[]{:S(2)}) collective-permute-start(bf16[4,96,384]{2,1,0:T(8,128)(2,1)S(1)} %get-tuple-element.86), channel_id=1, source_target_pairs={{0,4},{4,0},{8,12},{12,8},{16,20},{20,16},{24,28},{28,24},{1,5},{5... | collective-permute-start | bytes 884744 | tf_op jit(solution)/shard_map/ppermute | solution.py:284
  71.1 5.4 %collective-permute-done.12 = bf16[4,96,384]{2,1,0:T(8,128)(2,1)S(1)} collective-permute-done((bf16[4,96,384]{2,1,0:T(8,128)(2,1)S(1)}, bf16[4,96,384]{2,1,0:T(8,128)(2,1)S(1)}, u32[]{:S(2)}, u32[]{:S(2)}) %collective-permute-start.12) | collective-permute-done | bytes 294944 | tf_op jit(solution)/shard_map/ppermute | solution.py:284
  76.6 2.0 %collective-permute-start.18 = (bf16[2,96,384]{2,1,0:T(8,128)(2,1)S(1)}, bf16[2,96,384]{2,1,0:T(8,128)(2,1)S(1)}, u32[]{:S(2)}, u32[]{:S(2)}) collective-permute-start(bf16[2,96,384]{2,1,0:T(8,128)(2,1)S(1)} %get-tuple-element.80), channel_id=1, source_target_pairs={{0,16},{4,20},{8,24},{12,28},{16,0},{20,4},{24,8},{28,12},{1,17},{... | collective-permute-start | bytes 442376 | tf_op jit(solution)/shard_map/ppermute | solution.py:284
  78.7 1.5 %collective-permute-start.16 = (bf16[2,96,384]{2,1,0:T(8,128)(2,1)S(1)}, bf16[2,96,384]{2,1,0:T(8,128)(2,1)S(1)}, u32[]{:S(2)}, u32[]{:S(2)}) collective-permute-start(bf16[2,96,384]{2,1,0:T(8,128)(2,1)S(1)} %get-tuple-element.92), channel_id=1, source_target_pairs={{0,8},{4,12},{8,0},{12,4},{16,24},{20,28},{24,16},{28,20},{1,9},{5... | collective-permute-start | bytes 442376 | tf_op jit(solution)/shard_map/ppermute | solution.py:284
  80.2 1.9 %shard_map.71 = bf16[512,384]{1,0:T(8,128)(2,1)} custom-call(s32[2]{0:T(128)} %copy-done, bf16[8,32,384]{2,1,0:T(8,128)(2,1)} %get-tuple-element.74.refs_0_, bf16[8,32,384]{2,1,0:T(8,128)(2,1)} %copy-done.2), custom_call_target="tpu_custom_call" | custom-call | bytes 786432 | tf_op jit(solution)/shard_map/pallas_call | solution.py:379
  82.1 1.8 %collective-permute-done.18 = bf16[2,96,384]{2,1,0:T(8,128)(2,1)S(1)} collective-permute-done((bf16[2,96,384]{2,1,0:T(8,128)(2,1)S(1)}, bf16[2,96,384]{2,1,0:T(8,128)(2,1)S(1)}, u32[]{:S(2)}, u32[]{:S(2)}) %collective-permute-start.18) | collective-permute-done | bytes 147488 | tf_op jit(solution)/shard_map/ppermute | solution.py:284
  83.9 1.8 %collective-permute-start.19 = (bf16[1,96,384]{2,1,0:T(8,128)(2,1)S(1)}, bf16[1,96,384]{2,1,0:T(8,128)(2,1)S(1)}, u32[]{:S(2)}, u32[]{:S(2)}) collective-permute-start(bf16[1,96,384]{2,1,0:T(8,128)(2,1)S(1)} %fusion.10), channel_id=1, source_target_pairs={{0,8},{4,12},{8,0},{12,4},{16,24},{20,28},{24,16},{28,20},{1,9},{5... | collective-permute-start | bytes 221192 | tf_op jit(solution)/shard_map/ppermute | solution.py:284
  85.9 2.5 %collective-permute-start.17 = (bf16[1,96,384]{2,1,0:T(8,128)(2,1)S(1)}, bf16[1,96,384]{2,1,0:T(8,128)(2,1)S(1)}, u32[]{:S(2)}, u32[]{:S(2)}) collective-permute-start(bf16[1,96,384]{2,1,0:T(8,128)(2,1)S(1)} %fusion.12), channel_id=1, source_target_pairs={{0,16},{4,20},{8,24},{12,28},{16,0},{20,4},{24,8},{28,12},{1,17},{... | collective-permute-start | bytes 221192 | tf_op jit(solution)/shard_map/ppermute | solution.py:284
  88.3 0.7 add_bitcast_fusion
  89.0 2.9 %collective-permute-done.17 = bf16[1,96,384]{2,1,0:T(8,128)(2,1)S(1)} collective-permute-done((bf16[1,96,384]{2,1,0:T(8,128)(2,1)S(1)}, bf16[1,96,384]{2,1,0:T(8,128)(2,1)S(1)}, u32[]{:S(2)}, u32[]{:S(2)}) %collective-permute-start.17) | collective-permute-done | bytes 73760 | tf_op jit(solution)/shard_map/ppermute | solution.py:284
  (48 shorter events, 5.2 us)
Async XLA Ops:
  0.6 7.6 %copy-start.1 = (bf16[512,384]{1,0:T(8,128)(2,1)S(1)}, bf16[512,384]{1,0:T(8,128)(2,1)}, u32[]{:S(2)}) copy-start(bf16[512,384]{1,0:T(8,128)(2,1)} %param.7) | copy-start | bytes 1179652
  0.6 21.7 %all-to-all-start = ((bf16[16,32,384]{2,1,0:T(8,128)(2,1)}), bf16[16,32,384]{2,1,0:T(8,128)(2,1)S(1)}, u32[]{:S(2)}, u32[]{:S(2)}) async-start(bf16[16,32,384]{2,1,0:T(8,128)(2,1)} %bitcast.93), calls=%async_computation | async-start | bytes 786432 | tf_op jit(solution)/shard_map/all_to_all | solution.py:40
  8.3 41.0 %copy-start = (s32[2]{0:T(128)}, s32[2]{0:T(128)S(1)}, u32[]{:S(2)}) copy-start(s32[2]{0:T(128)S(1)} %pad_add_fusion.place_ref) | copy-start | bytes 28
  8.3 1.5 %collective-permute-start = (bf16[2,2,2,1,32,384]{5,4,2,1,0,3:T(8,128)(2,1)S(1)}, bf16[2,2,2,1,32,384]{5,4,2,1,0,3:T(8,128)(2,1)S(1)}, u32[]{:S(2)}, u32[]{:S(2)}) collective-permute-start(bf16[2,2,2,1,32,384]{5,4,2,1,0,3:T(8,128)(2,1)S(1)} %get-tuple-element.107), channel_id=1, source_target_pairs={{0,1},{1,0},{2,3},{3,2},{4,5},{5,4},{6,7},{7,6},{8,9},{9,8},{10,11... | collective-permute-start | bytes 589832 | tf_op jit(solution)/shard_map/ppermute | solution.py:284
  10.0 6.7 %collective-permute-start.1 = (bf16[2,2,32,384]{3,2,1,0:T(8,128)(2,1)S(1)}, bf16[2,2,32,384]{3,2,1,0:T(8,128)(2,1)S(1)}, u32[]{:S(2)}, u32[]{:S(2)}) collective-permute-start(bf16[2,2,32,384]{3,2,1,0:T(8,128)(2,1)S(1)} %bitcast.99), channel_id=1, source_target_pairs={{0,2},{1,3},{2,0},{3,1},{4,6},{5,7},{6,4},{7,5},{8,10},{9,11},{10,... | collective-permute-start | bytes 294920 | tf_op jit(solution)/shard_map/ppermute | solution.py:284
  11.8 6.1 %collective-permute-start.2 = (bf16[2,2,32,384]{3,2,1,0:T(8,128)(2,1)S(1)}, bf16[2,2,32,384]{3,2,1,0:T(8,128)(2,1)S(1)}, u32[]{:S(2)}, u32[]{:S(2)}) collective-permute-start(bf16[2,2,32,384]{3,2,1,0:T(8,128)(2,1)S(1)} %bitcast.98), channel_id=1, source_target_pairs={{0,4},{4,0},{8,12},{12,8},{16,20},{20,16},{24,28},{28,24},{1,5},{5... | collective-permute-start | bytes 294920 | tf_op jit(solution)/shard_map/ppermute | solution.py:284
  13.3 5.5 %collective-permute-start.3 = (bf16[2,2,32,384]{3,2,1,0:T(8,128)(2,1)S(1)}, bf16[2,2,32,384]{3,2,1,0:T(8,128)(2,1)S(1)}, u32[]{:S(2)}, u32[]{:S(2)}) collective-permute-start(bf16[2,2,32,384]{3,2,1,0:T(8,128)(2,1)S(1)} %bitcast.97), channel_id=1, source_target_pairs={{0,6},{1,7},{2,4},{3,5},{4,2},{5,3},{6,0},{7,1},{8,14},{9,15},{10,... | collective-permute-start | bytes 294920 | tf_op jit(solution)/shard_map/ppermute | solution.py:373
  22.3 16.8 %collective-permute-start.7 = (bf16[8,32,384]{2,1,0:T(8,128)(2,1)S(1)}, bf16[8,32,384]{2,1,0:T(8,128)(2,1)S(1)}, u32[]{:S(2)}, u32[]{:S(2)}) collective-permute-start(bf16[8,32,384]{2,1,0:T(8,128)(2,1)S(1)} %get-tuple-element.58), channel_id=1, source_target_pairs={{0,16},{4,20},{8,24},{12,28},{16,0},{20,4},{24,8},{28,12},{1,17},{... | collective-permute-start | bytes 589832 | tf_op jit(solution)/shard_map/ppermute | solution.py:284
  32.0 5.7 %collective-permute-start.4 = (bf16[2,2,1,32,384]{4,3,2,1,0:T(8,128)(2,1)S(1)}, bf16[2,2,1,32,384]{4,3,2,1,0:T(8,128)(2,1)S(1)}, u32[]{:S(2)}, u32[]{:S(2)}) collective-permute-start(bf16[2,2,1,32,384]{4,3,2,1,0:T(8,128)(2,1)S(1)} %get-tuple-element.54), channel_id=1, source_target_pairs={{0,2},{1,3},{2,0},{3,1},{4,6},{5,7},{6,4},{7,5},{8,10},{9,11},{10,... | collective-permute-start | bytes 294920 | tf_op jit(solution)/shard_map/ppermute | solution.py:284
  32.6 6.5 %collective-permute-start.5 = (bf16[2,2,1,32,384]{4,3,2,1,0:T(8,128)(2,1)S(1)}, bf16[2,2,1,32,384]{4,3,2,1,0:T(8,128)(2,1)S(1)}, u32[]{:S(2)}, u32[]{:S(2)}) collective-permute-start(bf16[2,2,1,32,384]{4,3,2,1,0:T(8,128)(2,1)S(1)} %get-tuple-element.55), channel_id=1, source_target_pairs={{0,4},{4,0},{8,12},{12,8},{16,20},{20,16},{24,28},{28,24},{1,5},{5... | collective-permute-start | bytes 294920 | tf_op jit(solution)/shard_map/ppermute | solution.py:284
  33.2 5.9 %collective-permute-start.6 = (bf16[2,2,1,32,384]{4,3,2,1,0:T(8,128)(2,1)S(1)}, bf16[2,2,1,32,384]{4,3,2,1,0:T(8,128)(2,1)S(1)}, u32[]{:S(2)}, u32[]{:S(2)}) collective-permute-start(bf16[2,2,1,32,384]{4,3,2,1,0:T(8,128)(2,1)S(1)} %get-tuple-element.56), channel_id=1, source_target_pairs={{0,6},{1,7},{2,4},{3,5},{4,2},{5,3},{6,0},{7,1},{8,14},{9,15},{10,... | collective-permute-start | bytes 294920 | tf_op jit(solution)/shard_map/ppermute | solution.py:373
  48.7 3.8 %collective-permute-start.9 = (bf16[16,96,384]{2,1,0:T(8,128)(2,1)S(1)}, bf16[16,96,384]{2,1,0:T(8,128)(2,1)S(1)}, u32[]{:S(2)}, u32[]{:S(2)}) collective-permute-start(bf16[16,96,384]{2,1,0:T(8,128)(2,1)S(1)} %get-tuple-element.71), channel_id=1, source_target_pairs={{0,1},{1,0},{2,3},{3,2},{4,5},{5,4},{6,7},{7,6},{8,9},{9,8},{10,11... | collective-permute-start | bytes 3538952 | tf_op jit(solution)/shard_map/ppermute | solution.py:284
  48.8 5.2 %collective-permute-start.13 = (bf16[16,96,384]{2,1,0:T(8,128)(2,1)S(1)}, bf16[16,96,384]{2,1,0:T(8,128)(2,1)S(1)}, u32[]{:S(2)}, u32[]{:S(2)}) collective-permute-start(bf16[16,96,384]{2,1,0:T(8,128)(2,1)S(1)} %get-tuple-element.77), channel_id=1, source_target_pairs={{0,1},{1,0},{2,3},{3,2},{4,5},{5,4},{6,7},{7,6},{8,9},{9,8},{10,11... | collective-permute-start | bytes 3538952 | tf_op jit(solution)/shard_map/ppermute | solution.py:284
  52.8 15.4 %collective-permute-start.10 = (bf16[8,96,384]{2,1,0:T(8,128)(2,1)S(1)}, bf16[8,96,384]{2,1,0:T(8,128)(2,1)S(1)}, u32[]{:S(2)}, u32[]{:S(2)}) collective-permute-start(bf16[8,96,384]{2,1,0:T(8,128)(2,1)S(1)} %get-tuple-element.84), channel_id=1, source_target_pairs={{0,4},{4,0},{8,12},{12,8},{16,20},{20,16},{24,28},{28,24},{1,5},{5... | collective-permute-start | bytes 1769480 | tf_op jit(solution)/shard_map/ppermute | solution.py:284
  54.3 15.5 %collective-permute-start.14 = (bf16[8,96,384]{2,1,0:T(8,128)(2,1)S(1)}, bf16[8,96,384]{2,1,0:T(8,128)(2,1)S(1)}, u32[]{:S(2)}, u32[]{:S(2)}) collective-permute-start(bf16[8,96,384]{2,1,0:T(8,128)(2,1)S(1)} %get-tuple-element.82), channel_id=1, source_target_pairs={{0,2},{1,3},{2,0},{3,1},{4,6},{5,7},{6,4},{7,5},{8,10},{9,11},{10,... | collective-permute-start | bytes 1769480 | tf_op jit(solution)/shard_map/ppermute | solution.py:284
  55.7 11.4 %collective-permute-start.8 = (bf16[2,4,32,384]{3,2,1,0:T(8,128)(2,1)S(1)}, bf16[2,4,32,384]{3,2,1,0:T(8,128)(2,1)S(1)}, u32[]{:S(2)}, u32[]{:S(2)}) collective-permute-start(bf16[2,4,32,384]{3,2,1,0:T(8,128)(2,1)S(1)} %get-tuple-element.67), channel_id=1, source_target_pairs={{0,16},{4,20},{8,24},{12,28},{16,0},{20,4},{24,8},{28,12},{1,17},{... | collective-permute-start | bytes 589832 | tf_op jit(solution)/shard_map/ppermute | solution.py:284
  68.3 8.2 %collective-permute-start.12 = (bf16[4,96,384]{2,1,0:T(8,128)(2,1)S(1)}, bf16[4,96,384]{2,1,0:T(8,128)(2,1)S(1)}, u32[]{:S(2)}, u32[]{:S(2)}) collective-permute-start(bf16[4,96,384]{2,1,0:T(8,128)(2,1)S(1)} %get-tuple-element.73), channel_id=1, source_target_pairs={{0,2},{1,3},{2,0},{3,1},{4,6},{5,7},{6,4},{7,5},{8,10},{9,11},{10,... | collective-permute-start | bytes 884744 | tf_op jit(solution)/shard_map/ppermute | solution.py:284
  69.9 8.7 %collective-permute-start.15 = (bf16[4,96,384]{2,1,0:T(8,128)(2,1)S(1)}, bf16[4,96,384]{2,1,0:T(8,128)(2,1)S(1)}, u32[]{:S(2)}, u32[]{:S(2)}) collective-permute-start(bf16[4,96,384]{2,1,0:T(8,128)(2,1)S(1)} %get-tuple-element.86), channel_id=1, source_target_pairs={{0,4},{4,0},{8,12},{12,8},{16,20},{20,16},{24,28},{28,24},{1,5},{5... | collective-permute-start | bytes 884744 | tf_op jit(solution)/shard_map/ppermute | solution.py:284
  71.1 5.5 %collective-permute-start.11 = (bf16[8,32,384]{2,1,0:T(8,128)(2,1)S(1)}, bf16[8,32,384]{2,1,0:T(8,128)(2,1)S(1)}, u32[]{:S(2)}, u32[]{:S(2)}) collective-permute-start(bf16[8,32,384]{2,1,0:T(8,128)(2,1)S(1)} %get-tuple-element.72), channel_id=1, source_target_pairs={{0,1},{1,0},{2,3},{3,2},{4,5},{5,4},{6,7},{7,6},{8,9},{9,8},{10,11... | collective-permute-start | bytes 589832 | tf_op jit(solution)/shard_map/ppermute | solution.py:284
  76.6 3.6 %copy-start.2 = (bf16[8,32,384]{2,1,0:T(8,128)(2,1)}, bf16[8,32,384]{2,1,0:T(8,128)(2,1)S(1)}, u32[]{:S(2)}) copy-start(bf16[8,32,384]{2,1,0:T(8,128)(2,1)S(1)} %collective-permute-done.11.refs_1_) | copy-start | bytes 589828
  76.6 7.3 %collective-permute-start.18 = (bf16[2,96,384]{2,1,0:T(8,128)(2,1)S(1)}, bf16[2,96,384]{2,1,0:T(8,128)(2,1)S(1)}, u32[]{:S(2)}, u32[]{:S(2)}) collective-permute-start(bf16[2,96,384]{2,1,0:T(8,128)(2,1)S(1)} %get-tuple-element.80), channel_id=1, source_target_pairs={{0,16},{4,20},{8,24},{12,28},{16,0},{20,4},{24,8},{28,12},{1,17},{... | collective-permute-start | bytes 442376 | tf_op jit(solution)/shard_map/ppermute | solution.py:284
  78.7 7.1 %collective-permute-start.16 = (bf16[2,96,384]{2,1,0:T(8,128)(2,1)S(1)}, bf16[2,96,384]{2,1,0:T(8,128)(2,1)S(1)}, u32[]{:S(2)}, u32[]{:S(2)}) collective-permute-start(bf16[2,96,384]{2,1,0:T(8,128)(2,1)S(1)} %get-tuple-element.92), channel_id=1, source_target_pairs={{0,8},{4,12},{8,0},{12,4},{16,24},{20,28},{24,16},{28,20},{1,9},{5... | collective-permute-start | bytes 442376 | tf_op jit(solution)/shard_map/ppermute | solution.py:284
  83.9 4.4 %collective-permute-start.19 = (bf16[1,96,384]{2,1,0:T(8,128)(2,1)S(1)}, bf16[1,96,384]{2,1,0:T(8,128)(2,1)S(1)}, u32[]{:S(2)}, u32[]{:S(2)}) collective-permute-start(bf16[1,96,384]{2,1,0:T(8,128)(2,1)S(1)} %fusion.10), channel_id=1, source_target_pairs={{0,8},{4,12},{8,0},{12,4},{16,24},{20,28},{24,16},{28,20},{1,9},{5... | collective-permute-start | bytes 221192 | tf_op jit(solution)/shard_map/ppermute | solution.py:284
  85.9 6.1 %collective-permute-start.17 = (bf16[1,96,384]{2,1,0:T(8,128)(2,1)S(1)}, bf16[1,96,384]{2,1,0:T(8,128)(2,1)S(1)}, u32[]{:S(2)}, u32[]{:S(2)}) collective-permute-start(bf16[1,96,384]{2,1,0:T(8,128)(2,1)S(1)} %fusion.12), channel_id=1, source_target_pairs={{0,16},{4,20},{8,24},{12,28},{16,0},{20,4},{24,8},{28,12},{1,17},{... | collective-permute-start | bytes 221192 | tf_op jit(solution)/shard_map/ppermute | solution.py:284

commit v24 on v18

--- a/solution.py
+++ b/solution.py
@@ -162,11 +162,8 @@
         write_blocks(places_up, place_ref[1], normed_t_ref, d_pre_ref, blocks[1])
 
 
-def keep_kernel(
-    places_down, places_up, place_ref, hidden_ref, d_pre_ref, normed_t_ref, grad_t_ref, down_ref, up_ref
-):
-    write_blocks(places_down, 1 - place_ref[1], grad_t_ref, hidden_ref, down_ref)
-    write_blocks(places_up, 1 - place_ref[1], normed_t_ref, d_pre_ref, up_ref)
+def keep_kernel(places, place_ref, left_ref, right_ref, out_ref):
+    write_blocks(places, 1 - place_ref[1], left_ref, right_ref, out_ref)
 
 
 def settle_kernel(sources, place_ref, *refs):
@@ -264,19 +261,18 @@
     )(place, grad, *in_vmem(*kept))
 
 
-def keep_blocks(place, hidden, d_pre, normed_t, grad_t, places, block):
-    total, units = hidden.shape
-    depth = normed_t.shape[0]
+def keep_blocks(place, left, right, places, block):
+    total, units = right.shape
     return pl.pallas_call(
-        functools.partial(keep_kernel, *places),
-        out_shape=[block] * 2,
-        in_specs=[spec(pltpu.SMEM)] + [spec(pltpu.VMEM)] * 4,
-        out_specs=[spec(pltpu.VMEM)] * 2,
+        functools.partial(keep_kernel, places),
+        out_shape=block,
+        in_specs=[spec(pltpu.SMEM)] + [spec(pltpu.VMEM)] * 2,
+        out_specs=spec(pltpu.VMEM),
         compiler_params=pltpu.CompilerParams(vmem_limit_bytes=KEEP_BYTES),
         cost_estimate=pl.CostEstimate(
-            flops=2 * total * depth * units, bytes_accessed=8 * total * units, transcendentals=0
+            flops=total * left.shape[0] * units, bytes_accessed=4 * total * units, transcendentals=0
         ),
-    )(place, *in_vmem(hidden, d_pre, normed_t, grad_t))
+    )(place, *in_vmem(left, right))
 
 
 def swap(block, axis, bit):
@@ -430,7 +426,8 @@
         grad_up = scatter_narrow(halves, normed_t, d_pre, [steps[core]] + order_up, span_x, span_y)
         return (mixed_out, grad_up, grad_down)
     take_down, take_up = [swap(part, *steps[core]) for part in given]
-    keep_down, keep_up = keep_blocks(place, hidden, d_pre, normed_t, grad_t, places, block)
+    keep_up = keep_blocks(place, normed_t, d_pre, places[1], block)
+    keep_down = keep_blocks(place, grad_t, hidden, places[0], block)
 
     def beside(phase, give):
         if phase == 1:

time: 88.4 us -> 89.3 us (1.010)
    pallas_call x1 -> x2, Pallas kernels: 3.17 us -> 3.89 us  [keep_blocks(): pl.pallas_call(functools.partial(keep_kernel, places), out_shape=block, i...]
  transfers between devices with their start and end apart: 21 -> 21, of which waited for: 13 -> 13; matrix products, arithmetic and copies ran while one was open for 3% -> 3% of each run, Pallas kernels for 18% -> 19%
where the time goes in v24:
time: 89.3 us; the launch traced here: 89 us
  waiting for transfers between devices  34.8 us (39%)
  Pallas kernels  26.2 us (29%)
  starting transfers between devices  22.7 us (25%)
  other arithmetic  3.52 us (4%)
  between operations  1.01 us (1%)
    ppermute x18, waiting for transfers between devices, swap(): return lax.ppermute(block, axis, pairs)  30.5 us
    ppermute x18, starting transfers between devices, swap(): return lax.ppermute(block, axis, pairs)  11.1 us
    pallas_call x1, Pallas kernels, backward(): pl.pallas_call(functools.partial(backward_kernel, *places), out_shape=out...  9.45 us
    pallas_call x1, Pallas kernels, forward(): pl.pallas_call(forward_kernel, out_shape=outs, in_specs=[spec(pltpu.VMEM)...  8.77 us
    all_to_all x1, starting transfers between devices, exchange(): lax.all_to_all(block, ('gx', 'gy'), split_axis=0, concat_axis=0, axis_ind...  7.44 us
    ppermute x2, starting transfers between devices, swap_both(): return lax.ppermute(block, ('gx', 'gy'), pairs)  4.21 us
    pallas_call x2, Pallas kernels, keep_blocks(): pl.pallas_call(functools.partial(keep_kernel, places), out_shape=block, i...  3.89 us
    all_to_all x1, waiting for transfers between devices, exchange(): lax.all_to_all(block, ('gx', 'gy'), split_axis=0, concat_axis=0, axis_ind...  3.45 us
  transfers between devices with their start and end apart: 21, of which 13 were waited for; matrix products, arithmetic and copies ran while one was open for 3% of the time, Pallas kernels for 19%

profile of v24, /device:TPU:0, one launch (start us, length us, event | category | flops | bytes accessed | tf_op | source)
XLA Modules:
  0.0 89.0 jit_solution(4726615920072333852)
XLA Ops:
  0.6 7.4 %all-to-all-start = ((bf16[16,32,384]{2,1,0:T(8,128)(2,1)}), bf16[16,32,384]{2,1,0:T(8,128)(2,1)S(1)}, u32[]{:S(2)}, u32[]{:S(2)}) async-start(bf16[16,32,384]{2,1,0:T(8,128)(2,1)} %bitcast.98), calls=%async_computation | async-start | bytes 786432 | tf_op jit(solution)/shard_map/all_to_all | solution.py:40
  8.7 1.1 %collective-permute-done = bf16[2,2,2,1,32,384]{5,4,2,1,0,3:T(8,128)(2,1)S(1)} collective-permute-done((bf16[2,2,2,1,32,384]{5,4,2,1,0,3:T(8,128)(2,1)S(1)}, bf16[2,2,2,1,32,384]{5,4,2,1,0,3:T(8,128)(2,1)S(1)}, u32[]{:S(2)}, u32[]{:S(2)}) %collective-permute-start) | collective-permute-done | bytes 196640 | tf_op jit(solution)/shard_map/ppermute | solution.py:280
  9.9 2.8 %collective-permute-start.3 = (bf16[2,2,32,384]{3,2,1,0:T(8,128)(2,1)S(1)}, bf16[2,2,32,384]{3,2,1,0:T(8,128)(2,1)S(1)}, u32[]{:S(2)}, u32[]{:S(2)}) collective-permute-start(bf16[2,2,32,384]{3,2,1,0:T(8,128)(2,1)S(1)} %bitcast.103), channel_id=1, source_target_pairs={{0,6},{1,7},{2,4},{3,5},{4,2},{5,3},{6,0},{7,1},{8,14},{9,15},{10,... | collective-permute-start | bytes 294920 | tf_op jit(solution)/shard_map/ppermute | solution.py:369
  12.7 0.6 collective-permute-start.2
  13.6 2.2 %shard_map.67.up_ref = bf16[768,1536]{1,0:T(8,128)(2,1)S(1)} custom-call(s32[2]{0:T(128)S(1)} %pad_add_fusion.place_ref, bf16[768,1536]{1,0:T(8,128)(2,1)} %source.1), custom_call_target="tpu_custom_call" | custom-call | bytes 4718592 | tf_op jit(solution)/shard_map/pallas_call | solution.py:206
  15.9 0.9 collective-permute-done.3
  16.7 2.0 %collective-permute-done.2 = bf16[2,2,32,384]{3,2,1,0:T(8,128)(2,1)S(1)} collective-permute-done((bf16[2,2,32,384]{3,2,1,0:T(8,128)(2,1)S(1)}, bf16[2,2,32,384]{3,2,1,0:T(8,128)(2,1)S(1)}, u32[]{:S(2)}, u32[]{:S(2)}) %collective-permute-start.2) | collective-permute-done | bytes 98336 | tf_op jit(solution)/shard_map/ppermute | solution.py:280
  18.9 3.5 %all-to-all-done.state_ref = bf16[16,32,384]{2,1,0:T(8,128)(2,1)S(1)} async-done(((bf16[16,32,384]{2,1,0:T(8,128)(2,1)}), bf16[16,32,384]{2,1,0:T(8,128)(2,1)S(1)}, u32[]{:S(2)}, u32[]{:S(2)}) %all-to-all-start) | async-done | bytes 393248 | tf_op jit(solution)/shard_map/all_to_all | solution.py:40
  22.6 8.8 %shard_map.68 = (bf16[16,32,384]{2,1,0:T(8,128)(2,1)S(1)}, bf16[1024,1536]{1,0:T(8,128)(2,1)S(1)}, bf16[1024,1536]{1,0:T(8,128)(2,1)S(1)}, bf16[1024,768]{1,0:T(...) custom-call(bf16[16,32,384]{2,1,0:T(8,128)(2,1)S(1)} %all-to-all-don, ...), custom_call_target="tpu_custom_call" | custom-call | flops 12079595520 | bytes 25165824 | tf_op jit(solution)/shard_map/pallas_call | solution.py:232
  31.4 1.9 %collective-permute-done.4 = bf16[8,32,384]{2,1,0:T(8,128)(2,1)S(1)} collective-permute-done((bf16[8,32,384]{2,1,0:T(8,128)(2,1)S(1)}, bf16[8,32,384]{2,1,0:T(8,128)(2,1)S(1)}, u32[]{:S(2)}, u32[]{:S(2)}) %collective-permute-start.4) | collective-permute-done | bytes 196640 | tf_op jit(solution)/shard_map/ppermute | solution.py:280
  33.4 9.4 %shard_map.69 = (bf16[1024,1536]{1,0:T(8,128)(2,1)S(1)}, bf16[768,1024]{1,0:T(8,128)(2,1)S(1)}, bf16[16,96,384]{2,1,0:T(8,128)(2,1)S(1)}, bf16[16,96,384]{2,1,0:T(8,128)(2,1)S(1)}) custom-call(s32[2]{0:T(128)S(1)} %pad_add_fusion.place_ref, bf16[16,32,384]{2,1,0:T(8,128)(2,1)S(1)} %pad_maximum_fusion.1.grad_ref, ...), custom_call_target="tpu_custom_call" | custom-call | flops 12079595520 | bytes 25165824 | tf_op jit(solution)/shard_map/pallas_call | solution.py:251
  43.4 1.9 %shard_map.70 = bf16[16,96,384]{2,1,0:T(8,128)(2,1)S(1)} custom-call(s32[2]{0:T(128)S(1)} %pad_add_fusion.place_ref, bf16[768,1024]{1,0:T(8,128)(2,1)S(1)} %get-tuple-element.63.left_ref, bf16[1024,1536]{1,0:T(8,128)(2,1)S(1)} %get-tuple-element.56.hidden_ref.right_ref), custom_call_target="tpu_custom_call" | custom-call | flops 1207959552 | bytes 6291456 | tf_op jit(solution)/shard_map/pallas_call | solution.py:266
  45.4 1.9 %shard_map.72 = bf16[16,96,384]{2,1,0:T(8,128)(2,1)S(1)} custom-call(s32[2]{0:T(128)S(1)} %pad_add_fusion.place_ref, bf16[768,1024]{1,0:T(8,128)(2,1)S(1)} %get-tuple-element.59.normed_t_ref.left_ref, bf16[1024,1536]{1,0:T(8,128)(2,1)S(1)} %get-tuple-element.77.right_ref), custom_call_target="tpu_custom_call" | custom-call | flops 1207959552 | bytes 6291456 | tf_op jit(solution)/shard_map/pallas_call | solution.py:266
  47.7 1.1 %collective-permute-start.7 = (bf16[8,96,384]{2,1,0:T(8,128)(2,1)S(1)}, bf16[8,96,384]{2,1,0:T(8,128)(2,1)S(1)}, u32[]{:S(2)}, u32[]{:S(2)}) collective-permute-start(bf16[8,96,384]{2,1,0:T(8,128)(2,1)S(1)} %get-tuple-element.84), channel_id=1, source_target_pairs={{0,4},{4,0},{8,12},{12,8},{16,20},{20,16},{24,28},{28,24},{1,5},{5... | collective-permute-start | bytes 1769480 | tf_op jit(solution)/shard_map/ppermute | solution.py:280
  49.1 1.2 %collective-permute-start.15 = (bf16[8,96,384]{2,1,0:T(8,128)(2,1)S(1)}, bf16[8,96,384]{2,1,0:T(8,128)(2,1)S(1)}, u32[]{:S(2)}, u32[]{:S(2)}) collective-permute-start(bf16[8,96,384]{2,1,0:T(8,128)(2,1)S(1)} %get-tuple-element.82), channel_id=1, source_target_pairs={{0,2},{1,3},{2,0},{3,1},{4,6},{5,7},{6,4},{7,5},{8,10},{9,11},{10,... | collective-permute-start | bytes 1769480 | tf_op jit(solution)/shard_map/ppermute | solution.py:280
  50.3 11.1 %collective-permute-done.5 = bf16[2,2,2,1,32,384]{5,4,2,1,0,3:T(8,128)(2,1)S(1)} collective-permute-done((bf16[2,2,2,1,32,384]{5,4,2,1,0,3:T(8,128)(2,1)S(1)}, bf16[2,2,2,1,32,384]{5,4,2,1,0,3:T(8,128)(2,1)S(1)}, u32[]{:S(2)}, u32[]{:S(2)}) %collective-permute-start.5) | collective-permute-done | bytes 196640 | tf_op jit(solution)/shard_map/ppermute | solution.py:280
  61.4 1.6 %collective-permute-done.7 = bf16[8,96,384]{2,1,0:T(8,128)(2,1)S(1)} collective-permute-done((bf16[8,96,384]{2,1,0:T(8,128)(2,1)S(1)}, bf16[8,96,384]{2,1,0:T(8,128)(2,1)S(1)}, u32[]{:S(2)}, u32[]{:S(2)}) %collective-permute-start.7) | collective-permute-done | bytes 589856 | tf_op jit(solution)/shard_map/ppermute | solution.py:280
  63.3 0.9 %collective-permute-done.15 = bf16[8,96,384]{2,1,0:T(8,128)(2,1)S(1)} collective-permute-done((bf16[8,96,384]{2,1,0:T(8,128)(2,1)S(1)}, bf16[8,96,384]{2,1,0:T(8,128)(2,1)S(1)}, u32[]{:S(2)}, u32[]{:S(2)}) %collective-permute-start.15) | collective-permute-done | bytes 589856 | tf_op jit(solution)/shard_map/ppermute | solution.py:280
  64.4 1.1 %collective-permute-start.16 = (bf16[4,96,384]{2,1,0:T(8,128)(2,1)S(1)}, bf16[4,96,384]{2,1,0:T(8,128)(2,1)S(1)}, u32[]{:S(2)}, u32[]{:S(2)}) collective-permute-start(bf16[4,96,384]{2,1,0:T(8,128)(2,1)S(1)} %get-tuple-element.86), channel_id=1, source_target_pairs={{0,4},{4,0},{8,12},{12,8},{16,20},{20,16},{24,28},{28,24},{1,5},{5... | collective-permute-start | bytes 884744 | tf_op jit(solution)/shard_map/ppermute | solution.py:280
  65.4 0.7 collective-permute-start.9
  66.2 0.7 fusion.13
  66.9 6.0 %collective-permute-done.16 = bf16[4,96,384]{2,1,0:T(8,128)(2,1)S(1)} collective-permute-done((bf16[4,96,384]{2,1,0:T(8,128)(2,1)S(1)}, bf16[4,96,384]{2,1,0:T(8,128)(2,1)S(1)}, u32[]{:S(2)}, u32[]{:S(2)}) %collective-permute-start.16) | collective-permute-done | bytes 294944 | tf_op jit(solution)/shard_map/ppermute | solution.py:280
  73.8 1.8 %collective-permute-start.13 = (bf16[2,96,384]{2,1,0:T(8,128)(2,1)S(1)}, bf16[2,96,384]{2,1,0:T(8,128)(2,1)S(1)}, u32[]{:S(2)}, u32[]{:S(2)}) collective-permute-start(bf16[2,96,384]{2,1,0:T(8,128)(2,1)S(1)} %get-tuple-element.72), channel_id=1, source_target_pairs={{0,16},{4,20},{8,24},{12,28},{16,0},{20,4},{24,8},{28,12},{1,17},{... | collective-permute-start | bytes 442376 | tf_op jit(solution)/shard_map/ppermute | solution.py:280
  75.5 1.5 %collective-permute-start.10 = (bf16[4,32,384]{2,1,0:T(8,128)(2,1)S(1)}, bf16[4,32,384]{2,1,0:T(8,128)(2,1)S(1)}, u32[]{:S(2)}, u32[]{:S(2)}) collective-permute-start(bf16[4,32,384]{2,1,0:T(8,128)(2,1)S(1)} %get-tuple-element.68), channel_id=1, source_target_pairs={{0,2},{1,3},{2,0},{3,1},{4,6},{5,7},{6,4},{7,5},{8,10},{9,11},{10,... | collective-permute-start | bytes 294920 | tf_op jit(solution)/shard_map/ppermute | solution.py:280
  77.6 1.4 %collective-permute-start.12 = (bf16[4,32,384]{2,1,0:T(8,128)(2,1)S(1)}, bf16[4,32,384]{2,1,0:T(8,128)(2,1)S(1)}, u32[]{:S(2)}, u32[]{:S(2)}) collective-permute-start(bf16[4,32,384]{2,1,0:T(8,128)(2,1)S(1)} %get-tuple-element.70), channel_id=1, source_target_pairs={{0,6},{1,7},{2,4},{3,5},{4,2},{5,3},{6,0},{7,1},{8,14},{9,15},{10,... | collective-permute-start | bytes 294920 | tf_op jit(solution)/shard_map/ppermute | solution.py:369
  79.0 0.9 %collective-permute-done.17 = bf16[2,96,384]{2,1,0:T(8,128)(2,1)S(1)} collective-permute-done((bf16[2,96,384]{2,1,0:T(8,128)(2,1)S(1)}, bf16[2,96,384]{2,1,0:T(8,128)(2,1)S(1)}, u32[]{:S(2)}, u32[]{:S(2)}) %collective-permute-start.17) | collective-permute-done | bytes 147488 | tf_op jit(solution)/shard_map/ppermute | solution.py:280
  79.9 0.8 collective-permute-start.18
  80.7 3.1 %collective-permute-done.13 = bf16[2,96,384]{2,1,0:T(8,128)(2,1)S(1)} collective-permute-done((bf16[2,96,384]{2,1,0:T(8,128)(2,1)S(1)}, bf16[2,96,384]{2,1,0:T(8,128)(2,1)S(1)}, u32[]{:S(2)}, u32[]{:S(2)}) %collective-permute-start.13) | collective-permute-done | bytes 147488 | tf_op jit(solution)/shard_map/ppermute | solution.py:280
  84.5 1.9 %shard_map.71 = bf16[512,384]{1,0:T(8,128)(2,1)} custom-call(s32[2]{0:T(128)} %copy-done, bf16[4,32,384]{2,1,0:T(8,128)(2,1)} %get-tuple-element.73.refs_0_, bf16[4,32,384]{2,1,0:T(8,128)(2,1)} %copy-done.2, bf16[4,32,384]{2,1,0:T(8,128)(2,1)} %copy-done.3, bf16[4,32,384]{2,1,0:T(8,128)(2,1)} %copy-done.4), custom_call_target="tpu_custom_call" | custom-call | bytes 786432 | tf_op jit(solution)/shard_map/pallas_call | solution.py:375
  86.4 0.7 add_bitcast_fusion.1
  87.1 1.1 %collective-permute-done.19 = bf16[1,96,384]{2,1,0:T(8,128)(2,1)S(1)} collective-permute-done((bf16[1,96,384]{2,1,0:T(8,128)(2,1)S(1)}, bf16[1,96,384]{2,1,0:T(8,128)(2,1)S(1)}, u32[]{:S(2)}, u32[]{:S(2)}) %collective-permute-start.19) | collective-permute-done | bytes 73760 | tf_op jit(solution)/shard_map/ppermute | solution.py:280
  88.3 0.7 add_bitcast_fusion
  (51 shorter events, 5.1 us)
Async XLA Ops:
  0.6 7.6 %copy-start.1 = (bf16[512,384]{1,0:T(8,128)(2,1)S(1)}, bf16[512,384]{1,0:T(8,128)(2,1)}, u32[]{:S(2)}) copy-start(bf16[512,384]{1,0:T(8,128)(2,1)} %param.7) | copy-start | bytes 1179652
  0.6 21.7 %all-to-all-start = ((bf16[16,32,384]{2,1,0:T(8,128)(2,1)}), bf16[16,32,384]{2,1,0:T(8,128)(2,1)S(1)}, u32[]{:S(2)}, u32[]{:S(2)}) async-start(bf16[16,32,384]{2,1,0:T(8,128)(2,1)} %bitcast.98), calls=%async_computation | async-start | bytes 786432 | tf_op jit(solution)/shard_map/all_to_all | solution.py:40
  8.3 37.1 %copy-start = (s32[2]{0:T(128)}, s32[2]{0:T(128)S(1)}, u32[]{:S(2)}) copy-start(s32[2]{0:T(128)S(1)} %pad_add_fusion.place_ref) | copy-start | bytes 28
  8.3 1.5 %collective-permute-start = (bf16[2,2,2,1,32,384]{5,4,2,1,0,3:T(8,128)(2,1)S(1)}, bf16[2,2,2,1,32,384]{5,4,2,1,0,3:T(8,128)(2,1)S(1)}, u32[]{:S(2)}, u32[]{:S(2)}) collective-permute-start(bf16[2,2,2,1,32,384]{5,4,2,1,0,3:T(8,128)(2,1)S(1)} %get-tuple-element.107), channel_id=1, source_target_pairs={{0,1},{1,0},{2,3},{3,2},{4,5},{5,4},{6,7},{7,6},{8,9},{9,8},{10,11... | collective-permute-start | bytes 589832 | tf_op jit(solution)/shard_map/ppermute | solution.py:280
  9.9 6.8 %collective-permute-start.3 = (bf16[2,2,32,384]{3,2,1,0:T(8,128)(2,1)S(1)}, bf16[2,2,32,384]{3,2,1,0:T(8,128)(2,1)S(1)}, u32[]{:S(2)}, u32[]{:S(2)}) collective-permute-start(bf16[2,2,32,384]{3,2,1,0:T(8,128)(2,1)S(1)} %bitcast.103), channel_id=1, source_target_pairs={{0,6},{1,7},{2,4},{3,5},{4,2},{5,3},{6,0},{7,1},{8,14},{9,15},{10,... | collective-permute-start | bytes 294920 | tf_op jit(solution)/shard_map/ppermute | solution.py:369
  12.7 6.0 %collective-permute-start.2 = (bf16[2,2,32,384]{3,2,1,0:T(8,128)(2,1)S(1)}, bf16[2,2,32,384]{3,2,1,0:T(8,128)(2,1)S(1)}, u32[]{:S(2)}, u32[]{:S(2)}) collective-permute-start(bf16[2,2,32,384]{3,2,1,0:T(8,128)(2,1)S(1)} %bitcast.104), channel_id=1, source_target_pairs={{0,4},{4,0},{8,12},{12,8},{16,20},{20,16},{24,28},{28,24},{1,5},{5... | collective-permute-start | bytes 294920 | tf_op jit(solution)/shard_map/ppermute | solution.py:280
  13.4 5.4 %collective-permute-start.1 = (bf16[2,2,32,384]{3,2,1,0:T(8,128)(2,1)S(1)}, bf16[2,2,32,384]{3,2,1,0:T(8,128)(2,1)S(1)}, u32[]{:S(2)}, u32[]{:S(2)}) collective-permute-start(bf16[2,2,32,384]{3,2,1,0:T(8,128)(2,1)S(1)} %bitcast.105), channel_id=1, source_target_pairs={{0,2},{1,3},{2,0},{3,1},{4,6},{5,7},{6,4},{7,5},{8,10},{9,11},{10,... | collective-permute-start | bytes 294920 | tf_op jit(solution)/shard_map/ppermute | solution.py:280
  22.3 11.0 %collective-permute-start.4 = (bf16[8,32,384]{2,1,0:T(8,128)(2,1)S(1)}, bf16[8,32,384]{2,1,0:T(8,128)(2,1)S(1)}, u32[]{:S(2)}, u32[]{:S(2)}) collective-permute-start(bf16[8,32,384]{2,1,0:T(8,128)(2,1)S(1)} %get-tuple-element.53), channel_id=1, source_target_pairs={{0,16},{4,20},{8,24},{12,28},{16,0},{20,4},{24,8},{28,12},{1,17},{... | collective-permute-start | bytes 589832 | tf_op jit(solution)/shard_map/ppermute | solution.py:280
  42.9 4.5 %collective-permute-start.6 = (bf16[16,96,384]{2,1,0:T(8,128)(2,1)S(1)}, bf16[16,96,384]{2,1,0:T(8,128)(2,1)S(1)}, u32[]{:S(2)}, u32[]{:S(2)}) collective-permute-start(bf16[16,96,384]{2,1,0:T(8,128)(2,1)S(1)} %get-tuple-element.64), channel_id=1, source_target_pairs={{0,1},{1,0},{2,3},{3,2},{4,5},{5,4},{6,7},{7,6},{8,9},{9,8},{10,11... | collective-permute-start | bytes 3538952 | tf_op jit(solution)/shard_map/ppermute | solution.py:280
  42.9 5.8 %collective-permute-start.14 = (bf16[16,96,384]{2,1,0:T(8,128)(2,1)S(1)}, bf16[16,96,384]{2,1,0:T(8,128)(2,1)S(1)}, u32[]{:S(2)}, u32[]{:S(2)}) collective-permute-start(bf16[16,96,384]{2,1,0:T(8,128)(2,1)S(1)} %get-tuple-element.78), channel_id=1, source_target_pairs={{0,1},{1,0},{2,3},{3,2},{4,5},{5,4},{6,7},{7,6},{8,9},{9,8},{10,11... | collective-permute-start | bytes 3538952 | tf_op jit(solution)/shard_map/ppermute | solution.py:280
  47.7 15.4 %collective-permute-start.7 = (bf16[8,96,384]{2,1,0:T(8,128)(2,1)S(1)}, bf16[8,96,384]{2,1,0:T(8,128)(2,1)S(1)}, u32[]{:S(2)}, u32[]{:S(2)}) collective-permute-start(bf16[8,96,384]{2,1,0:T(8,128)(2,1)S(1)} %get-tuple-element.84), channel_id=1, source_target_pairs={{0,4},{4,0},{8,12},{12,8},{16,20},{20,16},{24,28},{28,24},{1,5},{5... | collective-permute-start | bytes 1769480 | tf_op jit(solution)/shard_map/ppermute | solution.py:280
  49.1 15.1 %collective-permute-start.15 = (bf16[8,96,384]{2,1,0:T(8,128)(2,1)S(1)}, bf16[8,96,384]{2,1,0:T(8,128)(2,1)S(1)}, u32[]{:S(2)}, u32[]{:S(2)}) collective-permute-start(bf16[8,96,384]{2,1,0:T(8,128)(2,1)S(1)} %get-tuple-element.82), channel_id=1, source_target_pairs={{0,2},{1,3},{2,0},{3,1},{4,6},{5,7},{6,4},{7,5},{8,10},{9,11},{10,... | collective-permute-start | bytes 1769480 | tf_op jit(solution)/shard_map/ppermute | solution.py:280
  50.3 11.1 %collective-permute-start.5 = (bf16[2,2,2,1,32,384]{5,4,2,1,0,3:T(8,128)(2,1)S(1)}, bf16[2,2,2,1,32,384]{5,4,2,1,0,3:T(8,128)(2,1)S(1)}, u32[]{:S(2)}, u32[]{:S(2)}) collective-permute-start(bf16[2,2,2,1,32,384]{5,4,2,1,0,3:T(8,128)(2,1)S(1)} %get-tuple-element.54), channel_id=1, source_target_pairs={{0,16},{4,20},{8,24},{12,28},{16,0},{20,4},{24,8},{28,12},{1,17},{... | collective-permute-start | bytes 589832 | tf_op jit(solution)/shard_map/ppermute | solution.py:280
  63.2 3.0 %collective-permute-start.8 = (bf16[2,2,2,32,384]{4,3,2,1,0:T(8,128)(2,1)S(1)}, bf16[2,2,2,32,384]{4,3,2,1,0:T(8,128)(2,1)S(1)}, u32[]{:S(2)}, u32[]{:S(2)}) collective-permute-start(bf16[2,2,2,32,384]{4,3,2,1,0:T(8,128)(2,1)S(1)} %bitcast.102), channel_id=1, source_target_pairs={{0,1},{1,0},{2,3},{3,2},{4,5},{5,4},{6,7},{7,6},{8,9},{9,8},{10,11... | collective-permute-start | bytes 589832 | tf_op jit(solution)/shard_map/ppermute | solution.py:280
  64.4 8.6 %collective-permute-start.16 = (bf16[4,96,384]{2,1,0:T(8,128)(2,1)S(1)}, bf16[4,96,384]{2,1,0:T(8,128)(2,1)S(1)}, u32[]{:S(2)}, u32[]{:S(2)}) collective-permute-start(bf16[4,96,384]{2,1,0:T(8,128)(2,1)S(1)} %get-tuple-element.86), channel_id=1, source_target_pairs={{0,4},{4,0},{8,12},{12,8},{16,20},{20,16},{24,28},{28,24},{1,5},{5... | collective-permute-start | bytes 884744 | tf_op jit(solution)/shard_map/ppermute | solution.py:280
  65.4 8.3 %collective-permute-start.9 = (bf16[4,96,384]{2,1,0:T(8,128)(2,1)S(1)}, bf16[4,96,384]{2,1,0:T(8,128)(2,1)S(1)}, u32[]{:S(2)}, u32[]{:S(2)}) collective-permute-start(bf16[4,96,384]{2,1,0:T(8,128)(2,1)S(1)} %get-tuple-element.66), channel_id=1, source_target_pairs={{0,2},{1,3},{2,0},{3,1},{4,6},{5,7},{6,4},{7,5},{8,10},{9,11},{10,... | collective-permute-start | bytes 884744 | tf_op jit(solution)/shard_map/ppermute | solution.py:280
  73.0 6.9 %collective-permute-start.17 = (bf16[2,96,384]{2,1,0:T(8,128)(2,1)S(1)}, bf16[2,96,384]{2,1,0:T(8,128)(2,1)S(1)}, u32[]{:S(2)}, u32[]{:S(2)}) collective-permute-start(bf16[2,96,384]{2,1,0:T(8,128)(2,1)S(1)} %get-tuple-element.90), channel_id=1, source_target_pairs={{0,8},{4,12},{8,0},{12,4},{16,24},{20,28},{24,16},{28,20},{1,9},{5... | collective-permute-start | bytes 442376 | tf_op jit(solution)/shard_map/ppermute | solution.py:280
  73.8 10.0 %collective-permute-start.13 = (bf16[2,96,384]{2,1,0:T(8,128)(2,1)S(1)}, bf16[2,96,384]{2,1,0:T(8,128)(2,1)S(1)}, u32[]{:S(2)}, u32[]{:S(2)}) collective-permute-start(bf16[2,96,384]{2,1,0:T(8,128)(2,1)S(1)} %get-tuple-element.72), channel_id=1, source_target_pairs={{0,16},{4,20},{8,24},{12,28},{16,0},{20,4},{24,8},{28,12},{1,17},{... | collective-permute-start | bytes 442376 | tf_op jit(solution)/shard_map/ppermute | solution.py:280
  75.5 8.3 %collective-permute-start.10 = (bf16[4,32,384]{2,1,0:T(8,128)(2,1)S(1)}, bf16[4,32,384]{2,1,0:T(8,128)(2,1)S(1)}, u32[]{:S(2)}, u32[]{:S(2)}) collective-permute-start(bf16[4,32,384]{2,1,0:T(8,128)(2,1)S(1)} %get-tuple-element.68), channel_id=1, source_target_pairs={{0,2},{1,3},{2,0},{3,1},{4,6},{5,7},{6,4},{7,5},{8,10},{9,11},{10,... | collective-permute-start | bytes 294920 | tf_op jit(solution)/shard_map/ppermute | solution.py:280
  77.0 6.8 %collective-permute-start.11 = (bf16[4,32,384]{2,1,0:T(8,128)(2,1)S(1)}, bf16[4,32,384]{2,1,0:T(8,128)(2,1)S(1)}, u32[]{:S(2)}, u32[]{:S(2)}) collective-permute-start(bf16[4,32,384]{2,1,0:T(8,128)(2,1)S(1)} %get-tuple-element.69), channel_id=1, source_target_pairs={{0,4},{4,0},{8,12},{12,8},{16,20},{20,16},{24,28},{28,24},{1,5},{5... | collective-permute-start | bytes 294920 | tf_op jit(solution)/shard_map/ppermute | solution.py:280
  77.6 6.3 %collective-permute-start.12 = (bf16[4,32,384]{2,1,0:T(8,128)(2,1)S(1)}, bf16[4,32,384]{2,1,0:T(8,128)(2,1)S(1)}, u32[]{:S(2)}, u32[]{:S(2)}) collective-permute-start(bf16[4,32,384]{2,1,0:T(8,128)(2,1)S(1)} %get-tuple-element.70), channel_id=1, source_target_pairs={{0,6},{1,7},{2,4},{3,5},{4,2},{5,3},{6,0},{7,1},{8,14},{9,15},{10,... | collective-permute-start | bytes 294920 | tf_op jit(solution)/shard_map/ppermute | solution.py:369
  79.9 6.5 %collective-permute-start.18 = (bf16[1,96,384]{2,1,0:T(8,128)(2,1)S(1)}, bf16[1,96,384]{2,1,0:T(8,128)(2,1)S(1)}, u32[]{:S(2)}, u32[]{:S(2)}) collective-permute-start(bf16[1,96,384]{2,1,0:T(8,128)(2,1)S(1)} %fusion.9), channel_id=1, source_target_pairs={{0,16},{4,20},{8,24},{12,28},{16,0},{20,4},{24,8},{28,12},{1,17},{... | collective-permute-start | bytes 221192 | tf_op jit(solution)/shard_map/ppermute | solution.py:280
  83.8 0.6 copy-start.2
  83.8 0.6 copy-start.3
  83.8 0.7 copy-start.4
  83.9 4.4 %collective-permute-start.19 = (bf16[1,96,384]{2,1,0:T(8,128)(2,1)S(1)}, bf16[1,96,384]{2,1,0:T(8,128)(2,1)S(1)}, u32[]{:S(2)}, u32[]{:S(2)}) collective-permute-start(bf16[1,96,384]{2,1,0:T(8,128)(2,1)S(1)} %fusion.11), channel_id=1, source_target_pairs={{0,8},{4,12},{8,0},{12,4},{16,24},{20,28},{24,16},{28,20},{1,9},{5... | collective-permute-start | bytes 221192 | tf_op jit(solution)/shard_map/ppermute | solution.py:280
